TPU v7x, 32 devices: a whole 2x2x4 slice. The times are simulated.
32 devices in a mesh: group: 2 (over y), expert: 4 (over x, core), dp: 4 (over z).
Axes of the slice: x: 2, y: 2, z: 4, core: 2. Of those that a mesh axis runs over, the one named last changes fastest.
Arguments:
- tokens: bfloat16 [1024, 2048], P(('group', 'expert'), 'dp'), parts along dimension 0, may hold values from -6 to 6
- expert_ids: int32 [1024, 8], P(('group', 'expert')), parts along dimension 0, may hold values from 0 to 15, all different within a row; in each aligned block of 128 rows (0 to 127, 128 to 255, ...) at most 80 rows name the same one
- combine: float32 [1024, 8], P(('group', 'expert')), parts along dimension 0, may hold values from 0.05 to 1
- gate_weight: bfloat16 [16, 2048, 768], P('expert', 'dp'), may hold values from -0.125 to 0.125
- up_weight: bfloat16 [16, 2048, 768], P('expert', 'dp'), may hold values from -0.125 to 0.125
- down_weight: bfloat16 [16, 768, 2048], P('expert', None, 'dp'), may hold values from -0.21875 to 0.21875
- out_grad: bfloat16 [1024, 2048], P(('group', 'expert'), 'dp'), parts along dimension 0, may hold values from -6 to 6
Outputs:
- layer_out: bfloat16 [1024, 2048], P(('group', 'expert'), 'dp'), parts along dimension 0
- token_grad: bfloat16 [1024, 2048], P(('group', 'expert'), 'dp'), parts along dimension 0
- gate_grad: bfloat16 [32, 2048, 768], P(('group', 'expert'), 'dp'), parts along dimension 0
- up_grad: bfloat16 [32, 2048, 768], P(('group', 'expert'), 'dp'), parts along dimension 0
- down_grad: bfloat16 [32, 768, 2048], P(('group', 'expert'), None, 'dp'), parts along dimension 0
- combine_grad: float32 [1024, 8], P(('group', 'expert')), parts along dimension 0
There are 2 independent parts, one for each index of `group`. A program takes and returns all parts, laid end to end along the dimension named above; an argument that names none is the same for every part. Nothing has to cross between parts.
Inputs may be any that keep to these rules, and one draw needn't show every extreme that they name: `expert_ids`: each token names 8 different experts. Among the 128 tokens of one block no expert is named more than 80 times, and in some block one expert is named exactly 80 times.
All inputs are finite; a program needn't handle non-finite values.
Results may differ from a plain program's by a relative error of at most 0.019.
Values may be sent and summed in bfloat16 or wider, within the bound.
No kernel may reach another device: no remote copies, remote signals or barrier semaphores. Data moves between devices by JAX's collectives and lax.ppermute only.
A program may use at most 128 MiB of HBM per device.

v0:
```python
import jax
import jax.numpy as jnp
from jax import lax
from jax.sharding import PartitionSpec as P


def delta_pair(hidden_delta, gate_total, up_total):
    wide_grad = hidden_delta.astype(jnp.float32)
    sigmoid_gate = jax.nn.sigmoid(gate_total)
    gate_delta = (
        wide_grad * up_total * sigmoid_gate * (1.0 + gate_total * (1.0 - sigmoid_gate))
    ).astype(jnp.bfloat16)
    up_delta = (wide_grad * (gate_total * sigmoid_gate)).astype(jnp.bfloat16)
    return (gate_delta, up_delta)


def body(tokens, expert_ids, combine, gate_weight, up_weight, down_weight, out_grad):
    expert_peers = lax.axis_size("expert")
    local_count, local_width, hidden_width = gate_weight.shape
    token_count, choose = expert_ids.shape
    experts_all = expert_peers * local_count
    capacity = token_count * choose * 5 // (4 * experts_all)
    pair_count = token_count * choose
    buffer_rows = local_count * expert_peers * capacity
    expert_rows = expert_peers * capacity
    block_shape = (local_count, expert_peers, capacity, local_width)
    flat_ids = expert_ids.reshape(pair_count)
    onehot = (flat_ids[:, None] == jnp.arange(experts_all, dtype=jnp.int32)[None, :]).astype(
        jnp.int32
    )
    before = jnp.cumsum(onehot, axis=0) - onehot
    slot_index = jnp.sum(before * onehot, axis=1)
    target = (
        flat_ids % local_count * expert_peers + flat_ids // local_count
    ) * capacity + slot_index
    token_index = jnp.arange(pair_count, dtype=jnp.int32) // choose
    outgoing = (
        jnp.zeros((buffer_rows, local_width), jnp.bfloat16).at[target].set(tokens[token_index])
    )
    arrived = lax.all_to_all(
        outgoing.reshape(block_shape), "expert", split_axis=1, concat_axis=1, tiled=True
    )
    arrived = arrived.reshape(local_count, expert_rows, local_width)
    gate_part = jnp.einsum("erd,edf->erf", arrived, gate_weight, preferred_element_type=jnp.float32)
    up_part = jnp.einsum("erd,edf->erf", arrived, up_weight, preferred_element_type=jnp.float32)
    gate_total, up_total = (
        lax.psum(gate_part.astype(jnp.bfloat16), "dp").astype(jnp.float32),
        lax.psum(up_part.astype(jnp.bfloat16), "dp").astype(jnp.float32),
    )
    hidden = (gate_total * jax.nn.sigmoid(gate_total) * up_total).astype(jnp.bfloat16)
    expert_out = jnp.einsum(
        "erf,efd->erd", hidden, down_weight, preferred_element_type=jnp.float32
    ).astype(jnp.bfloat16)
    returned = lax.all_to_all(
        expert_out.reshape(block_shape), "expert", split_axis=1, concat_axis=1, tiled=True
    )
    picked = (
        returned.reshape(buffer_rows, local_width)[target]
        .astype(jnp.float32)
        .reshape(token_count, choose, local_width)
    )
    layer_out = jnp.sum(combine[:, :, None] * picked, axis=1).astype(jnp.bfloat16)
    wide_grad = out_grad.astype(jnp.float32)
    combine_grad = lax.psum(jnp.sum(picked * wide_grad[:, None, :], axis=2), "dp")
    scaled = (
        (combine[:, :, None] * wide_grad[:, None, :])
        .astype(jnp.bfloat16)
        .reshape(pair_count, local_width)
    )
    cot_outgoing = jnp.zeros((buffer_rows, local_width), jnp.bfloat16).at[target].set(scaled)
    cot_arrived = lax.all_to_all(
        cot_outgoing.reshape(block_shape), "expert", split_axis=1, concat_axis=1, tiled=True
    )
    cot_arrived = cot_arrived.reshape(local_count, expert_rows, local_width)
    down_grad = jnp.einsum(
        "erf,erd->efd", hidden, cot_arrived, preferred_element_type=jnp.float32
    ).astype(jnp.bfloat16)
    hidden_term = jnp.einsum(
        "erd,efd->erf", cot_arrived, down_weight, preferred_element_type=jnp.float32
    )
    hidden_term = hidden_term.reshape(buffer_rows, hidden_width)
    hidden_share = lax.psum_scatter(
        hidden_term.astype(jnp.bfloat16), "dp", scatter_dimension=0, tiled=True
    )
    gate_flat = gate_total.reshape(buffer_rows, hidden_width)
    up_flat = up_total.reshape(buffer_rows, hidden_width)
    share_rows = hidden_share.shape[0]
    first_row = lax.axis_index("dp") * share_rows
    gate_own = lax.dynamic_slice_in_dim(gate_flat, first_row, share_rows, 0)
    up_own = lax.dynamic_slice_in_dim(up_flat, first_row, share_rows, 0)
    gate_piece, up_piece = delta_pair(hidden_share, gate_own, up_own)
    gate_delta, up_delta = (
        lax.all_gather(gate_piece, "dp", axis=0, tiled=True),
        lax.all_gather(up_piece, "dp", axis=0, tiled=True),
    )
    gate_delta = gate_delta.reshape(local_count, expert_rows, hidden_width)
    up_delta = up_delta.reshape(local_count, expert_rows, hidden_width)
    gate_grad = jnp.einsum(
        "erd,erf->edf", arrived, gate_delta, preferred_element_type=jnp.float32
    ).astype(jnp.bfloat16)
    up_grad = jnp.einsum(
        "erd,erf->edf", arrived, up_delta, preferred_element_type=jnp.float32
    ).astype(jnp.bfloat16)
    input_delta = (
        jnp.einsum("erf,edf->erd", gate_delta, gate_weight, preferred_element_type=jnp.float32)
        + jnp.einsum("erf,edf->erd", up_delta, up_weight, preferred_element_type=jnp.float32)
    ).astype(jnp.bfloat16)
    back_grad = lax.all_to_all(
        input_delta.reshape(block_shape), "expert", split_axis=1, concat_axis=1, tiled=True
    )
    gathered = back_grad.reshape(buffer_rows, local_width)[target].astype(jnp.float32)
    token_grad = jnp.sum(gathered.reshape(token_count, choose, local_width), axis=1).astype(
        jnp.bfloat16
    )
    return (layer_out, token_grad, gate_grad, up_grad, down_grad, combine_grad)


def solution(mesh):
    return jax.shard_map(
        body,
        mesh=mesh,
        in_specs=(
            P(("group", "expert"), "dp"),
            P(("group", "expert"), None),
            P(("group", "expert"), None),
            P("expert", "dp", None),
            P("expert", "dp", None),
            P("expert", None, "dp"),
            P(("group", "expert"), "dp"),
        ),
        out_specs=(
            P(("group", "expert"), "dp"),
            P(("group", "expert"), "dp"),
            P(("group", "expert"), "dp", None),
            P(("group", "expert"), "dp", None),
            P(("group", "expert"), None, "dp"),
            P(("group", "expert"), None),
        ),
        check_vma=False,
    )
```

profile of v0, /device:TPU:0, one launch (start us, length us, event | category | flops | bytes accessed | tf_op | source)
XLA Modules:
  0.0 392.0 jit_solution(17045456511472587932)
XLA Ops:
  7.2 0.0 copy-start
  7.2 0.0 all-reduce.3.cloned.1.call-start
  7.2 0.9 copy.38
  8.2 0.1 eq.31
  8.3 0.1 eq.27
  8.4 0.1 reshape.254
  8.5 4.5 %reduce-window.6 = s32[16,8,128]{2,1,0:T(8,128)S(1)} reduce-window(s32[16,8,128]{2,1,0:T(8,128)S(1)} %fusion.18, s32[]{:T(128)} %constant.54.clone.1), window={size=1x1x128 pad=0_0x0_0x127_0}, to_apply=%region_0.0 | reduce-window | flops 2080768 | bytes 131076 | tf_op jit(solution)/shard_map/reduce-window
  13.0 0.1 slice.14
  13.1 0.1 copy.41
  13.3 0.1 copy.42
  13.3 0.1 broadcast_add_fusion
  13.5 14.0 %scatter_custom_fusion = bf16[1280,512]{1,0:T(8,128)(2,1)} fusion(s32[1024]{0:T(1024)S(1)} %bitcast.87, bf16[128,512]{1,0:T(8,128)(2,1)} %param.7, s32[1024]{0:T(1024)S(1)} %broadcast_clamp_fusion.1, bf16[]{:T(256)} %constant.53.clone.1), kind=kCustom, calls=%fused_computation.24 | custom fusion | bytes 1311232 | tf_op jit(solution)/shard_map/scatter | solution.py:38
  27.5 1.4 copy.43
  28.9 0.0 copy-start.4
  28.9 21.5 %all_to_all.20 = bf16[4,4,80,512]{3,2,0,1:T(8,128)(2,1)S(1)} all-to-all(bf16[4,4,80,512]{3,2,0,1:T(8,128)(2,1)S(1)} %copy.43), channel_id=1, replica_groups=mesh['group'=2,'expert'=4,'dp'=4] {'expert'}, dimensions={1} | all-to-all | bytes 2621440 | tf_op jit(solution)/shard_map/all_to_all | solution.py:40
  50.4 0.1 copy.44
  50.6 0.0 copy-start.2
  50.6 0.0 copy-start.6
  50.6 2.5 convolution_convert_fusion.4
  53.1 0.4 copy-done.6
  53.4 2.5 convolution_convert_fusion.5
  55.9 0.0 all-reduce.3.cloned.1.call-update
  55.9 0.0 reduce-scatter.2.cloned.1.call-start
  56.0 0.6 copy-done.11
  56.6 0.1 copy.37
  56.7 0.1 mul.98
  56.8 0.9 convert_element_type.87
  57.7 6.6 %scatter_custom_fusion.1 = bf16[1280,512]{1,0:T(8,128)(2,1)} fusion(s32[1024]{0:T(1024)S(1)} %bitcast.88, f32[128,512]{1,0:T(8,128)S(1)} %convert_element_type.87, f32[1024]{0:T(1024)S(1)} %mul.98, bf16[]{:T(256)} %constant.53.clone.1), kind=kCustom, calls=%fused_computation.22 | custom fusion | flops 1048576 | bytes 1576962 | tf_op jit(solution)/shard_map/scatter | solution.py:70
  64.3 1.4 copy.48
  65.7 19.7 %all_to_all.21 = bf16[4,4,80,512]{3,2,0,1:T(8,128)(2,1)S(1)} all-to-all(bf16[4,4,80,512]{3,2,0,1:T(8,128)(2,1)S(1)} %copy.48), channel_id=1, replica_groups=mesh['group'=2,'expert'=4,'dp'=4] {'expert'}, dimensions={1} | all-to-all | bytes 2621440 | tf_op jit(solution)/shard_map/all_to_all | solution.py:71
  85.5 0.1 copy.49
  85.6 2.5 convolution_convert_fusion.3
  88.1 0.0 reduce-scatter.2.cloned.1.call-update
  88.1 0.0 all-gather.3.cloned.1.call-start
  88.1 115.1 %all-reduce.3.cloned.1.call-done = (bf16[4,320,768]{2,1,0:T(8,128)(2,1)}, bf16[4,320,768]{2,1,0:T(8,128)(2,1)}) async-done(((bf16[4,320,768]{2,1,0:T(8,128)(2,1)}, bf16[4,320,768]{2,1,0:T(8,128)(2,1)}), (bf16[4,320,768]{2,1,0:T(8,128)(2,1)}, bf16[4,320,768]{2,1,0:T(8,128)(2,1)})) %all-reduce.3.cloned.1.call-update) | async-done | bytes 3932176 | tf_op jit(solution)/shard_map/psum | solution.py:48
  203.3 3.8 bitcast_convert_fusion
  207.1 2.3 bitcast_convert_fusion.1
  209.4 37.2 %reduce-scatter.2.cloned.1.call-done = bf16[320,768]{1,0:T(8,128)(2,1)} async-done(((bf16[1280,768]{1,0:T(8,128)(2,1)}), bf16[320,768]{1,0:T(8,128)(2,1)}) %reduce-scatter.2.cloned.1.call-update) | async-done | bytes 491536 | tf_op jit(solution)/shard_map/reduce_scatter | solution.py:82
  246.6 3.1 fusion.12
  249.8 0.0 all-gather.3.cloned.1.call-update
  249.8 0.0 all-gather.5.cloned.1.call-start
  249.8 0.5 all-gather.5.cloned.1.call-update
  250.4 3.5 convolution_convert_fusion.6
  253.8 1.2 copy.45
  255.0 3.7 all-to-all-start.1
  258.7 5.8 %convolution_convert_fusion = bf16[4,768,512]{2,1,0:T(8,128)(2,1)} fusion(bf16[4,320,512]{2,1,0:T(8,128)(2,1)S(1)} %bitcast.82, bf16[4,320,768]{2,1,0:T(8,128)(2,1)} %get-tuple-element.20, bf16[4,320,768]{2,1,0:T(8,128)(2,1)} %get-tuple-element.21), kind=kOutput, calls=%fused_computation.9 | convolution fusion | flops 1016070144 | bytes 8388608 | tf_op jit(solution)/shard_map/erf,erd->efd/dot_general | solution.py:75
  264.6 11.4 %all-to-all-done.1 = bf16[4,4,80,512]{3,2,0,1:T(8,128)(2,1)S(1)} async-done(((bf16[4,4,80,512]{3,2,0,1:T(8,128)(2,1)}), bf16[4,4,80,512]{3,2,0,1:T(8,128)(2,1)S(1)}, u32[]{:S(2)}, u32[]{:S(2)}) %all-to-all-start.1) | async-done | bytes 1310752 | tf_op jit(solution)/shard_map/all_to_all | solution.py:54
  276.0 0.1 copy.46
  276.1 5.1 %gather_fusion = bf16[1024,512]{1,0:T(8,128)(2,1)} fusion(bf16[1280,512]{1,0:T(8,128)(2,1)S(1)} %bitcast.68, s32[1024]{0:T(1024)S(1)} %broadcast_clamp_fusion), kind=kCustom, calls=%fused_computation.1 | custom fusion | bytes 2101248 | tf_op jit(solution)/shard_map/gather | solution.py:58
  281.2 11.6 %all-gather.3.cloned.1.call-done = bf16[1280,768]{1,0:T(8,128)(2,1)} async-done(((bf16[320,768]{1,0:T(8,128)(2,1)}), bf16[1280,768]{1,0:T(8,128)(2,1)}) %all-gather.3.cloned.1.call-update) | async-done | bytes 1966096 | tf_op jit(solution)/shard_map/all_gather | solution.py:93
  292.7 5.3 %fusion.21 = f32[4,320,512]{2,1,0:T(8,128)} fusion(bf16[4,320,768]{2,1,0:T(8,128)(2,1)} %bitcast.76, bf16[4,512,768]{2,1,0:T(8,128)(2,1)} %param.10), kind=kOutput, calls=%fused_computation.60 | convolution fusion | flops 1006632960 | bytes 7733248 | tf_op jit(solution)/shard_map/erf,edf->erd/dot_general | solution.py:105
  298.1 38.5 %all-gather.5.cloned.1.call-done = bf16[1280,768]{1,0:T(8,128)(2,1)} async-done(((bf16[320,768]{1,0:T(8,128)(2,1)}), bf16[1280,768]{1,0:T(8,128)(2,1)}) %all-gather.5.cloned.1.call-update) | async-done | bytes 1966096 | tf_op jit(solution)/shard_map/all_gather | solution.py:94
  336.6 3.5 add_convert_fusion
  340.1 1.2 copy.50
  341.3 3.7 all-to-all-start.3
  345.0 2.9 fusion.1
  347.9 17.7 %psum.23 = f32[128,8]{1,0:T(8,128)S(1)} all-reduce(f32[128,8]{1,0:T(8,128)S(1)} %get-tuple-element.18), channel_id=1, replica_groups=mesh['group'=2,'expert'=4,'dp'=4] {'dp'}, use_global_device_ids=true, to_apply=%region_11.12 | all-reduce | flops 1024 | bytes 8192 | tf_op jit(solution)/shard_map/psum | solution.py:64
  365.6 0.7 copy.52
  366.2 5.2 %convolution_convert_fusion.1 = bf16[4,512,768]{2,1,0:T(8,128)(2,1)} fusion(bf16[4,320,512]{2,1,0:T(8,128)(2,1)S(1)} %bitcast.71, bf16[4,320,768]{2,1,0:T(8,128)(2,1)} %bitcast.74), kind=kOutput, calls=%fused_computation.10 | convolution fusion | flops 1008205824 | bytes 6422528 | tf_op jit(solution)/shard_map/erd,erf->edf/dot_general | solution.py:101
  371.4 3.5 convolution_convert_fusion.2
  374.9 0.0 all-to-all-done.3
  374.9 1.2 copy.51
  376.1 6.7 %gather_fusion.1 = bf16[1024,512]{1,0:T(8,128)(2,1)} fusion(bf16[1280,512]{1,0:T(8,128)(2,1)} %bitcast.67, s32[1024]{0:T(1024)S(1)} %broadcast_clamp_fusion), kind=kCustom, calls=%fused_computation.2 | custom fusion | bytes 2101248 | tf_op jit(solution)/shard_map/gather | solution.py:111
  382.9 2.6 bitcast_reduce_fusion
  (26 shorter events, 0.2 us)
Async XLA Ops:
  7.2 78.4 %copy-start = (bf16[4,768,512]{2,1,0:T(8,128)(2,1)S(1)}, bf16[4,768,512]{2,1,0:T(8,128)(2,1)}, u32[]{:S(2)}) copy-start(bf16[4,768,512]{2,1,0:T(8,128)(2,1)} %param.12) | copy-start | bytes 9437188
  7.2 196.1 %all-reduce.3.cloned.1.call-start = ((), (), s32[]{:S(2)}) async-start(), calls=%async_computation.8 | async-start | bytes 7864320 | tf_op jit(solution)/shard_map/psum | solution.py:48
  28.9 21.7 %copy-start.4 = (bf16[4,512,768]{2,1,0:T(8,128)(2,1)S(1)}, bf16[4,512,768]{2,1,0:T(8,128)(2,1)}, u32[]{:S(2)}) copy-start(bf16[4,512,768]{2,1,0:T(8,128)(2,1)} %param.11) | copy-start | bytes 9437188
  50.6 2.5 copy-start.2
  50.6 2.9 copy-start.6
  55.9 0.7 copy-start.11
  55.9 190.7 %reduce-scatter.2.cloned.1.call-start = ((), (), s32[]{:S(2)}) async-start(), calls=%async_computation.5 | async-start | bytes 2457600 | tf_op jit(solution)/shard_map/reduce_scatter | solution.py:82
  85.5 2.5 copy-start.8
  88.1 204.6 %all-gather.3.cloned.1.call-start = ((), (), s32[]{:S(2)}) async-start(), calls=%async_computation.6 | async-start | bytes 2457600 | tf_op jit(solution)/shard_map/all_gather | solution.py:93
  203.2 3.9 copy-start.10
  249.8 86.8 %all-gather.5.cloned.1.call-start = ((), (), s32[]{:S(2)}) async-start(), calls=%async_computation.7 | async-start | bytes 2457600 | tf_op jit(solution)/shard_map/all_gather | solution.py:94
  255.0 3.7 copy-start.9
  255.0 20.9 %all-to-all-start.1 = ((bf16[4,4,80,512]{3,2,0,1:T(8,128)(2,1)}), bf16[4,4,80,512]{3,2,0,1:T(8,128)(2,1)S(1)}, u32[]{:S(2)}, u32[]{:S(2)}) async-start(bf16[4,4,80,512]{3,2,0,1:T(8,128)(2,1)} %copy.45), calls=%async_computation.1 | async-start | bytes 2621440 | tf_op jit(solution)/shard_map/all_to_all | solution.py:54
  292.7 43.9 %copy-start.5 = (bf16[4,512,768]{2,1,0:T(8,128)(2,1)S(1)}, bf16[4,512,768]{2,1,0:T(8,128)(2,1)}, u32[]{:S(2)}) copy-start(bf16[4,512,768]{2,1,0:T(8,128)(2,1)} %param.11) | copy-start | bytes 9437188
  341.3 24.9 %copy-start.3 = (bf16[4,4,80,512]{3,2,1,0:T(8,128)(2,1)S(1)}, bf16[4,4,80,512]{3,2,1,0:T(8,128)(2,1)}, u32[]{:S(2)}) copy-start(bf16[4,4,80,512]{3,2,1,0:T(8,128)(2,1)} %copy-done.2) | copy-start | bytes 3932164
  341.3 33.6 %all-to-all-start.3 = ((bf16[4,4,80,512]{3,2,0,1:T(8,128)(2,1)}), bf16[4,4,80,512]{3,2,0,1:T(8,128)(2,1)S(1)}, u32[]{:S(2)}, u32[]{:S(2)}) async-start(bf16[4,4,80,512]{3,2,0,1:T(8,128)(2,1)} %copy.50), calls=%async_computation.4 | async-start | bytes 2621440 | tf_op jit(solution)/shard_map/all_to_all | solution.py:108
  366.2 5.2 %copy-start.7 = (bf16[1280,768]{1,0:T(8,128)(2,1)S(1)}, bf16[1280,768]{1,0:T(8,128)(2,1)}, u32[]{:S(2)}) copy-start(bf16[1280,768]{1,0:T(8,128)(2,1)} %all-gather.3.cloned.1.call-done) | copy-start | bytes 5898244
  376.1 9.3 %copy-start.1 = (bf16[4,768,512]{2,1,0:T(8,128)(2,1)S(1)}, bf16[4,768,512]{2,1,0:T(8,128)(2,1)}, u32[]{:S(2)}) copy-start(bf16[4,768,512]{2,1,0:T(8,128)(2,1)} %param.12) | copy-start | bytes 9437188
Sparse Core Ops, SparseCore 0:
  56.0 147.1 all-reduce.2
  206.1 40.4 reduce-scatter.1
  249.9 42.7 all-gather.2
  294.1 42.3 all-gather.4
where the time goes:
time: 393 us; the launch traced here: 392 us
  waiting for transfers between devices  214 us (54%)
  blocking collectives  58.9 us (15%)
  local copies, waits for them, and re-layouts  35.8 us (9%)
  matrix products  34.3 us (9%)
  other arithmetic  27.1 us (7%)
  between operations  14 us (4%)
  starting transfers between devices  7.54 us (2%)
    psum x1, waiting for transfers between devices, body(): lax.psum(up_part.astype(jnp.bfloat16), 'dp').astype(jnp.float32)  115 us
    all_gather x1, waiting for transfers between devices, body(): lax.all_gather(up_piece, 'dp', axis=0, tiled=True)  38.5 us
    reduce_scatter x1, waiting for transfers between devices, body(): lax.psum_scatter(hidden_term.astype(jnp.bfloat16), 'dp', scatter_dimensio...  37.2 us
    all_to_all x1, blocking collectives, body(): lax.all_to_all(outgoing.reshape(block_shape), 'expert', split_axis=1, con...  21.5 us
    all_to_all x1, blocking collectives, body(): lax.all_to_all(cot_outgoing.reshape(block_shape), 'expert', split_axis=1,...  19.7 us
    psum x1, blocking collectives, body(): lax.psum(jnp.sum(picked * wide_grad[:, None, :], axis=2), 'dp')  17.7 us
    scatter x1, local copies, waits for them, and re-layouts, body(): jnp.zeros((buffer_rows, local_width), jnp.bfloat16).at[target]  14 us
    all_gather x1, waiting for transfers between devices, body(): lax.all_gather(gate_piece, 'dp', axis=0, tiled=True)  11.6 us
  transfers between devices with their start and end apart: 6, of which 5 were waited for; matrix products, arithmetic and copies ran while one was open for 13% of the time, Pallas kernels for 0%

commit v1 on v0

v1 whole, which is shorter than its diff:
```python
import functools

import jax
import jax.numpy as jnp
from jax import lax
from jax.experimental import pallas as pl
from jax.experimental.pallas import tpu as pltpu
from jax.sharding import PartitionSpec as P

F32, BF16 = jnp.float32, jnp.bfloat16
VMEM_BYTES = 48 << 20


def line_pairs(n, gather, step):
    if gather:
        senders = [i for i in range(step - 1, n - 1)]
    else:
        senders = [i for i in range(0, min(step, n - 1))]
    right = [(i, i + 1) for i in senders]
    left = [(n - 1 - i, n - 2 - i) for i in senders]
    return right, left


class Line:
    def __init__(self, axis, n, stride):
        self.axis, self.n, self.stride = axis, n, stride

    def send(self, value, pairs):
        wide = [
            (a * self.stride + c, b * self.stride + c) for a, b in pairs for c in range(self.stride)
        ]
        return lax.ppermute(value, self.axis, wide)

    def gather(self, own):
        n = self.n
        if n == 2:
            both = self.send(own, [(0, 1), (1, 0)])
            return [(both, both)]
        right, left, rights, lefts = own, own, [], []
        for step in range(1, n):
            pairs_r, pairs_l = line_pairs(n, True, step)
            right, left = self.send(right, pairs_r), self.send(left, pairs_l)
            rights.append(right)
            lefts.append(left)
        return [(rights[q - 1], lefts[n - q - 1]) for q in range(1, n)]

    def scatter(self, parts, add):
        n = self.n
        if n == 2:
            return self.send(parts[1], [(0, 1), (1, 0)]), None
        right, left = parts[1], parts[n - 1]
        for step in range(1, n):
            pairs_r, pairs_l = line_pairs(n, False, step)
            right, left = self.send(right, pairs_r), self.send(left, pairs_l)
            if step < n - 1:
                right, left = add(parts[step + 1], right), add(parts[n - 1 - step], left)
        return right, left


def add_rounded(a, b):
    return (a.astype(F32) + b.astype(F32)).astype(BF16)


def dot(a, b, dims=((1,), (0,))):
    return lax.dot_general(a, b, (dims, ((), ())), preferred_element_type=F32)


def place_of(scal, q, n, chips):
    block = lax.rem(scal[0] - q + n, n)
    core = lax.rem(lax.rem(block, 2) + scal[2], 2)
    return core * chips + lax.rem(scal[1] - block // 2 + chips, chips)


def routing(scal, w_ref, expert, n, rows):
    chips, (experts_all, tokens) = w_ref.shape[0] // 2, w_ref.shape[1:]
    local = experts_all // (2 * chips)
    which = (scal[1] * 2 + scal[2]) * local + expert
    ids = lax.broadcasted_iota(jnp.int32, (experts_all, tokens), 0)
    places = [place_of(scal, q, n, chips) for q in range(n)]
    weights = jnp.concatenate(
        [jnp.sum(jnp.where(ids == which, w_ref[p], 0.0), axis=0, keepdims=True) for p in places],
        axis=0,
    )
    chosen = weights > 0.0
    earlier = lax.broadcasted_iota(jnp.int32, (tokens, tokens), 0) < lax.broadcasted_iota(
        jnp.int32, (tokens, tokens), 1
    )
    slots = dot(chosen.astype(F32).astype(BF16), earlier.astype(F32).astype(BF16))
    slots = jnp.where(chosen, slots, -1.0).astype(jnp.int32)
    row = lax.broadcasted_iota(jnp.int32, (rows, tokens), 0)
    return [(places[q], weights[q : q + 1], row == slots[q : q + 1]) for q in range(n)]


def pre_kernel(n, expert, scal, w_ref, tok_ref, og_ref, gw, uw, dw, in_ref, cot_ref, *outs):
    rows = in_ref.shape[0] // n

    @pl.when(pl.program_id(0) == 0)
    def _():
        for q, (place, weight, hit) in enumerate(routing(scal, w_ref, expert, n, rows)):
            pick = hit.astype(F32).astype(BF16)
            span = pl.ds(q * rows, rows)
            in_ref[span, :] = dot(pick, tok_ref[place]).astype(BF16)
            scale = jnp.sum(jnp.where(hit, weight, 0.0), axis=1, keepdims=True)
            cot_ref[span, :] = (dot(pick, og_ref[place]) * scale).astype(BF16)

    tile = gw.shape[2]
    gate = dot(in_ref[...], gw[0]).astype(BF16).reshape(n, rows, tile)
    up = dot(in_ref[...], uw[0]).astype(BF16).reshape(n, rows, tile)
    back = dot(cot_ref[...], dw[0], ((1,), (1,))).astype(BF16).reshape(n, rows, tile)
    for q in range(n):
        outs[q][0] = gate[q]
        outs[q][1] = up[q]
        outs[q][2] = back[q]


def mid_kernel(own, right, left, out, product):
    total = own[...].astype(F32) + right[...].astype(F32) + left[...].astype(F32)
    gate, up, back = total[0], total[1], total[2]
    sig = jax.nn.sigmoid(gate)
    hidden = (gate * sig * up).astype(BF16)
    delta = back.astype(BF16).astype(F32)
    out[0] = hidden
    out[1] = (delta * up * sig * (1.0 + gate * (1.0 - sig))).astype(BF16)
    out[2] = (delta * (gate * sig)).astype(BF16)
    prod = hidden.astype(F32) * back
    lanes = product.shape[1]
    acc = prod[:, 0:lanes]
    for k in range(1, prod.shape[1] // lanes):
        acc = acc + prod[:, k * lanes : (k + 1) * lanes]
    product[...] = acc


def load_rows(scal, n, which, pieces):
    own, rest = pieces[0], pieces[1:]
    values = [own[which]]
    for q in range(1, n):
        values.append(jnp.where(scal[0] >= q, rest[2 * q - 2][which], rest[2 * q - 1][which]))
    return jnp.concatenate(values, axis=0)


def out_kernel(n, expert, has_prev, scal, w_ref, *refs):
    if has_prev:
        prev, refs = refs[0], refs[1:]
    pieces, refs = refs[: 2 * n - 1], refs[2 * n - 1 :]
    gw, uw, dw, out, eo, idl = refs
    step = pl.program_id(0)

    @pl.when(step == 0)
    def _():
        eo[...] = jnp.zeros_like(eo)
        idl[...] = jnp.zeros_like(idl)

    eo[...] += dot(load_rows(scal, n, 0, pieces), dw[0])
    idl[...] += dot(load_rows(scal, n, 1, pieces), gw[0], ((1,), (1,))) + dot(
        load_rows(scal, n, 2, pieces), uw[0], ((1,), (1,))
    )

    @pl.when(step == pl.num_programs(0) - 1)
    def _():
        rows = eo.shape[0] // n
        for q, (place, weight, hit) in enumerate(routing(scal, w_ref, expert, n, rows)):
            pick = hit.astype(F32)
            scaled = (pick * weight).astype(BF16)
            span = pl.ds(q * rows, rows)
            layer = dot(scaled, eo[span, :].astype(BF16), ((0,), (0,)))
            token = dot(pick.astype(BF16), idl[span, :].astype(BF16), ((0,), (0,)))
            if has_prev:
                layer, token = layer + prev[place, 0], token + prev[place, 1]
            out[place, 0] = layer.astype(out.dtype)
            out[place, 1] = token.astype(out.dtype)


def grad_kernel(n, has_prev, scal, in_ref, cot_ref, *refs):
    pieces, refs = refs[: 2 * n - 1], refs[2 * n - 1 :]
    if has_prev:
        refs = refs[3:]
    gg, ug, dg = refs
    gg[0] = dot(in_ref[...], load_rows(scal, n, 1, pieces), ((0,), (0,))).astype(BF16)
    ug[0] = dot(in_ref[...], load_rows(scal, n, 2, pieces), ((0,), (0,))).astype(BF16)
    dg[0] = dot(load_rows(scal, n, 0, pieces), cot_ref[...], ((0,), (0,))).astype(BF16)


def whole_spec(shape):
    return pl.BlockSpec(tuple(shape), lambda g: (0,) * len(shape))


SMEM_SPEC = pl.BlockSpec(memory_space=pltpu.SMEM)


def call(kernel, grid, in_specs, out_specs, out_shape, flops, moved, **rest):
    return pl.pallas_call(
        kernel,
        grid=(grid,),
        in_specs=in_specs,
        out_specs=out_specs,
        out_shape=out_shape,
        compiler_params=pltpu.CompilerParams(vmem_limit_bytes=VMEM_BYTES),
        cost_estimate=pl.CostEstimate(flops=flops, bytes_accessed=moved, transcendentals=0),
        **rest,
    )


def body(tokens, expert_ids, combine, gate_weight, up_weight, down_weight, out_grad):
    peers, n = lax.axis_size("expert"), lax.axis_size("dp")
    assert peers == n
    chips = peers // 2
    local, width, hidden = gate_weight.shape
    count, choose = expert_ids.shape
    experts_all = peers * local
    capacity = count * choose * 5 // (4 * experts_all)
    rows = -(-capacity // 16) * 16
    all_rows = n * rows
    tile = 256
    grid = hidden // tile
    me = lax.axis_index("expert")
    scal = jnp.stack([lax.axis_index("dp"), me // 2, lax.rem(me, 2)]).astype(jnp.int32)

    ids_t, combine_t = expert_ids.T, combine.T
    named = ids_t[:, None, :] == jnp.arange(experts_all, dtype=jnp.int32)[None, :, None]
    dense = jnp.sum(jnp.where(named, combine_t[:, None, :], 0.0), axis=0)

    along_x, across = Line("expert", chips, 2), Line("expert", peers, 1)
    swap = [(2 * x + c, 2 * x + 1 - c) for x in range(chips) for c in range(2)]

    def gather_blocks(own):
        others = along_x.gather(own)
        here = [own] + [
            right if right is left else jnp.where(scal[1] >= q + 1, right, left)
            for q, (right, left) in enumerate(others)
        ]
        there = [across.send(piece, swap) for piece in here]
        return jnp.stack(here + there)

    w_all = gather_blocks(dense)
    tok_all = gather_blocks(tokens)
    og_all = gather_blocks(out_grad)

    mac = all_rows * width * hidden
    weight_bytes = 2 * width * hidden
    piece_shape = jax.ShapeDtypeStruct((3, rows, hidden), BF16)
    piece_spec = pl.BlockSpec((3, rows, tile), lambda g: (0, 0, g))
    slot_shape = jax.ShapeDtypeStruct((all_rows, width), BF16)
    slot_spec = whole_spec((all_rows, width))

    def weight_specs(e):
        wide = pl.BlockSpec((1, width, tile), lambda g: (e, 0, g))
        return [wide, wide, pl.BlockSpec((1, tile, width), lambda g: (e, g, 0))]

    along_z = Line("dp", n, 1)
    arrived, totals = [], []
    for e in range(local):
        inputs, cot, *parts = call(
            functools.partial(pre_kernel, n, e),
            grid,
            [SMEM_SPEC, whole_spec(w_all.shape), whole_spec(tok_all.shape), whole_spec(og_all.shape)]
            + weight_specs(e),
            [slot_spec] * 2 + [piece_spec] * n,
            [slot_shape] * 2 + [piece_shape] * n,
            6 * mac,
            3 * weight_bytes + 5 * 2 * all_rows * hidden,
        )(scal, w_all, tok_all, og_all, gate_weight, up_weight, down_weight)
        arrived.append((inputs, cot))
        totals.append((parts[0], *along_z.scatter(parts, add_rounded)))

    products, grads, partial_sums = [], None, None
    for e in range(local):
        own, product = call(
            mid_kernel,
            1,
            [whole_spec(piece_shape.shape)] * 3,
            [whole_spec(piece_shape.shape), whole_spec((rows, 128))],
            [piece_shape, jax.ShapeDtypeStruct((rows, 128), F32)],
            20 * rows * hidden,
            24 * rows * hidden,
        )(*totals[e])
        products.append(product)
        pieces = [own]
        for right, left in along_z.gather(own):
            pieces += [right, left]
        piece_specs = [piece_spec] * len(pieces)
        last = e == local - 1
        sum_shape = (2 * chips, 2, count, width)
        partial_sums = call(
            functools.partial(out_kernel, n, e, e > 0),
            grid,
            [SMEM_SPEC, whole_spec(w_all.shape)]
            + ([whole_spec(sum_shape)] if e > 0 else [])
            + piece_specs
            + weight_specs(e),
            whole_spec(sum_shape),
            jax.ShapeDtypeStruct(sum_shape, BF16 if last else F32),
            6 * mac,
            3 * weight_bytes + 9 * 2 * all_rows * hidden,
            scratch_shapes=[pltpu.VMEM((all_rows, width), F32)] * 2,
        )(
            scal,
            w_all,
            *([partial_sums] if e > 0 else []),
            *pieces,
            gate_weight,
            up_weight,
            down_weight,
        )
        inputs, cot = arrived[e]
        base = 3 + len(pieces)
        grads = call(
            functools.partial(grad_kernel, n, e > 0),
            grid,
            [SMEM_SPEC, slot_spec, slot_spec]
            + piece_specs
            + ([pl.BlockSpec(memory_space=pl.ANY)] * 3 if e > 0 else []),
            weight_specs(e),
            [
                jax.ShapeDtypeStruct(gate_weight.shape, BF16),
                jax.ShapeDtypeStruct(up_weight.shape, BF16),
                jax.ShapeDtypeStruct(down_weight.shape, BF16),
            ],
            6 * mac,
            3 * weight_bytes + 8 * 2 * all_rows * hidden,
            input_output_aliases={base + k: k for k in range(3)} if e > 0 else {},
        )(scal, inputs, cot, *pieces, *(grads if e > 0 else []))

    near, far = partial_sums[:chips], partial_sums[chips:]
    near = add_rounded(near, across.send(far, swap))
    right, left = along_x.scatter([near[q] for q in range(chips)], add_rounded)
    home = near[0].astype(F32) + right.astype(F32)
    if left is not None:
        home = home + left.astype(F32)
    home = home.astype(BF16)

    own_products = jnp.sum(jnp.stack(products), axis=2)
    all_products = lax.all_gather(own_products, ("expert", "dp"), axis=0, tiled=False)
    all_products = all_products.reshape(peers, n, local, rows)
    mine = lax.dynamic_index_in_dim(all_products, me, 1, keepdims=False).reshape(experts_all, rows)
    chosen = dense > 0.0
    earlier = (jnp.arange(count)[:, None] < jnp.arange(count)[None, :]).astype(BF16)
    slots = jnp.dot(chosen.astype(BF16), earlier, preferred_element_type=F32).astype(jnp.int32)
    at_slot = slots[:, None, :] == jnp.arange(rows, dtype=jnp.int32)[None, :, None]
    per_expert = jnp.sum(jnp.where(at_slot, mine[:, :, None], 0.0), axis=1)
    combine_grad = jnp.sum(jnp.where(named, per_expert[None], 0.0), axis=1) / combine_t
    return (home[0], home[1], *grads, combine_grad.T)


def solution(mesh):
    return jax.shard_map(
        body,
        mesh=mesh,
        in_specs=(
            P(("group", "expert"), "dp"),
            P(("group", "expert"), None),
            P(("group", "expert"), None),
            P("expert", "dp", None),
            P("expert", "dp", None),
            P("expert", None, "dp"),
            P(("group", "expert"), "dp"),
        ),
        out_specs=(
            P(("group", "expert"), "dp"),
            P(("group", "expert"), "dp"),
            P(("group", "expert"), "dp", None),
            P(("group", "expert"), "dp", None),
            P(("group", "expert"), None, "dp"),
            P(("group", "expert"), None),
        ),
        check_vma=False,
    )
```

time: 393 us -> 311 us (0.79)
  waiting for transfers between devices: 214 us -> 44.9 us
  starting transfers between devices: 7.54 us -> 148 us
  Pallas kernels: 0 us -> 50.4 us
  matrix products: 34.3 us -> 0.14 us
  local copies, waits for them, and re-layouts: 35.8 us -> 13.1 us
  other arithmetic: 27.1 us -> 5.38 us
  blocking collectives: 58.9 us -> 45.1 us
  between operations: 14 us -> 1.85 us
    ppermute x0 -> x59, starting transfers between devices: none -> 148 us  [send(): return lax.ppermute(value, self.axis, wide)]
    psum x1 -> x0, waiting for transfers between devices: 115 us -> none  [body(): lax.psum(up_part.astype(jnp.bfloat16), 'dp').astype(jnp.float32)]
    pallas_call x0 -> x16, Pallas kernels: none -> 50.4 us  [the longest x4 18.5 us: body(): call(functools.partial(out_kernel, n, e, e > 0), grid, [SMEM_SPEC, whole_...]
    all_gather x2 -> x0, waiting for transfers between devices: 50.1 us -> none  [the longest x1 38.5 us: body(): lax.all_gather(up_piece, 'dp', axis=0, tiled=True)]
    all_gather x0 -> x1, blocking collectives: none -> 45.1 us  [body(): lax.all_gather(own_products, ('expert', 'dp'), axis=0, tiled=False)]
    ppermute x0 -> x59, waiting for transfers between devices: none -> 44.9 us  [send(): return lax.ppermute(value, self.axis, wide)]
    all_to_all x2 -> x0, blocking collectives: 41.3 us -> none  [the longest x1 21.5 us: body(): lax.all_to_all(outgoing.reshape(block_shape), 'expert', split_axis=1, con...]
    reduce_scatter x1 -> x0, waiting for transfers between devices: 37.2 us -> none  [body(): lax.psum_scatter(hidden_term.astype(jnp.bfloat16), 'dp', scatter_dimensio...]
  transfers between devices with their start and end apart: 6 -> 59, of which waited for: 5 -> 18; matrix products, arithmetic and copies ran while one was open for 13% -> 1% of each run, Pallas kernels for 0% -> 14%
where the time goes in v1:
time: 311 us; the launch traced here: 309 us
  starting transfers between devices  148 us (48%)
  Pallas kernels  50.4 us (16%)
  blocking collectives  45.1 us (15%)
  waiting for transfers between devices  44.9 us (14%)
  local copies, waits for them, and re-layouts  13.1 us (4%)
  other arithmetic  5.38 us (2%)
    ppermute x59, starting transfers between devices, send(): return lax.ppermute(value, self.axis, wide)  148 us
    all_gather x1, blocking collectives, body(): lax.all_gather(own_products, ('expert', 'dp'), axis=0, tiled=False)  45.1 us
    ppermute x59, waiting for transfers between devices, send(): return lax.ppermute(value, self.axis, wide)  44.9 us
    pallas_call x4, Pallas kernels, body(): call(functools.partial(out_kernel, n, e, e > 0), grid, [SMEM_SPEC, whole_...  18.5 us
    pallas_call x4, Pallas kernels, body(): call(functools.partial(grad_kernel, n, e > 0), grid, [SMEM_SPEC, slot_spe...  15.7 us
    pallas_call x4, Pallas kernels, body(): call(functools.partial(pre_kernel, n, e), grid, [SMEM_SPEC, whole_spec(w_...  15 us
    unnamed x78, local copies, waits for them, and re-layouts  12.3 us
  transfers between devices with their start and end apart: 59, of which 18 were waited for; matrix products, arithmetic and copies ran while one was open for 1% of the time, Pallas kernels for 14%

profile of v1, /device:TPU:0, one launch (start us, length us, event | category | flops | bytes accessed | tf_op | source)
XLA Modules:
  0.0 308.9 jit_solution(15216727713187965482)
XLA Ops:
  0.6 7.1 %collective-permute-start.3 = (bf16[128,512]{1,0:T(8,128)(2,1)}, bf16[128,512]{1,0:T(8,128)(2,1)S(1)}, u32[]{:S(2)}, u32[]{:S(2)}) collective-permute-start(bf16[128,512]{1,0:T(8,128)(2,1)} %param.7), channel_id=1, source_target_pairs={{0,8},{4,12},{8,0},{12,4},{1,9},{5,13},{9,1},{13,5},{2,10},{6,14},... | collective-permute-start | bytes 393224 | tf_op jit(solution)/shard_map/ppermute | solution.py:32
  7.8 5.7 %collective-permute-start.6 = (bf16[128,512]{1,0:T(8,128)(2,1)}, bf16[128,512]{1,0:T(8,128)(2,1)S(1)}, u32[]{:S(2)}, u32[]{:S(2)}) collective-permute-start(bf16[128,512]{1,0:T(8,128)(2,1)} %param.13), channel_id=1, source_target_pairs={{0,8},{4,12},{8,0},{12,4},{1,9},{5,13},{9,1},{13,5},{2,10},{6,14},... | collective-permute-start | bytes 393224 | tf_op jit(solution)/shard_map/ppermute | solution.py:32
  14.2 2.0 collective-permute-start
  16.2 4.5 %collective-permute-start.4 = (bf16[128,512]{1,0:T(8,128)(2,1)}, bf16[128,512]{1,0:T(8,128)(2,1)S(1)}, u32[]{:S(2)}, u32[]{:S(2)}) collective-permute-start(bf16[128,512]{1,0:T(8,128)(2,1)} %param.7), channel_id=1, source_target_pairs={{0,4},{4,0},{8,12},{12,8},{1,5},{5,1},{9,13},{13,9},{2,6},{6,2},{1... | collective-permute-start | bytes 393224 | tf_op jit(solution)/shard_map/ppermute | solution.py:32
  20.7 5.7 %collective-permute-start.2 = (f32[16,128]{1,0:T(8,128)S(1)}, f32[16,128]{1,0:T(8,128)S(1)}, u32[]{:S(2)}, u32[]{:S(2)}) collective-permute-start(f32[16,128]{1,0:T(8,128)S(1)} %collective-permute-done), channel_id=1, source_target_pairs={{0,4},{4,0},{8,12},{12,8},{1,5},{5,1},{9,13},{13,9},{2,6},{6,2},{1... | collective-permute-start | bytes 24584 | tf_op jit(solution)/shard_map/ppermute | solution.py:32
  26.4 5.7 %collective-permute-start.5 = (bf16[128,512]{1,0:T(8,128)(2,1)S(1)}, bf16[128,512]{1,0:T(8,128)(2,1)S(1)}, u32[]{:S(2)}, u32[]{:S(2)}) collective-permute-start(bf16[128,512]{1,0:T(8,128)(2,1)S(1)} %collective-permute-done.3), channel_id=1, source_target_pairs={{0,4},{4,0},{8,12},{12,8},{1,5},{5,1},{9,13},{13,9},{2,6},{6,2},{1... | collective-permute-start | bytes 393224 | tf_op jit(solution)/shard_map/ppermute | solution.py:32
  32.6 5.5 %collective-permute-start.8 = (bf16[128,512]{1,0:T(8,128)(2,1)S(1)}, bf16[128,512]{1,0:T(8,128)(2,1)S(1)}, u32[]{:S(2)}, u32[]{:S(2)}) collective-permute-start(bf16[128,512]{1,0:T(8,128)(2,1)S(1)} %collective-permute-done.6), channel_id=1, source_target_pairs={{0,4},{4,0},{8,12},{12,8},{1,5},{5,1},{9,13},{13,9},{2,6},{6,2},{1... | collective-permute-start | bytes 393224 | tf_op jit(solution)/shard_map/ppermute | solution.py:32
  40.3 3.7 %shard_map.127 = (bf16[320,512]{1,0:T(8,128)(2,1)S(1)}, bf16[320,512]{1,0:T(8,128)(2,1)S(1)}, bf16[3,80,768]{2,1,0:T(8,128)(2,1)S(1)}, bf16[3,80,768]{2,1,0:T(8,...) custom-call(s32[3]{0:T(128)S(1)} %pad_add_fusion.scal, ...), custom_call_target="tpu_custom_call" | custom-call | flops 754974720 | bytes 4816896 | tf_op jit(solution)/shard_map/pallas_call | solution.py:252
  45.5 3.6 %collective-permute-start.45 = (bf16[3,80,768]{2,1,0:T(8,128)(2,1)S(1)}, bf16[3,80,768]{2,1,0:T(8,128)(2,1)S(1)}, u32[]{:S(2)}, u32[]{:S(2)}) collective-permute-start(bf16[3,80,768]{2,1,0:T(8,128)(2,1)S(1)} %get-tuple-element.68), channel_id=1, source_target_pairs={{0,1},{4,5},{8,9},{12,13},{16,17},{20,21},{24,25},{28,29}} | collective-permute-start | bytes 1105928 | tf_op jit(solution)/shard_map/ppermute | solution.py:32
  49.1 3.7 %shard_map.124 = (bf16[320,512]{1,0:T(8,128)(2,1)S(1)}, bf16[320,512]{1,0:T(8,128)(2,1)S(1)}, bf16[3,80,768]{2,1,0:T(8,128)(2,1)S(1)}, bf16[3,80,768]{2,1,0:T(8,...) custom-call(s32[3]{0:T(128)S(1)} %pad_add_fusion.scal, ...), custom_call_target="tpu_custom_call" | custom-call | flops 754974720 | bytes 4816896 | tf_op jit(solution)/shard_map/pallas_call | solution.py:252
  54.3 1.3 collective-permute-start.33
  55.6 3.7 %shard_map.121 = (bf16[320,512]{1,0:T(8,128)(2,1)S(1)}, bf16[320,512]{1,0:T(8,128)(2,1)S(1)}, bf16[3,80,768]{2,1,0:T(8,128)(2,1)S(1)}, bf16[3,80,768]{2,1,0:T(8,...) custom-call(s32[3]{0:T(128)S(1)} %pad_add_fusion.scal, ...), custom_call_target="tpu_custom_call" | custom-call | flops 754974720 | bytes 4816896 | tf_op jit(solution)/shard_map/pallas_call | solution.py:252
  61.5 3.8 %shard_map.118 = (bf16[320,512]{1,0:T(8,128)(2,1)S(1)}, bf16[320,512]{1,0:T(8,128)(2,1)S(1)}, bf16[3,80,768]{2,1,0:T(8,128)(2,1)S(1)}, bf16[3,80,768]{2,1,0:T(8,...) custom-call(s32[3]{0:T(128)S(1)} %pad_add_fusion.scal, ...), custom_call_target="tpu_custom_call" | custom-call | flops 754974720 | bytes 4816896 | tf_op jit(solution)/shard_map/pallas_call | solution.py:252
  65.3 1.3 collective-permute-start.21
  67.5 1.3 collective-permute-start.9
  69.7 1.8 collective-permute-start.46
  71.6 4.0 %collective-permute-done.21 = bf16[3,80,768]{2,1,0:T(8,128)(2,1)S(1)} collective-permute-done((bf16[3,80,768]{2,1,0:T(8,128)(2,1)S(1)}, bf16[3,80,768]{2,1,0:T(8,128)(2,1)S(1)}, u32[]{:S(2)}, u32[]{:S(2)}) %collective-permute-start.21) | collective-permute-done | bytes 368672 | tf_op jit(solution)/shard_map/ppermute | solution.py:32
  76.4 6.0 %collective-permute-start.34 = (bf16[3,80,768]{2,1,0:T(8,128)(2,1)S(1)}, bf16[3,80,768]{2,1,0:T(8,128)(2,1)S(1)}, u32[]{:S(2)}, u32[]{:S(2)}) collective-permute-start(bf16[3,80,768]{2,1,0:T(8,128)(2,1)S(1)} %get-tuple-element.97), channel_id=1, source_target_pairs={{0,1},{1,2},{4,5},{5,6},{8,9},{9,10},{12,13},{13,14},{16,17},{17,1... | collective-permute-start | bytes 1105928 | tf_op jit(solution)/shard_map/ppermute | solution.py:32
  84.3 6.0 %collective-permute-start.22 = (bf16[3,80,768]{2,1,0:T(8,128)(2,1)S(1)}, bf16[3,80,768]{2,1,0:T(8,128)(2,1)S(1)}, u32[]{:S(2)}, u32[]{:S(2)}) collective-permute-start(bf16[3,80,768]{2,1,0:T(8,128)(2,1)S(1)} %get-tuple-element.99), channel_id=1, source_target_pairs={{0,1},{1,2},{4,5},{5,6},{8,9},{9,10},{12,13},{13,14},{16,17},{17,1... | collective-permute-start | bytes 1105928 | tf_op jit(solution)/shard_map/ppermute | solution.py:32
  92.1 6.1 %collective-permute-start.10 = (bf16[3,80,768]{2,1,0:T(8,128)(2,1)S(1)}, bf16[3,80,768]{2,1,0:T(8,128)(2,1)S(1)}, u32[]{:S(2)}, u32[]{:S(2)}) collective-permute-start(bf16[3,80,768]{2,1,0:T(8,128)(2,1)S(1)} %get-tuple-element.101), channel_id=1, source_target_pairs={{0,1},{1,2},{4,5},{5,6},{8,9},{9,10},{12,13},{13,14},{16,17},{17,1... | collective-permute-start | bytes 1105928 | tf_op jit(solution)/shard_map/ppermute | solution.py:32
  99.2 1.3 collective-permute-start.50
  100.6 6.1 %collective-permute-start.47 = (bf16[3,80,768]{2,1,0:T(8,128)(2,1)S(1)}, bf16[3,80,768]{2,1,0:T(8,128)(2,1)S(1)}, u32[]{:S(2)}, u32[]{:S(2)}) collective-permute-start(bf16[3,80,768]{2,1,0:T(8,128)(2,1)S(1)} %add_convert_fusion.2), channel_id=1, source_target_pairs={{0,1},{1,2},{2,3},{4,5},{5,6},{6,7},{8,9},{9,10},{10,11},{12,13},{... | collective-permute-start | bytes 1105928 | tf_op jit(solution)/shard_map/ppermute | solution.py:32
  107.1 1.3 collective-permute-start.38
  108.5 6.1 %collective-permute-start.35 = (bf16[3,80,768]{2,1,0:T(8,128)(2,1)S(1)}, bf16[3,80,768]{2,1,0:T(8,128)(2,1)S(1)}, u32[]{:S(2)}, u32[]{:S(2)}) collective-permute-start(bf16[3,80,768]{2,1,0:T(8,128)(2,1)S(1)} %add_convert_fusion.4), channel_id=1, source_target_pairs={{0,1},{1,2},{2,3},{4,5},{5,6},{6,7},{8,9},{9,10},{10,11},{12,13},{... | collective-permute-start | bytes 1105928 | tf_op jit(solution)/shard_map/ppermute | solution.py:32
  115.0 1.3 collective-permute-start.26
  116.3 6.0 %collective-permute-start.23 = (bf16[3,80,768]{2,1,0:T(8,128)(2,1)S(1)}, bf16[3,80,768]{2,1,0:T(8,128)(2,1)S(1)}, u32[]{:S(2)}, u32[]{:S(2)}) collective-permute-start(bf16[3,80,768]{2,1,0:T(8,128)(2,1)S(1)} %add_convert_fusion.6), channel_id=1, source_target_pairs={{0,1},{1,2},{2,3},{4,5},{5,6},{6,7},{8,9},{9,10},{10,11},{12,13},{... | collective-permute-start | bytes 1105928 | tf_op jit(solution)/shard_map/ppermute | solution.py:32
  122.9 1.3 collective-permute-start.14
  124.3 6.1 %collective-permute-start.11 = (bf16[3,80,768]{2,1,0:T(8,128)(2,1)S(1)}, bf16[3,80,768]{2,1,0:T(8,128)(2,1)S(1)}, u32[]{:S(2)}, u32[]{:S(2)}) collective-permute-start(bf16[3,80,768]{2,1,0:T(8,128)(2,1)S(1)} %add_convert_fusion.8), channel_id=1, source_target_pairs={{0,1},{1,2},{2,3},{4,5},{5,6},{6,7},{8,9},{9,10},{10,11},{12,13},{... | collective-permute-start | bytes 1105928 | tf_op jit(solution)/shard_map/ppermute | solution.py:32
  130.8 1.3 collective-permute-start.52
  132.4 6.3 %collective-permute-start.51 = (bf16[3,80,768]{2,1,0:T(8,128)(2,1)S(1)}, bf16[3,80,768]{2,1,0:T(8,128)(2,1)S(1)}, u32[]{:S(2)}, u32[]{:S(2)}) collective-permute-start(bf16[3,80,768]{2,1,0:T(8,128)(2,1)S(1)} %get-tuple-element.69.refs_1_.refs_0_), channel_id=1, source_target_pairs={{0,1},{1,2},{2,3},{4,5},{5,6},{6,7},{8,9},{9,10},{10,11},{12,13},{... | collective-permute-start | bytes 1105928 | tf_op jit(solution)/shard_map/ppermute | solution.py:32
  138.8 1.3 collective-permute-start.40
  140.1 6.0 %collective-permute-start.39 = (bf16[3,80,768]{2,1,0:T(8,128)(2,1)S(1)}, bf16[3,80,768]{2,1,0:T(8,128)(2,1)S(1)}, u32[]{:S(2)}, u32[]{:S(2)}) collective-permute-start(bf16[3,80,768]{2,1,0:T(8,128)(2,1)S(1)} %get-tuple-element.64.refs_1_.refs_0_), channel_id=1, source_target_pairs={{0,1},{1,2},{2,3},{4,5},{5,6},{6,7},{8,9},{9,10},{10,11},{12,13},{... | collective-permute-start | bytes 1105928 | tf_op jit(solution)/shard_map/ppermute | solution.py:32
  146.6 1.3 collective-permute-start.28
  148.2 6.3 %collective-permute-start.27 = (bf16[3,80,768]{2,1,0:T(8,128)(2,1)S(1)}, bf16[3,80,768]{2,1,0:T(8,128)(2,1)S(1)}, u32[]{:S(2)}, u32[]{:S(2)}) collective-permute-start(bf16[3,80,768]{2,1,0:T(8,128)(2,1)S(1)} %get-tuple-element.59.refs_1_.refs_0_), channel_id=1, source_target_pairs={{0,1},{1,2},{2,3},{4,5},{5,6},{6,7},{8,9},{9,10},{10,11},{12,13},{... | collective-permute-start | bytes 1105928 | tf_op jit(solution)/shard_map/ppermute | solution.py:32
  154.6 1.3 collective-permute-start.16
  155.9 6.0 %collective-permute-start.15 = (bf16[3,80,768]{2,1,0:T(8,128)(2,1)S(1)}, bf16[3,80,768]{2,1,0:T(8,128)(2,1)S(1)}, u32[]{:S(2)}, u32[]{:S(2)}) collective-permute-start(bf16[3,80,768]{2,1,0:T(8,128)(2,1)S(1)} %get-tuple-element.54.refs_0_), channel_id=1, source_target_pairs={{0,1},{1,2},{2,3},{4,5},{5,6},{6,7},{8,9},{9,10},{10,11},{12,13},{... | collective-permute-start | bytes 1105928 | tf_op jit(solution)/shard_map/ppermute | solution.py:32
  162.6 1.3 collective-permute-start.53
  166.1 4.3 %collective-permute-done.27.refs_2_.refs_1_ = bf16[3,80,768]{2,1,0:T(8,128)(2,1)S(1)} collective-permute-done((bf16[3,80,768]{2,1,0:T(8,128)(2,1)S(1)}, bf16[3,80,768]{2,1,0:T(8,128)(2,1)S(1)}, u32[]{:S(2)}, u32[]{:S(2)}) %collective-permute-start.27) | collective-permute-done | bytes 368672 | tf_op jit(solution)/shard_map/ppermute | solution.py:32
  171.6 1.3 collective-permute-start.29
  172.9 4.7 %collective-permute-done.15.refs_1_ = bf16[3,80,768]{2,1,0:T(8,128)(2,1)S(1)} collective-permute-done((bf16[3,80,768]{2,1,0:T(8,128)(2,1)S(1)}, bf16[3,80,768]{2,1,0:T(8,128)(2,1)S(1)}, u32[]{:S(2)}, u32[]{:S(2)}) %collective-permute-start.15) | collective-permute-done | bytes 368672 | tf_op jit(solution)/shard_map/ppermute | solution.py:32
  179.7 1.4 collective-permute-start.19
  181.8 1.4 collective-permute-start.31
  183.2 2.7 collective-permute-done.41.refs_5_.refs_4_
  186.6 7.2 %collective-permute-done.29.refs_5_.refs_4_ = bf16[3,80,768]{2,1,0:T(8,128)(2,1)S(1)} collective-permute-done((bf16[3,80,768]{2,1,0:T(8,128)(2,1)S(1)}, bf16[3,80,768]{2,1,0:T(8,128)(2,1)S(1)}, u32[]{:S(2)}, u32[]{:S(2)}) %collective-permute-start.29) | collective-permute-done | bytes 368672 | tf_op jit(solution)/shard_map/ppermute | solution.py:32
  193.8 1.3 collective-permute-start.30
  195.1 6.7 %collective-permute-done.17.refs_4_ = bf16[3,80,768]{2,1,0:T(8,128)(2,1)} collective-permute-done((bf16[3,80,768]{2,1,0:T(8,128)(2,1)S(1)}, bf16[3,80,768]{2,1,0:T(8,128)(2,1)}, u32[]{:S(2)}, u32[]{:S(2)}) %collective-permute-start.17) | collective-permute-done | bytes 368672 | tf_op jit(solution)/shard_map/ppermute | solution.py:32
  201.8 1.3 collective-permute-start.18
  203.1 1.4 collective-permute-start.20
  204.5 1.4 collective-permute-start.32
  206.0 1.3 collective-permute-start.54
  207.3 2.4 collective-permute-done.30.refs_3_.refs_2_
  210.4 7.2 %collective-permute-done.18.refs_2_ = bf16[3,80,768]{2,1,0:T(8,128)(2,1)} collective-permute-done((bf16[3,80,768]{2,1,0:T(8,128)(2,1)}, bf16[3,80,768]{2,1,0:T(8,128)(2,1)}, u32[]{:S(2)}, u32[]{:S(2)}) %collective-permute-start.18) | collective-permute-done | bytes 368672 | tf_op jit(solution)/shard_map/ppermute | solution.py:32
  217.6 1.3 collective-permute-start.42
  220.1 45.1 %all-gather.1 = f32[16,4,80]{2,1,0:T(4,128)S(1)} all-gather(f32[1,4,80]{2,1,0:T(4,128)S(1)} %bitcast.58), channel_id=2, replica_groups=mesh['group'=2,'expert'=4,'dp'=4] {'expert','dp'}, dimensions={0}, use_global_device_ids=true | all-gather | bytes 21760 | tf_op jit(solution)/shard_map/all_gather | solution.py:332
  268.1 4.4 %shard_map.120.refs_0_ = f32[4,2,128,512]{3,2,1,0:T(8,128)S(1)} custom-call(s32[3]{0:T(128)S(1)} %pad_add_fusion.scal, f32[4,16,128]{2,1,0:T(8,128)S(1)} %pad_maximum_fusion.2.w_ref, bf16[3,80,768]{2,1,0:T(8,128)(2,1)S(1)} %copy-done.3, bf16[3,80,768]{2,1,0:T(8,128)(2,1)S(1)} %copy-done.9, bf16[3,80,768]{2,1,0:T(8,128)(2,1)} %collective-permute-done.18.refs_2_, ...), custom_call_target="tpu_custom_call" | custom-call | flops 754974720 | bytes 6782976 | tf_op jit(solution)/shard_map/pallas_call | solution.py:283
  272.6 1.3 copy-done.1
  273.9 5.1 %shard_map.123.refs_0_ = f32[4,2,128,512]{3,2,1,0:T(8,128)S(1)} custom-call(s32[3]{0:T(128)S(1)} %pad_add_fusion.scal, f32[4,16,128]{2,1,0:T(8,128)S(1)} %pad_maximum_fusion.2.w_ref, f32[4,2,128,512]{3,2,1,0:T(8,128)} %copy-done.1, bf16[3,80,768]{2,1,0:T(8,128)(2,1)S(1)} %get-tuple-element.59.refs_1_.refs_0_, ...), custom_call_target="tpu_custom_call" | custom-call | flops 754974720 | bytes 6782976 | tf_op jit(solution)/shard_map/pallas_call | solution.py:283
  279.0 1.3 copy-done
  280.4 4.9 %shard_map.126.refs_0_ = f32[4,2,128,512]{3,2,1,0:T(8,128)S(1)} custom-call(s32[3]{0:T(128)S(1)} %pad_add_fusion.scal, f32[4,16,128]{2,1,0:T(8,128)S(1)} %pad_maximum_fusion.2.w_ref, f32[4,2,128,512]{3,2,1,0:T(8,128)} %copy-done, bf16[3,80,768]{2,1,0:T(8,128)(2,1)S(1)} %get-tuple-element.64.refs_1_.refs_0_, ...), custom_call_target="tpu_custom_call" | custom-call | flops 754974720 | bytes 6782976 | tf_op jit(solution)/shard_map/pallas_call | solution.py:283
  285.4 4.1 %shard_map.129 = bf16[4,2,128,512]{3,2,1,0:T(8,128)(2,1)S(1)} custom-call(s32[3]{0:T(128)S(1)} %pad_add_fusion.scal, f32[4,16,128]{2,1,0:T(8,128)S(1)} %pad_maximum_fusion.2.w_ref, f32[4,2,128,512]{3,2,1,0:T(8,128)S(1)} %shard_map.126.refs_0_, bf16[3,80,768]{2,1,0:T(8,128)(2,1)S(1)} %copy-done.12, bf16[3,80,768]{2,1,0:T(8,128)(2,1)S(1)} %copy-done.16, ...), custom_call_target="tpu_custom_call" | custom-call | flops 754974720 | bytes 6782976 | tf_op jit(solution)/shard_map/pallas_call | solution.py:283
  292.4 4.4 %shard_map.130 = (bf16[4,512,768]{2,1,0:T(8,128)(2,1)}, bf16[4,512,768]{2,1,0:T(8,128)(2,1)}, bf16[4,768,512]{2,1,0:T(8,128)(2,1)}) custom-call(s32[3]{0:T(128)S(1)} %pad_add_fusion.scal, bf16[320,512]{1,0:T(8,128)(2,1)S(1)} %copy-done.34, bf16[320,512]{1,0:T(8,128)(2,1)S(1)} %copy-done.36, bf16[3,80,768]{2,1,0:T(8,128)(2,1)S(1)} %copy-done.4, ...), custom_call_target="tpu_custom_call" | custom-call | flops 754974720 | bytes 6291456 | tf_op jit(solution)/shard_map/pallas_call | solution.py:306
  296.8 4.4 %shard_map.131 = (bf16[4,512,768]{2,1,0:T(8,128)(2,1)}, bf16[4,512,768]{2,1,0:T(8,128)(2,1)}, bf16[4,768,512]{2,1,0:T(8,128)(2,1)}) custom-call(s32[3]{0:T(128)S(1)} %pad_add_fusion.scal, bf16[320,512]{1,0:T(8,128)(2,1)S(1)} %copy-done.30, bf16[320,512]{1,0:T(8,128)(2,1)S(1)} %copy-done.32, ...), custom_call_target="tpu_custom_call", output_to_operand_aliasing={{0}: (10, {}), {1}: (11, {}), {2}: (12, {})} | custom-call | flops 754974720 | bytes 6291456 | tf_op jit(solution)/shard_map/pallas_call | solution.py:306
  301.2 3.5 %shard_map.132 = (bf16[4,512,768]{2,1,0:T(8,128)(2,1)}, bf16[4,512,768]{2,1,0:T(8,128)(2,1)}, bf16[4,768,512]{2,1,0:T(8,128)(2,1)}) custom-call(s32[3]{0:T(128)S(1)} %pad_add_fusion.scal, bf16[320,512]{1,0:T(8,128)(2,1)S(1)} %copy-done.26, bf16[320,512]{1,0:T(8,128)(2,1)S(1)} %copy-done.28, ...), custom_call_target="tpu_custom_call", output_to_operand_aliasing={{0}: (10, {}), {1}: (11, {}), {2}: (12, {})} | custom-call | flops 754974720 | bytes 6291456 | tf_op jit(solution)/shard_map/pallas_call | solution.py:306
  304.7 3.5 %shard_map.133 = (bf16[4,512,768]{2,1,0:T(8,128)(2,1)}, bf16[4,512,768]{2,1,0:T(8,128)(2,1)}, bf16[4,768,512]{2,1,0:T(8,128)(2,1)}) custom-call(s32[3]{0:T(128)S(1)} %pad_add_fusion.scal, bf16[320,512]{1,0:T(8,128)(2,1)S(1)} %copy-done.22, bf16[320,512]{1,0:T(8,128)(2,1)S(1)} %copy-done.24, ...), custom_call_target="tpu_custom_call", output_to_operand_aliasing={{0}: (10, {}), {1}: (11, {}), {2}: (12, {})} | custom-call | flops 754974720 | bytes 6291456 | tf_op jit(solution)/shard_map/pallas_call | solution.py:306
  (179 shorter events, 34.9 us)
Async XLA Ops:
  0.6 25.8 %collective-permute-start.3 = (bf16[128,512]{1,0:T(8,128)(2,1)}, bf16[128,512]{1,0:T(8,128)(2,1)S(1)}, u32[]{:S(2)}, u32[]{:S(2)}) collective-permute-start(bf16[128,512]{1,0:T(8,128)(2,1)} %param.7), channel_id=1, source_target_pairs={{0,8},{4,12},{8,0},{12,4},{1,9},{5,13},{9,1},{13,5},{2,10},{6,14},... | collective-permute-start | bytes 393224 | tf_op jit(solution)/shard_map/ppermute | solution.py:32
  7.8 24.8 %collective-permute-start.6 = (bf16[128,512]{1,0:T(8,128)(2,1)}, bf16[128,512]{1,0:T(8,128)(2,1)S(1)}, u32[]{:S(2)}, u32[]{:S(2)}) collective-permute-start(bf16[128,512]{1,0:T(8,128)(2,1)} %param.13), channel_id=1, source_target_pairs={{0,8},{4,12},{8,0},{12,4},{1,9},{5,13},{9,1},{13,5},{2,10},{6,14},... | collective-permute-start | bytes 393224 | tf_op jit(solution)/shard_map/ppermute | solution.py:32
  14.2 6.5 %collective-permute-start = (f32[16,128]{1,0:T(8,128)S(1)}, f32[16,128]{1,0:T(8,128)S(1)}, u32[]{:S(2)}, u32[]{:S(2)}) collective-permute-start(f32[16,128]{1,0:T(8,128)S(1)} %select_reduce_fusion.2), channel_id=1, source_target_pairs={{0,8},{4,12},{8,0},{12,4},{1,9},{5,13},{9,1},{13,5},{2,10},{6,14},... | collective-permute-start | bytes 24584 | tf_op jit(solution)/shard_map/ppermute | solution.py:32
  16.2 16.1 %collective-permute-start.1 = (f32[16,128]{1,0:T(8,128)S(1)}, f32[16,128]{1,0:T(8,128)S(1)}, u32[]{:S(2)}, u32[]{:S(2)}) collective-permute-start(f32[16,128]{1,0:T(8,128)S(1)} %select_reduce_fusion.2), channel_id=1, source_target_pairs={{0,4},{4,0},{8,12},{12,8},{1,5},{5,1},{9,13},{13,9},{2,6},{6,2},{1... | collective-permute-start | bytes 24584 | tf_op jit(solution)/shard_map/ppermute | solution.py:32
  16.2 22.0 %collective-permute-start.4 = (bf16[128,512]{1,0:T(8,128)(2,1)}, bf16[128,512]{1,0:T(8,128)(2,1)S(1)}, u32[]{:S(2)}, u32[]{:S(2)}) collective-permute-start(bf16[128,512]{1,0:T(8,128)(2,1)} %param.7), channel_id=1, source_target_pairs={{0,4},{4,0},{8,12},{12,8},{1,5},{5,1},{9,13},{13,9},{2,6},{6,2},{1... | collective-permute-start | bytes 393224 | tf_op jit(solution)/shard_map/ppermute | solution.py:32
  20.7 17.4 %collective-permute-start.2 = (f32[16,128]{1,0:T(8,128)S(1)}, f32[16,128]{1,0:T(8,128)S(1)}, u32[]{:S(2)}, u32[]{:S(2)}) collective-permute-start(f32[16,128]{1,0:T(8,128)S(1)} %collective-permute-done), channel_id=1, source_target_pairs={{0,4},{4,0},{8,12},{12,8},{1,5},{5,1},{9,13},{13,9},{2,6},{6,2},{1... | collective-permute-start | bytes 24584 | tf_op jit(solution)/shard_map/ppermute | solution.py:32
  26.4 11.7 %collective-permute-start.5 = (bf16[128,512]{1,0:T(8,128)(2,1)S(1)}, bf16[128,512]{1,0:T(8,128)(2,1)S(1)}, u32[]{:S(2)}, u32[]{:S(2)}) collective-permute-start(bf16[128,512]{1,0:T(8,128)(2,1)S(1)} %collective-permute-done.3), channel_id=1, source_target_pairs={{0,4},{4,0},{8,12},{12,8},{1,5},{5,1},{9,13},{13,9},{2,6},{6,2},{1... | collective-permute-start | bytes 393224 | tf_op jit(solution)/shard_map/ppermute | solution.py:32
  32.2 6.9 %collective-permute-start.7 = (bf16[128,512]{1,0:T(8,128)(2,1)}, bf16[128,512]{1,0:T(8,128)(2,1)S(1)}, u32[]{:S(2)}, u32[]{:S(2)}) collective-permute-start(bf16[128,512]{1,0:T(8,128)(2,1)} %param.13), channel_id=1, source_target_pairs={{0,4},{4,0},{8,12},{12,8},{1,5},{5,1},{9,13},{13,9},{2,6},{6,2},{1... | collective-permute-start | bytes 393224 | tf_op jit(solution)/shard_map/ppermute | solution.py:32
  32.6 6.7 %collective-permute-start.8 = (bf16[128,512]{1,0:T(8,128)(2,1)S(1)}, bf16[128,512]{1,0:T(8,128)(2,1)S(1)}, u32[]{:S(2)}, u32[]{:S(2)}) collective-permute-start(bf16[128,512]{1,0:T(8,128)(2,1)S(1)} %collective-permute-done.6), channel_id=1, source_target_pairs={{0,4},{4,0},{8,12},{12,8},{1,5},{5,1},{9,13},{13,9},{2,6},{6,2},{1... | collective-permute-start | bytes 393224 | tf_op jit(solution)/shard_map/ppermute | solution.py:32
  44.8 20.5 %collective-permute-start.48 = (bf16[3,80,768]{2,1,0:T(8,128)(2,1)S(1)}, bf16[3,80,768]{2,1,0:T(8,128)(2,1)S(1)}, u32[]{:S(2)}, u32[]{:S(2)}) collective-permute-start(bf16[3,80,768]{2,1,0:T(8,128)(2,1)S(1)} %get-tuple-element.66), channel_id=1, source_target_pairs={{3,2},{7,6},{11,10},{15,14},{19,18},{23,22},{27,26},{31,30}} | collective-permute-start | bytes 1105928 | tf_op jit(solution)/shard_map/ppermute | solution.py:32
  45.5 21.2 %collective-permute-start.45 = (bf16[3,80,768]{2,1,0:T(8,128)(2,1)S(1)}, bf16[3,80,768]{2,1,0:T(8,128)(2,1)S(1)}, u32[]{:S(2)}, u32[]{:S(2)}) collective-permute-start(bf16[3,80,768]{2,1,0:T(8,128)(2,1)S(1)} %get-tuple-element.68), channel_id=1, source_target_pairs={{0,1},{4,5},{8,9},{12,13},{16,17},{20,21},{24,25},{28,29}} | collective-permute-start | bytes 1105928 | tf_op jit(solution)/shard_map/ppermute | solution.py:32
  53.6 13.9 %collective-permute-start.36 = (bf16[3,80,768]{2,1,0:T(8,128)(2,1)S(1)}, bf16[3,80,768]{2,1,0:T(8,128)(2,1)S(1)}, u32[]{:S(2)}, u32[]{:S(2)}) collective-permute-start(bf16[3,80,768]{2,1,0:T(8,128)(2,1)S(1)} %get-tuple-element.61), channel_id=1, source_target_pairs={{3,2},{7,6},{11,10},{15,14},{19,18},{23,22},{27,26},{31,30}} | collective-permute-start | bytes 1105928 | tf_op jit(solution)/shard_map/ppermute | solution.py:32
  54.3 14.6 %collective-permute-start.33 = (bf16[3,80,768]{2,1,0:T(8,128)(2,1)S(1)}, bf16[3,80,768]{2,1,0:T(8,128)(2,1)S(1)}, u32[]{:S(2)}, u32[]{:S(2)}) collective-permute-start(bf16[3,80,768]{2,1,0:T(8,128)(2,1)S(1)} %get-tuple-element.63), channel_id=1, source_target_pairs={{0,1},{4,5},{8,9},{12,13},{16,17},{20,21},{24,25},{28,29}} | collective-permute-start | bytes 1105928 | tf_op jit(solution)/shard_map/ppermute | solution.py:32
  60.8 8.9 %collective-permute-start.24 = (bf16[3,80,768]{2,1,0:T(8,128)(2,1)S(1)}, bf16[3,80,768]{2,1,0:T(8,128)(2,1)S(1)}, u32[]{:S(2)}, u32[]{:S(2)}) collective-permute-start(bf16[3,80,768]{2,1,0:T(8,128)(2,1)S(1)} %get-tuple-element.56), channel_id=1, source_target_pairs={{3,2},{7,6},{11,10},{15,14},{19,18},{23,22},{27,26},{31,30}} | collective-permute-start | bytes 1105928 | tf_op jit(solution)/shard_map/ppermute | solution.py:32
  65.3 19.0 %copy-start.33 = (bf16[320,512]{1,0:T(8,128)(2,1)}, bf16[320,512]{1,0:T(8,128)(2,1)S(1)}, u32[]{:S(2)}) copy-start(bf16[320,512]{1,0:T(8,128)(2,1)S(1)} %get-tuple-element.76.in_ref) | copy-start | bytes 983044
  65.3 19.0 %copy-start.35 = (bf16[320,512]{1,0:T(8,128)(2,1)}, bf16[320,512]{1,0:T(8,128)(2,1)S(1)}, u32[]{:S(2)}) copy-start(bf16[320,512]{1,0:T(8,128)(2,1)S(1)} %get-tuple-element.77.cot_ref) | copy-start | bytes 983044
  65.3 10.2 %collective-permute-start.21 = (bf16[3,80,768]{2,1,0:T(8,128)(2,1)S(1)}, bf16[3,80,768]{2,1,0:T(8,128)(2,1)S(1)}, u32[]{:S(2)}, u32[]{:S(2)}) collective-permute-start(bf16[3,80,768]{2,1,0:T(8,128)(2,1)S(1)} %get-tuple-element.58), channel_id=1, source_target_pairs={{0,1},{4,5},{8,9},{12,13},{16,17},{20,21},{24,25},{28,29}} | collective-permute-start | bytes 1105928 | tf_op jit(solution)/shard_map/ppermute | solution.py:32
  66.7 9.7 %collective-permute-start.12 = (bf16[3,80,768]{2,1,0:T(8,128)(2,1)S(1)}, bf16[3,80,768]{2,1,0:T(8,128)(2,1)S(1)}, u32[]{:S(2)}, u32[]{:S(2)}) collective-permute-start(bf16[3,80,768]{2,1,0:T(8,128)(2,1)S(1)} %get-tuple-element.51), channel_id=1, source_target_pairs={{3,2},{7,6},{11,10},{15,14},{19,18},{23,22},{27,26},{31,30}} | collective-permute-start | bytes 1105928 | tf_op jit(solution)/shard_map/ppermute | solution.py:32
  67.5 15.9 %collective-permute-start.9 = (bf16[3,80,768]{2,1,0:T(8,128)(2,1)S(1)}, bf16[3,80,768]{2,1,0:T(8,128)(2,1)S(1)}, u32[]{:S(2)}, u32[]{:S(2)}) collective-permute-start(bf16[3,80,768]{2,1,0:T(8,128)(2,1)S(1)} %get-tuple-element.53), channel_id=1, source_target_pairs={{0,1},{4,5},{8,9},{12,13},{16,17},{20,21},{24,25},{28,29}} | collective-permute-start | bytes 1105928 | tf_op jit(solution)/shard_map/ppermute | solution.py:32
  68.9 15.4 %collective-permute-start.49 = (bf16[3,80,768]{2,1,0:T(8,128)(2,1)S(1)}, bf16[3,80,768]{2,1,0:T(8,128)(2,1)S(1)}, u32[]{:S(2)}, u32[]{:S(2)}) collective-permute-start(bf16[3,80,768]{2,1,0:T(8,128)(2,1)S(1)} %get-tuple-element.94), channel_id=1, source_target_pairs={{3,2},{2,1},{7,6},{6,5},{11,10},{10,9},{15,14},{14,13},{19,18},{18... | collective-permute-start | bytes 1105928 | tf_op jit(solution)/shard_map/ppermute | solution.py:32
  69.7 21.6 %collective-permute-start.46 = (bf16[3,80,768]{2,1,0:T(8,128)(2,1)S(1)}, bf16[3,80,768]{2,1,0:T(8,128)(2,1)S(1)}, u32[]{:S(2)}, u32[]{:S(2)}) collective-permute-start(bf16[3,80,768]{2,1,0:T(8,128)(2,1)S(1)} %get-tuple-element.95), channel_id=1, source_target_pairs={{0,1},{1,2},{4,5},{5,6},{8,9},{9,10},{12,13},{13,14},{16,17},{17,1... | collective-permute-start | bytes 1105928 | tf_op jit(solution)/shard_map/ppermute | solution.py:32
  75.5 16.6 %collective-permute-start.37 = (bf16[3,80,768]{2,1,0:T(8,128)(2,1)S(1)}, bf16[3,80,768]{2,1,0:T(8,128)(2,1)S(1)}, u32[]{:S(2)}, u32[]{:S(2)}) collective-permute-start(bf16[3,80,768]{2,1,0:T(8,128)(2,1)S(1)} %get-tuple-element.96), channel_id=1, source_target_pairs={{3,2},{2,1},{7,6},{6,5},{11,10},{10,9},{15,14},{14,13},{19,18},{18... | collective-permute-start | bytes 1105928 | tf_op jit(solution)/shard_map/ppermute | solution.py:32
  76.4 22.8 %collective-permute-start.34 = (bf16[3,80,768]{2,1,0:T(8,128)(2,1)S(1)}, bf16[3,80,768]{2,1,0:T(8,128)(2,1)S(1)}, u32[]{:S(2)}, u32[]{:S(2)}) collective-permute-start(bf16[3,80,768]{2,1,0:T(8,128)(2,1)S(1)} %get-tuple-element.97), channel_id=1, source_target_pairs={{0,1},{1,2},{4,5},{5,6},{8,9},{9,10},{12,13},{13,14},{16,17},{17,1... | collective-permute-start | bytes 1105928 | tf_op jit(solution)/shard_map/ppermute | solution.py:32
  83.4 17.2 %collective-permute-start.25 = (bf16[3,80,768]{2,1,0:T(8,128)(2,1)S(1)}, bf16[3,80,768]{2,1,0:T(8,128)(2,1)S(1)}, u32[]{:S(2)}, u32[]{:S(2)}) collective-permute-start(bf16[3,80,768]{2,1,0:T(8,128)(2,1)S(1)} %get-tuple-element.98), channel_id=1, source_target_pairs={{3,2},{2,1},{7,6},{6,5},{11,10},{10,9},{15,14},{14,13},{19,18},{18... | collective-permute-start | bytes 1105928 | tf_op jit(solution)/shard_map/ppermute | solution.py:32
  84.3 22.8 %collective-permute-start.22 = (bf16[3,80,768]{2,1,0:T(8,128)(2,1)S(1)}, bf16[3,80,768]{2,1,0:T(8,128)(2,1)S(1)}, u32[]{:S(2)}, u32[]{:S(2)}) collective-permute-start(bf16[3,80,768]{2,1,0:T(8,128)(2,1)S(1)} %get-tuple-element.99), channel_id=1, source_target_pairs={{0,1},{1,2},{4,5},{5,6},{8,9},{9,10},{12,13},{13,14},{16,17},{17,1... | collective-permute-start | bytes 1105928 | tf_op jit(solution)/shard_map/ppermute | solution.py:32
  91.3 17.2 %collective-permute-start.13 = (bf16[3,80,768]{2,1,0:T(8,128)(2,1)S(1)}, bf16[3,80,768]{2,1,0:T(8,128)(2,1)S(1)}, u32[]{:S(2)}, u32[]{:S(2)}) collective-permute-start(bf16[3,80,768]{2,1,0:T(8,128)(2,1)S(1)} %get-tuple-element.100), channel_id=1, source_target_pairs={{3,2},{2,1},{7,6},{6,5},{11,10},{10,9},{15,14},{14,13},{19,18},{18... | collective-permute-start | bytes 1105928 | tf_op jit(solution)/shard_map/ppermute | solution.py:32
  92.1 22.9 %collective-permute-start.10 = (bf16[3,80,768]{2,1,0:T(8,128)(2,1)S(1)}, bf16[3,80,768]{2,1,0:T(8,128)(2,1)S(1)}, u32[]{:S(2)}, u32[]{:S(2)}) collective-permute-start(bf16[3,80,768]{2,1,0:T(8,128)(2,1)S(1)} %get-tuple-element.101), channel_id=1, source_target_pairs={{0,1},{1,2},{4,5},{5,6},{8,9},{9,10},{12,13},{13,14},{16,17},{17,1... | collective-permute-start | bytes 1105928 | tf_op jit(solution)/shard_map/ppermute | solution.py:32
  99.2 17.1 %collective-permute-start.50 = (bf16[3,80,768]{2,1,0:T(8,128)(2,1)S(1)}, bf16[3,80,768]{2,1,0:T(8,128)(2,1)S(1)}, u32[]{:S(2)}, u32[]{:S(2)}) collective-permute-start(bf16[3,80,768]{2,1,0:T(8,128)(2,1)S(1)} %add_convert_fusion.1), channel_id=1, source_target_pairs={{3,2},{2,1},{1,0},{7,6},{6,5},{5,4},{11,10},{10,9},{9,8},{15,14},{... | collective-permute-start | bytes 1105928 | tf_op jit(solution)/shard_map/ppermute | solution.py:32
  100.6 22.3 %collective-permute-start.47 = (bf16[3,80,768]{2,1,0:T(8,128)(2,1)S(1)}, bf16[3,80,768]{2,1,0:T(8,128)(2,1)S(1)}, u32[]{:S(2)}, u32[]{:S(2)}) collective-permute-start(bf16[3,80,768]{2,1,0:T(8,128)(2,1)S(1)} %add_convert_fusion.2), channel_id=1, source_target_pairs={{0,1},{1,2},{2,3},{4,5},{5,6},{6,7},{8,9},{9,10},{10,11},{12,13},{... | collective-permute-start | bytes 1105928 | tf_op jit(solution)/shard_map/ppermute | solution.py:32
  107.1 17.2 %collective-permute-start.38 = (bf16[3,80,768]{2,1,0:T(8,128)(2,1)S(1)}, bf16[3,80,768]{2,1,0:T(8,128)(2,1)S(1)}, u32[]{:S(2)}, u32[]{:S(2)}) collective-permute-start(bf16[3,80,768]{2,1,0:T(8,128)(2,1)S(1)} %add_convert_fusion.3), channel_id=1, source_target_pairs={{3,2},{2,1},{1,0},{7,6},{6,5},{5,4},{11,10},{10,9},{9,8},{15,14},{... | collective-permute-start | bytes 1105928 | tf_op jit(solution)/shard_map/ppermute | solution.py:32
  108.5 22.3 %collective-permute-start.35 = (bf16[3,80,768]{2,1,0:T(8,128)(2,1)S(1)}, bf16[3,80,768]{2,1,0:T(8,128)(2,1)S(1)}, u32[]{:S(2)}, u32[]{:S(2)}) collective-permute-start(bf16[3,80,768]{2,1,0:T(8,128)(2,1)S(1)} %add_convert_fusion.4), channel_id=1, source_target_pairs={{0,1},{1,2},{2,3},{4,5},{5,6},{6,7},{8,9},{9,10},{10,11},{12,13},{... | collective-permute-start | bytes 1105928 | tf_op jit(solution)/shard_map/ppermute | solution.py:32
  115.0 17.4 %collective-permute-start.26 = (bf16[3,80,768]{2,1,0:T(8,128)(2,1)S(1)}, bf16[3,80,768]{2,1,0:T(8,128)(2,1)S(1)}, u32[]{:S(2)}, u32[]{:S(2)}) collective-permute-start(bf16[3,80,768]{2,1,0:T(8,128)(2,1)S(1)} %add_convert_fusion.5), channel_id=1, source_target_pairs={{3,2},{2,1},{1,0},{7,6},{6,5},{5,4},{11,10},{10,9},{9,8},{15,14},{... | collective-permute-start | bytes 1105928 | tf_op jit(solution)/shard_map/ppermute | solution.py:32
  116.3 22.4 %collective-permute-start.23 = (bf16[3,80,768]{2,1,0:T(8,128)(2,1)S(1)}, bf16[3,80,768]{2,1,0:T(8,128)(2,1)S(1)}, u32[]{:S(2)}, u32[]{:S(2)}) collective-permute-start(bf16[3,80,768]{2,1,0:T(8,128)(2,1)S(1)} %add_convert_fusion.6), channel_id=1, source_target_pairs={{0,1},{1,2},{2,3},{4,5},{5,6},{6,7},{8,9},{9,10},{10,11},{12,13},{... | collective-permute-start | bytes 1105928 | tf_op jit(solution)/shard_map/ppermute | solution.py:32
  122.9 17.1 %collective-permute-start.14 = (bf16[3,80,768]{2,1,0:T(8,128)(2,1)S(1)}, bf16[3,80,768]{2,1,0:T(8,128)(2,1)S(1)}, u32[]{:S(2)}, u32[]{:S(2)}) collective-permute-start(bf16[3,80,768]{2,1,0:T(8,128)(2,1)S(1)} %add_convert_fusion.7), channel_id=1, source_target_pairs={{3,2},{2,1},{1,0},{7,6},{6,5},{5,4},{11,10},{10,9},{9,8},{15,14},{... | collective-permute-start | bytes 1105928 | tf_op jit(solution)/shard_map/ppermute | solution.py:32
  124.3 22.3 %collective-permute-start.11 = (bf16[3,80,768]{2,1,0:T(8,128)(2,1)S(1)}, bf16[3,80,768]{2,1,0:T(8,128)(2,1)S(1)}, u32[]{:S(2)}, u32[]{:S(2)}) collective-permute-start(bf16[3,80,768]{2,1,0:T(8,128)(2,1)S(1)} %add_convert_fusion.8), channel_id=1, source_target_pairs={{0,1},{1,2},{2,3},{4,5},{5,6},{6,7},{8,9},{9,10},{10,11},{12,13},{... | collective-permute-start | bytes 1105928 | tf_op jit(solution)/shard_map/ppermute | solution.py:32
  130.7 23.8 %copy-start.11 = (bf16[3,80,768]{2,1,0:T(8,128)(2,1)}, bf16[3,80,768]{2,1,0:T(8,128)(2,1)S(1)}, u32[]{:S(2)}) copy-start(bf16[3,80,768]{2,1,0:T(8,128)(2,1)S(1)} %get-tuple-element.69.refs_1_.refs_0_) | copy-start | bytes 1105924
  130.8 17.4 %collective-permute-start.52 = (bf16[3,80,768]{2,1,0:T(8,128)(2,1)S(1)}, bf16[3,80,768]{2,1,0:T(8,128)(2,1)S(1)}, u32[]{:S(2)}, u32[]{:S(2)}) collective-permute-start(bf16[3,80,768]{2,1,0:T(8,128)(2,1)S(1)} %get-tuple-element.69.refs_1_.refs_0_), channel_id=1, source_target_pairs={{3,2},{2,1},{1,0},{7,6},{6,5},{5,4},{11,10},{10,9},{9,8},{15,14},{... | collective-permute-start | bytes 1105928 | tf_op jit(solution)/shard_map/ppermute | solution.py:32
  132.4 22.1 %collective-permute-start.51 = (bf16[3,80,768]{2,1,0:T(8,128)(2,1)S(1)}, bf16[3,80,768]{2,1,0:T(8,128)(2,1)S(1)}, u32[]{:S(2)}, u32[]{:S(2)}) collective-permute-start(bf16[3,80,768]{2,1,0:T(8,128)(2,1)S(1)} %get-tuple-element.69.refs_1_.refs_0_), channel_id=1, source_target_pairs={{0,1},{1,2},{2,3},{4,5},{5,6},{6,7},{8,9},{9,10},{10,11},{12,13},{... | collective-permute-start | bytes 1105928 | tf_op jit(solution)/shard_map/ppermute | solution.py:32
  138.8 17.1 %collective-permute-start.40 = (bf16[3,80,768]{2,1,0:T(8,128)(2,1)S(1)}, bf16[3,80,768]{2,1,0:T(8,128)(2,1)S(1)}, u32[]{:S(2)}, u32[]{:S(2)}) collective-permute-start(bf16[3,80,768]{2,1,0:T(8,128)(2,1)S(1)} %get-tuple-element.64.refs_1_.refs_0_), channel_id=1, source_target_pairs={{3,2},{2,1},{1,0},{7,6},{6,5},{5,4},{11,10},{10,9},{9,8},{15,14},{... | collective-permute-start | bytes 1105928 | tf_op jit(solution)/shard_map/ppermute | solution.py:32
  140.1 22.5 %collective-permute-start.39 = (bf16[3,80,768]{2,1,0:T(8,128)(2,1)S(1)}, bf16[3,80,768]{2,1,0:T(8,128)(2,1)S(1)}, u32[]{:S(2)}, u32[]{:S(2)}) collective-permute-start(bf16[3,80,768]{2,1,0:T(8,128)(2,1)S(1)} %get-tuple-element.64.refs_1_.refs_0_), channel_id=1, source_target_pairs={{0,1},{1,2},{2,3},{4,5},{5,6},{6,7},{8,9},{9,10},{10,11},{12,13},{... | collective-permute-start | bytes 1105928 | tf_op jit(solution)/shard_map/ppermute | solution.py:32
  146.6 18.0 %collective-permute-start.28 = (bf16[3,80,768]{2,1,0:T(8,128)(2,1)S(1)}, bf16[3,80,768]{2,1,0:T(8,128)(2,1)S(1)}, u32[]{:S(2)}, u32[]{:S(2)}) collective-permute-start(bf16[3,80,768]{2,1,0:T(8,128)(2,1)S(1)} %get-tuple-element.59.refs_1_.refs_0_), channel_id=1, source_target_pairs={{3,2},{2,1},{1,0},{7,6},{6,5},{5,4},{11,10},{10,9},{9,8},{15,14},{... | collective-permute-start | bytes 1105928 | tf_op jit(solution)/shard_map/ppermute | solution.py:32
  148.2 22.1 %collective-permute-start.27 = (bf16[3,80,768]{2,1,0:T(8,128)(2,1)S(1)}, bf16[3,80,768]{2,1,0:T(8,128)(2,1)S(1)}, u32[]{:S(2)}, u32[]{:S(2)}) collective-permute-start(bf16[3,80,768]{2,1,0:T(8,128)(2,1)S(1)} %get-tuple-element.59.refs_1_.refs_0_), channel_id=1, source_target_pairs={{0,1},{1,2},{2,3},{4,5},{5,6},{6,7},{8,9},{9,10},{10,11},{12,13},{... | collective-permute-start | bytes 1105928 | tf_op jit(solution)/shard_map/ppermute | solution.py:32
  154.6 17.1 %collective-permute-start.16 = (bf16[3,80,768]{2,1,0:T(8,128)(2,1)S(1)}, bf16[3,80,768]{2,1,0:T(8,128)(2,1)S(1)}, u32[]{:S(2)}, u32[]{:S(2)}) collective-permute-start(bf16[3,80,768]{2,1,0:T(8,128)(2,1)S(1)} %get-tuple-element.54.refs_0_), channel_id=1, source_target_pairs={{3,2},{2,1},{1,0},{7,6},{6,5},{5,4},{11,10},{10,9},{9,8},{15,14},{... | collective-permute-start | bytes 1105928 | tf_op jit(solution)/shard_map/ppermute | solution.py:32
  155.9 21.8 %collective-permute-start.15 = (bf16[3,80,768]{2,1,0:T(8,128)(2,1)S(1)}, bf16[3,80,768]{2,1,0:T(8,128)(2,1)S(1)}, u32[]{:S(2)}, u32[]{:S(2)}) collective-permute-start(bf16[3,80,768]{2,1,0:T(8,128)(2,1)S(1)} %get-tuple-element.54.refs_0_), channel_id=1, source_target_pairs={{0,1},{1,2},{2,3},{4,5},{5,6},{6,7},{8,9},{9,10},{10,11},{12,13},{... | collective-permute-start | bytes 1105928 | tf_op jit(solution)/shard_map/ppermute | solution.py:32
  162.6 17.1 %collective-permute-start.53 = (bf16[3,80,768]{2,1,0:T(8,128)(2,1)S(1)}, bf16[3,80,768]{2,1,0:T(8,128)(2,1)S(1)}, u32[]{:S(2)}, u32[]{:S(2)}) collective-permute-start(bf16[3,80,768]{2,1,0:T(8,128)(2,1)S(1)} %collective-permute-done.52.refs_7_.refs_6_), channel_id=1, source_target_pairs={{2,1},{1,0},{6,5},{5,4},{10,9},{9,8},{14,13},{13,12},{18,17},{17,1... | collective-permute-start | bytes 1105928 | tf_op jit(solution)/shard_map/ppermute | solution.py:32
  164.7 17.2 %collective-permute-start.55 = (bf16[3,80,768]{2,1,0:T(8,128)(2,1)S(1)}, bf16[3,80,768]{2,1,0:T(8,128)(2,1)S(1)}, u32[]{:S(2)}, u32[]{:S(2)}) collective-permute-start(bf16[3,80,768]{2,1,0:T(8,128)(2,1)S(1)} %collective-permute-done.51.refs_2_.refs_1_), channel_id=1, source_target_pairs={{1,2},{2,3},{5,6},{6,7},{9,10},{10,11},{13,14},{14,15},{17,18},{18... | collective-permute-start | bytes 1105928 | tf_op jit(solution)/shard_map/ppermute | solution.py:32
  170.3 15.6 %collective-permute-start.41 = (bf16[3,80,768]{2,1,0:T(8,128)(2,1)S(1)}, bf16[3,80,768]{2,1,0:T(8,128)(2,1)S(1)}, u32[]{:S(2)}, u32[]{:S(2)}) collective-permute-start(bf16[3,80,768]{2,1,0:T(8,128)(2,1)S(1)} %collective-permute-done.40.refs_7_.refs_6_), channel_id=1, source_target_pairs={{2,1},{1,0},{6,5},{5,4},{10,9},{9,8},{14,13},{13,12},{18,17},{17,1... | collective-permute-start | bytes 1105928 | tf_op jit(solution)/shard_map/ppermute | solution.py:32
  171.6 22.2 %collective-permute-start.29 = (bf16[3,80,768]{2,1,0:T(8,128)(2,1)S(1)}, bf16[3,80,768]{2,1,0:T(8,128)(2,1)S(1)}, u32[]{:S(2)}, u32[]{:S(2)}) collective-permute-start(bf16[3,80,768]{2,1,0:T(8,128)(2,1)S(1)} %collective-permute-done.28.refs_7_.refs_6_), channel_id=1, source_target_pairs={{2,1},{1,0},{6,5},{5,4},{10,9},{9,8},{14,13},{13,12},{18,17},{17,1... | collective-permute-start | bytes 1105928 | tf_op jit(solution)/shard_map/ppermute | solution.py:32
  177.6 24.2 %collective-permute-start.17 = (bf16[3,80,768]{2,1,0:T(8,128)(2,1)S(1)}, bf16[3,80,768]{2,1,0:T(8,128)(2,1)}, u32[]{:S(2)}, u32[]{:S(2)}) collective-permute-start(bf16[3,80,768]{2,1,0:T(8,128)(2,1)S(1)} %collective-permute-done.16.refs_6_), channel_id=1, source_target_pairs={{2,1},{1,0},{6,5},{5,4},{10,9},{9,8},{14,13},{13,12},{18,17},{17,1... | collective-permute-start | bytes 1105928 | tf_op jit(solution)/shard_map/ppermute | solution.py:32
  179.7 24.9 %copy-start.17 = (bf16[3,80,768]{2,1,0:T(8,128)(2,1)}, bf16[3,80,768]{2,1,0:T(8,128)(2,1)S(1)}, u32[]{:S(2)}) copy-start(bf16[3,80,768]{2,1,0:T(8,128)(2,1)S(1)} %collective-permute-done.53.refs_5_.refs_4_) | copy-start | bytes 1105924
  179.7 23.4 %collective-permute-start.19 = (bf16[3,80,768]{2,1,0:T(8,128)(2,1)S(1)}, bf16[3,80,768]{2,1,0:T(8,128)(2,1)}, u32[]{:S(2)}, u32[]{:S(2)}) collective-permute-start(bf16[3,80,768]{2,1,0:T(8,128)(2,1)S(1)} %collective-permute-done.15.refs_1_), channel_id=1, source_target_pairs={{1,2},{2,3},{5,6},{6,7},{9,10},{10,11},{13,14},{14,15},{17,18},{18... | collective-permute-start | bytes 1105928 | tf_op jit(solution)/shard_map/ppermute | solution.py:32
  181.8 22.7 %copy-start.19 = (bf16[3,80,768]{2,1,0:T(8,128)(2,1)}, bf16[3,80,768]{2,1,0:T(8,128)(2,1)S(1)}, u32[]{:S(2)}) copy-start(bf16[3,80,768]{2,1,0:T(8,128)(2,1)S(1)} %collective-permute-done.55.refs_4_.refs_3_) | copy-start | bytes 1105924
  181.8 22.7 %collective-permute-start.31 = (bf16[3,80,768]{2,1,0:T(8,128)(2,1)S(1)}, bf16[3,80,768]{2,1,0:T(8,128)(2,1)}, u32[]{:S(2)}, u32[]{:S(2)}) collective-permute-start(bf16[3,80,768]{2,1,0:T(8,128)(2,1)S(1)} %collective-permute-done.27.refs_2_.refs_1_), channel_id=1, source_target_pairs={{1,2},{2,3},{5,6},{6,7},{9,10},{10,11},{13,14},{14,15},{17,18},{18... | collective-permute-start | bytes 1105928 | tf_op jit(solution)/shard_map/ppermute | solution.py:32
  185.9 20.1 %collective-permute-start.43 = (bf16[3,80,768]{2,1,0:T(8,128)(2,1)S(1)}, bf16[3,80,768]{2,1,0:T(8,128)(2,1)S(1)}, u32[]{:S(2)}, u32[]{:S(2)}) collective-permute-start(bf16[3,80,768]{2,1,0:T(8,128)(2,1)S(1)} %collective-permute-done.39.refs_2_.refs_1_), channel_id=1, source_target_pairs={{1,2},{2,3},{5,6},{6,7},{9,10},{10,11},{13,14},{14,15},{17,18},{18... | collective-permute-start | bytes 1105928 | tf_op jit(solution)/shard_map/ppermute | solution.py:32
  193.8 15.9 %collective-permute-start.30 = (bf16[3,80,768]{2,1,0:T(8,128)(2,1)S(1)}, bf16[3,80,768]{2,1,0:T(8,128)(2,1)}, u32[]{:S(2)}, u32[]{:S(2)}) collective-permute-start(bf16[3,80,768]{2,1,0:T(8,128)(2,1)S(1)} %collective-permute-done.29.refs_5_.refs_4_), channel_id=1, source_target_pairs={{1,0},{5,4},{9,8},{13,12},{17,16},{21,20},{25,24},{29,28}} | collective-permute-start | bytes 1105928 | tf_op jit(solution)/shard_map/ppermute | solution.py:32
  201.8 15.8 %collective-permute-start.18 = (bf16[3,80,768]{2,1,0:T(8,128)(2,1)}, bf16[3,80,768]{2,1,0:T(8,128)(2,1)}, u32[]{:S(2)}, u32[]{:S(2)}) collective-permute-start(bf16[3,80,768]{2,1,0:T(8,128)(2,1)} %collective-permute-done.17.refs_4_), channel_id=1, source_target_pairs={{1,0},{5,4},{9,8},{13,12},{17,16},{21,20},{25,24},{29,28}} | collective-permute-start | bytes 1105928 | tf_op jit(solution)/shard_map/ppermute | solution.py:32
  203.1 15.8 %collective-permute-start.20 = (bf16[3,80,768]{2,1,0:T(8,128)(2,1)}, bf16[3,80,768]{2,1,0:T(8,128)(2,1)}, u32[]{:S(2)}, u32[]{:S(2)}) collective-permute-start(bf16[3,80,768]{2,1,0:T(8,128)(2,1)} %collective-permute-done.19.refs_3_), channel_id=1, source_target_pairs={{2,3},{6,7},{10,11},{14,15},{18,19},{22,23},{26,27},{30,31}} | collective-permute-start | bytes 1105928 | tf_op jit(solution)/shard_map/ppermute | solution.py:32
  204.5 69.4 %collective-permute-start.32 = (bf16[3,80,768]{2,1,0:T(8,128)(2,1)}, bf16[3,80,768]{2,1,0:T(8,128)(2,1)}, u32[]{:S(2)}, u32[]{:S(2)}) collective-permute-start(bf16[3,80,768]{2,1,0:T(8,128)(2,1)} %collective-permute-done.31.refs_4_.refs_3_), channel_id=1, source_target_pairs={{2,3},{6,7},{10,11},{14,15},{18,19},{22,23},{26,27},{30,31}} | collective-permute-start | bytes 1105928 | tf_op jit(solution)/shard_map/ppermute | solution.py:32
  206.0 79.3 %collective-permute-start.54 = (bf16[3,80,768]{2,1,0:T(8,128)(2,1)}, bf16[3,80,768]{2,1,0:T(8,128)(2,1)S(1)}, u32[]{:S(2)}, u32[]{:S(2)}) collective-permute-start(bf16[3,80,768]{2,1,0:T(8,128)(2,1)} %copy-done.17), channel_id=1, source_target_pairs={{1,0},{5,4},{9,8},{13,12},{17,16},{21,20},{25,24},{29,28}} | collective-permute-start | bytes 1105928 | tf_op jit(solution)/shard_map/ppermute | solution.py:32
  209.7 75.6 %collective-permute-start.56 = (bf16[3,80,768]{2,1,0:T(8,128)(2,1)}, bf16[3,80,768]{2,1,0:T(8,128)(2,1)S(1)}, u32[]{:S(2)}, u32[]{:S(2)}) collective-permute-start(bf16[3,80,768]{2,1,0:T(8,128)(2,1)} %copy-done.19), channel_id=1, source_target_pairs={{2,3},{6,7},{10,11},{14,15},{18,19},{22,23},{26,27},{30,31}} | collective-permute-start | bytes 1105928 | tf_op jit(solution)/shard_map/ppermute | solution.py:32
  217.6 62.7 %collective-permute-start.42 = (bf16[3,80,768]{2,1,0:T(8,128)(2,1)S(1)}, bf16[3,80,768]{2,1,0:T(8,128)(2,1)S(1)}, u32[]{:S(2)}, u32[]{:S(2)}) collective-permute-start(bf16[3,80,768]{2,1,0:T(8,128)(2,1)S(1)} %collective-permute-done.41.refs_5_.refs_4_), channel_id=1, source_target_pairs={{1,0},{5,4},{9,8},{13,12},{17,16},{21,20},{25,24},{29,28}} | collective-permute-start | bytes 1105928 | tf_op jit(solution)/shard_map/ppermute | solution.py:32
  218.9 61.4 %collective-permute-start.44 = (bf16[3,80,768]{2,1,0:T(8,128)(2,1)S(1)}, bf16[3,80,768]{2,1,0:T(8,128)(2,1)S(1)}, u32[]{:S(2)}, u32[]{:S(2)}) collective-permute-start(bf16[3,80,768]{2,1,0:T(8,128)(2,1)S(1)} %collective-permute-done.43.refs_4_.refs_3_), channel_id=1, source_target_pairs={{2,3},{6,7},{10,11},{14,15},{18,19},{22,23},{26,27},{30,31}} | collective-permute-start | bytes 1105928 | tf_op jit(solution)/shard_map/ppermute | solution.py:32
  289.6 2.0 collective-permute-start.57
  291.7 16.4 %collective-permute-start.58 = (bf16[2,128,512]{2,1,0:T(8,128)(2,1)S(1)}, bf16[2,128,512]{2,1,0:T(8,128)(2,1)S(1)}, u32[]{:S(2)}, u32[]{:S(2)}) collective-permute-start(bf16[2,128,512]{2,1,0:T(8,128)(2,1)S(1)} %slice_bitcast_fusion), channel_id=1, source_target_pairs={{0,8},{4,12},{8,0},{12,4},{1,9},{5,13},{9,1},{13,5},{2,10},{6,14},... | collective-permute-start | bytes 786440 | tf_op jit(solution)/shard_map/ppermute | solution.py:32
  (34 other events, 105.3 us)

commit v2 on v1

v2 whole, which is shorter than its diff:
```python
import functools

import jax
import jax.numpy as jnp
from jax import lax
from jax.experimental import pallas as pl
from jax.experimental.pallas import tpu as pltpu
from jax.sharding import PartitionSpec as P

F32, BF16 = jnp.float32, jnp.bfloat16
VMEM_BYTES = 48 << 20


def line_pairs(n, gather, step):
    if gather:
        senders = [i for i in range(step - 1, n - 1)]
    else:
        senders = [i for i in range(0, min(step, n - 1))]
    right = [(i, i + 1) for i in senders]
    left = [(n - 1 - i, n - 2 - i) for i in senders]
    return right, left


class Line:
    def __init__(self, axis, n, stride):
        self.axis, self.n, self.stride = axis, n, stride

    def send(self, value, pairs):
        wide = [
            (a * self.stride + c, b * self.stride + c) for a, b in pairs for c in range(self.stride)
        ]
        return lax.ppermute(value, self.axis, wide)

    def gather(self, own):
        n = self.n
        if n == 2:
            both = self.send(own, [(0, 1), (1, 0)])
            return [(both, both)]
        right, left, rights, lefts = own, own, [], []
        for step in range(1, n):
            pairs_r, pairs_l = line_pairs(n, True, step)
            right, left = self.send(right, pairs_r), self.send(left, pairs_l)
            rights.append(right)
            lefts.append(left)
        return [(rights[q - 1], lefts[n - q - 1]) for q in range(1, n)]

    def scatter(self, parts, add):
        n = self.n
        if n == 2:
            return self.send(parts[1], [(0, 1), (1, 0)]), None
        right, left = parts[1], parts[n - 1]
        for step in range(1, n):
            pairs_r, pairs_l = line_pairs(n, False, step)
            right, left = self.send(right, pairs_r), self.send(left, pairs_l)
            if step < n - 1:
                right, left = add(parts[step + 1], right), add(parts[n - 1 - step], left)
        return right, left


def add_rounded(a, b):
    return (a.astype(F32) + b.astype(F32)).astype(BF16)


def dot(a, b, dims=((1,), (0,))):
    return lax.dot_general(a, b, (dims, ((), ())), preferred_element_type=F32)


def routing(scal, w_refs, expert, rows):
    n = len(w_refs)
    experts_all, tokens = w_refs[0].shape
    ids = lax.broadcasted_iota(jnp.int32, (experts_all, tokens), 0)
    which = scal[2 * n] + expert
    weights = jnp.concatenate(
        [jnp.sum(jnp.where(ids == which, w[...], 0.0), axis=0, keepdims=True) for w in w_refs],
        axis=0,
    )
    chosen = weights > 0.0
    earlier = lax.broadcasted_iota(jnp.int32, (tokens, tokens), 0) < lax.broadcasted_iota(
        jnp.int32, (tokens, tokens), 1
    )
    slots = dot(chosen.astype(F32).astype(BF16), earlier.astype(F32).astype(BF16))
    slots = jnp.where(chosen, slots, -1.0).astype(jnp.int32)
    row = lax.broadcasted_iota(jnp.int32, (rows, tokens), 0)
    return [(scal[k], weights[k : k + 1], row == slots[k : k + 1]) for k in range(n)]


def span_of(position, rows):
    return pl.ds(pl.multiple_of(position * rows, rows), rows)


def pre_kernel(n, expert, deps, scal, *refs):
    refs = refs[deps:]
    w_refs, packs, refs = refs[:n], refs[n : 2 * n], refs[2 * n :]
    gw, uw, dw, in_ref, cot_ref, *outs = refs
    rows = in_ref.shape[0] // n
    half = pl.program_id(0)

    @pl.when(half == 0)
    def _():
        for k, (position, weight, hit) in enumerate(routing(scal, w_refs, expert, rows)):
            pick = hit.astype(F32).astype(BF16)
            span = span_of(position, rows)
            in_ref[span, :] = dot(pick, packs[k][0]).astype(BF16)
            scale = jnp.sum(jnp.where(hit, weight, 0.0), axis=1, keepdims=True)
            cot_ref[span, :] = (dot(pick, packs[k][1]) * scale).astype(BF16)

    gate = dot(in_ref[...], gw[0]).astype(BF16)
    up = dot(in_ref[...], uw[0]).astype(BF16)
    back = dot(cot_ref[...], dw[0], ((1,), (1,))).astype(BF16)
    for h in range(2):

        @pl.when(half == h)
        def _():
            for p in range(n):
                for k, value in enumerate((gate, up, back)):
                    outs[h * n + p][k] = value[p * rows : (p + 1) * rows]


def mid_kernel(deps, *refs):
    own, right, left, out, product = refs[deps:]
    total = own[...].astype(F32) + right[...].astype(F32) + left[...].astype(F32)
    gate, up, back = total[0], total[1], total[2]
    sig = jax.nn.sigmoid(gate)
    hidden = (gate * sig * up).astype(BF16)
    delta = back.astype(BF16).astype(F32)
    out[0] = hidden
    out[1] = (delta * up * sig * (1.0 + gate * (1.0 - sig))).astype(BF16)
    out[2] = (delta * (gate * sig)).astype(BF16)
    prod = hidden.astype(F32) * back
    lanes = product.shape[1]
    acc = prod[:, 0:lanes]
    for k in range(1, prod.shape[1] // lanes):
        acc = acc + prod[:, k * lanes : (k + 1) * lanes]
    product[...] = acc


def step_kernel(deps, select, add, scal, *refs):
    refs = list(refs[deps:])
    ins, outs = refs[: 2 * (select + add)], refs[2 * (select + add) :]
    if select:
        a, b, out = ins[0], ins[1], outs[0]
        out[...] = jnp.where(scal[scal.shape[0] - 1] > 0, a[...], b[...])
    if add:
        for k in range(add):
            a, b = ins[2 * (select + k)], ins[2 * (select + k) + 1]
            outs[select + k][...] = (a[...].astype(F32) + b[...].astype(F32)).astype(BF16)


def load_rows(scal, n, which, pieces):
    values = [pieces[0][which]]
    for q, pair in enumerate(pieces[1:], 1):
        if len(pair) == 1:
            values.append(pair[0][which])
        else:
            values.append(jnp.where(scal[n + q] > 0, pair[0][which], pair[1][which]))
    return jnp.concatenate(values, axis=0)


def split_pieces(refs, sizes):
    halves, at = [], 0
    for _ in range(2):
        pieces = [refs[at]]
        at += 1
        for size in sizes:
            pieces.append(refs[at : at + size])
            at += size
        halves.append(pieces)
    return halves, refs[at:]


def out_kernel(n, expert, has_prev, sizes, scal, *refs):
    w_refs, refs = refs[:n], refs[n:]
    if has_prev:
        prev, refs = refs[:2], refs[2:]
    halves, refs = split_pieces(refs, sizes)
    gw, uw, dw, near, far, token, eo, idl = refs
    step = pl.program_id(0)

    for h in range(2):

        @pl.when(step == h)
        def _():
            layer = dot(load_rows(scal, n, 0, halves[h]), dw[0])
            back = dot(load_rows(scal, n, 1, halves[h]), gw[0], ((1,), (1,))) + dot(
                load_rows(scal, n, 2, halves[h]), uw[0], ((1,), (1,))
            )
            eo[...] = layer if h == 0 else eo[...] + layer
            idl[...] = back if h == 0 else idl[...] + back

    @pl.when(step == 1)
    def _():
        rows = eo.shape[0] // n
        for k, (position, weight, hit) in enumerate(routing(scal, w_refs, expert, rows)):
            pick = hit.astype(F32)
            scaled = (pick * weight).astype(BF16)
            span = span_of(position, rows)
            layer = dot(scaled, eo[span, :].astype(BF16), ((0,), (0,)))
            back = dot(pick.astype(BF16), idl[span, :].astype(BF16), ((0,), (0,)))
            which, place = (near, k) if k < n // 2 else (far, k - n // 2)
            if has_prev:
                before = prev[0 if k < n // 2 else 1]
                layer, back = layer + before[place, 0], back + before[place, 1]
            which[place, 0] = layer.astype(which.dtype)
            which[place, 1] = back.astype(which.dtype)
        token[...] = jnp.zeros_like(token)


def grad_kernel(n, has_prev, sizes, scal, in_ref, cot_ref, *refs):
    halves, refs = split_pieces(refs, sizes)
    if has_prev:
        refs = refs[3:]
    gg, ug, dg, token = refs
    step = pl.program_id(0)
    token[...] = jnp.zeros_like(token)
    for h in range(2):

        @pl.when(step == h)
        def _():
            gg[0] = dot(in_ref[...], load_rows(scal, n, 1, halves[h]), ((0,), (0,))).astype(BF16)
            ug[0] = dot(in_ref[...], load_rows(scal, n, 2, halves[h]), ((0,), (0,))).astype(BF16)
            dg[0] = dot(load_rows(scal, n, 0, halves[h]), cot_ref[...], ((0,), (0,))).astype(BF16)


def home_kernel(n, local, sizes, scal, *refs):
    w_refs, own, refs = refs[:n], refs[n], refs[n + 1 :]
    pairs = []
    for size in sizes:
        pairs.append(refs[:size])
        refs = refs[size:]
    near, far, held = refs
    held[0] = own[...]
    for q, pair in enumerate(pairs, 1):
        held[q] = (
            pair[0][...]
            if len(pair) == 1
            else jnp.where(scal[n + q] > 0, pair[0][...], pair[1][...])
        )
    experts_all, tokens = w_refs[0].shape
    ids = lax.broadcasted_iota(jnp.int32, (experts_all, tokens), 0)
    sums = [jnp.zeros((experts_all, tokens), F32) for _ in range(n)]
    for e in range(local):
        for k, (position, _, hit) in enumerate(routing(scal, w_refs, e, own.shape[0])):
            column = held[position][:, e : e + 1]
            value = jnp.sum(jnp.where(hit, column, 0.0), axis=0, keepdims=True)
            sums[k] = sums[k] + jnp.where(ids == scal[2 * n] + e, value, 0.0)
    for k in range(n):
        if k < n // 2:
            near[k] = sums[k]
        else:
            far[k - n // 2] = sums[k]


def whole_spec(shape):
    return pl.BlockSpec(tuple(shape), lambda g: (0,) * len(shape))


def spec_of(array):
    return whole_spec(array.shape)


def like(shape, dtype=BF16):
    return jax.ShapeDtypeStruct(tuple(shape), dtype)


SMEM_SPEC = pl.BlockSpec(memory_space=pltpu.SMEM)
ANY_SPEC = pl.BlockSpec(memory_space=pl.ANY)
TOKEN = (8, 128)


def call(kernel, grid, in_specs, out_specs, out_shape, flops, moved, **rest):
    return pl.pallas_call(
        kernel,
        grid=(grid,),
        in_specs=in_specs,
        out_specs=out_specs,
        out_shape=out_shape,
        compiler_params=pltpu.CompilerParams(vmem_limit_bytes=VMEM_BYTES),
        cost_estimate=pl.CostEstimate(flops=flops, bytes_accessed=moved, transcendentals=0),
        **rest,
    )


def body(tokens, expert_ids, combine, gate_weight, up_weight, down_weight, out_grad):
    peers, n = lax.axis_size("expert"), lax.axis_size("dp")
    assert peers == n
    chips = peers // 2
    local, width, hidden = gate_weight.shape
    count, choose = expert_ids.shape
    experts_all = peers * local
    capacity = count * choose * 5 // (4 * experts_all)
    rows = -(-capacity // 16) * 16
    all_rows = n * rows
    tile = hidden // 2
    swaps = n == 4

    me, here = lax.axis_index("expert"), lax.axis_index("dp")
    at_end = (here == 0) | (here == n - 1)
    table = []
    for place in range(n):
        block = 2 * lax.rem(me // 2 - place % chips + chips, chips) + lax.rem(
            lax.rem(me, 2) + place // chips, 2
        )
        if swaps:
            across_middle = jnp.where((block == 0) | (block == 3), 3, 2)
            position = jnp.where(
                block == here, 0, jnp.where(block // 2 == here // 2, 1, across_middle)
            )
        else:
            position = lax.rem(here - block + n, n)
        table.append(position)
    flags = [at_end if swaps else here >= q for q in range(n)]
    scal = jnp.stack(
        [jnp.asarray(v).astype(jnp.int32) for v in table + flags + [me * local, at_end]]
    )

    ids_t, combine_t = expert_ids.T, combine.T
    named = ids_t[:, None, :] == jnp.arange(experts_all, dtype=jnp.int32)[None, :, None]
    dense = jnp.sum(jnp.where(named, combine_t[:, None, :], 0.0), axis=0)

    along_x, across = Line("expert", chips, 2), Line("expert", peers, 1)
    swap = [(2 * x + c, 2 * x + 1 - c) for x in range(chips) for c in range(2)]

    def gather_blocks(own):
        found = [own] + [
            right if right is left else jnp.where(me // 2 >= q, right, left)
            for q, (right, left) in enumerate(along_x.gather(own), 1)
        ]
        return found + [across.send(piece, swap) for piece in found]

    packs = gather_blocks(jnp.stack([tokens, out_grad]))
    w_all = gather_blocks(dense)
    w_specs, pack_specs = [spec_of(w) for w in w_all], [spec_of(p) for p in packs]

    mac = all_rows * width * hidden
    weight_bytes = 2 * width * hidden
    piece_shape = (3, rows, tile)
    piece_bytes = 2 * 3 * rows * tile
    slot_shape = (all_rows, width)

    def weight_specs(e):
        wide = pl.BlockSpec((1, width, tile), lambda g: (e, 0, g))
        return [wide, wide, pl.BlockSpec((1, tile, width), lambda g: (e, g, 0))]

    def pre(e, deps):
        inputs, cot, *parts = call(
            functools.partial(pre_kernel, n, e, len(deps)),
            2,
            [SMEM_SPEC] + [ANY_SPEC] * len(deps) + w_specs + pack_specs + weight_specs(e),
            [whole_spec(slot_shape)] * 2 + [whole_spec(piece_shape)] * (2 * n),
            [like(slot_shape)] * 2 + [like(piece_shape)] * (2 * n),
            6 * mac,
            3 * weight_bytes + 2 * n * piece_bytes,
        )(scal, *deps, *w_all, *packs, gate_weight, up_weight, down_weight)
        return (inputs, cot), [parts[:n], parts[n:]]

    def mid(own, right, left, deps):
        return call(
            functools.partial(mid_kernel, len(deps)),
            1,
            [ANY_SPEC] * len(deps) + [whole_spec(piece_shape)] * 3,
            [whole_spec(piece_shape), whole_spec((rows, 128))],
            [like(piece_shape), like((rows, 128), F32)],
            20 * rows * tile,
            4 * piece_bytes,
        )(*deps, own, right, left)

    def step(select, adds, deps=()):
        pairs = ([select] if select is not None else []) + list(adds)
        flat = [x for pair in pairs for x in pair]
        return call(
            functools.partial(step_kernel, len(deps), int(select is not None), len(adds)),
            1,
            [SMEM_SPEC] + [ANY_SPEC] * len(deps) + [whole_spec(piece_shape)] * len(flat),
            [whole_spec(piece_shape)] * len(pairs),
            [like(piece_shape)] * len(pairs),
            3 * rows * tile * len(pairs),
            3 * piece_bytes * len(pairs),
        )(scal, *deps, *flat)

    def flatten(halves):
        return [x for pieces in halves for group in pieces for x in group]

    def sizes_of(pieces):
        return [len(group) for group in pieces[1:]]

    def out(e, halves, prev):
        flat = flatten(halves)
        sum_shape = (chips, 2, count, width)
        return call(
            functools.partial(out_kernel, n, e, e > 0, sizes_of(halves[0])),
            2,
            [SMEM_SPEC]
            + w_specs
            + ([whole_spec(sum_shape)] * 2 if e > 0 else [])
            + [whole_spec(piece_shape)] * len(flat)
            + weight_specs(e),
            [whole_spec(sum_shape)] * 2 + [whole_spec(TOKEN)],
            [like(sum_shape, BF16 if e == local - 1 else F32)] * 2 + [like(TOKEN, F32)],
            6 * mac,
            3 * weight_bytes + len(flat) * piece_bytes,
            scratch_shapes=[pltpu.VMEM(slot_shape, F32)] * 2,
        )(scal, *w_all, *prev, *flat, gate_weight, up_weight, down_weight)

    def grad(e, slots, halves, prev):
        flat = flatten(halves)
        base = 3 + len(flat)
        return call(
            functools.partial(grad_kernel, n, e > 0, sizes_of(halves[0])),
            2,
            [SMEM_SPEC]
            + [whole_spec(slot_shape)] * 2
            + [whole_spec(piece_shape)] * len(flat)
            + ([ANY_SPEC] * 3 if e > 0 else []),
            weight_specs(e) + [whole_spec(TOKEN)],
            [like(w.shape) for w in (gate_weight, up_weight, down_weight)] + [like(TOKEN, F32)],
            6 * mac,
            3 * weight_bytes + len(flat) * piece_bytes,
            input_output_aliases={base + k: k for k in range(3)} if e > 0 else {},
        )(scal, *slots, *flat, *prev)

    along_z = Line("dp", n, 1)

    def outer(value):
        return along_z.send(value, [(0, 1), (1, 0), (2, 3), (3, 2)])

    def inner(value):
        return along_z.send(value, [(1, 2), (2, 1)])

    products, sums, grads = [], [], []

    def finish(e, slots, halves):
        nonlocal sums, grads
        *sums, token_a = out(e, halves, sums)
        *grads, token_b = grad(e, slots, halves, grads)
        return token_a, token_b

    if swaps:
        tokens_of, flight, arrived, deps = None, [None, None], None, []
        for e in range(local):
            slots, parts = pre(e, deps)
            deps, halves = [], []
            for h in range(2):
                x, last = parts[h], flight[h]
                if last is None:
                    a1 = outer(x[3])
                    send_a2, (send_b2,) = x[2], step(None, [(x[3], a1)])
                else:
                    y, got_a, got_b, wait = last
                    (send_a1,) = step((x[3], got_b), [], wait)
                    a1, b1 = outer(send_a1), inner(got_a)
                    send_a2, send_b2 = step((x[2], b1), [(x[3], a1)])
                a2, b2 = outer(send_a2), inner(send_b2)
                if last is not None:
                    halves.append([(y,), (got_a,), (a1, got_b), (a2, b1)])
                send_a3, send_b3 = step(None, [(x[1], b2), (x[2], a2)])
                a3, b3 = outer(send_a3), inner(send_b3)
                parts[h] = (x[0], a3, b3)
            wait_mid, wait_next = [], []
            if e > 0:
                token_a, token_b = finish(e - 1, arrived, halves)
                wait_mid, wait_next = [token_a], [token_b]
            for h in range(2):
                y, product = mid(*parts[h], wait_mid if h == 1 else [])
                products.append(product)
                flight[h] = (y, outer(y), inner(y), wait_next if h == 1 else [])
            deps = [parts[1][1]] if e > 0 else [parts[0][1]]
            arrived = slots
        halves = []
        for h in range(2):
            y, got_a, got_b, _ = flight[h]
            a1, b1 = outer(got_b), inner(got_a)
            a2 = outer(b1)
            halves.append([(y,), (got_a,), (a1, got_b), (a2, b1)])
        finish(local - 1, arrived, halves)
    else:
        begun = []
        for e in range(local):
            slots, parts = pre(e, [])
            begun.append((slots, [(x[0], *along_z.scatter(x, add_rounded)) for x in parts]))
        for e in range(local):
            halves = []
            for h in range(2):
                y, product = mid(*begun[e][1][h], [])
                products.append(product)
                halves.append([(y,)] + along_z.gather(y))
            finish(e, begun[e][0], halves)

    own = jnp.stack(
        [jnp.sum(products[2 * e] + products[2 * e + 1], axis=1) for e in range(local)], axis=1
    )
    if swaps:
        got_a, got_b = outer(own), inner(own)
        a1, b1 = outer(got_b), inner(got_a)
        pairs = [(got_a,), (a1, got_b), (outer(b1), b1)]
    else:
        pairs = along_z.gather(own)
    flat = [x for pair in pairs for x in pair]
    dense_shape = (chips, experts_all, count)
    near_p, far_p = call(
        functools.partial(home_kernel, n, local, [len(pair) for pair in pairs]),
        1,
        [SMEM_SPEC] + w_specs + [spec_of(own)] * (1 + len(flat)),
        [whole_spec(dense_shape)] * 2,
        [like(dense_shape, F32)] * 2,
        local * all_rows * count * 4,
        4 * experts_all * count * n,
        scratch_shapes=[pltpu.VMEM((n, rows, local), F32)],
    )(scal, *w_all, own, *flat)

    def send_home(near, far, add):
        near = add(near, across.send(far, swap))
        right, left = along_x.scatter([near[q] for q in range(chips)], add)
        home = near[0].astype(F32) + right.astype(F32)
        return home if left is None else home + left.astype(F32)

    per_expert = send_home(near_p, far_p, lambda a, b: a + b)
    combine_grad = jnp.sum(jnp.where(named, per_expert[None], 0.0), axis=1) / combine_t
    home = send_home(*sums, add_rounded)
    return (home[0].astype(BF16), home[1].astype(BF16), *grads, combine_grad.T)


def solution(mesh):
    return jax.shard_map(
        body,
        mesh=mesh,
        in_specs=(
            P(("group", "expert"), "dp"),
            P(("group", "expert"), None),
            P(("group", "expert"), None),
            P("expert", "dp", None),
            P("expert", "dp", None),
            P("expert", None, "dp"),
            P(("group", "expert"), "dp"),
        ),
        out_specs=(
            P(("group", "expert"), "dp"),
            P(("group", "expert"), "dp"),
            P(("group", "expert"), "dp", None),
            P(("group", "expert"), "dp", None),
            P(("group", "expert"), None, "dp"),
            P(("group", "expert"), None),
        ),
        check_vma=False,
    )
```

time: 311 us -> 256 us (0.82)
  blocking collectives: 45.1 us -> 0 us
  Pallas kernels: 50.4 us -> 58.1 us
  waiting for transfers between devices: 44.9 us -> 38.1 us
  starting transfers between devices: 148 us -> 143 us
    all_gather x1 -> x0, blocking collectives: 45.1 us -> none  [body(): lax.all_gather(own_products, ('expert', 'dp'), axis=0, tiled=False)]
    pallas_call x16 -> x43, Pallas kernels: 50.4 us -> 58.1 us  [the longest x4 14.8 us: out(): call(functools.partial(out_kernel, n, e, e > 0, sizes_of(halves[0])), 2,...]
    ppermute x59 -> x83, waiting for transfers between devices: 44.9 us -> 38.1 us  [send(): return lax.ppermute(value, self.axis, wide)]
    ppermute x59 -> x83, starting transfers between devices: 148 us -> 143 us  [send(): return lax.ppermute(value, self.axis, wide)]
    unnamed x78 -> x50, local copies, waits for them, and re-layouts: 12.3 us -> 9.92 us
  transfers between devices with their start and end apart: 59 -> 83, of which waited for: 18 -> 22; matrix products, arithmetic and copies ran while one was open for 1% -> 1% of each run, Pallas kernels for 14% -> 20%
where the time goes in v2:
time: 256 us; the launch traced here: 254 us
  starting transfers between devices  143 us (56%)
  Pallas kernels  58.1 us (23%)
  waiting for transfers between devices  38.1 us (15%)
  local copies, waits for them, and re-layouts  10.8 us (4%)
  other arithmetic  2.98 us (1%)
    ppermute x83, starting transfers between devices, send(): return lax.ppermute(value, self.axis, wide)  143 us
    ppermute x83, waiting for transfers between devices, send(): return lax.ppermute(value, self.axis, wide)  38.1 us
    pallas_call x4, Pallas kernels, out(): call(functools.partial(out_kernel, n, e, e > 0, sizes_of(halves[0])), 2,...  14.8 us
    pallas_call x4, Pallas kernels, grad(): call(functools.partial(grad_kernel, n, e > 0, sizes_of(halves[0])), 2, [S...  14.6 us
    pallas_call x22, Pallas kernels, step(): call(functools.partial(step_kernel, len(deps), int(select is not None), l...  13.4 us
    pallas_call x4, Pallas kernels, pre(): call(functools.partial(pre_kernel, n, e, len(deps)), 2, [SMEM_SPEC] + [AN...  13.2 us
    unnamed x50, local copies, waits for them, and re-layouts  9.92 us
  transfers between devices with their start and end apart: 83, of which 22 were waited for; matrix products, arithmetic and copies ran while one was open for 1% of the time, Pallas kernels for 20%

profile of v2, /device:TPU:0, one launch (start us, length us, event | category | flops | bytes accessed | tf_op | source)
XLA Modules:
  0.0 254.2 jit_solution(16371247293740959953)
XLA Ops:
  1.6 3.0 %collective-permute-start.3 = (bf16[2,128,512]{2,1,0:T(8,128)(2,1)S(1)}, bf16[2,128,512]{2,1,0:T(8,128)(2,1)S(1)}, u32[]{:S(2)}, u32[]{:S(2)}) collective-permute-start(bf16[2,128,512]{2,1,0:T(8,128)(2,1)S(1)} %pad_maximum_fusion.refs_4_.refs_5_), channel_id=1, source_target_pairs={{0,8},{4,12},{8,0},{12,4},{1,9},{5,13},{9,1},{13,5},{2,10},{6,14},... | collective-permute-start | bytes 786440 | tf_op jit(solution)/shard_map/ppermute | solution.py:32
  4.6 6.3 %collective-permute-done.3.refs_5_.refs_6_ = bf16[2,128,512]{2,1,0:T(8,128)(2,1)S(1)} collective-permute-done((bf16[2,128,512]{2,1,0:T(8,128)(2,1)S(1)}, bf16[2,128,512]{2,1,0:T(8,128)(2,1)S(1)}, u32[]{:S(2)}, u32[]{:S(2)}) %collective-permute-start.3) | collective-permute-done | bytes 262176 | tf_op jit(solution)/shard_map/ppermute | solution.py:32
  11.7 1.8 collective-permute-start
  13.7 1.7 collective-permute-done.refs_1_.refs_2_
  16.6 3.3 %shard_map.118 = (bf16[320,512]{1,0:T(8,128)(2,1)S(1)}, bf16[320,512]{1,0:T(8,128)(2,1)S(1)}, bf16[3,80,384]{2,1,0:T(8,128)(2,1)S(1)}, bf16[3,80,384]{2,1,0:T(8,...) custom-call(s32[10]{0:T(128)S(1)} %stack.59.scal, ...), custom_call_target="tpu_custom_call" | custom-call | flops 754974720 | bytes 3833856 | tf_op jit(solution)/shard_map/pallas_call | solution.py:345
  19.9 1.9 collective-permute-start.6
  22.0 1.8 collective-permute-start.8
  23.8 3.6 %collective-permute-done.6.refs_1_ = bf16[3,80,384]{2,1,0:T(8,128)(2,1)S(1)} collective-permute-done((bf16[3,80,384]{2,1,0:T(8,128)(2,1)S(1)}, bf16[3,80,384]{2,1,0:T(8,128)(2,1)S(1)}, u32[]{:S(2)}, u32[]{:S(2)}) %collective-permute-start.6) | collective-permute-done | bytes 184352 | tf_op jit(solution)/shard_map/ppermute | solution.py:32
  28.7 4.7 %collective-permute-start.18 = (bf16[3,80,384]{2,1,0:T(8,128)(2,1)S(1)}, bf16[3,80,384]{2,1,0:T(8,128)(2,1)S(1)}, u32[]{:S(2)}, u32[]{:S(2)}) collective-permute-start(bf16[3,80,384]{2,1,0:T(8,128)(2,1)S(1)} %get-tuple-element.130.refs_2_), channel_id=1, source_target_pairs={{0,1},{1,0},{2,3},{3,2},{4,5},{5,4},{6,7},{7,6},{8,9},{9,8},{10,11... | collective-permute-start | bytes 552968 | tf_op jit(solution)/shard_map/ppermute | solution.py:32
  35.9 2.4 collective-permute-start.9
  39.9 3.7 %collective-permute-start.19 = (bf16[3,80,384]{2,1,0:T(8,128)(2,1)S(1)}, bf16[3,80,384]{2,1,0:T(8,128)(2,1)S(1)}, u32[]{:S(2)}, u32[]{:S(2)}) collective-permute-start(bf16[3,80,384]{2,1,0:T(8,128)(2,1)S(1)} %get-tuple-element.131), channel_id=1, source_target_pairs={{0,1},{1,0},{2,3},{3,2},{4,5},{5,4},{6,7},{7,6},{8,9},{9,8},{10,11... | collective-permute-start | bytes 552968 | tf_op jit(solution)/shard_map/ppermute | solution.py:32
  44.5 2.6 %collective-permute-start.11 = (bf16[3,80,384]{2,1,0:T(8,128)(2,1)S(1)}, bf16[3,80,384]{2,1,0:T(8,128)(2,1)S(1)}, u32[]{:S(2)}, u32[]{:S(2)}) collective-permute-start(bf16[3,80,384]{2,1,0:T(8,128)(2,1)S(1)} %get-tuple-element.123.refs_4_.refs_0_), channel_id=1, source_target_pairs={{0,1},{1,0},{2,3},{3,2},{4,5},{5,4},{6,7},{7,6},{8,9},{9,8},{10,11... | collective-permute-start | bytes 552968 | tf_op jit(solution)/shard_map/ppermute | solution.py:32
  48.5 4.3 %collective-permute-start.21 = (bf16[3,80,384]{2,1,0:T(8,128)(2,1)S(1)}, bf16[3,80,384]{2,1,0:T(8,128)(2,1)S(1)}, u32[]{:S(2)}, u32[]{:S(2)}) collective-permute-start(bf16[3,80,384]{2,1,0:T(8,128)(2,1)S(1)} %get-tuple-element.133.refs_10_.refs_6_), channel_id=1, source_target_pairs={{0,1},{1,0},{2,3},{3,2},{4,5},{5,4},{6,7},{7,6},{8,9},{9,8},{10,11... | collective-permute-start | bytes 552968 | tf_op jit(solution)/shard_map/ppermute | solution.py:32
  53.5 3.3 %shard_map.122 = (bf16[320,512]{1,0:T(8,128)(2,1)S(1)}, bf16[320,512]{1,0:T(8,128)(2,1)S(1)}, bf16[3,80,384]{2,1,0:T(8,128)(2,1)S(1)}, bf16[3,80,384]{2,1,0:T(8,...) custom-call(s32[10]{0:T(128)S(1)} %stack.59.scal, ...), custom_call_target="tpu_custom_call" | custom-call | flops 754974720 | bytes 3833856 | tf_op jit(solution)/shard_map/pallas_call | solution.py:345
  58.1 4.6 %collective-permute-start.13 = (bf16[3,80,384]{2,1,0:T(8,128)(2,1)S(1)}, bf16[3,80,384]{2,1,0:T(8,128)(2,1)S(1)}, u32[]{:S(2)}, u32[]{:S(2)}) collective-permute-start(bf16[3,80,384]{2,1,0:T(8,128)(2,1)S(1)} %shard_map.123), channel_id=1, source_target_pairs={{0,1},{1,0},{2,3},{3,2},{4,5},{5,4},{6,7},{7,6},{8,9},{9,8},{10,11... | collective-permute-start | bytes 552968 | tf_op jit(solution)/shard_map/ppermute | solution.py:32
  64.0 2.7 %collective-permute-start.23 = (bf16[3,80,384]{2,1,0:T(8,128)(2,1)S(1)}, bf16[3,80,384]{2,1,0:T(8,128)(2,1)S(1)}, u32[]{:S(2)}, u32[]{:S(2)}) collective-permute-start(bf16[3,80,384]{2,1,0:T(8,128)(2,1)S(1)} %shard_map.128), channel_id=1, source_target_pairs={{0,1},{1,0},{2,3},{3,2},{4,5},{5,4},{6,7},{7,6},{8,9},{9,8},{10,11... | collective-permute-start | bytes 552968 | tf_op jit(solution)/shard_map/ppermute | solution.py:32
  66.7 1.5 collective-permute-done.13.refs_3_.refs_6_.refs_2_
  68.8 2.1 collective-permute-start.15
  72.9 2.1 collective-permute-start.25
  76.9 3.1 %collective-permute-start.27 = (bf16[3,80,384]{2,1,0:T(8,128)(2,1)S(1)}, bf16[3,80,384]{2,1,0:T(8,128)(2,1)S(1)}, u32[]{:S(2)}, u32[]{:S(2)}) collective-permute-start(bf16[3,80,384]{2,1,0:T(8,128)(2,1)S(1)} %get-tuple-element.142), channel_id=1, source_target_pairs={{0,1},{1,0},{2,3},{3,2},{4,5},{5,4},{6,7},{7,6},{8,9},{9,8},{10,11... | collective-permute-start | bytes 552968 | tf_op jit(solution)/shard_map/ppermute | solution.py:32
  81.4 3.0 %collective-permute-start.31 = (bf16[3,80,384]{2,1,0:T(8,128)(2,1)S(1)}, bf16[3,80,384]{2,1,0:T(8,128)(2,1)S(1)}, u32[]{:S(2)}, u32[]{:S(2)}) collective-permute-start(bf16[3,80,384]{2,1,0:T(8,128)(2,1)S(1)} %get-tuple-element.147), channel_id=1, source_target_pairs={{0,1},{1,0},{2,3},{3,2},{4,5},{5,4},{6,7},{7,6},{8,9},{9,8},{10,11... | collective-permute-start | bytes 552968 | tf_op jit(solution)/shard_map/ppermute | solution.py:32
  85.7 3.7 %collective-permute-start.29 = (bf16[3,80,384]{2,1,0:T(8,128)(2,1)S(1)}, bf16[3,80,384]{2,1,0:T(8,128)(2,1)S(1)}, u32[]{:S(2)}, u32[]{:S(2)}) collective-permute-start(bf16[3,80,384]{2,1,0:T(8,128)(2,1)S(1)} %get-tuple-element.144.refs_6_.refs_0_), channel_id=1, source_target_pairs={{0,1},{1,0},{2,3},{3,2},{4,5},{5,4},{6,7},{7,6},{8,9},{9,8},{10,11... | collective-permute-start | bytes 552968 | tf_op jit(solution)/shard_map/ppermute | solution.py:32
  90.0 3.2 %shard_map.130 = (f32[2,2,128,512]{3,2,1,0:T(8,128)S(1)}, f32[2,2,128,512]{3,2,1,0:T(8,128)S(1)}, f32[8,128]{1,0:T(8,128)S(1)}) custom-call(s32[10]{0:T(128)S(1)} %stack.59.scal, f32[16,128]{1,0:T(8,128)S(1)} %select_reduce_fusion.1.refs_0_.refs_1_, f32[16,128]{1,0:T(8,128)S(1)} %collective-permute-done.refs_1_.refs_2_, ...), custom_call_target="tpu_custom_call" | custom-call | flops 754974720 | bytes 4571136 | tf_op jit(solution)/shard_map/pallas_call | solution.py:389
  94.4 2.7 %collective-permute-start.37 = (bf16[3,80,384]{2,1,0:T(8,128)(2,1)S(1)}, bf16[3,80,384]{2,1,0:T(8,128)(2,1)S(1)}, u32[]{:S(2)}, u32[]{:S(2)}) collective-permute-start(bf16[3,80,384]{2,1,0:T(8,128)(2,1)S(1)} %get-tuple-element.154.refs_12_.refs_6_), channel_id=1, source_target_pairs={{0,1},{1,0},{2,3},{3,2},{4,5},{5,4},{6,7},{7,6},{8,9},{9,8},{10,11... | collective-permute-start | bytes 552968 | tf_op jit(solution)/shard_map/ppermute | solution.py:32
  97.7 3.3 %shard_map.134 = (bf16[320,512]{1,0:T(8,128)(2,1)S(1)}, bf16[320,512]{1,0:T(8,128)(2,1)S(1)}, bf16[3,80,384]{2,1,0:T(8,128)(2,1)S(1)}, bf16[3,80,384]{2,1,0:T(8,...) custom-call(s32[10]{0:T(128)S(1)} %stack.59.scal, ...), custom_call_target="tpu_custom_call" | custom-call | flops 754974720 | bytes 3833856 | tf_op jit(solution)/shard_map/pallas_call | solution.py:345
  102.3 4.6 %collective-permute-start.33 = (bf16[3,80,384]{2,1,0:T(8,128)(2,1)S(1)}, bf16[3,80,384]{2,1,0:T(8,128)(2,1)S(1)}, u32[]{:S(2)}, u32[]{:S(2)}) collective-permute-start(bf16[3,80,384]{2,1,0:T(8,128)(2,1)S(1)} %shard_map.135), channel_id=1, source_target_pairs={{0,1},{1,0},{2,3},{3,2},{4,5},{5,4},{6,7},{7,6},{8,9},{9,8},{10,11... | collective-permute-start | bytes 552968 | tf_op jit(solution)/shard_map/ppermute | solution.py:32
  106.9 3.4 %shard_map.138 = (bf16[4,512,768]{2,1,0:T(8,128)(2,1)}, bf16[4,512,768]{2,1,0:T(8,128)(2,1)}, bf16[4,768,512]{2,1,0:T(8,128)(2,1)}, f32[8,128]{1,0:T(8,128)S(1)}) custom-call(s32[10]{0:T(128)S(1)} %stack.59.scal, bf16[320,512]{1,0:T(8,128)(2,1)S(1)} %get-tuple-element.155.in_ref, bf16[320,512]{1,0:T(8,128)(2,1)S(1)} %get-tuple-element.156.cot_ref, ...), custom_call_target="tpu_custom_call" | custom-call | flops 754974720 | bytes 4571136 | tf_op jit(solution)/shard_map/pallas_call | solution.py:407
  111.5 2.1 collective-permute-start.39
  115.1 3.0 %collective-permute-done.39.refs_3_.refs_14_.refs_8_ = bf16[3,80,384]{2,1,0:T(8,128)(2,1)S(1)} collective-permute-done((bf16[3,80,384]{2,1,0:T(8,128)(2,1)S(1)}, bf16[3,80,384]{2,1,0:T(8,128)(2,1)S(1)}, u32[]{:S(2)}, u32[]{:S(2)}) %collective-permute-start.39) | collective-permute-done | bytes 184352 | tf_op jit(solution)/shard_map/ppermute | solution.py:32
  118.7 1.8 collective-permute-start.41
  122.6 3.9 %collective-permute-start.43 = (bf16[3,80,384]{2,1,0:T(8,128)(2,1)S(1)}, bf16[3,80,384]{2,1,0:T(8,128)(2,1)S(1)}, u32[]{:S(2)}, u32[]{:S(2)}) collective-permute-start(bf16[3,80,384]{2,1,0:T(8,128)(2,1)S(1)} %get-tuple-element.166), channel_id=1, source_target_pairs={{0,1},{1,0},{2,3},{3,2},{4,5},{5,4},{6,7},{7,6},{8,9},{9,8},{10,11... | collective-permute-start | bytes 552968 | tf_op jit(solution)/shard_map/ppermute | solution.py:32
  127.8 2.5 collective-permute-start.47
  132.1 5.1 %collective-permute-start.45 = (bf16[3,80,384]{2,1,0:T(8,128)(2,1)S(1)}, bf16[3,80,384]{2,1,0:T(8,128)(2,1)S(1)}, u32[]{:S(2)}, u32[]{:S(2)}) collective-permute-start(bf16[3,80,384]{2,1,0:T(8,128)(2,1)S(1)} %get-tuple-element.168.refs_6_.refs_0_), channel_id=1, source_target_pairs={{0,1},{1,0},{2,3},{3,2},{4,5},{5,4},{6,7},{7,6},{8,9},{9,8},{10,11... | collective-permute-start | bytes 552968 | tf_op jit(solution)/shard_map/ppermute | solution.py:32
  137.2 3.6 %shard_map.141 = (f32[2,2,128,512]{3,2,1,0:T(8,128)S(1)}, f32[2,2,128,512]{3,2,1,0:T(8,128)S(1)}, f32[8,128]{1,0:T(8,128)S(1)}) custom-call(s32[10]{0:T(128)S(1)} %stack.59.scal, f32[16,128]{1,0:T(8,128)S(1)} %select_reduce_fusion.1.refs_0_.refs_1_, f32[16,128]{1,0:T(8,128)S(1)} %collective-permute-done.refs_1_.refs_2_, ...), custom_call_target="tpu_custom_call" | custom-call | flops 754974720 | bytes 4571136 | tf_op jit(solution)/shard_map/pallas_call | solution.py:389
  142.7 3.3 %shard_map.145 = (bf16[320,512]{1,0:T(8,128)(2,1)S(1)}, bf16[320,512]{1,0:T(8,128)(2,1)S(1)}, bf16[3,80,384]{2,1,0:T(8,128)(2,1)S(1)}, bf16[3,80,384]{2,1,0:T(8,...) custom-call(s32[10]{0:T(128)S(1)} %stack.59.scal, ...), custom_call_target="tpu_custom_call" | custom-call | flops 754974720 | bytes 3833856 | tf_op jit(solution)/shard_map/pallas_call | solution.py:345
  146.7 4.3 %collective-permute-start.49 = (bf16[3,80,384]{2,1,0:T(8,128)(2,1)S(1)}, bf16[3,80,384]{2,1,0:T(8,128)(2,1)S(1)}, u32[]{:S(2)}, u32[]{:S(2)}) collective-permute-start(bf16[3,80,384]{2,1,0:T(8,128)(2,1)S(1)} %shard_map.146), channel_id=1, source_target_pairs={{0,1},{1,0},{2,3},{3,2},{4,5},{5,4},{6,7},{7,6},{8,9},{9,8},{10,11... | collective-permute-start | bytes 552968 | tf_op jit(solution)/shard_map/ppermute | solution.py:32
  151.7 3.4 %shard_map.149 = (bf16[4,512,768]{2,1,0:T(8,128)(2,1)}, bf16[4,512,768]{2,1,0:T(8,128)(2,1)}, bf16[4,768,512]{2,1,0:T(8,128)(2,1)}, f32[8,128]{1,0:T(8,128)S(1)}) custom-call(s32[10]{0:T(128)S(1)} %stack.59.scal, bf16[320,512]{1,0:T(8,128)(2,1)S(1)} %get-tuple-element.179.in_ref, ...), custom_call_target="tpu_custom_call", output_to_operand_aliasing={{0}: (15, {}), {1}: (16, {}), {2}: (17, {})} | custom-call | flops 754974720 | bytes 4571136 | tf_op jit(solution)/shard_map/pallas_call | solution.py:407
  156.4 4.6 %collective-permute-start.55 = (bf16[3,80,384]{2,1,0:T(8,128)(2,1)S(1)}, bf16[3,80,384]{2,1,0:T(8,128)(2,1)S(1)}, u32[]{:S(2)}, u32[]{:S(2)}) collective-permute-start(bf16[3,80,384]{2,1,0:T(8,128)(2,1)S(1)} %shard_map.150), channel_id=1, source_target_pairs={{0,1},{1,0},{2,3},{3,2},{4,5},{5,4},{6,7},{7,6},{8,9},{9,8},{10,11... | collective-permute-start | bytes 552968 | tf_op jit(solution)/shard_map/ppermute | solution.py:32
  162.4 3.2 %collective-permute-done.55.refs_3_.refs_14_.refs_8_ = bf16[3,80,384]{2,1,0:T(8,128)(2,1)S(1)} collective-permute-done((bf16[3,80,384]{2,1,0:T(8,128)(2,1)S(1)}, bf16[3,80,384]{2,1,0:T(8,128)(2,1)S(1)}, u32[]{:S(2)}, u32[]{:S(2)}) %collective-permute-start.55) | collective-permute-done | bytes 184352 | tf_op jit(solution)/shard_map/ppermute | solution.py:32
  166.2 1.8 collective-permute-start.57
  169.4 2.8 %collective-permute-start.59 = (bf16[3,80,384]{2,1,0:T(8,128)(2,1)S(1)}, bf16[3,80,384]{2,1,0:T(8,128)(2,1)S(1)}, u32[]{:S(2)}, u32[]{:S(2)}) collective-permute-start(bf16[3,80,384]{2,1,0:T(8,128)(2,1)S(1)} %get-tuple-element.193), channel_id=1, source_target_pairs={{0,1},{1,0},{2,3},{3,2},{4,5},{5,4},{6,7},{7,6},{8,9},{9,8},{10,11... | collective-permute-start | bytes 552968 | tf_op jit(solution)/shard_map/ppermute | solution.py:32
  174.4 2.9 %collective-permute-start.67 = (bf16[3,80,384]{2,1,0:T(8,128)(2,1)S(1)}, bf16[3,80,384]{2,1,0:T(8,128)(2,1)S(1)}, u32[]{:S(2)}, u32[]{:S(2)}) collective-permute-start(bf16[3,80,384]{2,1,0:T(8,128)(2,1)S(1)} %get-tuple-element.200), channel_id=1, source_target_pairs={{0,1},{1,0},{2,3},{3,2},{4,5},{5,4},{6,7},{7,6},{8,9},{9,8},{10,11... | collective-permute-start | bytes 552968 | tf_op jit(solution)/shard_map/ppermute | solution.py:32
  178.0 3.7 %shard_map.152 = (f32[2,2,128,512]{3,2,1,0:T(8,128)S(1)}, f32[2,2,128,512]{3,2,1,0:T(8,128)S(1)}, f32[8,128]{1,0:T(8,128)S(1)}) custom-call(s32[10]{0:T(128)S(1)} %stack.59.scal, f32[16,128]{1,0:T(8,128)S(1)} %select_reduce_fusion.1.refs_0_.refs_1_, f32[16,128]{1,0:T(8,128)S(1)} %collective-permute-done.refs_1_.refs_2_, ...), custom_call_target="tpu_custom_call" | custom-call | flops 754974720 | bytes 4571136 | tf_op jit(solution)/shard_map/pallas_call | solution.py:389
  182.8 3.0 %collective-permute-start.61 = (bf16[3,80,384]{2,1,0:T(8,128)(2,1)S(1)}, bf16[3,80,384]{2,1,0:T(8,128)(2,1)S(1)}, u32[]{:S(2)}, u32[]{:S(2)}) collective-permute-start(bf16[3,80,384]{2,1,0:T(8,128)(2,1)S(1)} %get-tuple-element.195.refs_6_.refs_0_), channel_id=1, source_target_pairs={{0,1},{1,0},{2,3},{3,2},{4,5},{5,4},{6,7},{7,6},{8,9},{9,8},{10,11... | collective-permute-start | bytes 552968 | tf_op jit(solution)/shard_map/ppermute | solution.py:32
  187.1 1.3 collective-permute-start.62
  188.5 1.3 collective-permute-start.70
  191.4 1.3 collective-permute-start.64
  193.4 1.9 collective-permute-done.69.refs_13_.refs_7_
  195.3 1.3 collective-permute-start.72
  197.6 4.6 %collective-permute-start.63 = (bf16[3,80,384]{2,1,0:T(8,128)(2,1)}, bf16[3,80,384]{2,1,0:T(8,128)(2,1)}, u32[]{:S(2)}, u32[]{:S(2)}) collective-permute-start(bf16[3,80,384]{2,1,0:T(8,128)(2,1)} %collective-permute-done.62.refs_9_.refs_3_), channel_id=1, source_target_pairs={{0,1},{1,0},{2,3},{3,2},{4,5},{5,4},{6,7},{7,6},{8,9},{9,8},{10,11... | collective-permute-start | bytes 552968 | tf_op jit(solution)/shard_map/ppermute | solution.py:32
  202.3 1.9 collective-permute-start.65
  204.2 1.2 collective-permute-start.73
  206.4 6.0 %collective-permute-start.76 = (f32[80,4]{1,0:T(8,128)S(1)}, f32[80,4]{1,0:T(8,128)S(1)}, u32[]{:S(2)}, u32[]{:S(2)}) collective-permute-start(f32[80,4]{1,0:T(8,128)S(1)} %copy.31.refs_4_), channel_id=1, source_target_pairs={{0,1},{1,0},{2,3},{3,2},{4,5},{5,4},{6,7},{7,6},{8,9},{9,8},{10,11... | collective-permute-start | bytes 3848 | tf_op jit(solution)/shard_map/ppermute | solution.py:32
  212.4 2.0 collective-permute-done.76.refs_5_
  214.4 2.0 collective-permute-start.78
  216.4 2.0 collective-permute-done.78.refs_6_
  219.3 7.0 %collective-permute-start.80 = (f32[80,4]{1,0:T(8,128)S(1)}, f32[80,4]{1,0:T(8,128)S(1)}, u32[]{:S(2)}, u32[]{:S(2)}) collective-permute-start(f32[80,4]{1,0:T(8,128)S(1)} %collective-permute-done.79.refs_9_), channel_id=1, source_target_pairs={{0,1},{1,0},{2,3},{3,2},{4,5},{5,4},{6,7},{7,6},{8,9},{9,8},{10,11... | collective-permute-start | bytes 3848 | tf_op jit(solution)/shard_map/ppermute | solution.py:32
  226.3 2.0 collective-permute-done.80.refs_8_
  230.4 1.2 copy-done.2
  235.3 4.4 %shard_map.157 = (bf16[2,2,128,512]{3,2,1,0:T(8,128)(2,1)S(1)}, bf16[2,2,128,512]{3,2,1,0:T(8,128)(2,1)S(1)}, f32[8,128]{1,0:T(8,128)}) custom-call(s32[10]{0:T(128)S(1)} %stack.59.scal, f32[16,128]{1,0:T(8,128)S(1)} %select_reduce_fusion.1.refs_0_.refs_1_, f32[16,128]{1,0:T(8,128)S(1)} %collective-permute-done.refs_1_.refs_2_, ...), custom_call_target="tpu_custom_call" | custom-call | flops 754974720 | bytes 4571136 | tf_op jit(solution)/shard_map/pallas_call | solution.py:389
  239.8 1.5 collective-permute-start.82
  241.4 3.5 %shard_map.158 = (bf16[4,512,768]{2,1,0:T(8,128)(2,1)}, bf16[4,512,768]{2,1,0:T(8,128)(2,1)}, bf16[4,768,512]{2,1,0:T(8,128)(2,1)}, f32[8,128]{1,0:T(8,128)}) custom-call(s32[10]{0:T(128)S(1)} %stack.59.scal, bf16[320,512]{1,0:T(8,128)(2,1)S(1)} %copy-done.16, ...), custom_call_target="tpu_custom_call", output_to_operand_aliasing={{0}: (15, {}), {1}: (16, {}), {2}: (17, {})} | custom-call | flops 754974720 | bytes 4571136 | tf_op jit(solution)/shard_map/pallas_call | solution.py:407
  246.3 4.3 %shard_map.159 = (bf16[4,512,768]{2,1,0:T(8,128)(2,1)}, bf16[4,512,768]{2,1,0:T(8,128)(2,1)}, bf16[4,768,512]{2,1,0:T(8,128)(2,1)}, f32[8,128]{1,0:T(8,128)}) custom-call(s32[10]{0:T(128)S(1)} %stack.59.scal, bf16[320,512]{1,0:T(8,128)(2,1)S(1)} %copy-done.20, ...), custom_call_target="tpu_custom_call", output_to_operand_aliasing={{0}: (15, {}), {1}: (16, {}), {2}: (17, {})} | custom-call | flops 754974720 | bytes 4571136 | tf_op jit(solution)/shard_map/pallas_call | solution.py:407
  250.6 2.8 %collective-permute-done.75 = bf16[2,128,512]{2,1,0:T(8,128)(2,1)S(1)} collective-permute-done((bf16[2,128,512]{2,1,0:T(8,128)(2,1)S(1)}, bf16[2,128,512]{2,1,0:T(8,128)(2,1)S(1)}, u32[]{:S(2)}, u32[]{:S(2)}) %collective-permute-start.75) | collective-permute-done | bytes 262176 | tf_op jit(solution)/shard_map/ppermute | solution.py:32
  (213 shorter events, 59.2 us)
Async XLA Ops:
  1.6 9.3 %collective-permute-start.3 = (bf16[2,128,512]{2,1,0:T(8,128)(2,1)S(1)}, bf16[2,128,512]{2,1,0:T(8,128)(2,1)S(1)}, u32[]{:S(2)}, u32[]{:S(2)}) collective-permute-start(bf16[2,128,512]{2,1,0:T(8,128)(2,1)S(1)} %pad_maximum_fusion.refs_4_.refs_5_), channel_id=1, source_target_pairs={{0,8},{4,12},{8,0},{12,4},{1,9},{5,13},{9,1},{13,5},{2,10},{6,14},... | collective-permute-start | bytes 786440 | tf_op jit(solution)/shard_map/ppermute | solution.py:32
  4.6 11.9 %collective-permute-start.4 = (bf16[2,128,512]{2,1,0:T(8,128)(2,1)S(1)}, bf16[2,128,512]{2,1,0:T(8,128)(2,1)S(1)}, u32[]{:S(2)}, u32[]{:S(2)}) collective-permute-start(bf16[2,128,512]{2,1,0:T(8,128)(2,1)S(1)} %pad_maximum_fusion.refs_4_.refs_5_), channel_id=1, source_target_pairs={{0,4},{4,0},{8,12},{12,8},{1,5},{5,1},{9,13},{13,9},{2,6},{6,2},{1... | collective-permute-start | bytes 786440 | tf_op jit(solution)/shard_map/ppermute | solution.py:32
  19.9 7.5 %collective-permute-start.6 = (bf16[3,80,384]{2,1,0:T(8,128)(2,1)S(1)}, bf16[3,80,384]{2,1,0:T(8,128)(2,1)S(1)}, u32[]{:S(2)}, u32[]{:S(2)}) collective-permute-start(bf16[3,80,384]{2,1,0:T(8,128)(2,1)S(1)} %get-tuple-element.119.refs_0_), channel_id=1, source_target_pairs={{0,1},{1,0},{2,3},{3,2},{4,5},{5,4},{6,7},{7,6},{8,9},{9,8},{10,11... | collective-permute-start | bytes 552968 | tf_op jit(solution)/shard_map/ppermute | solution.py:32
  21.8 11.6 %collective-permute-start.16 = (bf16[3,80,384]{2,1,0:T(8,128)(2,1)S(1)}, bf16[3,80,384]{2,1,0:T(8,128)(2,1)S(1)}, u32[]{:S(2)}, u32[]{:S(2)}) collective-permute-start(bf16[3,80,384]{2,1,0:T(8,128)(2,1)S(1)} %get-tuple-element.129.refs_0_), channel_id=1, source_target_pairs={{0,1},{1,0},{2,3},{3,2},{4,5},{5,4},{6,7},{7,6},{8,9},{9,8},{10,11... | collective-permute-start | bytes 552968 | tf_op jit(solution)/shard_map/ppermute | solution.py:32
  22.0 13.3 %collective-permute-start.8 = (bf16[3,80,384]{2,1,0:T(8,128)(2,1)S(1)}, bf16[3,80,384]{2,1,0:T(8,128)(2,1)S(1)}, u32[]{:S(2)}, u32[]{:S(2)}) collective-permute-start(bf16[3,80,384]{2,1,0:T(8,128)(2,1)S(1)} %get-tuple-element.120.refs_2_), channel_id=1, source_target_pairs={{0,1},{1,0},{2,3},{3,2},{4,5},{5,4},{6,7},{7,6},{8,9},{9,8},{10,11... | collective-permute-start | bytes 552968 | tf_op jit(solution)/shard_map/ppermute | solution.py:32
  28.0 7.3 %collective-permute-start.7 = (bf16[3,80,384]{2,1,0:T(8,128)(2,1)S(1)}, bf16[3,80,384]{2,1,0:T(8,128)(2,1)S(1)}, u32[]{:S(2)}, u32[]{:S(2)}) collective-permute-start(bf16[3,80,384]{2,1,0:T(8,128)(2,1)S(1)} %shard_map.119), channel_id=1, source_target_pairs={{1,2},{2,1},{5,6},{6,5},{9,10},{10,9},{13,14},{14,13},{17,18},{18,... | collective-permute-start | bytes 552968 | tf_op jit(solution)/shard_map/ppermute | solution.py:32
  28.7 10.6 %collective-permute-start.18 = (bf16[3,80,384]{2,1,0:T(8,128)(2,1)S(1)}, bf16[3,80,384]{2,1,0:T(8,128)(2,1)S(1)}, u32[]{:S(2)}, u32[]{:S(2)}) collective-permute-start(bf16[3,80,384]{2,1,0:T(8,128)(2,1)S(1)} %get-tuple-element.130.refs_2_), channel_id=1, source_target_pairs={{0,1},{1,0},{2,3},{3,2},{4,5},{5,4},{6,7},{7,6},{8,9},{9,8},{10,11... | collective-permute-start | bytes 552968 | tf_op jit(solution)/shard_map/ppermute | solution.py:32
  35.9 8.4 %collective-permute-start.9 = (bf16[3,80,384]{2,1,0:T(8,128)(2,1)S(1)}, bf16[3,80,384]{2,1,0:T(8,128)(2,1)S(1)}, u32[]{:S(2)}, u32[]{:S(2)}) collective-permute-start(bf16[3,80,384]{2,1,0:T(8,128)(2,1)S(1)} %get-tuple-element.121), channel_id=1, source_target_pairs={{0,1},{1,0},{2,3},{3,2},{4,5},{5,4},{6,7},{7,6},{8,9},{9,8},{10,11... | collective-permute-start | bytes 552968 | tf_op jit(solution)/shard_map/ppermute | solution.py:32
  39.9 8.5 %collective-permute-start.19 = (bf16[3,80,384]{2,1,0:T(8,128)(2,1)S(1)}, bf16[3,80,384]{2,1,0:T(8,128)(2,1)S(1)}, u32[]{:S(2)}, u32[]{:S(2)}) collective-permute-start(bf16[3,80,384]{2,1,0:T(8,128)(2,1)S(1)} %get-tuple-element.131), channel_id=1, source_target_pairs={{0,1},{1,0},{2,3},{3,2},{4,5},{5,4},{6,7},{7,6},{8,9},{9,8},{10,11... | collective-permute-start | bytes 552968 | tf_op jit(solution)/shard_map/ppermute | solution.py:32
  44.5 12.4 %collective-permute-start.11 = (bf16[3,80,384]{2,1,0:T(8,128)(2,1)S(1)}, bf16[3,80,384]{2,1,0:T(8,128)(2,1)S(1)}, u32[]{:S(2)}, u32[]{:S(2)}) collective-permute-start(bf16[3,80,384]{2,1,0:T(8,128)(2,1)S(1)} %get-tuple-element.123.refs_4_.refs_0_), channel_id=1, source_target_pairs={{0,1},{1,0},{2,3},{3,2},{4,5},{5,4},{6,7},{7,6},{8,9},{9,8},{10,11... | collective-permute-start | bytes 552968 | tf_op jit(solution)/shard_map/ppermute | solution.py:32
  47.1 10.4 %collective-permute-start.12 = (bf16[3,80,384]{2,1,0:T(8,128)(2,1)S(1)}, bf16[3,80,384]{2,1,0:T(8,128)(2,1)S(1)}, u32[]{:S(2)}, u32[]{:S(2)}) collective-permute-start(bf16[3,80,384]{2,1,0:T(8,128)(2,1)S(1)} %get-tuple-element.123.refs_4_.refs_0_), channel_id=1, source_target_pairs={{1,2},{2,1},{5,6},{6,5},{9,10},{10,9},{13,14},{14,13},{17,18},{18,... | collective-permute-start | bytes 552968 | tf_op jit(solution)/shard_map/ppermute | solution.py:32
  48.5 14.2 %collective-permute-start.21 = (bf16[3,80,384]{2,1,0:T(8,128)(2,1)S(1)}, bf16[3,80,384]{2,1,0:T(8,128)(2,1)S(1)}, u32[]{:S(2)}, u32[]{:S(2)}) collective-permute-start(bf16[3,80,384]{2,1,0:T(8,128)(2,1)S(1)} %get-tuple-element.133.refs_10_.refs_6_), channel_id=1, source_target_pairs={{0,1},{1,0},{2,3},{3,2},{4,5},{5,4},{6,7},{7,6},{8,9},{9,8},{10,11... | collective-permute-start | bytes 552968 | tf_op jit(solution)/shard_map/ppermute | solution.py:32
  52.8 10.5 %collective-permute-start.22 = (bf16[3,80,384]{2,1,0:T(8,128)(2,1)S(1)}, bf16[3,80,384]{2,1,0:T(8,128)(2,1)S(1)}, u32[]{:S(2)}, u32[]{:S(2)}) collective-permute-start(bf16[3,80,384]{2,1,0:T(8,128)(2,1)S(1)} %get-tuple-element.133.refs_10_.refs_6_), channel_id=1, source_target_pairs={{1,2},{2,1},{5,6},{6,5},{9,10},{10,9},{13,14},{14,13},{17,18},{18,... | collective-permute-start | bytes 552968 | tf_op jit(solution)/shard_map/ppermute | solution.py:32
  56.9 9.9 %collective-permute-start.14 = (bf16[3,80,384]{2,1,0:T(8,128)(2,1)S(1)}, bf16[3,80,384]{2,1,0:T(8,128)(2,1)S(1)}, u32[]{:S(2)}, u32[]{:S(2)}) collective-permute-start(bf16[3,80,384]{2,1,0:T(8,128)(2,1)S(1)} %collective-permute-done.11.refs_5_.refs_1_), channel_id=1, source_target_pairs={{1,2},{2,1},{5,6},{6,5},{9,10},{10,9},{13,14},{14,13},{17,18},{18,... | collective-permute-start | bytes 552968 | tf_op jit(solution)/shard_map/ppermute | solution.py:32
  58.1 10.1 %collective-permute-start.13 = (bf16[3,80,384]{2,1,0:T(8,128)(2,1)S(1)}, bf16[3,80,384]{2,1,0:T(8,128)(2,1)S(1)}, u32[]{:S(2)}, u32[]{:S(2)}) collective-permute-start(bf16[3,80,384]{2,1,0:T(8,128)(2,1)S(1)} %shard_map.123), channel_id=1, source_target_pairs={{0,1},{1,0},{2,3},{3,2},{4,5},{5,4},{6,7},{7,6},{8,9},{9,8},{10,11... | collective-permute-start | bytes 552968 | tf_op jit(solution)/shard_map/ppermute | solution.py:32
  62.7 8.9 %collective-permute-start.24 = (bf16[3,80,384]{2,1,0:T(8,128)(2,1)S(1)}, bf16[3,80,384]{2,1,0:T(8,128)(2,1)S(1)}, u32[]{:S(2)}, u32[]{:S(2)}) collective-permute-start(bf16[3,80,384]{2,1,0:T(8,128)(2,1)S(1)} %collective-permute-done.21.refs_11_.refs_7_), channel_id=1, source_target_pairs={{1,2},{2,1},{5,6},{6,5},{9,10},{10,9},{13,14},{14,13},{17,18},{18,... | collective-permute-start | bytes 552968 | tf_op jit(solution)/shard_map/ppermute | solution.py:32
  64.0 8.3 %collective-permute-start.23 = (bf16[3,80,384]{2,1,0:T(8,128)(2,1)S(1)}, bf16[3,80,384]{2,1,0:T(8,128)(2,1)S(1)}, u32[]{:S(2)}, u32[]{:S(2)}) collective-permute-start(bf16[3,80,384]{2,1,0:T(8,128)(2,1)S(1)} %shard_map.128), channel_id=1, source_target_pairs={{0,1},{1,0},{2,3},{3,2},{4,5},{5,4},{6,7},{7,6},{8,9},{9,8},{10,11... | collective-permute-start | bytes 552968 | tf_op jit(solution)/shard_map/ppermute | solution.py:32
  68.8 7.4 %collective-permute-start.15 = (bf16[3,80,384]{2,1,0:T(8,128)(2,1)S(1)}, bf16[3,80,384]{2,1,0:T(8,128)(2,1)S(1)}, u32[]{:S(2)}, u32[]{:S(2)}) collective-permute-start(bf16[3,80,384]{2,1,0:T(8,128)(2,1)S(1)} %get-tuple-element.126), channel_id=1, source_target_pairs={{0,1},{1,0},{2,3},{3,2},{4,5},{5,4},{6,7},{7,6},{8,9},{9,8},{10,11... | collective-permute-start | bytes 552968 | tf_op jit(solution)/shard_map/ppermute | solution.py:32
  72.9 7.8 %collective-permute-start.25 = (bf16[3,80,384]{2,1,0:T(8,128)(2,1)S(1)}, bf16[3,80,384]{2,1,0:T(8,128)(2,1)S(1)}, u32[]{:S(2)}, u32[]{:S(2)}) collective-permute-start(bf16[3,80,384]{2,1,0:T(8,128)(2,1)S(1)} %get-tuple-element.136), channel_id=1, source_target_pairs={{0,1},{1,0},{2,3},{3,2},{4,5},{5,4},{6,7},{7,6},{8,9},{9,8},{10,11... | collective-permute-start | bytes 552968 | tf_op jit(solution)/shard_map/ppermute | solution.py:32
  76.9 8.6 %collective-permute-start.27 = (bf16[3,80,384]{2,1,0:T(8,128)(2,1)S(1)}, bf16[3,80,384]{2,1,0:T(8,128)(2,1)S(1)}, u32[]{:S(2)}, u32[]{:S(2)}) collective-permute-start(bf16[3,80,384]{2,1,0:T(8,128)(2,1)S(1)} %get-tuple-element.142), channel_id=1, source_target_pairs={{0,1},{1,0},{2,3},{3,2},{4,5},{5,4},{6,7},{7,6},{8,9},{9,8},{10,11... | collective-permute-start | bytes 552968 | tf_op jit(solution)/shard_map/ppermute | solution.py:32
  81.4 12.8 %collective-permute-start.31 = (bf16[3,80,384]{2,1,0:T(8,128)(2,1)S(1)}, bf16[3,80,384]{2,1,0:T(8,128)(2,1)S(1)}, u32[]{:S(2)}, u32[]{:S(2)}) collective-permute-start(bf16[3,80,384]{2,1,0:T(8,128)(2,1)S(1)} %get-tuple-element.147), channel_id=1, source_target_pairs={{0,1},{1,0},{2,3},{3,2},{4,5},{5,4},{6,7},{7,6},{8,9},{9,8},{10,11... | collective-permute-start | bytes 552968 | tf_op jit(solution)/shard_map/ppermute | solution.py:32
  84.3 9.9 %collective-permute-start.36 = (bf16[3,80,384]{2,1,0:T(8,128)(2,1)S(1)}, bf16[3,80,384]{2,1,0:T(8,128)(2,1)S(1)}, u32[]{:S(2)}, u32[]{:S(2)}) collective-permute-start(bf16[3,80,384]{2,1,0:T(8,128)(2,1)S(1)} %get-tuple-element.153), channel_id=1, source_target_pairs={{1,2},{2,1},{5,6},{6,5},{9,10},{10,9},{13,14},{14,13},{17,18},{18,... | collective-permute-start | bytes 552968 | tf_op jit(solution)/shard_map/ppermute | solution.py:32
  85.7 15.4 %collective-permute-start.29 = (bf16[3,80,384]{2,1,0:T(8,128)(2,1)S(1)}, bf16[3,80,384]{2,1,0:T(8,128)(2,1)S(1)}, u32[]{:S(2)}, u32[]{:S(2)}) collective-permute-start(bf16[3,80,384]{2,1,0:T(8,128)(2,1)S(1)} %get-tuple-element.144.refs_6_.refs_0_), channel_id=1, source_target_pairs={{0,1},{1,0},{2,3},{3,2},{4,5},{5,4},{6,7},{7,6},{8,9},{9,8},{10,11... | collective-permute-start | bytes 552968 | tf_op jit(solution)/shard_map/ppermute | solution.py:32
  89.4 12.4 %collective-permute-start.32 = (bf16[3,80,384]{2,1,0:T(8,128)(2,1)S(1)}, bf16[3,80,384]{2,1,0:T(8,128)(2,1)S(1)}, u32[]{:S(2)}, u32[]{:S(2)}) collective-permute-start(bf16[3,80,384]{2,1,0:T(8,128)(2,1)S(1)} %get-tuple-element.144.refs_6_.refs_0_), channel_id=1, source_target_pairs={{1,2},{2,1},{5,6},{6,5},{9,10},{10,9},{13,14},{14,13},{17,18},{18,... | collective-permute-start | bytes 552968 | tf_op jit(solution)/shard_map/ppermute | solution.py:32
  94.4 15.9 %collective-permute-start.37 = (bf16[3,80,384]{2,1,0:T(8,128)(2,1)S(1)}, bf16[3,80,384]{2,1,0:T(8,128)(2,1)S(1)}, u32[]{:S(2)}, u32[]{:S(2)}) collective-permute-start(bf16[3,80,384]{2,1,0:T(8,128)(2,1)S(1)} %get-tuple-element.154.refs_12_.refs_6_), channel_id=1, source_target_pairs={{0,1},{1,0},{2,3},{3,2},{4,5},{5,4},{6,7},{7,6},{8,9},{9,8},{10,11... | collective-permute-start | bytes 552968 | tf_op jit(solution)/shard_map/ppermute | solution.py:32
  97.0 13.9 %collective-permute-start.38 = (bf16[3,80,384]{2,1,0:T(8,128)(2,1)S(1)}, bf16[3,80,384]{2,1,0:T(8,128)(2,1)S(1)}, u32[]{:S(2)}, u32[]{:S(2)}) collective-permute-start(bf16[3,80,384]{2,1,0:T(8,128)(2,1)S(1)} %get-tuple-element.154.refs_12_.refs_6_), channel_id=1, source_target_pairs={{1,2},{2,1},{5,6},{6,5},{9,10},{10,9},{13,14},{14,13},{17,18},{18,... | collective-permute-start | bytes 552968 | tf_op jit(solution)/shard_map/ppermute | solution.py:32
  101.1 12.6 %collective-permute-start.34 = (bf16[3,80,384]{2,1,0:T(8,128)(2,1)S(1)}, bf16[3,80,384]{2,1,0:T(8,128)(2,1)S(1)}, u32[]{:S(2)}, u32[]{:S(2)}) collective-permute-start(bf16[3,80,384]{2,1,0:T(8,128)(2,1)S(1)} %collective-permute-done.29.refs_7_.refs_1_), channel_id=1, source_target_pairs={{1,2},{2,1},{5,6},{6,5},{9,10},{10,9},{13,14},{14,13},{17,18},{18,... | collective-permute-start | bytes 552968 | tf_op jit(solution)/shard_map/ppermute | solution.py:32
  102.3 11.3 %collective-permute-start.33 = (bf16[3,80,384]{2,1,0:T(8,128)(2,1)S(1)}, bf16[3,80,384]{2,1,0:T(8,128)(2,1)S(1)}, u32[]{:S(2)}, u32[]{:S(2)}) collective-permute-start(bf16[3,80,384]{2,1,0:T(8,128)(2,1)S(1)} %shard_map.135), channel_id=1, source_target_pairs={{0,1},{1,0},{2,3},{3,2},{4,5},{5,4},{6,7},{7,6},{8,9},{9,8},{10,11... | collective-permute-start | bytes 552968 | tf_op jit(solution)/shard_map/ppermute | solution.py:32
  111.5 6.5 %collective-permute-start.39 = (bf16[3,80,384]{2,1,0:T(8,128)(2,1)S(1)}, bf16[3,80,384]{2,1,0:T(8,128)(2,1)S(1)}, u32[]{:S(2)}, u32[]{:S(2)}) collective-permute-start(bf16[3,80,384]{2,1,0:T(8,128)(2,1)S(1)} %shard_map.139), channel_id=1, source_target_pairs={{0,1},{1,0},{2,3},{3,2},{4,5},{5,4},{6,7},{7,6},{8,9},{9,8},{10,11... | collective-permute-start | bytes 552968 | tf_op jit(solution)/shard_map/ppermute | solution.py:32
  114.3 7.7 %collective-permute-start.35 = (bf16[3,80,384]{2,1,0:T(8,128)(2,1)S(1)}, bf16[3,80,384]{2,1,0:T(8,128)(2,1)S(1)}, u32[]{:S(2)}, u32[]{:S(2)}) collective-permute-start(bf16[3,80,384]{2,1,0:T(8,128)(2,1)S(1)} %get-tuple-element.150), channel_id=1, source_target_pairs={{0,1},{1,0},{2,3},{3,2},{4,5},{5,4},{6,7},{7,6},{8,9},{9,8},{10,11... | collective-permute-start | bytes 552968 | tf_op jit(solution)/shard_map/ppermute | solution.py:32
  114.4 7.6 %collective-permute-start.42 = (bf16[3,80,384]{2,1,0:T(8,128)(2,1)S(1)}, bf16[3,80,384]{2,1,0:T(8,128)(2,1)S(1)}, u32[]{:S(2)}, u32[]{:S(2)}) collective-permute-start(bf16[3,80,384]{2,1,0:T(8,128)(2,1)S(1)} %get-tuple-element.165), channel_id=1, source_target_pairs={{1,2},{2,1},{5,6},{6,5},{9,10},{10,9},{13,14},{14,13},{17,18},{18,... | collective-permute-start | bytes 552968 | tf_op jit(solution)/shard_map/ppermute | solution.py:32
  118.7 8.4 %collective-permute-start.41 = (bf16[3,80,384]{2,1,0:T(8,128)(2,1)S(1)}, bf16[3,80,384]{2,1,0:T(8,128)(2,1)S(1)}, u32[]{:S(2)}, u32[]{:S(2)}) collective-permute-start(bf16[3,80,384]{2,1,0:T(8,128)(2,1)S(1)} %get-tuple-element.160), channel_id=1, source_target_pairs={{0,1},{1,0},{2,3},{3,2},{4,5},{5,4},{6,7},{7,6},{8,9},{9,8},{10,11... | collective-permute-start | bytes 552968 | tf_op jit(solution)/shard_map/ppermute | solution.py:32
  120.5 6.7 %collective-permute-start.46 = (bf16[3,80,384]{2,1,0:T(8,128)(2,1)S(1)}, bf16[3,80,384]{2,1,0:T(8,128)(2,1)S(1)}, u32[]{:S(2)}, u32[]{:S(2)}) collective-permute-start(bf16[3,80,384]{2,1,0:T(8,128)(2,1)S(1)} %get-tuple-element.170), channel_id=1, source_target_pairs={{1,2},{2,1},{5,6},{6,5},{9,10},{10,9},{13,14},{14,13},{17,18},{18,... | collective-permute-start | bytes 552968 | tf_op jit(solution)/shard_map/ppermute | solution.py:32
  122.6 8.4 %collective-permute-start.43 = (bf16[3,80,384]{2,1,0:T(8,128)(2,1)S(1)}, bf16[3,80,384]{2,1,0:T(8,128)(2,1)S(1)}, u32[]{:S(2)}, u32[]{:S(2)}) collective-permute-start(bf16[3,80,384]{2,1,0:T(8,128)(2,1)S(1)} %get-tuple-element.166), channel_id=1, source_target_pairs={{0,1},{1,0},{2,3},{3,2},{4,5},{5,4},{6,7},{7,6},{8,9},{9,8},{10,11... | collective-permute-start | bytes 552968 | tf_op jit(solution)/shard_map/ppermute | solution.py:32
  127.8 14.0 %collective-permute-start.47 = (bf16[3,80,384]{2,1,0:T(8,128)(2,1)S(1)}, bf16[3,80,384]{2,1,0:T(8,128)(2,1)S(1)}, u32[]{:S(2)}, u32[]{:S(2)}) collective-permute-start(bf16[3,80,384]{2,1,0:T(8,128)(2,1)S(1)} %get-tuple-element.171), channel_id=1, source_target_pairs={{0,1},{1,0},{2,3},{3,2},{4,5},{5,4},{6,7},{7,6},{8,9},{9,8},{10,11... | collective-permute-start | bytes 552968 | tf_op jit(solution)/shard_map/ppermute | solution.py:32
  130.4 11.4 %collective-permute-start.52 = (bf16[3,80,384]{2,1,0:T(8,128)(2,1)S(1)}, bf16[3,80,384]{2,1,0:T(8,128)(2,1)S(1)}, u32[]{:S(2)}, u32[]{:S(2)}) collective-permute-start(bf16[3,80,384]{2,1,0:T(8,128)(2,1)S(1)} %get-tuple-element.177), channel_id=1, source_target_pairs={{1,2},{2,1},{5,6},{6,5},{9,10},{10,9},{13,14},{14,13},{17,18},{18,... | collective-permute-start | bytes 552968 | tf_op jit(solution)/shard_map/ppermute | solution.py:32
  131.2 14.9 %collective-permute-start.48 = (bf16[3,80,384]{2,1,0:T(8,128)(2,1)S(1)}, bf16[3,80,384]{2,1,0:T(8,128)(2,1)S(1)}, u32[]{:S(2)}, u32[]{:S(2)}) collective-permute-start(bf16[3,80,384]{2,1,0:T(8,128)(2,1)S(1)} %get-tuple-element.168.refs_6_.refs_0_), channel_id=1, source_target_pairs={{1,2},{2,1},{5,6},{6,5},{9,10},{10,9},{13,14},{14,13},{17,18},{18,... | collective-permute-start | bytes 552968 | tf_op jit(solution)/shard_map/ppermute | solution.py:32
  132.1 19.0 %collective-permute-start.45 = (bf16[3,80,384]{2,1,0:T(8,128)(2,1)S(1)}, bf16[3,80,384]{2,1,0:T(8,128)(2,1)S(1)}, u32[]{:S(2)}, u32[]{:S(2)}) collective-permute-start(bf16[3,80,384]{2,1,0:T(8,128)(2,1)S(1)} %get-tuple-element.168.refs_6_.refs_0_), channel_id=1, source_target_pairs={{0,1},{1,0},{2,3},{3,2},{4,5},{5,4},{6,7},{7,6},{8,9},{9,8},{10,11... | collective-permute-start | bytes 552968 | tf_op jit(solution)/shard_map/ppermute | solution.py:32
  142.0 13.2 %collective-permute-start.53 = (bf16[3,80,384]{2,1,0:T(8,128)(2,1)S(1)}, bf16[3,80,384]{2,1,0:T(8,128)(2,1)S(1)}, u32[]{:S(2)}, u32[]{:S(2)}) collective-permute-start(bf16[3,80,384]{2,1,0:T(8,128)(2,1)S(1)} %get-tuple-element.178.refs_12_.refs_6_), channel_id=1, source_target_pairs={{0,1},{1,0},{2,3},{3,2},{4,5},{5,4},{6,7},{7,6},{8,9},{9,8},{10,11... | collective-permute-start | bytes 552968 | tf_op jit(solution)/shard_map/ppermute | solution.py:32
  142.1 13.8 %collective-permute-start.54 = (bf16[3,80,384]{2,1,0:T(8,128)(2,1)S(1)}, bf16[3,80,384]{2,1,0:T(8,128)(2,1)S(1)}, u32[]{:S(2)}, u32[]{:S(2)}) collective-permute-start(bf16[3,80,384]{2,1,0:T(8,128)(2,1)S(1)} %get-tuple-element.178.refs_12_.refs_6_), channel_id=1, source_target_pairs={{1,2},{2,1},{5,6},{6,5},{9,10},{10,9},{13,14},{14,13},{17,18},{18,... | collective-permute-start | bytes 552968 | tf_op jit(solution)/shard_map/ppermute | solution.py:32
  146.7 14.4 %collective-permute-start.49 = (bf16[3,80,384]{2,1,0:T(8,128)(2,1)S(1)}, bf16[3,80,384]{2,1,0:T(8,128)(2,1)S(1)}, u32[]{:S(2)}, u32[]{:S(2)}) collective-permute-start(bf16[3,80,384]{2,1,0:T(8,128)(2,1)S(1)} %shard_map.146), channel_id=1, source_target_pairs={{0,1},{1,0},{2,3},{3,2},{4,5},{5,4},{6,7},{7,6},{8,9},{9,8},{10,11... | collective-permute-start | bytes 552968 | tf_op jit(solution)/shard_map/ppermute | solution.py:32
  151.0 10.0 %collective-permute-start.50 = (bf16[3,80,384]{2,1,0:T(8,128)(2,1)S(1)}, bf16[3,80,384]{2,1,0:T(8,128)(2,1)S(1)}, u32[]{:S(2)}, u32[]{:S(2)}) collective-permute-start(bf16[3,80,384]{2,1,0:T(8,128)(2,1)S(1)} %collective-permute-done.45.refs_7_.refs_1_), channel_id=1, source_target_pairs={{1,2},{2,1},{5,6},{6,5},{9,10},{10,9},{13,14},{14,13},{17,18},{18,... | collective-permute-start | bytes 552968 | tf_op jit(solution)/shard_map/ppermute | solution.py:32
  155.1 7.3 %collective-permute-start.56 = (bf16[3,80,384]{2,1,0:T(8,128)(2,1)S(1)}, bf16[3,80,384]{2,1,0:T(8,128)(2,1)S(1)}, u32[]{:S(2)}, u32[]{:S(2)}) collective-permute-start(bf16[3,80,384]{2,1,0:T(8,128)(2,1)S(1)} %collective-permute-done.53.refs_13_.refs_7_), channel_id=1, source_target_pairs={{1,2},{2,1},{5,6},{6,5},{9,10},{10,9},{13,14},{14,13},{17,18},{18,... | collective-permute-start | bytes 552968 | tf_op jit(solution)/shard_map/ppermute | solution.py:32
  156.4 9.2 %collective-permute-start.55 = (bf16[3,80,384]{2,1,0:T(8,128)(2,1)S(1)}, bf16[3,80,384]{2,1,0:T(8,128)(2,1)S(1)}, u32[]{:S(2)}, u32[]{:S(2)}) collective-permute-start(bf16[3,80,384]{2,1,0:T(8,128)(2,1)S(1)} %shard_map.150), channel_id=1, source_target_pairs={{0,1},{1,0},{2,3},{3,2},{4,5},{5,4},{6,7},{7,6},{8,9},{9,8},{10,11... | collective-permute-start | bytes 552968 | tf_op jit(solution)/shard_map/ppermute | solution.py:32
  161.7 7.1 %collective-permute-start.51 = (bf16[3,80,384]{2,1,0:T(8,128)(2,1)S(1)}, bf16[3,80,384]{2,1,0:T(8,128)(2,1)S(1)}, u32[]{:S(2)}, u32[]{:S(2)}) collective-permute-start(bf16[3,80,384]{2,1,0:T(8,128)(2,1)S(1)} %get-tuple-element.174), channel_id=1, source_target_pairs={{0,1},{1,0},{2,3},{3,2},{4,5},{5,4},{6,7},{7,6},{8,9},{9,8},{10,11... | collective-permute-start | bytes 552968 | tf_op jit(solution)/shard_map/ppermute | solution.py:32
  161.8 7.0 %collective-permute-start.58 = (bf16[3,80,384]{2,1,0:T(8,128)(2,1)S(1)}, bf16[3,80,384]{2,1,0:T(8,128)(2,1)S(1)}, u32[]{:S(2)}, u32[]{:S(2)}) collective-permute-start(bf16[3,80,384]{2,1,0:T(8,128)(2,1)S(1)} %get-tuple-element.192), channel_id=1, source_target_pairs={{1,2},{2,1},{5,6},{6,5},{9,10},{10,9},{13,14},{14,13},{17,18},{18,... | collective-permute-start | bytes 552968 | tf_op jit(solution)/shard_map/ppermute | solution.py:32
  166.2 7.5 %collective-permute-start.57 = (bf16[3,80,384]{2,1,0:T(8,128)(2,1)S(1)}, bf16[3,80,384]{2,1,0:T(8,128)(2,1)S(1)}, u32[]{:S(2)}, u32[]{:S(2)}) collective-permute-start(bf16[3,80,384]{2,1,0:T(8,128)(2,1)S(1)} %get-tuple-element.187), channel_id=1, source_target_pairs={{0,1},{1,0},{2,3},{3,2},{4,5},{5,4},{6,7},{7,6},{8,9},{9,8},{10,11... | collective-permute-start | bytes 552968 | tf_op jit(solution)/shard_map/ppermute | solution.py:32
  169.4 13.3 %collective-permute-start.59 = (bf16[3,80,384]{2,1,0:T(8,128)(2,1)S(1)}, bf16[3,80,384]{2,1,0:T(8,128)(2,1)S(1)}, u32[]{:S(2)}, u32[]{:S(2)}) collective-permute-start(bf16[3,80,384]{2,1,0:T(8,128)(2,1)S(1)} %get-tuple-element.193), channel_id=1, source_target_pairs={{0,1},{1,0},{2,3},{3,2},{4,5},{5,4},{6,7},{7,6},{8,9},{9,8},{10,11... | collective-permute-start | bytes 552968 | tf_op jit(solution)/shard_map/ppermute | solution.py:32
  172.2 10.5 %collective-permute-start.60 = (bf16[3,80,384]{2,1,0:T(8,128)(2,1)S(1)}, bf16[3,80,384]{2,1,0:T(8,128)(2,1)S(1)}, u32[]{:S(2)}, u32[]{:S(2)}) collective-permute-start(bf16[3,80,384]{2,1,0:T(8,128)(2,1)S(1)} %get-tuple-element.194), channel_id=1, source_target_pairs={{1,2},{2,1},{5,6},{6,5},{9,10},{10,9},{13,14},{14,13},{17,18},{18,... | collective-permute-start | bytes 552968 | tf_op jit(solution)/shard_map/ppermute | solution.py:32
  174.4 11.5 %collective-permute-start.67 = (bf16[3,80,384]{2,1,0:T(8,128)(2,1)S(1)}, bf16[3,80,384]{2,1,0:T(8,128)(2,1)S(1)}, u32[]{:S(2)}, u32[]{:S(2)}) collective-permute-start(bf16[3,80,384]{2,1,0:T(8,128)(2,1)S(1)} %get-tuple-element.200), channel_id=1, source_target_pairs={{0,1},{1,0},{2,3},{3,2},{4,5},{5,4},{6,7},{7,6},{8,9},{9,8},{10,11... | collective-permute-start | bytes 552968 | tf_op jit(solution)/shard_map/ppermute | solution.py:32
  177.3 8.5 %collective-permute-start.68 = (bf16[3,80,384]{2,1,0:T(8,128)(2,1)S(1)}, bf16[3,80,384]{2,1,0:T(8,128)(2,1)S(1)}, u32[]{:S(2)}, u32[]{:S(2)}) collective-permute-start(bf16[3,80,384]{2,1,0:T(8,128)(2,1)S(1)} %get-tuple-element.201), channel_id=1, source_target_pairs={{1,2},{2,1},{5,6},{6,5},{9,10},{10,9},{13,14},{14,13},{17,18},{18,... | collective-permute-start | bytes 552968 | tf_op jit(solution)/shard_map/ppermute | solution.py:32
  182.8 8.6 %collective-permute-start.61 = (bf16[3,80,384]{2,1,0:T(8,128)(2,1)S(1)}, bf16[3,80,384]{2,1,0:T(8,128)(2,1)S(1)}, u32[]{:S(2)}, u32[]{:S(2)}) collective-permute-start(bf16[3,80,384]{2,1,0:T(8,128)(2,1)S(1)} %get-tuple-element.195.refs_6_.refs_0_), channel_id=1, source_target_pairs={{0,1},{1,0},{2,3},{3,2},{4,5},{5,4},{6,7},{7,6},{8,9},{9,8},{10,11... | collective-permute-start | bytes 552968 | tf_op jit(solution)/shard_map/ppermute | solution.py:32
  186.0 9.3 %collective-permute-start.69 = (bf16[3,80,384]{2,1,0:T(8,128)(2,1)S(1)}, bf16[3,80,384]{2,1,0:T(8,128)(2,1)S(1)}, u32[]{:S(2)}, u32[]{:S(2)}) collective-permute-start(bf16[3,80,384]{2,1,0:T(8,128)(2,1)S(1)} %get-tuple-element.202.refs_12_.refs_6_), channel_id=1, source_target_pairs={{0,1},{1,0},{2,3},{3,2},{4,5},{5,4},{6,7},{7,6},{8,9},{9,8},{10,11... | collective-permute-start | bytes 552968 | tf_op jit(solution)/shard_map/ppermute | solution.py:32
  187.1 10.4 %collective-permute-start.62 = (bf16[3,80,384]{2,1,0:T(8,128)(2,1)S(1)}, bf16[3,80,384]{2,1,0:T(8,128)(2,1)}, u32[]{:S(2)}, u32[]{:S(2)}) collective-permute-start(bf16[3,80,384]{2,1,0:T(8,128)(2,1)S(1)} %get-tuple-element.195.refs_6_.refs_0_), channel_id=1, source_target_pairs={{1,2},{2,1},{5,6},{6,5},{9,10},{10,9},{13,14},{14,13},{17,18},{18,... | collective-permute-start | bytes 552968 | tf_op jit(solution)/shard_map/ppermute | solution.py:32
  188.5 13.7 %collective-permute-start.70 = (bf16[3,80,384]{2,1,0:T(8,128)(2,1)S(1)}, bf16[3,80,384]{2,1,0:T(8,128)(2,1)}, u32[]{:S(2)}, u32[]{:S(2)}) collective-permute-start(bf16[3,80,384]{2,1,0:T(8,128)(2,1)S(1)} %get-tuple-element.202.refs_12_.refs_6_), channel_id=1, source_target_pairs={{1,2},{2,1},{5,6},{6,5},{9,10},{10,9},{13,14},{14,13},{17,18},{18,... | collective-permute-start | bytes 552968 | tf_op jit(solution)/shard_map/ppermute | solution.py:32
  191.4 10.9 %collective-permute-start.64 = (bf16[3,80,384]{2,1,0:T(8,128)(2,1)S(1)}, bf16[3,80,384]{2,1,0:T(8,128)(2,1)}, u32[]{:S(2)}, u32[]{:S(2)}) collective-permute-start(bf16[3,80,384]{2,1,0:T(8,128)(2,1)S(1)} %collective-permute-done.61.refs_7_.refs_1_), channel_id=1, source_target_pairs={{1,2},{2,1},{5,6},{6,5},{9,10},{10,9},{13,14},{14,13},{17,18},{18,... | collective-permute-start | bytes 552968 | tf_op jit(solution)/shard_map/ppermute | solution.py:32
  195.3 8.9 %collective-permute-start.72 = (bf16[3,80,384]{2,1,0:T(8,128)(2,1)S(1)}, bf16[3,80,384]{2,1,0:T(8,128)(2,1)}, u32[]{:S(2)}, u32[]{:S(2)}) collective-permute-start(bf16[3,80,384]{2,1,0:T(8,128)(2,1)S(1)} %collective-permute-done.69.refs_13_.refs_7_), channel_id=1, source_target_pairs={{1,2},{2,1},{5,6},{6,5},{9,10},{10,9},{13,14},{14,13},{17,18},{18,... | collective-permute-start | bytes 552968 | tf_op jit(solution)/shard_map/ppermute | solution.py:32
  197.6 32.8 %collective-permute-start.63 = (bf16[3,80,384]{2,1,0:T(8,128)(2,1)}, bf16[3,80,384]{2,1,0:T(8,128)(2,1)}, u32[]{:S(2)}, u32[]{:S(2)}) collective-permute-start(bf16[3,80,384]{2,1,0:T(8,128)(2,1)} %collective-permute-done.62.refs_9_.refs_3_), channel_id=1, source_target_pairs={{0,1},{1,0},{2,3},{3,2},{4,5},{5,4},{6,7},{7,6},{8,9},{9,8},{10,11... | collective-permute-start | bytes 552968 | tf_op jit(solution)/shard_map/ppermute | solution.py:32
  202.2 28.1 %collective-permute-start.71 = (bf16[3,80,384]{2,1,0:T(8,128)(2,1)}, bf16[3,80,384]{2,1,0:T(8,128)(2,1)}, u32[]{:S(2)}, u32[]{:S(2)}) collective-permute-start(bf16[3,80,384]{2,1,0:T(8,128)(2,1)} %collective-permute-done.70.refs_15_.refs_9_), channel_id=1, source_target_pairs={{0,1},{1,0},{2,3},{3,2},{4,5},{5,4},{6,7},{7,6},{8,9},{9,8},{10,11... | collective-permute-start | bytes 552968 | tf_op jit(solution)/shard_map/ppermute | solution.py:32
  202.3 28.1 %collective-permute-start.65 = (bf16[3,80,384]{2,1,0:T(8,128)(2,1)}, bf16[3,80,384]{2,1,0:T(8,128)(2,1)}, u32[]{:S(2)}, u32[]{:S(2)}) collective-permute-start(bf16[3,80,384]{2,1,0:T(8,128)(2,1)} %collective-permute-done.64.refs_11_.refs_5_), channel_id=1, source_target_pairs={{0,1},{1,0},{2,3},{3,2},{4,5},{5,4},{6,7},{7,6},{8,9},{9,8},{10,11... | collective-permute-start | bytes 552968 | tf_op jit(solution)/shard_map/ppermute | solution.py:32
  204.2 26.1 %collective-permute-start.73 = (bf16[3,80,384]{2,1,0:T(8,128)(2,1)}, bf16[3,80,384]{2,1,0:T(8,128)(2,1)}, u32[]{:S(2)}, u32[]{:S(2)}) collective-permute-start(bf16[3,80,384]{2,1,0:T(8,128)(2,1)} %collective-permute-done.72.refs_17_.refs_11_), channel_id=1, source_target_pairs={{0,1},{1,0},{2,3},{3,2},{4,5},{5,4},{6,7},{7,6},{8,9},{9,8},{10,11... | collective-permute-start | bytes 552968 | tf_op jit(solution)/shard_map/ppermute | solution.py:32
  206.4 8.0 %collective-permute-start.76 = (f32[80,4]{1,0:T(8,128)S(1)}, f32[80,4]{1,0:T(8,128)S(1)}, u32[]{:S(2)}, u32[]{:S(2)}) collective-permute-start(f32[80,4]{1,0:T(8,128)S(1)} %copy.31.refs_4_), channel_id=1, source_target_pairs={{0,1},{1,0},{2,3},{3,2},{4,5},{5,4},{6,7},{7,6},{8,9},{9,8},{10,11... | collective-permute-start | bytes 3848 | tf_op jit(solution)/shard_map/ppermute | solution.py:32
  219.3 9.0 %collective-permute-start.80 = (f32[80,4]{1,0:T(8,128)S(1)}, f32[80,4]{1,0:T(8,128)S(1)}, u32[]{:S(2)}, u32[]{:S(2)}) collective-permute-start(f32[80,4]{1,0:T(8,128)S(1)} %collective-permute-done.79.refs_9_), channel_id=1, source_target_pairs={{0,1},{1,0},{2,3},{3,2},{4,5},{5,4},{6,7},{7,6},{8,9},{9,8},{10,11... | collective-permute-start | bytes 3848 | tf_op jit(solution)/shard_map/ppermute | solution.py:32
  245.1 8.3 %collective-permute-start.75 = (bf16[2,128,512]{2,1,0:T(8,128)(2,1)S(1)}, bf16[2,128,512]{2,1,0:T(8,128)(2,1)S(1)}, u32[]{:S(2)}, u32[]{:S(2)}) collective-permute-start(bf16[2,128,512]{2,1,0:T(8,128)(2,1)S(1)} %slice_bitcast_fusion), channel_id=1, source_target_pairs={{0,8},{4,12},{8,0},{12,4},{1,9},{5,13},{9,1},{13,5},{2,10},{6,14},... | collective-permute-start | bytes 786440 | tf_op jit(solution)/shard_map/ppermute | solution.py:32
  (44 other events, 207.5 us)

commit v3 on v2

--- a/solution.py
+++ b/solution.py
@@ -8,7 +8,7 @@
 from jax.sharding import PartitionSpec as P
 
 F32, BF16 = jnp.float32, jnp.bfloat16
-VMEM_BYTES = 48 << 20
+VMEM_BYTES = 26 << 20
 
 
 def line_pairs(n, gather, step):
@@ -113,53 +113,66 @@
         def _():
             for p in range(n):
                 for k, value in enumerate((gate, up, back)):
-                    outs[h * n + p][k] = value[p * rows : (p + 1) * rows]
-
-
-def mid_kernel(deps, *refs):
-    own, right, left, out, product = refs[deps:]
+                    outs[h * n + p][pl.ds(k * rows, rows), :] = value[p * rows : (p + 1) * rows]
+
+
+def thirds(value):
+    high = value.astype(BF16)
+    rest = value - high.astype(F32)
+    middle = rest.astype(BF16)
+    return high, middle, (rest - middle.astype(F32)).astype(BF16)
+
+
+def mid_kernel(deps, others, *refs):
+    own, right, left, *rest = refs[deps:]
+    earlier, (out, product) = rest[:others], rest[others:]
+    rows, tile = own.shape[0] // 3, own.shape[1]
     total = own[...].astype(F32) + right[...].astype(F32) + left[...].astype(F32)
-    gate, up, back = total[0], total[1], total[2]
+    gate, up, back = (total[k * rows : (k + 1) * rows] for k in range(3))
     sig = jax.nn.sigmoid(gate)
     hidden = (gate * sig * up).astype(BF16)
     delta = back.astype(BF16).astype(F32)
-    out[0] = hidden
-    out[1] = (delta * up * sig * (1.0 + gate * (1.0 - sig))).astype(BF16)
-    out[2] = (delta * (gate * sig)).astype(BF16)
+    out[0:rows, :] = hidden
+    out[rows : 2 * rows, :] = (delta * up * sig * (1.0 + gate * (1.0 - sig))).astype(BF16)
+    out[2 * rows : 3 * rows, :] = (delta * (gate * sig)).astype(BF16)
     prod = hidden.astype(F32) * back
     lanes = product.shape[1]
     acc = prod[:, 0:lanes]
-    for k in range(1, prod.shape[1] // lanes):
+    for k in range(1, tile // lanes):
         acc = acc + prod[:, k * lanes : (k + 1) * lanes]
     product[...] = acc
-
-
-def step_kernel(deps, select, add, scal, *refs):
-    refs = list(refs[deps:])
-    ins, outs = refs[: 2 * (select + add)], refs[2 * (select + add) :]
-    if select:
-        a, b, out = ins[0], ins[1], outs[0]
-        out[...] = jnp.where(scal[scal.shape[0] - 1] > 0, a[...], b[...])
-    if add:
-        for k in range(add):
-            a, b = ins[2 * (select + k)], ins[2 * (select + k) + 1]
-            outs[select + k][...] = (a[...].astype(F32) + b[...].astype(F32)).astype(BF16)
+    if others:
+        partial = [ref[...] for ref in earlier] + [acc]
+        ones, fill = jnp.ones((8, lanes), BF16), jnp.zeros((lanes - rows, lanes), F32)
+        lines = []
+        for e in range(len(partial) // 2):
+            wide = jnp.concatenate([partial[2 * e] + partial[2 * e + 1], fill], axis=0)
+            total = sum(dot(ones, part, ((1,), (1,))) for part in thirds(wide))[0:1]
+            lines += [part.astype(F32) for part in thirds(total)]
+        extra = out.shape[0] - 3 * rows
+        lines.append(jnp.zeros((extra - len(lines), lanes), F32))
+        out[3 * rows :, :] = jnp.zeros((extra, tile), BF16)
+        out[3 * rows :, 0:lanes] = jnp.concatenate(lines, axis=0).astype(BF16)
+
+
+def part_of(scal, n, q, group, start, size):
+    span = pl.ds(start, size)
+    if len(group) == 1:
+        return group[0][span, :]
+    return jnp.where(scal[n + q] > 0, group[0][span, :], group[1][span, :])
 
 
 def load_rows(scal, n, which, pieces):
-    values = [pieces[0][which]]
-    for q, pair in enumerate(pieces[1:], 1):
-        if len(pair) == 1:
-            values.append(pair[0][which])
-        else:
-            values.append(jnp.where(scal[n + q] > 0, pair[0][which], pair[1][which]))
-    return jnp.concatenate(values, axis=0)
+    rows = pieces[0][0].shape[0] // 48 * 16
+    return jnp.concatenate(
+        [part_of(scal, n, q, group, which * rows, rows) for q, group in enumerate(pieces)], axis=0
+    )
 
 
 def split_pieces(refs, sizes):
     halves, at = [], 0
     for _ in range(2):
-        pieces = [refs[at]]
+        pieces = [refs[at : at + 1]]
         at += 1
         for size in sizes:
             pieces.append(refs[at : at + size])
@@ -168,12 +181,16 @@
     return halves, refs[at:]
 
 
-def out_kernel(n, expert, has_prev, sizes, scal, *refs):
+def out_kernel(n, expert, has_prev, last, sizes, deps, scal, *refs):
+    refs = refs[deps:]
     w_refs, refs = refs[:n], refs[n:]
     if has_prev:
         prev, refs = refs[:2], refs[2:]
     halves, refs = split_pieces(refs, sizes)
-    gw, uw, dw, near, far, token, eo, idl = refs
+    gw, uw, dw, near, far, token, *refs = refs
+    if last:
+        near_p, far_p, *refs, held = refs
+    eo, idl = refs
     step = pl.program_id(0)
 
     for h in range(2):
@@ -203,6 +220,8 @@
             which[place, 0] = layer.astype(which.dtype)
             which[place, 1] = back.astype(which.dtype)
         token[...] = jnp.zeros_like(token)
+        if last:
+            send_products(scal, w_refs, expert + 1, halves[1], held, near_p, far_p)
 
 
 def grad_kernel(n, has_prev, sizes, scal, in_ref, cot_ref, *refs):
@@ -221,33 +240,34 @@
             dg[0] = dot(load_rows(scal, n, 0, halves[h]), cot_ref[...], ((0,), (0,))).astype(BF16)
 
 
-def home_kernel(n, local, sizes, scal, *refs):
-    w_refs, own, refs = refs[:n], refs[n], refs[n + 1 :]
-    pairs = []
-    for size in sizes:
-        pairs.append(refs[:size])
-        refs = refs[size:]
-    near, far, held = refs
-    held[0] = own[...]
-    for q, pair in enumerate(pairs, 1):
-        held[q] = (
-            pair[0][...]
-            if len(pair) == 1
-            else jnp.where(scal[n + q] > 0, pair[0][...], pair[1][...])
-        )
+def send_products(scal, w_refs, local, pieces, held, near, far):
+    n, (_, extra, lanes) = len(w_refs), held.shape
+    first = pieces[0][0].shape[0] - extra
+    for q, group in enumerate(pieces):
+        held[q] = part_of(scal, n, q, group, first, extra)[:, 0:lanes]
     experts_all, tokens = w_refs[0].shape
     ids = lax.broadcasted_iota(jnp.int32, (experts_all, tokens), 0)
     sums = [jnp.zeros((experts_all, tokens), F32) for _ in range(n)]
     for e in range(local):
-        for k, (position, _, hit) in enumerate(routing(scal, w_refs, e, own.shape[0])):
-            column = held[position][:, e : e + 1]
-            value = jnp.sum(jnp.where(hit, column, 0.0), axis=0, keepdims=True)
+        for k, (position, _, hit) in enumerate(routing(scal, w_refs, e, lanes)):
+            found = dot(held[position], hit.astype(F32).astype(BF16))
+            value = found[3 * e : 3 * e + 1] + found[3 * e + 1 : 3 * e + 2] + found[3 * e + 2 : 3 * e + 3]
             sums[k] = sums[k] + jnp.where(ids == scal[2 * n] + e, value, 0.0)
     for k in range(n):
         if k < n // 2:
             near[k] = sums[k]
         else:
             far[k - n // 2] = sums[k]
+
+
+def pack_kernel(ids, combine, tokens, grads, pack, dense):
+    pack[0] = tokens[...]
+    pack[1] = grads[...]
+    expert = lax.broadcasted_iota(jnp.int32, dense.shape, 0)
+    total = jnp.zeros(dense.shape, F32)
+    for k in range(ids.shape[0]):
+        total = total + jnp.where(expert == ids[k : k + 1, :], combine[k : k + 1, :], 0.0)
+    dense[...] = total
 
 
 def whole_spec(shape):
@@ -315,7 +335,15 @@
 
     ids_t, combine_t = expert_ids.T, combine.T
     named = ids_t[:, None, :] == jnp.arange(experts_all, dtype=jnp.int32)[None, :, None]
-    dense = jnp.sum(jnp.where(named, combine_t[:, None, :], 0.0), axis=0)
+    pack, dense = call(
+        pack_kernel,
+        1,
+        [spec_of(ids_t), spec_of(combine_t), spec_of(tokens), spec_of(out_grad)],
+        [whole_spec((2, count, width)), whole_spec((experts_all, count))],
+        [like((2, count, width)), like((experts_all, count), F32)],
+        choose * experts_all * count,
+        8 * count * width,
+    )(ids_t, combine_t, tokens, out_grad)
 
     along_x, across = Line("expert", chips, 2), Line("expert", peers, 1)
     swap = [(2 * x + c, 2 * x + 1 - c) for x in range(chips) for c in range(2)]
@@ -327,13 +355,15 @@
         ]
         return found + [across.send(piece, swap) for piece in found]
 
-    packs = gather_blocks(jnp.stack([tokens, out_grad]))
     w_all = gather_blocks(dense)
+    packs = gather_blocks(pack)
     w_specs, pack_specs = [spec_of(w) for w in w_all], [spec_of(p) for p in packs]
 
     mac = all_rows * width * hidden
     weight_bytes = 2 * width * hidden
-    piece_shape = (3, rows, tile)
+    piece_shape = (3 * rows, tile)
+    extra = -(-3 * local // 16) * 16
+    wide_shape = (3 * rows + extra, tile)
     piece_bytes = 2 * 3 * rows * tile
     slot_shape = (all_rows, width)
 
@@ -353,29 +383,20 @@
         )(scal, *deps, *w_all, *packs, gate_weight, up_weight, down_weight)
         return (inputs, cot), [parts[:n], parts[n:]]
 
-    def mid(own, right, left, deps):
+    def mid(e, h, totals, products, deps=()):
+        others = products if e == local - 1 and h == 1 else []
+        shape = wide_shape if others else piece_shape
         return call(
-            functools.partial(mid_kernel, len(deps)),
+            functools.partial(mid_kernel, len(deps), len(others)),
             1,
-            [ANY_SPEC] * len(deps) + [whole_spec(piece_shape)] * 3,
-            [whole_spec(piece_shape), whole_spec((rows, 128))],
-            [like(piece_shape), like((rows, 128), F32)],
+            [ANY_SPEC] * len(deps)
+            + [whole_spec(piece_shape)] * 3
+            + [whole_spec((rows, 128))] * len(others),
+            [whole_spec(shape), whole_spec((rows, 128))],
+            [like(shape), like((rows, 128), F32)],
             20 * rows * tile,
             4 * piece_bytes,
-        )(*deps, own, right, left)
-
-    def step(select, adds, deps=()):
-        pairs = ([select] if select is not None else []) + list(adds)
-        flat = [x for pair in pairs for x in pair]
-        return call(
-            functools.partial(step_kernel, len(deps), int(select is not None), len(adds)),
-            1,
-            [SMEM_SPEC] + [ANY_SPEC] * len(deps) + [whole_spec(piece_shape)] * len(flat),
-            [whole_spec(piece_shape)] * len(pairs),
-            [like(piece_shape)] * len(pairs),
-            3 * rows * tile * len(pairs),
-            3 * piece_bytes * len(pairs),
-        )(scal, *deps, *flat)
+        )(*deps, *totals, *others)
 
     def flatten(halves):
         return [x for pieces in halves for group in pieces for x in group]
@@ -383,23 +404,31 @@
     def sizes_of(pieces):
         return [len(group) for group in pieces[1:]]
 
-    def out(e, halves, prev):
+    def out(e, halves, prev, deps):
         flat = flatten(halves)
+        last = e == local - 1
+        dense_shape = (chips, experts_all, count)
         sum_shape = (chips, 2, count, width)
         return call(
-            functools.partial(out_kernel, n, e, e > 0, sizes_of(halves[0])),
+            functools.partial(out_kernel, n, e, e > 0, last, sizes_of(halves[0]), len(deps)),
             2,
             [SMEM_SPEC]
+            + [ANY_SPEC] * len(deps)
             + w_specs
             + ([whole_spec(sum_shape)] * 2 if e > 0 else [])
-            + [whole_spec(piece_shape)] * len(flat)
+            + [spec_of(x) for x in flat]
             + weight_specs(e),
-            [whole_spec(sum_shape)] * 2 + [whole_spec(TOKEN)],
-            [like(sum_shape, BF16 if e == local - 1 else F32)] * 2 + [like(TOKEN, F32)],
+            [whole_spec(sum_shape)] * 2
+            + [whole_spec(TOKEN)]
+            + ([whole_spec(dense_shape)] * 2 if last else []),
+            [like(sum_shape, BF16 if last else F32)] * 2
+            + [like(TOKEN, F32)]
+            + ([like(dense_shape, F32)] * 2 if last else []),
             6 * mac,
             3 * weight_bytes + len(flat) * piece_bytes,
-            scratch_shapes=[pltpu.VMEM(slot_shape, F32)] * 2,
-        )(scal, *w_all, *prev, *flat, gate_weight, up_weight, down_weight)
+            scratch_shapes=[pltpu.VMEM(slot_shape, F32)] * 2
+            + ([pltpu.VMEM((n, extra, 128), BF16)] if last else []),
+        )(scal, *deps, *w_all, *prev, *flat, gate_weight, up_weight, down_weight)
 
     def grad(e, slots, halves, prev):
         flat = flatten(halves)
@@ -409,7 +438,7 @@
             2,
             [SMEM_SPEC]
             + [whole_spec(slot_shape)] * 2
-            + [whole_spec(piece_shape)] * len(flat)
+            + [spec_of(x) for x in flat]
             + ([ANY_SPEC] * 3 if e > 0 else []),
             weight_specs(e) + [whole_spec(TOKEN)],
             [like(w.shape) for w in (gate_weight, up_weight, down_weight)] + [like(TOKEN, F32)],
@@ -424,54 +453,56 @@
         return along_z.send(value, [(0, 1), (1, 0), (2, 3), (3, 2)])
 
     def inner(value):
-        return along_z.send(value, [(1, 2), (2, 1)])
-
-    products, sums, grads = [], [], []
-
-    def finish(e, slots, halves):
-        nonlocal sums, grads
-        *sums, token_a = out(e, halves, sums)
+        return along_z.send(value, [(1, 2), (2, 1), (0, 0), (3, 3)])
+
+    def unless_end(value):
+        return jnp.where(at_end, jnp.zeros_like(value), value)
+
+    products, sums, grads, home_sums = [], [], [], []
+
+    def finish(e, slots, halves, deps=()):
+        nonlocal sums, grads, home_sums
+        near, far, token_a, *home_sums = out(e, halves, sums, deps)
         *grads, token_b = grad(e, slots, halves, grads)
+        sums = [near, far]
         return token_a, token_b
 
     if swaps:
-        tokens_of, flight, arrived, deps = None, [None, None], None, []
+        flight, arrived, deps, token_b = [None, None], None, [], None
         for e in range(local):
             slots, parts = pre(e, deps)
-            deps, halves = [], []
+            halves, totals = [], []
             for h in range(2):
                 x, last = parts[h], flight[h]
                 if last is None:
-                    a1 = outer(x[3])
-                    send_a2, (send_b2,) = x[2], step(None, [(x[3], a1)])
+                    a1, send_a2 = outer(x[3]), x[2]
                 else:
-                    y, got_a, got_b, wait = last
-                    (send_a1,) = step((x[3], got_b), [], wait)
-                    a1, b1 = outer(send_a1), inner(got_a)
-                    send_a2, send_b2 = step((x[2], b1), [(x[3], a1)])
-                a2, b2 = outer(send_a2), inner(send_b2)
+                    y, got_a, got_b = last
+                    a1, b1 = outer(jnp.where(at_end, x[3], got_b)), inner(got_a)
+                    send_a2 = jnp.where(at_end, x[2], b1)
+                a2, b2 = outer(send_a2), inner(unless_end(add_rounded(x[3], a1)))
                 if last is not None:
                     halves.append([(y,), (got_a,), (a1, got_b), (a2, b1)])
-                send_a3, send_b3 = step(None, [(x[1], b2), (x[2], a2)])
-                a3, b3 = outer(send_a3), inner(send_b3)
-                parts[h] = (x[0], a3, b3)
-            wait_mid, wait_next = [], []
+                a3 = outer(add_rounded(x[1], b2))
+                b3 = inner(unless_end(add_rounded(x[2], a2)))
+                totals.append((x[0], a3, b3))
+            token_a = None
             if e > 0:
                 token_a, token_b = finish(e - 1, arrived, halves)
-                wait_mid, wait_next = [token_a], [token_b]
             for h in range(2):
-                y, product = mid(*parts[h], wait_mid if h == 1 else [])
+                wait = [token_a] if e > 0 and h == 1 else []
+                y, product = mid(e, h, totals[h], products, wait)
                 products.append(product)
-                flight[h] = (y, outer(y), inner(y), wait_next if h == 1 else [])
-            deps = [parts[1][1]] if e > 0 else [parts[0][1]]
+                flight[h] = (y, outer(y), inner(y))
+            deps = [totals[0][1]] if e == 0 else [token_b]
             arrived = slots
         halves = []
         for h in range(2):
-            y, got_a, got_b, _ = flight[h]
+            y, got_a, got_b = flight[h]
             a1, b1 = outer(got_b), inner(got_a)
             a2 = outer(b1)
             halves.append([(y,), (got_a,), (a1, got_b), (a2, b1)])
-        finish(local - 1, arrived, halves)
+        finish(local - 1, arrived, halves, [token_b])
     else:
         begun = []
         for e in range(local):
@@ -480,32 +511,10 @@
         for e in range(local):
             halves = []
             for h in range(2):
-                y, product = mid(*begun[e][1][h], [])
+                y, product = mid(e, h, begun[e][1][h], products)
                 products.append(product)
                 halves.append([(y,)] + along_z.gather(y))
             finish(e, begun[e][0], halves)
-
-    own = jnp.stack(
-        [jnp.sum(products[2 * e] + products[2 * e + 1], axis=1) for e in range(local)], axis=1
-    )
-    if swaps:
-        got_a, got_b = outer(own), inner(own)
-        a1, b1 = outer(got_b), inner(got_a)
-        pairs = [(got_a,), (a1, got_b), (outer(b1), b1)]
-    else:
-        pairs = along_z.gather(own)
-    flat = [x for pair in pairs for x in pair]
-    dense_shape = (chips, experts_all, count)
-    near_p, far_p = call(
-        functools.partial(home_kernel, n, local, [len(pair) for pair in pairs]),
-        1,
-        [SMEM_SPEC] + w_specs + [spec_of(own)] * (1 + len(flat)),
-        [whole_spec(dense_shape)] * 2,
-        [like(dense_shape, F32)] * 2,
-        local * all_rows * count * 4,
-        4 * experts_all * count * n,
-        scratch_shapes=[pltpu.VMEM((n, rows, local), F32)],
-    )(scal, *w_all, own, *flat)
 
     def send_home(near, far, add):
         near = add(near, across.send(far, swap))
@@ -513,7 +522,7 @@
         home = near[0].astype(F32) + right.astype(F32)
         return home if left is None else home + left.astype(F32)
 
-    per_expert = send_home(near_p, far_p, lambda a, b: a + b)
+    per_expert = send_home(*home_sums, lambda a, b: a + b)
     combine_grad = jnp.sum(jnp.where(named, per_expert[None], 0.0), axis=1) / combine_t
     home = send_home(*sums, add_rounded)
     return (home[0].astype(BF16), home[1].astype(BF16), *grads, combine_grad.T)

time: 256 us -> 246 us (0.961)
  Pallas kernels: 58.1 us -> 37.7 us
  starting transfers between devices: 143 us -> 153 us
    pallas_call x35 -> x13, Pallas kernels: 30.2 us -> 13.4 us  [the longest x4 11.5 us: out(): call(functools.partial(out_kernel, n, e, e > 0, last, sizes_of(halves[0])...]
    ppermute x83 -> x78, starting transfers between devices: 143 us -> 153 us  [send(): return lax.ppermute(value, self.axis, wide)]
    pallas_call x4, Pallas kernels: 13.2 us -> 10.6 us  [pre(): call(functools.partial(pre_kernel, n, e, len(deps)), 2, [SMEM_SPEC] + [AN...]
    ppermute x83 -> x78, waiting for transfers between devices: 38.1 us -> 39.5 us  [send(): return lax.ppermute(value, self.axis, wide)]
    unnamed x50 -> x24, local copies, waits for them, and re-layouts: 9.92 us -> 8.87 us
  transfers between devices with their start and end apart: 83 -> 78, of which waited for: 22 -> 13; matrix products, arithmetic and copies ran while one was open for 1% -> 1% of each run, Pallas kernels for 20% -> 12%
where the time goes in v3:
time: 246 us; the launch traced here: 244 us
  starting transfers between devices  153 us (62%)
  waiting for transfers between devices  39.5 us (16%)
  Pallas kernels  37.7 us (15%)
  local copies, waits for them, and re-layouts  9.69 us (4%)
  other arithmetic  2.57 us (1%)
    ppermute x78, starting transfers between devices, send(): return lax.ppermute(value, self.axis, wide)  153 us
    ppermute x78, waiting for transfers between devices, send(): return lax.ppermute(value, self.axis, wide)  39.5 us
    pallas_call x4, Pallas kernels, grad(): call(functools.partial(grad_kernel, n, e > 0, sizes_of(halves[0])), 2, [S...  13.7 us
    pallas_call x4, Pallas kernels, out(): call(functools.partial(out_kernel, n, e, e > 0, last, sizes_of(halves[0])...  11.5 us
    pallas_call x4, Pallas kernels, pre(): call(functools.partial(pre_kernel, n, e, len(deps)), 2, [SMEM_SPEC] + [AN...  10.6 us
    unnamed x24, local copies, waits for them, and re-layouts  8.87 us
  transfers between devices with their start and end apart: 78, of which 13 were waited for; matrix products, arithmetic and copies ran while one was open for 1% of the time, Pallas kernels for 12%

profile of v3, /device:TPU:0, one launch (start us, length us, event | category | flops | bytes accessed | tf_op | source)
XLA Modules:
  0.0 244.4 jit_solution(10062220438321881105)
XLA Ops:
  0.6 0.9 copy-done.6
  1.5 0.9 copy-done.7
  3.8 3.0 %collective-permute-start.3 = (bf16[2,128,512]{2,1,0:T(8,128)(2,1)S(1)}, bf16[2,128,512]{2,1,0:T(8,128)(2,1)S(1)}, u32[]{:S(2)}, u32[]{:S(2)}) collective-permute-start(bf16[2,128,512]{2,1,0:T(8,128)(2,1)S(1)} %get-tuple-element.92.refs_4_.refs_5_), channel_id=1, source_target_pairs={{0,8},{4,12},{8,0},{12,4},{1,9},{5,13},{9,1},{13,5},{2,10},{6,14},... | collective-permute-start | bytes 786440 | tf_op jit(solution)/shard_map/ppermute | solution.py:32
  6.9 6.3 %collective-permute-done.3.refs_5_.refs_6_ = bf16[2,128,512]{2,1,0:T(8,128)(2,1)S(1)} collective-permute-done((bf16[2,128,512]{2,1,0:T(8,128)(2,1)S(1)}, bf16[2,128,512]{2,1,0:T(8,128)(2,1)S(1)}, u32[]{:S(2)}, u32[]{:S(2)}) %collective-permute-start.3) | collective-permute-done | bytes 262176 | tf_op jit(solution)/shard_map/ppermute | solution.py:32
  13.2 1.7 collective-permute-start
  15.1 1.7 collective-permute-done.refs_1_.refs_2_
  16.9 1.1 collective-permute-done.2.refs_3_.refs_4_
  18.0 1.9 copy-done
  19.9 1.9 copy-done.2
  21.8 1.9 copy-done.4
  23.7 2.7 %shard_map.119 = (bf16[320,512]{1,0:T(8,128)(2,1)S(1)}, bf16[320,512]{1,0:T(8,128)(2,1)S(1)}, bf16[240,384]{1,0:T(8,128)(2,1)S(1)}, bf16[240,384]{1,0:T(8,128)(2...) custom-call(s32[10]{0:T(128)S(1)} %stack.35.scal, ...), custom_call_target="tpu_custom_call" | custom-call | flops 754974720 | bytes 3833856 | tf_op jit(solution)/shard_map/pallas_call | solution.py:375
  26.3 1.9 collective-permute-start.6
  28.4 1.8 collective-permute-start.16
  30.4 3.4 %collective-permute-done.6 = bf16[240,384]{1,0:T(8,128)(2,1)S(1)} collective-permute-done((bf16[240,384]{1,0:T(8,128)(2,1)S(1)}, bf16[240,384]{1,0:T(8,128)(2,1)S(1)}, u32[]{:S(2)}, u32[]{:S(2)}) %collective-permute-start.6) | collective-permute-done | bytes 184352 | tf_op jit(solution)/shard_map/ppermute | solution.py:32
  34.6 3.2 %collective-permute-done.9 = bf16[240,384]{1,0:T(8,128)(2,1)S(1)} collective-permute-done((bf16[240,384]{1,0:T(8,128)(2,1)S(1)}, bf16[240,384]{1,0:T(8,128)(2,1)S(1)}, u32[]{:S(2)}, u32[]{:S(2)}) %collective-permute-start.9) | collective-permute-done | bytes 184352 | tf_op jit(solution)/shard_map/ppermute | solution.py:32
  38.5 3.2 %collective-permute-done.16 = bf16[240,384]{1,0:T(8,128)(2,1)S(1)} collective-permute-done((bf16[240,384]{1,0:T(8,128)(2,1)S(1)}, bf16[240,384]{1,0:T(8,128)(2,1)S(1)}, u32[]{:S(2)}, u32[]{:S(2)}) %collective-permute-start.16) | collective-permute-done | bytes 184352 | tf_op jit(solution)/shard_map/ppermute | solution.py:32
  42.5 2.5 %collective-permute-done.19 = bf16[240,384]{1,0:T(8,128)(2,1)S(1)} collective-permute-done((bf16[240,384]{1,0:T(8,128)(2,1)S(1)}, bf16[240,384]{1,0:T(8,128)(2,1)S(1)}, u32[]{:S(2)}, u32[]{:S(2)}) %collective-permute-start.19) | collective-permute-done | bytes 184352 | tf_op jit(solution)/shard_map/ppermute | solution.py:32
  45.8 4.6 %collective-permute-start.8 = (bf16[240,384]{1,0:T(8,128)(2,1)S(1)}, bf16[240,384]{1,0:T(8,128)(2,1)S(1)}, u32[]{:S(2)}, u32[]{:S(2)}) collective-permute-start(bf16[240,384]{1,0:T(8,128)(2,1)S(1)} %add_convert_fusion.23), channel_id=1, source_target_pairs={{0,1},{1,0},{2,3},{3,2},{4,5},{5,4},{6,7},{7,6},{8,9},{9,8},{10,11... | collective-permute-start | bytes 552968 | tf_op jit(solution)/shard_map/ppermute | solution.py:32
  50.5 1.1 collective-permute-start.18
  51.6 4.4 %collective-permute-done.8.refs_1_.refs_0_ = bf16[240,384]{1,0:T(8,128)(2,1)S(1)} collective-permute-done((bf16[240,384]{1,0:T(8,128)(2,1)S(1)}, bf16[240,384]{1,0:T(8,128)(2,1)S(1)}, u32[]{:S(2)}, u32[]{:S(2)}) %collective-permute-start.8) | collective-permute-done | bytes 184352 | tf_op jit(solution)/shard_map/ppermute | solution.py:32
  56.9 3.8 %collective-permute-start.11 = (bf16[240,384]{1,0:T(8,128)(2,1)S(1)}, bf16[240,384]{1,0:T(8,128)(2,1)S(1)}, u32[]{:S(2)}, u32[]{:S(2)}) collective-permute-start(bf16[240,384]{1,0:T(8,128)(2,1)S(1)} %get-tuple-element.99.refs_0_.refs_4_), channel_id=1, source_target_pairs={{0,1},{1,0},{2,3},{3,2},{4,5},{5,4},{6,7},{7,6},{8,9},{9,8},{10,11... | collective-permute-start | bytes 552968 | tf_op jit(solution)/shard_map/ppermute | solution.py:32
  61.8 2.7 %shard_map.121 = (bf16[320,512]{1,0:T(8,128)(2,1)S(1)}, bf16[320,512]{1,0:T(8,128)(2,1)S(1)}, bf16[240,384]{1,0:T(8,128)(2,1)S(1)}, bf16[240,384]{1,0:T(8,128)(2...) custom-call(s32[10]{0:T(128)S(1)} %stack.35.scal, ...), custom_call_target="tpu_custom_call" | custom-call | flops 754974720 | bytes 3833856 | tf_op jit(solution)/shard_map/pallas_call | solution.py:375
  64.5 4.7 %collective-permute-start.13 = (bf16[240,384]{1,0:T(8,128)(2,1)S(1)}, bf16[240,384]{1,0:T(8,128)(2,1)S(1)}, u32[]{:S(2)}, u32[]{:S(2)}) collective-permute-start(bf16[240,384]{1,0:T(8,128)(2,1)S(1)} %broadcast_select_fusion.11), channel_id=1, source_target_pairs={{0,1},{1,0},{2,3},{3,2},{4,5},{5,4},{6,7},{7,6},{8,9},{9,8},{10,11... | collective-permute-start | bytes 552968 | tf_op jit(solution)/shard_map/ppermute | solution.py:32
  69.9 2.0 collective-permute-start.23
  72.6 4.3 %collective-permute-start.15 = (bf16[240,384]{1,0:T(8,128)(2,1)S(1)}, bf16[240,384]{1,0:T(8,128)(2,1)S(1)}, u32[]{:S(2)}, u32[]{:S(2)}) collective-permute-start(bf16[240,384]{1,0:T(8,128)(2,1)S(1)} %broadcast_select_fusion.10), channel_id=1, source_target_pairs={{0,1},{1,0},{2,3},{3,2},{4,5},{5,4},{6,7},{7,6},{8,9},{9,8},{10,11... | collective-permute-start | bytes 552968 | tf_op jit(solution)/shard_map/ppermute | solution.py:32
  76.9 2.8 %collective-permute-start.25 = (bf16[240,384]{1,0:T(8,128)(2,1)S(1)}, bf16[240,384]{1,0:T(8,128)(2,1)S(1)}, u32[]{:S(2)}, u32[]{:S(2)}) collective-permute-start(bf16[240,384]{1,0:T(8,128)(2,1)S(1)} %broadcast_select_fusion.8), channel_id=1, source_target_pairs={{0,1},{1,0},{2,3},{3,2},{4,5},{5,4},{6,7},{7,6},{8,9},{9,8},{10,11... | collective-permute-start | bytes 552968 | tf_op jit(solution)/shard_map/ppermute | solution.py:32
  81.3 7.3 %collective-permute-start.27 = (bf16[240,384]{1,0:T(8,128)(2,1)S(1)}, bf16[240,384]{1,0:T(8,128)(2,1)S(1)}, u32[]{:S(2)}, u32[]{:S(2)}) collective-permute-start(bf16[240,384]{1,0:T(8,128)(2,1)S(1)} %add_convert_fusion.17), channel_id=1, source_target_pairs={{0,1},{1,0},{2,3},{3,2},{4,5},{5,4},{6,7},{7,6},{8,9},{9,8},{10,11... | collective-permute-start | bytes 552968 | tf_op jit(solution)/shard_map/ppermute | solution.py:32
  89.4 3.7 %collective-permute-start.39 = (bf16[240,384]{1,0:T(8,128)(2,1)S(1)}, bf16[240,384]{1,0:T(8,128)(2,1)S(1)}, u32[]{:S(2)}, u32[]{:S(2)}) collective-permute-start(bf16[240,384]{1,0:T(8,128)(2,1)S(1)} %add_convert_fusion.11), channel_id=1, source_target_pairs={{0,1},{1,0},{2,3},{3,2},{4,5},{5,4},{6,7},{7,6},{8,9},{9,8},{10,11... | collective-permute-start | bytes 552968 | tf_op jit(solution)/shard_map/ppermute | solution.py:32
  94.7 2.6 %shard_map.127 = (f32[2,2,128,512]{3,2,1,0:T(8,128)S(1)}, f32[2,2,128,512]{3,2,1,0:T(8,128)S(1)}, f32[8,128]{1,0:T(8,128)S(1)}) custom-call(s32[10]{0:T(128)S(1)} %stack.35.scal, f32[16,128]{1,0:T(8,128)S(1)} %get-tuple-element.91.refs_0_.refs_1_, f32[16,128]{1,0:T(8,128)S(1)} %collective-permute-done.refs_1_.refs_2_, ...), custom_call_target="tpu_custom_call" | custom-call | flops 754974720 | bytes 4571136 | tf_op jit(solution)/shard_map/pallas_call | solution.py:412
  97.3 3.4 %shard_map.123 = (bf16[4,512,768]{2,1,0:T(8,128)(2,1)}, bf16[4,512,768]{2,1,0:T(8,128)(2,1)}, bf16[4,768,512]{2,1,0:T(8,128)(2,1)}, f32[8,128]{1,0:T(8,128)S(1)}) custom-call(s32[10]{0:T(128)S(1)} %stack.35.scal, bf16[320,512]{1,0:T(8,128)(2,1)S(1)} %get-tuple-element.93.in_ref, bf16[320,512]{1,0:T(8,128)(2,1)S(1)} %get-tuple-element.94.cot_ref, ...), custom_call_target="tpu_custom_call" | custom-call | flops 754974720 | bytes 4571136 | tf_op jit(solution)/shard_map/pallas_call | solution.py:436
  100.7 2.7 %shard_map.124 = (bf16[320,512]{1,0:T(8,128)(2,1)S(1)}, bf16[320,512]{1,0:T(8,128)(2,1)S(1)}, bf16[240,384]{1,0:T(8,128)(2,1)S(1)}, bf16[240,384]{1,0:T(8,128)(2...) custom-call(s32[10]{0:T(128)S(1)} %stack.35.scal, ...), custom_call_target="tpu_custom_call" | custom-call | flops 754974720 | bytes 3833856 | tf_op jit(solution)/shard_map/pallas_call | solution.py:375
  103.4 7.6 %collective-permute-start.33 = (bf16[240,384]{1,0:T(8,128)(2,1)S(1)}, bf16[240,384]{1,0:T(8,128)(2,1)S(1)}, u32[]{:S(2)}, u32[]{:S(2)}) collective-permute-start(bf16[240,384]{1,0:T(8,128)(2,1)S(1)} %get-tuple-element.117.refs_0_.refs_6_), channel_id=1, source_target_pairs={{0,1},{1,0},{2,3},{3,2},{4,5},{5,4},{6,7},{7,6},{8,9},{9,8},{10,11... | collective-permute-start | bytes 552968 | tf_op jit(solution)/shard_map/ppermute | solution.py:32
  111.9 3.3 %collective-permute-start.30 = (bf16[240,384]{1,0:T(8,128)(2,1)S(1)}, bf16[240,384]{1,0:T(8,128)(2,1)S(1)}, u32[]{:S(2)}, u32[]{:S(2)}) collective-permute-start(bf16[240,384]{1,0:T(8,128)(2,1)S(1)} %broadcast_select_fusion.7), channel_id=1, source_target_pairs={{0,1},{1,0},{2,3},{3,2},{4,5},{5,4},{6,7},{7,6},{8,9},{9,8},{10,11... | collective-permute-start | bytes 552968 | tf_op jit(solution)/shard_map/ppermute | solution.py:32
  115.3 6.5 %collective-permute-start.43 = (bf16[240,384]{1,0:T(8,128)(2,1)S(1)}, bf16[240,384]{1,0:T(8,128)(2,1)S(1)}, u32[]{:S(2)}, u32[]{:S(2)}) collective-permute-start(bf16[240,384]{1,0:T(8,128)(2,1)S(1)} %broadcast_select_fusion.5), channel_id=1, source_target_pairs={{0,1},{1,0},{2,3},{3,2},{4,5},{5,4},{6,7},{7,6},{8,9},{9,8},{10,11... | collective-permute-start | bytes 552968 | tf_op jit(solution)/shard_map/ppermute | solution.py:32
  124.0 6.4 %collective-permute-start.35 = (bf16[240,384]{1,0:T(8,128)(2,1)S(1)}, bf16[240,384]{1,0:T(8,128)(2,1)S(1)}, u32[]{:S(2)}, u32[]{:S(2)}) collective-permute-start(bf16[240,384]{1,0:T(8,128)(2,1)S(1)} %broadcast_select_fusion.6), channel_id=1, source_target_pairs={{0,1},{1,0},{2,3},{3,2},{4,5},{5,4},{6,7},{7,6},{8,9},{9,8},{10,11... | collective-permute-start | bytes 552968 | tf_op jit(solution)/shard_map/ppermute | solution.py:32
  130.4 3.3 %collective-permute-start.45 = (bf16[240,384]{1,0:T(8,128)(2,1)S(1)}, bf16[240,384]{1,0:T(8,128)(2,1)S(1)}, u32[]{:S(2)}, u32[]{:S(2)}) collective-permute-start(bf16[240,384]{1,0:T(8,128)(2,1)S(1)} %broadcast_select_fusion.4), channel_id=1, source_target_pairs={{0,1},{1,0},{2,3},{3,2},{4,5},{5,4},{6,7},{7,6},{8,9},{9,8},{10,11... | collective-permute-start | bytes 552968 | tf_op jit(solution)/shard_map/ppermute | solution.py:32
  134.5 3.1 %collective-permute-start.32 = (bf16[240,384]{1,0:T(8,128)(2,1)S(1)}, bf16[240,384]{1,0:T(8,128)(2,1)S(1)}, u32[]{:S(2)}, u32[]{:S(2)}) collective-permute-start(bf16[240,384]{1,0:T(8,128)(2,1)S(1)} %add_convert_fusion.14), channel_id=1, source_target_pairs={{0,1},{1,0},{2,3},{3,2},{4,5},{5,4},{6,7},{7,6},{8,9},{9,8},{10,11... | collective-permute-start | bytes 552968 | tf_op jit(solution)/shard_map/ppermute | solution.py:32
  137.6 0.9 collective-permute-start.36
  138.5 3.6 %collective-permute-start.51 = (bf16[240,384]{1,0:T(8,128)(2,1)S(1)}, bf16[240,384]{1,0:T(8,128)(2,1)S(1)}, u32[]{:S(2)}, u32[]{:S(2)}) collective-permute-start(bf16[240,384]{1,0:T(8,128)(2,1)S(1)} %add_convert_fusion.8), channel_id=1, source_target_pairs={{0,1},{1,0},{2,3},{3,2},{4,5},{5,4},{6,7},{7,6},{8,9},{9,8},{10,11... | collective-permute-start | bytes 552968 | tf_op jit(solution)/shard_map/ppermute | solution.py:32
  143.7 3.4 %shard_map.129 = (bf16[4,512,768]{2,1,0:T(8,128)(2,1)}, bf16[4,512,768]{2,1,0:T(8,128)(2,1)}, bf16[4,768,512]{2,1,0:T(8,128)(2,1)}, f32[8,128]{1,0:T(8,128)S(1)}) custom-call(s32[10]{0:T(128)S(1)} %stack.35.scal, bf16[320,512]{1,0:T(8,128)(2,1)S(1)} %get-tuple-element.120.in_ref, ...), custom_call_target="tpu_custom_call", output_to_operand_aliasing={{0}: (15, {}), {1}: (16, {}), {2}: (17, {})} | custom-call | flops 754974720 | bytes 4571136 | tf_op jit(solution)/shard_map/pallas_call | solution.py:436
  147.2 2.6 %shard_map.130 = (bf16[320,512]{1,0:T(8,128)(2,1)S(1)}, bf16[320,512]{1,0:T(8,128)(2,1)S(1)}, bf16[240,384]{1,0:T(8,128)(2,1)S(1)}, bf16[240,384]{1,0:T(8,128)(2...) custom-call(s32[10]{0:T(128)S(1)} %stack.35.scal, ...), custom_call_target="tpu_custom_call" | custom-call | flops 754974720 | bytes 3833856 | tf_op jit(solution)/shard_map/pallas_call | solution.py:375
  149.8 2.6 %shard_map.131 = (f32[2,2,128,512]{3,2,1,0:T(8,128)S(1)}, f32[2,2,128,512]{3,2,1,0:T(8,128)S(1)}, f32[8,128]{1,0:T(8,128)S(1)}) custom-call(s32[10]{0:T(128)S(1)} %stack.35.scal, f32[16,128]{1,0:T(8,128)S(1)} %get-tuple-element.91.refs_0_.refs_1_, f32[16,128]{1,0:T(8,128)S(1)} %collective-permute-done.refs_1_.refs_2_, ...), custom_call_target="tpu_custom_call" | custom-call | flops 754974720 | bytes 4571136 | tf_op jit(solution)/shard_map/pallas_call | solution.py:412
  152.4 4.8 %collective-permute-start.37 = (bf16[240,384]{1,0:T(8,128)(2,1)S(1)}, bf16[240,384]{1,0:T(8,128)(2,1)S(1)}, u32[]{:S(2)}, u32[]{:S(2)}) collective-permute-start(bf16[240,384]{1,0:T(8,128)(2,1)S(1)} %get-tuple-element.119.refs_0_.refs_6_), channel_id=1, source_target_pairs={{0,1},{1,0},{2,3},{3,2},{4,5},{5,4},{6,7},{7,6},{8,9},{9,8},{10,11... | collective-permute-start | bytes 552968 | tf_op jit(solution)/shard_map/ppermute | solution.py:32
  158.1 4.8 %collective-permute-start.47 = (bf16[240,384]{1,0:T(8,128)(2,1)S(1)}, bf16[240,384]{1,0:T(8,128)(2,1)S(1)}, u32[]{:S(2)}, u32[]{:S(2)}) collective-permute-start(bf16[240,384]{1,0:T(8,128)(2,1)S(1)} %broadcast_select_fusion.3), channel_id=1, source_target_pairs={{0,1},{1,0},{2,3},{3,2},{4,5},{5,4},{6,7},{7,6},{8,9},{9,8},{10,11... | collective-permute-start | bytes 552968 | tf_op jit(solution)/shard_map/ppermute | solution.py:32
  163.6 4.4 %collective-permute-start.55 = (bf16[240,384]{1,0:T(8,128)(2,1)S(1)}, bf16[240,384]{1,0:T(8,128)(2,1)S(1)}, u32[]{:S(2)}, u32[]{:S(2)}) collective-permute-start(bf16[240,384]{1,0:T(8,128)(2,1)S(1)} %broadcast_select_fusion.1), channel_id=1, source_target_pairs={{0,1},{1,0},{2,3},{3,2},{4,5},{5,4},{6,7},{7,6},{8,9},{9,8},{10,11... | collective-permute-start | bytes 552968 | tf_op jit(solution)/shard_map/ppermute | solution.py:32
  168.7 4.2 %collective-permute-start.49 = (bf16[240,384]{1,0:T(8,128)(2,1)S(1)}, bf16[240,384]{1,0:T(8,128)(2,1)S(1)}, u32[]{:S(2)}, u32[]{:S(2)}) collective-permute-start(bf16[240,384]{1,0:T(8,128)(2,1)S(1)} %broadcast_select_fusion.2), channel_id=1, source_target_pairs={{0,1},{1,0},{2,3},{3,2},{4,5},{5,4},{6,7},{7,6},{8,9},{9,8},{10,11... | collective-permute-start | bytes 552968 | tf_op jit(solution)/shard_map/ppermute | solution.py:32
  173.0 4.4 %collective-permute-start.57 = (bf16[240,384]{1,0:T(8,128)(2,1)S(1)}, bf16[240,384]{1,0:T(8,128)(2,1)S(1)}, u32[]{:S(2)}, u32[]{:S(2)}) collective-permute-start(bf16[240,384]{1,0:T(8,128)(2,1)S(1)} %broadcast_select_fusion), channel_id=1, source_target_pairs={{0,1},{1,0},{2,3},{3,2},{4,5},{5,4},{6,7},{7,6},{8,9},{9,8},{10,11... | collective-permute-start | bytes 552968 | tf_op jit(solution)/shard_map/ppermute | solution.py:32
  179.0 6.1 %collective-permute-start.59 = (bf16[240,384]{1,0:T(8,128)(2,1)S(1)}, bf16[240,384]{1,0:T(8,128)(2,1)S(1)}, u32[]{:S(2)}, u32[]{:S(2)}) collective-permute-start(bf16[240,384]{1,0:T(8,128)(2,1)S(1)} %add_convert_fusion.5), channel_id=1, source_target_pairs={{0,1},{1,0},{2,3},{3,2},{4,5},{5,4},{6,7},{7,6},{8,9},{9,8},{10,11... | collective-permute-start | bytes 552968 | tf_op jit(solution)/shard_map/ppermute | solution.py:32
  185.9 4.8 %collective-permute-start.67 = (bf16[240,384]{1,0:T(8,128)(2,1)S(1)}, bf16[240,384]{1,0:T(8,128)(2,1)S(1)}, u32[]{:S(2)}, u32[]{:S(2)}) collective-permute-start(bf16[240,384]{1,0:T(8,128)(2,1)S(1)} %add_convert_fusion.2), channel_id=1, source_target_pairs={{0,1},{1,0},{2,3},{3,2},{4,5},{5,4},{6,7},{7,6},{8,9},{9,8},{10,11... | collective-permute-start | bytes 552968 | tf_op jit(solution)/shard_map/ppermute | solution.py:32
  191.4 2.6 %shard_map.134 = (f32[2,2,128,512]{3,2,1,0:T(8,128)S(1)}, f32[2,2,128,512]{3,2,1,0:T(8,128)S(1)}, f32[8,128]{1,0:T(8,128)S(1)}) custom-call(s32[10]{0:T(128)S(1)} %stack.35.scal, f32[16,128]{1,0:T(8,128)S(1)} %get-tuple-element.91.refs_0_.refs_1_, f32[16,128]{1,0:T(8,128)S(1)} %collective-permute-done.refs_1_.refs_2_, ...), custom_call_target="tpu_custom_call" | custom-call | flops 754974720 | bytes 4571136 | tf_op jit(solution)/shard_map/pallas_call | solution.py:412
  194.2 0.8 shard_map.136
  195.0 6.0 %collective-permute-start.69 = (bf16[256,384]{1,0:T(8,128)(2,1)S(1)}, bf16[256,384]{1,0:T(8,128)(2,1)S(1)}, u32[]{:S(2)}, u32[]{:S(2)}) collective-permute-start(bf16[256,384]{1,0:T(8,128)(2,1)S(1)} %get-tuple-element.163.refs_13_.refs_6_), channel_id=1, source_target_pairs={{0,1},{1,0},{2,3},{3,2},{4,5},{5,4},{6,7},{7,6},{8,9},{9,8},{10,11... | collective-permute-start | bytes 589832 | tf_op jit(solution)/shard_map/ppermute | solution.py:32
  201.7 3.5 %collective-permute-done.69.refs_14_.refs_7_ = bf16[256,384]{1,0:T(8,128)(2,1)S(1)} collective-permute-done((bf16[256,384]{1,0:T(8,128)(2,1)S(1)}, bf16[256,384]{1,0:T(8,128)(2,1)S(1)}, u32[]{:S(2)}, u32[]{:S(2)}) %collective-permute-start.69) | collective-permute-done | bytes 196640 | tf_op jit(solution)/shard_map/ppermute | solution.py:32
  207.2 0.9 collective-permute-start.64
  208.1 7.6 %collective-permute-start.71 = (bf16[256,384]{1,0:T(8,128)(2,1)S(1)}, bf16[256,384]{1,0:T(8,128)(2,1)S(1)}, u32[]{:S(2)}, u32[]{:S(2)}) collective-permute-start(bf16[256,384]{1,0:T(8,128)(2,1)S(1)} %collective-permute-done.70.refs_16_.refs_9_), channel_id=1, source_target_pairs={{0,1},{1,0},{2,3},{3,2},{4,5},{5,4},{6,7},{7,6},{8,9},{9,8},{10,11... | collective-permute-start | bytes 589832 | tf_op jit(solution)/shard_map/ppermute | solution.py:32
  215.8 1.9 collective-permute-start.63
  217.8 2.5 %collective-permute-start.65 = (bf16[240,384]{1,0:T(8,128)(2,1)S(1)}, bf16[240,384]{1,0:T(8,128)(2,1)S(1)}, u32[]{:S(2)}, u32[]{:S(2)}) collective-permute-start(bf16[240,384]{1,0:T(8,128)(2,1)S(1)} %collective-permute-done.64.refs_12_.refs_5_), channel_id=1, source_target_pairs={{0,1},{1,0},{2,3},{3,2},{4,5},{5,4},{6,7},{7,6},{8,9},{9,8},{10,11... | collective-permute-start | bytes 552968 | tf_op jit(solution)/shard_map/ppermute | solution.py:32
  220.3 3.4 %shard_map.133 = (bf16[4,512,768]{2,1,0:T(8,128)(2,1)}, bf16[4,512,768]{2,1,0:T(8,128)(2,1)}, bf16[4,768,512]{2,1,0:T(8,128)(2,1)}, f32[8,128]{1,0:T(8,128)S(1)}) custom-call(s32[10]{0:T(128)S(1)} %stack.35.scal, bf16[320,512]{1,0:T(8,128)(2,1)S(1)} %get-tuple-element.110.in_ref, ...), custom_call_target="tpu_custom_call", output_to_operand_aliasing={{0}: (15, {}), {1}: (16, {}), {2}: (17, {})} | custom-call | flops 754974720 | bytes 4571136 | tf_op jit(solution)/shard_map/pallas_call | solution.py:436
  223.7 1.7 collective-permute-done.65.refs_11_.refs_4_
  225.4 3.8 %shard_map.137 = (bf16[2,2,128,512]{3,2,1,0:T(8,128)(2,1)S(1)}, bf16[2,2,128,512]{3,2,1,0:T(8,128)(2,1)S(1)}, f32[8,128]{1,0:T(8,128)}, f32[2,16,128]{2,1,0:T(8,128)S(1)}, f32[2,16,128]{2,1,0:T(8,128)S(1)}) custom-call(s32[10]{0:T(128)S(1)} %stack.35.scal, f32[8,128]{1,0:T(8,128)S(1)} %get-tuple-element.145.refs_0_, ...), custom_call_target="tpu_custom_call" | custom-call | flops 754974720 | bytes 4571136 | tf_op jit(solution)/shard_map/pallas_call | solution.py:412
  230.4 1.5 collective-permute-start.77
  231.9 3.4 %shard_map.138 = (bf16[4,512,768]{2,1,0:T(8,128)(2,1)}, bf16[4,512,768]{2,1,0:T(8,128)(2,1)}, bf16[4,768,512]{2,1,0:T(8,128)(2,1)}, f32[8,128]{1,0:T(8,128)}) custom-call(s32[10]{0:T(128)S(1)} %stack.35.scal, bf16[320,512]{1,0:T(8,128)(2,1)S(1)} %get-tuple-element.166.in_ref, ...), custom_call_target="tpu_custom_call", output_to_operand_aliasing={{0}: (15, {}), {1}: (16, {}), {2}: (17, {})} | custom-call | flops 754974720 | bytes 4571136 | tf_op jit(solution)/shard_map/pallas_call | solution.py:436
  236.7 6.9 %collective-permute-done.75 = bf16[2,128,512]{2,1,0:T(8,128)(2,1)S(1)} collective-permute-done((bf16[2,128,512]{2,1,0:T(8,128)(2,1)S(1)}, bf16[2,128,512]{2,1,0:T(8,128)(2,1)S(1)}, u32[]{:S(2)}, u32[]{:S(2)}) %collective-permute-start.75) | collective-permute-done | bytes 262176 | tf_op jit(solution)/shard_map/ppermute | solution.py:32
  243.7 0.7 slice_bitcast_fusion.2
  (183 shorter events, 29.1 us)
Async XLA Ops:
  3.8 9.3 %collective-permute-start.3 = (bf16[2,128,512]{2,1,0:T(8,128)(2,1)S(1)}, bf16[2,128,512]{2,1,0:T(8,128)(2,1)S(1)}, u32[]{:S(2)}, u32[]{:S(2)}) collective-permute-start(bf16[2,128,512]{2,1,0:T(8,128)(2,1)S(1)} %get-tuple-element.92.refs_4_.refs_5_), channel_id=1, source_target_pairs={{0,8},{4,12},{8,0},{12,4},{1,9},{5,13},{9,1},{13,5},{2,10},{6,14},... | collective-permute-start | bytes 786440 | tf_op jit(solution)/shard_map/ppermute | solution.py:32
  6.8 11.1 %collective-permute-start.4 = (bf16[2,128,512]{2,1,0:T(8,128)(2,1)S(1)}, bf16[2,128,512]{2,1,0:T(8,128)(2,1)S(1)}, u32[]{:S(2)}, u32[]{:S(2)}) collective-permute-start(bf16[2,128,512]{2,1,0:T(8,128)(2,1)S(1)} %get-tuple-element.92.refs_4_.refs_5_), channel_id=1, source_target_pairs={{0,4},{4,0},{8,12},{12,8},{1,5},{5,1},{9,13},{13,9},{2,6},{6,2},{1... | collective-permute-start | bytes 786440 | tf_op jit(solution)/shard_map/ppermute | solution.py:32
  26.3 7.5 %collective-permute-start.6 = (bf16[240,384]{1,0:T(8,128)(2,1)S(1)}, bf16[240,384]{1,0:T(8,128)(2,1)S(1)}, u32[]{:S(2)}, u32[]{:S(2)}) collective-permute-start(bf16[240,384]{1,0:T(8,128)(2,1)S(1)} %get-tuple-element.97), channel_id=1, source_target_pairs={{0,1},{1,0},{2,3},{3,2},{4,5},{5,4},{6,7},{7,6},{8,9},{9,8},{10,11... | collective-permute-start | bytes 552968 | tf_op jit(solution)/shard_map/ppermute | solution.py:32
  28.2 9.6 %collective-permute-start.9 = (bf16[240,384]{1,0:T(8,128)(2,1)S(1)}, bf16[240,384]{1,0:T(8,128)(2,1)S(1)}, u32[]{:S(2)}, u32[]{:S(2)}) collective-permute-start(bf16[240,384]{1,0:T(8,128)(2,1)S(1)} %get-tuple-element.98), channel_id=1, source_target_pairs={{0,1},{1,0},{2,3},{3,2},{4,5},{5,4},{6,7},{7,6},{8,9},{9,8},{10,11... | collective-permute-start | bytes 552968 | tf_op jit(solution)/shard_map/ppermute | solution.py:32
  28.4 13.3 %collective-permute-start.16 = (bf16[240,384]{1,0:T(8,128)(2,1)S(1)}, bf16[240,384]{1,0:T(8,128)(2,1)S(1)}, u32[]{:S(2)}, u32[]{:S(2)}) collective-permute-start(bf16[240,384]{1,0:T(8,128)(2,1)S(1)} %get-tuple-element.104), channel_id=1, source_target_pairs={{0,1},{1,0},{2,3},{3,2},{4,5},{5,4},{6,7},{7,6},{8,9},{9,8},{10,11... | collective-permute-start | bytes 552968 | tf_op jit(solution)/shard_map/ppermute | solution.py:32
  30.2 14.8 %collective-permute-start.19 = (bf16[240,384]{1,0:T(8,128)(2,1)S(1)}, bf16[240,384]{1,0:T(8,128)(2,1)S(1)}, u32[]{:S(2)}, u32[]{:S(2)}) collective-permute-start(bf16[240,384]{1,0:T(8,128)(2,1)S(1)} %get-tuple-element.105), channel_id=1, source_target_pairs={{0,1},{1,0},{2,3},{3,2},{4,5},{5,4},{6,7},{7,6},{8,9},{9,8},{10,11... | collective-permute-start | bytes 552968 | tf_op jit(solution)/shard_map/ppermute | solution.py:32
  33.9 11.9 %collective-permute-start.7 = (bf16[240,384]{1,0:T(8,128)(2,1)S(1)}, bf16[240,384]{1,0:T(8,128)(2,1)S(1)}, u32[]{:S(2)}, u32[]{:S(2)}) collective-permute-start(bf16[240,384]{1,0:T(8,128)(2,1)S(1)} %fusion.1), channel_id=1, source_target_pairs={{1,2},{2,1},{0,0},{3,3},{5,6},{6,5},{4,4},{7,7},{9,10},{10,9},{8,8... | collective-permute-start | bytes 552968 | tf_op jit(solution)/shard_map/ppermute | solution.py:32
  37.9 13.7 %collective-permute-start.10 = (bf16[240,384]{1,0:T(8,128)(2,1)S(1)}, bf16[240,384]{1,0:T(8,128)(2,1)S(1)}, u32[]{:S(2)}, u32[]{:S(2)}) collective-permute-start(bf16[240,384]{1,0:T(8,128)(2,1)S(1)} %fusion.2), channel_id=1, source_target_pairs={{1,2},{2,1},{0,0},{3,3},{5,6},{6,5},{4,4},{7,7},{9,10},{10,9},{8,8... | collective-permute-start | bytes 552968 | tf_op jit(solution)/shard_map/ppermute | solution.py:32
  41.8 8.6 %collective-permute-start.17 = (bf16[240,384]{1,0:T(8,128)(2,1)S(1)}, bf16[240,384]{1,0:T(8,128)(2,1)S(1)}, u32[]{:S(2)}, u32[]{:S(2)}) collective-permute-start(bf16[240,384]{1,0:T(8,128)(2,1)S(1)} %fusion.3), channel_id=1, source_target_pairs={{1,2},{2,1},{0,0},{3,3},{5,6},{6,5},{4,4},{7,7},{9,10},{10,9},{8,8... | collective-permute-start | bytes 552968 | tf_op jit(solution)/shard_map/ppermute | solution.py:32
  45.1 15.5 %collective-permute-start.20 = (bf16[240,384]{1,0:T(8,128)(2,1)S(1)}, bf16[240,384]{1,0:T(8,128)(2,1)S(1)}, u32[]{:S(2)}, u32[]{:S(2)}) collective-permute-start(bf16[240,384]{1,0:T(8,128)(2,1)S(1)} %fusion.4), channel_id=1, source_target_pairs={{1,2},{2,1},{0,0},{3,3},{5,6},{6,5},{4,4},{7,7},{9,10},{10,9},{8,8... | collective-permute-start | bytes 552968 | tf_op jit(solution)/shard_map/ppermute | solution.py:32
  45.8 10.2 %collective-permute-start.8 = (bf16[240,384]{1,0:T(8,128)(2,1)S(1)}, bf16[240,384]{1,0:T(8,128)(2,1)S(1)}, u32[]{:S(2)}, u32[]{:S(2)}) collective-permute-start(bf16[240,384]{1,0:T(8,128)(2,1)S(1)} %add_convert_fusion.23), channel_id=1, source_target_pairs={{0,1},{1,0},{2,3},{3,2},{4,5},{5,4},{6,7},{7,6},{8,9},{9,8},{10,11... | collective-permute-start | bytes 552968 | tf_op jit(solution)/shard_map/ppermute | solution.py:32
  50.5 10.1 %collective-permute-start.18 = (bf16[240,384]{1,0:T(8,128)(2,1)S(1)}, bf16[240,384]{1,0:T(8,128)(2,1)S(1)}, u32[]{:S(2)}, u32[]{:S(2)}) collective-permute-start(bf16[240,384]{1,0:T(8,128)(2,1)S(1)} %add_convert_fusion.20), channel_id=1, source_target_pairs={{0,1},{1,0},{2,3},{3,2},{4,5},{5,4},{6,7},{7,6},{8,9},{9,8},{10,11... | collective-permute-start | bytes 552968 | tf_op jit(solution)/shard_map/ppermute | solution.py:32
  56.2 8.3 %collective-permute-start.12 = (bf16[240,384]{1,0:T(8,128)(2,1)S(1)}, bf16[240,384]{1,0:T(8,128)(2,1)S(1)}, u32[]{:S(2)}, u32[]{:S(2)}) collective-permute-start(bf16[240,384]{1,0:T(8,128)(2,1)S(1)} %get-tuple-element.99.refs_0_.refs_4_), channel_id=1, source_target_pairs={{1,2},{2,1},{0,0},{3,3},{5,6},{6,5},{4,4},{7,7},{9,10},{10,9},{8,8... | collective-permute-start | bytes 552968 | tf_op jit(solution)/shard_map/ppermute | solution.py:32
  56.9 12.3 %collective-permute-start.11 = (bf16[240,384]{1,0:T(8,128)(2,1)S(1)}, bf16[240,384]{1,0:T(8,128)(2,1)S(1)}, u32[]{:S(2)}, u32[]{:S(2)}) collective-permute-start(bf16[240,384]{1,0:T(8,128)(2,1)S(1)} %get-tuple-element.99.refs_0_.refs_4_), channel_id=1, source_target_pairs={{0,1},{1,0},{2,3},{3,2},{4,5},{5,4},{6,7},{7,6},{8,9},{9,8},{10,11... | collective-permute-start | bytes 552968 | tf_op jit(solution)/shard_map/ppermute | solution.py:32
  60.8 11.1 %collective-permute-start.21 = (bf16[240,384]{1,0:T(8,128)(2,1)S(1)}, bf16[240,384]{1,0:T(8,128)(2,1)S(1)}, u32[]{:S(2)}, u32[]{:S(2)}) collective-permute-start(bf16[240,384]{1,0:T(8,128)(2,1)S(1)} %get-tuple-element.106.refs_6_.refs_10_), channel_id=1, source_target_pairs={{0,1},{1,0},{2,3},{3,2},{4,5},{5,4},{6,7},{7,6},{8,9},{9,8},{10,11... | collective-permute-start | bytes 552968 | tf_op jit(solution)/shard_map/ppermute | solution.py:32
  61.1 8.8 %collective-permute-start.22 = (bf16[240,384]{1,0:T(8,128)(2,1)S(1)}, bf16[240,384]{1,0:T(8,128)(2,1)S(1)}, u32[]{:S(2)}, u32[]{:S(2)}) collective-permute-start(bf16[240,384]{1,0:T(8,128)(2,1)S(1)} %get-tuple-element.106.refs_6_.refs_10_), channel_id=1, source_target_pairs={{1,2},{2,1},{0,0},{3,3},{5,6},{6,5},{4,4},{7,7},{9,10},{10,9},{8,8... | collective-permute-start | bytes 552968 | tf_op jit(solution)/shard_map/ppermute | solution.py:32
  64.5 15.2 %collective-permute-start.13 = (bf16[240,384]{1,0:T(8,128)(2,1)S(1)}, bf16[240,384]{1,0:T(8,128)(2,1)S(1)}, u32[]{:S(2)}, u32[]{:S(2)}) collective-permute-start(bf16[240,384]{1,0:T(8,128)(2,1)S(1)} %broadcast_select_fusion.11), channel_id=1, source_target_pairs={{0,1},{1,0},{2,3},{3,2},{4,5},{5,4},{6,7},{7,6},{8,9},{9,8},{10,11... | collective-permute-start | bytes 552968 | tf_op jit(solution)/shard_map/ppermute | solution.py:32
  69.9 10.6 %collective-permute-start.23 = (bf16[240,384]{1,0:T(8,128)(2,1)S(1)}, bf16[240,384]{1,0:T(8,128)(2,1)S(1)}, u32[]{:S(2)}, u32[]{:S(2)}) collective-permute-start(bf16[240,384]{1,0:T(8,128)(2,1)S(1)} %broadcast_select_fusion.9), channel_id=1, source_target_pairs={{0,1},{1,0},{2,3},{3,2},{4,5},{5,4},{6,7},{7,6},{8,9},{9,8},{10,11... | collective-permute-start | bytes 552968 | tf_op jit(solution)/shard_map/ppermute | solution.py:32
  71.9 5.0 %collective-permute-start.24 = (bf16[240,384]{1,0:T(8,128)(2,1)S(1)}, bf16[240,384]{1,0:T(8,128)(2,1)S(1)}, u32[]{:S(2)}, u32[]{:S(2)}) collective-permute-start(bf16[240,384]{1,0:T(8,128)(2,1)S(1)} %collective-permute-done.21.refs_7_.refs_11_), channel_id=1, source_target_pairs={{1,2},{2,1},{0,0},{3,3},{5,6},{6,5},{4,4},{7,7},{9,10},{10,9},{8,8... | collective-permute-start | bytes 552968 | tf_op jit(solution)/shard_map/ppermute | solution.py:32
  72.6 16.0 %collective-permute-start.15 = (bf16[240,384]{1,0:T(8,128)(2,1)S(1)}, bf16[240,384]{1,0:T(8,128)(2,1)S(1)}, u32[]{:S(2)}, u32[]{:S(2)}) collective-permute-start(bf16[240,384]{1,0:T(8,128)(2,1)S(1)} %broadcast_select_fusion.10), channel_id=1, source_target_pairs={{0,1},{1,0},{2,3},{3,2},{4,5},{5,4},{6,7},{7,6},{8,9},{9,8},{10,11... | collective-permute-start | bytes 552968 | tf_op jit(solution)/shard_map/ppermute | solution.py:32
  76.9 16.2 %collective-permute-start.25 = (bf16[240,384]{1,0:T(8,128)(2,1)S(1)}, bf16[240,384]{1,0:T(8,128)(2,1)S(1)}, u32[]{:S(2)}, u32[]{:S(2)}) collective-permute-start(bf16[240,384]{1,0:T(8,128)(2,1)S(1)} %broadcast_select_fusion.8), channel_id=1, source_target_pairs={{0,1},{1,0},{2,3},{3,2},{4,5},{5,4},{6,7},{7,6},{8,9},{9,8},{10,11... | collective-permute-start | bytes 552968 | tf_op jit(solution)/shard_map/ppermute | solution.py:32
  80.6 8.8 %collective-permute-start.38 = (bf16[240,384]{1,0:T(8,128)(2,1)S(1)}, bf16[240,384]{1,0:T(8,128)(2,1)S(1)}, u32[]{:S(2)}, u32[]{:S(2)}) collective-permute-start(bf16[240,384]{1,0:T(8,128)(2,1)S(1)} %fusion.9), channel_id=1, source_target_pairs={{1,2},{2,1},{0,0},{3,3},{5,6},{6,5},{4,4},{7,7},{9,10},{10,9},{8,8... | collective-permute-start | bytes 552968 | tf_op jit(solution)/shard_map/ppermute | solution.py:32
  81.3 12.5 %collective-permute-start.27 = (bf16[240,384]{1,0:T(8,128)(2,1)S(1)}, bf16[240,384]{1,0:T(8,128)(2,1)S(1)}, u32[]{:S(2)}, u32[]{:S(2)}) collective-permute-start(bf16[240,384]{1,0:T(8,128)(2,1)S(1)} %add_convert_fusion.17), channel_id=1, source_target_pairs={{0,1},{1,0},{2,3},{3,2},{4,5},{5,4},{6,7},{7,6},{8,9},{9,8},{10,11... | collective-permute-start | bytes 552968 | tf_op jit(solution)/shard_map/ppermute | solution.py:32
  88.7 5.2 %collective-permute-start.28 = (bf16[240,384]{1,0:T(8,128)(2,1)S(1)}, bf16[240,384]{1,0:T(8,128)(2,1)S(1)}, u32[]{:S(2)}, u32[]{:S(2)}) collective-permute-start(bf16[240,384]{1,0:T(8,128)(2,1)S(1)} %fusion.6), channel_id=1, source_target_pairs={{1,2},{2,1},{0,0},{3,3},{5,6},{6,5},{4,4},{7,7},{9,10},{10,9},{8,8... | collective-permute-start | bytes 552968 | tf_op jit(solution)/shard_map/ppermute | solution.py:32
  89.4 21.6 %collective-permute-start.39 = (bf16[240,384]{1,0:T(8,128)(2,1)S(1)}, bf16[240,384]{1,0:T(8,128)(2,1)S(1)}, u32[]{:S(2)}, u32[]{:S(2)}) collective-permute-start(bf16[240,384]{1,0:T(8,128)(2,1)S(1)} %add_convert_fusion.11), channel_id=1, source_target_pairs={{0,1},{1,0},{2,3},{3,2},{4,5},{5,4},{6,7},{7,6},{8,9},{9,8},{10,11... | collective-permute-start | bytes 552968 | tf_op jit(solution)/shard_map/ppermute | solution.py:32
  93.1 17.8 %collective-permute-start.40 = (bf16[240,384]{1,0:T(8,128)(2,1)S(1)}, bf16[240,384]{1,0:T(8,128)(2,1)S(1)}, u32[]{:S(2)}, u32[]{:S(2)}) collective-permute-start(bf16[240,384]{1,0:T(8,128)(2,1)S(1)} %fusion.10), channel_id=1, source_target_pairs={{1,2},{2,1},{0,0},{3,3},{5,6},{6,5},{4,4},{7,7},{9,10},{10,9},{8,8... | collective-permute-start | bytes 552968 | tf_op jit(solution)/shard_map/ppermute | solution.py:32
  94.0 17.9 %collective-permute-start.29 = (bf16[240,384]{1,0:T(8,128)(2,1)S(1)}, bf16[240,384]{1,0:T(8,128)(2,1)S(1)}, u32[]{:S(2)}, u32[]{:S(2)}) collective-permute-start(bf16[240,384]{1,0:T(8,128)(2,1)S(1)} %get-tuple-element.117.refs_0_.refs_6_), channel_id=1, source_target_pairs={{1,2},{2,1},{0,0},{3,3},{5,6},{6,5},{4,4},{7,7},{9,10},{10,9},{8,8... | collective-permute-start | bytes 552968 | tf_op jit(solution)/shard_map/ppermute | solution.py:32
  103.4 18.4 %collective-permute-start.33 = (bf16[240,384]{1,0:T(8,128)(2,1)S(1)}, bf16[240,384]{1,0:T(8,128)(2,1)S(1)}, u32[]{:S(2)}, u32[]{:S(2)}) collective-permute-start(bf16[240,384]{1,0:T(8,128)(2,1)S(1)} %get-tuple-element.117.refs_0_.refs_6_), channel_id=1, source_target_pairs={{0,1},{1,0},{2,3},{3,2},{4,5},{5,4},{6,7},{7,6},{8,9},{9,8},{10,11... | collective-permute-start | bytes 552968 | tf_op jit(solution)/shard_map/ppermute | solution.py:32
  111.1 11.4 %collective-permute-start.41 = (bf16[240,384]{1,0:T(8,128)(2,1)S(1)}, bf16[240,384]{1,0:T(8,128)(2,1)S(1)}, u32[]{:S(2)}, u32[]{:S(2)}) collective-permute-start(bf16[240,384]{1,0:T(8,128)(2,1)S(1)} %get-tuple-element.125.refs_6_.refs_12_), channel_id=1, source_target_pairs={{0,1},{1,0},{2,3},{3,2},{4,5},{5,4},{6,7},{7,6},{8,9},{9,8},{10,11... | collective-permute-start | bytes 552968 | tf_op jit(solution)/shard_map/ppermute | solution.py:32
  111.9 11.3 %collective-permute-start.30 = (bf16[240,384]{1,0:T(8,128)(2,1)S(1)}, bf16[240,384]{1,0:T(8,128)(2,1)S(1)}, u32[]{:S(2)}, u32[]{:S(2)}) collective-permute-start(bf16[240,384]{1,0:T(8,128)(2,1)S(1)} %broadcast_select_fusion.7), channel_id=1, source_target_pairs={{0,1},{1,0},{2,3},{3,2},{4,5},{5,4},{6,7},{7,6},{8,9},{9,8},{10,11... | collective-permute-start | bytes 552968 | tf_op jit(solution)/shard_map/ppermute | solution.py:32
  115.3 18.4 %collective-permute-start.43 = (bf16[240,384]{1,0:T(8,128)(2,1)S(1)}, bf16[240,384]{1,0:T(8,128)(2,1)S(1)}, u32[]{:S(2)}, u32[]{:S(2)}) collective-permute-start(bf16[240,384]{1,0:T(8,128)(2,1)S(1)} %broadcast_select_fusion.5), channel_id=1, source_target_pairs={{0,1},{1,0},{2,3},{3,2},{4,5},{5,4},{6,7},{7,6},{8,9},{9,8},{10,11... | collective-permute-start | bytes 552968 | tf_op jit(solution)/shard_map/ppermute | solution.py:32
  122.5 7.9 %collective-permute-start.44 = (bf16[240,384]{1,0:T(8,128)(2,1)S(1)}, bf16[240,384]{1,0:T(8,128)(2,1)S(1)}, u32[]{:S(2)}, u32[]{:S(2)}) collective-permute-start(bf16[240,384]{1,0:T(8,128)(2,1)S(1)} %collective-permute-done.41.refs_7_.refs_13_), channel_id=1, source_target_pairs={{1,2},{2,1},{0,0},{3,3},{5,6},{6,5},{4,4},{7,7},{9,10},{10,9},{8,8... | collective-permute-start | bytes 552968 | tf_op jit(solution)/shard_map/ppermute | solution.py:32
  123.3 11.2 %collective-permute-start.31 = (bf16[240,384]{1,0:T(8,128)(2,1)S(1)}, bf16[240,384]{1,0:T(8,128)(2,1)S(1)}, u32[]{:S(2)}, u32[]{:S(2)}) collective-permute-start(bf16[240,384]{1,0:T(8,128)(2,1)S(1)} %fusion.7), channel_id=1, source_target_pairs={{1,2},{2,1},{0,0},{3,3},{5,6},{6,5},{4,4},{7,7},{9,10},{10,9},{8,8... | collective-permute-start | bytes 552968 | tf_op jit(solution)/shard_map/ppermute | solution.py:32
  124.0 13.6 %collective-permute-start.35 = (bf16[240,384]{1,0:T(8,128)(2,1)S(1)}, bf16[240,384]{1,0:T(8,128)(2,1)S(1)}, u32[]{:S(2)}, u32[]{:S(2)}) collective-permute-start(bf16[240,384]{1,0:T(8,128)(2,1)S(1)} %broadcast_select_fusion.6), channel_id=1, source_target_pairs={{0,1},{1,0},{2,3},{3,2},{4,5},{5,4},{6,7},{7,6},{8,9},{9,8},{10,11... | collective-permute-start | bytes 552968 | tf_op jit(solution)/shard_map/ppermute | solution.py:32
  130.4 11.7 %collective-permute-start.45 = (bf16[240,384]{1,0:T(8,128)(2,1)S(1)}, bf16[240,384]{1,0:T(8,128)(2,1)S(1)}, u32[]{:S(2)}, u32[]{:S(2)}) collective-permute-start(bf16[240,384]{1,0:T(8,128)(2,1)S(1)} %broadcast_select_fusion.4), channel_id=1, source_target_pairs={{0,1},{1,0},{2,3},{3,2},{4,5},{5,4},{6,7},{7,6},{8,9},{9,8},{10,11... | collective-permute-start | bytes 552968 | tf_op jit(solution)/shard_map/ppermute | solution.py:32
  134.5 8.4 %collective-permute-start.32 = (bf16[240,384]{1,0:T(8,128)(2,1)S(1)}, bf16[240,384]{1,0:T(8,128)(2,1)S(1)}, u32[]{:S(2)}, u32[]{:S(2)}) collective-permute-start(bf16[240,384]{1,0:T(8,128)(2,1)S(1)} %add_convert_fusion.14), channel_id=1, source_target_pairs={{0,1},{1,0},{2,3},{3,2},{4,5},{5,4},{6,7},{7,6},{8,9},{9,8},{10,11... | collective-permute-start | bytes 552968 | tf_op jit(solution)/shard_map/ppermute | solution.py:32
  137.6 5.3 %collective-permute-start.36 = (bf16[240,384]{1,0:T(8,128)(2,1)S(1)}, bf16[240,384]{1,0:T(8,128)(2,1)S(1)}, u32[]{:S(2)}, u32[]{:S(2)}) collective-permute-start(bf16[240,384]{1,0:T(8,128)(2,1)S(1)} %fusion.8), channel_id=1, source_target_pairs={{1,2},{2,1},{0,0},{3,3},{5,6},{6,5},{4,4},{7,7},{9,10},{10,9},{8,8... | collective-permute-start | bytes 552968 | tf_op jit(solution)/shard_map/ppermute | solution.py:32
  138.5 18.6 %collective-permute-start.51 = (bf16[240,384]{1,0:T(8,128)(2,1)S(1)}, bf16[240,384]{1,0:T(8,128)(2,1)S(1)}, u32[]{:S(2)}, u32[]{:S(2)}) collective-permute-start(bf16[240,384]{1,0:T(8,128)(2,1)S(1)} %add_convert_fusion.8), channel_id=1, source_target_pairs={{0,1},{1,0},{2,3},{3,2},{4,5},{5,4},{6,7},{7,6},{8,9},{9,8},{10,11... | collective-permute-start | bytes 552968 | tf_op jit(solution)/shard_map/ppermute | solution.py:32
  142.2 15.0 %collective-permute-start.52 = (bf16[240,384]{1,0:T(8,128)(2,1)S(1)}, bf16[240,384]{1,0:T(8,128)(2,1)S(1)}, u32[]{:S(2)}, u32[]{:S(2)}) collective-permute-start(bf16[240,384]{1,0:T(8,128)(2,1)S(1)} %fusion.12), channel_id=1, source_target_pairs={{1,2},{2,1},{0,0},{3,3},{5,6},{6,5},{4,4},{7,7},{9,10},{10,9},{8,8... | collective-permute-start | bytes 552968 | tf_op jit(solution)/shard_map/ppermute | solution.py:32
  143.0 15.0 %collective-permute-start.46 = (bf16[240,384]{1,0:T(8,128)(2,1)S(1)}, bf16[240,384]{1,0:T(8,128)(2,1)S(1)}, u32[]{:S(2)}, u32[]{:S(2)}) collective-permute-start(bf16[240,384]{1,0:T(8,128)(2,1)S(1)} %get-tuple-element.119.refs_0_.refs_6_), channel_id=1, source_target_pairs={{1,2},{2,1},{0,0},{3,3},{5,6},{6,5},{4,4},{7,7},{9,10},{10,9},{8,8... | collective-permute-start | bytes 552968 | tf_op jit(solution)/shard_map/ppermute | solution.py:32
  152.4 10.5 %collective-permute-start.37 = (bf16[240,384]{1,0:T(8,128)(2,1)S(1)}, bf16[240,384]{1,0:T(8,128)(2,1)S(1)}, u32[]{:S(2)}, u32[]{:S(2)}) collective-permute-start(bf16[240,384]{1,0:T(8,128)(2,1)S(1)} %get-tuple-element.119.refs_0_.refs_6_), channel_id=1, source_target_pairs={{0,1},{1,0},{2,3},{3,2},{4,5},{5,4},{6,7},{7,6},{8,9},{9,8},{10,11... | collective-permute-start | bytes 552968 | tf_op jit(solution)/shard_map/ppermute | solution.py:32
  157.3 10.7 %collective-permute-start.53 = (bf16[240,384]{1,0:T(8,128)(2,1)S(1)}, bf16[240,384]{1,0:T(8,128)(2,1)S(1)}, u32[]{:S(2)}, u32[]{:S(2)}) collective-permute-start(bf16[240,384]{1,0:T(8,128)(2,1)S(1)} %get-tuple-element.139.refs_6_.refs_12_), channel_id=1, source_target_pairs={{0,1},{1,0},{2,3},{3,2},{4,5},{5,4},{6,7},{7,6},{8,9},{9,8},{10,11... | collective-permute-start | bytes 552968 | tf_op jit(solution)/shard_map/ppermute | solution.py:32
  157.4 6.2 %collective-permute-start.54 = (bf16[240,384]{1,0:T(8,128)(2,1)S(1)}, bf16[240,384]{1,0:T(8,128)(2,1)S(1)}, u32[]{:S(2)}, u32[]{:S(2)}) collective-permute-start(bf16[240,384]{1,0:T(8,128)(2,1)S(1)} %get-tuple-element.139.refs_6_.refs_12_), channel_id=1, source_target_pairs={{1,2},{2,1},{0,0},{3,3},{5,6},{6,5},{4,4},{7,7},{9,10},{10,9},{8,8... | collective-permute-start | bytes 552968 | tf_op jit(solution)/shard_map/ppermute | solution.py:32
  158.1 19.3 %collective-permute-start.47 = (bf16[240,384]{1,0:T(8,128)(2,1)S(1)}, bf16[240,384]{1,0:T(8,128)(2,1)S(1)}, u32[]{:S(2)}, u32[]{:S(2)}) collective-permute-start(bf16[240,384]{1,0:T(8,128)(2,1)S(1)} %broadcast_select_fusion.3), channel_id=1, source_target_pairs={{0,1},{1,0},{2,3},{3,2},{4,5},{5,4},{6,7},{7,6},{8,9},{9,8},{10,11... | collective-permute-start | bytes 552968 | tf_op jit(solution)/shard_map/ppermute | solution.py:32
  162.9 5.8 %collective-permute-start.48 = (bf16[240,384]{1,0:T(8,128)(2,1)S(1)}, bf16[240,384]{1,0:T(8,128)(2,1)S(1)}, u32[]{:S(2)}, u32[]{:S(2)}) collective-permute-start(bf16[240,384]{1,0:T(8,128)(2,1)S(1)} %collective-permute-done.37.refs_1_.refs_7_), channel_id=1, source_target_pairs={{1,2},{2,1},{0,0},{3,3},{5,6},{6,5},{4,4},{7,7},{9,10},{10,9},{8,8... | collective-permute-start | bytes 552968 | tf_op jit(solution)/shard_map/ppermute | solution.py:32
  163.6 14.6 %collective-permute-start.55 = (bf16[240,384]{1,0:T(8,128)(2,1)S(1)}, bf16[240,384]{1,0:T(8,128)(2,1)S(1)}, u32[]{:S(2)}, u32[]{:S(2)}) collective-permute-start(bf16[240,384]{1,0:T(8,128)(2,1)S(1)} %broadcast_select_fusion.1), channel_id=1, source_target_pairs={{0,1},{1,0},{2,3},{3,2},{4,5},{5,4},{6,7},{7,6},{8,9},{9,8},{10,11... | collective-permute-start | bytes 552968 | tf_op jit(solution)/shard_map/ppermute | solution.py:32
  168.7 16.3 %collective-permute-start.49 = (bf16[240,384]{1,0:T(8,128)(2,1)S(1)}, bf16[240,384]{1,0:T(8,128)(2,1)S(1)}, u32[]{:S(2)}, u32[]{:S(2)}) collective-permute-start(bf16[240,384]{1,0:T(8,128)(2,1)S(1)} %broadcast_select_fusion.2), channel_id=1, source_target_pairs={{0,1},{1,0},{2,3},{3,2},{4,5},{5,4},{6,7},{7,6},{8,9},{9,8},{10,11... | collective-permute-start | bytes 552968 | tf_op jit(solution)/shard_map/ppermute | solution.py:32
  173.0 17.6 %collective-permute-start.57 = (bf16[240,384]{1,0:T(8,128)(2,1)S(1)}, bf16[240,384]{1,0:T(8,128)(2,1)S(1)}, u32[]{:S(2)}, u32[]{:S(2)}) collective-permute-start(bf16[240,384]{1,0:T(8,128)(2,1)S(1)} %broadcast_select_fusion), channel_id=1, source_target_pairs={{0,1},{1,0},{2,3},{3,2},{4,5},{5,4},{6,7},{7,6},{8,9},{9,8},{10,11... | collective-permute-start | bytes 552968 | tf_op jit(solution)/shard_map/ppermute | solution.py:32
  178.2 7.6 %collective-permute-start.66 = (bf16[240,384]{1,0:T(8,128)(2,1)S(1)}, bf16[240,384]{1,0:T(8,128)(2,1)S(1)}, u32[]{:S(2)}, u32[]{:S(2)}) collective-permute-start(bf16[240,384]{1,0:T(8,128)(2,1)S(1)} %fusion.15), channel_id=1, source_target_pairs={{1,2},{2,1},{0,0},{3,3},{5,6},{6,5},{4,4},{7,7},{9,10},{10,9},{8,8... | collective-permute-start | bytes 552968 | tf_op jit(solution)/shard_map/ppermute | solution.py:32
  179.0 15.0 %collective-permute-start.59 = (bf16[240,384]{1,0:T(8,128)(2,1)S(1)}, bf16[240,384]{1,0:T(8,128)(2,1)S(1)}, u32[]{:S(2)}, u32[]{:S(2)}) collective-permute-start(bf16[240,384]{1,0:T(8,128)(2,1)S(1)} %add_convert_fusion.5), channel_id=1, source_target_pairs={{0,1},{1,0},{2,3},{3,2},{4,5},{5,4},{6,7},{7,6},{8,9},{9,8},{10,11... | collective-permute-start | bytes 552968 | tf_op jit(solution)/shard_map/ppermute | solution.py:32
  185.1 8.9 %collective-permute-start.60 = (bf16[240,384]{1,0:T(8,128)(2,1)S(1)}, bf16[240,384]{1,0:T(8,128)(2,1)S(1)}, u32[]{:S(2)}, u32[]{:S(2)}) collective-permute-start(bf16[240,384]{1,0:T(8,128)(2,1)S(1)} %fusion.14), channel_id=1, source_target_pairs={{1,2},{2,1},{0,0},{3,3},{5,6},{6,5},{4,4},{7,7},{9,10},{10,9},{8,8... | collective-permute-start | bytes 552968 | tf_op jit(solution)/shard_map/ppermute | solution.py:32
  185.9 8.3 %collective-permute-start.67 = (bf16[240,384]{1,0:T(8,128)(2,1)S(1)}, bf16[240,384]{1,0:T(8,128)(2,1)S(1)}, u32[]{:S(2)}, u32[]{:S(2)}) collective-permute-start(bf16[240,384]{1,0:T(8,128)(2,1)S(1)} %add_convert_fusion.2), channel_id=1, source_target_pairs={{0,1},{1,0},{2,3},{3,2},{4,5},{5,4},{6,7},{7,6},{8,9},{9,8},{10,11... | collective-permute-start | bytes 552968 | tf_op jit(solution)/shard_map/ppermute | solution.py:32
  195.0 10.3 %collective-permute-start.69 = (bf16[256,384]{1,0:T(8,128)(2,1)S(1)}, bf16[256,384]{1,0:T(8,128)(2,1)S(1)}, u32[]{:S(2)}, u32[]{:S(2)}) collective-permute-start(bf16[256,384]{1,0:T(8,128)(2,1)S(1)} %get-tuple-element.163.refs_13_.refs_6_), channel_id=1, source_target_pairs={{0,1},{1,0},{2,3},{3,2},{4,5},{5,4},{6,7},{7,6},{8,9},{9,8},{10,11... | collective-permute-start | bytes 589832 | tf_op jit(solution)/shard_map/ppermute | solution.py:32
  201.0 6.2 %collective-permute-start.61 = (bf16[240,384]{1,0:T(8,128)(2,1)S(1)}, bf16[240,384]{1,0:T(8,128)(2,1)S(1)}, u32[]{:S(2)}, u32[]{:S(2)}) collective-permute-start(bf16[240,384]{1,0:T(8,128)(2,1)S(1)} %get-tuple-element.152.refs_7_.refs_0_), channel_id=1, source_target_pairs={{0,1},{1,0},{2,3},{3,2},{4,5},{5,4},{6,7},{7,6},{8,9},{9,8},{10,11... | collective-permute-start | bytes 552968 | tf_op jit(solution)/shard_map/ppermute | solution.py:32
  201.0 7.1 %collective-permute-start.70 = (bf16[256,384]{1,0:T(8,128)(2,1)S(1)}, bf16[256,384]{1,0:T(8,128)(2,1)S(1)}, u32[]{:S(2)}, u32[]{:S(2)}) collective-permute-start(bf16[256,384]{1,0:T(8,128)(2,1)S(1)} %get-tuple-element.163.refs_13_.refs_6_), channel_id=1, source_target_pairs={{1,2},{2,1},{0,0},{3,3},{5,6},{6,5},{4,4},{7,7},{9,10},{10,9},{8,8... | collective-permute-start | bytes 589832 | tf_op jit(solution)/shard_map/ppermute | solution.py:32
  205.3 10.5 %collective-permute-start.72 = (bf16[256,384]{1,0:T(8,128)(2,1)S(1)}, bf16[256,384]{1,0:T(8,128)(2,1)S(1)}, u32[]{:S(2)}, u32[]{:S(2)}) collective-permute-start(bf16[256,384]{1,0:T(8,128)(2,1)S(1)} %collective-permute-done.69.refs_14_.refs_7_), channel_id=1, source_target_pairs={{1,2},{2,1},{0,0},{3,3},{5,6},{6,5},{4,4},{7,7},{9,10},{10,9},{8,8... | collective-permute-start | bytes 589832 | tf_op jit(solution)/shard_map/ppermute | solution.py:32
  205.9 9.9 %collective-permute-start.62 = (bf16[240,384]{1,0:T(8,128)(2,1)S(1)}, bf16[240,384]{1,0:T(8,128)(2,1)S(1)}, u32[]{:S(2)}, u32[]{:S(2)}) collective-permute-start(bf16[240,384]{1,0:T(8,128)(2,1)S(1)} %get-tuple-element.152.refs_7_.refs_0_), channel_id=1, source_target_pairs={{1,2},{2,1},{0,0},{3,3},{5,6},{6,5},{4,4},{7,7},{9,10},{10,9},{8,8... | collective-permute-start | bytes 552968 | tf_op jit(solution)/shard_map/ppermute | solution.py:32
  207.2 10.5 %collective-permute-start.64 = (bf16[240,384]{1,0:T(8,128)(2,1)S(1)}, bf16[240,384]{1,0:T(8,128)(2,1)S(1)}, u32[]{:S(2)}, u32[]{:S(2)}) collective-permute-start(bf16[240,384]{1,0:T(8,128)(2,1)S(1)} %collective-permute-done.61.refs_8_.refs_1_), channel_id=1, source_target_pairs={{1,2},{2,1},{0,0},{3,3},{5,6},{6,5},{4,4},{7,7},{9,10},{10,9},{8,8... | collective-permute-start | bytes 552968 | tf_op jit(solution)/shard_map/ppermute | solution.py:32
  208.1 15.6 %collective-permute-start.71 = (bf16[256,384]{1,0:T(8,128)(2,1)S(1)}, bf16[256,384]{1,0:T(8,128)(2,1)S(1)}, u32[]{:S(2)}, u32[]{:S(2)}) collective-permute-start(bf16[256,384]{1,0:T(8,128)(2,1)S(1)} %collective-permute-done.70.refs_16_.refs_9_), channel_id=1, source_target_pairs={{0,1},{1,0},{2,3},{3,2},{4,5},{5,4},{6,7},{7,6},{8,9},{9,8},{10,11... | collective-permute-start | bytes 589832 | tf_op jit(solution)/shard_map/ppermute | solution.py:32
  215.7 9.7 %collective-permute-start.73 = (bf16[256,384]{1,0:T(8,128)(2,1)S(1)}, bf16[256,384]{1,0:T(8,128)(2,1)S(1)}, u32[]{:S(2)}, u32[]{:S(2)}) collective-permute-start(bf16[256,384]{1,0:T(8,128)(2,1)S(1)} %collective-permute-done.72.refs_18_.refs_11_), channel_id=1, source_target_pairs={{0,1},{1,0},{2,3},{3,2},{4,5},{5,4},{6,7},{7,6},{8,9},{9,8},{10,11... | collective-permute-start | bytes 589832 | tf_op jit(solution)/shard_map/ppermute | solution.py:32
  215.8 7.9 %collective-permute-start.63 = (bf16[240,384]{1,0:T(8,128)(2,1)S(1)}, bf16[240,384]{1,0:T(8,128)(2,1)S(1)}, u32[]{:S(2)}, u32[]{:S(2)}) collective-permute-start(bf16[240,384]{1,0:T(8,128)(2,1)S(1)} %collective-permute-done.62.refs_10_.refs_3_), channel_id=1, source_target_pairs={{0,1},{1,0},{2,3},{3,2},{4,5},{5,4},{6,7},{7,6},{8,9},{9,8},{10,11... | collective-permute-start | bytes 552968 | tf_op jit(solution)/shard_map/ppermute | solution.py:32
  217.8 7.7 %collective-permute-start.65 = (bf16[240,384]{1,0:T(8,128)(2,1)S(1)}, bf16[240,384]{1,0:T(8,128)(2,1)S(1)}, u32[]{:S(2)}, u32[]{:S(2)}) collective-permute-start(bf16[240,384]{1,0:T(8,128)(2,1)S(1)} %collective-permute-done.64.refs_12_.refs_5_), channel_id=1, source_target_pairs={{0,1},{1,0},{2,3},{3,2},{4,5},{5,4},{6,7},{7,6},{8,9},{9,8},{10,11... | collective-permute-start | bytes 552968 | tf_op jit(solution)/shard_map/ppermute | solution.py:32
  229.2 6.1 %collective-permute-start.74 = (bf16[2,2,128,512]{3,2,1,0:T(8,128)(2,1)S(1)}, bf16[2,2,128,512]{3,2,1,0:T(8,128)(2,1)S(1)}, u32[]{:S(2)}, u32[]{:S(2)}) collective-permute-start(bf16[2,2,128,512]{3,2,1,0:T(8,128)(2,1)S(1)} %get-tuple-element.165), channel_id=1, source_target_pairs={{0,4},{4,0},{8,12},{12,8},{1,5},{5,1},{9,13},{13,9},{2,6},{6,2},{1... | collective-permute-start | bytes 1572872 | tf_op jit(solution)/shard_map/ppermute | solution.py:32
  235.5 8.2 %collective-permute-start.75 = (bf16[2,128,512]{2,1,0:T(8,128)(2,1)S(1)}, bf16[2,128,512]{2,1,0:T(8,128)(2,1)S(1)}, u32[]{:S(2)}, u32[]{:S(2)}) collective-permute-start(bf16[2,128,512]{2,1,0:T(8,128)(2,1)S(1)} %slice_bitcast_fusion), channel_id=1, source_target_pairs={{0,8},{4,12},{8,0},{12,4},{1,9},{5,13},{9,1},{13,5},{2,10},{6,14},... | collective-permute-start | bytes 786440 | tf_op jit(solution)/shard_map/ppermute | solution.py:32
  (26 other events, 156.6 us)

commit v4 on v3

--- a/solution.py
+++ b/solution.py
@@ -88,32 +88,50 @@
     return pl.ds(pl.multiple_of(position * rows, rows), rows)
 
 
+def weight_copies(expert, weights, held, sems):
+    halves = []
+    for h in range(2):
+        copies = []
+        for k, (source, target) in enumerate(zip(weights, held)):
+            size = target.shape[0 if k == 2 else 1] // 2
+            span = pl.ds(h * size, size)
+            src, dst = (
+                (source.at[expert, span, :], target.at[span, :])
+                if k == 2
+                else (source.at[expert, :, span], target.at[:, span])
+            )
+            copies.append(pltpu.make_async_copy(src, dst, sems.at[h, k]))
+        halves.append(copies)
+    return halves
+
+
 def pre_kernel(n, expert, deps, scal, *refs):
     refs = refs[deps:]
-    w_refs, packs, refs = refs[:n], refs[n : 2 * n], refs[2 * n :]
-    gw, uw, dw, in_ref, cot_ref, *outs = refs
-    rows = in_ref.shape[0] // n
-    half = pl.program_id(0)
-
-    @pl.when(half == 0)
-    def _():
-        for k, (position, weight, hit) in enumerate(routing(scal, w_refs, expert, rows)):
-            pick = hit.astype(F32).astype(BF16)
-            span = span_of(position, rows)
-            in_ref[span, :] = dot(pick, packs[k][0]).astype(BF16)
-            scale = jnp.sum(jnp.where(hit, weight, 0.0), axis=1, keepdims=True)
-            cot_ref[span, :] = (dot(pick, packs[k][1]) * scale).astype(BF16)
-
-    gate = dot(in_ref[...], gw[0]).astype(BF16)
-    up = dot(in_ref[...], uw[0]).astype(BF16)
-    back = dot(cot_ref[...], dw[0], ((1,), (1,))).astype(BF16)
+    w_refs, toks, ogs, refs = refs[:n], refs[n : 2 * n], refs[2 * n : 3 * n], refs[3 * n :]
+    weights, (in_ref, cot_ref, *refs) = refs[:3], refs[3:]
+    outs, (token, gw, uw, dw, sems) = refs[: 2 * n], refs[2 * n :]
+    rows, tile = in_ref.shape[0] // n, gw.shape[1] // 2
+    copies = weight_copies(expert, weights, (gw, uw, dw), sems)
+    for group in copies:
+        for copy in group:
+            copy.start()
+    token[...] = jnp.zeros_like(token)
+    for k, (position, weight, hit) in enumerate(routing(scal, w_refs, expert, rows)):
+        pick = hit.astype(F32).astype(BF16)
+        span = span_of(position, rows)
+        in_ref[span, :] = dot(pick, toks[k][...]).astype(BF16)
+        scale = jnp.sum(jnp.where(hit, weight, 0.0), axis=1, keepdims=True)
+        cot_ref[span, :] = (dot(pick, ogs[k][...]) * scale).astype(BF16)
     for h in range(2):
-
-        @pl.when(half == h)
-        def _():
-            for p in range(n):
-                for k, value in enumerate((gate, up, back)):
-                    outs[h * n + p][pl.ds(k * rows, rows), :] = value[p * rows : (p + 1) * rows]
+        for copy in copies[h]:
+            copy.wait()
+        part = slice(h * tile, (h + 1) * tile)
+        gate = dot(in_ref[...], gw[:, part]).astype(BF16)
+        up = dot(in_ref[...], uw[:, part]).astype(BF16)
+        back = dot(cot_ref[...], dw[part, :], ((1,), (1,))).astype(BF16)
+        for p in range(n):
+            for k, value in enumerate((gate, up, back)):
+                outs[h * n + p][pl.ds(k * rows, rows), :] = value[p * rows : (p + 1) * rows]
 
 
 def thirds(value):
@@ -187,44 +205,45 @@
     if has_prev:
         prev, refs = refs[:2], refs[2:]
     halves, refs = split_pieces(refs, sizes)
-    gw, uw, dw, near, far, token, *refs = refs
+    weights, (near, far, token, *refs) = refs[:3], refs[3:]
     if last:
         near_p, far_p, *refs, held = refs
-    eo, idl = refs
-    step = pl.program_id(0)
-
+    gw, uw, dw, sems, eo_ref, idl_ref = refs
+    copies = weight_copies(expert, weights, (gw, uw, dw), sems)
+    for group in copies:
+        for copy in group:
+            copy.start()
+    token[...] = jnp.zeros_like(token)
+    routes = routing(scal, w_refs, expert, halves[0][0][0].shape[0] // 48 * 16)
+    if last:
+        send_products(scal, w_refs, expert + 1, halves[1], held, near_p, far_p)
+    tile = gw.shape[1] // 2
+    eo, idl = 0.0, 0.0
     for h in range(2):
-
-        @pl.when(step == h)
-        def _():
-            layer = dot(load_rows(scal, n, 0, halves[h]), dw[0])
-            back = dot(load_rows(scal, n, 1, halves[h]), gw[0], ((1,), (1,))) + dot(
-                load_rows(scal, n, 2, halves[h]), uw[0], ((1,), (1,))
-            )
-            eo[...] = layer if h == 0 else eo[...] + layer
-            idl[...] = back if h == 0 else idl[...] + back
-
-    @pl.when(step == 1)
-    def _():
-        rows = eo.shape[0] // n
-        for k, (position, weight, hit) in enumerate(routing(scal, w_refs, expert, rows)):
-            pick = hit.astype(F32)
-            scaled = (pick * weight).astype(BF16)
-            span = span_of(position, rows)
-            layer = dot(scaled, eo[span, :].astype(BF16), ((0,), (0,)))
-            back = dot(pick.astype(BF16), idl[span, :].astype(BF16), ((0,), (0,)))
-            which, place = (near, k) if k < n // 2 else (far, k - n // 2)
-            if has_prev:
-                before = prev[0 if k < n // 2 else 1]
-                layer, back = layer + before[place, 0], back + before[place, 1]
-            which[place, 0] = layer.astype(which.dtype)
-            which[place, 1] = back.astype(which.dtype)
-        token[...] = jnp.zeros_like(token)
-        if last:
-            send_products(scal, w_refs, expert + 1, halves[1], held, near_p, far_p)
-
-
-def grad_kernel(n, has_prev, sizes, scal, in_ref, cot_ref, *refs):
+        for copy in copies[h]:
+            copy.wait()
+        part = slice(h * tile, (h + 1) * tile)
+        eo = eo + dot(load_rows(scal, n, 0, halves[h]), dw[part, :])
+        idl = idl + dot(load_rows(scal, n, 1, halves[h]), gw[:, part], ((1,), (1,)))
+        idl = idl + dot(load_rows(scal, n, 2, halves[h]), uw[:, part], ((1,), (1,)))
+    rows = eo.shape[0] // n
+    eo_ref[...], idl_ref[...] = eo.astype(BF16), idl.astype(BF16)
+    for k, (position, weight, hit) in enumerate(routes):
+        pick = hit.astype(F32)
+        scaled = (pick * weight).astype(BF16)
+        span = span_of(position, rows)
+        layer = dot(scaled, eo_ref[span, :], ((0,), (0,)))
+        back = dot(pick.astype(BF16), idl_ref[span, :], ((0,), (0,)))
+        which, place = (near, k) if k < n // 2 else (far, k - n // 2)
+        if has_prev:
+            before = prev[0 if k < n // 2 else 1]
+            layer, back = layer + before[place, 0], back + before[place, 1]
+        which[place, 0] = layer.astype(which.dtype)
+        which[place, 1] = back.astype(which.dtype)
+
+
+def grad_kernel(n, has_prev, sizes, deps, scal, in_ref, cot_ref, *refs):
+    refs = refs[deps:]
     halves, refs = split_pieces(refs, sizes)
     if has_prev:
         refs = refs[3:]
@@ -260,16 +279,6 @@
             far[k - n // 2] = sums[k]
 
 
-def pack_kernel(ids, combine, tokens, grads, pack, dense):
-    pack[0] = tokens[...]
-    pack[1] = grads[...]
-    expert = lax.broadcasted_iota(jnp.int32, dense.shape, 0)
-    total = jnp.zeros(dense.shape, F32)
-    for k in range(ids.shape[0]):
-        total = total + jnp.where(expert == ids[k : k + 1, :], combine[k : k + 1, :], 0.0)
-    dense[...] = total
-
-
 def whole_spec(shape):
     return pl.BlockSpec(tuple(shape), lambda g: (0,) * len(shape))
 
@@ -284,6 +293,7 @@
 
 SMEM_SPEC = pl.BlockSpec(memory_space=pltpu.SMEM)
 ANY_SPEC = pl.BlockSpec(memory_space=pl.ANY)
+HBM_SPEC = pl.BlockSpec(memory_space=pltpu.HBM)
 TOKEN = (8, 128)
 
 
@@ -335,15 +345,7 @@
 
     ids_t, combine_t = expert_ids.T, combine.T
     named = ids_t[:, None, :] == jnp.arange(experts_all, dtype=jnp.int32)[None, :, None]
-    pack, dense = call(
-        pack_kernel,
-        1,
-        [spec_of(ids_t), spec_of(combine_t), spec_of(tokens), spec_of(out_grad)],
-        [whole_spec((2, count, width)), whole_spec((experts_all, count))],
-        [like((2, count, width)), like((experts_all, count), F32)],
-        choose * experts_all * count,
-        8 * count * width,
-    )(ids_t, combine_t, tokens, out_grad)
+    dense = jnp.sum(jnp.where(named, combine_t[:, None, :], 0.0), axis=0)
 
     along_x, across = Line("expert", chips, 2), Line("expert", peers, 1)
     swap = [(2 * x + c, 2 * x + 1 - c) for x in range(chips) for c in range(2)]
@@ -355,9 +357,8 @@
         ]
         return found + [across.send(piece, swap) for piece in found]
 
-    w_all = gather_blocks(dense)
-    packs = gather_blocks(pack)
-    w_specs, pack_specs = [spec_of(w) for w in w_all], [spec_of(p) for p in packs]
+    tok_all, og_all, w_all = gather_blocks(tokens), gather_blocks(out_grad), gather_blocks(dense)
+    w_specs, block_specs = [spec_of(w) for w in w_all], [spec_of(x) for x in tok_all + og_all]
 
     mac = all_rows * width * hidden
     weight_bytes = 2 * width * hidden
@@ -367,21 +368,27 @@
     piece_bytes = 2 * 3 * rows * tile
     slot_shape = (all_rows, width)
 
-    def weight_specs(e):
+    weights = (gate_weight, up_weight, down_weight)
+    held_weights = [pltpu.VMEM(w.shape[1:], BF16) for w in weights] + [
+        pltpu.SemaphoreType.DMA((2, 3))
+    ]
+
+    def grad_specs(e):
         wide = pl.BlockSpec((1, width, tile), lambda g: (e, 0, g))
         return [wide, wide, pl.BlockSpec((1, tile, width), lambda g: (e, g, 0))]
 
     def pre(e, deps):
-        inputs, cot, *parts = call(
+        inputs, cot, *parts, token = call(
             functools.partial(pre_kernel, n, e, len(deps)),
-            2,
-            [SMEM_SPEC] + [ANY_SPEC] * len(deps) + w_specs + pack_specs + weight_specs(e),
-            [whole_spec(slot_shape)] * 2 + [whole_spec(piece_shape)] * (2 * n),
-            [like(slot_shape)] * 2 + [like(piece_shape)] * (2 * n),
+            1,
+            [SMEM_SPEC] + [ANY_SPEC] * len(deps) + w_specs + block_specs + [HBM_SPEC] * 3,
+            [whole_spec(slot_shape)] * 2 + [whole_spec(piece_shape)] * (2 * n) + [whole_spec(TOKEN)],
+            [like(slot_shape)] * 2 + [like(piece_shape)] * (2 * n) + [like(TOKEN, F32)],
             6 * mac,
             3 * weight_bytes + 2 * n * piece_bytes,
-        )(scal, *deps, *w_all, *packs, gate_weight, up_weight, down_weight)
-        return (inputs, cot), [parts[:n], parts[n:]]
+            scratch_shapes=held_weights,
+        )(scal, *deps, *w_all, *tok_all, *og_all, *weights)
+        return (inputs, cot), [parts[:n], parts[n:]], token
 
     def mid(e, h, totals, products, deps=()):
         others = products if e == local - 1 and h == 1 else []
@@ -411,13 +418,13 @@
         sum_shape = (chips, 2, count, width)
         return call(
             functools.partial(out_kernel, n, e, e > 0, last, sizes_of(halves[0]), len(deps)),
-            2,
+            1,
             [SMEM_SPEC]
             + [ANY_SPEC] * len(deps)
             + w_specs
             + ([whole_spec(sum_shape)] * 2 if e > 0 else [])
             + [spec_of(x) for x in flat]
-            + weight_specs(e),
+            + [HBM_SPEC] * 3,
             [whole_spec(sum_shape)] * 2
             + [whole_spec(TOKEN)]
             + ([whole_spec(dense_shape)] * 2 if last else []),
@@ -426,26 +433,28 @@
             + ([like(dense_shape, F32)] * 2 if last else []),
             6 * mac,
             3 * weight_bytes + len(flat) * piece_bytes,
-            scratch_shapes=[pltpu.VMEM(slot_shape, F32)] * 2
+            scratch_shapes=held_weights
+            + [pltpu.VMEM(slot_shape, BF16)] * 2
             + ([pltpu.VMEM((n, extra, 128), BF16)] if last else []),
-        )(scal, *deps, *w_all, *prev, *flat, gate_weight, up_weight, down_weight)
-
-    def grad(e, slots, halves, prev):
+        )(scal, *deps, *w_all, *prev, *flat, *weights)
+
+    def grad(e, slots, halves, prev, deps):
         flat = flatten(halves)
-        base = 3 + len(flat)
+        base = 3 + len(deps) + len(flat)
         return call(
-            functools.partial(grad_kernel, n, e > 0, sizes_of(halves[0])),
+            functools.partial(grad_kernel, n, e > 0, sizes_of(halves[0]), len(deps)),
             2,
             [SMEM_SPEC]
             + [whole_spec(slot_shape)] * 2
+            + [ANY_SPEC] * len(deps)
             + [spec_of(x) for x in flat]
             + ([ANY_SPEC] * 3 if e > 0 else []),
-            weight_specs(e) + [whole_spec(TOKEN)],
-            [like(w.shape) for w in (gate_weight, up_weight, down_weight)] + [like(TOKEN, F32)],
+            grad_specs(e) + [whole_spec(TOKEN)],
+            [like(w.shape) for w in weights] + [like(TOKEN, F32)],
             6 * mac,
             3 * weight_bytes + len(flat) * piece_bytes,
             input_output_aliases={base + k: k for k in range(3)} if e > 0 else {},
-        )(scal, *slots, *flat, *prev)
+        )(scal, *slots, *deps, *flat, *prev)
 
     along_z = Line("dp", n, 1)
 
@@ -455,76 +464,90 @@
     def inner(value):
         return along_z.send(value, [(1, 2), (2, 1), (0, 0), (3, 3)])
 
-    def unless_end(value):
-        return jnp.where(at_end, jnp.zeros_like(value), value)
-
-    products, sums, grads, home_sums = [], [], [], []
-
-    def finish(e, slots, halves, deps=()):
-        nonlocal sums, grads, home_sums
-        near, far, token_a, *home_sums = out(e, halves, sums, deps)
-        *grads, token_b = grad(e, slots, halves, grads)
-        sums = [near, far]
-        return token_a, token_b
+    def after(token):
+        return at_end if token is None else at_end & (token[0, 0] == 0.0)
+
+    def unless(end, value):
+        return jnp.where(end, jnp.zeros_like(value), value)
+
+    products, sums, grads = [], [], []
+
+    def send_home(near, far, add):
+        near = add(near, across.send(far, swap))
+        right, left = along_x.scatter([near[q] for q in range(chips)], add)
+        home = near[0].astype(F32) + right.astype(F32)
+        return near, home if left is None else home + left.astype(F32)
 
     if swaps:
-        flight, arrived, deps, token_b = [None, None], None, [], None
+        flight, arrived = [None, None], None
+        slots, parts, pre_token = pre(0, [])
+        grad_token = None
         for e in range(local):
-            slots, parts = pre(e, deps)
-            halves, totals = [], []
+            more = e < local - 1
+            first, second, totals, halves = [], [], [], []
             for h in range(2):
-                x, last = parts[h], flight[h]
-                if last is None:
-                    a1, send_a2 = outer(x[3]), x[2]
+                x = parts[h]
+                if e == 0:
+                    first.append((outer(x[3]), None))
                 else:
-                    y, got_a, got_b = last
-                    a1, b1 = outer(jnp.where(at_end, x[3], got_b)), inner(got_a)
-                    send_a2 = jnp.where(at_end, x[2], b1)
-                a2, b2 = outer(send_a2), inner(unless_end(add_rounded(x[3], a1)))
-                if last is not None:
-                    halves.append([(y,), (got_a,), (a1, got_b), (a2, b1)])
+                    y, got_a, got_b = flight[h]
+                    end = after(grad_token if h == 0 else None)
+                    first.append((outer(jnp.where(end, x[3], got_b)), inner(got_a)))
+            if more:
+                begun = pre(e + 1, [first[0][0]] if e == 0 else [flight[1][2]])
+            for h in range(2):
+                x, (a1, b1) = parts[h], first[h]
+                end = after(begun[2] if more and h == int(e == 0) else None)
+                send_a2 = x[2] if e == 0 else jnp.where(end, x[2], b1)
+                second.append((outer(send_a2), inner(unless(end, add_rounded(x[3], a1)))))
+                if e > 0:
+                    y, got_a, got_b = flight[h]
+                    halves.append([(y,), (got_a,), (a1, got_b), (second[h][0], b1)])
+            for h in range(2):
+                x, (a2, b2) = parts[h], second[h]
                 a3 = outer(add_rounded(x[1], b2))
-                b3 = inner(unless_end(add_rounded(x[2], a2)))
+                b3 = inner(unless(at_end, add_rounded(x[2], a2)))
                 totals.append((x[0], a3, b3))
-            token_a = None
+            wait = []
             if e > 0:
-                token_a, token_b = finish(e - 1, arrived, halves)
+                *sums, out_token = out(e - 1, halves, sums, [])
+                wait = [out_token]
             for h in range(2):
-                wait = [token_a] if e > 0 and h == 1 else []
-                y, product = mid(e, h, totals[h], products, wait)
+                y, product = mid(e, h, totals[h], products, wait if h == 0 else [])
                 products.append(product)
                 flight[h] = (y, outer(y), inner(y))
-            deps = [totals[0][1]] if e == 0 else [token_b]
+            if e > 0:
+                *grads, grad_token = grad(e - 1, arrived, halves, grads, [flight[1][0]])
             arrived = slots
+            if more:
+                slots, parts, _ = begun
         halves = []
         for h in range(2):
             y, got_a, got_b = flight[h]
             a1, b1 = outer(got_b), inner(got_a)
             a2 = outer(b1)
             halves.append([(y,), (got_a,), (a1, got_b), (a2, b1)])
-        finish(local - 1, arrived, halves, [token_b])
+        wait = [grad_token]
     else:
         begun = []
         for e in range(local):
-            slots, parts = pre(e, [])
+            slots, parts, _ = pre(e, [])
             begun.append((slots, [(x[0], *along_z.scatter(x, add_rounded)) for x in parts]))
         for e in range(local):
-            halves = []
+            halves, arrived, wait = [], begun[e][0], []
             for h in range(2):
                 y, product = mid(e, h, begun[e][1][h], products)
                 products.append(product)
                 halves.append([(y,)] + along_z.gather(y))
-            finish(e, begun[e][0], halves)
-
-    def send_home(near, far, add):
-        near = add(near, across.send(far, swap))
-        right, left = along_x.scatter([near[q] for q in range(chips)], add)
-        home = near[0].astype(F32) + right.astype(F32)
-        return home if left is None else home + left.astype(F32)
-
-    per_expert = send_home(*home_sums, lambda a, b: a + b)
+            if e < local - 1:
+                *sums, _ = out(e, halves, sums, [])
+                *grads, _ = grad(e, arrived, halves, grads, [])
+
+    near, far, _, near_p, far_p = out(local - 1, halves, sums, wait)
+    hop, home = send_home(near, far, add_rounded)
+    _, per_expert = send_home(near_p, far_p, lambda a, b: a + b)
+    *grads, _ = grad(local - 1, arrived, halves, grads, [hop])
     combine_grad = jnp.sum(jnp.where(named, per_expert[None], 0.0), axis=1) / combine_t
-    home = send_home(*sums, add_rounded)
     return (home[0].astype(BF16), home[1].astype(BF16), *grads, combine_grad.T)
 
 

time: 246 us -> 319 us (1.30)
  local copies, waits for them, and re-layouts: 9.69 us -> 64.2 us
  other arithmetic: 2.57 us -> 31.2 us
  starting transfers between devices: 153 us -> 133 us
  Pallas kernels: 37.7 us -> 51.1 us
  waiting for transfers between devices: 39.5 us -> 31.1 us
  between operations: 1.51 us -> 5.41 us
    unnamed x24 -> x236, local copies, waits for them, and re-layouts: 8.87 us -> 60.8 us
    select_n x28, other arithmetic: 1.34 us -> 23.6 us  [the longest x16 12.6 us: unless(): return jnp.where(end, jnp.zeros_like(value), value)]
    ppermute x78 -> x81, starting transfers between devices: 153 us -> 133 us  [send(): return lax.ppermute(value, self.axis, wide)]
    ppermute x78 -> x81, waiting for transfers between devices: 39.5 us -> 31.1 us  [send(): return lax.ppermute(value, self.axis, wide)]
    convert_element_type x9, other arithmetic: 0.53 us -> 6.19 us  [add_rounded(): return (a.astype(F32) + b.astype(F32)).astype(BF16)]
    pallas_call x8, Pallas kernels: 1.86 us -> 7.19 us  [mid(): call(functools.partial(mid_kernel, len(deps), len(others)), 1, [ANY_SPEC]...]
    pallas_call x9 -> x8, Pallas kernels: 24.4 us -> 28.6 us  [the longest x4 16 us: grad(): call(functools.partial(grad_kernel, n, e > 0, sizes_of(halves[0]), len(de...]
    pallas_call x4, Pallas kernels: 11.5 us -> 15.4 us  [out(): call(functools.partial(out_kernel, n, e, e > 0, last, sizes_of(halves[0])...]
  transfers between devices with their start and end apart: 78 -> 81, of which waited for: 13 -> 15; matrix products, arithmetic and copies ran while one was open for 1% -> 11% of each run, Pallas kernels for 12% -> 14%
where the time goes in v4:
time: 319 us; the launch traced here: 316 us
  starting transfers between devices  133 us (42%)
  local copies, waits for them, and re-layouts  64.2 us (20%)
  Pallas kernels  51.1 us (16%)
  other arithmetic  31.2 us (10%)
  waiting for transfers between devices  31.1 us (10%)
  between operations  5.41 us (2%)
    ppermute x81, starting transfers between devices, send(): return lax.ppermute(value, self.axis, wide)  133 us
    unnamed x236, local copies, waits for them, and re-layouts  60.8 us
    ppermute x81, waiting for transfers between devices, send(): return lax.ppermute(value, self.axis, wide)  31.1 us
    pallas_call x4, Pallas kernels, grad(): call(functools.partial(grad_kernel, n, e > 0, sizes_of(halves[0]), len(de...  16 us
    pallas_call x4, Pallas kernels, out(): call(functools.partial(out_kernel, n, e, e > 0, last, sizes_of(halves[0])...  15.4 us
    select_n x16, other arithmetic, unless(): return jnp.where(end, jnp.zeros_like(value), value)  12.6 us
    pallas_call x4, Pallas kernels, pre(): call(functools.partial(pre_kernel, n, e, len(deps)), 1, [SMEM_SPEC] + [AN...  12.5 us
    pallas_call x8, Pallas kernels, mid(): call(functools.partial(mid_kernel, len(deps), len(others)), 1, [ANY_SPEC]...  7.19 us
  transfers between devices with their start and end apart: 81, of which 15 were waited for; matrix products, arithmetic and copies ran while one was open for 11% of the time, Pallas kernels for 14%

profile of v4, /device:TPU:0, one launch (start us, length us, event | category | flops | bytes accessed | tf_op | source)
XLA Modules:
  0.0 315.7 jit_solution(1324990635619874661)
XLA Ops:
  0.6 3.0 collective-permute-start.3
  4.2 3.9 %collective-permute-done.3.refs_5_.refs_6_ = bf16[128,512]{1,0:T(8,128)(2,1)S(1)} collective-permute-done((bf16[128,512]{1,0:T(8,128)(2,1)}, bf16[128,512]{1,0:T(8,128)(2,1)S(1)}, u32[]{:S(2)}, u32[]{:S(2)}) %collective-permute-start.3) | collective-permute-done | bytes 131104 | tf_op jit(solution)/shard_map/ppermute | solution.py:32
  8.2 2.0 collective-permute-done.6.refs_9_.refs_10_
  10.9 1.8 collective-permute-start
  12.7 1.9 collective-permute-done.refs_1_.refs_2_
  17.1 2.0 copy-done
  19.0 1.9 copy-done.2
  20.9 1.9 copy-done.8
  24.6 3.6 %shard_map.118 = (bf16[320,512]{1,0:T(8,128)(2,1)S(1)}, bf16[320,512]{1,0:T(8,128)(2,1)S(1)}, bf16[240,384]{1,0:T(8,128)(2,1)S(1)}, bf16[240,384]{1,0:T(8,128)(2...) custom-call(s32[10]{0:T(128)S(1)} %stack.35.scal, ...), custom_call_target="tpu_custom_call" | custom-call | flops 754974720 | bytes 3833856 | tf_op jit(solution)/shard_map/pallas_call | solution.py:381
  29.0 1.9 collective-permute-start.9
  31.1 1.8 collective-permute-start.13
  33.1 3.4 %collective-permute-done.9.refs_0_ = bf16[240,384]{1,0:T(8,128)(2,1)S(1)} collective-permute-done((bf16[240,384]{1,0:T(8,128)(2,1)S(1)}, bf16[240,384]{1,0:T(8,128)(2,1)S(1)}, u32[]{:S(2)}, u32[]{:S(2)}) %collective-permute-start.9) | collective-permute-done | bytes 184352 | tf_op jit(solution)/shard_map/ppermute | solution.py:32
  37.3 3.0 collective-permute-start.39
  41.3 3.0 collective-permute-start.42
  44.3 3.0 shard_map.119
  60.0 9.2 %collective-permute-start.12 = (bf16[240,384]{1,0:T(8,128)(2,1)S(1)}, bf16[240,384]{1,0:T(8,128)(2,1)S(1)}, u32[]{:S(2)}, u32[]{:S(2)}) collective-permute-start(bf16[240,384]{1,0:T(8,128)(2,1)S(1)} %add_convert_fusion.23), channel_id=1, source_target_pairs={{0,1},{1,0},{2,3},{3,2},{4,5},{5,4},{6,7},{7,6},{8,9},{9,8},{10,11... | collective-permute-start | bytes 552968 | tf_op jit(solution)/shard_map/ppermute | solution.py:32
  70.3 2.4 collective-permute-done.12.refs_1_
  77.5 1.7 shard_map.125
  79.9 3.0 collective-permute-start.44
  82.9 3.4 %collective-permute-start.43 = (bf16[240,384]{1,0:T(8,128)(2,1)}, bf16[240,384]{1,0:T(8,128)(2,1)}, u32[]{:S(2)}, u32[]{:S(2)}) collective-permute-start(bf16[240,384]{1,0:T(8,128)(2,1)} %get-tuple-element.120.refs_4_.refs_1_), channel_id=1, source_target_pairs={{0,1},{1,0},{2,3},{3,2},{4,5},{5,4},{6,7},{7,6},{8,9},{9,8},{10,11... | collective-permute-start | bytes 552968 | tf_op jit(solution)/shard_map/ppermute | solution.py:32
  86.3 1.9 copy-done.3
  88.2 1.9 copy-done.9
  96.5 3.0 shard_map.121
  108.7 2.0 collective-permute-start.45
  115.9 4.6 %collective-permute-start.47 = (bf16[240,384]{1,0:T(8,128)(2,1)S(1)}, bf16[240,384]{1,0:T(8,128)(2,1)S(1)}, u32[]{:S(2)}, u32[]{:S(2)}) collective-permute-start(bf16[240,384]{1,0:T(8,128)(2,1)S(1)} %broadcast_select_fusion.3), channel_id=1, source_target_pairs={{0,1},{1,0},{2,3},{3,2},{4,5},{5,4},{6,7},{7,6},{8,9},{9,8},{10,11... | collective-permute-start | bytes 552968 | tf_op jit(solution)/shard_map/ppermute | solution.py:32
  123.1 1.8 collective-permute-start.21
  128.2 2.3 collective-permute-done.21.refs_14_.refs_11_
  131.4 4.1 %collective-permute-start.18 = (bf16[240,384]{1,0:T(8,128)(2,1)S(1)}, bf16[240,384]{1,0:T(8,128)(2,1)S(1)}, u32[]{:S(2)}, u32[]{:S(2)}) collective-permute-start(bf16[240,384]{1,0:T(8,128)(2,1)S(1)} %add_convert_fusion.20), channel_id=1, source_target_pairs={{0,1},{1,0},{2,3},{3,2},{4,5},{5,4},{6,7},{7,6},{8,9},{9,8},{10,11... | collective-permute-start | bytes 552968 | tf_op jit(solution)/shard_map/ppermute | solution.py:32
  135.7 3.4 %collective-permute-done.18.refs_1_ = bf16[240,384]{1,0:T(8,128)(2,1)S(1)} collective-permute-done((bf16[240,384]{1,0:T(8,128)(2,1)S(1)}, bf16[240,384]{1,0:T(8,128)(2,1)S(1)}, u32[]{:S(2)}, u32[]{:S(2)}) %collective-permute-start.18) | collective-permute-done | bytes 184352 | tf_op jit(solution)/shard_map/ppermute | solution.py:32
  142.1 1.9 copy-done.10
  144.0 3.8 %shard_map.126 = (f32[2,2,128,512]{3,2,1,0:T(8,128)S(1)}, f32[2,2,128,512]{3,2,1,0:T(8,128)S(1)}, f32[8,128]{1,0:T(8,128)S(1)}) custom-call(s32[10]{0:T(128)S(1)} %stack.35.scal, f32[16,128]{1,0:T(8,128)S(1)} %select_reduce_fusion.1.refs_0_.refs_1_, f32[16,128]{1,0:T(8,128)S(1)} %collective-permute-done.refs_1_.refs_2_, ...), custom_call_target="tpu_custom_call" | custom-call | flops 754974720 | bytes 4571136 | tf_op jit(solution)/shard_map/pallas_call | solution.py:419
  149.4 3.0 collective-permute-start.52
  152.4 4.2 %collective-permute-start.51 = (bf16[240,384]{1,0:T(8,128)(2,1)}, bf16[240,384]{1,0:T(8,128)(2,1)}, u32[]{:S(2)}, u32[]{:S(2)}) collective-permute-start(bf16[240,384]{1,0:T(8,128)(2,1)} %get-tuple-element.131.refs_6_.refs_1_), channel_id=1, source_target_pairs={{0,1},{1,0},{2,3},{3,2},{4,5},{5,4},{6,7},{7,6},{8,9},{9,8},{10,11... | collective-permute-start | bytes 552968 | tf_op jit(solution)/shard_map/ppermute | solution.py:32
  156.7 4.2 %shard_map.128 = (bf16[4,512,768]{2,1,0:T(8,128)(2,1)}, bf16[4,512,768]{2,1,0:T(8,128)(2,1)}, bf16[4,768,512]{2,1,0:T(8,128)(2,1)}, f32[8,128]{1,0:T(8,128)S(1)}) custom-call(s32[10]{0:T(128)S(1)} %stack.35.scal, bf16[320,512]{1,0:T(8,128)(2,1)S(1)} %copy-done.75, bf16[320,512]{1,0:T(8,128)(2,1)S(1)} %copy-done.77, ...), custom_call_target="tpu_custom_call" | custom-call | flops 754974720 | bytes 4571136 | tf_op jit(solution)/shard_map/pallas_call | solution.py:444
  162.0 1.9 copy-done.5
  163.9 1.9 copy-done.11
  173.0 3.0 shard_map.123
  185.2 2.0 collective-permute-start.53
  193.2 3.2 %collective-permute-start.55 = (bf16[240,384]{1,0:T(8,128)(2,1)S(1)}, bf16[240,384]{1,0:T(8,128)(2,1)S(1)}, u32[]{:S(2)}, u32[]{:S(2)}) collective-permute-start(bf16[240,384]{1,0:T(8,128)(2,1)S(1)} %broadcast_select_fusion.1), channel_id=1, source_target_pairs={{0,1},{1,0},{2,3},{3,2},{4,5},{5,4},{6,7},{7,6},{8,9},{9,8},{10,11... | collective-permute-start | bytes 552968 | tf_op jit(solution)/shard_map/ppermute | solution.py:32
  198.2 3.0 collective-permute-start.29
  205.5 4.6 %collective-permute-start.57 = (bf16[240,384]{1,0:T(8,128)(2,1)S(1)}, bf16[240,384]{1,0:T(8,128)(2,1)S(1)}, u32[]{:S(2)}, u32[]{:S(2)}) collective-permute-start(bf16[240,384]{1,0:T(8,128)(2,1)S(1)} %add_convert_fusion.5), channel_id=1, source_target_pairs={{0,1},{1,0},{2,3},{3,2},{4,5},{5,4},{6,7},{7,6},{8,9},{9,8},{10,11... | collective-permute-start | bytes 552968 | tf_op jit(solution)/shard_map/ppermute | solution.py:32
  211.8 2.2 collective-permute-start.26
  214.0 1.9 copy-done.12
  215.9 3.8 %shard_map.129 = (f32[2,2,128,512]{3,2,1,0:T(8,128)S(1)}, f32[2,2,128,512]{3,2,1,0:T(8,128)S(1)}, f32[8,128]{1,0:T(8,128)S(1)}) custom-call(s32[10]{0:T(128)S(1)} %stack.35.scal, f32[16,128]{1,0:T(8,128)S(1)} %select_reduce_fusion.1.refs_0_.refs_1_, f32[16,128]{1,0:T(8,128)S(1)} %collective-permute-done.refs_1_.refs_2_, ...), custom_call_target="tpu_custom_call" | custom-call | flops 754974720 | bytes 4571136 | tf_op jit(solution)/shard_map/pallas_call | solution.py:419
  223.0 1.6 collective-permute-start.59
  225.8 3.0 collective-permute-start.31
  228.8 4.2 %shard_map.131 = (bf16[4,512,768]{2,1,0:T(8,128)(2,1)}, bf16[4,512,768]{2,1,0:T(8,128)(2,1)}, bf16[4,768,512]{2,1,0:T(8,128)(2,1)}, f32[8,128]{1,0:T(8,128)S(1)}) custom-call(s32[10]{0:T(128)S(1)} %stack.35.scal, bf16[320,512]{1,0:T(8,128)(2,1)S(1)} %copy-done.71, ...), custom_call_target="tpu_custom_call", output_to_operand_aliasing={{0}: (16, {}), {1}: (17, {}), {2}: (18, {})} | custom-call | flops 754974720 | bytes 4571136 | tf_op jit(solution)/shard_map/pallas_call | solution.py:444
  235.8 1.7 collective-permute-start.62
  238.4 3.1 collective-permute-start.32
  244.1 2.6 collective-permute-start.63
  249.3 2.0 collective-permute-start.37
  255.7 4.6 %collective-permute-start.65 = (bf16[240,384]{1,0:T(8,128)(2,1)S(1)}, bf16[240,384]{1,0:T(8,128)(2,1)S(1)}, u32[]{:S(2)}, u32[]{:S(2)}) collective-permute-start(bf16[240,384]{1,0:T(8,128)(2,1)S(1)} %add_convert_fusion.2), channel_id=1, source_target_pairs={{0,1},{1,0},{2,3},{3,2},{4,5},{5,4},{6,7},{7,6},{8,9},{9,8},{10,11... | collective-permute-start | bytes 552968 | tf_op jit(solution)/shard_map/ppermute | solution.py:32
  262.3 2.9 collective-permute-start.34
  265.3 1.9 copy-done.13
  267.2 3.9 %shard_map.132 = (f32[2,2,128,512]{3,2,1,0:T(8,128)S(1)}, f32[2,2,128,512]{3,2,1,0:T(8,128)S(1)}, f32[8,128]{1,0:T(8,128)S(1)}) custom-call(s32[10]{0:T(128)S(1)} %stack.35.scal, f32[16,128]{1,0:T(8,128)S(1)} %select_reduce_fusion.1.refs_0_.refs_1_, f32[16,128]{1,0:T(8,128)S(1)} %collective-permute-done.refs_1_.refs_2_, ...), custom_call_target="tpu_custom_call" | custom-call | flops 754974720 | bytes 4571136 | tf_op jit(solution)/shard_map/pallas_call | solution.py:419
  274.8 4.2 %collective-permute-done.72.refs_14_.refs_8_ = bf16[256,384]{1,0:T(8,128)(2,1)S(1)} collective-permute-done((bf16[256,384]{1,0:T(8,128)(2,1)S(1)}, bf16[256,384]{1,0:T(8,128)(2,1)S(1)}, u32[]{:S(2)}, u32[]{:S(2)}) %collective-permute-start.72) | collective-permute-done | bytes 196640 | tf_op jit(solution)/shard_map/ppermute | solution.py:32
  281.7 7.1 %collective-permute-start.74 = (bf16[256,384]{1,0:T(8,128)(2,1)S(1)}, bf16[256,384]{1,0:T(8,128)(2,1)S(1)}, u32[]{:S(2)}, u32[]{:S(2)}) collective-permute-start(bf16[256,384]{1,0:T(8,128)(2,1)S(1)} %collective-permute-done.73.refs_16_.refs_10_), channel_id=1, source_target_pairs={{0,1},{1,0},{2,3},{3,2},{4,5},{5,4},{6,7},{7,6},{8,9},{9,8},{10,11... | collective-permute-start | bytes 589832 | tf_op jit(solution)/shard_map/ppermute | solution.py:32
  288.9 1.9 collective-permute-start.69
  290.8 3.4 %collective-permute-start.71 = (bf16[240,384]{1,0:T(8,128)(2,1)S(1)}, bf16[240,384]{1,0:T(8,128)(2,1)S(1)}, u32[]{:S(2)}, u32[]{:S(2)}) collective-permute-start(bf16[240,384]{1,0:T(8,128)(2,1)S(1)} %collective-permute-done.70.refs_12_.refs_6_), channel_id=1, source_target_pairs={{0,1},{1,0},{2,3},{3,2},{4,5},{5,4},{6,7},{7,6},{8,9},{9,8},{10,11... | collective-permute-start | bytes 552968 | tf_op jit(solution)/shard_map/ppermute | solution.py:32
  294.2 4.3 %shard_map.135 = (bf16[4,512,768]{2,1,0:T(8,128)(2,1)}, bf16[4,512,768]{2,1,0:T(8,128)(2,1)}, bf16[4,768,512]{2,1,0:T(8,128)(2,1)}, f32[8,128]{1,0:T(8,128)S(1)}) custom-call(s32[10]{0:T(128)S(1)} %stack.35.scal, bf16[320,512]{1,0:T(8,128)(2,1)S(1)} %copy-done.63, ...), custom_call_target="tpu_custom_call", output_to_operand_aliasing={{0}: (16, {}), {1}: (17, {}), {2}: (18, {})} | custom-call | flops 754974720 | bytes 4571136 | tf_op jit(solution)/shard_map/pallas_call | solution.py:444
  298.6 3.9 %shard_map.136 = (bf16[2,2,128,512]{3,2,1,0:T(8,128)(2,1)S(1)}, bf16[2,2,128,512]{3,2,1,0:T(8,128)(2,1)S(1)}, f32[8,128]{1,0:T(8,128)}, f32[2,16,128]{2,1,0:T(8,128)S(1)}, f32[2,16,128]{2,1,0:T(8,128)S(1)}) custom-call(s32[10]{0:T(128)S(1)} %stack.35.scal, f32[8,128]{1,0:T(8,128)S(1)} %get-tuple-element.162.refs_0_, ...), custom_call_target="tpu_custom_call" | custom-call | flops 754974720 | bytes 4571136 | tf_op jit(solution)/shard_map/pallas_call | solution.py:419
  305.3 2.1 collective-permute-done.80
  309.8 3.4 %shard_map.137 = (bf16[4,512,768]{2,1,0:T(8,128)(2,1)}, bf16[4,512,768]{2,1,0:T(8,128)(2,1)}, bf16[4,768,512]{2,1,0:T(8,128)(2,1)}, f32[8,128]{1,0:T(8,128)}) custom-call(s32[10]{0:T(128)S(1)} %stack.35.scal, bf16[320,512]{1,0:T(8,128)(2,1)S(1)} %copy-done.67, ...), custom_call_target="tpu_custom_call", output_to_operand_aliasing={{0}: (16, {}), {1}: (17, {}), {2}: (18, {})} | custom-call | flops 754974720 | bytes 4571136 | tf_op jit(solution)/shard_map/pallas_call | solution.py:444
  313.3 1.7 collective-permute-done.78
  (406 shorter events, 119.6 us)
Async XLA Ops:
  0.6 7.5 %collective-permute-start.3 = (bf16[128,512]{1,0:T(8,128)(2,1)}, bf16[128,512]{1,0:T(8,128)(2,1)S(1)}, u32[]{:S(2)}, u32[]{:S(2)}) collective-permute-start(bf16[128,512]{1,0:T(8,128)(2,1)} %refs_5_.5), channel_id=1, source_target_pairs={{0,8},{4,12},{8,0},{12,4},{1,9},{5,13},{9,1},{13,5},{2,10},{6,14},... | collective-permute-start | bytes 393224 | tf_op jit(solution)/shard_map/ppermute | solution.py:32
  3.7 13.3 %collective-permute-start.4 = (bf16[128,512]{1,0:T(8,128)(2,1)}, bf16[128,512]{1,0:T(8,128)(2,1)S(1)}, u32[]{:S(2)}, u32[]{:S(2)}) collective-permute-start(bf16[128,512]{1,0:T(8,128)(2,1)} %refs_5_.5), channel_id=1, source_target_pairs={{0,4},{4,0},{8,12},{12,8},{1,5},{5,1},{9,13},{13,9},{2,6},{6,2},{1... | collective-permute-start | bytes 393224 | tf_op jit(solution)/shard_map/ppermute | solution.py:32
  3.7 13.3 %collective-permute-start.7 = (bf16[128,512]{1,0:T(8,128)(2,1)}, bf16[128,512]{1,0:T(8,128)(2,1)S(1)}, u32[]{:S(2)}, u32[]{:S(2)}) collective-permute-start(bf16[128,512]{1,0:T(8,128)(2,1)} %refs_9_.5), channel_id=1, source_target_pairs={{0,4},{4,0},{8,12},{12,8},{1,5},{5,1},{9,13},{13,9},{2,6},{6,2},{1... | collective-permute-start | bytes 393224 | tf_op jit(solution)/shard_map/ppermute | solution.py:32
  8.2 8.8 %collective-permute-start.5 = (bf16[128,512]{1,0:T(8,128)(2,1)S(1)}, bf16[128,512]{1,0:T(8,128)(2,1)S(1)}, u32[]{:S(2)}, u32[]{:S(2)}) collective-permute-start(bf16[128,512]{1,0:T(8,128)(2,1)S(1)} %collective-permute-done.3.refs_5_.refs_6_), channel_id=1, source_target_pairs={{0,4},{4,0},{8,12},{12,8},{1,5},{5,1},{9,13},{13,9},{2,6},{6,2},{1... | collective-permute-start | bytes 393224 | tf_op jit(solution)/shard_map/ppermute | solution.py:32
  29.0 7.5 %collective-permute-start.9 = (bf16[240,384]{1,0:T(8,128)(2,1)S(1)}, bf16[240,384]{1,0:T(8,128)(2,1)S(1)}, u32[]{:S(2)}, u32[]{:S(2)}) collective-permute-start(bf16[240,384]{1,0:T(8,128)(2,1)S(1)} %get-tuple-element.94), channel_id=1, source_target_pairs={{0,1},{1,0},{2,3},{3,2},{4,5},{5,4},{6,7},{7,6},{8,9},{9,8},{10,11... | collective-permute-start | bytes 552968 | tf_op jit(solution)/shard_map/ppermute | solution.py:32
  30.9 9.6 %collective-permute-start.41 = (bf16[240,384]{1,0:T(8,128)(2,1)S(1)}, bf16[240,384]{1,0:T(8,128)(2,1)S(1)}, u32[]{:S(2)}, u32[]{:S(2)}) collective-permute-start(bf16[240,384]{1,0:T(8,128)(2,1)S(1)} %get-tuple-element.117), channel_id=1, source_target_pairs={{0,1},{1,0},{2,3},{3,2},{4,5},{5,4},{6,7},{7,6},{8,9},{9,8},{10,11... | collective-permute-start | bytes 552968 | tf_op jit(solution)/shard_map/ppermute | solution.py:32
  31.1 26.2 %collective-permute-start.13 = (bf16[240,384]{1,0:T(8,128)(2,1)S(1)}, bf16[240,384]{1,0:T(8,128)(2,1)}, u32[]{:S(2)}, u32[]{:S(2)}) collective-permute-start(bf16[240,384]{1,0:T(8,128)(2,1)S(1)} %get-tuple-element.97), channel_id=1, source_target_pairs={{0,1},{1,0},{2,3},{3,2},{4,5},{5,4},{6,7},{7,6},{8,9},{9,8},{10,11... | collective-permute-start | bytes 552968 | tf_op jit(solution)/shard_map/ppermute | solution.py:32
  32.9 22.6 %collective-permute-start.10 = (bf16[240,384]{1,0:T(8,128)(2,1)}, bf16[240,384]{1,0:T(8,128)(2,1)}, u32[]{:S(2)}, u32[]{:S(2)}) collective-permute-start(bf16[240,384]{1,0:T(8,128)(2,1)} %get-tuple-element.96), channel_id=1, source_target_pairs={{0,1},{1,0},{2,3},{3,2},{4,5},{5,4},{6,7},{7,6},{8,9},{9,8},{10,11... | collective-permute-start | bytes 552968 | tf_op jit(solution)/shard_map/ppermute | solution.py:32
  37.3 31.9 %collective-permute-start.39 = (bf16[240,384]{1,0:T(8,128)(2,1)}, bf16[240,384]{1,0:T(8,128)(2,1)}, u32[]{:S(2)}, u32[]{:S(2)}) collective-permute-start(bf16[240,384]{1,0:T(8,128)(2,1)} %fusion.9), channel_id=1, source_target_pairs={{1,2},{2,1},{0,0},{3,3},{5,6},{6,5},{4,4},{7,7},{9,10},{10,9},{8,8... | collective-permute-start | bytes 552968 | tf_op jit(solution)/shard_map/ppermute | solution.py:32
  41.3 35.3 %collective-permute-start.42 = (bf16[240,384]{1,0:T(8,128)(2,1)}, bf16[240,384]{1,0:T(8,128)(2,1)}, u32[]{:S(2)}, u32[]{:S(2)}) collective-permute-start(bf16[240,384]{1,0:T(8,128)(2,1)} %fusion.10), channel_id=1, source_target_pairs={{1,2},{2,1},{0,0},{3,3},{5,6},{6,5},{4,4},{7,7},{9,10},{10,9},{8,8... | collective-permute-start | bytes 552968 | tf_op jit(solution)/shard_map/ppermute | solution.py:32
  58.3 12.0 %collective-permute-start.14 = (bf16[240,384]{1,0:T(8,128)(2,1)S(1)}, bf16[240,384]{1,0:T(8,128)(2,1)S(1)}, u32[]{:S(2)}, u32[]{:S(2)}) collective-permute-start(bf16[240,384]{1,0:T(8,128)(2,1)S(1)} %fusion.2), channel_id=1, source_target_pairs={{1,2},{2,1},{0,0},{3,3},{5,6},{6,5},{4,4},{7,7},{9,10},{10,9},{8,8... | collective-permute-start | bytes 552968 | tf_op jit(solution)/shard_map/ppermute | solution.py:32
  60.0 12.7 %collective-permute-start.12 = (bf16[240,384]{1,0:T(8,128)(2,1)S(1)}, bf16[240,384]{1,0:T(8,128)(2,1)S(1)}, u32[]{:S(2)}, u32[]{:S(2)}) collective-permute-start(bf16[240,384]{1,0:T(8,128)(2,1)S(1)} %add_convert_fusion.23), channel_id=1, source_target_pairs={{0,1},{1,0},{2,3},{3,2},{4,5},{5,4},{6,7},{7,6},{8,9},{9,8},{10,11... | collective-permute-start | bytes 552968 | tf_op jit(solution)/shard_map/ppermute | solution.py:32
  75.0 11.3 %collective-permute-start.15 = (bf16[240,384]{1,0:T(8,128)(2,1)}, bf16[240,384]{1,0:T(8,128)(2,1)S(1)}, u32[]{:S(2)}, u32[]{:S(2)}) collective-permute-start(bf16[240,384]{1,0:T(8,128)(2,1)} %get-tuple-element.98.refs_10_.refs_7_), channel_id=1, source_target_pairs={{1,2},{2,1},{0,0},{3,3},{5,6},{6,5},{4,4},{7,7},{9,10},{10,9},{8,8... | collective-permute-start | bytes 552968 | tf_op jit(solution)/shard_map/ppermute | solution.py:32
  79.9 27.7 %collective-permute-start.44 = (bf16[240,384]{1,0:T(8,128)(2,1)}, bf16[240,384]{1,0:T(8,128)(2,1)}, u32[]{:S(2)}, u32[]{:S(2)}) collective-permute-start(bf16[240,384]{1,0:T(8,128)(2,1)} %get-tuple-element.120.refs_4_.refs_1_), channel_id=1, source_target_pairs={{1,2},{2,1},{0,0},{3,3},{5,6},{6,5},{4,4},{7,7},{9,10},{10,9},{8,8... | collective-permute-start | bytes 552968 | tf_op jit(solution)/shard_map/ppermute | solution.py:32
  82.9 27.8 %collective-permute-start.43 = (bf16[240,384]{1,0:T(8,128)(2,1)}, bf16[240,384]{1,0:T(8,128)(2,1)}, u32[]{:S(2)}, u32[]{:S(2)}) collective-permute-start(bf16[240,384]{1,0:T(8,128)(2,1)} %get-tuple-element.120.refs_4_.refs_1_), channel_id=1, source_target_pairs={{0,1},{1,0},{2,3},{3,2},{4,5},{5,4},{6,7},{7,6},{8,9},{9,8},{10,11... | collective-permute-start | bytes 552968 | tf_op jit(solution)/shard_map/ppermute | solution.py:32
  86.2 27.1 %collective-permute-start.19 = (bf16[240,384]{1,0:T(8,128)(2,1)}, bf16[240,384]{1,0:T(8,128)(2,1)}, u32[]{:S(2)}, u32[]{:S(2)}) collective-permute-start(bf16[240,384]{1,0:T(8,128)(2,1)} %get-tuple-element.98.refs_10_.refs_7_), channel_id=1, source_target_pairs={{0,1},{1,0},{2,3},{3,2},{4,5},{5,4},{6,7},{7,6},{8,9},{9,8},{10,11... | collective-permute-start | bytes 552968 | tf_op jit(solution)/shard_map/ppermute | solution.py:32
  108.7 11.8 %collective-permute-start.45 = (bf16[240,384]{1,0:T(8,128)(2,1)S(1)}, bf16[240,384]{1,0:T(8,128)(2,1)S(1)}, u32[]{:S(2)}, u32[]{:S(2)}) collective-permute-start(bf16[240,384]{1,0:T(8,128)(2,1)S(1)} %broadcast_select_fusion.5), channel_id=1, source_target_pairs={{0,1},{1,0},{2,3},{3,2},{4,5},{5,4},{6,7},{7,6},{8,9},{9,8},{10,11... | collective-permute-start | bytes 552968 | tf_op jit(solution)/shard_map/ppermute | solution.py:32
  113.2 11.7 %collective-permute-start.16 = (bf16[240,384]{1,0:T(8,128)(2,1)S(1)}, bf16[240,384]{1,0:T(8,128)(2,1)S(1)}, u32[]{:S(2)}, u32[]{:S(2)}) collective-permute-start(bf16[240,384]{1,0:T(8,128)(2,1)S(1)} %broadcast_select_fusion.11), channel_id=1, source_target_pairs={{0,1},{1,0},{2,3},{3,2},{4,5},{5,4},{6,7},{7,6},{8,9},{9,8},{10,11... | collective-permute-start | bytes 552968 | tf_op jit(solution)/shard_map/ppermute | solution.py:32
  113.3 8.8 %collective-permute-start.20 = (bf16[240,384]{1,0:T(8,128)(2,1)}, bf16[240,384]{1,0:T(8,128)(2,1)S(1)}, u32[]{:S(2)}, u32[]{:S(2)}) collective-permute-start(bf16[240,384]{1,0:T(8,128)(2,1)} %collective-permute-done.19.refs_11_.refs_8_), channel_id=1, source_target_pairs={{1,2},{2,1},{0,0},{3,3},{5,6},{6,5},{4,4},{7,7},{9,10},{10,9},{8,8... | collective-permute-start | bytes 552968 | tf_op jit(solution)/shard_map/ppermute | solution.py:32
  115.9 10.7 %collective-permute-start.47 = (bf16[240,384]{1,0:T(8,128)(2,1)S(1)}, bf16[240,384]{1,0:T(8,128)(2,1)S(1)}, u32[]{:S(2)}, u32[]{:S(2)}) collective-permute-start(bf16[240,384]{1,0:T(8,128)(2,1)S(1)} %broadcast_select_fusion.3), channel_id=1, source_target_pairs={{0,1},{1,0},{2,3},{3,2},{4,5},{5,4},{6,7},{7,6},{8,9},{9,8},{10,11... | collective-permute-start | bytes 552968 | tf_op jit(solution)/shard_map/ppermute | solution.py:32
  121.4 14.1 %collective-permute-start.48 = (bf16[240,384]{1,0:T(8,128)(2,1)S(1)}, bf16[240,384]{1,0:T(8,128)(2,1)S(1)}, u32[]{:S(2)}, u32[]{:S(2)}) collective-permute-start(bf16[240,384]{1,0:T(8,128)(2,1)S(1)} %fusion.11), channel_id=1, source_target_pairs={{1,2},{2,1},{0,0},{3,3},{5,6},{6,5},{4,4},{7,7},{9,10},{10,9},{8,8... | collective-permute-start | bytes 552968 | tf_op jit(solution)/shard_map/ppermute | solution.py:32
  123.1 7.5 %collective-permute-start.21 = (bf16[240,384]{1,0:T(8,128)(2,1)S(1)}, bf16[240,384]{1,0:T(8,128)(2,1)S(1)}, u32[]{:S(2)}, u32[]{:S(2)}) collective-permute-start(bf16[240,384]{1,0:T(8,128)(2,1)S(1)} %broadcast_select_fusion.10), channel_id=1, source_target_pairs={{0,1},{1,0},{2,3},{3,2},{4,5},{5,4},{6,7},{7,6},{8,9},{9,8},{10,11... | collective-permute-start | bytes 552968 | tf_op jit(solution)/shard_map/ppermute | solution.py:32
  127.6 20.2 %collective-permute-start.50 = (bf16[240,384]{1,0:T(8,128)(2,1)S(1)}, bf16[240,384]{1,0:T(8,128)(2,1)S(1)}, u32[]{:S(2)}, u32[]{:S(2)}) collective-permute-start(bf16[240,384]{1,0:T(8,128)(2,1)S(1)} %fusion.12), channel_id=1, source_target_pairs={{1,2},{2,1},{0,0},{3,3},{5,6},{6,5},{4,4},{7,7},{9,10},{10,9},{8,8... | collective-permute-start | bytes 552968 | tf_op jit(solution)/shard_map/ppermute | solution.py:32
  131.4 7.6 %collective-permute-start.18 = (bf16[240,384]{1,0:T(8,128)(2,1)S(1)}, bf16[240,384]{1,0:T(8,128)(2,1)S(1)}, u32[]{:S(2)}, u32[]{:S(2)}) collective-permute-start(bf16[240,384]{1,0:T(8,128)(2,1)S(1)} %add_convert_fusion.20), channel_id=1, source_target_pairs={{0,1},{1,0},{2,3},{3,2},{4,5},{5,4},{6,7},{7,6},{8,9},{9,8},{10,11... | collective-permute-start | bytes 552968 | tf_op jit(solution)/shard_map/ppermute | solution.py:32
  135.6 12.2 %collective-permute-start.49 = (bf16[240,384]{1,0:T(8,128)(2,1)S(1)}, bf16[240,384]{1,0:T(8,128)(2,1)S(1)}, u32[]{:S(2)}, u32[]{:S(2)}) collective-permute-start(bf16[240,384]{1,0:T(8,128)(2,1)S(1)} %add_convert_fusion.8), channel_id=1, source_target_pairs={{0,1},{1,0},{2,3},{3,2},{4,5},{5,4},{6,7},{7,6},{8,9},{9,8},{10,11... | collective-permute-start | bytes 552968 | tf_op jit(solution)/shard_map/ppermute | solution.py:32
  140.5 21.5 %collective-permute-start.23 = (bf16[240,384]{1,0:T(8,128)(2,1)}, bf16[240,384]{1,0:T(8,128)(2,1)S(1)}, u32[]{:S(2)}, u32[]{:S(2)}) collective-permute-start(bf16[240,384]{1,0:T(8,128)(2,1)} %get-tuple-element.105.refs_0_.refs_12_.refs_7_), channel_id=1, source_target_pairs={{1,2},{2,1},{0,0},{3,3},{5,6},{6,5},{4,4},{7,7},{9,10},{10,9},{8,8... | collective-permute-start | bytes 552968 | tf_op jit(solution)/shard_map/ppermute | solution.py:32
  149.4 34.7 %collective-permute-start.52 = (bf16[240,384]{1,0:T(8,128)(2,1)}, bf16[240,384]{1,0:T(8,128)(2,1)}, u32[]{:S(2)}, u32[]{:S(2)}) collective-permute-start(bf16[240,384]{1,0:T(8,128)(2,1)} %get-tuple-element.131.refs_6_.refs_1_), channel_id=1, source_target_pairs={{1,2},{2,1},{0,0},{3,3},{5,6},{6,5},{4,4},{7,7},{9,10},{10,9},{8,8... | collective-permute-start | bytes 552968 | tf_op jit(solution)/shard_map/ppermute | solution.py:32
  152.4 34.8 %collective-permute-start.51 = (bf16[240,384]{1,0:T(8,128)(2,1)}, bf16[240,384]{1,0:T(8,128)(2,1)}, u32[]{:S(2)}, u32[]{:S(2)}) collective-permute-start(bf16[240,384]{1,0:T(8,128)(2,1)} %get-tuple-element.131.refs_6_.refs_1_), channel_id=1, source_target_pairs={{0,1},{1,0},{2,3},{3,2},{4,5},{5,4},{6,7},{7,6},{8,9},{9,8},{10,11... | collective-permute-start | bytes 552968 | tf_op jit(solution)/shard_map/ppermute | solution.py:32
  156.6 34.1 %collective-permute-start.27 = (bf16[240,384]{1,0:T(8,128)(2,1)}, bf16[240,384]{1,0:T(8,128)(2,1)}, u32[]{:S(2)}, u32[]{:S(2)}) collective-permute-start(bf16[240,384]{1,0:T(8,128)(2,1)} %get-tuple-element.105.refs_0_.refs_12_.refs_7_), channel_id=1, source_target_pairs={{0,1},{1,0},{2,3},{3,2},{4,5},{5,4},{6,7},{7,6},{8,9},{9,8},{10,11... | collective-permute-start | bytes 552968 | tf_op jit(solution)/shard_map/ppermute | solution.py:32
  185.2 11.2 %collective-permute-start.53 = (bf16[240,384]{1,0:T(8,128)(2,1)S(1)}, bf16[240,384]{1,0:T(8,128)(2,1)S(1)}, u32[]{:S(2)}, u32[]{:S(2)}) collective-permute-start(bf16[240,384]{1,0:T(8,128)(2,1)S(1)} %broadcast_select_fusion.2), channel_id=1, source_target_pairs={{0,1},{1,0},{2,3},{3,2},{4,5},{5,4},{6,7},{7,6},{8,9},{9,8},{10,11... | collective-permute-start | bytes 552968 | tf_op jit(solution)/shard_map/ppermute | solution.py:32
  189.8 11.4 %collective-permute-start.24 = (bf16[240,384]{1,0:T(8,128)(2,1)S(1)}, bf16[240,384]{1,0:T(8,128)(2,1)S(1)}, u32[]{:S(2)}, u32[]{:S(2)}) collective-permute-start(bf16[240,384]{1,0:T(8,128)(2,1)S(1)} %broadcast_select_fusion.9), channel_id=1, source_target_pairs={{0,1},{1,0},{2,3},{3,2},{4,5},{5,4},{6,7},{7,6},{8,9},{9,8},{10,11... | collective-permute-start | bytes 552968 | tf_op jit(solution)/shard_map/ppermute | solution.py:32
  190.7 7.4 %collective-permute-start.28 = (bf16[240,384]{1,0:T(8,128)(2,1)}, bf16[240,384]{1,0:T(8,128)(2,1)S(1)}, u32[]{:S(2)}, u32[]{:S(2)}) collective-permute-start(bf16[240,384]{1,0:T(8,128)(2,1)} %collective-permute-done.27.refs_13_.refs_8_), channel_id=1, source_target_pairs={{1,2},{2,1},{0,0},{3,3},{5,6},{6,5},{4,4},{7,7},{9,10},{10,9},{8,8... | collective-permute-start | bytes 552968 | tf_op jit(solution)/shard_map/ppermute | solution.py:32
  193.2 9.6 %collective-permute-start.55 = (bf16[240,384]{1,0:T(8,128)(2,1)S(1)}, bf16[240,384]{1,0:T(8,128)(2,1)S(1)}, u32[]{:S(2)}, u32[]{:S(2)}) collective-permute-start(bf16[240,384]{1,0:T(8,128)(2,1)S(1)} %broadcast_select_fusion.1), channel_id=1, source_target_pairs={{0,1},{1,0},{2,3},{3,2},{4,5},{5,4},{6,7},{7,6},{8,9},{9,8},{10,11... | collective-permute-start | bytes 552968 | tf_op jit(solution)/shard_map/ppermute | solution.py:32
  197.4 7.0 %collective-permute-start.56 = (bf16[240,384]{1,0:T(8,128)(2,1)S(1)}, bf16[240,384]{1,0:T(8,128)(2,1)S(1)}, u32[]{:S(2)}, u32[]{:S(2)}) collective-permute-start(bf16[240,384]{1,0:T(8,128)(2,1)S(1)} %fusion.13), channel_id=1, source_target_pairs={{1,2},{2,1},{0,0},{3,3},{5,6},{6,5},{4,4},{7,7},{9,10},{10,9},{8,8... | collective-permute-start | bytes 552968 | tf_op jit(solution)/shard_map/ppermute | solution.py:32
  198.2 11.9 %collective-permute-start.29 = (bf16[240,384]{1,0:T(8,128)(2,1)S(1)}, bf16[240,384]{1,0:T(8,128)(2,1)S(1)}, u32[]{:S(2)}, u32[]{:S(2)}) collective-permute-start(bf16[240,384]{1,0:T(8,128)(2,1)S(1)} %broadcast_select_fusion.8), channel_id=1, source_target_pairs={{0,1},{1,0},{2,3},{3,2},{4,5},{5,4},{6,7},{7,6},{8,9},{9,8},{10,11... | collective-permute-start | bytes 552968 | tf_op jit(solution)/shard_map/ppermute | solution.py:32
  202.1 8.7 %collective-permute-start.25 = (bf16[240,384]{1,0:T(8,128)(2,1)S(1)}, bf16[240,384]{1,0:T(8,128)(2,1)S(1)}, u32[]{:S(2)}, u32[]{:S(2)}) collective-permute-start(bf16[240,384]{1,0:T(8,128)(2,1)S(1)} %fusion.5), channel_id=1, source_target_pairs={{1,2},{2,1},{0,0},{3,3},{5,6},{6,5},{4,4},{7,7},{9,10},{10,9},{8,8... | collective-permute-start | bytes 552968 | tf_op jit(solution)/shard_map/ppermute | solution.py:32
  203.8 15.9 %collective-permute-start.58 = (bf16[240,384]{1,0:T(8,128)(2,1)S(1)}, bf16[240,384]{1,0:T(8,128)(2,1)S(1)}, u32[]{:S(2)}, u32[]{:S(2)}) collective-permute-start(bf16[240,384]{1,0:T(8,128)(2,1)S(1)} %fusion.14), channel_id=1, source_target_pairs={{1,2},{2,1},{0,0},{3,3},{5,6},{6,5},{4,4},{7,7},{9,10},{10,9},{8,8... | collective-permute-start | bytes 552968 | tf_op jit(solution)/shard_map/ppermute | solution.py:32
  205.5 14.3 %collective-permute-start.57 = (bf16[240,384]{1,0:T(8,128)(2,1)S(1)}, bf16[240,384]{1,0:T(8,128)(2,1)S(1)}, u32[]{:S(2)}, u32[]{:S(2)}) collective-permute-start(bf16[240,384]{1,0:T(8,128)(2,1)S(1)} %add_convert_fusion.5), channel_id=1, source_target_pairs={{0,1},{1,0},{2,3},{3,2},{4,5},{5,4},{6,7},{7,6},{8,9},{9,8},{10,11... | collective-permute-start | bytes 552968 | tf_op jit(solution)/shard_map/ppermute | solution.py:32
  210.1 14.5 %collective-permute-start.30 = (bf16[240,384]{1,0:T(8,128)(2,1)S(1)}, bf16[240,384]{1,0:T(8,128)(2,1)S(1)}, u32[]{:S(2)}, u32[]{:S(2)}) collective-permute-start(bf16[240,384]{1,0:T(8,128)(2,1)S(1)} %fusion.6), channel_id=1, source_target_pairs={{1,2},{2,1},{0,0},{3,3},{5,6},{6,5},{4,4},{7,7},{9,10},{10,9},{8,8... | collective-permute-start | bytes 552968 | tf_op jit(solution)/shard_map/ppermute | solution.py:32
  211.8 12.8 %collective-permute-start.26 = (bf16[240,384]{1,0:T(8,128)(2,1)S(1)}, bf16[240,384]{1,0:T(8,128)(2,1)S(1)}, u32[]{:S(2)}, u32[]{:S(2)}) collective-permute-start(bf16[240,384]{1,0:T(8,128)(2,1)S(1)} %add_convert_fusion.17), channel_id=1, source_target_pairs={{0,1},{1,0},{2,3},{3,2},{4,5},{5,4},{6,7},{7,6},{8,9},{9,8},{10,11... | collective-permute-start | bytes 552968 | tf_op jit(solution)/shard_map/ppermute | solution.py:32
  221.4 12.8 %collective-permute-start.60 = (bf16[240,384]{1,0:T(8,128)(2,1)}, bf16[240,384]{1,0:T(8,128)(2,1)S(1)}, u32[]{:S(2)}, u32[]{:S(2)}) collective-permute-start(bf16[240,384]{1,0:T(8,128)(2,1)} %get-tuple-element.145.refs_6_.refs_1_), channel_id=1, source_target_pairs={{1,2},{2,1},{0,0},{3,3},{5,6},{6,5},{4,4},{7,7},{9,10},{10,9},{8,8... | collective-permute-start | bytes 552968 | tf_op jit(solution)/shard_map/ppermute | solution.py:32
  223.0 12.8 %collective-permute-start.59 = (bf16[240,384]{1,0:T(8,128)(2,1)}, bf16[240,384]{1,0:T(8,128)(2,1)}, u32[]{:S(2)}, u32[]{:S(2)}) collective-permute-start(bf16[240,384]{1,0:T(8,128)(2,1)} %get-tuple-element.145.refs_6_.refs_1_), channel_id=1, source_target_pairs={{0,1},{1,0},{2,3},{3,2},{4,5},{5,4},{6,7},{7,6},{8,9},{9,8},{10,11... | collective-permute-start | bytes 552968 | tf_op jit(solution)/shard_map/ppermute | solution.py:32
  225.4 16.1 %collective-permute-start.35 = (bf16[240,384]{1,0:T(8,128)(2,1)}, bf16[240,384]{1,0:T(8,128)(2,1)}, u32[]{:S(2)}, u32[]{:S(2)}) collective-permute-start(bf16[240,384]{1,0:T(8,128)(2,1)} %get-tuple-element.113.refs_0_.refs_12_.refs_7_), channel_id=1, source_target_pairs={{0,1},{1,0},{2,3},{3,2},{4,5},{5,4},{6,7},{7,6},{8,9},{9,8},{10,11... | collective-permute-start | bytes 552968 | tf_op jit(solution)/shard_map/ppermute | solution.py:32
  225.8 11.6 %collective-permute-start.31 = (bf16[240,384]{1,0:T(8,128)(2,1)}, bf16[240,384]{1,0:T(8,128)(2,1)}, u32[]{:S(2)}, u32[]{:S(2)}) collective-permute-start(bf16[240,384]{1,0:T(8,128)(2,1)} %get-tuple-element.113.refs_0_.refs_12_.refs_7_), channel_id=1, source_target_pairs={{1,2},{2,1},{0,0},{3,3},{5,6},{6,5},{4,4},{7,7},{9,10},{10,9},{8,8... | collective-permute-start | bytes 552968 | tf_op jit(solution)/shard_map/ppermute | solution.py:32
  235.3 11.4 %collective-permute-start.61 = (bf16[240,384]{1,0:T(8,128)(2,1)S(1)}, bf16[240,384]{1,0:T(8,128)(2,1)S(1)}, u32[]{:S(2)}, u32[]{:S(2)}) collective-permute-start(bf16[240,384]{1,0:T(8,128)(2,1)S(1)} %broadcast_select_fusion), channel_id=1, source_target_pairs={{0,1},{1,0},{2,3},{3,2},{4,5},{5,4},{6,7},{7,6},{8,9},{9,8},{10,11... | collective-permute-start | bytes 552968 | tf_op jit(solution)/shard_map/ppermute | solution.py:32
  235.8 7.4 %collective-permute-start.62 = (bf16[240,384]{1,0:T(8,128)(2,1)}, bf16[240,384]{1,0:T(8,128)(2,1)S(1)}, u32[]{:S(2)}, u32[]{:S(2)}) collective-permute-start(bf16[240,384]{1,0:T(8,128)(2,1)} %collective-permute-done.59.refs_7_.refs_2_), channel_id=1, source_target_pairs={{1,2},{2,1},{0,0},{3,3},{5,6},{6,5},{4,4},{7,7},{9,10},{10,9},{8,8... | collective-permute-start | bytes 552968 | tf_op jit(solution)/shard_map/ppermute | solution.py:32
  238.4 12.9 %collective-permute-start.32 = (bf16[240,384]{1,0:T(8,128)(2,1)S(1)}, bf16[240,384]{1,0:T(8,128)(2,1)S(1)}, u32[]{:S(2)}, u32[]{:S(2)}) collective-permute-start(bf16[240,384]{1,0:T(8,128)(2,1)S(1)} %broadcast_select_fusion.7), channel_id=1, source_target_pairs={{0,1},{1,0},{2,3},{3,2},{4,5},{5,4},{6,7},{7,6},{8,9},{9,8},{10,11... | collective-permute-start | bytes 552968 | tf_op jit(solution)/shard_map/ppermute | solution.py:32
  244.1 9.0 %collective-permute-start.63 = (bf16[240,384]{1,0:T(8,128)(2,1)S(1)}, bf16[240,384]{1,0:T(8,128)(2,1)S(1)}, u32[]{:S(2)}, u32[]{:S(2)}) collective-permute-start(bf16[240,384]{1,0:T(8,128)(2,1)S(1)} %broadcast_select_fusion.4), channel_id=1, source_target_pairs={{0,1},{1,0},{2,3},{3,2},{4,5},{5,4},{6,7},{7,6},{8,9},{9,8},{10,11... | collective-permute-start | bytes 552968 | tf_op jit(solution)/shard_map/ppermute | solution.py:32
  249.3 11.0 %collective-permute-start.37 = (bf16[240,384]{1,0:T(8,128)(2,1)S(1)}, bf16[240,384]{1,0:T(8,128)(2,1)S(1)}, u32[]{:S(2)}, u32[]{:S(2)}) collective-permute-start(bf16[240,384]{1,0:T(8,128)(2,1)S(1)} %broadcast_select_fusion.6), channel_id=1, source_target_pairs={{0,1},{1,0},{2,3},{3,2},{4,5},{5,4},{6,7},{7,6},{8,9},{9,8},{10,11... | collective-permute-start | bytes 552968 | tf_op jit(solution)/shard_map/ppermute | solution.py:32
  252.3 9.0 %collective-permute-start.33 = (bf16[240,384]{1,0:T(8,128)(2,1)S(1)}, bf16[240,384]{1,0:T(8,128)(2,1)S(1)}, u32[]{:S(2)}, u32[]{:S(2)}) collective-permute-start(bf16[240,384]{1,0:T(8,128)(2,1)S(1)} %fusion.7), channel_id=1, source_target_pairs={{1,2},{2,1},{0,0},{3,3},{5,6},{6,5},{4,4},{7,7},{9,10},{10,9},{8,8... | collective-permute-start | bytes 552968 | tf_op jit(solution)/shard_map/ppermute | solution.py:32
  254.0 17.1 %collective-permute-start.66 = (bf16[240,384]{1,0:T(8,128)(2,1)S(1)}, bf16[240,384]{1,0:T(8,128)(2,1)S(1)}, u32[]{:S(2)}, u32[]{:S(2)}) collective-permute-start(bf16[240,384]{1,0:T(8,128)(2,1)S(1)} %fusion.16), channel_id=1, source_target_pairs={{1,2},{2,1},{0,0},{3,3},{5,6},{6,5},{4,4},{7,7},{9,10},{10,9},{8,8... | collective-permute-start | bytes 552968 | tf_op jit(solution)/shard_map/ppermute | solution.py:32
  255.7 15.4 %collective-permute-start.65 = (bf16[240,384]{1,0:T(8,128)(2,1)S(1)}, bf16[240,384]{1,0:T(8,128)(2,1)S(1)}, u32[]{:S(2)}, u32[]{:S(2)}) collective-permute-start(bf16[240,384]{1,0:T(8,128)(2,1)S(1)} %add_convert_fusion.2), channel_id=1, source_target_pairs={{0,1},{1,0},{2,3},{3,2},{4,5},{5,4},{6,7},{7,6},{8,9},{9,8},{10,11... | collective-permute-start | bytes 552968 | tf_op jit(solution)/shard_map/ppermute | solution.py:32
  260.4 10.9 %collective-permute-start.38 = (bf16[240,384]{1,0:T(8,128)(2,1)S(1)}, bf16[240,384]{1,0:T(8,128)(2,1)S(1)}, u32[]{:S(2)}, u32[]{:S(2)}) collective-permute-start(bf16[240,384]{1,0:T(8,128)(2,1)S(1)} %fusion.8), channel_id=1, source_target_pairs={{1,2},{2,1},{0,0},{3,3},{5,6},{6,5},{4,4},{7,7},{9,10},{10,9},{8,8... | collective-permute-start | bytes 552968 | tf_op jit(solution)/shard_map/ppermute | solution.py:32
  262.3 9.0 %collective-permute-start.34 = (bf16[240,384]{1,0:T(8,128)(2,1)S(1)}, bf16[240,384]{1,0:T(8,128)(2,1)S(1)}, u32[]{:S(2)}, u32[]{:S(2)}) collective-permute-start(bf16[240,384]{1,0:T(8,128)(2,1)S(1)} %add_convert_fusion.14), channel_id=1, source_target_pairs={{0,1},{1,0},{2,3},{3,2},{4,5},{5,4},{6,7},{7,6},{8,9},{9,8},{10,11... | collective-permute-start | bytes 552968 | tf_op jit(solution)/shard_map/ppermute | solution.py:32
  273.1 7.9 %collective-permute-start.67 = (bf16[240,384]{1,0:T(8,128)(2,1)S(1)}, bf16[240,384]{1,0:T(8,128)(2,1)S(1)}, u32[]{:S(2)}, u32[]{:S(2)}) collective-permute-start(bf16[240,384]{1,0:T(8,128)(2,1)S(1)} %get-tuple-element.165.refs_7_.refs_1_), channel_id=1, source_target_pairs={{0,1},{1,0},{2,3},{3,2},{4,5},{5,4},{6,7},{7,6},{8,9},{9,8},{10,11... | collective-permute-start | bytes 552968 | tf_op jit(solution)/shard_map/ppermute | solution.py:32
  274.2 7.5 %collective-permute-start.73 = (bf16[256,384]{1,0:T(8,128)(2,1)S(1)}, bf16[256,384]{1,0:T(8,128)(2,1)S(1)}, u32[]{:S(2)}, u32[]{:S(2)}) collective-permute-start(bf16[256,384]{1,0:T(8,128)(2,1)S(1)} %get-tuple-element.158.refs_0_.refs_13_.refs_7_), channel_id=1, source_target_pairs={{1,2},{2,1},{0,0},{3,3},{5,6},{6,5},{4,4},{7,7},{9,10},{10,9},{8,8... | collective-permute-start | bytes 589832 | tf_op jit(solution)/shard_map/ppermute | solution.py:32
  279.0 9.8 %collective-permute-start.75 = (bf16[256,384]{1,0:T(8,128)(2,1)S(1)}, bf16[256,384]{1,0:T(8,128)(2,1)S(1)}, u32[]{:S(2)}, u32[]{:S(2)}) collective-permute-start(bf16[256,384]{1,0:T(8,128)(2,1)S(1)} %collective-permute-done.72.refs_14_.refs_8_), channel_id=1, source_target_pairs={{1,2},{2,1},{0,0},{3,3},{5,6},{6,5},{4,4},{7,7},{9,10},{10,9},{8,8... | collective-permute-start | bytes 589832 | tf_op jit(solution)/shard_map/ppermute | solution.py:32
  279.7 9.2 %collective-permute-start.68 = (bf16[240,384]{1,0:T(8,128)(2,1)S(1)}, bf16[240,384]{1,0:T(8,128)(2,1)S(1)}, u32[]{:S(2)}, u32[]{:S(2)}) collective-permute-start(bf16[240,384]{1,0:T(8,128)(2,1)S(1)} %get-tuple-element.165.refs_7_.refs_1_), channel_id=1, source_target_pairs={{1,2},{2,1},{0,0},{3,3},{5,6},{6,5},{4,4},{7,7},{9,10},{10,9},{8,8... | collective-permute-start | bytes 552968 | tf_op jit(solution)/shard_map/ppermute | solution.py:32
  281.0 9.8 %collective-permute-start.70 = (bf16[240,384]{1,0:T(8,128)(2,1)S(1)}, bf16[240,384]{1,0:T(8,128)(2,1)S(1)}, u32[]{:S(2)}, u32[]{:S(2)}) collective-permute-start(bf16[240,384]{1,0:T(8,128)(2,1)S(1)} %collective-permute-done.67.refs_8_.refs_2_), channel_id=1, source_target_pairs={{1,2},{2,1},{0,0},{3,3},{5,6},{6,5},{4,4},{7,7},{9,10},{10,9},{8,8... | collective-permute-start | bytes 552968 | tf_op jit(solution)/shard_map/ppermute | solution.py:32
  281.7 16.9 %collective-permute-start.74 = (bf16[256,384]{1,0:T(8,128)(2,1)S(1)}, bf16[256,384]{1,0:T(8,128)(2,1)S(1)}, u32[]{:S(2)}, u32[]{:S(2)}) collective-permute-start(bf16[256,384]{1,0:T(8,128)(2,1)S(1)} %collective-permute-done.73.refs_16_.refs_10_), channel_id=1, source_target_pairs={{0,1},{1,0},{2,3},{3,2},{4,5},{5,4},{6,7},{7,6},{8,9},{9,8},{10,11... | collective-permute-start | bytes 589832 | tf_op jit(solution)/shard_map/ppermute | solution.py:32
  288.8 9.8 %collective-permute-start.76 = (bf16[256,384]{1,0:T(8,128)(2,1)S(1)}, bf16[256,384]{1,0:T(8,128)(2,1)S(1)}, u32[]{:S(2)}, u32[]{:S(2)}) collective-permute-start(bf16[256,384]{1,0:T(8,128)(2,1)S(1)} %collective-permute-done.75.refs_18_.refs_12_), channel_id=1, source_target_pairs={{0,1},{1,0},{2,3},{3,2},{4,5},{5,4},{6,7},{7,6},{8,9},{9,8},{10,11... | collective-permute-start | bytes 589832 | tf_op jit(solution)/shard_map/ppermute | solution.py:32
  288.9 9.7 %collective-permute-start.69 = (bf16[240,384]{1,0:T(8,128)(2,1)S(1)}, bf16[240,384]{1,0:T(8,128)(2,1)S(1)}, u32[]{:S(2)}, u32[]{:S(2)}) collective-permute-start(bf16[240,384]{1,0:T(8,128)(2,1)S(1)} %collective-permute-done.68.refs_10_.refs_4_), channel_id=1, source_target_pairs={{0,1},{1,0},{2,3},{3,2},{4,5},{5,4},{6,7},{7,6},{8,9},{9,8},{10,11... | collective-permute-start | bytes 552968 | tf_op jit(solution)/shard_map/ppermute | solution.py:32
  290.8 7.7 %collective-permute-start.71 = (bf16[240,384]{1,0:T(8,128)(2,1)S(1)}, bf16[240,384]{1,0:T(8,128)(2,1)S(1)}, u32[]{:S(2)}, u32[]{:S(2)}) collective-permute-start(bf16[240,384]{1,0:T(8,128)(2,1)S(1)} %collective-permute-done.70.refs_12_.refs_6_), channel_id=1, source_target_pairs={{0,1},{1,0},{2,3},{3,2},{4,5},{5,4},{6,7},{7,6},{8,9},{9,8},{10,11... | collective-permute-start | bytes 552968 | tf_op jit(solution)/shard_map/ppermute | solution.py:32
  307.7 7.3 %collective-permute-start.78 = (bf16[2,128,512]{2,1,0:T(8,128)(2,1)S(1)}, bf16[2,128,512]{2,1,0:T(8,128)(2,1)S(1)}, u32[]{:S(2)}, u32[]{:S(2)}) collective-permute-start(bf16[2,128,512]{2,1,0:T(8,128)(2,1)S(1)} %slice_bitcast_fusion), channel_id=1, source_target_pairs={{0,8},{4,12},{8,0},{12,4},{1,9},{5,13},{9,1},{13,5},{2,10},{6,14},... | collective-permute-start | bytes 786440 | tf_op jit(solution)/shard_map/ppermute | solution.py:32
  (135 other events, 1078.2 us)

commit v5 on v4

--- a/solution.py
+++ b/solution.py
@@ -8,7 +8,7 @@
 from jax.sharding import PartitionSpec as P
 
 F32, BF16 = jnp.float32, jnp.bfloat16
-VMEM_BYTES = 26 << 20
+VMEM_BYTES = 20 << 20
 
 
 def line_pairs(n, gather, step):
@@ -65,23 +65,25 @@
     return lax.dot_general(a, b, (dims, ((), ())), preferred_element_type=F32)
 
 
-def routing(scal, w_refs, expert, rows):
-    n = len(w_refs)
-    experts_all, tokens = w_refs[0].shape
-    ids = lax.broadcasted_iota(jnp.int32, (experts_all, tokens), 0)
+def routing(scal, names, scales, expert, rows):
+    n = len(names)
+    tokens = names[0].shape[1]
     which = scal[2 * n] + expert
-    weights = jnp.concatenate(
-        [jnp.sum(jnp.where(ids == which, w[...], 0.0), axis=0, keepdims=True) for w in w_refs],
-        axis=0,
+    hits = [ids[...] == which for ids in names]
+    weights = [
+        jnp.sum(jnp.where(hit, scale[...], 0.0), axis=0, keepdims=True)
+        for hit, scale in zip(hits, scales)
+    ]
+    chosen = jnp.concatenate(
+        [jnp.sum(jnp.where(hit, 1.0, 0.0), axis=0, keepdims=True) for hit in hits], axis=0
     )
-    chosen = weights > 0.0
     earlier = lax.broadcasted_iota(jnp.int32, (tokens, tokens), 0) < lax.broadcasted_iota(
         jnp.int32, (tokens, tokens), 1
     )
-    slots = dot(chosen.astype(F32).astype(BF16), earlier.astype(F32).astype(BF16))
-    slots = jnp.where(chosen, slots, -1.0).astype(jnp.int32)
+    slots = dot(chosen.astype(BF16), earlier.astype(F32).astype(BF16))
+    slots = jnp.where(chosen > 0.0, slots, -1.0).astype(jnp.int32)
     row = lax.broadcasted_iota(jnp.int32, (rows, tokens), 0)
-    return [(scal[k], weights[k : k + 1], row == slots[k : k + 1]) for k in range(n)]
+    return [(scal[k], weights[k], row == slots[k : k + 1]) for k in range(n)]
 
 
 def span_of(position, rows):
@@ -107,7 +109,7 @@
 
 def pre_kernel(n, expert, deps, scal, *refs):
     refs = refs[deps:]
-    w_refs, toks, ogs, refs = refs[:n], refs[n : 2 * n], refs[2 * n : 3 * n], refs[3 * n :]
+    names, scales, toks, ogs, refs = *(refs[k * n : (k + 1) * n] for k in range(4)), refs[4 * n :]
     weights, (in_ref, cot_ref, *refs) = refs[:3], refs[3:]
     outs, (token, gw, uw, dw, sems) = refs[: 2 * n], refs[2 * n :]
     rows, tile = in_ref.shape[0] // n, gw.shape[1] // 2
@@ -116,7 +118,7 @@
         for copy in group:
             copy.start()
     token[...] = jnp.zeros_like(token)
-    for k, (position, weight, hit) in enumerate(routing(scal, w_refs, expert, rows)):
+    for k, (position, weight, hit) in enumerate(routing(scal, names, scales, expert, rows)):
         pick = hit.astype(F32).astype(BF16)
         span = span_of(position, rows)
         in_ref[span, :] = dot(pick, toks[k][...]).astype(BF16)
@@ -173,6 +175,11 @@
         out[3 * rows :, 0:lanes] = jnp.concatenate(lines, axis=0).astype(BF16)
 
 
+def add_kernel(deps, *refs):
+    a, b, out = refs[deps:]
+    out[...] = (a[...].astype(F32) + b[...].astype(F32)).astype(BF16)
+
+
 def part_of(scal, n, q, group, start, size):
     span = pl.ds(start, size)
     if len(group) == 1:
@@ -201,7 +208,7 @@
 
 def out_kernel(n, expert, has_prev, last, sizes, deps, scal, *refs):
     refs = refs[deps:]
-    w_refs, refs = refs[:n], refs[n:]
+    names, scales, refs = refs[:n], refs[n : 2 * n], refs[2 * n :]
     if has_prev:
         prev, refs = refs[:2], refs[2:]
     halves, refs = split_pieces(refs, sizes)
@@ -214,9 +221,9 @@
         for copy in group:
             copy.start()
     token[...] = jnp.zeros_like(token)
-    routes = routing(scal, w_refs, expert, halves[0][0][0].shape[0] // 48 * 16)
+    routes = routing(scal, names, scales, expert, halves[0][0][0].shape[0] // 48 * 16)
     if last:
-        send_products(scal, w_refs, expert + 1, halves[1], held, near_p, far_p)
+        send_products(scal, names, scales, expert + 1, halves[1], held, near_p, far_p)
     tile = gw.shape[1] // 2
     eo, idl = 0.0, 0.0
     for h in range(2):
@@ -259,16 +266,16 @@
             dg[0] = dot(load_rows(scal, n, 0, halves[h]), cot_ref[...], ((0,), (0,))).astype(BF16)
 
 
-def send_products(scal, w_refs, local, pieces, held, near, far):
-    n, (_, extra, lanes) = len(w_refs), held.shape
+def send_products(scal, names, scales, local, pieces, held, near, far):
+    n, (_, extra, lanes) = len(names), held.shape
     first = pieces[0][0].shape[0] - extra
     for q, group in enumerate(pieces):
         held[q] = part_of(scal, n, q, group, first, extra)[:, 0:lanes]
-    experts_all, tokens = w_refs[0].shape
+    experts_all, tokens = near.shape[1:]
     ids = lax.broadcasted_iota(jnp.int32, (experts_all, tokens), 0)
     sums = [jnp.zeros((experts_all, tokens), F32) for _ in range(n)]
     for e in range(local):
-        for k, (position, _, hit) in enumerate(routing(scal, w_refs, e, lanes)):
+        for k, (position, _, hit) in enumerate(routing(scal, names, scales, e, lanes)):
             found = dot(held[position], hit.astype(F32).astype(BF16))
             value = found[3 * e : 3 * e + 1] + found[3 * e + 1 : 3 * e + 2] + found[3 * e + 2 : 3 * e + 3]
             sums[k] = sums[k] + jnp.where(ids == scal[2 * n] + e, value, 0.0)
@@ -277,6 +284,10 @@
             near[k] = sums[k]
         else:
             far[k - n // 2] = sums[k]
+
+
+def in_hbm(array):
+    return pltpu.with_memory_space_constraint(array, pltpu.HBM)
 
 
 def whole_spec(shape):
@@ -345,7 +356,6 @@
 
     ids_t, combine_t = expert_ids.T, combine.T
     named = ids_t[:, None, :] == jnp.arange(experts_all, dtype=jnp.int32)[None, :, None]
-    dense = jnp.sum(jnp.where(named, combine_t[:, None, :], 0.0), axis=0)
 
     along_x, across = Line("expert", chips, 2), Line("expert", peers, 1)
     swap = [(2 * x + c, 2 * x + 1 - c) for x in range(chips) for c in range(2)]
@@ -357,8 +367,11 @@
         ]
         return found + [across.send(piece, swap) for piece in found]
 
-    tok_all, og_all, w_all = gather_blocks(tokens), gather_blocks(out_grad), gather_blocks(dense)
-    w_specs, block_specs = [spec_of(w) for w in w_all], [spec_of(x) for x in tok_all + og_all]
+    routes = gather_blocks(ids_t) + gather_blocks(combine_t)
+    blocks = gather_blocks(tokens) + gather_blocks(out_grad)
+    for held in (routes, blocks):
+        held[0], held[n] = in_hbm(held[0]), in_hbm(held[n])
+    route_specs, block_specs = [spec_of(x) for x in routes], [spec_of(x) for x in blocks]
 
     mac = all_rows * width * hidden
     weight_bytes = 2 * width * hidden
@@ -368,7 +381,7 @@
     piece_bytes = 2 * 3 * rows * tile
     slot_shape = (all_rows, width)
 
-    weights = (gate_weight, up_weight, down_weight)
+    weights = [in_hbm(w) for w in (gate_weight, up_weight, down_weight)]
     held_weights = [pltpu.VMEM(w.shape[1:], BF16) for w in weights] + [
         pltpu.SemaphoreType.DMA((2, 3))
     ]
@@ -381,13 +394,13 @@
         inputs, cot, *parts, token = call(
             functools.partial(pre_kernel, n, e, len(deps)),
             1,
-            [SMEM_SPEC] + [ANY_SPEC] * len(deps) + w_specs + block_specs + [HBM_SPEC] * 3,
+            [SMEM_SPEC] + [ANY_SPEC] * len(deps) + route_specs + block_specs + [HBM_SPEC] * 3,
             [whole_spec(slot_shape)] * 2 + [whole_spec(piece_shape)] * (2 * n) + [whole_spec(TOKEN)],
             [like(slot_shape)] * 2 + [like(piece_shape)] * (2 * n) + [like(TOKEN, F32)],
             6 * mac,
             3 * weight_bytes + 2 * n * piece_bytes,
             scratch_shapes=held_weights,
-        )(scal, *deps, *w_all, *tok_all, *og_all, *weights)
+        )(scal, *deps, *routes, *blocks, *weights)
         return (inputs, cot), [parts[:n], parts[n:]], token
 
     def mid(e, h, totals, products, deps=()):
@@ -405,6 +418,17 @@
             4 * piece_bytes,
         )(*deps, *totals, *others)
 
+    def add(a, b, deps):
+        return call(
+            functools.partial(add_kernel, len(deps)),
+            1,
+            [ANY_SPEC] * len(deps) + [whole_spec(piece_shape)] * 2,
+            whole_spec(piece_shape),
+            like(piece_shape),
+            3 * rows * tile,
+            3 * piece_bytes,
+        )(*deps, a, b)
+
     def flatten(halves):
         return [x for pieces in halves for group in pieces for x in group]
 
@@ -421,7 +445,7 @@
             1,
             [SMEM_SPEC]
             + [ANY_SPEC] * len(deps)
-            + w_specs
+            + route_specs
             + ([whole_spec(sum_shape)] * 2 if e > 0 else [])
             + [spec_of(x) for x in flat]
             + [HBM_SPEC] * 3,
@@ -436,7 +460,7 @@
             scratch_shapes=held_weights
             + [pltpu.VMEM(slot_shape, BF16)] * 2
             + ([pltpu.VMEM((n, extra, 128), BF16)] if last else []),
-        )(scal, *deps, *w_all, *prev, *flat, *weights)
+        )(scal, *deps, *routes, *prev, *flat, *weights)
 
     def grad(e, slots, halves, prev, deps):
         flat = flatten(halves)
@@ -464,11 +488,8 @@
     def inner(value):
         return along_z.send(value, [(1, 2), (2, 1), (0, 0), (3, 3)])
 
-    def after(token):
-        return at_end if token is None else at_end & (token[0, 0] == 0.0)
-
-    def unless(end, value):
-        return jnp.where(end, jnp.zeros_like(value), value)
+    def unless_end(value):
+        return jnp.where(at_end, jnp.zeros_like(value), value)
 
     products, sums, grads = [], [], []
 
@@ -480,7 +501,7 @@
 
     if swaps:
         flight, arrived = [None, None], None
-        slots, parts, pre_token = pre(0, [])
+        slots, parts, _ = pre(0, [])
         grad_token = None
         for e in range(local):
             more = e < local - 1
@@ -491,22 +512,23 @@
                     first.append((outer(x[3]), None))
                 else:
                     y, got_a, got_b = flight[h]
-                    end = after(grad_token if h == 0 else None)
-                    first.append((outer(jnp.where(end, x[3], got_b)), inner(got_a)))
+                    first.append((outer(jnp.where(at_end, x[3], got_b)), inner(got_a)))
             if more:
                 begun = pre(e + 1, [first[0][0]] if e == 0 else [flight[1][2]])
             for h in range(2):
                 x, (a1, b1) = parts[h], first[h]
-                end = after(begun[2] if more and h == int(e == 0) else None)
-                send_a2 = x[2] if e == 0 else jnp.where(end, x[2], b1)
-                second.append((outer(send_a2), inner(unless(end, add_rounded(x[3], a1)))))
+                tokens_seen = [begun[2]] if more and h == 1 else []
+                if grad_token is not None and h == 0:
+                    tokens_seen = [grad_token]
+                send_a2 = x[2] if e == 0 else jnp.where(at_end, x[2], b1)
+                second.append((outer(send_a2), inner(add(x[3], a1, tokens_seen))))
                 if e > 0:
                     y, got_a, got_b = flight[h]
                     halves.append([(y,), (got_a,), (a1, got_b), (second[h][0], b1)])
             for h in range(2):
                 x, (a2, b2) = parts[h], second[h]
-                a3 = outer(add_rounded(x[1], b2))
-                b3 = inner(unless(at_end, add_rounded(x[2], a2)))
+                a3 = outer(jnp.where(at_end, x[1], add_rounded(x[1], b2)))
+                b3 = inner(unless_end(add_rounded(x[2], a2)))
                 totals.append((x[0], a3, b3))
             wait = []
             if e > 0:

time: 319 us -> 237 us (0.74)
  local copies, waits for them, and re-layouts: 64.2 us -> 0.83 us
  other arithmetic: 31.2 us -> 2.18 us
  waiting for transfers between devices: 31.1 us -> 46.3 us
  starting transfers between devices: 133 us -> 137 us
  between operations: 5.41 us -> 1.45 us
  Pallas kernels: 51.1 us -> 47.7 us
    unnamed x236 -> x4, local copies, waits for them, and re-layouts: 60.8 us -> 0.01 us
    select_n x28, other arithmetic: 23.6 us -> 1.34 us  [the longest x8 0.5 us: body(): a3 = outer(jnp.where(at_end, x[1], add_rounded(x[1], b2)))]
    ppermute x81 -> x84, waiting for transfers between devices: 31.1 us -> 46.3 us  [send(): return lax.ppermute(value, self.axis, wide)]
    convert_element_type x9 -> x1, other arithmetic: 6.19 us -> 0.15 us  [add_rounded(): return (a.astype(F32) + b.astype(F32)).astype(BF16)]
    pallas_call x8, Pallas kernels: 7.19 us -> 1.85 us  [mid(): call(functools.partial(mid_kernel, len(deps), len(others)), 1, [ANY_SPEC]...]
    ppermute x81 -> x84, starting transfers between devices: 133 us -> 137 us  [send(): return lax.ppermute(value, self.axis, wide)]
    pallas_call x4, Pallas kernels: 12.5 us -> 16.4 us  [pre(): call(functools.partial(pre_kernel, n, e, len(deps)), 1, [SMEM_SPEC] + [AN...]
  transfers between devices with their start and end apart: 81 -> 84, of which waited for: 15 -> 23; matrix products, arithmetic and copies ran while one was open for 11% -> 1% of each run, Pallas kernels for 14% -> 16%
where the time goes in v5:
time: 237 us; the launch traced here: 236 us
  starting transfers between devices  137 us (58%)
  Pallas kernels  47.7 us (20%)
  waiting for transfers between devices  46.3 us (20%)
    ppermute x84, starting transfers between devices, send(): return lax.ppermute(value, self.axis, wide)  137 us
    ppermute x84, waiting for transfers between devices, send(): return lax.ppermute(value, self.axis, wide)  46.3 us
    pallas_call x4, Pallas kernels, pre(): call(functools.partial(pre_kernel, n, e, len(deps)), 1, [SMEM_SPEC] + [AN...  16.4 us
    pallas_call x4, Pallas kernels, out(): call(functools.partial(out_kernel, n, e, e > 0, last, sizes_of(halves[0])...  15.4 us
    pallas_call x4, Pallas kernels, grad(): call(functools.partial(grad_kernel, n, e > 0, sizes_of(halves[0]), len(de...  13.7 us
  transfers between devices with their start and end apart: 84, of which 23 were waited for; matrix products, arithmetic and copies ran while one was open for 1% of the time, Pallas kernels for 16%

profile of v5, /device:TPU:0, one launch (start us, length us, event | category | flops | bytes accessed | tf_op | source)
XLA Modules:
  0.0 235.8 jit_solution(11791709399498629691)
XLA Ops:
  0.6 3.0 %collective-permute-start.9 = (bf16[128,512]{1,0:T(8,128)(2,1)}, bf16[128,512]{1,0:T(8,128)(2,1)S(1)}, u32[]{:S(2)}, u32[]{:S(2)}) collective-permute-start(bf16[128,512]{1,0:T(8,128)(2,1)} %refs_13_.5), channel_id=1, source_target_pairs={{0,8},{4,12},{8,0},{12,4},{1,9},{5,13},{9,1},{13,5},{2,10},{6,14},... | collective-permute-start | bytes 393224 | tf_op jit(solution)/shard_map/ppermute | solution.py:32
  4.2 3.9 %collective-permute-done.9.refs_13_.refs_14_ = bf16[128,512]{1,0:T(8,128)(2,1)S(1)} collective-permute-done((bf16[128,512]{1,0:T(8,128)(2,1)}, bf16[128,512]{1,0:T(8,128)(2,1)S(1)}, u32[]{:S(2)}, u32[]{:S(2)}) %collective-permute-start.9) | collective-permute-done | bytes 131104 | tf_op jit(solution)/shard_map/ppermute | solution.py:32
  8.2 2.0 collective-permute-done.6.refs_9_.refs_10_
  10.2 1.7 collective-permute-start
  11.9 2.1 collective-permute-done.refs_1_.refs_2_
  14.0 1.7 collective-permute-start.3
  15.7 2.1 collective-permute-done.3.refs_5_.refs_6_
  17.8 1.4 collective-permute-done.1.refs_2_.refs_3_
  19.3 1.2 collective-permute-done.4.refs_6_.refs_7_
  20.7 1.0 collective-permute-done.2.refs_3_.refs_4_
  22.0 0.9 collective-permute-done.5.refs_7_.refs_8_
  22.9 4.3 %shard_map.118 = (bf16[320,512]{1,0:T(8,128)(2,1)S(1)}, bf16[320,512]{1,0:T(8,128)(2,1)S(1)}, bf16[240,384]{1,0:T(8,128)(2,1)S(1)}, bf16[240,384]{1,0:T(8,128)(2...) custom-call(s32[10]{0:T(128)S(1)} %stack.35.scal, ...), custom_call_target="tpu_custom_call" | custom-call | flops 754974720 | bytes 3833856 | tf_op jit(solution)/shard_map/pallas_call | solution.py:394
  27.3 1.9 collective-permute-start.12
  29.3 1.8 collective-permute-start.16
  31.4 3.4 %collective-permute-done.12.refs_0_.refs_1_ = bf16[240,384]{1,0:T(8,128)(2,1)S(1)} collective-permute-done((bf16[240,384]{1,0:T(8,128)(2,1)S(1)}, bf16[240,384]{1,0:T(8,128)(2,1)S(1)}, u32[]{:S(2)}, u32[]{:S(2)}) %collective-permute-start.12) | collective-permute-done | bytes 184352 | tf_op jit(solution)/shard_map/ppermute | solution.py:32
  35.5 3.2 %collective-permute-done.44 = bf16[240,384]{1,0:T(8,128)(2,1)S(1)} collective-permute-done((bf16[240,384]{1,0:T(8,128)(2,1)S(1)}, bf16[240,384]{1,0:T(8,128)(2,1)S(1)}, u32[]{:S(2)}, u32[]{:S(2)}) %collective-permute-start.44) | collective-permute-done | bytes 184352 | tf_op jit(solution)/shard_map/ppermute | solution.py:32
  39.5 3.2 %collective-permute-done.16 = bf16[240,384]{1,0:T(8,128)(2,1)S(1)} collective-permute-done((bf16[240,384]{1,0:T(8,128)(2,1)S(1)}, bf16[240,384]{1,0:T(8,128)(2,1)S(1)}, u32[]{:S(2)}, u32[]{:S(2)}) %collective-permute-start.16) | collective-permute-done | bytes 184352 | tf_op jit(solution)/shard_map/ppermute | solution.py:32
  43.4 4.0 %shard_map.119 = (bf16[320,512]{1,0:T(8,128)(2,1)S(1)}, bf16[320,512]{1,0:T(8,128)(2,1)S(1)}, bf16[240,384]{1,0:T(8,128)(2,1)S(1)}, bf16[240,384]{1,0:T(8,128)(2...) custom-call(s32[10]{0:T(128)S(1)} %stack.35.scal, ...), custom_call_target="tpu_custom_call" | custom-call | flops 754974720 | bytes 3833856 | tf_op jit(solution)/shard_map/pallas_call | solution.py:394
  48.3 6.4 %collective-permute-start.43 = (bf16[240,384]{1,0:T(8,128)(2,1)S(1)}, bf16[240,384]{1,0:T(8,128)(2,1)S(1)}, u32[]{:S(2)}, u32[]{:S(2)}) collective-permute-start(bf16[240,384]{1,0:T(8,128)(2,1)S(1)} %fusion.5), channel_id=1, source_target_pairs={{0,1},{1,0},{2,3},{3,2},{4,5},{5,4},{6,7},{7,6},{8,9},{9,8},{10,11... | collective-permute-start | bytes 552968 | tf_op jit(solution)/shard_map/ppermute | solution.py:32
  54.7 5.0 %collective-permute-start.15 = (bf16[240,384]{1,0:T(8,128)(2,1)S(1)}, bf16[240,384]{1,0:T(8,128)(2,1)S(1)}, u32[]{:S(2)}, u32[]{:S(2)}) collective-permute-start(bf16[240,384]{1,0:T(8,128)(2,1)S(1)} %fusion.1), channel_id=1, source_target_pairs={{0,1},{1,0},{2,3},{3,2},{4,5},{5,4},{6,7},{7,6},{8,9},{9,8},{10,11... | collective-permute-start | bytes 552968 | tf_op jit(solution)/shard_map/ppermute | solution.py:32
  60.6 5.2 %collective-permute-start.46 = (bf16[240,384]{1,0:T(8,128)(2,1)S(1)}, bf16[240,384]{1,0:T(8,128)(2,1)S(1)}, u32[]{:S(2)}, u32[]{:S(2)}) collective-permute-start(bf16[240,384]{1,0:T(8,128)(2,1)S(1)} %get-tuple-element.122.refs_8_.refs_1_), channel_id=1, source_target_pairs={{0,1},{1,0},{2,3},{3,2},{4,5},{5,4},{6,7},{7,6},{8,9},{9,8},{10,11... | collective-permute-start | bytes 552968 | tf_op jit(solution)/shard_map/ppermute | solution.py:32
  66.0 1.4 collective-permute-start.22
  68.1 2.9 %collective-permute-start.48 = (bf16[240,384]{1,0:T(8,128)(2,1)S(1)}, bf16[240,384]{1,0:T(8,128)(2,1)S(1)}, u32[]{:S(2)}, u32[]{:S(2)}) collective-permute-start(bf16[240,384]{1,0:T(8,128)(2,1)S(1)} %broadcast_select_fusion.5), channel_id=1, source_target_pairs={{0,1},{1,0},{2,3},{3,2},{4,5},{5,4},{6,7},{7,6},{8,9},{9,8},{10,11... | collective-permute-start | bytes 552968 | tf_op jit(solution)/shard_map/ppermute | solution.py:32
  71.0 2.5 %collective-permute-done.22.refs_15_.refs_8_ = bf16[240,384]{1,0:T(8,128)(2,1)S(1)} collective-permute-done((bf16[240,384]{1,0:T(8,128)(2,1)S(1)}, bf16[240,384]{1,0:T(8,128)(2,1)S(1)}, u32[]{:S(2)}, u32[]{:S(2)}) %collective-permute-start.22) | collective-permute-done | bytes 184352 | tf_op jit(solution)/shard_map/ppermute | solution.py:32
  74.2 3.6 %collective-permute-start.19 = (bf16[240,384]{1,0:T(8,128)(2,1)S(1)}, bf16[240,384]{1,0:T(8,128)(2,1)S(1)}, u32[]{:S(2)}, u32[]{:S(2)}) collective-permute-start(bf16[240,384]{1,0:T(8,128)(2,1)S(1)} %broadcast_select_fusion.11), channel_id=1, source_target_pairs={{0,1},{1,0},{2,3},{3,2},{4,5},{5,4},{6,7},{7,6},{8,9},{9,8},{10,11... | collective-permute-start | bytes 552968 | tf_op jit(solution)/shard_map/ppermute | solution.py:32
  78.5 4.0 %shard_map.122 = (bf16[320,512]{1,0:T(8,128)(2,1)S(1)}, bf16[320,512]{1,0:T(8,128)(2,1)S(1)}, bf16[240,384]{1,0:T(8,128)(2,1)S(1)}, bf16[240,384]{1,0:T(8,128)(2...) custom-call(s32[10]{0:T(128)S(1)} %stack.35.scal, ...), custom_call_target="tpu_custom_call" | custom-call | flops 754974720 | bytes 3833856 | tf_op jit(solution)/shard_map/pallas_call | solution.py:394
  82.6 3.3 %collective-permute-start.24 = (bf16[240,384]{1,0:T(8,128)(2,1)S(1)}, bf16[240,384]{1,0:T(8,128)(2,1)S(1)}, u32[]{:S(2)}, u32[]{:S(2)}) collective-permute-start(bf16[240,384]{1,0:T(8,128)(2,1)S(1)} %broadcast_select_fusion.10), channel_id=1, source_target_pairs={{0,1},{1,0},{2,3},{3,2},{4,5},{5,4},{6,7},{7,6},{8,9},{9,8},{10,11... | collective-permute-start | bytes 552968 | tf_op jit(solution)/shard_map/ppermute | solution.py:32
  88.1 1.4 collective-permute-done.24.refs_18_.refs_11_
  90.2 1.4 collective-permute-done.50.refs_12_.refs_5_
  92.4 7.8 %collective-permute-start.52 = (bf16[240,384]{1,0:T(8,128)(2,1)S(1)}, bf16[240,384]{1,0:T(8,128)(2,1)S(1)}, u32[]{:S(2)}, u32[]{:S(2)}) collective-permute-start(bf16[240,384]{1,0:T(8,128)(2,1)S(1)} %fusion.6), channel_id=1, source_target_pairs={{0,1},{1,0},{2,3},{3,2},{4,5},{5,4},{6,7},{7,6},{8,9},{9,8},{10,11... | collective-permute-start | bytes 552968 | tf_op jit(solution)/shard_map/ppermute | solution.py:32
  100.4 3.7 %shard_map.131 = (f32[2,2,128,512]{3,2,1,0:T(8,128)S(1)}, f32[2,2,128,512]{3,2,1,0:T(8,128)S(1)}, f32[8,128]{1,0:T(8,128)S(1)}) custom-call(s32[10]{0:T(128)S(1)} %stack.35.scal, s32[8,128]{1,0:T(8,128)} %bitcast.42, s32[8,128]{1,0:T(8,128)S(1)} %collective-permute-done.refs_1_.refs_2_, s32[8,128]{1,0:T(8,128)S(1)} %collective-permute-done.1.refs_2_.refs_3_, ...), custom_call_target="tpu_custom_call" | custom-call | flops 754974720 | bytes 4571136 | tf_op jit(solution)/shard_map/pallas_call | solution.py:443
  104.1 1.6 collective-permute-done.52.refs_2_
  106.6 4.4 %collective-permute-start.54 = (bf16[240,384]{1,0:T(8,128)(2,1)S(1)}, bf16[240,384]{1,0:T(8,128)(2,1)S(1)}, u32[]{:S(2)}, u32[]{:S(2)}) collective-permute-start(bf16[240,384]{1,0:T(8,128)(2,1)S(1)} %get-tuple-element.132.refs_10_.refs_1_), channel_id=1, source_target_pairs={{0,1},{1,0},{2,3},{3,2},{4,5},{5,4},{6,7},{7,6},{8,9},{9,8},{10,11... | collective-permute-start | bytes 552968 | tf_op jit(solution)/shard_map/ppermute | solution.py:32
  112.1 3.5 %shard_map.135 = (bf16[4,512,768]{2,1,0:T(8,128)(2,1)}, bf16[4,512,768]{2,1,0:T(8,128)(2,1)}, bf16[4,768,512]{2,1,0:T(8,128)(2,1)}, f32[8,128]{1,0:T(8,128)S(1)}) custom-call(s32[10]{0:T(128)S(1)} %stack.35.scal, bf16[320,512]{1,0:T(8,128)(2,1)S(1)} %get-tuple-element.138.in_ref, bf16[320,512]{1,0:T(8,128)(2,1)S(1)} %get-tuple-element.139.cot_ref, ...), custom_call_target="tpu_custom_call" | custom-call | flops 754974720 | bytes 4571136 | tf_op jit(solution)/shard_map/pallas_call | solution.py:468
  115.6 4.3 %collective-permute-start.56 = (bf16[240,384]{1,0:T(8,128)(2,1)S(1)}, bf16[240,384]{1,0:T(8,128)(2,1)S(1)}, u32[]{:S(2)}, u32[]{:S(2)}) collective-permute-start(bf16[240,384]{1,0:T(8,128)(2,1)S(1)} %broadcast_select_fusion.3), channel_id=1, source_target_pairs={{0,1},{1,0},{2,3},{3,2},{4,5},{5,4},{6,7},{7,6},{8,9},{9,8},{10,11... | collective-permute-start | bytes 552968 | tf_op jit(solution)/shard_map/ppermute | solution.py:32
  120.6 2.3 collective-permute-start.27
  123.6 4.0 %shard_map.125 = (bf16[320,512]{1,0:T(8,128)(2,1)S(1)}, bf16[320,512]{1,0:T(8,128)(2,1)S(1)}, bf16[240,384]{1,0:T(8,128)(2,1)S(1)}, bf16[240,384]{1,0:T(8,128)(2...) custom-call(s32[10]{0:T(128)S(1)} %stack.35.scal, ...), custom_call_target="tpu_custom_call" | custom-call | flops 754974720 | bytes 3833856 | tf_op jit(solution)/shard_map/pallas_call | solution.py:394
  128.4 4.6 %collective-permute-start.58 = (bf16[240,384]{1,0:T(8,128)(2,1)S(1)}, bf16[240,384]{1,0:T(8,128)(2,1)S(1)}, u32[]{:S(2)}, u32[]{:S(2)}) collective-permute-start(bf16[240,384]{1,0:T(8,128)(2,1)S(1)} %broadcast_select_fusion.2), channel_id=1, source_target_pairs={{0,1},{1,0},{2,3},{3,2},{4,5},{5,4},{6,7},{7,6},{8,9},{9,8},{10,11... | collective-permute-start | bytes 552968 | tf_op jit(solution)/shard_map/ppermute | solution.py:32
  134.0 4.7 %collective-permute-start.60 = (bf16[240,384]{1,0:T(8,128)(2,1)S(1)}, bf16[240,384]{1,0:T(8,128)(2,1)S(1)}, u32[]{:S(2)}, u32[]{:S(2)}) collective-permute-start(bf16[240,384]{1,0:T(8,128)(2,1)S(1)} %fusion.7), channel_id=1, source_target_pairs={{0,1},{1,0},{2,3},{3,2},{4,5},{5,4},{6,7},{7,6},{8,9},{9,8},{10,11... | collective-permute-start | bytes 552968 | tf_op jit(solution)/shard_map/ppermute | solution.py:32
  140.4 5.1 %collective-permute-start.29 = (bf16[240,384]{1,0:T(8,128)(2,1)S(1)}, bf16[240,384]{1,0:T(8,128)(2,1)S(1)}, u32[]{:S(2)}, u32[]{:S(2)}) collective-permute-start(bf16[240,384]{1,0:T(8,128)(2,1)S(1)} %fusion.3), channel_id=1, source_target_pairs={{0,1},{1,0},{2,3},{3,2},{4,5},{5,4},{6,7},{7,6},{8,9},{9,8},{10,11... | collective-permute-start | bytes 552968 | tf_op jit(solution)/shard_map/ppermute | solution.py:32
  145.5 3.7 %shard_map.134 = (f32[2,2,128,512]{3,2,1,0:T(8,128)S(1)}, f32[2,2,128,512]{3,2,1,0:T(8,128)S(1)}, f32[8,128]{1,0:T(8,128)S(1)}) custom-call(s32[10]{0:T(128)S(1)} %stack.35.scal, s32[8,128]{1,0:T(8,128)} %bitcast.44, s32[8,128]{1,0:T(8,128)S(1)} %collective-permute-done.refs_1_.refs_2_, s32[8,128]{1,0:T(8,128)S(1)} %collective-permute-done.1.refs_2_.refs_3_, ...), custom_call_target="tpu_custom_call" | custom-call | flops 754974720 | bytes 4571136 | tf_op jit(solution)/shard_map/pallas_call | solution.py:443
  150.1 2.4 %collective-permute-start.62 = (bf16[240,384]{1,0:T(8,128)(2,1)S(1)}, bf16[240,384]{1,0:T(8,128)(2,1)S(1)}, u32[]{:S(2)}, u32[]{:S(2)}) collective-permute-start(bf16[240,384]{1,0:T(8,128)(2,1)S(1)} %get-tuple-element.145.refs_10_.refs_1_), channel_id=1, source_target_pairs={{0,1},{1,0},{2,3},{3,2},{4,5},{5,4},{6,7},{7,6},{8,9},{9,8},{10,11... | collective-permute-start | bytes 552968 | tf_op jit(solution)/shard_map/ppermute | solution.py:32
  153.5 3.4 %shard_map.139 = (bf16[4,512,768]{2,1,0:T(8,128)(2,1)}, bf16[4,512,768]{2,1,0:T(8,128)(2,1)}, bf16[4,768,512]{2,1,0:T(8,128)(2,1)}, f32[8,128]{1,0:T(8,128)S(1)}) custom-call(s32[10]{0:T(128)S(1)} %stack.35.scal, bf16[320,512]{1,0:T(8,128)(2,1)S(1)} %get-tuple-element.151.in_ref, ...), custom_call_target="tpu_custom_call", output_to_operand_aliasing={{0}: (16, {}), {1}: (17, {}), {2}: (18, {})} | custom-call | flops 754974720 | bytes 4571136 | tf_op jit(solution)/shard_map/pallas_call | solution.py:468
  156.9 4.2 %collective-permute-start.64 = (bf16[240,384]{1,0:T(8,128)(2,1)S(1)}, bf16[240,384]{1,0:T(8,128)(2,1)S(1)}, u32[]{:S(2)}, u32[]{:S(2)}) collective-permute-start(bf16[240,384]{1,0:T(8,128)(2,1)S(1)} %broadcast_select_fusion.1), channel_id=1, source_target_pairs={{0,1},{1,0},{2,3},{3,2},{4,5},{5,4},{6,7},{7,6},{8,9},{9,8},{10,11... | collective-permute-start | bytes 552968 | tf_op jit(solution)/shard_map/ppermute | solution.py:32
  161.9 2.4 %collective-permute-start.35 = (bf16[240,384]{1,0:T(8,128)(2,1)S(1)}, bf16[240,384]{1,0:T(8,128)(2,1)S(1)}, u32[]{:S(2)}, u32[]{:S(2)}) collective-permute-start(bf16[240,384]{1,0:T(8,128)(2,1)S(1)} %broadcast_select_fusion.7), channel_id=1, source_target_pairs={{0,1},{1,0},{2,3},{3,2},{4,5},{5,4},{6,7},{7,6},{8,9},{9,8},{10,11... | collective-permute-start | bytes 552968 | tf_op jit(solution)/shard_map/ppermute | solution.py:32
  165.0 5.6 %collective-permute-start.66 = (bf16[240,384]{1,0:T(8,128)(2,1)S(1)}, bf16[240,384]{1,0:T(8,128)(2,1)S(1)}, u32[]{:S(2)}, u32[]{:S(2)}) collective-permute-start(bf16[240,384]{1,0:T(8,128)(2,1)S(1)} %broadcast_select_fusion), channel_id=1, source_target_pairs={{0,1},{1,0},{2,3},{3,2},{4,5},{5,4},{6,7},{7,6},{8,9},{9,8},{10,11... | collective-permute-start | bytes 552968 | tf_op jit(solution)/shard_map/ppermute | solution.py:32
  171.4 2.4 %collective-permute-start.40 = (bf16[240,384]{1,0:T(8,128)(2,1)S(1)}, bf16[240,384]{1,0:T(8,128)(2,1)S(1)}, u32[]{:S(2)}, u32[]{:S(2)}) collective-permute-start(bf16[240,384]{1,0:T(8,128)(2,1)S(1)} %broadcast_select_fusion.6), channel_id=1, source_target_pairs={{0,1},{1,0},{2,3},{3,2},{4,5},{5,4},{6,7},{7,6},{8,9},{9,8},{10,11... | collective-permute-start | bytes 552968 | tf_op jit(solution)/shard_map/ppermute | solution.py:32
  175.4 4.6 %collective-permute-start.68 = (bf16[240,384]{1,0:T(8,128)(2,1)S(1)}, bf16[240,384]{1,0:T(8,128)(2,1)S(1)}, u32[]{:S(2)}, u32[]{:S(2)}) collective-permute-start(bf16[240,384]{1,0:T(8,128)(2,1)S(1)} %fusion.8), channel_id=1, source_target_pairs={{0,1},{1,0},{2,3},{3,2},{4,5},{5,4},{6,7},{7,6},{8,9},{9,8},{10,11... | collective-permute-start | bytes 552968 | tf_op jit(solution)/shard_map/ppermute | solution.py:32
  180.8 3.8 %collective-permute-start.37 = (bf16[240,384]{1,0:T(8,128)(2,1)S(1)}, bf16[240,384]{1,0:T(8,128)(2,1)S(1)}, u32[]{:S(2)}, u32[]{:S(2)}) collective-permute-start(bf16[240,384]{1,0:T(8,128)(2,1)S(1)} %fusion.4), channel_id=1, source_target_pairs={{0,1},{1,0},{2,3},{3,2},{4,5},{5,4},{6,7},{7,6},{8,9},{9,8},{10,11... | collective-permute-start | bytes 552968 | tf_op jit(solution)/shard_map/ppermute | solution.py:32
  184.6 3.7 %shard_map.138 = (f32[2,2,128,512]{3,2,1,0:T(8,128)S(1)}, f32[2,2,128,512]{3,2,1,0:T(8,128)S(1)}, f32[8,128]{1,0:T(8,128)S(1)}) custom-call(s32[10]{0:T(128)S(1)} %stack.35.scal, s32[8,128]{1,0:T(8,128)} %bitcast.45, s32[8,128]{1,0:T(8,128)S(1)} %collective-permute-done.refs_1_.refs_2_, s32[8,128]{1,0:T(8,128)S(1)} %collective-permute-done.1.refs_2_.refs_3_, ...), custom_call_target="tpu_custom_call" | custom-call | flops 754974720 | bytes 4571136 | tf_op jit(solution)/shard_map/pallas_call | solution.py:443
  189.4 2.3 collective-permute-start.75
  192.4 5.1 %collective-permute-done.75.refs_18_.refs_8_ = bf16[256,384]{1,0:T(8,128)(2,1)S(1)} collective-permute-done((bf16[256,384]{1,0:T(8,128)(2,1)S(1)}, bf16[256,384]{1,0:T(8,128)(2,1)S(1)}, u32[]{:S(2)}, u32[]{:S(2)}) %collective-permute-start.75) | collective-permute-done | bytes 196640 | tf_op jit(solution)/shard_map/ppermute | solution.py:32
  198.9 2.6 %collective-permute-done.70.refs_12_.refs_2_ = bf16[240,384]{1,0:T(8,128)(2,1)S(1)} collective-permute-done((bf16[240,384]{1,0:T(8,128)(2,1)S(1)}, bf16[240,384]{1,0:T(8,128)(2,1)S(1)}, u32[]{:S(2)}, u32[]{:S(2)}) %collective-permute-start.70) | collective-permute-done | bytes 184352 | tf_op jit(solution)/shard_map/ppermute | solution.py:32
  202.4 6.4 %collective-permute-start.77 = (bf16[256,384]{1,0:T(8,128)(2,1)S(1)}, bf16[256,384]{1,0:T(8,128)(2,1)S(1)}, u32[]{:S(2)}, u32[]{:S(2)}) collective-permute-start(bf16[256,384]{1,0:T(8,128)(2,1)S(1)} %collective-permute-done.76.refs_20_.refs_10_), channel_id=1, source_target_pairs={{0,1},{1,0},{2,3},{3,2},{4,5},{5,4},{6,7},{7,6},{8,9},{9,8},{10,11... | collective-permute-start | bytes 589832 | tf_op jit(solution)/shard_map/ppermute | solution.py:32
  208.8 1.9 collective-permute-start.72
  210.8 2.0 collective-permute-start.74
  212.8 3.4 %shard_map.143 = (bf16[4,512,768]{2,1,0:T(8,128)(2,1)}, bf16[4,512,768]{2,1,0:T(8,128)(2,1)}, bf16[4,768,512]{2,1,0:T(8,128)(2,1)}, f32[8,128]{1,0:T(8,128)S(1)}) custom-call(s32[10]{0:T(128)S(1)} %stack.35.scal, bf16[320,512]{1,0:T(8,128)(2,1)S(1)} %get-tuple-element.99.in_ref, ...), custom_call_target="tpu_custom_call", output_to_operand_aliasing={{0}: (16, {}), {1}: (17, {}), {2}: (18, {})} | custom-call | flops 754974720 | bytes 4571136 | tf_op jit(solution)/shard_map/pallas_call | solution.py:468
  216.5 2.0 collective-permute-done.74.refs_15_.refs_5_
  218.5 4.2 %shard_map.144 = (bf16[2,2,128,512]{3,2,1,0:T(8,128)(2,1)S(1)}, bf16[2,2,128,512]{3,2,1,0:T(8,128)(2,1)S(1)}, f32[8,128]{1,0:T(8,128)}, f32[2,16,128]{2,1,0:T(8,128)S(1)}, f32[2,16,128]{2,1,0:T(8,128)S(1)}) custom-call(s32[10]{0:T(128)S(1)} %stack.35.scal, f32[8,128]{1,0:T(8,128)S(1)} %get-tuple-element.162.refs_0_, s32[8,128]{1,0:T(8,128)} %bitcast.46, ...), custom_call_target="tpu_custom_call" | custom-call | flops 754974720 | bytes 4571136 | tf_op jit(solution)/shard_map/pallas_call | solution.py:443
  223.9 1.4 collective-permute-start.83
  225.3 2.3 collective-permute-done.83
  227.8 1.5 collective-permute-start.81
  229.8 3.4 %shard_map.145 = (bf16[4,512,768]{2,1,0:T(8,128)(2,1)}, bf16[4,512,768]{2,1,0:T(8,128)(2,1)}, bf16[4,768,512]{2,1,0:T(8,128)(2,1)}, f32[8,128]{1,0:T(8,128)}) custom-call(s32[10]{0:T(128)S(1)} %stack.35.scal, bf16[320,512]{1,0:T(8,128)(2,1)S(1)} %get-tuple-element.168.in_ref, ...), custom_call_target="tpu_custom_call", output_to_operand_aliasing={{0}: (16, {}), {1}: (17, {}), {2}: (18, {})} | custom-call | flops 754974720 | bytes 4571136 | tf_op jit(solution)/shard_map/pallas_call | solution.py:468
  233.2 1.9 collective-permute-done.81
  (174 shorter events, 31.5 us)
Async XLA Ops:
  0.6 7.5 %collective-permute-start.9 = (bf16[128,512]{1,0:T(8,128)(2,1)}, bf16[128,512]{1,0:T(8,128)(2,1)S(1)}, u32[]{:S(2)}, u32[]{:S(2)}) collective-permute-start(bf16[128,512]{1,0:T(8,128)(2,1)} %refs_13_.5), channel_id=1, source_target_pairs={{0,8},{4,12},{8,0},{12,4},{1,9},{5,13},{9,1},{13,5},{2,10},{6,14},... | collective-permute-start | bytes 393224 | tf_op jit(solution)/shard_map/ppermute | solution.py:32
  3.7 19.2 %collective-permute-start.10 = (bf16[128,512]{1,0:T(8,128)(2,1)}, bf16[128,512]{1,0:T(8,128)(2,1)S(1)}, u32[]{:S(2)}, u32[]{:S(2)}) collective-permute-start(bf16[128,512]{1,0:T(8,128)(2,1)} %refs_13_.5), channel_id=1, source_target_pairs={{0,4},{4,0},{8,12},{12,8},{1,5},{5,1},{9,13},{13,9},{2,6},{6,2},{1... | collective-permute-start | bytes 393224 | tf_op jit(solution)/shard_map/ppermute | solution.py:32
  3.7 19.2 %collective-permute-start.7 = (bf16[128,512]{1,0:T(8,128)(2,1)}, bf16[128,512]{1,0:T(8,128)(2,1)S(1)}, u32[]{:S(2)}, u32[]{:S(2)}) collective-permute-start(bf16[128,512]{1,0:T(8,128)(2,1)} %refs_9_.5), channel_id=1, source_target_pairs={{0,4},{4,0},{8,12},{12,8},{1,5},{5,1},{9,13},{13,9},{2,6},{6,2},{1... | collective-permute-start | bytes 393224 | tf_op jit(solution)/shard_map/ppermute | solution.py:32
  8.2 14.7 %collective-permute-start.11 = (bf16[128,512]{1,0:T(8,128)(2,1)S(1)}, bf16[128,512]{1,0:T(8,128)(2,1)S(1)}, u32[]{:S(2)}, u32[]{:S(2)}) collective-permute-start(bf16[128,512]{1,0:T(8,128)(2,1)S(1)} %collective-permute-done.9.refs_13_.refs_14_), channel_id=1, source_target_pairs={{0,4},{4,0},{8,12},{12,8},{1,5},{5,1},{9,13},{13,9},{2,6},{6,2},{1... | collective-permute-start | bytes 393224 | tf_op jit(solution)/shard_map/ppermute | solution.py:32
  10.2 12.7 %collective-permute-start.8 = (bf16[128,512]{1,0:T(8,128)(2,1)S(1)}, bf16[128,512]{1,0:T(8,128)(2,1)S(1)}, u32[]{:S(2)}, u32[]{:S(2)}) collective-permute-start(bf16[128,512]{1,0:T(8,128)(2,1)S(1)} %collective-permute-done.6.refs_9_.refs_10_), channel_id=1, source_target_pairs={{0,4},{4,0},{8,12},{12,8},{1,5},{5,1},{9,13},{13,9},{2,6},{6,2},{1... | collective-permute-start | bytes 393224 | tf_op jit(solution)/shard_map/ppermute | solution.py:32
  27.3 7.5 %collective-permute-start.12 = (bf16[240,384]{1,0:T(8,128)(2,1)S(1)}, bf16[240,384]{1,0:T(8,128)(2,1)S(1)}, u32[]{:S(2)}, u32[]{:S(2)}) collective-permute-start(bf16[240,384]{1,0:T(8,128)(2,1)S(1)} %get-tuple-element.94.refs_0_), channel_id=1, source_target_pairs={{0,1},{1,0},{2,3},{3,2},{4,5},{5,4},{6,7},{7,6},{8,9},{9,8},{10,11... | collective-permute-start | bytes 552968 | tf_op jit(solution)/shard_map/ppermute | solution.py:32
  29.1 9.6 %collective-permute-start.44 = (bf16[240,384]{1,0:T(8,128)(2,1)S(1)}, bf16[240,384]{1,0:T(8,128)(2,1)S(1)}, u32[]{:S(2)}, u32[]{:S(2)}) collective-permute-start(bf16[240,384]{1,0:T(8,128)(2,1)S(1)} %get-tuple-element.119), channel_id=1, source_target_pairs={{0,1},{1,0},{2,3},{3,2},{4,5},{5,4},{6,7},{7,6},{8,9},{9,8},{10,11... | collective-permute-start | bytes 552968 | tf_op jit(solution)/shard_map/ppermute | solution.py:32
  29.3 13.3 %collective-permute-start.16 = (bf16[240,384]{1,0:T(8,128)(2,1)S(1)}, bf16[240,384]{1,0:T(8,128)(2,1)S(1)}, u32[]{:S(2)}, u32[]{:S(2)}) collective-permute-start(bf16[240,384]{1,0:T(8,128)(2,1)S(1)} %get-tuple-element.97), channel_id=1, source_target_pairs={{0,1},{1,0},{2,3},{3,2},{4,5},{5,4},{6,7},{7,6},{8,9},{9,8},{10,11... | collective-permute-start | bytes 552968 | tf_op jit(solution)/shard_map/ppermute | solution.py:32
  31.2 16.3 %collective-permute-start.13 = (bf16[240,384]{1,0:T(8,128)(2,1)S(1)}, bf16[240,384]{1,0:T(8,128)(2,1)S(1)}, u32[]{:S(2)}, u32[]{:S(2)}) collective-permute-start(bf16[240,384]{1,0:T(8,128)(2,1)S(1)} %get-tuple-element.96.refs_1_), channel_id=1, source_target_pairs={{0,1},{1,0},{2,3},{3,2},{4,5},{5,4},{6,7},{7,6},{8,9},{9,8},{10,11... | collective-permute-start | bytes 552968 | tf_op jit(solution)/shard_map/ppermute | solution.py:32
  34.8 13.4 %collective-permute-start.42 = (bf16[240,384]{1,0:T(8,128)(2,1)S(1)}, bf16[240,384]{1,0:T(8,128)(2,1)S(1)}, u32[]{:S(2)}, u32[]{:S(2)}) collective-permute-start(bf16[240,384]{1,0:T(8,128)(2,1)S(1)} %shard_map.129), channel_id=1, source_target_pairs={{1,2},{2,1},{0,0},{3,3},{5,6},{6,5},{4,4},{7,7},{9,10},{10,9},{8,8... | collective-permute-start | bytes 552968 | tf_op jit(solution)/shard_map/ppermute | solution.py:32
  38.8 20.9 %collective-permute-start.45 = (bf16[240,384]{1,0:T(8,128)(2,1)S(1)}, bf16[240,384]{1,0:T(8,128)(2,1)S(1)}, u32[]{:S(2)}, u32[]{:S(2)}) collective-permute-start(bf16[240,384]{1,0:T(8,128)(2,1)S(1)} %fusion.13), channel_id=1, source_target_pairs={{1,2},{2,1},{0,0},{3,3},{5,6},{6,5},{4,4},{7,7},{9,10},{10,9},{8,8... | collective-permute-start | bytes 552968 | tf_op jit(solution)/shard_map/ppermute | solution.py:32
  42.7 23.1 %collective-permute-start.17 = (bf16[240,384]{1,0:T(8,128)(2,1)S(1)}, bf16[240,384]{1,0:T(8,128)(2,1)S(1)}, u32[]{:S(2)}, u32[]{:S(2)}) collective-permute-start(bf16[240,384]{1,0:T(8,128)(2,1)S(1)} %fusion.9), channel_id=1, source_target_pairs={{1,2},{2,1},{0,0},{3,3},{5,6},{6,5},{4,4},{7,7},{9,10},{10,9},{8,8... | collective-permute-start | bytes 552968 | tf_op jit(solution)/shard_map/ppermute | solution.py:32
  47.5 7.2 %collective-permute-start.14 = (bf16[240,384]{1,0:T(8,128)(2,1)S(1)}, bf16[240,384]{1,0:T(8,128)(2,1)S(1)}, u32[]{:S(2)}, u32[]{:S(2)}) collective-permute-start(bf16[240,384]{1,0:T(8,128)(2,1)S(1)} %shard_map.120), channel_id=1, source_target_pairs={{1,2},{2,1},{0,0},{3,3},{5,6},{6,5},{4,4},{7,7},{9,10},{10,9},{8,8... | collective-permute-start | bytes 552968 | tf_op jit(solution)/shard_map/ppermute | solution.py:32
  48.3 11.5 %collective-permute-start.43 = (bf16[240,384]{1,0:T(8,128)(2,1)S(1)}, bf16[240,384]{1,0:T(8,128)(2,1)S(1)}, u32[]{:S(2)}, u32[]{:S(2)}) collective-permute-start(bf16[240,384]{1,0:T(8,128)(2,1)S(1)} %fusion.5), channel_id=1, source_target_pairs={{0,1},{1,0},{2,3},{3,2},{4,5},{5,4},{6,7},{7,6},{8,9},{9,8},{10,11... | collective-permute-start | bytes 552968 | tf_op jit(solution)/shard_map/ppermute | solution.py:32
  54.7 11.1 %collective-permute-start.15 = (bf16[240,384]{1,0:T(8,128)(2,1)S(1)}, bf16[240,384]{1,0:T(8,128)(2,1)S(1)}, u32[]{:S(2)}, u32[]{:S(2)}) collective-permute-start(bf16[240,384]{1,0:T(8,128)(2,1)S(1)} %fusion.1), channel_id=1, source_target_pairs={{0,1},{1,0},{2,3},{3,2},{4,5},{5,4},{6,7},{7,6},{8,9},{9,8},{10,11... | collective-permute-start | bytes 552968 | tf_op jit(solution)/shard_map/ppermute | solution.py:32
  59.9 8.2 %collective-permute-start.47 = (bf16[240,384]{1,0:T(8,128)(2,1)S(1)}, bf16[240,384]{1,0:T(8,128)(2,1)S(1)}, u32[]{:S(2)}, u32[]{:S(2)}) collective-permute-start(bf16[240,384]{1,0:T(8,128)(2,1)S(1)} %get-tuple-element.122.refs_8_.refs_1_), channel_id=1, source_target_pairs={{1,2},{2,1},{0,0},{3,3},{5,6},{6,5},{4,4},{7,7},{9,10},{10,9},{8,8... | collective-permute-start | bytes 552968 | tf_op jit(solution)/shard_map/ppermute | solution.py:32
  60.6 17.3 %collective-permute-start.46 = (bf16[240,384]{1,0:T(8,128)(2,1)S(1)}, bf16[240,384]{1,0:T(8,128)(2,1)S(1)}, u32[]{:S(2)}, u32[]{:S(2)}) collective-permute-start(bf16[240,384]{1,0:T(8,128)(2,1)S(1)} %get-tuple-element.122.refs_8_.refs_1_), channel_id=1, source_target_pairs={{0,1},{1,0},{2,3},{3,2},{4,5},{5,4},{6,7},{7,6},{8,9},{9,8},{10,11... | collective-permute-start | bytes 552968 | tf_op jit(solution)/shard_map/ppermute | solution.py:32
  66.0 7.6 %collective-permute-start.22 = (bf16[240,384]{1,0:T(8,128)(2,1)S(1)}, bf16[240,384]{1,0:T(8,128)(2,1)S(1)}, u32[]{:S(2)}, u32[]{:S(2)}) collective-permute-start(bf16[240,384]{1,0:T(8,128)(2,1)S(1)} %get-tuple-element.98.refs_14_.refs_7_), channel_id=1, source_target_pairs={{0,1},{1,0},{2,3},{3,2},{4,5},{5,4},{6,7},{7,6},{8,9},{9,8},{10,11... | collective-permute-start | bytes 552968 | tf_op jit(solution)/shard_map/ppermute | solution.py:32
  68.1 19.3 %collective-permute-start.48 = (bf16[240,384]{1,0:T(8,128)(2,1)S(1)}, bf16[240,384]{1,0:T(8,128)(2,1)S(1)}, u32[]{:S(2)}, u32[]{:S(2)}) collective-permute-start(bf16[240,384]{1,0:T(8,128)(2,1)S(1)} %broadcast_select_fusion.5), channel_id=1, source_target_pairs={{0,1},{1,0},{2,3},{3,2},{4,5},{5,4},{6,7},{7,6},{8,9},{9,8},{10,11... | collective-permute-start | bytes 552968 | tf_op jit(solution)/shard_map/ppermute | solution.py:32
  73.5 9.0 %collective-permute-start.23 = (bf16[240,384]{1,0:T(8,128)(2,1)S(1)}, bf16[240,384]{1,0:T(8,128)(2,1)S(1)}, u32[]{:S(2)}, u32[]{:S(2)}) collective-permute-start(bf16[240,384]{1,0:T(8,128)(2,1)S(1)} %collective-permute-done.22.refs_15_.refs_8_), channel_id=1, source_target_pairs={{1,2},{2,1},{0,0},{3,3},{5,6},{6,5},{4,4},{7,7},{9,10},{10,9},{8,8... | collective-permute-start | bytes 552968 | tf_op jit(solution)/shard_map/ppermute | solution.py:32
  74.2 12.4 %collective-permute-start.19 = (bf16[240,384]{1,0:T(8,128)(2,1)S(1)}, bf16[240,384]{1,0:T(8,128)(2,1)S(1)}, u32[]{:S(2)}, u32[]{:S(2)}) collective-permute-start(bf16[240,384]{1,0:T(8,128)(2,1)S(1)} %broadcast_select_fusion.11), channel_id=1, source_target_pairs={{0,1},{1,0},{2,3},{3,2},{4,5},{5,4},{6,7},{7,6},{8,9},{9,8},{10,11... | collective-permute-start | bytes 552968 | tf_op jit(solution)/shard_map/ppermute | solution.py:32
  77.9 8.1 %collective-permute-start.49 = (bf16[240,384]{1,0:T(8,128)(2,1)S(1)}, bf16[240,384]{1,0:T(8,128)(2,1)S(1)}, u32[]{:S(2)}, u32[]{:S(2)}) collective-permute-start(bf16[240,384]{1,0:T(8,128)(2,1)S(1)} %collective-permute-done.46.refs_9_.refs_2_), channel_id=1, source_target_pairs={{1,2},{2,1},{0,0},{3,3},{5,6},{6,5},{4,4},{7,7},{9,10},{10,9},{8,8... | collective-permute-start | bytes 552968 | tf_op jit(solution)/shard_map/ppermute | solution.py:32
  86.7 13.5 %collective-permute-start.20 = (bf16[240,384]{1,0:T(8,128)(2,1)S(1)}, bf16[240,384]{1,0:T(8,128)(2,1)S(1)}, u32[]{:S(2)}, u32[]{:S(2)}) collective-permute-start(bf16[240,384]{1,0:T(8,128)(2,1)S(1)} %shard_map.123), channel_id=1, source_target_pairs={{1,2},{2,1},{0,0},{3,3},{5,6},{6,5},{4,4},{7,7},{9,10},{10,9},{8,8... | collective-permute-start | bytes 552968 | tf_op jit(solution)/shard_map/ppermute | solution.py:32
  89.5 21.4 %collective-permute-start.25 = (bf16[240,384]{1,0:T(8,128)(2,1)S(1)}, bf16[240,384]{1,0:T(8,128)(2,1)S(1)}, u32[]{:S(2)}, u32[]{:S(2)}) collective-permute-start(bf16[240,384]{1,0:T(8,128)(2,1)S(1)} %fusion.10), channel_id=1, source_target_pairs={{1,2},{2,1},{0,0},{3,3},{5,6},{6,5},{4,4},{7,7},{9,10},{10,9},{8,8... | collective-permute-start | bytes 552968 | tf_op jit(solution)/shard_map/ppermute | solution.py:32
  91.7 12.5 %collective-permute-start.53 = (bf16[240,384]{1,0:T(8,128)(2,1)S(1)}, bf16[240,384]{1,0:T(8,128)(2,1)S(1)}, u32[]{:S(2)}, u32[]{:S(2)}) collective-permute-start(bf16[240,384]{1,0:T(8,128)(2,1)S(1)} %fusion.14), channel_id=1, source_target_pairs={{1,2},{2,1},{0,0},{3,3},{5,6},{6,5},{4,4},{7,7},{9,10},{10,9},{8,8... | collective-permute-start | bytes 552968 | tf_op jit(solution)/shard_map/ppermute | solution.py:32
  92.4 13.3 %collective-permute-start.52 = (bf16[240,384]{1,0:T(8,128)(2,1)S(1)}, bf16[240,384]{1,0:T(8,128)(2,1)S(1)}, u32[]{:S(2)}, u32[]{:S(2)}) collective-permute-start(bf16[240,384]{1,0:T(8,128)(2,1)S(1)} %fusion.6), channel_id=1, source_target_pairs={{0,1},{1,0},{2,3},{3,2},{4,5},{5,4},{6,7},{7,6},{8,9},{9,8},{10,11... | collective-permute-start | bytes 552968 | tf_op jit(solution)/shard_map/ppermute | solution.py:32
  100.3 10.7 %collective-permute-start.21 = (bf16[240,384]{1,0:T(8,128)(2,1)S(1)}, bf16[240,384]{1,0:T(8,128)(2,1)S(1)}, u32[]{:S(2)}, u32[]{:S(2)}) collective-permute-start(bf16[240,384]{1,0:T(8,128)(2,1)S(1)} %fusion.2), channel_id=1, source_target_pairs={{0,1},{1,0},{2,3},{3,2},{4,5},{5,4},{6,7},{7,6},{8,9},{9,8},{10,11... | collective-permute-start | bytes 552968 | tf_op jit(solution)/shard_map/ppermute | solution.py:32
  105.9 9.7 %collective-permute-start.55 = (bf16[240,384]{1,0:T(8,128)(2,1)S(1)}, bf16[240,384]{1,0:T(8,128)(2,1)S(1)}, u32[]{:S(2)}, u32[]{:S(2)}) collective-permute-start(bf16[240,384]{1,0:T(8,128)(2,1)S(1)} %get-tuple-element.132.refs_10_.refs_1_), channel_id=1, source_target_pairs={{1,2},{2,1},{0,0},{3,3},{5,6},{6,5},{4,4},{7,7},{9,10},{10,9},{8,8... | collective-permute-start | bytes 552968 | tf_op jit(solution)/shard_map/ppermute | solution.py:32
  106.6 13.3 %collective-permute-start.54 = (bf16[240,384]{1,0:T(8,128)(2,1)S(1)}, bf16[240,384]{1,0:T(8,128)(2,1)S(1)}, u32[]{:S(2)}, u32[]{:S(2)}) collective-permute-start(bf16[240,384]{1,0:T(8,128)(2,1)S(1)} %get-tuple-element.132.refs_10_.refs_1_), channel_id=1, source_target_pairs={{0,1},{1,0},{2,3},{3,2},{4,5},{5,4},{6,7},{7,6},{8,9},{9,8},{10,11... | collective-permute-start | bytes 552968 | tf_op jit(solution)/shard_map/ppermute | solution.py:32
  111.1 11.8 %collective-permute-start.30 = (bf16[240,384]{1,0:T(8,128)(2,1)S(1)}, bf16[240,384]{1,0:T(8,128)(2,1)S(1)}, u32[]{:S(2)}, u32[]{:S(2)}) collective-permute-start(bf16[240,384]{1,0:T(8,128)(2,1)S(1)} %get-tuple-element.106.refs_16_.refs_0_.refs_7_), channel_id=1, source_target_pairs={{0,1},{1,0},{2,3},{3,2},{4,5},{5,4},{6,7},{7,6},{8,9},{9,8},{10,11... | collective-permute-start | bytes 552968 | tf_op jit(solution)/shard_map/ppermute | solution.py:32
  111.2 9.3 %collective-permute-start.26 = (bf16[240,384]{1,0:T(8,128)(2,1)S(1)}, bf16[240,384]{1,0:T(8,128)(2,1)S(1)}, u32[]{:S(2)}, u32[]{:S(2)}) collective-permute-start(bf16[240,384]{1,0:T(8,128)(2,1)S(1)} %get-tuple-element.106.refs_16_.refs_0_.refs_7_), channel_id=1, source_target_pairs={{1,2},{2,1},{0,0},{3,3},{5,6},{6,5},{4,4},{7,7},{9,10},{10,9},{8,8... | collective-permute-start | bytes 552968 | tf_op jit(solution)/shard_map/ppermute | solution.py:32
  115.6 12.1 %collective-permute-start.56 = (bf16[240,384]{1,0:T(8,128)(2,1)S(1)}, bf16[240,384]{1,0:T(8,128)(2,1)S(1)}, u32[]{:S(2)}, u32[]{:S(2)}) collective-permute-start(bf16[240,384]{1,0:T(8,128)(2,1)S(1)} %broadcast_select_fusion.3), channel_id=1, source_target_pairs={{0,1},{1,0},{2,3},{3,2},{4,5},{5,4},{6,7},{7,6},{8,9},{9,8},{10,11... | collective-permute-start | bytes 552968 | tf_op jit(solution)/shard_map/ppermute | solution.py:32
  119.9 8.5 %collective-permute-start.57 = (bf16[240,384]{1,0:T(8,128)(2,1)S(1)}, bf16[240,384]{1,0:T(8,128)(2,1)S(1)}, u32[]{:S(2)}, u32[]{:S(2)}) collective-permute-start(bf16[240,384]{1,0:T(8,128)(2,1)S(1)} %collective-permute-done.54.refs_11_.refs_2_), channel_id=1, source_target_pairs={{1,2},{2,1},{0,0},{3,3},{5,6},{6,5},{4,4},{7,7},{9,10},{10,9},{8,8... | collective-permute-start | bytes 552968 | tf_op jit(solution)/shard_map/ppermute | solution.py:32
  120.6 12.6 %collective-permute-start.27 = (bf16[240,384]{1,0:T(8,128)(2,1)S(1)}, bf16[240,384]{1,0:T(8,128)(2,1)S(1)}, u32[]{:S(2)}, u32[]{:S(2)}) collective-permute-start(bf16[240,384]{1,0:T(8,128)(2,1)S(1)} %broadcast_select_fusion.9), channel_id=1, source_target_pairs={{0,1},{1,0},{2,3},{3,2},{4,5},{5,4},{6,7},{7,6},{8,9},{9,8},{10,11... | collective-permute-start | bytes 552968 | tf_op jit(solution)/shard_map/ppermute | solution.py:32
  122.9 10.1 %collective-permute-start.31 = (bf16[240,384]{1,0:T(8,128)(2,1)S(1)}, bf16[240,384]{1,0:T(8,128)(2,1)S(1)}, u32[]{:S(2)}, u32[]{:S(2)}) collective-permute-start(bf16[240,384]{1,0:T(8,128)(2,1)S(1)} %collective-permute-done.30.refs_17_.refs_8_), channel_id=1, source_target_pairs={{1,2},{2,1},{0,0},{3,3},{5,6},{6,5},{4,4},{7,7},{9,10},{10,9},{8,8... | collective-permute-start | bytes 552968 | tf_op jit(solution)/shard_map/ppermute | solution.py:32
  128.4 10.2 %collective-permute-start.58 = (bf16[240,384]{1,0:T(8,128)(2,1)S(1)}, bf16[240,384]{1,0:T(8,128)(2,1)S(1)}, u32[]{:S(2)}, u32[]{:S(2)}) collective-permute-start(bf16[240,384]{1,0:T(8,128)(2,1)S(1)} %broadcast_select_fusion.2), channel_id=1, source_target_pairs={{0,1},{1,0},{2,3},{3,2},{4,5},{5,4},{6,7},{7,6},{8,9},{9,8},{10,11... | collective-permute-start | bytes 552968 | tf_op jit(solution)/shard_map/ppermute | solution.py:32
  133.2 7.1 %collective-permute-start.28 = (bf16[240,384]{1,0:T(8,128)(2,1)S(1)}, bf16[240,384]{1,0:T(8,128)(2,1)S(1)}, u32[]{:S(2)}, u32[]{:S(2)}) collective-permute-start(bf16[240,384]{1,0:T(8,128)(2,1)S(1)} %shard_map.126), channel_id=1, source_target_pairs={{1,2},{2,1},{0,0},{3,3},{5,6},{6,5},{4,4},{7,7},{9,10},{10,9},{8,8... | collective-permute-start | bytes 552968 | tf_op jit(solution)/shard_map/ppermute | solution.py:32
  134.0 15.3 %collective-permute-start.60 = (bf16[240,384]{1,0:T(8,128)(2,1)S(1)}, bf16[240,384]{1,0:T(8,128)(2,1)S(1)}, u32[]{:S(2)}, u32[]{:S(2)}) collective-permute-start(bf16[240,384]{1,0:T(8,128)(2,1)S(1)} %fusion.7), channel_id=1, source_target_pairs={{0,1},{1,0},{2,3},{3,2},{4,5},{5,4},{6,7},{7,6},{8,9},{9,8},{10,11... | collective-permute-start | bytes 552968 | tf_op jit(solution)/shard_map/ppermute | solution.py:32
  138.7 10.5 %collective-permute-start.61 = (bf16[240,384]{1,0:T(8,128)(2,1)S(1)}, bf16[240,384]{1,0:T(8,128)(2,1)S(1)}, u32[]{:S(2)}, u32[]{:S(2)}) collective-permute-start(bf16[240,384]{1,0:T(8,128)(2,1)S(1)} %fusion.15), channel_id=1, source_target_pairs={{1,2},{2,1},{0,0},{3,3},{5,6},{6,5},{4,4},{7,7},{9,10},{10,9},{8,8... | collective-permute-start | bytes 552968 | tf_op jit(solution)/shard_map/ppermute | solution.py:32
  139.7 12.9 %collective-permute-start.33 = (bf16[240,384]{1,0:T(8,128)(2,1)S(1)}, bf16[240,384]{1,0:T(8,128)(2,1)S(1)}, u32[]{:S(2)}, u32[]{:S(2)}) collective-permute-start(bf16[240,384]{1,0:T(8,128)(2,1)S(1)} %fusion.11), channel_id=1, source_target_pairs={{1,2},{2,1},{0,0},{3,3},{5,6},{6,5},{4,4},{7,7},{9,10},{10,9},{8,8... | collective-permute-start | bytes 552968 | tf_op jit(solution)/shard_map/ppermute | solution.py:32
  140.4 12.1 %collective-permute-start.29 = (bf16[240,384]{1,0:T(8,128)(2,1)S(1)}, bf16[240,384]{1,0:T(8,128)(2,1)S(1)}, u32[]{:S(2)}, u32[]{:S(2)}) collective-permute-start(bf16[240,384]{1,0:T(8,128)(2,1)S(1)} %fusion.3), channel_id=1, source_target_pairs={{0,1},{1,0},{2,3},{3,2},{4,5},{5,4},{6,7},{7,6},{8,9},{9,8},{10,11... | collective-permute-start | bytes 552968 | tf_op jit(solution)/shard_map/ppermute | solution.py:32
  149.4 7.5 %collective-permute-start.63 = (bf16[240,384]{1,0:T(8,128)(2,1)S(1)}, bf16[240,384]{1,0:T(8,128)(2,1)S(1)}, u32[]{:S(2)}, u32[]{:S(2)}) collective-permute-start(bf16[240,384]{1,0:T(8,128)(2,1)S(1)} %get-tuple-element.145.refs_10_.refs_1_), channel_id=1, source_target_pairs={{1,2},{2,1},{0,0},{3,3},{5,6},{6,5},{4,4},{7,7},{9,10},{10,9},{8,8... | collective-permute-start | bytes 552968 | tf_op jit(solution)/shard_map/ppermute | solution.py:32
  150.1 11.1 %collective-permute-start.62 = (bf16[240,384]{1,0:T(8,128)(2,1)S(1)}, bf16[240,384]{1,0:T(8,128)(2,1)S(1)}, u32[]{:S(2)}, u32[]{:S(2)}) collective-permute-start(bf16[240,384]{1,0:T(8,128)(2,1)S(1)} %get-tuple-element.145.refs_10_.refs_1_), channel_id=1, source_target_pairs={{0,1},{1,0},{2,3},{3,2},{4,5},{5,4},{6,7},{7,6},{8,9},{9,8},{10,11... | collective-permute-start | bytes 552968 | tf_op jit(solution)/shard_map/ppermute | solution.py:32
  152.7 11.6 %collective-permute-start.38 = (bf16[240,384]{1,0:T(8,128)(2,1)S(1)}, bf16[240,384]{1,0:T(8,128)(2,1)S(1)}, u32[]{:S(2)}, u32[]{:S(2)}) collective-permute-start(bf16[240,384]{1,0:T(8,128)(2,1)S(1)} %get-tuple-element.115.refs_16_.refs_0_.refs_7_), channel_id=1, source_target_pairs={{0,1},{1,0},{2,3},{3,2},{4,5},{5,4},{6,7},{7,6},{8,9},{9,8},{10,11... | collective-permute-start | bytes 552968 | tf_op jit(solution)/shard_map/ppermute | solution.py:32
  152.8 9.0 %collective-permute-start.34 = (bf16[240,384]{1,0:T(8,128)(2,1)S(1)}, bf16[240,384]{1,0:T(8,128)(2,1)S(1)}, u32[]{:S(2)}, u32[]{:S(2)}) collective-permute-start(bf16[240,384]{1,0:T(8,128)(2,1)S(1)} %get-tuple-element.115.refs_16_.refs_0_.refs_7_), channel_id=1, source_target_pairs={{1,2},{2,1},{0,0},{3,3},{5,6},{6,5},{4,4},{7,7},{9,10},{10,9},{8,8... | collective-permute-start | bytes 552968 | tf_op jit(solution)/shard_map/ppermute | solution.py:32
  156.9 13.7 %collective-permute-start.64 = (bf16[240,384]{1,0:T(8,128)(2,1)S(1)}, bf16[240,384]{1,0:T(8,128)(2,1)S(1)}, u32[]{:S(2)}, u32[]{:S(2)}) collective-permute-start(bf16[240,384]{1,0:T(8,128)(2,1)S(1)} %broadcast_select_fusion.1), channel_id=1, source_target_pairs={{0,1},{1,0},{2,3},{3,2},{4,5},{5,4},{6,7},{7,6},{8,9},{9,8},{10,11... | collective-permute-start | bytes 552968 | tf_op jit(solution)/shard_map/ppermute | solution.py:32
  161.9 12.0 %collective-permute-start.35 = (bf16[240,384]{1,0:T(8,128)(2,1)S(1)}, bf16[240,384]{1,0:T(8,128)(2,1)S(1)}, u32[]{:S(2)}, u32[]{:S(2)}) collective-permute-start(bf16[240,384]{1,0:T(8,128)(2,1)S(1)} %broadcast_select_fusion.7), channel_id=1, source_target_pairs={{0,1},{1,0},{2,3},{3,2},{4,5},{5,4},{6,7},{7,6},{8,9},{9,8},{10,11... | collective-permute-start | bytes 552968 | tf_op jit(solution)/shard_map/ppermute | solution.py:32
  165.0 9.6 %collective-permute-start.66 = (bf16[240,384]{1,0:T(8,128)(2,1)S(1)}, bf16[240,384]{1,0:T(8,128)(2,1)S(1)}, u32[]{:S(2)}, u32[]{:S(2)}) collective-permute-start(bf16[240,384]{1,0:T(8,128)(2,1)S(1)} %broadcast_select_fusion), channel_id=1, source_target_pairs={{0,1},{1,0},{2,3},{3,2},{4,5},{5,4},{6,7},{7,6},{8,9},{9,8},{10,11... | collective-permute-start | bytes 552968 | tf_op jit(solution)/shard_map/ppermute | solution.py:32
  171.4 8.6 %collective-permute-start.40 = (bf16[240,384]{1,0:T(8,128)(2,1)S(1)}, bf16[240,384]{1,0:T(8,128)(2,1)S(1)}, u32[]{:S(2)}, u32[]{:S(2)}) collective-permute-start(bf16[240,384]{1,0:T(8,128)(2,1)S(1)} %broadcast_select_fusion.6), channel_id=1, source_target_pairs={{0,1},{1,0},{2,3},{3,2},{4,5},{5,4},{6,7},{7,6},{8,9},{9,8},{10,11... | collective-permute-start | bytes 552968 | tf_op jit(solution)/shard_map/ppermute | solution.py:32
  174.7 13.7 %collective-permute-start.69 = (bf16[240,384]{1,0:T(8,128)(2,1)S(1)}, bf16[240,384]{1,0:T(8,128)(2,1)S(1)}, u32[]{:S(2)}, u32[]{:S(2)}) collective-permute-start(bf16[240,384]{1,0:T(8,128)(2,1)S(1)} %fusion.16), channel_id=1, source_target_pairs={{1,2},{2,1},{0,0},{3,3},{5,6},{6,5},{4,4},{7,7},{9,10},{10,9},{8,8... | collective-permute-start | bytes 552968 | tf_op jit(solution)/shard_map/ppermute | solution.py:32
  175.4 12.9 %collective-permute-start.68 = (bf16[240,384]{1,0:T(8,128)(2,1)S(1)}, bf16[240,384]{1,0:T(8,128)(2,1)S(1)}, u32[]{:S(2)}, u32[]{:S(2)}) collective-permute-start(bf16[240,384]{1,0:T(8,128)(2,1)S(1)} %fusion.8), channel_id=1, source_target_pairs={{0,1},{1,0},{2,3},{3,2},{4,5},{5,4},{6,7},{7,6},{8,9},{9,8},{10,11... | collective-permute-start | bytes 552968 | tf_op jit(solution)/shard_map/ppermute | solution.py:32
  180.1 8.5 %collective-permute-start.41 = (bf16[240,384]{1,0:T(8,128)(2,1)S(1)}, bf16[240,384]{1,0:T(8,128)(2,1)S(1)}, u32[]{:S(2)}, u32[]{:S(2)}) collective-permute-start(bf16[240,384]{1,0:T(8,128)(2,1)S(1)} %fusion.12), channel_id=1, source_target_pairs={{1,2},{2,1},{0,0},{3,3},{5,6},{6,5},{4,4},{7,7},{9,10},{10,9},{8,8... | collective-permute-start | bytes 552968 | tf_op jit(solution)/shard_map/ppermute | solution.py:32
  180.8 7.7 %collective-permute-start.37 = (bf16[240,384]{1,0:T(8,128)(2,1)S(1)}, bf16[240,384]{1,0:T(8,128)(2,1)S(1)}, u32[]{:S(2)}, u32[]{:S(2)}) collective-permute-start(bf16[240,384]{1,0:T(8,128)(2,1)S(1)} %fusion.4), channel_id=1, source_target_pairs={{0,1},{1,0},{2,3},{3,2},{4,5},{5,4},{6,7},{7,6},{8,9},{9,8},{10,11... | collective-permute-start | bytes 552968 | tf_op jit(solution)/shard_map/ppermute | solution.py:32
  189.4 8.1 %collective-permute-start.75 = (bf16[256,384]{1,0:T(8,128)(2,1)S(1)}, bf16[256,384]{1,0:T(8,128)(2,1)S(1)}, u32[]{:S(2)}, u32[]{:S(2)}) collective-permute-start(bf16[256,384]{1,0:T(8,128)(2,1)S(1)} %get-tuple-element.158.refs_0_.refs_17_.refs_7_), channel_id=1, source_target_pairs={{0,1},{1,0},{2,3},{3,2},{4,5},{5,4},{6,7},{7,6},{8,9},{9,8},{10,11... | collective-permute-start | bytes 589832 | tf_op jit(solution)/shard_map/ppermute | solution.py:32
  191.7 9.8 %collective-permute-start.70 = (bf16[240,384]{1,0:T(8,128)(2,1)S(1)}, bf16[240,384]{1,0:T(8,128)(2,1)S(1)}, u32[]{:S(2)}, u32[]{:S(2)}) collective-permute-start(bf16[240,384]{1,0:T(8,128)(2,1)S(1)} %get-tuple-element.165.refs_11_.refs_1_), channel_id=1, source_target_pairs={{0,1},{1,0},{2,3},{3,2},{4,5},{5,4},{6,7},{7,6},{8,9},{9,8},{10,11... | collective-permute-start | bytes 552968 | tf_op jit(solution)/shard_map/ppermute | solution.py:32
  191.7 10.6 %collective-permute-start.76 = (bf16[256,384]{1,0:T(8,128)(2,1)S(1)}, bf16[256,384]{1,0:T(8,128)(2,1)S(1)}, u32[]{:S(2)}, u32[]{:S(2)}) collective-permute-start(bf16[256,384]{1,0:T(8,128)(2,1)S(1)} %get-tuple-element.158.refs_0_.refs_17_.refs_7_), channel_id=1, source_target_pairs={{1,2},{2,1},{0,0},{3,3},{5,6},{6,5},{4,4},{7,7},{9,10},{10,9},{8,8... | collective-permute-start | bytes 589832 | tf_op jit(solution)/shard_map/ppermute | solution.py:32
  197.5 11.2 %collective-permute-start.78 = (bf16[256,384]{1,0:T(8,128)(2,1)S(1)}, bf16[256,384]{1,0:T(8,128)(2,1)S(1)}, u32[]{:S(2)}, u32[]{:S(2)}) collective-permute-start(bf16[256,384]{1,0:T(8,128)(2,1)S(1)} %collective-permute-done.75.refs_18_.refs_8_), channel_id=1, source_target_pairs={{1,2},{2,1},{0,0},{3,3},{5,6},{6,5},{4,4},{7,7},{9,10},{10,9},{8,8... | collective-permute-start | bytes 589832 | tf_op jit(solution)/shard_map/ppermute | solution.py:32
  198.2 10.7 %collective-permute-start.71 = (bf16[240,384]{1,0:T(8,128)(2,1)S(1)}, bf16[240,384]{1,0:T(8,128)(2,1)S(1)}, u32[]{:S(2)}, u32[]{:S(2)}) collective-permute-start(bf16[240,384]{1,0:T(8,128)(2,1)S(1)} %get-tuple-element.165.refs_11_.refs_1_), channel_id=1, source_target_pairs={{1,2},{2,1},{0,0},{3,3},{5,6},{6,5},{4,4},{7,7},{9,10},{10,9},{8,8... | collective-permute-start | bytes 552968 | tf_op jit(solution)/shard_map/ppermute | solution.py:32
  201.5 9.3 %collective-permute-start.73 = (bf16[240,384]{1,0:T(8,128)(2,1)S(1)}, bf16[240,384]{1,0:T(8,128)(2,1)S(1)}, u32[]{:S(2)}, u32[]{:S(2)}) collective-permute-start(bf16[240,384]{1,0:T(8,128)(2,1)S(1)} %collective-permute-done.70.refs_12_.refs_2_), channel_id=1, source_target_pairs={{1,2},{2,1},{0,0},{3,3},{5,6},{6,5},{4,4},{7,7},{9,10},{10,9},{8,8... | collective-permute-start | bytes 552968 | tf_op jit(solution)/shard_map/ppermute | solution.py:32
  202.4 14.1 %collective-permute-start.77 = (bf16[256,384]{1,0:T(8,128)(2,1)S(1)}, bf16[256,384]{1,0:T(8,128)(2,1)S(1)}, u32[]{:S(2)}, u32[]{:S(2)}) collective-permute-start(bf16[256,384]{1,0:T(8,128)(2,1)S(1)} %collective-permute-done.76.refs_20_.refs_10_), channel_id=1, source_target_pairs={{0,1},{1,0},{2,3},{3,2},{4,5},{5,4},{6,7},{7,6},{8,9},{9,8},{10,11... | collective-permute-start | bytes 589832 | tf_op jit(solution)/shard_map/ppermute | solution.py:32
  208.7 9.7 %collective-permute-start.79 = (bf16[256,384]{1,0:T(8,128)(2,1)S(1)}, bf16[256,384]{1,0:T(8,128)(2,1)S(1)}, u32[]{:S(2)}, u32[]{:S(2)}) collective-permute-start(bf16[256,384]{1,0:T(8,128)(2,1)S(1)} %collective-permute-done.78.refs_22_.refs_12_), channel_id=1, source_target_pairs={{0,1},{1,0},{2,3},{3,2},{4,5},{5,4},{6,7},{7,6},{8,9},{9,8},{10,11... | collective-permute-start | bytes 589832 | tf_op jit(solution)/shard_map/ppermute | solution.py:32
  208.8 7.6 %collective-permute-start.72 = (bf16[240,384]{1,0:T(8,128)(2,1)S(1)}, bf16[240,384]{1,0:T(8,128)(2,1)S(1)}, u32[]{:S(2)}, u32[]{:S(2)}) collective-permute-start(bf16[240,384]{1,0:T(8,128)(2,1)S(1)} %collective-permute-done.71.refs_14_.refs_4_), channel_id=1, source_target_pairs={{0,1},{1,0},{2,3},{3,2},{4,5},{5,4},{6,7},{7,6},{8,9},{9,8},{10,11... | collective-permute-start | bytes 552968 | tf_op jit(solution)/shard_map/ppermute | solution.py:32
  210.8 7.7 %collective-permute-start.74 = (bf16[240,384]{1,0:T(8,128)(2,1)S(1)}, bf16[240,384]{1,0:T(8,128)(2,1)S(1)}, u32[]{:S(2)}, u32[]{:S(2)}) collective-permute-start(bf16[240,384]{1,0:T(8,128)(2,1)S(1)} %collective-permute-done.73.refs_16_.refs_6_), channel_id=1, source_target_pairs={{0,1},{1,0},{2,3},{3,2},{4,5},{5,4},{6,7},{7,6},{8,9},{9,8},{10,11... | collective-permute-start | bytes 552968 | tf_op jit(solution)/shard_map/ppermute | solution.py:32
  227.8 7.3 %collective-permute-start.81 = (bf16[2,128,512]{2,1,0:T(8,128)(2,1)S(1)}, bf16[2,128,512]{2,1,0:T(8,128)(2,1)S(1)}, u32[]{:S(2)}, u32[]{:S(2)}) collective-permute-start(bf16[2,128,512]{2,1,0:T(8,128)(2,1)S(1)} %slice_bitcast_fusion), channel_id=1, source_target_pairs={{0,8},{4,12},{8,0},{12,4},{1,9},{5,13},{9,1},{13,5},{2,10},{6,14},... | collective-permute-start | bytes 786440 | tf_op jit(solution)/shard_map/ppermute | solution.py:32
  (22 other events, 108.2 us)

commit v6 on v5

--- a/solution.py
+++ b/solution.py
@@ -65,14 +65,14 @@
     return lax.dot_general(a, b, (dims, ((), ())), preferred_element_type=F32)
 
 
-def routing(scal, names, scales, expert, rows):
-    n = len(names)
-    tokens = names[0].shape[1]
-    which = scal[2 * n] + expert
-    hits = [ids[...] == which for ids in names]
+def routing(scal, routes, expert, rows):
+    n = len(routes)
+    choose, tokens = routes[0].shape[0] // 2, routes[0].shape[1]
+    which = (scal[2 * n] + expert).astype(F32)
+    hits = [route[0:choose, :] == which for route in routes]
     weights = [
-        jnp.sum(jnp.where(hit, scale[...], 0.0), axis=0, keepdims=True)
-        for hit, scale in zip(hits, scales)
+        jnp.sum(jnp.where(hit, route[choose:, :], 0.0), axis=0, keepdims=True)
+        for hit, route in zip(hits, routes)
     ]
     chosen = jnp.concatenate(
         [jnp.sum(jnp.where(hit, 1.0, 0.0), axis=0, keepdims=True) for hit in hits], axis=0
@@ -109,7 +109,7 @@
 
 def pre_kernel(n, expert, deps, scal, *refs):
     refs = refs[deps:]
-    names, scales, toks, ogs, refs = *(refs[k * n : (k + 1) * n] for k in range(4)), refs[4 * n :]
+    routes, packs, refs = refs[:n], refs[n : 2 * n], refs[2 * n :]
     weights, (in_ref, cot_ref, *refs) = refs[:3], refs[3:]
     outs, (token, gw, uw, dw, sems) = refs[: 2 * n], refs[2 * n :]
     rows, tile = in_ref.shape[0] // n, gw.shape[1] // 2
@@ -118,12 +118,12 @@
         for copy in group:
             copy.start()
     token[...] = jnp.zeros_like(token)
-    for k, (position, weight, hit) in enumerate(routing(scal, names, scales, expert, rows)):
+    for k, (position, weight, hit) in enumerate(routing(scal, routes, expert, rows)):
         pick = hit.astype(F32).astype(BF16)
         span = span_of(position, rows)
-        in_ref[span, :] = dot(pick, toks[k][...]).astype(BF16)
+        in_ref[span, :] = dot(pick, packs[k][0]).astype(BF16)
         scale = jnp.sum(jnp.where(hit, weight, 0.0), axis=1, keepdims=True)
-        cot_ref[span, :] = (dot(pick, ogs[k][...]) * scale).astype(BF16)
+        cot_ref[span, :] = (dot(pick, packs[k][1]) * scale).astype(BF16)
     for h in range(2):
         for copy in copies[h]:
             copy.wait()
@@ -175,9 +175,16 @@
         out[3 * rows :, 0:lanes] = jnp.concatenate(lines, axis=0).astype(BF16)
 
 
+def pack_kernel(ids, combine, tokens, grads, pack, route):
+    pack[0] = tokens[...]
+    pack[1] = grads[...]
+    route[0 : ids.shape[0], :] = ids[...].astype(F32)
+    route[ids.shape[0] :, :] = combine[...]
+
+
 def add_kernel(deps, *refs):
     a, b, out = refs[deps:]
-    out[...] = (a[...].astype(F32) + b[...].astype(F32)).astype(BF16)
+    out[...] = (a[...].astype(F32) + b[...].astype(F32)).astype(out.dtype)
 
 
 def part_of(scal, n, q, group, start, size):
@@ -208,7 +215,7 @@
 
 def out_kernel(n, expert, has_prev, last, sizes, deps, scal, *refs):
     refs = refs[deps:]
-    names, scales, refs = refs[:n], refs[n : 2 * n], refs[2 * n :]
+    routes, refs = refs[:n], refs[n:]
     if has_prev:
         prev, refs = refs[:2], refs[2:]
     halves, refs = split_pieces(refs, sizes)
@@ -221,9 +228,9 @@
         for copy in group:
             copy.start()
     token[...] = jnp.zeros_like(token)
-    routes = routing(scal, names, scales, expert, halves[0][0][0].shape[0] // 48 * 16)
+    spots = routing(scal, routes, expert, halves[0][0][0].shape[0] // 48 * 16)
     if last:
-        send_products(scal, names, scales, expert + 1, halves[1], held, near_p, far_p)
+        send_products(scal, routes, expert + 1, halves[1], held, near_p, far_p)
     tile = gw.shape[1] // 2
     eo, idl = 0.0, 0.0
     for h in range(2):
@@ -235,7 +242,7 @@
         idl = idl + dot(load_rows(scal, n, 2, halves[h]), uw[:, part], ((1,), (1,)))
     rows = eo.shape[0] // n
     eo_ref[...], idl_ref[...] = eo.astype(BF16), idl.astype(BF16)
-    for k, (position, weight, hit) in enumerate(routes):
+    for k, (position, weight, hit) in enumerate(spots):
         pick = hit.astype(F32)
         scaled = (pick * weight).astype(BF16)
         span = span_of(position, rows)
@@ -266,8 +273,8 @@
             dg[0] = dot(load_rows(scal, n, 0, halves[h]), cot_ref[...], ((0,), (0,))).astype(BF16)
 
 
-def send_products(scal, names, scales, local, pieces, held, near, far):
-    n, (_, extra, lanes) = len(names), held.shape
+def send_products(scal, routes, local, pieces, held, near, far):
+    n, (_, extra, lanes) = len(routes), held.shape
     first = pieces[0][0].shape[0] - extra
     for q, group in enumerate(pieces):
         held[q] = part_of(scal, n, q, group, first, extra)[:, 0:lanes]
@@ -275,7 +282,7 @@
     ids = lax.broadcasted_iota(jnp.int32, (experts_all, tokens), 0)
     sums = [jnp.zeros((experts_all, tokens), F32) for _ in range(n)]
     for e in range(local):
-        for k, (position, _, hit) in enumerate(routing(scal, names, scales, e, lanes)):
+        for k, (position, _, hit) in enumerate(routing(scal, routes, e, lanes)):
             found = dot(held[position], hit.astype(F32).astype(BF16))
             value = found[3 * e : 3 * e + 1] + found[3 * e + 1 : 3 * e + 2] + found[3 * e + 2 : 3 * e + 3]
             sums[k] = sums[k] + jnp.where(ids == scal[2 * n] + e, value, 0.0)
@@ -367,11 +374,17 @@
         ]
         return found + [across.send(piece, swap) for piece in found]
 
-    routes = gather_blocks(ids_t) + gather_blocks(combine_t)
-    blocks = gather_blocks(tokens) + gather_blocks(out_grad)
-    for held in (routes, blocks):
-        held[0], held[n] = in_hbm(held[0]), in_hbm(held[n])
-    route_specs, block_specs = [spec_of(x) for x in routes], [spec_of(x) for x in blocks]
+    pack, route = call(
+        pack_kernel,
+        1,
+        [spec_of(ids_t), spec_of(combine_t), spec_of(tokens), spec_of(out_grad)],
+        [whole_spec((2, count, width)), whole_spec((2 * choose, count))],
+        [like((2, count, width)), like((2 * choose, count), F32)],
+        count * width,
+        8 * count * width,
+    )(*(in_hbm(x) for x in (ids_t, combine_t, tokens, out_grad)))
+    routes, packs = gather_blocks(route), gather_blocks(pack)
+    route_specs, pack_specs = [spec_of(x) for x in routes], [spec_of(x) for x in packs]
 
     mac = all_rows * width * hidden
     weight_bytes = 2 * width * hidden
@@ -394,13 +407,13 @@
         inputs, cot, *parts, token = call(
             functools.partial(pre_kernel, n, e, len(deps)),
             1,
-            [SMEM_SPEC] + [ANY_SPEC] * len(deps) + route_specs + block_specs + [HBM_SPEC] * 3,
+            [SMEM_SPEC] + [ANY_SPEC] * len(deps) + route_specs + pack_specs + [HBM_SPEC] * 3,
             [whole_spec(slot_shape)] * 2 + [whole_spec(piece_shape)] * (2 * n) + [whole_spec(TOKEN)],
             [like(slot_shape)] * 2 + [like(piece_shape)] * (2 * n) + [like(TOKEN, F32)],
             6 * mac,
             3 * weight_bytes + 2 * n * piece_bytes,
             scratch_shapes=held_weights,
-        )(scal, *deps, *routes, *blocks, *weights)
+        )(scal, *deps, *routes, *packs, *weights)
         return (inputs, cot), [parts[:n], parts[n:]], token
 
     def mid(e, h, totals, products, deps=()):
@@ -422,11 +435,11 @@
         return call(
             functools.partial(add_kernel, len(deps)),
             1,
-            [ANY_SPEC] * len(deps) + [whole_spec(piece_shape)] * 2,
-            whole_spec(piece_shape),
-            like(piece_shape),
-            3 * rows * tile,
-            3 * piece_bytes,
+            [ANY_SPEC] * len(deps) + [spec_of(a)] * 2,
+            spec_of(a),
+            like(a.shape, a.dtype),
+            a.size,
+            3 * a.size * a.dtype.itemsize,
         )(*deps, a, b)
 
     def flatten(halves):
@@ -486,7 +499,11 @@
         return along_z.send(value, [(0, 1), (1, 0), (2, 3), (3, 2)])
 
     def inner(value):
-        return along_z.send(value, [(1, 2), (2, 1), (0, 0), (3, 3)])
+        pairs = []
+        for p in range(peers):
+            pairs += [(p * n + 1, p * n + 2), (p * n + 2, p * n + 1)]
+            pairs += [(p * n + end, (p ^ 1) * n + end) for end in (0, n - 1)]
+        return lax.ppermute(value, ("expert", "dp"), pairs)
 
     def unless_end(value):
         return jnp.where(at_end, jnp.zeros_like(value), value)
@@ -567,7 +584,7 @@
 
     near, far, _, near_p, far_p = out(local - 1, halves, sums, wait)
     hop, home = send_home(near, far, add_rounded)
-    _, per_expert = send_home(near_p, far_p, lambda a, b: a + b)
+    _, per_expert = send_home(near_p, far_p, lambda a, b: add(a, b, [hop]))
     *grads, _ = grad(local - 1, arrived, halves, grads, [hop])
     combine_grad = jnp.sum(jnp.where(named, per_expert[None], 0.0), axis=1) / combine_t
     return (home[0].astype(BF16), home[1].astype(BF16), *grads, combine_grad.T)

time: 237 us -> 205 us (0.86)
  starting transfers between devices: 137 us -> 92.5 us
  waiting for transfers between devices: 46.3 us -> 62.1 us
    ppermute x84 -> x46, starting transfers between devices: 137 us -> 89.6 us  [send(): return lax.ppermute(value, self.axis, wide)]
    ppermute x84 -> x46, waiting for transfers between devices: 46.3 us -> 62 us  [send(): return lax.ppermute(value, self.axis, wide)]
    ppermute x0 -> x32, starting transfers between devices: none -> 2.98 us  [inner(): return lax.ppermute(value, ('expert', 'dp'), pairs)]
  transfers between devices with their start and end apart: 84 -> 78, of which waited for: 23 -> 23; matrix products, arithmetic and copies ran while one was open for 1% -> 1% of each run, Pallas kernels for 16% -> 18%
where the time goes in v6:
time: 205 us
  starting transfers between devices  92.5 us (45%)
  waiting for transfers between devices  62.1 us (30%)
  Pallas kernels  46.2 us (23%)
  other arithmetic  2.13 us (1%)
    ppermute x46, starting transfers between devices, send(): return lax.ppermute(value, self.axis, wide)  89.6 us
    ppermute x46, waiting for transfers between devices, send(): return lax.ppermute(value, self.axis, wide)  62 us
    pallas_call x4, Pallas kernels, out(): call(functools.partial(out_kernel, n, e, e > 0, last, sizes_of(halves[0])...  14.7 us
    pallas_call x4, Pallas kernels, pre(): call(functools.partial(pre_kernel, n, e, len(deps)), 1, [SMEM_SPEC] + [AN...  14.6 us
    pallas_call x4, Pallas kernels, grad(): call(functools.partial(grad_kernel, n, e > 0, sizes_of(halves[0]), len(de...  13.6 us
  transfers between devices with their start and end apart: 78, of which 23 were waited for; matrix products, arithmetic and copies ran while one was open for 1% of the time, Pallas kernels for 18%

profile of v6, /device:TPU:0, one launch (start us, length us, event | category | flops | bytes accessed | tf_op | source)
XLA Modules:
  0.0 205.0 jit_solution(2055971319113011979)
XLA Ops:
  1.7 3.0 %collective-permute-start.3 = (bf16[2,128,512]{2,1,0:T(8,128)(2,1)S(1)}, bf16[2,128,512]{2,1,0:T(8,128)(2,1)S(1)}, u32[]{:S(2)}, u32[]{:S(2)}) collective-permute-start(bf16[2,128,512]{2,1,0:T(8,128)(2,1)S(1)} %get-tuple-element.95.refs_4_.refs_5_), channel_id=1, source_target_pairs={{0,8},{4,12},{8,0},{12,4},{1,9},{5,13},{9,1},{13,5},{2,10},{6,14},... | collective-permute-start | bytes 786440 | tf_op jit(solution)/shard_map/ppermute | solution.py:32
  4.7 6.3 %collective-permute-done.3.refs_5_.refs_6_ = bf16[2,128,512]{2,1,0:T(8,128)(2,1)S(1)} collective-permute-done((bf16[2,128,512]{2,1,0:T(8,128)(2,1)S(1)}, bf16[2,128,512]{2,1,0:T(8,128)(2,1)S(1)}, u32[]{:S(2)}, u32[]{:S(2)}) %collective-permute-start.3) | collective-permute-done | bytes 262176 | tf_op jit(solution)/shard_map/ppermute | solution.py:32
  11.0 1.7 collective-permute-start
  12.9 1.7 collective-permute-done.refs_1_.refs_2_
  14.7 1.1 collective-permute-done.2.refs_3_.refs_4_
  15.8 3.9 %shard_map.119 = (bf16[320,512]{1,0:T(8,128)(2,1)S(1)}, bf16[320,512]{1,0:T(8,128)(2,1)S(1)}, bf16[240,384]{1,0:T(8,128)(2,1)S(1)}, bf16[240,384]{1,0:T(8,128)(2...) custom-call(s32[10]{0:T(128)S(1)} %stack.35.scal, ...), custom_call_target="tpu_custom_call" | custom-call | flops 754974720 | bytes 3833856 | tf_op jit(solution)/shard_map/pallas_call | solution.py:407
  19.7 1.9 collective-permute-start.6
  21.8 1.8 collective-permute-start.10
  23.9 3.4 %collective-permute-done.6.refs_0_.refs_1_ = bf16[240,384]{1,0:T(8,128)(2,1)S(1)} collective-permute-done((bf16[240,384]{1,0:T(8,128)(2,1)S(1)}, bf16[240,384]{1,0:T(8,128)(2,1)S(1)}, u32[]{:S(2)}, u32[]{:S(2)}) %collective-permute-start.6) | collective-permute-done | bytes 184352 | tf_op jit(solution)/shard_map/ppermute | solution.py:32
  27.4 3.8 %collective-permute-done.38 = bf16[240,384]{1,0:T(8,128)(2,1)S(1)} collective-permute-done((bf16[240,384]{1,0:T(8,128)(2,1)S(1)}, bf16[240,384]{1,0:T(8,128)(2,1)S(1)}, u32[]{:S(2)}, u32[]{:S(2)}) %collective-permute-start.38) | collective-permute-done | bytes 184352 | tf_op jit(solution)/shard_map/ppermute | solution.py:32
  31.4 3.8 %collective-permute-done.10 = bf16[240,384]{1,0:T(8,128)(2,1)S(1)} collective-permute-done((bf16[240,384]{1,0:T(8,128)(2,1)S(1)}, bf16[240,384]{1,0:T(8,128)(2,1)S(1)}, u32[]{:S(2)}, u32[]{:S(2)}) %collective-permute-start.10) | collective-permute-done | bytes 184352 | tf_op jit(solution)/shard_map/ppermute | solution.py:32
  35.3 3.6 %shard_map.120 = (bf16[320,512]{1,0:T(8,128)(2,1)S(1)}, bf16[320,512]{1,0:T(8,128)(2,1)S(1)}, bf16[240,384]{1,0:T(8,128)(2,1)S(1)}, bf16[240,384]{1,0:T(8,128)(2...) custom-call(s32[10]{0:T(128)S(1)} %stack.35.scal, ...), custom_call_target="tpu_custom_call" | custom-call | flops 754974720 | bytes 3833856 | tf_op jit(solution)/shard_map/pallas_call | solution.py:407
  39.6 3.4 %collective-permute-start.37 = (bf16[240,384]{1,0:T(8,128)(2,1)S(1)}, bf16[240,384]{1,0:T(8,128)(2,1)S(1)}, u32[]{:S(2)}, u32[]{:S(2)}) collective-permute-start(bf16[240,384]{1,0:T(8,128)(2,1)S(1)} %fusion.5), channel_id=1, source_target_pairs={{0,1},{1,0},{2,3},{3,2},{4,5},{5,4},{6,7},{7,6},{8,9},{9,8},{10,11... | collective-permute-start | bytes 552968 | tf_op jit(solution)/shard_map/ppermute | solution.py:32
  43.1 5.0 %collective-permute-start.9 = (bf16[240,384]{1,0:T(8,128)(2,1)S(1)}, bf16[240,384]{1,0:T(8,128)(2,1)S(1)}, u32[]{:S(2)}, u32[]{:S(2)}) collective-permute-start(bf16[240,384]{1,0:T(8,128)(2,1)S(1)} %fusion.1), channel_id=1, source_target_pairs={{0,1},{1,0},{2,3},{3,2},{4,5},{5,4},{6,7},{7,6},{8,9},{9,8},{10,11... | collective-permute-start | bytes 552968 | tf_op jit(solution)/shard_map/ppermute | solution.py:32
  48.3 3.4 %collective-permute-start.40 = (bf16[240,384]{1,0:T(8,128)(2,1)S(1)}, bf16[240,384]{1,0:T(8,128)(2,1)S(1)}, u32[]{:S(2)}, u32[]{:S(2)}) collective-permute-start(bf16[240,384]{1,0:T(8,128)(2,1)S(1)} %get-tuple-element.126.refs_4_.refs_1_), channel_id=1, source_target_pairs={{0,1},{1,0},{2,3},{3,2},{4,5},{5,4},{6,7},{7,6},{8,9},{9,8},{10,11... | collective-permute-start | bytes 552968 | tf_op jit(solution)/shard_map/ppermute | solution.py:32
  51.7 1.3 collective-permute-done.9.refs_1_
  53.2 2.5 %collective-permute-start.16 = (bf16[240,384]{1,0:T(8,128)(2,1)S(1)}, bf16[240,384]{1,0:T(8,128)(2,1)S(1)}, u32[]{:S(2)}, u32[]{:S(2)}) collective-permute-start(bf16[240,384]{1,0:T(8,128)(2,1)S(1)} %get-tuple-element.102.refs_10_.refs_7_), channel_id=1, source_target_pairs={{0,1},{1,0},{2,3},{3,2},{4,5},{5,4},{6,7},{7,6},{8,9},{9,8},{10,11... | collective-permute-start | bytes 552968 | tf_op jit(solution)/shard_map/ppermute | solution.py:32
  56.0 5.0 %collective-permute-done.16.refs_11_.refs_8_ = bf16[240,384]{1,0:T(8,128)(2,1)S(1)} collective-permute-done((bf16[240,384]{1,0:T(8,128)(2,1)S(1)}, bf16[240,384]{1,0:T(8,128)(2,1)S(1)}, u32[]{:S(2)}, u32[]{:S(2)}) %collective-permute-start.16) | collective-permute-done | bytes 184352 | tf_op jit(solution)/shard_map/ppermute | solution.py:32
  61.0 2.5 %collective-permute-start.13 = (bf16[240,384]{1,0:T(8,128)(2,1)S(1)}, bf16[240,384]{1,0:T(8,128)(2,1)S(1)}, u32[]{:S(2)}, u32[]{:S(2)}) collective-permute-start(bf16[240,384]{1,0:T(8,128)(2,1)S(1)} %broadcast_select_fusion.11), channel_id=1, source_target_pairs={{0,1},{1,0},{2,3},{3,2},{4,5},{5,4},{6,7},{7,6},{8,9},{9,8},{10,11... | collective-permute-start | bytes 552968 | tf_op jit(solution)/shard_map/ppermute | solution.py:32
  63.6 3.6 %shard_map.123 = (bf16[320,512]{1,0:T(8,128)(2,1)S(1)}, bf16[320,512]{1,0:T(8,128)(2,1)S(1)}, bf16[240,384]{1,0:T(8,128)(2,1)S(1)}, bf16[240,384]{1,0:T(8,128)(2...) custom-call(s32[10]{0:T(128)S(1)} %stack.35.scal, ...), custom_call_target="tpu_custom_call" | custom-call | flops 754974720 | bytes 3833856 | tf_op jit(solution)/shard_map/pallas_call | solution.py:407
  67.2 2.8 %collective-permute-start.18 = (bf16[240,384]{1,0:T(8,128)(2,1)S(1)}, bf16[240,384]{1,0:T(8,128)(2,1)S(1)}, u32[]{:S(2)}, u32[]{:S(2)}) collective-permute-start(bf16[240,384]{1,0:T(8,128)(2,1)S(1)} %broadcast_select_fusion.10), channel_id=1, source_target_pairs={{0,1},{1,0},{2,3},{3,2},{4,5},{5,4},{6,7},{7,6},{8,9},{9,8},{10,11... | collective-permute-start | bytes 552968 | tf_op jit(solution)/shard_map/ppermute | solution.py:32
  70.0 1.9 collective-permute-start.44
  72.7 2.8 %collective-permute-done.18.refs_14_.refs_11_ = bf16[240,384]{1,0:T(8,128)(2,1)S(1)} collective-permute-done((bf16[240,384]{1,0:T(8,128)(2,1)S(1)}, bf16[240,384]{1,0:T(8,128)(2,1)S(1)}, u32[]{:S(2)}, u32[]{:S(2)}) %collective-permute-start.18) | collective-permute-done | bytes 184352 | tf_op jit(solution)/shard_map/ppermute | solution.py:32
  75.6 2.6 %collective-permute-done.44.refs_8_.refs_5_ = bf16[240,384]{1,0:T(8,128)(2,1)S(1)} collective-permute-done((bf16[240,384]{1,0:T(8,128)(2,1)S(1)}, bf16[240,384]{1,0:T(8,128)(2,1)S(1)}, u32[]{:S(2)}, u32[]{:S(2)}) %collective-permute-start.44) | collective-permute-done | bytes 184352 | tf_op jit(solution)/shard_map/ppermute | solution.py:32
  78.5 5.4 %collective-permute-start.46 = (bf16[240,384]{1,0:T(8,128)(2,1)S(1)}, bf16[240,384]{1,0:T(8,128)(2,1)S(1)}, u32[]{:S(2)}, u32[]{:S(2)}) collective-permute-start(bf16[240,384]{1,0:T(8,128)(2,1)S(1)} %fusion.6), channel_id=1, source_target_pairs={{0,1},{1,0},{2,3},{3,2},{4,5},{5,4},{6,7},{7,6},{8,9},{9,8},{10,11... | collective-permute-start | bytes 552968 | tf_op jit(solution)/shard_map/ppermute | solution.py:32
  84.0 3.5 %shard_map.132 = (f32[2,2,128,512]{3,2,1,0:T(8,128)S(1)}, f32[2,2,128,512]{3,2,1,0:T(8,128)S(1)}, f32[8,128]{1,0:T(8,128)S(1)}) custom-call(s32[10]{0:T(128)S(1)} %stack.35.scal, f32[16,128]{1,0:T(8,128)S(1)} %get-tuple-element.94.refs_0_.refs_1_, f32[16,128]{1,0:T(8,128)S(1)} %collective-permute-done.refs_1_.refs_2_, ...), custom_call_target="tpu_custom_call" | custom-call | flops 754974720 | bytes 4571136 | tf_op jit(solution)/shard_map/pallas_call | solution.py:456
  87.8 2.8 %collective-permute-start.48 = (bf16[240,384]{1,0:T(8,128)(2,1)S(1)}, bf16[240,384]{1,0:T(8,128)(2,1)S(1)}, u32[]{:S(2)}, u32[]{:S(2)}) collective-permute-start(bf16[240,384]{1,0:T(8,128)(2,1)S(1)} %get-tuple-element.136.refs_6_.refs_1_), channel_id=1, source_target_pairs={{0,1},{1,0},{2,3},{3,2},{4,5},{5,4},{6,7},{7,6},{8,9},{9,8},{10,11... | collective-permute-start | bytes 552968 | tf_op jit(solution)/shard_map/ppermute | solution.py:32
  91.7 3.4 %shard_map.136 = (bf16[4,512,768]{2,1,0:T(8,128)(2,1)}, bf16[4,512,768]{2,1,0:T(8,128)(2,1)}, bf16[4,768,512]{2,1,0:T(8,128)(2,1)}, f32[8,128]{1,0:T(8,128)S(1)}) custom-call(s32[10]{0:T(128)S(1)} %stack.35.scal, bf16[320,512]{1,0:T(8,128)(2,1)S(1)} %get-tuple-element.142.in_ref, bf16[320,512]{1,0:T(8,128)(2,1)S(1)} %get-tuple-element.143.cot_ref, ...), custom_call_target="tpu_custom_call" | custom-call | flops 754974720 | bytes 4571136 | tf_op jit(solution)/shard_map/pallas_call | solution.py:481
  95.1 2.5 %collective-permute-start.50 = (bf16[240,384]{1,0:T(8,128)(2,1)S(1)}, bf16[240,384]{1,0:T(8,128)(2,1)S(1)}, u32[]{:S(2)}, u32[]{:S(2)}) collective-permute-start(bf16[240,384]{1,0:T(8,128)(2,1)S(1)} %broadcast_select_fusion.3), channel_id=1, source_target_pairs={{0,1},{1,0},{2,3},{3,2},{4,5},{5,4},{6,7},{7,6},{8,9},{9,8},{10,11... | collective-permute-start | bytes 552968 | tf_op jit(solution)/shard_map/ppermute | solution.py:32
  97.6 1.6 collective-permute-start.21
  99.3 3.6 %shard_map.126 = (bf16[320,512]{1,0:T(8,128)(2,1)S(1)}, bf16[320,512]{1,0:T(8,128)(2,1)S(1)}, bf16[240,384]{1,0:T(8,128)(2,1)S(1)}, bf16[240,384]{1,0:T(8,128)(2...) custom-call(s32[10]{0:T(128)S(1)} %stack.35.scal, ...), custom_call_target="tpu_custom_call" | custom-call | flops 754974720 | bytes 3833856 | tf_op jit(solution)/shard_map/pallas_call | solution.py:407
  103.6 3.3 %collective-permute-start.52 = (bf16[240,384]{1,0:T(8,128)(2,1)S(1)}, bf16[240,384]{1,0:T(8,128)(2,1)S(1)}, u32[]{:S(2)}, u32[]{:S(2)}) collective-permute-start(bf16[240,384]{1,0:T(8,128)(2,1)S(1)} %broadcast_select_fusion.2), channel_id=1, source_target_pairs={{0,1},{1,0},{2,3},{3,2},{4,5},{5,4},{6,7},{7,6},{8,9},{9,8},{10,11... | collective-permute-start | bytes 552968 | tf_op jit(solution)/shard_map/ppermute | solution.py:32
  106.9 2.2 %collective-permute-start.26 = (bf16[240,384]{1,0:T(8,128)(2,1)S(1)}, bf16[240,384]{1,0:T(8,128)(2,1)S(1)}, u32[]{:S(2)}, u32[]{:S(2)}) collective-permute-start(bf16[240,384]{1,0:T(8,128)(2,1)S(1)} %broadcast_select_fusion.8), channel_id=1, source_target_pairs={{0,1},{1,0},{2,3},{3,2},{4,5},{5,4},{6,7},{7,6},{8,9},{9,8},{10,11... | collective-permute-start | bytes 552968 | tf_op jit(solution)/shard_map/ppermute | solution.py:32
  109.3 4.7 %collective-permute-start.54 = (bf16[240,384]{1,0:T(8,128)(2,1)S(1)}, bf16[240,384]{1,0:T(8,128)(2,1)S(1)}, u32[]{:S(2)}, u32[]{:S(2)}) collective-permute-start(bf16[240,384]{1,0:T(8,128)(2,1)S(1)} %fusion.7), channel_id=1, source_target_pairs={{0,1},{1,0},{2,3},{3,2},{4,5},{5,4},{6,7},{7,6},{8,9},{9,8},{10,11... | collective-permute-start | bytes 552968 | tf_op jit(solution)/shard_map/ppermute | solution.py:32
  114.1 2.3 %collective-permute-done.26.refs_16_.refs_11_ = bf16[240,384]{1,0:T(8,128)(2,1)S(1)} collective-permute-done((bf16[240,384]{1,0:T(8,128)(2,1)S(1)}, bf16[240,384]{1,0:T(8,128)(2,1)S(1)}, u32[]{:S(2)}, u32[]{:S(2)}) %collective-permute-start.26) | collective-permute-done | bytes 184352 | tf_op jit(solution)/shard_map/ppermute | solution.py:32
  116.6 2.5 %collective-permute-start.23 = (bf16[240,384]{1,0:T(8,128)(2,1)S(1)}, bf16[240,384]{1,0:T(8,128)(2,1)S(1)}, u32[]{:S(2)}, u32[]{:S(2)}) collective-permute-start(bf16[240,384]{1,0:T(8,128)(2,1)S(1)} %fusion.3), channel_id=1, source_target_pairs={{0,1},{1,0},{2,3},{3,2},{4,5},{5,4},{6,7},{7,6},{8,9},{9,8},{10,11... | collective-permute-start | bytes 552968 | tf_op jit(solution)/shard_map/ppermute | solution.py:32
  119.1 3.5 %shard_map.135 = (f32[2,2,128,512]{3,2,1,0:T(8,128)S(1)}, f32[2,2,128,512]{3,2,1,0:T(8,128)S(1)}, f32[8,128]{1,0:T(8,128)S(1)}) custom-call(s32[10]{0:T(128)S(1)} %stack.35.scal, f32[16,128]{1,0:T(8,128)S(1)} %get-tuple-element.94.refs_0_.refs_1_, f32[16,128]{1,0:T(8,128)S(1)} %collective-permute-done.refs_1_.refs_2_, ...), custom_call_target="tpu_custom_call" | custom-call | flops 754974720 | bytes 4571136 | tf_op jit(solution)/shard_map/pallas_call | solution.py:456
  122.9 1.3 collective-permute-start.56
  125.2 3.4 %shard_map.140 = (bf16[4,512,768]{2,1,0:T(8,128)(2,1)}, bf16[4,512,768]{2,1,0:T(8,128)(2,1)}, bf16[4,768,512]{2,1,0:T(8,128)(2,1)}, f32[8,128]{1,0:T(8,128)S(1)}) custom-call(s32[10]{0:T(128)S(1)} %stack.35.scal, bf16[320,512]{1,0:T(8,128)(2,1)S(1)} %get-tuple-element.155.in_ref, ...), custom_call_target="tpu_custom_call", output_to_operand_aliasing={{0}: (16, {}), {1}: (17, {}), {2}: (18, {})} | custom-call | flops 754974720 | bytes 4571136 | tf_op jit(solution)/shard_map/pallas_call | solution.py:481
  128.6 2.5 %collective-permute-start.58 = (bf16[240,384]{1,0:T(8,128)(2,1)S(1)}, bf16[240,384]{1,0:T(8,128)(2,1)S(1)}, u32[]{:S(2)}, u32[]{:S(2)}) collective-permute-start(bf16[240,384]{1,0:T(8,128)(2,1)S(1)} %broadcast_select_fusion.1), channel_id=1, source_target_pairs={{0,1},{1,0},{2,3},{3,2},{4,5},{5,4},{6,7},{7,6},{8,9},{9,8},{10,11... | collective-permute-start | bytes 552968 | tf_op jit(solution)/shard_map/ppermute | solution.py:32
  131.1 2.1 %collective-permute-start.29 = (bf16[240,384]{1,0:T(8,128)(2,1)S(1)}, bf16[240,384]{1,0:T(8,128)(2,1)S(1)}, u32[]{:S(2)}, u32[]{:S(2)}) collective-permute-start(bf16[240,384]{1,0:T(8,128)(2,1)S(1)} %broadcast_select_fusion.7), channel_id=1, source_target_pairs={{0,1},{1,0},{2,3},{3,2},{4,5},{5,4},{6,7},{7,6},{8,9},{9,8},{10,11... | collective-permute-start | bytes 552968 | tf_op jit(solution)/shard_map/ppermute | solution.py:32
  133.3 1.1 collective-permute-done.32.refs_13_.refs_8_
  134.4 4.5 %collective-permute-start.60 = (bf16[240,384]{1,0:T(8,128)(2,1)S(1)}, bf16[240,384]{1,0:T(8,128)(2,1)S(1)}, u32[]{:S(2)}, u32[]{:S(2)}) collective-permute-start(bf16[240,384]{1,0:T(8,128)(2,1)S(1)} %broadcast_select_fusion), channel_id=1, source_target_pairs={{0,1},{1,0},{2,3},{3,2},{4,5},{5,4},{6,7},{7,6},{8,9},{9,8},{10,11... | collective-permute-start | bytes 552968 | tf_op jit(solution)/shard_map/ppermute | solution.py:32
  139.1 3.6 %collective-permute-start.34 = (bf16[240,384]{1,0:T(8,128)(2,1)S(1)}, bf16[240,384]{1,0:T(8,128)(2,1)S(1)}, u32[]{:S(2)}, u32[]{:S(2)}) collective-permute-start(bf16[240,384]{1,0:T(8,128)(2,1)S(1)} %broadcast_select_fusion.6), channel_id=1, source_target_pairs={{0,1},{1,0},{2,3},{3,2},{4,5},{5,4},{6,7},{7,6},{8,9},{9,8},{10,11... | collective-permute-start | bytes 552968 | tf_op jit(solution)/shard_map/ppermute | solution.py:32
  142.8 3.4 %collective-permute-done.60.refs_10_.refs_5_ = bf16[240,384]{1,0:T(8,128)(2,1)S(1)} collective-permute-done((bf16[240,384]{1,0:T(8,128)(2,1)S(1)}, bf16[240,384]{1,0:T(8,128)(2,1)S(1)}, u32[]{:S(2)}, u32[]{:S(2)}) %collective-permute-start.60) | collective-permute-done | bytes 184352 | tf_op jit(solution)/shard_map/ppermute | solution.py:32
  146.4 2.1 %collective-permute-start.62 = (bf16[240,384]{1,0:T(8,128)(2,1)S(1)}, bf16[240,384]{1,0:T(8,128)(2,1)S(1)}, u32[]{:S(2)}, u32[]{:S(2)}) collective-permute-start(bf16[240,384]{1,0:T(8,128)(2,1)S(1)} %fusion.8), channel_id=1, source_target_pairs={{0,1},{1,0},{2,3},{3,2},{4,5},{5,4},{6,7},{7,6},{8,9},{9,8},{10,11... | collective-permute-start | bytes 552968 | tf_op jit(solution)/shard_map/ppermute | solution.py:32
  148.5 1.3 collective-permute-done.34.refs_16_.refs_11_
  150.0 1.2 collective-permute-start.31
  151.1 3.6 %shard_map.139 = (f32[2,2,128,512]{3,2,1,0:T(8,128)S(1)}, f32[2,2,128,512]{3,2,1,0:T(8,128)S(1)}, f32[8,128]{1,0:T(8,128)S(1)}) custom-call(s32[10]{0:T(128)S(1)} %stack.35.scal, f32[16,128]{1,0:T(8,128)S(1)} %get-tuple-element.94.refs_0_.refs_1_, f32[16,128]{1,0:T(8,128)S(1)} %collective-permute-done.refs_1_.refs_2_, ...), custom_call_target="tpu_custom_call" | custom-call | flops 754974720 | bytes 4571136 | tf_op jit(solution)/shard_map/pallas_call | solution.py:456
  154.9 2.7 %collective-permute-done.31.refs_1_ = bf16[240,384]{1,0:T(8,128)(2,1)S(1)} collective-permute-done((bf16[240,384]{1,0:T(8,128)(2,1)S(1)}, bf16[240,384]{1,0:T(8,128)(2,1)S(1)}, u32[]{:S(2)}, u32[]{:S(2)}) %collective-permute-start.31) | collective-permute-done | bytes 184352 | tf_op jit(solution)/shard_map/ppermute | solution.py:32
  159.1 1.4 collective-permute-start.64
  160.4 5.8 %collective-permute-done.69.refs_14_.refs_8_ = bf16[256,384]{1,0:T(8,128)(2,1)S(1)} collective-permute-done((bf16[256,384]{1,0:T(8,128)(2,1)S(1)}, bf16[256,384]{1,0:T(8,128)(2,1)S(1)}, u32[]{:S(2)}, u32[]{:S(2)}) %collective-permute-start.69) | collective-permute-done | bytes 196640 | tf_op jit(solution)/shard_map/ppermute | solution.py:32
  166.7 2.3 %collective-permute-done.64.refs_8_.refs_2_ = bf16[240,384]{1,0:T(8,128)(2,1)S(1)} collective-permute-done((bf16[240,384]{1,0:T(8,128)(2,1)S(1)}, bf16[240,384]{1,0:T(8,128)(2,1)S(1)}, u32[]{:S(2)}, u32[]{:S(2)}) %collective-permute-start.64) | collective-permute-done | bytes 184352 | tf_op jit(solution)/shard_map/ppermute | solution.py:32
  170.0 4.8 %collective-permute-start.73 = (bf16[256,384]{1,0:T(8,128)(2,1)S(1)}, bf16[256,384]{1,0:T(8,128)(2,1)S(1)}, u32[]{:S(2)}, u32[]{:S(2)}) collective-permute-start(bf16[256,384]{1,0:T(8,128)(2,1)S(1)} %collective-permute-done.72.refs_18_.refs_12_), channel_id=1, source_target_pairs={{0,1},{1,0},{2,3},{3,2},{4,5},{5,4},{6,7},{7,6},{8,9},{9,8},{10,11... | collective-permute-start | bytes 589832 | tf_op jit(solution)/shard_map/ppermute | solution.py:32
  174.8 2.2 %collective-permute-start.66 = (bf16[240,384]{1,0:T(8,128)(2,1)S(1)}, bf16[240,384]{1,0:T(8,128)(2,1)S(1)}, u32[]{:S(2)}, u32[]{:S(2)}) collective-permute-start(bf16[240,384]{1,0:T(8,128)(2,1)S(1)} %collective-permute-done.65.refs_10_.refs_4_), channel_id=1, source_target_pairs={{0,1},{1,0},{2,3},{3,2},{4,5},{5,4},{6,7},{7,6},{8,9},{9,8},{10,11... | collective-permute-start | bytes 552968 | tf_op jit(solution)/shard_map/ppermute | solution.py:32
  177.0 2.0 collective-permute-start.68
  178.9 3.4 %shard_map.144 = (bf16[4,512,768]{2,1,0:T(8,128)(2,1)}, bf16[4,512,768]{2,1,0:T(8,128)(2,1)}, bf16[4,768,512]{2,1,0:T(8,128)(2,1)}, f32[8,128]{1,0:T(8,128)S(1)}) custom-call(s32[10]{0:T(128)S(1)} %stack.35.scal, bf16[320,512]{1,0:T(8,128)(2,1)S(1)} %get-tuple-element.103.in_ref, ...), custom_call_target="tpu_custom_call", output_to_operand_aliasing={{0}: (16, {}), {1}: (17, {}), {2}: (18, {})} | custom-call | flops 754974720 | bytes 4571136 | tf_op jit(solution)/shard_map/pallas_call | solution.py:481
  182.3 2.5 %collective-permute-done.66.refs_9_.refs_3_ = bf16[240,384]{1,0:T(8,128)(2,1)S(1)} collective-permute-done((bf16[240,384]{1,0:T(8,128)(2,1)S(1)}, bf16[240,384]{1,0:T(8,128)(2,1)S(1)}, u32[]{:S(2)}, u32[]{:S(2)}) %collective-permute-start.66) | collective-permute-done | bytes 184352 | tf_op jit(solution)/shard_map/ppermute | solution.py:32
  184.9 3.6 %collective-permute-done.68.refs_11_.refs_5_ = bf16[240,384]{1,0:T(8,128)(2,1)S(1)} collective-permute-done((bf16[240,384]{1,0:T(8,128)(2,1)S(1)}, bf16[240,384]{1,0:T(8,128)(2,1)S(1)}, u32[]{:S(2)}, u32[]{:S(2)}) %collective-permute-start.68) | collective-permute-done | bytes 184352 | tf_op jit(solution)/shard_map/ppermute | solution.py:32
  188.4 4.1 %shard_map.145 = (bf16[2,2,128,512]{3,2,1,0:T(8,128)(2,1)S(1)}, bf16[2,2,128,512]{3,2,1,0:T(8,128)(2,1)S(1)}, f32[8,128]{1,0:T(8,128)}, f32[2,16,128]{2,1,0:T(8,128)S(1)}, f32[2,16,128]{2,1,0:T(8,128)S(1)}) custom-call(s32[10]{0:T(128)S(1)} %stack.35.scal, f32[8,128]{1,0:T(8,128)S(1)} %get-tuple-element.166.refs_0_, ...), custom_call_target="tpu_custom_call" | custom-call | flops 754974720 | bytes 4571136 | tf_op jit(solution)/shard_map/pallas_call | solution.py:456
  193.1 1.4 collective-permute-done.74
  194.7 1.5 collective-permute-start.77
  196.8 3.4 %shard_map.146 = (bf16[4,512,768]{2,1,0:T(8,128)(2,1)}, bf16[4,512,768]{2,1,0:T(8,128)(2,1)}, bf16[4,768,512]{2,1,0:T(8,128)(2,1)}, f32[8,128]{1,0:T(8,128)}) custom-call(s32[10]{0:T(128)S(1)} %stack.35.scal, bf16[320,512]{1,0:T(8,128)(2,1)S(1)} %get-tuple-element.172.in_ref, ...), custom_call_target="tpu_custom_call", output_to_operand_aliasing={{0}: (16, {}), {1}: (17, {}), {2}: (18, {})} | custom-call | flops 754974720 | bytes 4571136 | tf_op jit(solution)/shard_map/pallas_call | solution.py:481
  200.8 3.4 %collective-permute-done.75 = bf16[2,128,512]{2,1,0:T(8,128)(2,1)S(1)} collective-permute-done((bf16[2,128,512]{2,1,0:T(8,128)(2,1)S(1)}, bf16[2,128,512]{2,1,0:T(8,128)(2,1)S(1)}, u32[]{:S(2)}, u32[]{:S(2)}) %collective-permute-start.75) | collective-permute-done | bytes 262176 | tf_op jit(solution)/shard_map/ppermute | solution.py:32
  (163 shorter events, 15.3 us)
Async XLA Ops:
  1.7 9.3 %collective-permute-start.3 = (bf16[2,128,512]{2,1,0:T(8,128)(2,1)S(1)}, bf16[2,128,512]{2,1,0:T(8,128)(2,1)S(1)}, u32[]{:S(2)}, u32[]{:S(2)}) collective-permute-start(bf16[2,128,512]{2,1,0:T(8,128)(2,1)S(1)} %get-tuple-element.95.refs_4_.refs_5_), channel_id=1, source_target_pairs={{0,8},{4,12},{8,0},{12,4},{1,9},{5,13},{9,1},{13,5},{2,10},{6,14},... | collective-permute-start | bytes 786440 | tf_op jit(solution)/shard_map/ppermute | solution.py:32
  4.7 11.1 %collective-permute-start.4 = (bf16[2,128,512]{2,1,0:T(8,128)(2,1)S(1)}, bf16[2,128,512]{2,1,0:T(8,128)(2,1)S(1)}, u32[]{:S(2)}, u32[]{:S(2)}) collective-permute-start(bf16[2,128,512]{2,1,0:T(8,128)(2,1)S(1)} %get-tuple-element.95.refs_4_.refs_5_), channel_id=1, source_target_pairs={{0,4},{4,0},{8,12},{12,8},{1,5},{5,1},{9,13},{13,9},{2,6},{6,2},{1... | collective-permute-start | bytes 786440 | tf_op jit(solution)/shard_map/ppermute | solution.py:32
  19.7 7.5 %collective-permute-start.6 = (bf16[240,384]{1,0:T(8,128)(2,1)S(1)}, bf16[240,384]{1,0:T(8,128)(2,1)S(1)}, u32[]{:S(2)}, u32[]{:S(2)}) collective-permute-start(bf16[240,384]{1,0:T(8,128)(2,1)S(1)} %get-tuple-element.98.refs_0_), channel_id=1, source_target_pairs={{0,1},{1,0},{2,3},{3,2},{4,5},{5,4},{6,7},{7,6},{8,9},{9,8},{10,11... | collective-permute-start | bytes 552968 | tf_op jit(solution)/shard_map/ppermute | solution.py:32
  21.6 9.6 %collective-permute-start.38 = (bf16[240,384]{1,0:T(8,128)(2,1)S(1)}, bf16[240,384]{1,0:T(8,128)(2,1)S(1)}, u32[]{:S(2)}, u32[]{:S(2)}) collective-permute-start(bf16[240,384]{1,0:T(8,128)(2,1)S(1)} %get-tuple-element.123), channel_id=1, source_target_pairs={{0,1},{1,0},{2,3},{3,2},{4,5},{5,4},{6,7},{7,6},{8,9},{9,8},{10,11... | collective-permute-start | bytes 552968 | tf_op jit(solution)/shard_map/ppermute | solution.py:32
  21.8 13.3 %collective-permute-start.10 = (bf16[240,384]{1,0:T(8,128)(2,1)S(1)}, bf16[240,384]{1,0:T(8,128)(2,1)S(1)}, u32[]{:S(2)}, u32[]{:S(2)}) collective-permute-start(bf16[240,384]{1,0:T(8,128)(2,1)S(1)} %get-tuple-element.101), channel_id=1, source_target_pairs={{0,1},{1,0},{2,3},{3,2},{4,5},{5,4},{6,7},{7,6},{8,9},{9,8},{10,11... | collective-permute-start | bytes 552968 | tf_op jit(solution)/shard_map/ppermute | solution.py:32
  23.7 15.2 %collective-permute-start.7 = (bf16[240,384]{1,0:T(8,128)(2,1)S(1)}, bf16[240,384]{1,0:T(8,128)(2,1)S(1)}, u32[]{:S(2)}, u32[]{:S(2)}) collective-permute-start(bf16[240,384]{1,0:T(8,128)(2,1)S(1)} %get-tuple-element.100.refs_1_), channel_id=1, source_target_pairs={{0,1},{1,0},{2,3},{3,2},{4,5},{5,4},{6,7},{7,6},{8,9},{9,8},{10,11... | collective-permute-start | bytes 552968 | tf_op jit(solution)/shard_map/ppermute | solution.py:32
  27.3 12.2 %collective-permute-start.36 = (bf16[240,384]{1,0:T(8,128)(2,1)S(1)}, bf16[240,384]{1,0:T(8,128)(2,1)S(1)}, u32[]{:S(2)}, u32[]{:S(2)}) collective-permute-start(bf16[240,384]{1,0:T(8,128)(2,1)S(1)} %shard_map.130), channel_id=1, source_target_pairs={{1,2},{2,1},{0,4},{3,7},{5,6},{6,5},{4,0},{7,3},{9,10},{10,9},{8,1... | collective-permute-start | bytes 552968 | tf_op jit(solution)/shard_map/ppermute | solution.py:506
  31.3 16.8 %collective-permute-start.39 = (bf16[240,384]{1,0:T(8,128)(2,1)S(1)}, bf16[240,384]{1,0:T(8,128)(2,1)S(1)}, u32[]{:S(2)}, u32[]{:S(2)}) collective-permute-start(bf16[240,384]{1,0:T(8,128)(2,1)S(1)} %fusion.13), channel_id=1, source_target_pairs={{1,2},{2,1},{0,4},{3,7},{5,6},{6,5},{4,0},{7,3},{9,10},{10,9},{8,1... | collective-permute-start | bytes 552968 | tf_op jit(solution)/shard_map/ppermute | solution.py:506
  35.2 16.5 %collective-permute-start.11 = (bf16[240,384]{1,0:T(8,128)(2,1)S(1)}, bf16[240,384]{1,0:T(8,128)(2,1)S(1)}, u32[]{:S(2)}, u32[]{:S(2)}) collective-permute-start(bf16[240,384]{1,0:T(8,128)(2,1)S(1)} %fusion.9), channel_id=1, source_target_pairs={{1,2},{2,1},{0,4},{3,7},{5,6},{6,5},{4,0},{7,3},{9,10},{10,9},{8,1... | collective-permute-start | bytes 552968 | tf_op jit(solution)/shard_map/ppermute | solution.py:506
  39.6 8.5 %collective-permute-start.37 = (bf16[240,384]{1,0:T(8,128)(2,1)S(1)}, bf16[240,384]{1,0:T(8,128)(2,1)S(1)}, u32[]{:S(2)}, u32[]{:S(2)}) collective-permute-start(bf16[240,384]{1,0:T(8,128)(2,1)S(1)} %fusion.5), channel_id=1, source_target_pairs={{0,1},{1,0},{2,3},{3,2},{4,5},{5,4},{6,7},{7,6},{8,9},{9,8},{10,11... | collective-permute-start | bytes 552968 | tf_op jit(solution)/shard_map/ppermute | solution.py:32
  43.1 10.0 %collective-permute-start.9 = (bf16[240,384]{1,0:T(8,128)(2,1)S(1)}, bf16[240,384]{1,0:T(8,128)(2,1)S(1)}, u32[]{:S(2)}, u32[]{:S(2)}) collective-permute-start(bf16[240,384]{1,0:T(8,128)(2,1)S(1)} %fusion.1), channel_id=1, source_target_pairs={{0,1},{1,0},{2,3},{3,2},{4,5},{5,4},{6,7},{7,6},{8,9},{9,8},{10,11... | collective-permute-start | bytes 552968 | tf_op jit(solution)/shard_map/ppermute | solution.py:32
  48.3 7.5 %collective-permute-start.41 = (bf16[240,384]{1,0:T(8,128)(2,1)S(1)}, bf16[240,384]{1,0:T(8,128)(2,1)S(1)}, u32[]{:S(2)}, u32[]{:S(2)}) collective-permute-start(bf16[240,384]{1,0:T(8,128)(2,1)S(1)} %get-tuple-element.126.refs_4_.refs_1_), channel_id=1, source_target_pairs={{1,2},{2,1},{0,4},{3,7},{5,6},{6,5},{4,0},{7,3},{9,10},{10,9},{8,1... | collective-permute-start | bytes 552968 | tf_op jit(solution)/shard_map/ppermute | solution.py:506
  48.3 15.2 %collective-permute-start.40 = (bf16[240,384]{1,0:T(8,128)(2,1)S(1)}, bf16[240,384]{1,0:T(8,128)(2,1)S(1)}, u32[]{:S(2)}, u32[]{:S(2)}) collective-permute-start(bf16[240,384]{1,0:T(8,128)(2,1)S(1)} %get-tuple-element.126.refs_4_.refs_1_), channel_id=1, source_target_pairs={{0,1},{1,0},{2,3},{3,2},{4,5},{5,4},{6,7},{7,6},{8,9},{9,8},{10,11... | collective-permute-start | bytes 552968 | tf_op jit(solution)/shard_map/ppermute | solution.py:32
  53.2 7.7 %collective-permute-start.16 = (bf16[240,384]{1,0:T(8,128)(2,1)S(1)}, bf16[240,384]{1,0:T(8,128)(2,1)S(1)}, u32[]{:S(2)}, u32[]{:S(2)}) collective-permute-start(bf16[240,384]{1,0:T(8,128)(2,1)S(1)} %get-tuple-element.102.refs_10_.refs_7_), channel_id=1, source_target_pairs={{0,1},{1,0},{2,3},{3,2},{4,5},{5,4},{6,7},{7,6},{8,9},{9,8},{10,11... | collective-permute-start | bytes 552968 | tf_op jit(solution)/shard_map/ppermute | solution.py:32
  55.8 16.3 %collective-permute-start.42 = (bf16[240,384]{1,0:T(8,128)(2,1)S(1)}, bf16[240,384]{1,0:T(8,128)(2,1)S(1)}, u32[]{:S(2)}, u32[]{:S(2)}) collective-permute-start(bf16[240,384]{1,0:T(8,128)(2,1)S(1)} %broadcast_select_fusion.5), channel_id=1, source_target_pairs={{0,1},{1,0},{2,3},{3,2},{4,5},{5,4},{6,7},{7,6},{8,9},{9,8},{10,11... | collective-permute-start | bytes 552968 | tf_op jit(solution)/shard_map/ppermute | solution.py:32
  61.0 6.2 %collective-permute-start.17 = (bf16[240,384]{1,0:T(8,128)(2,1)S(1)}, bf16[240,384]{1,0:T(8,128)(2,1)S(1)}, u32[]{:S(2)}, u32[]{:S(2)}) collective-permute-start(bf16[240,384]{1,0:T(8,128)(2,1)S(1)} %collective-permute-done.16.refs_11_.refs_8_), channel_id=1, source_target_pairs={{1,2},{2,1},{0,4},{3,7},{5,6},{6,5},{4,0},{7,3},{9,10},{10,9},{8,1... | collective-permute-start | bytes 552968 | tf_op jit(solution)/shard_map/ppermute | solution.py:506
  61.0 10.9 %collective-permute-start.13 = (bf16[240,384]{1,0:T(8,128)(2,1)S(1)}, bf16[240,384]{1,0:T(8,128)(2,1)S(1)}, u32[]{:S(2)}, u32[]{:S(2)}) collective-permute-start(bf16[240,384]{1,0:T(8,128)(2,1)S(1)} %broadcast_select_fusion.11), channel_id=1, source_target_pairs={{0,1},{1,0},{2,3},{3,2},{4,5},{5,4},{6,7},{7,6},{8,9},{9,8},{10,11... | collective-permute-start | bytes 552968 | tf_op jit(solution)/shard_map/ppermute | solution.py:32
  63.6 6.4 %collective-permute-start.43 = (bf16[240,384]{1,0:T(8,128)(2,1)S(1)}, bf16[240,384]{1,0:T(8,128)(2,1)S(1)}, u32[]{:S(2)}, u32[]{:S(2)}) collective-permute-start(bf16[240,384]{1,0:T(8,128)(2,1)S(1)} %collective-permute-done.40.refs_5_.refs_2_), channel_id=1, source_target_pairs={{1,2},{2,1},{0,4},{3,7},{5,6},{6,5},{4,0},{7,3},{9,10},{10,9},{8,1... | collective-permute-start | bytes 552968 | tf_op jit(solution)/shard_map/ppermute | solution.py:506
  67.2 8.3 %collective-permute-start.18 = (bf16[240,384]{1,0:T(8,128)(2,1)S(1)}, bf16[240,384]{1,0:T(8,128)(2,1)S(1)}, u32[]{:S(2)}, u32[]{:S(2)}) collective-permute-start(bf16[240,384]{1,0:T(8,128)(2,1)S(1)} %broadcast_select_fusion.10), channel_id=1, source_target_pairs={{0,1},{1,0},{2,3},{3,2},{4,5},{5,4},{6,7},{7,6},{8,9},{9,8},{10,11... | collective-permute-start | bytes 552968 | tf_op jit(solution)/shard_map/ppermute | solution.py:32
  70.0 8.2 %collective-permute-start.44 = (bf16[240,384]{1,0:T(8,128)(2,1)S(1)}, bf16[240,384]{1,0:T(8,128)(2,1)S(1)}, u32[]{:S(2)}, u32[]{:S(2)}) collective-permute-start(bf16[240,384]{1,0:T(8,128)(2,1)S(1)} %broadcast_select_fusion.4), channel_id=1, source_target_pairs={{0,1},{1,0},{2,3},{3,2},{4,5},{5,4},{6,7},{7,6},{8,9},{9,8},{10,11... | collective-permute-start | bytes 552968 | tf_op jit(solution)/shard_map/ppermute | solution.py:32
  72.0 11.9 %collective-permute-start.14 = (bf16[240,384]{1,0:T(8,128)(2,1)S(1)}, bf16[240,384]{1,0:T(8,128)(2,1)S(1)}, u32[]{:S(2)}, u32[]{:S(2)}) collective-permute-start(bf16[240,384]{1,0:T(8,128)(2,1)S(1)} %shard_map.124), channel_id=1, source_target_pairs={{1,2},{2,1},{0,4},{3,7},{5,6},{6,5},{4,0},{7,3},{9,10},{10,9},{8,1... | collective-permute-start | bytes 552968 | tf_op jit(solution)/shard_map/ppermute | solution.py:506
  72.1 6.2 %collective-permute-start.45 = (bf16[240,384]{1,0:T(8,128)(2,1)S(1)}, bf16[240,384]{1,0:T(8,128)(2,1)S(1)}, u32[]{:S(2)}, u32[]{:S(2)}) collective-permute-start(bf16[240,384]{1,0:T(8,128)(2,1)S(1)} %shard_map.133), channel_id=1, source_target_pairs={{1,2},{2,1},{0,4},{3,7},{5,6},{6,5},{4,0},{7,3},{9,10},{10,9},{8,1... | collective-permute-start | bytes 552968 | tf_op jit(solution)/shard_map/ppermute | solution.py:506
  75.5 15.1 %collective-permute-start.19 = (bf16[240,384]{1,0:T(8,128)(2,1)S(1)}, bf16[240,384]{1,0:T(8,128)(2,1)S(1)}, u32[]{:S(2)}, u32[]{:S(2)}) collective-permute-start(bf16[240,384]{1,0:T(8,128)(2,1)S(1)} %fusion.10), channel_id=1, source_target_pairs={{1,2},{2,1},{0,4},{3,7},{5,6},{6,5},{4,0},{7,3},{9,10},{10,9},{8,1... | collective-permute-start | bytes 552968 | tf_op jit(solution)/shard_map/ppermute | solution.py:506
  78.3 9.3 %collective-permute-start.47 = (bf16[240,384]{1,0:T(8,128)(2,1)S(1)}, bf16[240,384]{1,0:T(8,128)(2,1)S(1)}, u32[]{:S(2)}, u32[]{:S(2)}) collective-permute-start(bf16[240,384]{1,0:T(8,128)(2,1)S(1)} %fusion.14), channel_id=1, source_target_pairs={{1,2},{2,1},{0,4},{3,7},{5,6},{6,5},{4,0},{7,3},{9,10},{10,9},{8,1... | collective-permute-start | bytes 552968 | tf_op jit(solution)/shard_map/ppermute | solution.py:506
  78.5 9.1 %collective-permute-start.46 = (bf16[240,384]{1,0:T(8,128)(2,1)S(1)}, bf16[240,384]{1,0:T(8,128)(2,1)S(1)}, u32[]{:S(2)}, u32[]{:S(2)}) collective-permute-start(bf16[240,384]{1,0:T(8,128)(2,1)S(1)} %fusion.6), channel_id=1, source_target_pairs={{0,1},{1,0},{2,3},{3,2},{4,5},{5,4},{6,7},{7,6},{8,9},{9,8},{10,11... | collective-permute-start | bytes 552968 | tf_op jit(solution)/shard_map/ppermute | solution.py:32
  83.9 6.7 %collective-permute-start.15 = (bf16[240,384]{1,0:T(8,128)(2,1)S(1)}, bf16[240,384]{1,0:T(8,128)(2,1)S(1)}, u32[]{:S(2)}, u32[]{:S(2)}) collective-permute-start(bf16[240,384]{1,0:T(8,128)(2,1)S(1)} %fusion.2), channel_id=1, source_target_pairs={{0,1},{1,0},{2,3},{3,2},{4,5},{5,4},{6,7},{7,6},{8,9},{9,8},{10,11... | collective-permute-start | bytes 552968 | tf_op jit(solution)/shard_map/ppermute | solution.py:32
  87.8 7.3 %collective-permute-start.49 = (bf16[240,384]{1,0:T(8,128)(2,1)S(1)}, bf16[240,384]{1,0:T(8,128)(2,1)S(1)}, u32[]{:S(2)}, u32[]{:S(2)}) collective-permute-start(bf16[240,384]{1,0:T(8,128)(2,1)S(1)} %get-tuple-element.136.refs_6_.refs_1_), channel_id=1, source_target_pairs={{1,2},{2,1},{0,4},{3,7},{5,6},{6,5},{4,0},{7,3},{9,10},{10,9},{8,1... | collective-permute-start | bytes 552968 | tf_op jit(solution)/shard_map/ppermute | solution.py:506
  87.8 9.7 %collective-permute-start.48 = (bf16[240,384]{1,0:T(8,128)(2,1)S(1)}, bf16[240,384]{1,0:T(8,128)(2,1)S(1)}, u32[]{:S(2)}, u32[]{:S(2)}) collective-permute-start(bf16[240,384]{1,0:T(8,128)(2,1)S(1)} %get-tuple-element.136.refs_6_.refs_1_), channel_id=1, source_target_pairs={{0,1},{1,0},{2,3},{3,2},{4,5},{5,4},{6,7},{7,6},{8,9},{9,8},{10,11... | collective-permute-start | bytes 552968 | tf_op jit(solution)/shard_map/ppermute | solution.py:32
  90.8 8.5 %collective-permute-start.24 = (bf16[240,384]{1,0:T(8,128)(2,1)S(1)}, bf16[240,384]{1,0:T(8,128)(2,1)S(1)}, u32[]{:S(2)}, u32[]{:S(2)}) collective-permute-start(bf16[240,384]{1,0:T(8,128)(2,1)S(1)} %get-tuple-element.110.refs_12_.refs_0_.refs_7_), channel_id=1, source_target_pairs={{0,1},{1,0},{2,3},{3,2},{4,5},{5,4},{6,7},{7,6},{8,9},{9,8},{10,11... | collective-permute-start | bytes 552968 | tf_op jit(solution)/shard_map/ppermute | solution.py:32
  91.7 5.9 %collective-permute-start.20 = (bf16[240,384]{1,0:T(8,128)(2,1)S(1)}, bf16[240,384]{1,0:T(8,128)(2,1)S(1)}, u32[]{:S(2)}, u32[]{:S(2)}) collective-permute-start(bf16[240,384]{1,0:T(8,128)(2,1)S(1)} %get-tuple-element.110.refs_12_.refs_0_.refs_7_), channel_id=1, source_target_pairs={{1,2},{2,1},{0,4},{3,7},{5,6},{6,5},{4,0},{7,3},{9,10},{10,9},{8,1... | collective-permute-start | bytes 552968 | tf_op jit(solution)/shard_map/ppermute | solution.py:506
  95.1 8.2 %collective-permute-start.50 = (bf16[240,384]{1,0:T(8,128)(2,1)S(1)}, bf16[240,384]{1,0:T(8,128)(2,1)S(1)}, u32[]{:S(2)}, u32[]{:S(2)}) collective-permute-start(bf16[240,384]{1,0:T(8,128)(2,1)S(1)} %broadcast_select_fusion.3), channel_id=1, source_target_pairs={{0,1},{1,0},{2,3},{3,2},{4,5},{5,4},{6,7},{7,6},{8,9},{9,8},{10,11... | collective-permute-start | bytes 552968 | tf_op jit(solution)/shard_map/ppermute | solution.py:32
  97.6 6.0 %collective-permute-start.51 = (bf16[240,384]{1,0:T(8,128)(2,1)S(1)}, bf16[240,384]{1,0:T(8,128)(2,1)S(1)}, u32[]{:S(2)}, u32[]{:S(2)}) collective-permute-start(bf16[240,384]{1,0:T(8,128)(2,1)S(1)} %collective-permute-done.48.refs_7_.refs_2_), channel_id=1, source_target_pairs={{1,2},{2,1},{0,4},{3,7},{5,6},{6,5},{4,0},{7,3},{9,10},{10,9},{8,1... | collective-permute-start | bytes 552968 | tf_op jit(solution)/shard_map/ppermute | solution.py:506
  97.6 11.5 %collective-permute-start.21 = (bf16[240,384]{1,0:T(8,128)(2,1)S(1)}, bf16[240,384]{1,0:T(8,128)(2,1)S(1)}, u32[]{:S(2)}, u32[]{:S(2)}) collective-permute-start(bf16[240,384]{1,0:T(8,128)(2,1)S(1)} %broadcast_select_fusion.9), channel_id=1, source_target_pairs={{0,1},{1,0},{2,3},{3,2},{4,5},{5,4},{6,7},{7,6},{8,9},{9,8},{10,11... | collective-permute-start | bytes 552968 | tf_op jit(solution)/shard_map/ppermute | solution.py:32
  99.3 7.6 %collective-permute-start.25 = (bf16[240,384]{1,0:T(8,128)(2,1)S(1)}, bf16[240,384]{1,0:T(8,128)(2,1)S(1)}, u32[]{:S(2)}, u32[]{:S(2)}) collective-permute-start(bf16[240,384]{1,0:T(8,128)(2,1)S(1)} %collective-permute-done.24.refs_13_.refs_8_), channel_id=1, source_target_pairs={{1,2},{2,1},{0,4},{3,7},{5,6},{6,5},{4,0},{7,3},{9,10},{10,9},{8,1... | collective-permute-start | bytes 552968 | tf_op jit(solution)/shard_map/ppermute | solution.py:506
  103.3 5.9 %collective-permute-start.53 = (bf16[240,384]{1,0:T(8,128)(2,1)S(1)}, bf16[240,384]{1,0:T(8,128)(2,1)S(1)}, u32[]{:S(2)}, u32[]{:S(2)}) collective-permute-start(bf16[240,384]{1,0:T(8,128)(2,1)S(1)} %shard_map.137), channel_id=1, source_target_pairs={{1,2},{2,1},{0,4},{3,7},{5,6},{6,5},{4,0},{7,3},{9,10},{10,9},{8,1... | collective-permute-start | bytes 552968 | tf_op jit(solution)/shard_map/ppermute | solution.py:506
  103.6 10.4 %collective-permute-start.52 = (bf16[240,384]{1,0:T(8,128)(2,1)S(1)}, bf16[240,384]{1,0:T(8,128)(2,1)S(1)}, u32[]{:S(2)}, u32[]{:S(2)}) collective-permute-start(bf16[240,384]{1,0:T(8,128)(2,1)S(1)} %broadcast_select_fusion.2), channel_id=1, source_target_pairs={{0,1},{1,0},{2,3},{3,2},{4,5},{5,4},{6,7},{7,6},{8,9},{9,8},{10,11... | collective-permute-start | bytes 552968 | tf_op jit(solution)/shard_map/ppermute | solution.py:32
  106.9 9.5 %collective-permute-start.26 = (bf16[240,384]{1,0:T(8,128)(2,1)S(1)}, bf16[240,384]{1,0:T(8,128)(2,1)S(1)}, u32[]{:S(2)}, u32[]{:S(2)}) collective-permute-start(bf16[240,384]{1,0:T(8,128)(2,1)S(1)} %broadcast_select_fusion.8), channel_id=1, source_target_pairs={{0,1},{1,0},{2,3},{3,2},{4,5},{5,4},{6,7},{7,6},{8,9},{9,8},{10,11... | collective-permute-start | bytes 552968 | tf_op jit(solution)/shard_map/ppermute | solution.py:32
  109.2 7.4 %collective-permute-start.22 = (bf16[240,384]{1,0:T(8,128)(2,1)S(1)}, bf16[240,384]{1,0:T(8,128)(2,1)S(1)}, u32[]{:S(2)}, u32[]{:S(2)}) collective-permute-start(bf16[240,384]{1,0:T(8,128)(2,1)S(1)} %shard_map.127), channel_id=1, source_target_pairs={{1,2},{2,1},{0,4},{3,7},{5,6},{6,5},{4,0},{7,3},{9,10},{10,9},{8,1... | collective-permute-start | bytes 552968 | tf_op jit(solution)/shard_map/ppermute | solution.py:506
  109.3 13.3 %collective-permute-start.54 = (bf16[240,384]{1,0:T(8,128)(2,1)S(1)}, bf16[240,384]{1,0:T(8,128)(2,1)S(1)}, u32[]{:S(2)}, u32[]{:S(2)}) collective-permute-start(bf16[240,384]{1,0:T(8,128)(2,1)S(1)} %fusion.7), channel_id=1, source_target_pairs={{0,1},{1,0},{2,3},{3,2},{4,5},{5,4},{6,7},{7,6},{8,9},{9,8},{10,11... | collective-permute-start | bytes 552968 | tf_op jit(solution)/shard_map/ppermute | solution.py:32
  114.1 8.6 %collective-permute-start.55 = (bf16[240,384]{1,0:T(8,128)(2,1)S(1)}, bf16[240,384]{1,0:T(8,128)(2,1)S(1)}, u32[]{:S(2)}, u32[]{:S(2)}) collective-permute-start(bf16[240,384]{1,0:T(8,128)(2,1)S(1)} %fusion.15), channel_id=1, source_target_pairs={{1,2},{2,1},{0,4},{3,7},{5,6},{6,5},{4,0},{7,3},{9,10},{10,9},{8,1... | collective-permute-start | bytes 552968 | tf_op jit(solution)/shard_map/ppermute | solution.py:506
  116.5 7.7 %collective-permute-start.27 = (bf16[240,384]{1,0:T(8,128)(2,1)S(1)}, bf16[240,384]{1,0:T(8,128)(2,1)S(1)}, u32[]{:S(2)}, u32[]{:S(2)}) collective-permute-start(bf16[240,384]{1,0:T(8,128)(2,1)S(1)} %fusion.11), channel_id=1, source_target_pairs={{1,2},{2,1},{0,4},{3,7},{5,6},{6,5},{4,0},{7,3},{9,10},{10,9},{8,1... | collective-permute-start | bytes 552968 | tf_op jit(solution)/shard_map/ppermute | solution.py:506
  116.6 7.5 %collective-permute-start.23 = (bf16[240,384]{1,0:T(8,128)(2,1)S(1)}, bf16[240,384]{1,0:T(8,128)(2,1)S(1)}, u32[]{:S(2)}, u32[]{:S(2)}) collective-permute-start(bf16[240,384]{1,0:T(8,128)(2,1)S(1)} %fusion.3), channel_id=1, source_target_pairs={{0,1},{1,0},{2,3},{3,2},{4,5},{5,4},{6,7},{7,6},{8,9},{9,8},{10,11... | collective-permute-start | bytes 552968 | tf_op jit(solution)/shard_map/ppermute | solution.py:32
  122.9 8.2 %collective-permute-start.56 = (bf16[240,384]{1,0:T(8,128)(2,1)S(1)}, bf16[240,384]{1,0:T(8,128)(2,1)S(1)}, u32[]{:S(2)}, u32[]{:S(2)}) collective-permute-start(bf16[240,384]{1,0:T(8,128)(2,1)S(1)} %get-tuple-element.149.refs_6_.refs_1_), channel_id=1, source_target_pairs={{0,1},{1,0},{2,3},{3,2},{4,5},{5,4},{6,7},{7,6},{8,9},{9,8},{10,11... | collective-permute-start | bytes 552968 | tf_op jit(solution)/shard_map/ppermute | solution.py:32
  124.3 10.0 %collective-permute-start.32 = (bf16[240,384]{1,0:T(8,128)(2,1)S(1)}, bf16[240,384]{1,0:T(8,128)(2,1)S(1)}, u32[]{:S(2)}, u32[]{:S(2)}) collective-permute-start(bf16[240,384]{1,0:T(8,128)(2,1)S(1)} %get-tuple-element.119.refs_12_.refs_0_.refs_7_), channel_id=1, source_target_pairs={{0,1},{1,0},{2,3},{3,2},{4,5},{5,4},{6,7},{7,6},{8,9},{9,8},{10,11... | collective-permute-start | bytes 552968 | tf_op jit(solution)/shard_map/ppermute | solution.py:32
  125.2 5.9 %collective-permute-start.28 = (bf16[240,384]{1,0:T(8,128)(2,1)S(1)}, bf16[240,384]{1,0:T(8,128)(2,1)S(1)}, u32[]{:S(2)}, u32[]{:S(2)}) collective-permute-start(bf16[240,384]{1,0:T(8,128)(2,1)S(1)} %get-tuple-element.119.refs_12_.refs_0_.refs_7_), channel_id=1, source_target_pairs={{1,2},{2,1},{0,4},{3,7},{5,6},{6,5},{4,0},{7,3},{9,10},{10,9},{8,1... | collective-permute-start | bytes 552968 | tf_op jit(solution)/shard_map/ppermute | solution.py:506
  128.6 10.2 %collective-permute-start.58 = (bf16[240,384]{1,0:T(8,128)(2,1)S(1)}, bf16[240,384]{1,0:T(8,128)(2,1)S(1)}, u32[]{:S(2)}, u32[]{:S(2)}) collective-permute-start(bf16[240,384]{1,0:T(8,128)(2,1)S(1)} %broadcast_select_fusion.1), channel_id=1, source_target_pairs={{0,1},{1,0},{2,3},{3,2},{4,5},{5,4},{6,7},{7,6},{8,9},{9,8},{10,11... | collective-permute-start | bytes 552968 | tf_op jit(solution)/shard_map/ppermute | solution.py:32
  131.1 11.6 %collective-permute-start.29 = (bf16[240,384]{1,0:T(8,128)(2,1)S(1)}, bf16[240,384]{1,0:T(8,128)(2,1)S(1)}, u32[]{:S(2)}, u32[]{:S(2)}) collective-permute-start(bf16[240,384]{1,0:T(8,128)(2,1)S(1)} %broadcast_select_fusion.7), channel_id=1, source_target_pairs={{0,1},{1,0},{2,3},{3,2},{4,5},{5,4},{6,7},{7,6},{8,9},{9,8},{10,11... | collective-permute-start | bytes 552968 | tf_op jit(solution)/shard_map/ppermute | solution.py:32
  134.4 11.8 %collective-permute-start.60 = (bf16[240,384]{1,0:T(8,128)(2,1)S(1)}, bf16[240,384]{1,0:T(8,128)(2,1)S(1)}, u32[]{:S(2)}, u32[]{:S(2)}) collective-permute-start(bf16[240,384]{1,0:T(8,128)(2,1)S(1)} %broadcast_select_fusion), channel_id=1, source_target_pairs={{0,1},{1,0},{2,3},{3,2},{4,5},{5,4},{6,7},{7,6},{8,9},{9,8},{10,11... | collective-permute-start | bytes 552968 | tf_op jit(solution)/shard_map/ppermute | solution.py:32
  138.9 7.4 %collective-permute-start.61 = (bf16[240,384]{1,0:T(8,128)(2,1)S(1)}, bf16[240,384]{1,0:T(8,128)(2,1)S(1)}, u32[]{:S(2)}, u32[]{:S(2)}) collective-permute-start(bf16[240,384]{1,0:T(8,128)(2,1)S(1)} %shard_map.141), channel_id=1, source_target_pairs={{1,2},{2,1},{0,4},{3,7},{5,6},{6,5},{4,0},{7,3},{9,10},{10,9},{8,1... | collective-permute-start | bytes 552968 | tf_op jit(solution)/shard_map/ppermute | solution.py:506
  139.1 10.7 %collective-permute-start.34 = (bf16[240,384]{1,0:T(8,128)(2,1)S(1)}, bf16[240,384]{1,0:T(8,128)(2,1)S(1)}, u32[]{:S(2)}, u32[]{:S(2)}) collective-permute-start(bf16[240,384]{1,0:T(8,128)(2,1)S(1)} %broadcast_select_fusion.6), channel_id=1, source_target_pairs={{0,1},{1,0},{2,3},{3,2},{4,5},{5,4},{6,7},{7,6},{8,9},{9,8},{10,11... | collective-permute-start | bytes 552968 | tf_op jit(solution)/shard_map/ppermute | solution.py:32
  142.8 7.2 %collective-permute-start.30 = (bf16[240,384]{1,0:T(8,128)(2,1)S(1)}, bf16[240,384]{1,0:T(8,128)(2,1)S(1)}, u32[]{:S(2)}, u32[]{:S(2)}) collective-permute-start(bf16[240,384]{1,0:T(8,128)(2,1)S(1)} %shard_map.129), channel_id=1, source_target_pairs={{1,2},{2,1},{0,4},{3,7},{5,6},{6,5},{4,0},{7,3},{9,10},{10,9},{8,1... | collective-permute-start | bytes 552968 | tf_op jit(solution)/shard_map/ppermute | solution.py:506
  146.3 8.4 %collective-permute-start.63 = (bf16[240,384]{1,0:T(8,128)(2,1)S(1)}, bf16[240,384]{1,0:T(8,128)(2,1)S(1)}, u32[]{:S(2)}, u32[]{:S(2)}) collective-permute-start(bf16[240,384]{1,0:T(8,128)(2,1)S(1)} %fusion.16), channel_id=1, source_target_pairs={{1,2},{2,1},{0,4},{3,7},{5,6},{6,5},{4,0},{7,3},{9,10},{10,9},{8,1... | collective-permute-start | bytes 552968 | tf_op jit(solution)/shard_map/ppermute | solution.py:506
  146.4 8.3 %collective-permute-start.62 = (bf16[240,384]{1,0:T(8,128)(2,1)S(1)}, bf16[240,384]{1,0:T(8,128)(2,1)S(1)}, u32[]{:S(2)}, u32[]{:S(2)}) collective-permute-start(bf16[240,384]{1,0:T(8,128)(2,1)S(1)} %fusion.8), channel_id=1, source_target_pairs={{0,1},{1,0},{2,3},{3,2},{4,5},{5,4},{6,7},{7,6},{8,9},{9,8},{10,11... | collective-permute-start | bytes 552968 | tf_op jit(solution)/shard_map/ppermute | solution.py:32
  150.0 7.6 %collective-permute-start.31 = (bf16[240,384]{1,0:T(8,128)(2,1)S(1)}, bf16[240,384]{1,0:T(8,128)(2,1)S(1)}, u32[]{:S(2)}, u32[]{:S(2)}) collective-permute-start(bf16[240,384]{1,0:T(8,128)(2,1)S(1)} %fusion.4), channel_id=1, source_target_pairs={{0,1},{1,0},{2,3},{3,2},{4,5},{5,4},{6,7},{7,6},{8,9},{9,8},{10,11... | collective-permute-start | bytes 552968 | tf_op jit(solution)/shard_map/ppermute | solution.py:32
  158.4 7.8 %collective-permute-start.69 = (bf16[256,384]{1,0:T(8,128)(2,1)S(1)}, bf16[256,384]{1,0:T(8,128)(2,1)S(1)}, u32[]{:S(2)}, u32[]{:S(2)}) collective-permute-start(bf16[256,384]{1,0:T(8,128)(2,1)S(1)} %get-tuple-element.162.refs_0_.refs_13_.refs_7_), channel_id=1, source_target_pairs={{0,1},{1,0},{2,3},{3,2},{4,5},{5,4},{6,7},{7,6},{8,9},{9,8},{10,11... | collective-permute-start | bytes 589832 | tf_op jit(solution)/shard_map/ppermute | solution.py:32
  159.1 9.9 %collective-permute-start.64 = (bf16[240,384]{1,0:T(8,128)(2,1)S(1)}, bf16[240,384]{1,0:T(8,128)(2,1)S(1)}, u32[]{:S(2)}, u32[]{:S(2)}) collective-permute-start(bf16[240,384]{1,0:T(8,128)(2,1)S(1)} %get-tuple-element.169.refs_7_.refs_1_), channel_id=1, source_target_pairs={{0,1},{1,0},{2,3},{3,2},{4,5},{5,4},{6,7},{7,6},{8,9},{9,8},{10,11... | collective-permute-start | bytes 552968 | tf_op jit(solution)/shard_map/ppermute | solution.py:32
  160.4 8.6 %collective-permute-start.70 = (bf16[256,384]{1,0:T(8,128)(2,1)S(1)}, bf16[256,384]{1,0:T(8,128)(2,1)S(1)}, u32[]{:S(2)}, u32[]{:S(2)}) collective-permute-start(bf16[256,384]{1,0:T(8,128)(2,1)S(1)} %get-tuple-element.162.refs_0_.refs_13_.refs_7_), channel_id=1, source_target_pairs={{1,2},{2,1},{0,4},{3,7},{5,6},{6,5},{4,0},{7,3},{9,10},{10,9},{8,1... | collective-permute-start | bytes 589832 | tf_op jit(solution)/shard_map/ppermute | solution.py:506
  166.2 8.6 %collective-permute-start.65 = (bf16[240,384]{1,0:T(8,128)(2,1)S(1)}, bf16[240,384]{1,0:T(8,128)(2,1)S(1)}, u32[]{:S(2)}, u32[]{:S(2)}) collective-permute-start(bf16[240,384]{1,0:T(8,128)(2,1)S(1)} %get-tuple-element.169.refs_7_.refs_1_), channel_id=1, source_target_pairs={{1,2},{2,1},{0,4},{3,7},{5,6},{6,5},{4,0},{7,3},{9,10},{10,9},{8,1... | collective-permute-start | bytes 552968 | tf_op jit(solution)/shard_map/ppermute | solution.py:506
  169.0 8.0 %collective-permute-start.67 = (bf16[240,384]{1,0:T(8,128)(2,1)S(1)}, bf16[240,384]{1,0:T(8,128)(2,1)S(1)}, u32[]{:S(2)}, u32[]{:S(2)}) collective-permute-start(bf16[240,384]{1,0:T(8,128)(2,1)S(1)} %collective-permute-done.64.refs_8_.refs_2_), channel_id=1, source_target_pairs={{1,2},{2,1},{0,4},{3,7},{5,6},{6,5},{4,0},{7,3},{9,10},{10,9},{8,1... | collective-permute-start | bytes 552968 | tf_op jit(solution)/shard_map/ppermute | solution.py:506
  169.0 15.9 %collective-permute-start.71 = (bf16[256,384]{1,0:T(8,128)(2,1)S(1)}, bf16[256,384]{1,0:T(8,128)(2,1)S(1)}, u32[]{:S(2)}, u32[]{:S(2)}) collective-permute-start(bf16[256,384]{1,0:T(8,128)(2,1)S(1)} %collective-permute-done.70.refs_16_.refs_10_), channel_id=1, source_target_pairs={{0,1},{1,0},{2,3},{3,2},{4,5},{5,4},{6,7},{7,6},{8,9},{9,8},{10,11... | collective-permute-start | bytes 589832 | tf_op jit(solution)/shard_map/ppermute | solution.py:32
  170.0 18.5 %collective-permute-start.73 = (bf16[256,384]{1,0:T(8,128)(2,1)S(1)}, bf16[256,384]{1,0:T(8,128)(2,1)S(1)}, u32[]{:S(2)}, u32[]{:S(2)}) collective-permute-start(bf16[256,384]{1,0:T(8,128)(2,1)S(1)} %collective-permute-done.72.refs_18_.refs_12_), channel_id=1, source_target_pairs={{0,1},{1,0},{2,3},{3,2},{4,5},{5,4},{6,7},{7,6},{8,9},{9,8},{10,11... | collective-permute-start | bytes 589832 | tf_op jit(solution)/shard_map/ppermute | solution.py:32
  174.8 10.1 %collective-permute-start.66 = (bf16[240,384]{1,0:T(8,128)(2,1)S(1)}, bf16[240,384]{1,0:T(8,128)(2,1)S(1)}, u32[]{:S(2)}, u32[]{:S(2)}) collective-permute-start(bf16[240,384]{1,0:T(8,128)(2,1)S(1)} %collective-permute-done.65.refs_10_.refs_4_), channel_id=1, source_target_pairs={{0,1},{1,0},{2,3},{3,2},{4,5},{5,4},{6,7},{7,6},{8,9},{9,8},{10,11... | collective-permute-start | bytes 552968 | tf_op jit(solution)/shard_map/ppermute | solution.py:32
  177.0 11.5 %collective-permute-start.68 = (bf16[240,384]{1,0:T(8,128)(2,1)S(1)}, bf16[240,384]{1,0:T(8,128)(2,1)S(1)}, u32[]{:S(2)}, u32[]{:S(2)}) collective-permute-start(bf16[240,384]{1,0:T(8,128)(2,1)S(1)} %collective-permute-done.67.refs_12_.refs_6_), channel_id=1, source_target_pairs={{0,1},{1,0},{2,3},{3,2},{4,5},{5,4},{6,7},{7,6},{8,9},{9,8},{10,11... | collective-permute-start | bytes 552968 | tf_op jit(solution)/shard_map/ppermute | solution.py:32
  196.2 8.1 %collective-permute-start.75 = (bf16[2,128,512]{2,1,0:T(8,128)(2,1)S(1)}, bf16[2,128,512]{2,1,0:T(8,128)(2,1)S(1)}, u32[]{:S(2)}, u32[]{:S(2)}) collective-permute-start(bf16[2,128,512]{2,1,0:T(8,128)(2,1)S(1)} %slice_bitcast_fusion), channel_id=1, source_target_pairs={{0,8},{4,12},{8,0},{12,4},{1,9},{5,13},{9,1},{13,5},{2,10},{6,14},... | collective-permute-start | bytes 786440 | tf_op jit(solution)/shard_map/ppermute | solution.py:32
  (16 other events, 59.8 us)

commit v7 on v6

--- a/solution.py
+++ b/solution.py
@@ -69,9 +69,10 @@
     n = len(routes)
     choose, tokens = routes[0].shape[0] // 2, routes[0].shape[1]
     which = (scal[2 * n] + expert).astype(F32)
-    hits = [route[0:choose, :] == which for route in routes]
+    routes = [route[...] for route in routes]
+    hits = [route[0:choose] == which for route in routes]
     weights = [
-        jnp.sum(jnp.where(hit, route[choose:, :], 0.0), axis=0, keepdims=True)
+        jnp.sum(jnp.where(hit, route[choose:], 0.0), axis=0, keepdims=True)
         for hit, route in zip(hits, routes)
     ]
     chosen = jnp.concatenate(
@@ -90,50 +91,87 @@
     return pl.ds(pl.multiple_of(position * rows, rows), rows)
 
 
-def weight_copies(expert, weights, held, sems):
-    halves = []
-    for h in range(2):
-        copies = []
-        for k, (source, target) in enumerate(zip(weights, held)):
-            size = target.shape[0 if k == 2 else 1] // 2
-            span = pl.ds(h * size, size)
-            src, dst = (
-                (source.at[expert, span, :], target.at[span, :])
-                if k == 2
-                else (source.at[expert, :, span], target.at[:, span])
-            )
-            copies.append(pltpu.make_async_copy(src, dst, sems.at[h, k]))
-        halves.append(copies)
-    return halves
-
-
-def pre_kernel(n, expert, deps, scal, *refs):
+def weight_copies(expert, half, weights, held, sems):
+    copies = []
+    for k, (source, target) in enumerate(zip(weights, held)):
+        size = target.shape[0 if k == 2 else 1]
+        span = pl.ds(half * size, size)
+        src = source.at[expert, span, :] if k == 2 else source.at[expert, :, span]
+        copies.append(pltpu.make_async_copy(src, target, sems.at[k]))
+    for copy in copies:
+        copy.start()
+    return copies
+
+
+def route_blocks(choose, count, width):
+    wide = max(1, width // count)
+    return [(16 * (b // wide), count * (b % wide)) for b in range(4 * choose // 16)]
+
+
+def pack_kernel(ids, combine, tokens, grads, pack):
+    count, width = tokens.shape
+    choose = ids.shape[0]
+    pack[0:count, :] = tokens[...]
+    pack[count : 2 * count, :] = grads[...]
+    lines = [ids[...].astype(F32)] + [part.astype(F32) for part in thirds(combine[...])]
+    lines = jnp.concatenate(lines, axis=0).astype(BF16)
+    blocks = route_blocks(choose, count, width)
+    pack[2 * count :, :] = jnp.zeros((pack.shape[0] - 2 * count, width), BF16)
+    for b, (row, lane) in enumerate(blocks):
+        pack[2 * count + row : 2 * count + row + 16, lane : lane + count] = lines[16 * b : 16 * b + 16]
+
+
+def unpack_route(pack, choose, count):
+    lines = [
+        pack[2 * count + row : 2 * count + row + 16, lane : lane + count]
+        for row, lane in route_blocks(choose, count, pack.shape[1])
+    ]
+    lines = jnp.concatenate(lines, axis=0).astype(F32)
+    ids, high, middle, low = (lines[k * choose : (k + 1) * choose] for k in range(4))
+    return jnp.concatenate([ids, (high + middle) + low], axis=0)
+
+
+def store_parts(outs, arrays):
+    n = len(outs)
+    for p in range(n):
+        rows = arrays[0].shape[0] // n
+        for k, value in enumerate(arrays):
+            outs[p][pl.ds(k * rows, rows), :] = value[p * rows : (p + 1) * rows]
+
+
+def fill_kernel(n, expert, choose, deps, scal, *refs):
     refs = refs[deps:]
-    routes, packs, refs = refs[:n], refs[n : 2 * n], refs[2 * n :]
-    weights, (in_ref, cot_ref, *refs) = refs[:3], refs[3:]
-    outs, (token, gw, uw, dw, sems) = refs[: 2 * n], refs[2 * n :]
-    rows, tile = in_ref.shape[0] // n, gw.shape[1] // 2
-    copies = weight_copies(expert, weights, (gw, uw, dw), sems)
-    for group in copies:
-        for copy in group:
-            copy.start()
+    packs, weights, (in_ref, cot_ref, *refs) = refs[:n], refs[n : n + 3], refs[n + 3 :]
+    outs, (token, routes, gw, uw, dw, sems) = refs[:n], refs[n:]
+    copies = weight_copies(expert, 0, weights, (gw, uw, dw), sems)
     token[...] = jnp.zeros_like(token)
-    for k, (position, weight, hit) in enumerate(routing(scal, routes, expert, rows)):
+    rows, count = in_ref.shape[0] // n, routes.shape[2]
+    found = [unpack_route(pack, choose, count) for pack in packs]
+    for k in range(n):
+        routes[k] = found[k]
+    for k, (position, weight, hit) in enumerate(routing(scal, found, expert, rows)):
         pick = hit.astype(F32).astype(BF16)
         span = span_of(position, rows)
-        in_ref[span, :] = dot(pick, packs[k][0]).astype(BF16)
+        in_ref[span, :] = dot(pick, packs[k][0:count, :]).astype(BF16)
         scale = jnp.sum(jnp.where(hit, weight, 0.0), axis=1, keepdims=True)
-        cot_ref[span, :] = (dot(pick, packs[k][1]) * scale).astype(BF16)
-    for h in range(2):
-        for copy in copies[h]:
-            copy.wait()
-        part = slice(h * tile, (h + 1) * tile)
-        gate = dot(in_ref[...], gw[:, part]).astype(BF16)
-        up = dot(in_ref[...], uw[:, part]).astype(BF16)
-        back = dot(cot_ref[...], dw[part, :], ((1,), (1,))).astype(BF16)
-        for p in range(n):
-            for k, value in enumerate((gate, up, back)):
-                outs[h * n + p][pl.ds(k * rows, rows), :] = value[p * rows : (p + 1) * rows]
+        cot_ref[span, :] = (dot(pick, packs[k][count : 2 * count, :]) * scale).astype(BF16)
+    for copy in copies:
+        copy.wait()
+    gate, up = dot(in_ref[...], gw[...]), dot(in_ref[...], uw[...])
+    back = dot(cot_ref[...], dw[...], ((1,), (1,)))
+    store_parts(outs, [x.astype(BF16) for x in (gate, up, back)])
+
+
+def more_kernel(n, expert, deps, *refs):
+    in_ref, cot_ref, *refs = refs[deps:]
+    weights, outs, (token, gw, uw, dw, sems) = refs[:3], refs[3 : 3 + n], refs[3 + n :]
+    copies = weight_copies(expert, 1, weights, (gw, uw, dw), sems)
+    token[...] = jnp.zeros_like(token)
+    for copy in copies:
+        copy.wait()
+    gate, up = dot(in_ref[...], gw[...]), dot(in_ref[...], uw[...])
+    back = dot(cot_ref[...], dw[...], ((1,), (1,)))
+    store_parts(outs, [x.astype(BF16) for x in (gate, up, back)])
 
 
 def thirds(value):
@@ -175,13 +213,6 @@
         out[3 * rows :, 0:lanes] = jnp.concatenate(lines, axis=0).astype(BF16)
 
 
-def pack_kernel(ids, combine, tokens, grads, pack, route):
-    pack[0] = tokens[...]
-    pack[1] = grads[...]
-    route[0 : ids.shape[0], :] = ids[...].astype(F32)
-    route[ids.shape[0] :, :] = combine[...]
-
-
 def add_kernel(deps, *refs):
     a, b, out = refs[deps:]
     out[...] = (a[...].astype(F32) + b[...].astype(F32)).astype(out.dtype)
@@ -202,46 +233,48 @@
 
 
 def split_pieces(refs, sizes):
-    halves, at = [], 0
-    for _ in range(2):
-        pieces = [refs[at : at + 1]]
-        at += 1
-        for size in sizes:
-            pieces.append(refs[at : at + size])
-            at += size
-        halves.append(pieces)
-    return halves, refs[at:]
+    pieces, at = [refs[0:1]], 1
+    for size in sizes:
+        pieces.append(refs[at : at + size])
+        at += size
+    return pieces, refs[at:]
+
+
+def terms(scal, n, pieces, copies, gw, uw, dw):
+    hidden, gate, up = (load_rows(scal, n, k, pieces) for k in range(3))
+    for copy in copies:
+        copy.wait()
+    back = dot(gate, gw[...], ((1,), (1,))) + dot(up, uw[...], ((1,), (1,)))
+    return dot(hidden, dw[...]), back
+
+
+def half_kernel(n, expert, sizes, deps, scal, *refs):
+    pieces, refs = split_pieces(refs[deps:], sizes)
+    weights, (eo, idl, token, gw, uw, dw, sems) = refs[:3], refs[3:]
+    copies = weight_copies(expert, 0, weights, (gw, uw, dw), sems)
+    token[...] = jnp.zeros_like(token)
+    eo[...], idl[...] = terms(scal, n, pieces, copies, gw, uw, dw)
 
 
 def out_kernel(n, expert, has_prev, last, sizes, deps, scal, *refs):
     refs = refs[deps:]
-    routes, refs = refs[:n], refs[n:]
+    routes, eo, idl, refs = refs[0], refs[1], refs[2], refs[3:]
+    routes = [routes.at[k] for k in range(n)]
     if has_prev:
         prev, refs = refs[:2], refs[2:]
-    halves, refs = split_pieces(refs, sizes)
+    pieces, refs = split_pieces(refs, sizes)
     weights, (near, far, token, *refs) = refs[:3], refs[3:]
     if last:
         near_p, far_p, *refs, held = refs
     gw, uw, dw, sems, eo_ref, idl_ref = refs
-    copies = weight_copies(expert, weights, (gw, uw, dw), sems)
-    for group in copies:
-        for copy in group:
-            copy.start()
+    copies = weight_copies(expert, 1, weights, (gw, uw, dw), sems)
     token[...] = jnp.zeros_like(token)
-    spots = routing(scal, routes, expert, halves[0][0][0].shape[0] // 48 * 16)
+    rows = eo.shape[0] // n
+    spots = routing(scal, routes, expert, rows)
     if last:
-        send_products(scal, routes, expert + 1, halves[1], held, near_p, far_p)
-    tile = gw.shape[1] // 2
-    eo, idl = 0.0, 0.0
-    for h in range(2):
-        for copy in copies[h]:
-            copy.wait()
-        part = slice(h * tile, (h + 1) * tile)
-        eo = eo + dot(load_rows(scal, n, 0, halves[h]), dw[part, :])
-        idl = idl + dot(load_rows(scal, n, 1, halves[h]), gw[:, part], ((1,), (1,)))
-        idl = idl + dot(load_rows(scal, n, 2, halves[h]), uw[:, part], ((1,), (1,)))
-    rows = eo.shape[0] // n
-    eo_ref[...], idl_ref[...] = eo.astype(BF16), idl.astype(BF16)
+        send_products(scal, routes, expert + 1, pieces, held, near_p, far_p)
+    layer, back = terms(scal, n, pieces, copies, gw, uw, dw)
+    eo_ref[...], idl_ref[...] = (eo[...] + layer).astype(BF16), (idl[...] + back).astype(BF16)
     for k, (position, weight, hit) in enumerate(spots):
         pick = hit.astype(F32)
         scaled = (pick * weight).astype(BF16)
@@ -257,20 +290,14 @@
 
 
 def grad_kernel(n, has_prev, sizes, deps, scal, in_ref, cot_ref, *refs):
-    refs = refs[deps:]
-    halves, refs = split_pieces(refs, sizes)
+    pieces, refs = split_pieces(refs[deps:], sizes)
     if has_prev:
         refs = refs[3:]
     gg, ug, dg, token = refs
-    step = pl.program_id(0)
     token[...] = jnp.zeros_like(token)
-    for h in range(2):
-
-        @pl.when(step == h)
-        def _():
-            gg[0] = dot(in_ref[...], load_rows(scal, n, 1, halves[h]), ((0,), (0,))).astype(BF16)
-            ug[0] = dot(in_ref[...], load_rows(scal, n, 2, halves[h]), ((0,), (0,))).astype(BF16)
-            dg[0] = dot(load_rows(scal, n, 0, halves[h]), cot_ref[...], ((0,), (0,))).astype(BF16)
+    gg[0] = dot(in_ref[...], load_rows(scal, n, 1, pieces), ((0,), (0,))).astype(BF16)
+    ug[0] = dot(in_ref[...], load_rows(scal, n, 2, pieces), ((0,), (0,))).astype(BF16)
+    dg[0] = dot(load_rows(scal, n, 0, pieces), cot_ref[...], ((0,), (0,))).astype(BF16)
 
 
 def send_products(scal, routes, local, pieces, held, near, far):
@@ -374,17 +401,19 @@
         ]
         return found + [across.send(piece, swap) for piece in found]
 
-    pack, route = call(
+    route_rows = 16 + max(row for row, _ in route_blocks(choose, count, width))
+    pack_shape = (2 * count + route_rows, width)
+    pack = call(
         pack_kernel,
         1,
         [spec_of(ids_t), spec_of(combine_t), spec_of(tokens), spec_of(out_grad)],
-        [whole_spec((2, count, width)), whole_spec((2 * choose, count))],
-        [like((2, count, width)), like((2 * choose, count), F32)],
+        whole_spec(pack_shape),
+        like(pack_shape),
         count * width,
         8 * count * width,
     )(*(in_hbm(x) for x in (ids_t, combine_t, tokens, out_grad)))
-    routes, packs = gather_blocks(route), gather_blocks(pack)
-    route_specs, pack_specs = [spec_of(x) for x in routes], [spec_of(x) for x in packs]
+    packs = gather_blocks(pack)
+    route_shape = (n, 2 * choose, count)
 
     mac = all_rows * width * hidden
     weight_bytes = 2 * width * hidden
@@ -395,26 +424,38 @@
     slot_shape = (all_rows, width)
 
     weights = [in_hbm(w) for w in (gate_weight, up_weight, down_weight)]
-    held_weights = [pltpu.VMEM(w.shape[1:], BF16) for w in weights] + [
-        pltpu.SemaphoreType.DMA((2, 3))
-    ]
-
-    def grad_specs(e):
-        wide = pl.BlockSpec((1, width, tile), lambda g: (e, 0, g))
-        return [wide, wide, pl.BlockSpec((1, tile, width), lambda g: (e, g, 0))]
-
-    def pre(e, deps):
-        inputs, cot, *parts, token = call(
-            functools.partial(pre_kernel, n, e, len(deps)),
+    held_weights = [pltpu.VMEM(shape, BF16) for shape in ((width, tile), (width, tile), (tile, width))]
+    held_weights += [pltpu.SemaphoreType.DMA((3,))]
+
+    def fill(e, deps):
+        inputs, cot, *parts, token, routes = call(
+            functools.partial(fill_kernel, n, e, choose, len(deps)),
             1,
-            [SMEM_SPEC] + [ANY_SPEC] * len(deps) + route_specs + pack_specs + [HBM_SPEC] * 3,
-            [whole_spec(slot_shape)] * 2 + [whole_spec(piece_shape)] * (2 * n) + [whole_spec(TOKEN)],
-            [like(slot_shape)] * 2 + [like(piece_shape)] * (2 * n) + [like(TOKEN, F32)],
-            6 * mac,
-            3 * weight_bytes + 2 * n * piece_bytes,
+            [SMEM_SPEC] + [ANY_SPEC] * len(deps) + [spec_of(x) for x in packs] + [HBM_SPEC] * 3,
+            [whole_spec(slot_shape)] * 2
+            + [whole_spec(piece_shape)] * n
+            + [whole_spec(TOKEN), whole_spec(route_shape)],
+            [like(slot_shape)] * 2
+            + [like(piece_shape)] * n
+            + [like(TOKEN, F32), like(route_shape, F32)],
+            3 * mac,
+            2 * weight_bytes + n * piece_bytes,
             scratch_shapes=held_weights,
-        )(scal, *deps, *routes, *packs, *weights)
-        return (inputs, cot), [parts[:n], parts[n:]], token
+        )(scal, *deps, *packs, *weights)
+        return (inputs, cot), parts, token, routes
+
+    def more(e, slots, deps):
+        *parts, token = call(
+            functools.partial(more_kernel, n, e, len(deps)),
+            1,
+            [ANY_SPEC] * len(deps) + [whole_spec(slot_shape)] * 2 + [HBM_SPEC] * 3,
+            [whole_spec(piece_shape)] * n + [whole_spec(TOKEN)],
+            [like(piece_shape)] * n + [like(TOKEN, F32)],
+            3 * mac,
+            2 * weight_bytes + n * piece_bytes,
+            scratch_shapes=held_weights,
+        )(*deps, *slots, *weights)
+        return parts, token
 
     def mid(e, h, totals, products, deps=()):
         others = products if e == local - 1 and h == 1 else []
@@ -442,23 +483,32 @@
             3 * a.size * a.dtype.itemsize,
         )(*deps, a, b)
 
-    def flatten(halves):
-        return [x for pieces in halves for group in pieces for x in group]
-
-    def sizes_of(pieces):
-        return [len(group) for group in pieces[1:]]
-
-    def out(e, halves, prev, deps):
-        flat = flatten(halves)
+    def half(e, pieces, deps):
+        flat = [x for group in pieces for x in group]
+        return call(
+            functools.partial(half_kernel, n, e, [len(g) for g in pieces[1:]], len(deps)),
+            1,
+            [SMEM_SPEC] + [ANY_SPEC] * len(deps) + [spec_of(x) for x in flat] + [HBM_SPEC] * 3,
+            [whole_spec(slot_shape)] * 2 + [whole_spec(TOKEN)],
+            [like(slot_shape, F32)] * 2 + [like(TOKEN, F32)],
+            3 * mac,
+            2 * weight_bytes + len(flat) * piece_bytes,
+            scratch_shapes=held_weights,
+        )(scal, *deps, *flat, *weights)
+
+    def out(e, begun, pieces, prev, deps):
+        flat = [x for group in pieces for x in group]
         last = e == local - 1
-        dense_shape = (chips, experts_all, count)
-        sum_shape = (chips, 2, count, width)
+        dense_shape, sum_shape = (chips, experts_all, count), (chips, 2, count, width)
         return call(
-            functools.partial(out_kernel, n, e, e > 0, last, sizes_of(halves[0]), len(deps)),
+            functools.partial(
+                out_kernel, n, e, e > 0, last, [len(g) for g in pieces[1:]], len(deps)
+            ),
             1,
             [SMEM_SPEC]
             + [ANY_SPEC] * len(deps)
-            + route_specs
+            + [whole_spec(route_shape)]
+            + [whole_spec(slot_shape)] * 2
             + ([whole_spec(sum_shape)] * 2 if e > 0 else [])
             + [spec_of(x) for x in flat]
             + [HBM_SPEC] * 3,
@@ -468,29 +518,32 @@
             [like(sum_shape, BF16 if last else F32)] * 2
             + [like(TOKEN, F32)]
             + ([like(dense_shape, F32)] * 2 if last else []),
-            6 * mac,
-            3 * weight_bytes + len(flat) * piece_bytes,
+            3 * mac,
+            2 * weight_bytes + len(flat) * piece_bytes,
             scratch_shapes=held_weights
             + [pltpu.VMEM(slot_shape, BF16)] * 2
             + ([pltpu.VMEM((n, extra, 128), BF16)] if last else []),
-        )(scal, *deps, *routes, *prev, *flat, *weights)
-
-    def grad(e, slots, halves, prev, deps):
-        flat = flatten(halves)
+        )(scal, *deps, routes, *begun, *prev, *flat, *weights)
+
+    def grad(e, h, slots, pieces, prev, deps):
+        flat = [x for group in pieces for x in group]
         base = 3 + len(deps) + len(flat)
+        wide = pl.BlockSpec((1, width, tile), lambda g: (e, 0, h))
         return call(
-            functools.partial(grad_kernel, n, e > 0, sizes_of(halves[0]), len(deps)),
-            2,
+            functools.partial(
+                grad_kernel, n, len(prev) > 0, [len(g) for g in pieces[1:]], len(deps)
+            ),
+            1,
             [SMEM_SPEC]
             + [whole_spec(slot_shape)] * 2
             + [ANY_SPEC] * len(deps)
             + [spec_of(x) for x in flat]
-            + ([ANY_SPEC] * 3 if e > 0 else []),
-            grad_specs(e) + [whole_spec(TOKEN)],
+            + [ANY_SPEC] * len(prev),
+            [wide, wide, pl.BlockSpec((1, tile, width), lambda g: (e, h, 0)), whole_spec(TOKEN)],
             [like(w.shape) for w in weights] + [like(TOKEN, F32)],
-            6 * mac,
-            3 * weight_bytes + len(flat) * piece_bytes,
-            input_output_aliases={base + k: k for k in range(3)} if e > 0 else {},
+            3 * mac,
+            2 * weight_bytes + len(flat) * piece_bytes,
+            input_output_aliases={base + k: k for k in range(len(prev))},
         )(scal, *slots, *deps, *flat, *prev)
 
     along_z = Line("dp", n, 1)
@@ -518,11 +571,11 @@
 
     if swaps:
         flight, arrived = [None, None], None
-        slots, parts, _ = pre(0, [])
-        grad_token = None
+        slots, x0, _, routes = fill(0, [])
+        parts, grad_token = [x0, more(0, slots, [])[0]], None
         for e in range(local):
-            more = e < local - 1
             first, second, totals, halves = [], [], [], []
+            following, seen = e < local - 1, [[], []]
             for h in range(2):
                 x = parts[h]
                 if e == 0:
@@ -530,36 +583,41 @@
                 else:
                     y, got_a, got_b = flight[h]
                     first.append((outer(jnp.where(at_end, x[3], got_b)), inner(got_a)))
-            if more:
-                begun = pre(e + 1, [first[0][0]] if e == 0 else [flight[1][2]])
+            if following:
+                next_slots, next0, token_0, _ = fill(e + 1, [] if e == 0 else [flight[0][2]])
+                next1, token_1 = more(e + 1, next_slots, [first[0][0] if e == 0 else flight[1][2]])
+                seen = [[token_0], [token_1]]
+            if grad_token is not None:
+                seen[0].append(grad_token)
             for h in range(2):
                 x, (a1, b1) = parts[h], first[h]
-                tokens_seen = [begun[2]] if more and h == 1 else []
-                if grad_token is not None and h == 0:
-                    tokens_seen = [grad_token]
                 send_a2 = x[2] if e == 0 else jnp.where(at_end, x[2], b1)
-                second.append((outer(send_a2), inner(add(x[3], a1, tokens_seen))))
+                second.append((outer(send_a2), inner(add(x[3], a1, seen[h]))))
                 if e > 0:
                     y, got_a, got_b = flight[h]
                     halves.append([(y,), (got_a,), (a1, got_b), (second[h][0], b1)])
+            waits = [[], []]
+            if e > 0:
+                *begun, half_token = half(e - 1, halves[0], [])
+                *sums, out_token = out(e - 1, begun, halves[1], sums, [])
+                waits[0] = [out_token]
             for h in range(2):
                 x, (a2, b2) = parts[h], second[h]
-                a3 = outer(jnp.where(at_end, x[1], add_rounded(x[1], b2)))
+                both = add(x[1], b2, [half_token]) if e > 0 and h == 1 else add_rounded(x[1], b2)
+                a3 = outer(jnp.where(at_end, x[1], both))
                 b3 = inner(unless_end(add_rounded(x[2], a2)))
                 totals.append((x[0], a3, b3))
-            wait = []
-            if e > 0:
-                *sums, out_token = out(e - 1, halves, sums, [])
-                wait = [out_token]
             for h in range(2):
-                y, product = mid(e, h, totals[h], products, wait if h == 0 else [])
+                y, product = mid(e, h, totals[h], products, waits[h])
                 products.append(product)
                 flight[h] = (y, outer(y), inner(y))
-            if e > 0:
-                *grads, grad_token = grad(e - 1, arrived, halves, grads, [flight[1][0]])
+                if e > 0:
+                    *grads, grad_token = grad(e - 1, h, arrived, halves[h], grads, [y])
+                    if h == 0:
+                        waits[1] = [grad_token]
             arrived = slots
-            if more:
-                slots, parts, _ = begun
+            if following:
+                slots, parts = next_slots, [next0, next1]
         halves = []
         for h in range(2):
             y, got_a, got_b = flight[h]
@@ -568,24 +626,29 @@
             halves.append([(y,), (got_a,), (a1, got_b), (a2, b1)])
         wait = [grad_token]
     else:
-        begun = []
+        started = []
         for e in range(local):
-            slots, parts, _ = pre(e, [])
-            begun.append((slots, [(x[0], *along_z.scatter(x, add_rounded)) for x in parts]))
+            slots, x0, _, routes = fill(e, [])
+            parts = [x0, more(e, slots, [])[0]]
+            started.append((slots, [(x[0], *along_z.scatter(x, add_rounded)) for x in parts]))
         for e in range(local):
-            halves, arrived, wait = [], begun[e][0], []
+            halves, arrived, wait = [], started[e][0], []
             for h in range(2):
-                y, product = mid(e, h, begun[e][1][h], products)
+                y, product = mid(e, h, started[e][1][h], products)
                 products.append(product)
                 halves.append([(y,)] + along_z.gather(y))
             if e < local - 1:
-                *sums, _ = out(e, halves, sums, [])
-                *grads, _ = grad(e, arrived, halves, grads, [])
-
-    near, far, _, near_p, far_p = out(local - 1, halves, sums, wait)
+                *begun, _ = half(e, halves[0], [])
+                *sums, _ = out(e, begun, halves[1], sums, [])
+                for h in range(2):
+                    *grads, _ = grad(e, h, arrived, halves[h], grads, [])
+
+    *begun, _ = half(local - 1, halves[0], wait)
+    near, far, _, near_p, far_p = out(local - 1, begun, halves[1], sums, [])
     hop, home = send_home(near, far, add_rounded)
     _, per_expert = send_home(near_p, far_p, lambda a, b: add(a, b, [hop]))
-    *grads, _ = grad(local - 1, arrived, halves, grads, [hop])
+    for h in range(2):
+        *grads, _ = grad(local - 1, h, arrived, halves[h], grads, [hop])
     combine_grad = jnp.sum(jnp.where(named, per_expert[None], 0.0), axis=1) / combine_t
     return (home[0].astype(BF16), home[1].astype(BF16), *grads, combine_grad.T)
 

time: 205 us -> 200 us (0.976)
  waiting for transfers between devices: 62.1 us -> 30.3 us
  Pallas kernels: 46.2 us -> 64.9 us
  starting transfers between devices: 92.5 us -> 100 us
    ppermute x46 -> x43, waiting for transfers between devices: 62 us -> 29.6 us  [send(): return lax.ppermute(value, self.axis, wide)]
    pallas_call x12 -> x24, Pallas kernels: 42.9 us -> 61.5 us  [the longest x8 17.5 us: grad(): call(functools.partial(grad_kernel, n, len(prev) > 0, [len(g) for g in pi...]
    ppermute x46 -> x43, starting transfers between devices: 89.6 us -> 97.4 us  [send(): return lax.ppermute(value, self.axis, wide)]
  transfers between devices with their start and end apart: 78 -> 75, of which waited for: 23 -> 14; matrix products, arithmetic and copies ran while one was open for 1% -> 1% of each run, Pallas kernels for 18% -> 28%
where the time goes in v7:
time: 200 us
  starting transfers between devices  100 us (50%)
  Pallas kernels  64.9 us (32%)
  waiting for transfers between devices  30.3 us (15%)
  other arithmetic  2.07 us (1%)
    ppermute x43, starting transfers between devices, send(): return lax.ppermute(value, self.axis, wide)  97.4 us
    ppermute x43, waiting for transfers between devices, send(): return lax.ppermute(value, self.axis, wide)  29.6 us
    pallas_call x8, Pallas kernels, grad(): call(functools.partial(grad_kernel, n, len(prev) > 0, [len(g) for g in pi...  17.5 us
    pallas_call x4, Pallas kernels, fill(): call(functools.partial(fill_kernel, n, e, choose, len(deps)), 1, [SMEM_SP...  13.2 us
    pallas_call x4, Pallas kernels, out(): call(functools.partial(out_kernel, n, e, e > 0, last, [len(g) for g in pi...  12.6 us
    pallas_call x4, Pallas kernels, half(): call(functools.partial(half_kernel, n, e, [len(g) for g in pieces[1:]], l...  10 us
    pallas_call x4, Pallas kernels, more(): call(functools.partial(more_kernel, n, e, len(deps)), 1, [ANY_SPEC] * len...  8.18 us
  transfers between devices with their start and end apart: 75, of which 14 were waited for; matrix products, arithmetic and copies ran while one was open for 1% of the time, Pallas kernels for 28%

profile of v7, /device:TPU:0, one launch (start us, length us, event | category | flops | bytes accessed | tf_op | source)
XLA Modules:
  0.0 199.8 jit_solution(1851537317049287097)
XLA Ops:
  1.7 3.0 %collective-permute-start = (bf16[272,512]{1,0:T(8,128)(2,1)S(1)}, bf16[272,512]{1,0:T(8,128)(2,1)S(1)}, u32[]{:S(2)}, u32[]{:S(2)}) collective-permute-start(bf16[272,512]{1,0:T(8,128)(2,1)S(1)} %shard_map.118.refs_0_.refs_1_), channel_id=1, source_target_pairs={{0,8},{4,12},{8,0},{12,4},{1,9},{5,13},{9,1},{13,5},{2,10},{6,14},... | collective-permute-start | bytes 835592 | tf_op jit(solution)/shard_map/ppermute | solution.py:32
  4.7 6.7 %collective-permute-done.refs_1_.refs_2_ = bf16[272,512]{1,0:T(8,128)(2,1)S(1)} collective-permute-done((bf16[272,512]{1,0:T(8,128)(2,1)S(1)}, bf16[272,512]{1,0:T(8,128)(2,1)S(1)}, u32[]{:S(2)}, u32[]{:S(2)}) %collective-permute-start) | collective-permute-done | bytes 278560 | tf_op jit(solution)/shard_map/ppermute | solution.py:32
  11.4 1.5 collective-permute-done.2.refs_3_.refs_4_
  12.9 3.2 %shard_map.119 = (bf16[320,512]{1,0:T(8,128)(2,1)S(1)}, bf16[320,512]{1,0:T(8,128)(2,1)S(1)}, bf16[240,384]{1,0:T(8,128)(2,1)S(1)}, bf16[240,384]{1,0:T(8,128)(2...) custom-call(s32[10]{0:T(128)S(1)} %stack.35.scal, ...), custom_call_target="tpu_custom_call" | custom-call | flops 377487360 | bytes 2310144 | tf_op jit(solution)/shard_map/pallas_call | solution.py:431
  16.1 1.9 collective-permute-start.3
  18.2 2.4 %shard_map.125 = (bf16[240,384]{1,0:T(8,128)(2,1)S(1)}, bf16[240,384]{1,0:T(8,128)(2,1)S(1)}, bf16[240,384]{1,0:T(8,128)(2,1)S(1)}, bf16[240,384]{1,0:T(8,128)(2,1)S(1)}, f32[8,128]{1,0:T(8,128)}) custom-call(bf16[320,512]{1,0:T(8,128)(2,1)S(1)} %get-tuple-element.135.refs_0_.in_ref, bf16[320,512]{1,0:T(8,128)(2,1)S(1)} %get-tuple-element.136.refs_1_.cot_ref, ...), custom_call_target="tpu_custom_call" | custom-call | flops 377487360 | bytes 2310144 | tf_op jit(solution)/shard_map/pallas_call | solution.py:448
  20.6 1.9 collective-permute-start.13
  22.7 3.2 %shard_map.120 = (bf16[320,512]{1,0:T(8,128)(2,1)S(1)}, bf16[320,512]{1,0:T(8,128)(2,1)S(1)}, bf16[240,384]{1,0:T(8,128)(2,1)S(1)}, bf16[240,384]{1,0:T(8,128)(2...) custom-call(s32[10]{0:T(128)S(1)} %stack.35.scal, ...), custom_call_target="tpu_custom_call" | custom-call | flops 377487360 | bytes 2310144 | tf_op jit(solution)/shard_map/pallas_call | solution.py:431
  26.1 1.5 collective-permute-done.6
  27.7 1.9 shard_map.126
  29.7 1.9 collective-permute-done.13.refs_2_
  31.7 3.1 %collective-permute-done.16 = bf16[240,384]{1,0:T(8,128)(2,1)S(1)} collective-permute-done((bf16[240,384]{1,0:T(8,128)(2,1)S(1)}, bf16[240,384]{1,0:T(8,128)(2,1)S(1)}, u32[]{:S(2)}, u32[]{:S(2)}) %collective-permute-start.16) | collective-permute-done | bytes 184352 | tf_op jit(solution)/shard_map/ppermute | solution.py:32
  35.0 3.4 %collective-permute-start.5 = (bf16[240,384]{1,0:T(8,128)(2,1)S(1)}, bf16[240,384]{1,0:T(8,128)(2,1)S(1)}, u32[]{:S(2)}, u32[]{:S(2)}) collective-permute-start(bf16[240,384]{1,0:T(8,128)(2,1)S(1)} %fusion.1), channel_id=1, source_target_pairs={{0,1},{1,0},{2,3},{3,2},{4,5},{5,4},{6,7},{7,6},{8,9},{9,8},{10,11... | collective-permute-start | bytes 552968 | tf_op jit(solution)/shard_map/ppermute | solution.py:32
  38.4 5.0 %collective-permute-start.15 = (bf16[240,384]{1,0:T(8,128)(2,1)S(1)}, bf16[240,384]{1,0:T(8,128)(2,1)S(1)}, u32[]{:S(2)}, u32[]{:S(2)}) collective-permute-start(bf16[240,384]{1,0:T(8,128)(2,1)S(1)} %fusion.2), channel_id=1, source_target_pairs={{0,1},{1,0},{2,3},{3,2},{4,5},{5,4},{6,7},{7,6},{8,9},{9,8},{10,11... | collective-permute-start | bytes 552968 | tf_op jit(solution)/shard_map/ppermute | solution.py:32
  44.2 2.4 %collective-permute-start.9 = (bf16[240,384]{1,0:T(8,128)(2,1)S(1)}, bf16[240,384]{1,0:T(8,128)(2,1)S(1)}, u32[]{:S(2)}, u32[]{:S(2)}) collective-permute-start(bf16[240,384]{1,0:T(8,128)(2,1)S(1)} %get-tuple-element.128.refs_0_.refs_1_), channel_id=1, source_target_pairs={{0,1},{1,0},{2,3},{3,2},{4,5},{5,4},{6,7},{7,6},{8,9},{9,8},{10,11... | collective-permute-start | bytes 552968 | tf_op jit(solution)/shard_map/ppermute | solution.py:32
  46.6 1.4 collective-permute-done.15.refs_1_
  48.1 2.5 %collective-permute-start.18 = (bf16[240,384]{1,0:T(8,128)(2,1)S(1)}, bf16[240,384]{1,0:T(8,128)(2,1)S(1)}, u32[]{:S(2)}, u32[]{:S(2)}) collective-permute-start(bf16[240,384]{1,0:T(8,128)(2,1)S(1)} %get-tuple-element.144.refs_3_.refs_1_), channel_id=1, source_target_pairs={{0,1},{1,0},{2,3},{3,2},{4,5},{5,4},{6,7},{7,6},{8,9},{9,8},{10,11... | collective-permute-start | bytes 552968 | tf_op jit(solution)/shard_map/ppermute | solution.py:32
  50.7 2.2 %collective-permute-start.10 = (bf16[240,384]{1,0:T(8,128)(2,1)S(1)}, bf16[240,384]{1,0:T(8,128)(2,1)S(1)}, u32[]{:S(2)}, u32[]{:S(2)}) collective-permute-start(bf16[240,384]{1,0:T(8,128)(2,1)S(1)} %broadcast_select_fusion.14), channel_id=1, source_target_pairs={{0,1},{1,0},{2,3},{3,2},{4,5},{5,4},{6,7},{7,6},{8,9},{9,8},{10,11... | collective-permute-start | bytes 552968 | tf_op jit(solution)/shard_map/ppermute | solution.py:32
  53.0 4.1 %collective-permute-start.20 = (bf16[240,384]{1,0:T(8,128)(2,1)S(1)}, bf16[240,384]{1,0:T(8,128)(2,1)S(1)}, u32[]{:S(2)}, u32[]{:S(2)}) collective-permute-start(bf16[240,384]{1,0:T(8,128)(2,1)S(1)} %broadcast_select_fusion.12), channel_id=1, source_target_pairs={{0,1},{1,0},{2,3},{3,2},{4,5},{5,4},{6,7},{7,6},{8,9},{9,8},{10,11... | collective-permute-start | bytes 552968 | tf_op jit(solution)/shard_map/ppermute | solution.py:32
  57.0 3.2 %shard_map.123 = (bf16[320,512]{1,0:T(8,128)(2,1)S(1)}, bf16[320,512]{1,0:T(8,128)(2,1)S(1)}, bf16[240,384]{1,0:T(8,128)(2,1)S(1)}, bf16[240,384]{1,0:T(8,128)(2...) custom-call(s32[10]{0:T(128)S(1)} %stack.35.scal, ...), custom_call_target="tpu_custom_call" | custom-call | flops 377487360 | bytes 2310144 | tf_op jit(solution)/shard_map/pallas_call | solution.py:431
  60.3 1.9 shard_map.134
  62.3 3.1 %collective-permute-start.12 = (bf16[240,384]{1,0:T(8,128)(2,1)S(1)}, bf16[240,384]{1,0:T(8,128)(2,1)S(1)}, u32[]{:S(2)}, u32[]{:S(2)}) collective-permute-start(bf16[240,384]{1,0:T(8,128)(2,1)S(1)} %broadcast_select_fusion.13), channel_id=1, source_target_pairs={{0,1},{1,0},{2,3},{3,2},{4,5},{5,4},{6,7},{7,6},{8,9},{9,8},{10,11... | collective-permute-start | bytes 552968 | tf_op jit(solution)/shard_map/ppermute | solution.py:32
  67.0 5.0 %collective-permute-start.24 = (bf16[240,384]{1,0:T(8,128)(2,1)S(1)}, bf16[240,384]{1,0:T(8,128)(2,1)S(1)}, u32[]{:S(2)}, u32[]{:S(2)}) collective-permute-start(bf16[240,384]{1,0:T(8,128)(2,1)S(1)} %fusion.3), channel_id=1, source_target_pairs={{0,1},{1,0},{2,3},{3,2},{4,5},{5,4},{6,7},{7,6},{8,9},{9,8},{10,11... | collective-permute-start | bytes 552968 | tf_op jit(solution)/shard_map/ppermute | solution.py:32
  72.1 2.5 %shard_map.124 = (f32[320,512]{1,0:T(8,128)S(1)}, f32[320,512]{1,0:T(8,128)S(1)}, f32[8,128]{1,0:T(8,128)S(1)}) custom-call(s32[10]{0:T(128)S(1)} %stack.35.scal, bf16[240,384]{1,0:T(8,128)(2,1)S(1)} %get-tuple-element.128.refs_0_.refs_1_, bf16[240,384]{1,0:T(8,128)(2,1)S(1)} %collective-permute-done.9.refs_1_.refs_2_, ...), custom_call_target="tpu_custom_call" | custom-call | flops 377487360 | bytes 2678784 | tf_op jit(solution)/shard_map/pallas_call | solution.py:488
  74.7 1.9 collective-permute-start.32
  76.8 2.9 %shard_map.129 = (f32[2,2,128,512]{3,2,1,0:T(8,128)S(1)}, f32[2,2,128,512]{3,2,1,0:T(8,128)S(1)}, f32[8,128]{1,0:T(8,128)S(1)}) custom-call(s32[10]{0:T(128)S(1)} %stack.35.scal, f32[4,16,128]{2,1,0:T(8,128)S(1)} %get-tuple-element.122.refs_0_, f32[320,512]{1,0:T(8,128)S(1)} %get-tuple-element.133.refs_1_, f32[320,512]{1,0:T(8,128)S(1)} %get-tuple-element.134.refs_2_, ...), custom_call_target="tpu_custom_call" | custom-call | flops 377487360 | bytes 2678784 | tf_op jit(solution)/shard_map/pallas_call | solution.py:503
  80.5 1.7 collective-permute-start.26
  82.2 2.2 %shard_map.133 = (bf16[4,512,768]{2,1,0:T(8,128)(2,1)}, bf16[4,512,768]{2,1,0:T(8,128)(2,1)}, bf16[4,768,512]{2,1,0:T(8,128)(2,1)}, f32[8,128]{1,0:T(8,128)S(1)}) custom-call(s32[10]{0:T(128)S(1)} %stack.35.scal, bf16[320,512]{1,0:T(8,128)(2,1)S(1)} %get-tuple-element.135.refs_0_.in_ref, bf16[320,512]{1,0:T(8,128)(2,1)S(1)} %get-tuple-element.136.refs_1_.cot_ref, ...), custom_call_target="tpu_custom_call" | custom-call | flops 377487360 | bytes 2678784 | tf_op jit(solution)/shard_map/pallas_call | solution.py:532
  84.9 2.2 %shard_map.140 = (bf16[4,512,768]{2,1,0:T(8,128)(2,1)}, bf16[4,512,768]{2,1,0:T(8,128)(2,1)}, bf16[4,768,512]{2,1,0:T(8,128)(2,1)}, f32[8,128]{1,0:T(8,128)S(1)}) custom-call(s32[10]{0:T(128)S(1)} %stack.35.scal, bf16[320,512]{1,0:T(8,128)(2,1)S(1)} %get-tuple-element.135.refs_0_.in_ref, ...), custom_call_target="tpu_custom_call", output_to_operand_aliasing={{0}: (10, {}), {1}: (11, {}), {2}: (12, {})} | custom-call | flops 377487360 | bytes 2678784 | tf_op jit(solution)/shard_map/pallas_call | solution.py:532
  87.1 3.6 %collective-permute-start.28 = (bf16[240,384]{1,0:T(8,128)(2,1)S(1)}, bf16[240,384]{1,0:T(8,128)(2,1)S(1)}, u32[]{:S(2)}, u32[]{:S(2)}) collective-permute-start(bf16[240,384]{1,0:T(8,128)(2,1)S(1)} %broadcast_select_fusion.10), channel_id=1, source_target_pairs={{0,1},{1,0},{2,3},{3,2},{4,5},{5,4},{6,7},{7,6},{8,9},{9,8},{10,11... | collective-permute-start | bytes 552968 | tf_op jit(solution)/shard_map/ppermute | solution.py:32
  90.8 1.9 collective-permute-start.36
  92.6 3.4 %shard_map.139 = (bf16[320,512]{1,0:T(8,128)(2,1)S(1)}, bf16[320,512]{1,0:T(8,128)(2,1)S(1)}, bf16[240,384]{1,0:T(8,128)(2,1)S(1)}, bf16[240,384]{1,0:T(8,128)(2...) custom-call(s32[10]{0:T(128)S(1)} %stack.35.scal, ...), custom_call_target="tpu_custom_call" | custom-call | flops 377487360 | bytes 2310144 | tf_op jit(solution)/shard_map/pallas_call | solution.py:431
  96.1 1.9 shard_map.145
  98.1 3.0 %collective-permute-start.30 = (bf16[240,384]{1,0:T(8,128)(2,1)S(1)}, bf16[240,384]{1,0:T(8,128)(2,1)S(1)}, u32[]{:S(2)}, u32[]{:S(2)}) collective-permute-start(bf16[240,384]{1,0:T(8,128)(2,1)S(1)} %broadcast_select_fusion.9), channel_id=1, source_target_pairs={{0,1},{1,0},{2,3},{3,2},{4,5},{5,4},{6,7},{7,6},{8,9},{9,8},{10,11... | collective-permute-start | bytes 552968 | tf_op jit(solution)/shard_map/ppermute | solution.py:32
  102.6 5.7 %collective-permute-start.40 = (bf16[240,384]{1,0:T(8,128)(2,1)S(1)}, bf16[240,384]{1,0:T(8,128)(2,1)S(1)}, u32[]{:S(2)}, u32[]{:S(2)}) collective-permute-start(bf16[240,384]{1,0:T(8,128)(2,1)S(1)} %fusion.4), channel_id=1, source_target_pairs={{0,1},{1,0},{2,3},{3,2},{4,5},{5,4},{6,7},{7,6},{8,9},{9,8},{10,11... | collective-permute-start | bytes 552968 | tf_op jit(solution)/shard_map/ppermute | solution.py:32
  108.5 2.5 %shard_map.132 = (f32[320,512]{1,0:T(8,128)S(1)}, f32[320,512]{1,0:T(8,128)S(1)}, f32[8,128]{1,0:T(8,128)S(1)}) custom-call(s32[10]{0:T(128)S(1)} %stack.35.scal, bf16[240,384]{1,0:T(8,128)(2,1)S(1)} %get-tuple-element.151.refs_0_.refs_1_, bf16[240,384]{1,0:T(8,128)(2,1)S(1)} %collective-permute-done.26.refs_1_.refs_2_, ...), custom_call_target="tpu_custom_call" | custom-call | flops 377487360 | bytes 2678784 | tf_op jit(solution)/shard_map/pallas_call | solution.py:488
  111.1 1.6 collective-permute-start.48
  112.8 2.9 %shard_map.138 = (f32[2,2,128,512]{3,2,1,0:T(8,128)S(1)}, f32[2,2,128,512]{3,2,1,0:T(8,128)S(1)}, f32[8,128]{1,0:T(8,128)S(1)}) custom-call(s32[10]{0:T(128)S(1)} %stack.35.scal, f32[4,16,128]{2,1,0:T(8,128)S(1)} %get-tuple-element.122.refs_0_, f32[320,512]{1,0:T(8,128)S(1)} %get-tuple-element.154.refs_1_, f32[320,512]{1,0:T(8,128)S(1)} %get-tuple-element.155.refs_2_, ...), custom_call_target="tpu_custom_call" | custom-call | flops 377487360 | bytes 2678784 | tf_op jit(solution)/shard_map/pallas_call | solution.py:503
  116.5 2.1 %collective-permute-start.42 = (bf16[240,384]{1,0:T(8,128)(2,1)S(1)}, bf16[240,384]{1,0:T(8,128)(2,1)S(1)}, u32[]{:S(2)}, u32[]{:S(2)}) collective-permute-start(bf16[240,384]{1,0:T(8,128)(2,1)S(1)} %get-tuple-element.174.refs_0_.refs_1_), channel_id=1, source_target_pairs={{0,1},{1,0},{2,3},{3,2},{4,5},{5,4},{6,7},{7,6},{8,9},{9,8},{10,11... | collective-permute-start | bytes 552968 | tf_op jit(solution)/shard_map/ppermute | solution.py:32
  118.5 2.2 %shard_map.144 = (bf16[4,512,768]{2,1,0:T(8,128)(2,1)}, bf16[4,512,768]{2,1,0:T(8,128)(2,1)}, bf16[4,768,512]{2,1,0:T(8,128)(2,1)}, f32[8,128]{1,0:T(8,128)S(1)}) custom-call(s32[10]{0:T(128)S(1)} %stack.35.scal, bf16[320,512]{1,0:T(8,128)(2,1)S(1)} %get-tuple-element.139.refs_1_.in_ref, ...), custom_call_target="tpu_custom_call", output_to_operand_aliasing={{0}: (10, {}), {1}: (11, {}), {2}: (12, {})} | custom-call | flops 377487360 | bytes 2678784 | tf_op jit(solution)/shard_map/pallas_call | solution.py:532
  121.0 2.2 %shard_map.150 = (bf16[4,512,768]{2,1,0:T(8,128)(2,1)}, bf16[4,512,768]{2,1,0:T(8,128)(2,1)}, bf16[4,768,512]{2,1,0:T(8,128)(2,1)}, f32[8,128]{1,0:T(8,128)S(1)}) custom-call(s32[10]{0:T(128)S(1)} %stack.35.scal, bf16[320,512]{1,0:T(8,128)(2,1)S(1)} %get-tuple-element.139.refs_1_.in_ref, ...), custom_call_target="tpu_custom_call", output_to_operand_aliasing={{0}: (10, {}), {1}: (11, {}), {2}: (12, {})} | custom-call | flops 377487360 | bytes 2678784 | tf_op jit(solution)/shard_map/pallas_call | solution.py:532
  123.2 3.5 %collective-permute-start.44 = (bf16[240,384]{1,0:T(8,128)(2,1)S(1)}, bf16[240,384]{1,0:T(8,128)(2,1)S(1)}, u32[]{:S(2)}, u32[]{:S(2)}) collective-permute-start(bf16[240,384]{1,0:T(8,128)(2,1)S(1)} %broadcast_select_fusion.5), channel_id=1, source_target_pairs={{0,1},{1,0},{2,3},{3,2},{4,5},{5,4},{6,7},{7,6},{8,9},{9,8},{10,11... | collective-permute-start | bytes 552968 | tf_op jit(solution)/shard_map/ppermute | solution.py:32
  126.8 2.2 %collective-permute-start.52 = (bf16[240,384]{1,0:T(8,128)(2,1)S(1)}, bf16[240,384]{1,0:T(8,128)(2,1)S(1)}, u32[]{:S(2)}, u32[]{:S(2)}) collective-permute-start(bf16[240,384]{1,0:T(8,128)(2,1)S(1)} %broadcast_select_fusion.2), channel_id=1, source_target_pairs={{0,1},{1,0},{2,3},{3,2},{4,5},{5,4},{6,7},{7,6},{8,9},{9,8},{10,11... | collective-permute-start | bytes 552968 | tf_op jit(solution)/shard_map/ppermute | solution.py:32
  129.0 4.4 %collective-permute-start.46 = (bf16[240,384]{1,0:T(8,128)(2,1)S(1)}, bf16[240,384]{1,0:T(8,128)(2,1)S(1)}, u32[]{:S(2)}, u32[]{:S(2)}) collective-permute-start(bf16[240,384]{1,0:T(8,128)(2,1)S(1)} %broadcast_select_fusion.4), channel_id=1, source_target_pairs={{0,1},{1,0},{2,3},{3,2},{4,5},{5,4},{6,7},{7,6},{8,9},{9,8},{10,11... | collective-permute-start | bytes 552968 | tf_op jit(solution)/shard_map/ppermute | solution.py:32
  133.6 3.8 %collective-permute-start.54 = (bf16[240,384]{1,0:T(8,128)(2,1)S(1)}, bf16[240,384]{1,0:T(8,128)(2,1)S(1)}, u32[]{:S(2)}, u32[]{:S(2)}) collective-permute-start(bf16[240,384]{1,0:T(8,128)(2,1)S(1)} %broadcast_select_fusion.1), channel_id=1, source_target_pairs={{0,1},{1,0},{2,3},{3,2},{4,5},{5,4},{6,7},{7,6},{8,9},{9,8},{10,11... | collective-permute-start | bytes 552968 | tf_op jit(solution)/shard_map/ppermute | solution.py:32
  137.6 4.5 %collective-permute-start.56 = (bf16[240,384]{1,0:T(8,128)(2,1)S(1)}, bf16[240,384]{1,0:T(8,128)(2,1)S(1)}, u32[]{:S(2)}, u32[]{:S(2)}) collective-permute-start(bf16[240,384]{1,0:T(8,128)(2,1)S(1)} %fusion.5), channel_id=1, source_target_pairs={{0,1},{1,0},{2,3},{3,2},{4,5},{5,4},{6,7},{7,6},{8,9},{9,8},{10,11... | collective-permute-start | bytes 552968 | tf_op jit(solution)/shard_map/ppermute | solution.py:32
  142.3 2.5 %shard_map.143 = (f32[320,512]{1,0:T(8,128)S(1)}, f32[320,512]{1,0:T(8,128)S(1)}, f32[8,128]{1,0:T(8,128)S(1)}) custom-call(s32[10]{0:T(128)S(1)} %stack.35.scal, bf16[240,384]{1,0:T(8,128)(2,1)S(1)} %get-tuple-element.174.refs_0_.refs_1_, bf16[240,384]{1,0:T(8,128)(2,1)S(1)} %collective-permute-done.42.refs_1_.refs_2_, ...), custom_call_target="tpu_custom_call" | custom-call | flops 377487360 | bytes 2678784 | tf_op jit(solution)/shard_map/pallas_call | solution.py:488
  144.9 1.3 collective-permute-start.59
  146.3 2.9 %shard_map.149 = (f32[2,2,128,512]{3,2,1,0:T(8,128)S(1)}, f32[2,2,128,512]{3,2,1,0:T(8,128)S(1)}, f32[8,128]{1,0:T(8,128)S(1)}) custom-call(s32[10]{0:T(128)S(1)} %stack.35.scal, f32[4,16,128]{2,1,0:T(8,128)S(1)} %get-tuple-element.122.refs_0_, f32[320,512]{1,0:T(8,128)S(1)} %get-tuple-element.177.refs_1_, f32[320,512]{1,0:T(8,128)S(1)} %get-tuple-element.178.refs_2_, ...), custom_call_target="tpu_custom_call" | custom-call | flops 377487360 | bytes 2678784 | tf_op jit(solution)/shard_map/pallas_call | solution.py:503
  149.4 2.2 %shard_map.153 = (bf16[4,512,768]{2,1,0:T(8,128)(2,1)}, bf16[4,512,768]{2,1,0:T(8,128)(2,1)}, bf16[4,768,512]{2,1,0:T(8,128)(2,1)}, f32[8,128]{1,0:T(8,128)S(1)}) custom-call(s32[10]{0:T(128)S(1)} %stack.35.scal, bf16[320,512]{1,0:T(8,128)(2,1)S(1)} %get-tuple-element.129.refs_1_.in_ref, ...), custom_call_target="tpu_custom_call", output_to_operand_aliasing={{0}: (10, {}), {1}: (11, {}), {2}: (12, {})} | custom-call | flops 377487360 | bytes 2678784 | tf_op jit(solution)/shard_map/pallas_call | solution.py:532
  152.8 1.9 collective-permute-start.66
  154.8 8.9 %collective-permute-done.61.refs_2_ = bf16[240,384]{1,0:T(8,128)(2,1)S(1)} collective-permute-done((bf16[240,384]{1,0:T(8,128)(2,1)S(1)}, bf16[240,384]{1,0:T(8,128)(2,1)S(1)}, u32[]{:S(2)}, u32[]{:S(2)}) %collective-permute-start.61) | collective-permute-done | bytes 184352 | tf_op jit(solution)/shard_map/ppermute | solution.py:32
  164.2 3.8 %collective-permute-start.63 = (bf16[240,384]{1,0:T(8,128)(2,1)S(1)}, bf16[240,384]{1,0:T(8,128)(2,1)S(1)}, u32[]{:S(2)}, u32[]{:S(2)}) collective-permute-start(bf16[240,384]{1,0:T(8,128)(2,1)S(1)} %collective-permute-done.62.refs_4_), channel_id=1, source_target_pairs={{0,1},{1,0},{2,3},{3,2},{4,5},{5,4},{6,7},{7,6},{8,9},{9,8},{10,11... | collective-permute-start | bytes 552968 | tf_op jit(solution)/shard_map/ppermute | solution.py:32
  168.0 4.6 %collective-permute-start.65 = (bf16[240,384]{1,0:T(8,128)(2,1)S(1)}, bf16[240,384]{1,0:T(8,128)(2,1)S(1)}, u32[]{:S(2)}, u32[]{:S(2)}) collective-permute-start(bf16[240,384]{1,0:T(8,128)(2,1)S(1)} %collective-permute-done.64.refs_6_), channel_id=1, source_target_pairs={{0,1},{1,0},{2,3},{3,2},{4,5},{5,4},{6,7},{7,6},{8,9},{9,8},{10,11... | collective-permute-start | bytes 552968 | tf_op jit(solution)/shard_map/ppermute | solution.py:32
  172.7 4.1 %collective-permute-start.68 = (bf16[256,384]{1,0:T(8,128)(2,1)S(1)}, bf16[256,384]{1,0:T(8,128)(2,1)S(1)}, u32[]{:S(2)}, u32[]{:S(2)}) collective-permute-start(bf16[256,384]{1,0:T(8,128)(2,1)S(1)} %collective-permute-done.67.refs_8_.refs_4_), channel_id=1, source_target_pairs={{0,1},{1,0},{2,3},{3,2},{4,5},{5,4},{6,7},{7,6},{8,9},{9,8},{10,11... | collective-permute-start | bytes 589832 | tf_op jit(solution)/shard_map/ppermute | solution.py:32
  176.7 2.1 %collective-permute-start.70 = (bf16[256,384]{1,0:T(8,128)(2,1)S(1)}, bf16[256,384]{1,0:T(8,128)(2,1)S(1)}, u32[]{:S(2)}, u32[]{:S(2)}) collective-permute-start(bf16[256,384]{1,0:T(8,128)(2,1)S(1)} %collective-permute-done.69.refs_10_.refs_6_), channel_id=1, source_target_pairs={{0,1},{1,0},{2,3},{3,2},{4,5},{5,4},{6,7},{7,6},{8,9},{9,8},{10,11... | collective-permute-start | bytes 589832 | tf_op jit(solution)/shard_map/ppermute | solution.py:32
  178.8 2.2 %shard_map.157 = (bf16[4,512,768]{2,1,0:T(8,128)(2,1)}, bf16[4,512,768]{2,1,0:T(8,128)(2,1)}, bf16[4,768,512]{2,1,0:T(8,128)(2,1)}, f32[8,128]{1,0:T(8,128)S(1)}) custom-call(s32[10]{0:T(128)S(1)} %stack.35.scal, bf16[320,512]{1,0:T(8,128)(2,1)S(1)} %get-tuple-element.129.refs_1_.in_ref, ...), custom_call_target="tpu_custom_call", output_to_operand_aliasing={{0}: (10, {}), {1}: (11, {}), {2}: (12, {})} | custom-call | flops 377487360 | bytes 2678784 | tf_op jit(solution)/shard_map/pallas_call | solution.py:532
  181.0 2.5 %shard_map.158 = (f32[320,512]{1,0:T(8,128)S(1)}, f32[320,512]{1,0:T(8,128)S(1)}, f32[8,128]{1,0:T(8,128)}) custom-call(s32[10]{0:T(128)S(1)} %stack.35.scal, f32[8,128]{1,0:T(8,128)S(1)} %get-tuple-element.220.refs_0_, bf16[240,384]{1,0:T(8,128)(2,1)S(1)} %get-tuple-element.201.refs_0_.refs_1_, bf16[240,384]{1,0:T(8,128)(2,1)S(1)} %collective-permute-done.61.refs_2_, ...), custom_call_target="tpu_custom_call" | custom-call | flops 377487360 | bytes 2678784 | tf_op jit(solution)/shard_map/pallas_call | solution.py:488
  183.9 3.8 %shard_map.159 = (bf16[2,2,128,512]{3,2,1,0:T(8,128)(2,1)S(1)}, bf16[2,2,128,512]{3,2,1,0:T(8,128)(2,1)S(1)}, f32[8,128]{1,0:T(8,128)}, f32[2,16,128]{2,1,0:T(8,128)S(1)}, f32[2,16,128]{2,1,0:T(8,128)S(1)}) custom-call(s32[10]{0:T(128)S(1)} %stack.35.scal, f32[4,16,128]{2,1,0:T(8,128)S(1)} %get-tuple-element.122.refs_0_, ...), custom_call_target="tpu_custom_call" | custom-call | flops 377487360 | bytes 2678784 | tf_op jit(solution)/shard_map/pallas_call | solution.py:503
  188.2 1.4 collective-permute-done.71
  189.8 1.6 collective-permute-start.72
  192.0 2.2 %shard_map.160 = (bf16[4,512,768]{2,1,0:T(8,128)(2,1)}, bf16[4,512,768]{2,1,0:T(8,128)(2,1)}, bf16[4,768,512]{2,1,0:T(8,128)(2,1)}, f32[8,128]{1,0:T(8,128)}) custom-call(s32[10]{0:T(128)S(1)} %stack.35.scal, bf16[320,512]{1,0:T(8,128)(2,1)S(1)} %get-tuple-element.188.refs_1_.in_ref, ...), custom_call_target="tpu_custom_call", output_to_operand_aliasing={{0}: (10, {}), {1}: (11, {}), {2}: (12, {})} | custom-call | flops 377487360 | bytes 2678784 | tf_op jit(solution)/shard_map/pallas_call | solution.py:532
  194.2 2.2 %shard_map.161 = (bf16[4,512,768]{2,1,0:T(8,128)(2,1)}, bf16[4,512,768]{2,1,0:T(8,128)(2,1)}, bf16[4,768,512]{2,1,0:T(8,128)(2,1)}, f32[8,128]{1,0:T(8,128)}) custom-call(s32[10]{0:T(128)S(1)} %stack.35.scal, bf16[320,512]{1,0:T(8,128)(2,1)S(1)} %get-tuple-element.188.refs_1_.in_ref, ...), custom_call_target="tpu_custom_call", output_to_operand_aliasing={{0}: (10, {}), {1}: (11, {}), {2}: (12, {})} | custom-call | flops 377487360 | bytes 2678784 | tf_op jit(solution)/shard_map/pallas_call | solution.py:532
  196.3 2.1 %collective-permute-done.74 = f32[16,128]{1,0:T(8,128)S(1)} collective-permute-done((f32[16,128]{1,0:T(8,128)S(1)}, f32[16,128]{1,0:T(8,128)S(1)}, u32[]{:S(2)}, u32[]{:S(2)}) %collective-permute-start.74) | collective-permute-done | bytes 8224 | tf_op jit(solution)/shard_map/ppermute | solution.py:32
  (172 shorter events, 15.2 us)
Async XLA Ops:
  1.7 9.7 %collective-permute-start = (bf16[272,512]{1,0:T(8,128)(2,1)S(1)}, bf16[272,512]{1,0:T(8,128)(2,1)S(1)}, u32[]{:S(2)}, u32[]{:S(2)}) collective-permute-start(bf16[272,512]{1,0:T(8,128)(2,1)S(1)} %shard_map.118.refs_0_.refs_1_), channel_id=1, source_target_pairs={{0,8},{4,12},{8,0},{12,4},{1,9},{5,13},{9,1},{13,5},{2,10},{6,14},... | collective-permute-start | bytes 835592 | tf_op jit(solution)/shard_map/ppermute | solution.py:32
  4.7 6.7 %collective-permute-start.1 = (bf16[272,512]{1,0:T(8,128)(2,1)S(1)}, bf16[272,512]{1,0:T(8,128)(2,1)S(1)}, u32[]{:S(2)}, u32[]{:S(2)}) collective-permute-start(bf16[272,512]{1,0:T(8,128)(2,1)S(1)} %shard_map.118.refs_0_.refs_1_), channel_id=1, source_target_pairs={{0,4},{4,0},{8,12},{12,8},{1,5},{5,1},{9,13},{13,9},{2,6},{6,2},{1... | collective-permute-start | bytes 835592 | tf_op jit(solution)/shard_map/ppermute | solution.py:32
  16.1 9.8 %collective-permute-start.3 = (bf16[240,384]{1,0:T(8,128)(2,1)S(1)}, bf16[240,384]{1,0:T(8,128)(2,1)S(1)}, u32[]{:S(2)}, u32[]{:S(2)}) collective-permute-start(bf16[240,384]{1,0:T(8,128)(2,1)S(1)} %get-tuple-element.126.refs_1_), channel_id=1, source_target_pairs={{0,1},{1,0},{2,3},{3,2},{4,5},{5,4},{6,7},{7,6},{8,9},{9,8},{10,11... | collective-permute-start | bytes 552968 | tf_op jit(solution)/shard_map/ppermute | solution.py:32
  18.0 9.6 %collective-permute-start.6 = (bf16[240,384]{1,0:T(8,128)(2,1)S(1)}, bf16[240,384]{1,0:T(8,128)(2,1)S(1)}, u32[]{:S(2)}, u32[]{:S(2)}) collective-permute-start(bf16[240,384]{1,0:T(8,128)(2,1)S(1)} %get-tuple-element.127), channel_id=1, source_target_pairs={{0,1},{1,0},{2,3},{3,2},{4,5},{5,4},{6,7},{7,6},{8,9},{9,8},{10,11... | collective-permute-start | bytes 552968 | tf_op jit(solution)/shard_map/ppermute | solution.py:32
  20.6 11.0 %collective-permute-start.13 = (bf16[240,384]{1,0:T(8,128)(2,1)S(1)}, bf16[240,384]{1,0:T(8,128)(2,1)S(1)}, u32[]{:S(2)}, u32[]{:S(2)}) collective-permute-start(bf16[240,384]{1,0:T(8,128)(2,1)S(1)} %get-tuple-element.142.refs_1_), channel_id=1, source_target_pairs={{0,1},{1,0},{2,3},{3,2},{4,5},{5,4},{6,7},{7,6},{8,9},{9,8},{10,11... | collective-permute-start | bytes 552968 | tf_op jit(solution)/shard_map/ppermute | solution.py:32
  22.5 12.3 %collective-permute-start.16 = (bf16[240,384]{1,0:T(8,128)(2,1)S(1)}, bf16[240,384]{1,0:T(8,128)(2,1)S(1)}, u32[]{:S(2)}, u32[]{:S(2)}) collective-permute-start(bf16[240,384]{1,0:T(8,128)(2,1)S(1)} %get-tuple-element.143), channel_id=1, source_target_pairs={{0,1},{1,0},{2,3},{3,2},{4,5},{5,4},{6,7},{7,6},{8,9},{9,8},{10,11... | collective-permute-start | bytes 552968 | tf_op jit(solution)/shard_map/ppermute | solution.py:32
  26.0 9.0 %collective-permute-start.4 = (bf16[240,384]{1,0:T(8,128)(2,1)S(1)}, bf16[240,384]{1,0:T(8,128)(2,1)S(1)}, u32[]{:S(2)}, u32[]{:S(2)}) collective-permute-start(bf16[240,384]{1,0:T(8,128)(2,1)S(1)} %shard_map.121), channel_id=1, source_target_pairs={{1,2},{2,1},{0,4},{3,7},{5,6},{6,5},{4,0},{7,3},{9,10},{10,9},{8,1... | collective-permute-start | bytes 552968 | tf_op jit(solution)/shard_map/ppermute | solution.py:559
  27.7 15.8 %collective-permute-start.7 = (bf16[240,384]{1,0:T(8,128)(2,1)S(1)}, bf16[240,384]{1,0:T(8,128)(2,1)S(1)}, u32[]{:S(2)}, u32[]{:S(2)}) collective-permute-start(bf16[240,384]{1,0:T(8,128)(2,1)S(1)} %fusion.6), channel_id=1, source_target_pairs={{1,2},{2,1},{0,4},{3,7},{5,6},{6,5},{4,0},{7,3},{9,10},{10,9},{8,1... | collective-permute-start | bytes 552968 | tf_op jit(solution)/shard_map/ppermute | solution.py:559
  31.6 6.8 %collective-permute-start.14 = (bf16[240,384]{1,0:T(8,128)(2,1)S(1)}, bf16[240,384]{1,0:T(8,128)(2,1)S(1)}, u32[]{:S(2)}, u32[]{:S(2)}) collective-permute-start(bf16[240,384]{1,0:T(8,128)(2,1)S(1)} %shard_map.127), channel_id=1, source_target_pairs={{1,2},{2,1},{0,4},{3,7},{5,6},{6,5},{4,0},{7,3},{9,10},{10,9},{8,1... | collective-permute-start | bytes 552968 | tf_op jit(solution)/shard_map/ppermute | solution.py:559
  34.9 11.7 %collective-permute-start.17 = (bf16[240,384]{1,0:T(8,128)(2,1)S(1)}, bf16[240,384]{1,0:T(8,128)(2,1)S(1)}, u32[]{:S(2)}, u32[]{:S(2)}) collective-permute-start(bf16[240,384]{1,0:T(8,128)(2,1)S(1)} %fusion.7), channel_id=1, source_target_pairs={{1,2},{2,1},{0,4},{3,7},{5,6},{6,5},{4,0},{7,3},{9,10},{10,9},{8,1... | collective-permute-start | bytes 552968 | tf_op jit(solution)/shard_map/ppermute | solution.py:559
  35.0 8.9 %collective-permute-start.5 = (bf16[240,384]{1,0:T(8,128)(2,1)S(1)}, bf16[240,384]{1,0:T(8,128)(2,1)S(1)}, u32[]{:S(2)}, u32[]{:S(2)}) collective-permute-start(bf16[240,384]{1,0:T(8,128)(2,1)S(1)} %fusion.1), channel_id=1, source_target_pairs={{0,1},{1,0},{2,3},{3,2},{4,5},{5,4},{6,7},{7,6},{8,9},{9,8},{10,11... | collective-permute-start | bytes 552968 | tf_op jit(solution)/shard_map/ppermute | solution.py:32
  38.4 9.5 %collective-permute-start.15 = (bf16[240,384]{1,0:T(8,128)(2,1)S(1)}, bf16[240,384]{1,0:T(8,128)(2,1)S(1)}, u32[]{:S(2)}, u32[]{:S(2)}) collective-permute-start(bf16[240,384]{1,0:T(8,128)(2,1)S(1)} %fusion.2), channel_id=1, source_target_pairs={{0,1},{1,0},{2,3},{3,2},{4,5},{5,4},{6,7},{7,6},{8,9},{9,8},{10,11... | collective-permute-start | bytes 552968 | tf_op jit(solution)/shard_map/ppermute | solution.py:32
  44.1 6.6 %collective-permute-start.8 = (bf16[240,384]{1,0:T(8,128)(2,1)S(1)}, bf16[240,384]{1,0:T(8,128)(2,1)S(1)}, u32[]{:S(2)}, u32[]{:S(2)}) collective-permute-start(bf16[240,384]{1,0:T(8,128)(2,1)S(1)} %get-tuple-element.128.refs_0_.refs_1_), channel_id=1, source_target_pairs={{1,2},{2,1},{0,4},{3,7},{5,6},{6,5},{4,0},{7,3},{9,10},{10,9},{8,1... | collective-permute-start | bytes 552968 | tf_op jit(solution)/shard_map/ppermute | solution.py:559
  44.2 8.8 %collective-permute-start.9 = (bf16[240,384]{1,0:T(8,128)(2,1)S(1)}, bf16[240,384]{1,0:T(8,128)(2,1)S(1)}, u32[]{:S(2)}, u32[]{:S(2)}) collective-permute-start(bf16[240,384]{1,0:T(8,128)(2,1)S(1)} %get-tuple-element.128.refs_0_.refs_1_), channel_id=1, source_target_pairs={{0,1},{1,0},{2,3},{3,2},{4,5},{5,4},{6,7},{7,6},{8,9},{9,8},{10,11... | collective-permute-start | bytes 552968 | tf_op jit(solution)/shard_map/ppermute | solution.py:32
  48.1 8.9 %collective-permute-start.18 = (bf16[240,384]{1,0:T(8,128)(2,1)S(1)}, bf16[240,384]{1,0:T(8,128)(2,1)S(1)}, u32[]{:S(2)}, u32[]{:S(2)}) collective-permute-start(bf16[240,384]{1,0:T(8,128)(2,1)S(1)} %get-tuple-element.144.refs_3_.refs_1_), channel_id=1, source_target_pairs={{0,1},{1,0},{2,3},{3,2},{4,5},{5,4},{6,7},{7,6},{8,9},{9,8},{10,11... | collective-permute-start | bytes 552968 | tf_op jit(solution)/shard_map/ppermute | solution.py:32
  50.7 14.7 %collective-permute-start.10 = (bf16[240,384]{1,0:T(8,128)(2,1)S(1)}, bf16[240,384]{1,0:T(8,128)(2,1)S(1)}, u32[]{:S(2)}, u32[]{:S(2)}) collective-permute-start(bf16[240,384]{1,0:T(8,128)(2,1)S(1)} %broadcast_select_fusion.14), channel_id=1, source_target_pairs={{0,1},{1,0},{2,3},{3,2},{4,5},{5,4},{6,7},{7,6},{8,9},{9,8},{10,11... | collective-permute-start | bytes 552968 | tf_op jit(solution)/shard_map/ppermute | solution.py:32
  52.9 9.3 %collective-permute-start.11 = (bf16[240,384]{1,0:T(8,128)(2,1)S(1)}, bf16[240,384]{1,0:T(8,128)(2,1)S(1)}, u32[]{:S(2)}, u32[]{:S(2)}) collective-permute-start(bf16[240,384]{1,0:T(8,128)(2,1)S(1)} %collective-permute-done.9.refs_1_.refs_2_), channel_id=1, source_target_pairs={{1,2},{2,1},{0,4},{3,7},{5,6},{6,5},{4,0},{7,3},{9,10},{10,9},{8,1... | collective-permute-start | bytes 552968 | tf_op jit(solution)/shard_map/ppermute | solution.py:559
  53.0 13.3 %collective-permute-start.20 = (bf16[240,384]{1,0:T(8,128)(2,1)S(1)}, bf16[240,384]{1,0:T(8,128)(2,1)S(1)}, u32[]{:S(2)}, u32[]{:S(2)}) collective-permute-start(bf16[240,384]{1,0:T(8,128)(2,1)S(1)} %broadcast_select_fusion.12), channel_id=1, source_target_pairs={{0,1},{1,0},{2,3},{3,2},{4,5},{5,4},{6,7},{7,6},{8,9},{9,8},{10,11... | collective-permute-start | bytes 552968 | tf_op jit(solution)/shard_map/ppermute | solution.py:32
  57.0 8.5 %collective-permute-start.21 = (bf16[240,384]{1,0:T(8,128)(2,1)S(1)}, bf16[240,384]{1,0:T(8,128)(2,1)S(1)}, u32[]{:S(2)}, u32[]{:S(2)}) collective-permute-start(bf16[240,384]{1,0:T(8,128)(2,1)S(1)} %collective-permute-done.18.refs_4_.refs_2_), channel_id=1, source_target_pairs={{1,2},{2,1},{0,4},{3,7},{5,6},{6,5},{4,0},{7,3},{9,10},{10,9},{8,1... | collective-permute-start | bytes 552968 | tf_op jit(solution)/shard_map/ppermute | solution.py:559
  62.3 9.7 %collective-permute-start.12 = (bf16[240,384]{1,0:T(8,128)(2,1)S(1)}, bf16[240,384]{1,0:T(8,128)(2,1)S(1)}, u32[]{:S(2)}, u32[]{:S(2)}) collective-permute-start(bf16[240,384]{1,0:T(8,128)(2,1)S(1)} %broadcast_select_fusion.13), channel_id=1, source_target_pairs={{0,1},{1,0},{2,3},{3,2},{4,5},{5,4},{6,7},{7,6},{8,9},{9,8},{10,11... | collective-permute-start | bytes 552968 | tf_op jit(solution)/shard_map/ppermute | solution.py:32
  65.6 11.1 %collective-permute-start.22 = (bf16[240,384]{1,0:T(8,128)(2,1)S(1)}, bf16[240,384]{1,0:T(8,128)(2,1)S(1)}, u32[]{:S(2)}, u32[]{:S(2)}) collective-permute-start(bf16[240,384]{1,0:T(8,128)(2,1)S(1)} %broadcast_select_fusion.11), channel_id=1, source_target_pairs={{0,1},{1,0},{2,3},{3,2},{4,5},{5,4},{6,7},{7,6},{8,9},{9,8},{10,11... | collective-permute-start | bytes 552968 | tf_op jit(solution)/shard_map/ppermute | solution.py:32
  66.4 8.3 %collective-permute-start.31 = (bf16[240,384]{1,0:T(8,128)(2,1)S(1)}, bf16[240,384]{1,0:T(8,128)(2,1)S(1)}, u32[]{:S(2)}, u32[]{:S(2)}) collective-permute-start(bf16[240,384]{1,0:T(8,128)(2,1)S(1)} %shard_map.135), channel_id=1, source_target_pairs={{1,2},{2,1},{0,4},{3,7},{5,6},{6,5},{4,0},{7,3},{9,10},{10,9},{8,1... | collective-permute-start | bytes 552968 | tf_op jit(solution)/shard_map/ppermute | solution.py:559
  67.0 12.7 %collective-permute-start.24 = (bf16[240,384]{1,0:T(8,128)(2,1)S(1)}, bf16[240,384]{1,0:T(8,128)(2,1)S(1)}, u32[]{:S(2)}, u32[]{:S(2)}) collective-permute-start(bf16[240,384]{1,0:T(8,128)(2,1)S(1)} %fusion.3), channel_id=1, source_target_pairs={{0,1},{1,0},{2,3},{3,2},{4,5},{5,4},{6,7},{7,6},{8,9},{9,8},{10,11... | collective-permute-start | bytes 552968 | tf_op jit(solution)/shard_map/ppermute | solution.py:32
  72.1 7.7 %collective-permute-start.25 = (bf16[240,384]{1,0:T(8,128)(2,1)S(1)}, bf16[240,384]{1,0:T(8,128)(2,1)S(1)}, u32[]{:S(2)}, u32[]{:S(2)}) collective-permute-start(bf16[240,384]{1,0:T(8,128)(2,1)S(1)} %fusion.8), channel_id=1, source_target_pairs={{1,2},{2,1},{0,4},{3,7},{5,6},{6,5},{4,0},{7,3},{9,10},{10,9},{8,1... | collective-permute-start | bytes 552968 | tf_op jit(solution)/shard_map/ppermute | solution.py:559
  74.7 9.6 %collective-permute-start.32 = (bf16[240,384]{1,0:T(8,128)(2,1)S(1)}, bf16[240,384]{1,0:T(8,128)(2,1)S(1)}, u32[]{:S(2)}, u32[]{:S(2)}) collective-permute-start(bf16[240,384]{1,0:T(8,128)(2,1)S(1)} %broadcast_select_fusion.8), channel_id=1, source_target_pairs={{0,1},{1,0},{2,3},{3,2},{4,5},{5,4},{6,7},{7,6},{8,9},{9,8},{10,11... | collective-permute-start | bytes 552968 | tf_op jit(solution)/shard_map/ppermute | solution.py:32
  76.7 7.7 %collective-permute-start.33 = (bf16[240,384]{1,0:T(8,128)(2,1)S(1)}, bf16[240,384]{1,0:T(8,128)(2,1)S(1)}, u32[]{:S(2)}, u32[]{:S(2)}) collective-permute-start(bf16[240,384]{1,0:T(8,128)(2,1)S(1)} %fusion.9), channel_id=1, source_target_pairs={{1,2},{2,1},{0,4},{3,7},{5,6},{6,5},{4,0},{7,3},{9,10},{10,9},{8,1... | collective-permute-start | bytes 552968 | tf_op jit(solution)/shard_map/ppermute | solution.py:559
  79.9 7.2 %collective-permute-start.27 = (bf16[240,384]{1,0:T(8,128)(2,1)S(1)}, bf16[240,384]{1,0:T(8,128)(2,1)S(1)}, u32[]{:S(2)}, u32[]{:S(2)}) collective-permute-start(bf16[240,384]{1,0:T(8,128)(2,1)S(1)} %get-tuple-element.151.refs_0_.refs_1_), channel_id=1, source_target_pairs={{1,2},{2,1},{0,4},{3,7},{5,6},{6,5},{4,0},{7,3},{9,10},{10,9},{8,1... | collective-permute-start | bytes 552968 | tf_op jit(solution)/shard_map/ppermute | solution.py:559
  80.5 10.2 %collective-permute-start.26 = (bf16[240,384]{1,0:T(8,128)(2,1)S(1)}, bf16[240,384]{1,0:T(8,128)(2,1)S(1)}, u32[]{:S(2)}, u32[]{:S(2)}) collective-permute-start(bf16[240,384]{1,0:T(8,128)(2,1)S(1)} %get-tuple-element.151.refs_0_.refs_1_), channel_id=1, source_target_pairs={{0,1},{1,0},{2,3},{3,2},{4,5},{5,4},{6,7},{7,6},{8,9},{9,8},{10,11... | collective-permute-start | bytes 552968 | tf_op jit(solution)/shard_map/ppermute | solution.py:32
  84.5 8.1 %collective-permute-start.34 = (bf16[240,384]{1,0:T(8,128)(2,1)S(1)}, bf16[240,384]{1,0:T(8,128)(2,1)S(1)}, u32[]{:S(2)}, u32[]{:S(2)}) collective-permute-start(bf16[240,384]{1,0:T(8,128)(2,1)S(1)} %get-tuple-element.163.refs_5_.refs_0_.refs_1_), channel_id=1, source_target_pairs={{0,1},{1,0},{2,3},{3,2},{4,5},{5,4},{6,7},{7,6},{8,9},{9,8},{10,11... | collective-permute-start | bytes 552968 | tf_op jit(solution)/shard_map/ppermute | solution.py:32
  84.9 5.8 %collective-permute-start.35 = (bf16[240,384]{1,0:T(8,128)(2,1)S(1)}, bf16[240,384]{1,0:T(8,128)(2,1)S(1)}, u32[]{:S(2)}, u32[]{:S(2)}) collective-permute-start(bf16[240,384]{1,0:T(8,128)(2,1)S(1)} %get-tuple-element.163.refs_5_.refs_0_.refs_1_), channel_id=1, source_target_pairs={{1,2},{2,1},{0,4},{3,7},{5,6},{6,5},{4,0},{7,3},{9,10},{10,9},{8,1... | collective-permute-start | bytes 552968 | tf_op jit(solution)/shard_map/ppermute | solution.py:559
  87.1 13.9 %collective-permute-start.28 = (bf16[240,384]{1,0:T(8,128)(2,1)S(1)}, bf16[240,384]{1,0:T(8,128)(2,1)S(1)}, u32[]{:S(2)}, u32[]{:S(2)}) collective-permute-start(bf16[240,384]{1,0:T(8,128)(2,1)S(1)} %broadcast_select_fusion.10), channel_id=1, source_target_pairs={{0,1},{1,0},{2,3},{3,2},{4,5},{5,4},{6,7},{7,6},{8,9},{9,8},{10,11... | collective-permute-start | bytes 552968 | tf_op jit(solution)/shard_map/ppermute | solution.py:32
  90.7 7.3 %collective-permute-start.29 = (bf16[240,384]{1,0:T(8,128)(2,1)S(1)}, bf16[240,384]{1,0:T(8,128)(2,1)S(1)}, u32[]{:S(2)}, u32[]{:S(2)}) collective-permute-start(bf16[240,384]{1,0:T(8,128)(2,1)S(1)} %collective-permute-done.26.refs_1_.refs_2_), channel_id=1, source_target_pairs={{1,2},{2,1},{0,4},{3,7},{5,6},{6,5},{4,0},{7,3},{9,10},{10,9},{8,1... | collective-permute-start | bytes 552968 | tf_op jit(solution)/shard_map/ppermute | solution.py:559
  90.8 11.5 %collective-permute-start.36 = (bf16[240,384]{1,0:T(8,128)(2,1)S(1)}, bf16[240,384]{1,0:T(8,128)(2,1)S(1)}, u32[]{:S(2)}, u32[]{:S(2)}) collective-permute-start(bf16[240,384]{1,0:T(8,128)(2,1)S(1)} %broadcast_select_fusion.7), channel_id=1, source_target_pairs={{0,1},{1,0},{2,3},{3,2},{4,5},{5,4},{6,7},{7,6},{8,9},{9,8},{10,11... | collective-permute-start | bytes 552968 | tf_op jit(solution)/shard_map/ppermute | solution.py:32
  92.6 8.5 %collective-permute-start.37 = (bf16[240,384]{1,0:T(8,128)(2,1)S(1)}, bf16[240,384]{1,0:T(8,128)(2,1)S(1)}, u32[]{:S(2)}, u32[]{:S(2)}) collective-permute-start(bf16[240,384]{1,0:T(8,128)(2,1)S(1)} %collective-permute-done.34.refs_6_.refs_2_), channel_id=1, source_target_pairs={{1,2},{2,1},{0,4},{3,7},{5,6},{6,5},{4,0},{7,3},{9,10},{10,9},{8,1... | collective-permute-start | bytes 552968 | tf_op jit(solution)/shard_map/ppermute | solution.py:559
  98.1 10.3 %collective-permute-start.30 = (bf16[240,384]{1,0:T(8,128)(2,1)S(1)}, bf16[240,384]{1,0:T(8,128)(2,1)S(1)}, u32[]{:S(2)}, u32[]{:S(2)}) collective-permute-start(bf16[240,384]{1,0:T(8,128)(2,1)S(1)} %broadcast_select_fusion.9), channel_id=1, source_target_pairs={{0,1},{1,0},{2,3},{3,2},{4,5},{5,4},{6,7},{7,6},{8,9},{9,8},{10,11... | collective-permute-start | bytes 552968 | tf_op jit(solution)/shard_map/ppermute | solution.py:32
  101.2 11.5 %collective-permute-start.38 = (bf16[240,384]{1,0:T(8,128)(2,1)S(1)}, bf16[240,384]{1,0:T(8,128)(2,1)S(1)}, u32[]{:S(2)}, u32[]{:S(2)}) collective-permute-start(bf16[240,384]{1,0:T(8,128)(2,1)S(1)} %broadcast_select_fusion.6), channel_id=1, source_target_pairs={{0,1},{1,0},{2,3},{3,2},{4,5},{5,4},{6,7},{7,6},{8,9},{9,8},{10,11... | collective-permute-start | bytes 552968 | tf_op jit(solution)/shard_map/ppermute | solution.py:32
  102.4 8.6 %collective-permute-start.47 = (bf16[240,384]{1,0:T(8,128)(2,1)S(1)}, bf16[240,384]{1,0:T(8,128)(2,1)S(1)}, u32[]{:S(2)}, u32[]{:S(2)}) collective-permute-start(bf16[240,384]{1,0:T(8,128)(2,1)S(1)} %shard_map.146), channel_id=1, source_target_pairs={{1,2},{2,1},{0,4},{3,7},{5,6},{6,5},{4,0},{7,3},{9,10},{10,9},{8,1... | collective-permute-start | bytes 552968 | tf_op jit(solution)/shard_map/ppermute | solution.py:559
  102.6 13.1 %collective-permute-start.40 = (bf16[240,384]{1,0:T(8,128)(2,1)S(1)}, bf16[240,384]{1,0:T(8,128)(2,1)S(1)}, u32[]{:S(2)}, u32[]{:S(2)}) collective-permute-start(bf16[240,384]{1,0:T(8,128)(2,1)S(1)} %fusion.4), channel_id=1, source_target_pairs={{0,1},{1,0},{2,3},{3,2},{4,5},{5,4},{6,7},{7,6},{8,9},{9,8},{10,11... | collective-permute-start | bytes 552968 | tf_op jit(solution)/shard_map/ppermute | solution.py:32
  108.4 7.4 %collective-permute-start.41 = (bf16[240,384]{1,0:T(8,128)(2,1)S(1)}, bf16[240,384]{1,0:T(8,128)(2,1)S(1)}, u32[]{:S(2)}, u32[]{:S(2)}) collective-permute-start(bf16[240,384]{1,0:T(8,128)(2,1)S(1)} %fusion.10), channel_id=1, source_target_pairs={{1,2},{2,1},{0,4},{3,7},{5,6},{6,5},{4,0},{7,3},{9,10},{10,9},{8,1... | collective-permute-start | bytes 552968 | tf_op jit(solution)/shard_map/ppermute | solution.py:559
  111.1 9.6 %collective-permute-start.48 = (bf16[240,384]{1,0:T(8,128)(2,1)S(1)}, bf16[240,384]{1,0:T(8,128)(2,1)S(1)}, u32[]{:S(2)}, u32[]{:S(2)}) collective-permute-start(bf16[240,384]{1,0:T(8,128)(2,1)S(1)} %broadcast_select_fusion.3), channel_id=1, source_target_pairs={{0,1},{1,0},{2,3},{3,2},{4,5},{5,4},{6,7},{7,6},{8,9},{9,8},{10,11... | collective-permute-start | bytes 552968 | tf_op jit(solution)/shard_map/ppermute | solution.py:32
  112.7 8.0 %collective-permute-start.49 = (bf16[240,384]{1,0:T(8,128)(2,1)S(1)}, bf16[240,384]{1,0:T(8,128)(2,1)S(1)}, u32[]{:S(2)}, u32[]{:S(2)}) collective-permute-start(bf16[240,384]{1,0:T(8,128)(2,1)S(1)} %fusion.11), channel_id=1, source_target_pairs={{1,2},{2,1},{0,4},{3,7},{5,6},{6,5},{4,0},{7,3},{9,10},{10,9},{8,1... | collective-permute-start | bytes 552968 | tf_op jit(solution)/shard_map/ppermute | solution.py:559
  115.9 7.3 %collective-permute-start.43 = (bf16[240,384]{1,0:T(8,128)(2,1)S(1)}, bf16[240,384]{1,0:T(8,128)(2,1)S(1)}, u32[]{:S(2)}, u32[]{:S(2)}) collective-permute-start(bf16[240,384]{1,0:T(8,128)(2,1)S(1)} %get-tuple-element.174.refs_0_.refs_1_), channel_id=1, source_target_pairs={{1,2},{2,1},{0,4},{3,7},{5,6},{6,5},{4,0},{7,3},{9,10},{10,9},{8,1... | collective-permute-start | bytes 552968 | tf_op jit(solution)/shard_map/ppermute | solution.py:559
  116.5 10.2 %collective-permute-start.42 = (bf16[240,384]{1,0:T(8,128)(2,1)S(1)}, bf16[240,384]{1,0:T(8,128)(2,1)S(1)}, u32[]{:S(2)}, u32[]{:S(2)}) collective-permute-start(bf16[240,384]{1,0:T(8,128)(2,1)S(1)} %get-tuple-element.174.refs_0_.refs_1_), channel_id=1, source_target_pairs={{0,1},{1,0},{2,3},{3,2},{4,5},{5,4},{6,7},{7,6},{8,9},{9,8},{10,11... | collective-permute-start | bytes 552968 | tf_op jit(solution)/shard_map/ppermute | solution.py:32
  120.9 8.1 %collective-permute-start.50 = (bf16[240,384]{1,0:T(8,128)(2,1)S(1)}, bf16[240,384]{1,0:T(8,128)(2,1)S(1)}, u32[]{:S(2)}, u32[]{:S(2)}) collective-permute-start(bf16[240,384]{1,0:T(8,128)(2,1)S(1)} %get-tuple-element.191.refs_5_.refs_0_.refs_1_), channel_id=1, source_target_pairs={{0,1},{1,0},{2,3},{3,2},{4,5},{5,4},{6,7},{7,6},{8,9},{9,8},{10,11... | collective-permute-start | bytes 552968 | tf_op jit(solution)/shard_map/ppermute | solution.py:32
  120.9 5.8 %collective-permute-start.51 = (bf16[240,384]{1,0:T(8,128)(2,1)S(1)}, bf16[240,384]{1,0:T(8,128)(2,1)S(1)}, u32[]{:S(2)}, u32[]{:S(2)}) collective-permute-start(bf16[240,384]{1,0:T(8,128)(2,1)S(1)} %get-tuple-element.191.refs_5_.refs_0_.refs_1_), channel_id=1, source_target_pairs={{1,2},{2,1},{0,4},{3,7},{5,6},{6,5},{4,0},{7,3},{9,10},{10,9},{8,1... | collective-permute-start | bytes 552968 | tf_op jit(solution)/shard_map/ppermute | solution.py:559
  123.2 10.2 %collective-permute-start.44 = (bf16[240,384]{1,0:T(8,128)(2,1)S(1)}, bf16[240,384]{1,0:T(8,128)(2,1)S(1)}, u32[]{:S(2)}, u32[]{:S(2)}) collective-permute-start(bf16[240,384]{1,0:T(8,128)(2,1)S(1)} %broadcast_select_fusion.5), channel_id=1, source_target_pairs={{0,1},{1,0},{2,3},{3,2},{4,5},{5,4},{6,7},{7,6},{8,9},{9,8},{10,11... | collective-permute-start | bytes 552968 | tf_op jit(solution)/shard_map/ppermute | solution.py:32
  126.8 10.6 %collective-permute-start.52 = (bf16[240,384]{1,0:T(8,128)(2,1)S(1)}, bf16[240,384]{1,0:T(8,128)(2,1)S(1)}, u32[]{:S(2)}, u32[]{:S(2)}) collective-permute-start(bf16[240,384]{1,0:T(8,128)(2,1)S(1)} %broadcast_select_fusion.2), channel_id=1, source_target_pairs={{0,1},{1,0},{2,3},{3,2},{4,5},{5,4},{6,7},{7,6},{8,9},{9,8},{10,11... | collective-permute-start | bytes 552968 | tf_op jit(solution)/shard_map/ppermute | solution.py:32
  129.0 13.1 %collective-permute-start.46 = (bf16[240,384]{1,0:T(8,128)(2,1)S(1)}, bf16[240,384]{1,0:T(8,128)(2,1)S(1)}, u32[]{:S(2)}, u32[]{:S(2)}) collective-permute-start(bf16[240,384]{1,0:T(8,128)(2,1)S(1)} %broadcast_select_fusion.4), channel_id=1, source_target_pairs={{0,1},{1,0},{2,3},{3,2},{4,5},{5,4},{6,7},{7,6},{8,9},{9,8},{10,11... | collective-permute-start | bytes 552968 | tf_op jit(solution)/shard_map/ppermute | solution.py:32
  133.6 12.6 %collective-permute-start.54 = (bf16[240,384]{1,0:T(8,128)(2,1)S(1)}, bf16[240,384]{1,0:T(8,128)(2,1)S(1)}, u32[]{:S(2)}, u32[]{:S(2)}) collective-permute-start(bf16[240,384]{1,0:T(8,128)(2,1)S(1)} %broadcast_select_fusion.1), channel_id=1, source_target_pairs={{0,1},{1,0},{2,3},{3,2},{4,5},{5,4},{6,7},{7,6},{8,9},{9,8},{10,11... | collective-permute-start | bytes 552968 | tf_op jit(solution)/shard_map/ppermute | solution.py:32
  137.4 7.3 %collective-permute-start.58 = (bf16[240,384]{1,0:T(8,128)(2,1)S(1)}, bf16[240,384]{1,0:T(8,128)(2,1)S(1)}, u32[]{:S(2)}, u32[]{:S(2)}) collective-permute-start(bf16[240,384]{1,0:T(8,128)(2,1)S(1)} %shard_map.154), channel_id=1, source_target_pairs={{1,2},{2,1},{0,4},{3,7},{5,6},{6,5},{4,0},{7,3},{9,10},{10,9},{8,1... | collective-permute-start | bytes 552968 | tf_op jit(solution)/shard_map/ppermute | solution.py:559
  137.6 11.7 %collective-permute-start.56 = (bf16[240,384]{1,0:T(8,128)(2,1)S(1)}, bf16[240,384]{1,0:T(8,128)(2,1)S(1)}, u32[]{:S(2)}, u32[]{:S(2)}) collective-permute-start(bf16[240,384]{1,0:T(8,128)(2,1)S(1)} %fusion.5), channel_id=1, source_target_pairs={{0,1},{1,0},{2,3},{3,2},{4,5},{5,4},{6,7},{7,6},{8,9},{9,8},{10,11... | collective-permute-start | bytes 552968 | tf_op jit(solution)/shard_map/ppermute | solution.py:32
  142.2 7.1 %collective-permute-start.57 = (bf16[240,384]{1,0:T(8,128)(2,1)S(1)}, bf16[240,384]{1,0:T(8,128)(2,1)S(1)}, u32[]{:S(2)}, u32[]{:S(2)}) collective-permute-start(bf16[240,384]{1,0:T(8,128)(2,1)S(1)} %fusion.12), channel_id=1, source_target_pairs={{1,2},{2,1},{0,4},{3,7},{5,6},{6,5},{4,0},{7,3},{9,10},{10,9},{8,1... | collective-permute-start | bytes 552968 | tf_op jit(solution)/shard_map/ppermute | solution.py:559
  144.9 7.1 %collective-permute-start.59 = (bf16[240,384]{1,0:T(8,128)(2,1)S(1)}, bf16[240,384]{1,0:T(8,128)(2,1)S(1)}, u32[]{:S(2)}, u32[]{:S(2)}) collective-permute-start(bf16[240,384]{1,0:T(8,128)(2,1)S(1)} %broadcast_select_fusion), channel_id=1, source_target_pairs={{0,1},{1,0},{2,3},{3,2},{4,5},{5,4},{6,7},{7,6},{8,9},{9,8},{10,11... | collective-permute-start | bytes 552968 | tf_op jit(solution)/shard_map/ppermute | solution.py:32
  152.8 11.4 %collective-permute-start.66 = (bf16[256,384]{1,0:T(8,128)(2,1)S(1)}, bf16[256,384]{1,0:T(8,128)(2,1)S(1)}, u32[]{:S(2)}, u32[]{:S(2)}) collective-permute-start(bf16[256,384]{1,0:T(8,128)(2,1)S(1)} %get-tuple-element.216.refs_0_.refs_5_.refs_1_), channel_id=1, source_target_pairs={{0,1},{1,0},{2,3},{3,2},{4,5},{5,4},{6,7},{7,6},{8,9},{9,8},{10,11... | collective-permute-start | bytes 589832 | tf_op jit(solution)/shard_map/ppermute | solution.py:32
  154.7 9.0 %collective-permute-start.61 = (bf16[240,384]{1,0:T(8,128)(2,1)S(1)}, bf16[240,384]{1,0:T(8,128)(2,1)S(1)}, u32[]{:S(2)}, u32[]{:S(2)}) collective-permute-start(bf16[240,384]{1,0:T(8,128)(2,1)S(1)} %get-tuple-element.201.refs_0_.refs_1_), channel_id=1, source_target_pairs={{0,1},{1,0},{2,3},{3,2},{4,5},{5,4},{6,7},{7,6},{8,9},{9,8},{10,11... | collective-permute-start | bytes 552968 | tf_op jit(solution)/shard_map/ppermute | solution.py:32
  154.8 9.4 %collective-permute-start.62 = (bf16[240,384]{1,0:T(8,128)(2,1)S(1)}, bf16[240,384]{1,0:T(8,128)(2,1)S(1)}, u32[]{:S(2)}, u32[]{:S(2)}) collective-permute-start(bf16[240,384]{1,0:T(8,128)(2,1)S(1)} %get-tuple-element.201.refs_0_.refs_1_), channel_id=1, source_target_pairs={{1,2},{2,1},{0,4},{3,7},{5,6},{6,5},{4,0},{7,3},{9,10},{10,9},{8,1... | collective-permute-start | bytes 552968 | tf_op jit(solution)/shard_map/ppermute | solution.py:559
  163.7 9.0 %collective-permute-start.67 = (bf16[256,384]{1,0:T(8,128)(2,1)S(1)}, bf16[256,384]{1,0:T(8,128)(2,1)S(1)}, u32[]{:S(2)}, u32[]{:S(2)}) collective-permute-start(bf16[256,384]{1,0:T(8,128)(2,1)S(1)} %get-tuple-element.216.refs_0_.refs_5_.refs_1_), channel_id=1, source_target_pairs={{1,2},{2,1},{0,4},{3,7},{5,6},{6,5},{4,0},{7,3},{9,10},{10,9},{8,1... | collective-permute-start | bytes 589832 | tf_op jit(solution)/shard_map/ppermute | solution.py:559
  164.2 12.5 %collective-permute-start.69 = (bf16[256,384]{1,0:T(8,128)(2,1)S(1)}, bf16[256,384]{1,0:T(8,128)(2,1)S(1)}, u32[]{:S(2)}, u32[]{:S(2)}) collective-permute-start(bf16[256,384]{1,0:T(8,128)(2,1)S(1)} %collective-permute-done.66.refs_6_.refs_2_), channel_id=1, source_target_pairs={{1,2},{2,1},{0,4},{3,7},{5,6},{6,5},{4,0},{7,3},{9,10},{10,9},{8,1... | collective-permute-start | bytes 589832 | tf_op jit(solution)/shard_map/ppermute | solution.py:559
  164.2 16.8 %collective-permute-start.63 = (bf16[240,384]{1,0:T(8,128)(2,1)S(1)}, bf16[240,384]{1,0:T(8,128)(2,1)S(1)}, u32[]{:S(2)}, u32[]{:S(2)}) collective-permute-start(bf16[240,384]{1,0:T(8,128)(2,1)S(1)} %collective-permute-done.62.refs_4_), channel_id=1, source_target_pairs={{0,1},{1,0},{2,3},{3,2},{4,5},{5,4},{6,7},{7,6},{8,9},{9,8},{10,11... | collective-permute-start | bytes 552968 | tf_op jit(solution)/shard_map/ppermute | solution.py:32
  168.0 13.0 %collective-permute-start.65 = (bf16[240,384]{1,0:T(8,128)(2,1)S(1)}, bf16[240,384]{1,0:T(8,128)(2,1)S(1)}, u32[]{:S(2)}, u32[]{:S(2)}) collective-permute-start(bf16[240,384]{1,0:T(8,128)(2,1)S(1)} %collective-permute-done.64.refs_6_), channel_id=1, source_target_pairs={{0,1},{1,0},{2,3},{3,2},{4,5},{5,4},{6,7},{7,6},{8,9},{9,8},{10,11... | collective-permute-start | bytes 552968 | tf_op jit(solution)/shard_map/ppermute | solution.py:32
  172.7 10.9 %collective-permute-start.68 = (bf16[256,384]{1,0:T(8,128)(2,1)S(1)}, bf16[256,384]{1,0:T(8,128)(2,1)S(1)}, u32[]{:S(2)}, u32[]{:S(2)}) collective-permute-start(bf16[256,384]{1,0:T(8,128)(2,1)S(1)} %collective-permute-done.67.refs_8_.refs_4_), channel_id=1, source_target_pairs={{0,1},{1,0},{2,3},{3,2},{4,5},{5,4},{6,7},{7,6},{8,9},{9,8},{10,11... | collective-permute-start | bytes 589832 | tf_op jit(solution)/shard_map/ppermute | solution.py:32
  176.7 7.1 %collective-permute-start.70 = (bf16[256,384]{1,0:T(8,128)(2,1)S(1)}, bf16[256,384]{1,0:T(8,128)(2,1)S(1)}, u32[]{:S(2)}, u32[]{:S(2)}) collective-permute-start(bf16[256,384]{1,0:T(8,128)(2,1)S(1)} %collective-permute-done.69.refs_10_.refs_6_), channel_id=1, source_target_pairs={{0,1},{1,0},{2,3},{3,2},{4,5},{5,4},{6,7},{7,6},{8,9},{9,8},{10,11... | collective-permute-start | bytes 589832 | tf_op jit(solution)/shard_map/ppermute | solution.py:32
  189.8 9.2 %collective-permute-start.72 = (bf16[2,128,512]{2,1,0:T(8,128)(2,1)S(1)}, bf16[2,128,512]{2,1,0:T(8,128)(2,1)S(1)}, u32[]{:S(2)}, u32[]{:S(2)}) collective-permute-start(bf16[2,128,512]{2,1,0:T(8,128)(2,1)S(1)} %slice_bitcast_fusion), channel_id=1, source_target_pairs={{0,8},{4,12},{8,0},{12,4},{1,9},{5,13},{9,1},{13,5},{2,10},{6,14},... | collective-permute-start | bytes 786440 | tf_op jit(solution)/shard_map/ppermute | solution.py:32
  191.4 7.0 %collective-permute-start.74 = (f32[16,128]{1,0:T(8,128)S(1)}, f32[16,128]{1,0:T(8,128)S(1)}, u32[]{:S(2)}, u32[]{:S(2)}) collective-permute-start(f32[16,128]{1,0:T(8,128)S(1)} %slice_bitcast_fusion.4), channel_id=1, source_target_pairs={{0,8},{4,12},{8,0},{12,4},{1,9},{5,13},{9,1},{13,5},{2,10},{6,14},... | collective-permute-start | bytes 24584 | tf_op jit(solution)/shard_map/ppermute | solution.py:32
  (13 other events, 41.9 us)

commit v8 on v7

--- a/solution.py
+++ b/solution.py
@@ -218,6 +218,11 @@
     out[...] = (a[...].astype(F32) + b[...].astype(F32)).astype(out.dtype)
 
 
+def relay_kernel(deps, *refs):
+    value, out = refs[deps:]
+    out[...] = value[...]
+
+
 def part_of(scal, n, q, group, start, size):
     span = pl.ds(start, size)
     if len(group) == 1:
@@ -256,7 +261,7 @@
     eo[...], idl[...] = terms(scal, n, pieces, copies, gw, uw, dw)
 
 
-def out_kernel(n, expert, has_prev, last, sizes, deps, scal, *refs):
+def out_kernel(n, expert, has_prev, sizes, deps, scal, *refs):
     refs = refs[deps:]
     routes, eo, idl, refs = refs[0], refs[1], refs[2], refs[3:]
     routes = [routes.at[k] for k in range(n)]
@@ -264,15 +269,11 @@
         prev, refs = refs[:2], refs[2:]
     pieces, refs = split_pieces(refs, sizes)
     weights, (near, far, token, *refs) = refs[:3], refs[3:]
-    if last:
-        near_p, far_p, *refs, held = refs
     gw, uw, dw, sems, eo_ref, idl_ref = refs
     copies = weight_copies(expert, 1, weights, (gw, uw, dw), sems)
     token[...] = jnp.zeros_like(token)
     rows = eo.shape[0] // n
     spots = routing(scal, routes, expert, rows)
-    if last:
-        send_products(scal, routes, expert + 1, pieces, held, near_p, far_p)
     layer, back = terms(scal, n, pieces, copies, gw, uw, dw)
     eo_ref[...], idl_ref[...] = (eo[...] + layer).astype(BF16), (idl[...] + back).astype(BF16)
     for k, (position, weight, hit) in enumerate(spots):
@@ -300,8 +301,10 @@
     dg[0] = dot(load_rows(scal, n, 0, pieces), cot_ref[...], ((0,), (0,))).astype(BF16)
 
 
-def send_products(scal, routes, local, pieces, held, near, far):
-    n, (_, extra, lanes) = len(routes), held.shape
+def product_kernel(n, local, sizes, deps, scal, routes, *refs):
+    pieces, (near, far, held) = split_pieces(refs[deps:], sizes)
+    routes = [routes.at[k] for k in range(n)]
+    _, extra, lanes = held.shape
     first = pieces[0][0].shape[0] - extra
     for q, group in enumerate(pieces):
         held[q] = part_of(scal, n, q, group, first, extra)[:, 0:lanes]
@@ -499,11 +502,9 @@
     def out(e, begun, pieces, prev, deps):
         flat = [x for group in pieces for x in group]
         last = e == local - 1
-        dense_shape, sum_shape = (chips, experts_all, count), (chips, 2, count, width)
+        sum_shape = (chips, 2, count, width)
         return call(
-            functools.partial(
-                out_kernel, n, e, e > 0, last, [len(g) for g in pieces[1:]], len(deps)
-            ),
+            functools.partial(out_kernel, n, e, e > 0, [len(g) for g in pieces[1:]], len(deps)),
             1,
             [SMEM_SPEC]
             + [ANY_SPEC] * len(deps)
@@ -512,17 +513,11 @@
             + ([whole_spec(sum_shape)] * 2 if e > 0 else [])
             + [spec_of(x) for x in flat]
             + [HBM_SPEC] * 3,
-            [whole_spec(sum_shape)] * 2
-            + [whole_spec(TOKEN)]
-            + ([whole_spec(dense_shape)] * 2 if last else []),
-            [like(sum_shape, BF16 if last else F32)] * 2
-            + [like(TOKEN, F32)]
-            + ([like(dense_shape, F32)] * 2 if last else []),
+            [whole_spec(sum_shape)] * 2 + [whole_spec(TOKEN)],
+            [like(sum_shape, BF16 if last else F32)] * 2 + [like(TOKEN, F32)],
             3 * mac,
             2 * weight_bytes + len(flat) * piece_bytes,
-            scratch_shapes=held_weights
-            + [pltpu.VMEM(slot_shape, BF16)] * 2
-            + ([pltpu.VMEM((n, extra, 128), BF16)] if last else []),
+            scratch_shapes=held_weights + [pltpu.VMEM(slot_shape, BF16)] * 2,
         )(scal, *deps, routes, *begun, *prev, *flat, *weights)
 
     def grad(e, h, slots, pieces, prev, deps):
@@ -546,6 +541,33 @@
             input_output_aliases={base + k: k for k in range(len(prev))},
         )(scal, *slots, *deps, *flat, *prev)
 
+    def product_sums(pieces, deps):
+        flat = [x for group in pieces for x in group]
+        dense_shape = (chips, experts_all, count)
+        return call(
+            functools.partial(product_kernel, n, local, [len(g) for g in pieces[1:]], len(deps)),
+            1,
+            [SMEM_SPEC, whole_spec(route_shape)]
+            + [ANY_SPEC] * len(deps)
+            + [spec_of(x) for x in flat],
+            [whole_spec(dense_shape)] * 2,
+            [like(dense_shape, F32)] * 2,
+            local * all_rows * count * 16,
+            len(flat) * piece_bytes,
+            scratch_shapes=[pltpu.VMEM((n, extra, 128), BF16)],
+        )(scal, routes, *deps, *flat)
+
+    def relay(value, deps):
+        return call(
+            functools.partial(relay_kernel, len(deps)),
+            1,
+            [ANY_SPEC] * len(deps) + [spec_of(value)],
+            spec_of(value),
+            like(value.shape, value.dtype),
+            0,
+            2 * value.size * value.dtype.itemsize,
+        )(*deps, value)
+
     along_z = Line("dp", n, 1)
 
     def outer(value):
@@ -576,23 +598,29 @@
         for e in range(local):
             first, second, totals, halves = [], [], [], []
             following, seen = e < local - 1, [[], []]
+            if following:
+                next_slots, next0, token_0, _ = fill(e + 1, [] if e == 0 else [flight[0][2]])
             for h in range(2):
                 x = parts[h]
                 if e == 0:
                     first.append((outer(x[3]), None))
                 else:
                     y, got_a, got_b = flight[h]
+                    if h == 1 and following:
+                        x[3] = relay(x[3], [token_0])
                     first.append((outer(jnp.where(at_end, x[3], got_b)), inner(got_a)))
-            if following:
-                next_slots, next0, token_0, _ = fill(e + 1, [] if e == 0 else [flight[0][2]])
-                next1, token_1 = more(e + 1, next_slots, [first[0][0] if e == 0 else flight[1][2]])
-                seen = [[token_0], [token_1]]
             if grad_token is not None:
                 seen[0].append(grad_token)
+            if following and e == 0:
+                seen[0].append(token_0)
             for h in range(2):
                 x, (a1, b1) = parts[h], first[h]
                 send_a2 = x[2] if e == 0 else jnp.where(at_end, x[2], b1)
-                second.append((outer(send_a2), inner(add(x[3], a1, seen[h]))))
+                send_b2 = add(x[3], a1, seen[h])
+                second.append((outer(send_a2), inner(send_b2)))
+                if h == 0 and following:
+                    next1, token_1 = more(e + 1, next_slots, [send_b2])
+                    seen[1].append(token_1)
                 if e > 0:
                     y, got_a, got_b = flight[h]
                     halves.append([(y,), (got_a,), (a1, got_b), (second[h][0], b1)])
@@ -611,10 +639,11 @@
                 y, product = mid(e, h, totals[h], products, waits[h])
                 products.append(product)
                 flight[h] = (y, outer(y), inner(y))
-                if e > 0:
+                if e > 0 and following:
                     *grads, grad_token = grad(e - 1, h, arrived, halves[h], grads, [y])
                     if h == 0:
                         waits[1] = [grad_token]
+            late = (arrived, halves)
             arrived = slots
             if following:
                 slots, parts = next_slots, [next0, next1]
@@ -624,9 +653,10 @@
             a1, b1 = outer(got_b), inner(got_a)
             a2 = outer(b1)
             halves.append([(y,), (got_a,), (a1, got_b), (a2, b1)])
+        *grads, grad_token = grad(local - 2, 0, late[0], late[1][0], grads, [flight[0][1]])
         wait = [grad_token]
     else:
-        started = []
+        late, started = None, []
         for e in range(local):
             slots, x0, _, routes = fill(e, [])
             parts = [x0, more(e, slots, [])[0]]
@@ -644,9 +674,12 @@
                     *grads, _ = grad(e, h, arrived, halves[h], grads, [])
 
     *begun, _ = half(local - 1, halves[0], wait)
-    near, far, _, near_p, far_p = out(local - 1, begun, halves[1], sums, [])
+    near, far, _ = out(local - 1, begun, halves[1], sums, [])
+    near_p, far_p = product_sums(halves[1], [near])
     hop, home = send_home(near, far, add_rounded)
     _, per_expert = send_home(near_p, far_p, lambda a, b: add(a, b, [hop]))
+    if late is not None:
+        *grads, _ = grad(local - 2, 1, late[0], late[1][1], grads, [hop])
     for h in range(2):
         *grads, _ = grad(local - 1, h, arrived, halves[h], grads, [hop])
     combine_grad = jnp.sum(jnp.where(named, per_expert[None], 0.0), axis=1) / combine_t

time: 200 us -> 215 us (1.075)
  waiting for transfers between devices: 30.3 us -> 47.9 us
  starting transfers between devices: 100 us -> 96.3 us
    ppermute x43, waiting for transfers between devices: 29.6 us -> 47.8 us  [send(): return lax.ppermute(value, self.axis, wide)]
    ppermute x43, starting transfers between devices: 97.4 us -> 92.4 us  [send(): return lax.ppermute(value, self.axis, wide)]
    pallas_call x4 -> x7, Pallas kernels: 12.6 us -> 13.5 us  [the longest x4 11.9 us: out(): call(functools.partial(out_kernel, n, e, e > 0, [len(g) for g in pieces[1...]
  transfers between devices with their start and end apart: 75 -> 75, of which waited for: 14 -> 21; matrix products, arithmetic and copies ran while one was open for 1% -> 1% of each run, Pallas kernels for 28% -> 27%
where the time goes in v8:
time: 215 us; the launch traced here: 214 us
  starting transfers between devices  96.3 us (45%)
  Pallas kernels  65.6 us (31%)
  waiting for transfers between devices  47.9 us (22%)
    ppermute x43, starting transfers between devices, send(): return lax.ppermute(value, self.axis, wide)  92.4 us
    ppermute x43, waiting for transfers between devices, send(): return lax.ppermute(value, self.axis, wide)  47.8 us
    pallas_call x8, Pallas kernels, grad(): call(functools.partial(grad_kernel, n, len(prev) > 0, [len(g) for g in pi...  17.4 us
    pallas_call x4, Pallas kernels, fill(): call(functools.partial(fill_kernel, n, e, choose, len(deps)), 1, [SMEM_SP...  13 us
    pallas_call x4, Pallas kernels, out(): call(functools.partial(out_kernel, n, e, e > 0, [len(g) for g in pieces[1...  11.9 us
    pallas_call x4, Pallas kernels, half(): call(functools.partial(half_kernel, n, e, [len(g) for g in pieces[1:]], l...  10 us
    pallas_call x4, Pallas kernels, more(): call(functools.partial(more_kernel, n, e, len(deps)), 1, [ANY_SPEC] * len...  8.18 us
  transfers between devices with their start and end apart: 75, of which 21 were waited for; matrix products, arithmetic and copies ran while one was open for 1% of the time, Pallas kernels for 27%

profile of v8, /device:TPU:0, one launch (start us, length us, event | category | flops | bytes accessed | tf_op | source)
XLA Modules:
  0.0 214.0 jit_solution(17431892196569553986)
XLA Ops:
  1.7 3.0 %collective-permute-start = (bf16[272,512]{1,0:T(8,128)(2,1)S(1)}, bf16[272,512]{1,0:T(8,128)(2,1)S(1)}, u32[]{:S(2)}, u32[]{:S(2)}) collective-permute-start(bf16[272,512]{1,0:T(8,128)(2,1)S(1)} %shard_map.118.refs_0_.refs_1_), channel_id=1, source_target_pairs={{0,8},{4,12},{8,0},{12,4},{1,9},{5,13},{9,1},{13,5},{2,10},{6,14},... | collective-permute-start | bytes 835592 | tf_op jit(solution)/shard_map/ppermute | solution.py:32
  4.7 6.7 %collective-permute-done.refs_1_.refs_2_ = bf16[272,512]{1,0:T(8,128)(2,1)S(1)} collective-permute-done((bf16[272,512]{1,0:T(8,128)(2,1)S(1)}, bf16[272,512]{1,0:T(8,128)(2,1)S(1)}, u32[]{:S(2)}, u32[]{:S(2)}) %collective-permute-start) | collective-permute-done | bytes 278560 | tf_op jit(solution)/shard_map/ppermute | solution.py:32
  12.9 3.2 %shard_map.119 = (bf16[320,512]{1,0:T(8,128)(2,1)S(1)}, bf16[320,512]{1,0:T(8,128)(2,1)S(1)}, bf16[240,384]{1,0:T(8,128)(2,1)S(1)}, bf16[240,384]{1,0:T(8,128)(2...) custom-call(s32[10]{0:T(128)S(1)} %stack.35.scal, ...), custom_call_target="tpu_custom_call" | custom-call | flops 377487360 | bytes 2310144 | tf_op jit(solution)/shard_map/pallas_call | solution.py:434
  16.1 1.9 collective-permute-start.6
  18.2 2.4 %shard_map.125 = (bf16[240,384]{1,0:T(8,128)(2,1)S(1)}, bf16[240,384]{1,0:T(8,128)(2,1)S(1)}, bf16[240,384]{1,0:T(8,128)(2,1)S(1)}, bf16[240,384]{1,0:T(8,128)(2,1)S(1)}, f32[8,128]{1,0:T(8,128)}) custom-call(bf16[320,512]{1,0:T(8,128)(2,1)S(1)} %get-tuple-element.134.refs_0_.in_ref, bf16[320,512]{1,0:T(8,128)(2,1)S(1)} %get-tuple-element.135.refs_1_.cot_ref, ...), custom_call_target="tpu_custom_call" | custom-call | flops 377487360 | bytes 2310144 | tf_op jit(solution)/shard_map/pallas_call | solution.py:451
  20.6 1.9 collective-permute-start.16
  22.7 3.2 %shard_map.120 = (bf16[320,512]{1,0:T(8,128)(2,1)S(1)}, bf16[320,512]{1,0:T(8,128)(2,1)S(1)}, bf16[240,384]{1,0:T(8,128)(2,1)S(1)}, bf16[240,384]{1,0:T(8,128)(2...) custom-call(s32[10]{0:T(128)S(1)} %stack.35.scal, ...), custom_call_target="tpu_custom_call" | custom-call | flops 377487360 | bytes 2310144 | tf_op jit(solution)/shard_map/pallas_call | solution.py:434
  26.1 1.5 collective-permute-done.3.refs_2_
  27.7 3.8 %collective-permute-done.16 = bf16[240,384]{1,0:T(8,128)(2,1)S(1)} collective-permute-done((bf16[240,384]{1,0:T(8,128)(2,1)S(1)}, bf16[240,384]{1,0:T(8,128)(2,1)S(1)}, u32[]{:S(2)}, u32[]{:S(2)}) %collective-permute-start.16) | collective-permute-done | bytes 184352 | tf_op jit(solution)/shard_map/ppermute | solution.py:32
  31.7 1.9 shard_map.126
  35.0 4.5 %collective-permute-start.5 = (bf16[240,384]{1,0:T(8,128)(2,1)S(1)}, bf16[240,384]{1,0:T(8,128)(2,1)S(1)}, u32[]{:S(2)}, u32[]{:S(2)}) collective-permute-start(bf16[240,384]{1,0:T(8,128)(2,1)S(1)} %fusion.1), channel_id=1, source_target_pairs={{0,1},{1,0},{2,3},{3,2},{4,5},{5,4},{6,7},{7,6},{8,9},{9,8},{10,11... | collective-permute-start | bytes 552968 | tf_op jit(solution)/shard_map/ppermute | solution.py:32
  39.6 5.8 %collective-permute-start.15 = (bf16[240,384]{1,0:T(8,128)(2,1)S(1)}, bf16[240,384]{1,0:T(8,128)(2,1)S(1)}, u32[]{:S(2)}, u32[]{:S(2)}) collective-permute-start(bf16[240,384]{1,0:T(8,128)(2,1)S(1)} %fusion.2), channel_id=1, source_target_pairs={{0,1},{1,0},{2,3},{3,2},{4,5},{5,4},{6,7},{7,6},{8,9},{9,8},{10,11... | collective-permute-start | bytes 552968 | tf_op jit(solution)/shard_map/ppermute | solution.py:32
  45.7 1.6 collective-permute-start.9
  47.3 3.1 %collective-permute-done.15.refs_1_ = bf16[240,384]{1,0:T(8,128)(2,1)S(1)} collective-permute-done((bf16[240,384]{1,0:T(8,128)(2,1)S(1)}, bf16[240,384]{1,0:T(8,128)(2,1)S(1)}, u32[]{:S(2)}, u32[]{:S(2)}) %collective-permute-start.15) | collective-permute-done | bytes 184352 | tf_op jit(solution)/shard_map/ppermute | solution.py:32
  50.6 4.0 %collective-permute-start.18 = (bf16[240,384]{1,0:T(8,128)(2,1)S(1)}, bf16[240,384]{1,0:T(8,128)(2,1)S(1)}, u32[]{:S(2)}, u32[]{:S(2)}) collective-permute-start(bf16[240,384]{1,0:T(8,128)(2,1)S(1)} %get-tuple-element.143.refs_3_.refs_1_), channel_id=1, source_target_pairs={{0,1},{1,0},{2,3},{3,2},{4,5},{5,4},{6,7},{7,6},{8,9},{9,8},{10,11... | collective-permute-start | bytes 552968 | tf_op jit(solution)/shard_map/ppermute | solution.py:32
  54.8 3.3 %shard_map.123 = (bf16[320,512]{1,0:T(8,128)(2,1)S(1)}, bf16[320,512]{1,0:T(8,128)(2,1)S(1)}, bf16[240,384]{1,0:T(8,128)(2,1)S(1)}, bf16[240,384]{1,0:T(8,128)(2...) custom-call(s32[10]{0:T(128)S(1)} %stack.35.scal, ...), custom_call_target="tpu_custom_call" | custom-call | flops 377487360 | bytes 2310144 | tf_op jit(solution)/shard_map/pallas_call | solution.py:434
  58.1 2.1 collective-permute-start.20
  60.7 2.9 %collective-permute-done.10.refs_2_.refs_1_.refs_3_ = bf16[240,384]{1,0:T(8,128)(2,1)S(1)} collective-permute-done((bf16[240,384]{1,0:T(8,128)(2,1)S(1)}, bf16[240,384]{1,0:T(8,128)(2,1)S(1)}, u32[]{:S(2)}, u32[]{:S(2)}) %collective-permute-start.10) | collective-permute-done | bytes 184352 | tf_op jit(solution)/shard_map/ppermute | solution.py:32
  63.7 1.9 shard_map.135
  66.3 2.8 %collective-permute-start.12 = (bf16[240,384]{1,0:T(8,128)(2,1)S(1)}, bf16[240,384]{1,0:T(8,128)(2,1)S(1)}, u32[]{:S(2)}, u32[]{:S(2)}) collective-permute-start(bf16[240,384]{1,0:T(8,128)(2,1)S(1)} %broadcast_select_fusion.13), channel_id=1, source_target_pairs={{0,1},{1,0},{2,3},{3,2},{4,5},{5,4},{6,7},{7,6},{8,9},{9,8},{10,11... | collective-permute-start | bytes 552968 | tf_op jit(solution)/shard_map/ppermute | solution.py:32
  69.1 2.8 %collective-permute-start.22 = (bf16[240,384]{1,0:T(8,128)(2,1)S(1)}, bf16[240,384]{1,0:T(8,128)(2,1)S(1)}, u32[]{:S(2)}, u32[]{:S(2)}) collective-permute-start(bf16[240,384]{1,0:T(8,128)(2,1)S(1)} %broadcast_select_fusion.11), channel_id=1, source_target_pairs={{0,1},{1,0},{2,3},{3,2},{4,5},{5,4},{6,7},{7,6},{8,9},{9,8},{10,11... | collective-permute-start | bytes 552968 | tf_op jit(solution)/shard_map/ppermute | solution.py:32
  71.9 2.8 %collective-permute-done.12.refs_4_.refs_5_ = bf16[240,384]{1,0:T(8,128)(2,1)S(1)} collective-permute-done((bf16[240,384]{1,0:T(8,128)(2,1)S(1)}, bf16[240,384]{1,0:T(8,128)(2,1)S(1)}, u32[]{:S(2)}, u32[]{:S(2)}) %collective-permute-start.12) | collective-permute-done | bytes 184352 | tf_op jit(solution)/shard_map/ppermute | solution.py:32
  74.7 2.5 %shard_map.124 = (f32[320,512]{1,0:T(8,128)S(1)}, f32[320,512]{1,0:T(8,128)S(1)}, f32[8,128]{1,0:T(8,128)S(1)}) custom-call(s32[10]{0:T(128)S(1)} %stack.35.scal, bf16[240,384]{1,0:T(8,128)(2,1)S(1)} %get-tuple-element.127.refs_0_.refs_1_, bf16[240,384]{1,0:T(8,128)(2,1)S(1)} %collective-permute-done.9.refs_1_.refs_2_, ...), custom_call_target="tpu_custom_call" | custom-call | flops 377487360 | bytes 2678784 | tf_op jit(solution)/shard_map/pallas_call | solution.py:491
  80.3 2.9 %shard_map.130 = (f32[2,2,128,512]{3,2,1,0:T(8,128)S(1)}, f32[2,2,128,512]{3,2,1,0:T(8,128)S(1)}, f32[8,128]{1,0:T(8,128)S(1)}) custom-call(s32[10]{0:T(128)S(1)} %stack.35.scal, f32[4,16,128]{2,1,0:T(8,128)S(1)} %get-tuple-element.121.refs_0_.routes, f32[320,512]{1,0:T(8,128)S(1)} %get-tuple-element.132.refs_1_, f32[320,512]{1,0:T(8,128)S(1)} %get-tuple-element.133.refs_2_, ...), custom_call_target="tpu_custom_call" | custom-call | flops 377487360 | bytes 2678784 | tf_op jit(solution)/shard_map/pallas_call | solution.py:506
  83.2 1.6 collective-permute-done.24.refs_2_
  85.1 2.2 %shard_map.134 = (bf16[4,512,768]{2,1,0:T(8,128)(2,1)}, bf16[4,512,768]{2,1,0:T(8,128)(2,1)}, bf16[4,768,512]{2,1,0:T(8,128)(2,1)}, f32[8,128]{1,0:T(8,128)S(1)}) custom-call(s32[10]{0:T(128)S(1)} %stack.35.scal, bf16[320,512]{1,0:T(8,128)(2,1)S(1)} %get-tuple-element.134.refs_0_.in_ref, bf16[320,512]{1,0:T(8,128)(2,1)S(1)} %get-tuple-element.135.refs_1_.cot_ref, ...), custom_call_target="tpu_custom_call" | custom-call | flops 377487360 | bytes 2678784 | tf_op jit(solution)/shard_map/pallas_call | solution.py:527
  87.4 4.3 %collective-permute-start.34 = (bf16[240,384]{1,0:T(8,128)(2,1)S(1)}, bf16[240,384]{1,0:T(8,128)(2,1)S(1)}, u32[]{:S(2)}, u32[]{:S(2)}) collective-permute-start(bf16[240,384]{1,0:T(8,128)(2,1)S(1)} %get-tuple-element.162.refs_5_.refs_0_.refs_1_), channel_id=1, source_target_pairs={{0,1},{1,0},{2,3},{3,2},{4,5},{5,4},{6,7},{7,6},{8,9},{9,8},{10,11... | collective-permute-start | bytes 552968 | tf_op jit(solution)/shard_map/ppermute | solution.py:32
  92.2 2.2 %shard_map.142 = (bf16[4,512,768]{2,1,0:T(8,128)(2,1)}, bf16[4,512,768]{2,1,0:T(8,128)(2,1)}, bf16[4,768,512]{2,1,0:T(8,128)(2,1)}, f32[8,128]{1,0:T(8,128)S(1)}) custom-call(s32[10]{0:T(128)S(1)} %stack.35.scal, bf16[320,512]{1,0:T(8,128)(2,1)S(1)} %get-tuple-element.134.refs_0_.in_ref, ...), custom_call_target="tpu_custom_call", output_to_operand_aliasing={{0}: (10, {}), {1}: (11, {}), {2}: (12, {})} | custom-call | flops 377487360 | bytes 2678784 | tf_op jit(solution)/shard_map/pallas_call | solution.py:527
  94.4 1.7 collective-permute-start.28
  96.1 3.2 %shard_map.139 = (bf16[320,512]{1,0:T(8,128)(2,1)S(1)}, bf16[320,512]{1,0:T(8,128)(2,1)S(1)}, bf16[240,384]{1,0:T(8,128)(2,1)S(1)}, bf16[240,384]{1,0:T(8,128)(2...) custom-call(s32[10]{0:T(128)S(1)} %stack.35.scal, ...), custom_call_target="tpu_custom_call" | custom-call | flops 377487360 | bytes 2310144 | tf_op jit(solution)/shard_map/pallas_call | solution.py:434
  99.5 2.1 %collective-permute-start.36 = (bf16[240,384]{1,0:T(8,128)(2,1)S(1)}, bf16[240,384]{1,0:T(8,128)(2,1)S(1)}, u32[]{:S(2)}, u32[]{:S(2)}) collective-permute-start(bf16[240,384]{1,0:T(8,128)(2,1)S(1)} %broadcast_select_fusion.7), channel_id=1, source_target_pairs={{0,1},{1,0},{2,3},{3,2},{4,5},{5,4},{6,7},{7,6},{8,9},{9,8},{10,11... | collective-permute-start | bytes 552968 | tf_op jit(solution)/shard_map/ppermute | solution.py:32
  101.7 5.8 %collective-permute-start.38 = (bf16[240,384]{1,0:T(8,128)(2,1)S(1)}, bf16[240,384]{1,0:T(8,128)(2,1)S(1)}, u32[]{:S(2)}, u32[]{:S(2)}) collective-permute-start(bf16[240,384]{1,0:T(8,128)(2,1)S(1)} %broadcast_select_fusion.6), channel_id=1, source_target_pairs={{0,1},{1,0},{2,3},{3,2},{4,5},{5,4},{6,7},{7,6},{8,9},{9,8},{10,11... | collective-permute-start | bytes 552968 | tf_op jit(solution)/shard_map/ppermute | solution.py:32
  107.6 1.9 shard_map.147
  110.2 1.6 collective-permute-start.30
  112.0 3.4 %collective-permute-start.40 = (bf16[240,384]{1,0:T(8,128)(2,1)S(1)}, bf16[240,384]{1,0:T(8,128)(2,1)S(1)}, u32[]{:S(2)}, u32[]{:S(2)}) collective-permute-start(bf16[240,384]{1,0:T(8,128)(2,1)S(1)} %fusion.4), channel_id=1, source_target_pairs={{0,1},{1,0},{2,3},{3,2},{4,5},{5,4},{6,7},{7,6},{8,9},{9,8},{10,11... | collective-permute-start | bytes 552968 | tf_op jit(solution)/shard_map/ppermute | solution.py:32
  115.4 2.4 %collective-permute-done.30.refs_4_.refs_5_ = bf16[240,384]{1,0:T(8,128)(2,1)S(1)} collective-permute-done((bf16[240,384]{1,0:T(8,128)(2,1)S(1)}, bf16[240,384]{1,0:T(8,128)(2,1)S(1)}, u32[]{:S(2)}, u32[]{:S(2)}) %collective-permute-start.30) | collective-permute-done | bytes 184352 | tf_op jit(solution)/shard_map/ppermute | solution.py:32
  117.9 2.5 %shard_map.133 = (f32[320,512]{1,0:T(8,128)S(1)}, f32[320,512]{1,0:T(8,128)S(1)}, f32[8,128]{1,0:T(8,128)S(1)}) custom-call(s32[10]{0:T(128)S(1)} %stack.35.scal, bf16[240,384]{1,0:T(8,128)(2,1)S(1)} %get-tuple-element.150.refs_0_.refs_1_, bf16[240,384]{1,0:T(8,128)(2,1)S(1)} %collective-permute-done.26.refs_1_.refs_2_, ...), custom_call_target="tpu_custom_call" | custom-call | flops 377487360 | bytes 2678784 | tf_op jit(solution)/shard_map/pallas_call | solution.py:491
  120.5 3.1 %collective-permute-start.48 = (bf16[240,384]{1,0:T(8,128)(2,1)S(1)}, bf16[240,384]{1,0:T(8,128)(2,1)S(1)}, u32[]{:S(2)}, u32[]{:S(2)}) collective-permute-start(bf16[240,384]{1,0:T(8,128)(2,1)S(1)} %broadcast_select_fusion.3), channel_id=1, source_target_pairs={{0,1},{1,0},{2,3},{3,2},{4,5},{5,4},{6,7},{7,6},{8,9},{9,8},{10,11... | collective-permute-start | bytes 552968 | tf_op jit(solution)/shard_map/ppermute | solution.py:32
  123.6 3.0 %shard_map.141 = (f32[2,2,128,512]{3,2,1,0:T(8,128)S(1)}, f32[2,2,128,512]{3,2,1,0:T(8,128)S(1)}, f32[8,128]{1,0:T(8,128)S(1)}) custom-call(s32[10]{0:T(128)S(1)} %stack.35.scal, f32[4,16,128]{2,1,0:T(8,128)S(1)} %get-tuple-element.121.refs_0_.routes, f32[320,512]{1,0:T(8,128)S(1)} %get-tuple-element.153.refs_1_, f32[320,512]{1,0:T(8,128)S(1)} %get-tuple-element.154.refs_2_, ...), custom_call_target="tpu_custom_call" | custom-call | flops 377487360 | bytes 2678784 | tf_op jit(solution)/shard_map/pallas_call | solution.py:506
  126.7 2.2 %shard_map.146 = (bf16[4,512,768]{2,1,0:T(8,128)(2,1)}, bf16[4,512,768]{2,1,0:T(8,128)(2,1)}, bf16[4,768,512]{2,1,0:T(8,128)(2,1)}, f32[8,128]{1,0:T(8,128)S(1)}) custom-call(s32[10]{0:T(128)S(1)} %stack.35.scal, bf16[320,512]{1,0:T(8,128)(2,1)S(1)} %get-tuple-element.138.refs_1_.in_ref, ...), custom_call_target="tpu_custom_call", output_to_operand_aliasing={{0}: (10, {}), {1}: (11, {}), {2}: (12, {})} | custom-call | flops 377487360 | bytes 2678784 | tf_op jit(solution)/shard_map/pallas_call | solution.py:527
  131.3 2.2 %shard_map.152 = (bf16[4,512,768]{2,1,0:T(8,128)(2,1)}, bf16[4,512,768]{2,1,0:T(8,128)(2,1)}, bf16[4,768,512]{2,1,0:T(8,128)(2,1)}, f32[8,128]{1,0:T(8,128)S(1)}) custom-call(s32[10]{0:T(128)S(1)} %stack.35.scal, bf16[320,512]{1,0:T(8,128)(2,1)S(1)} %get-tuple-element.138.refs_1_.in_ref, ...), custom_call_target="tpu_custom_call", output_to_operand_aliasing={{0}: (10, {}), {1}: (11, {}), {2}: (12, {})} | custom-call | flops 377487360 | bytes 2678784 | tf_op jit(solution)/shard_map/pallas_call | solution.py:527
  133.5 2.4 %collective-permute-start.52 = (bf16[240,384]{1,0:T(8,128)(2,1)S(1)}, bf16[240,384]{1,0:T(8,128)(2,1)S(1)}, u32[]{:S(2)}, u32[]{:S(2)}) collective-permute-start(bf16[240,384]{1,0:T(8,128)(2,1)S(1)} %broadcast_select_fusion.2), channel_id=1, source_target_pairs={{0,1},{1,0},{2,3},{3,2},{4,5},{5,4},{6,7},{7,6},{8,9},{9,8},{10,11... | collective-permute-start | bytes 552968 | tf_op jit(solution)/shard_map/ppermute | solution.py:32
  136.7 2.6 %collective-permute-start.44 = (bf16[240,384]{1,0:T(8,128)(2,1)S(1)}, bf16[240,384]{1,0:T(8,128)(2,1)S(1)}, u32[]{:S(2)}, u32[]{:S(2)}) collective-permute-start(bf16[240,384]{1,0:T(8,128)(2,1)S(1)} %broadcast_select_fusion.5), channel_id=1, source_target_pairs={{0,1},{1,0},{2,3},{3,2},{4,5},{5,4},{6,7},{7,6},{8,9},{9,8},{10,11... | collective-permute-start | bytes 552968 | tf_op jit(solution)/shard_map/ppermute | solution.py:32
  140.6 3.0 %collective-permute-start.54 = (bf16[240,384]{1,0:T(8,128)(2,1)S(1)}, bf16[240,384]{1,0:T(8,128)(2,1)S(1)}, u32[]{:S(2)}, u32[]{:S(2)}) collective-permute-start(bf16[240,384]{1,0:T(8,128)(2,1)S(1)} %broadcast_select_fusion.1), channel_id=1, source_target_pairs={{0,1},{1,0},{2,3},{3,2},{4,5},{5,4},{6,7},{7,6},{8,9},{9,8},{10,11... | collective-permute-start | bytes 552968 | tf_op jit(solution)/shard_map/ppermute | solution.py:32
  144.7 2.9 %collective-permute-start.46 = (bf16[240,384]{1,0:T(8,128)(2,1)S(1)}, bf16[240,384]{1,0:T(8,128)(2,1)S(1)}, u32[]{:S(2)}, u32[]{:S(2)}) collective-permute-start(bf16[240,384]{1,0:T(8,128)(2,1)S(1)} %broadcast_select_fusion.4), channel_id=1, source_target_pairs={{0,1},{1,0},{2,3},{3,2},{4,5},{5,4},{6,7},{7,6},{8,9},{9,8},{10,11... | collective-permute-start | bytes 552968 | tf_op jit(solution)/shard_map/ppermute | solution.py:32
  148.6 3.8 %collective-permute-done.54.refs_9_.refs_5_ = bf16[240,384]{1,0:T(8,128)(2,1)S(1)} collective-permute-done((bf16[240,384]{1,0:T(8,128)(2,1)S(1)}, bf16[240,384]{1,0:T(8,128)(2,1)S(1)}, u32[]{:S(2)}, u32[]{:S(2)}) %collective-permute-start.54) | collective-permute-done | bytes 184352 | tf_op jit(solution)/shard_map/ppermute | solution.py:32
  152.7 3.0 %collective-permute-start.56 = (bf16[240,384]{1,0:T(8,128)(2,1)S(1)}, bf16[240,384]{1,0:T(8,128)(2,1)S(1)}, u32[]{:S(2)}, u32[]{:S(2)}) collective-permute-start(bf16[240,384]{1,0:T(8,128)(2,1)S(1)} %fusion.5), channel_id=1, source_target_pairs={{0,1},{1,0},{2,3},{3,2},{4,5},{5,4},{6,7},{7,6},{8,9},{9,8},{10,11... | collective-permute-start | bytes 552968 | tf_op jit(solution)/shard_map/ppermute | solution.py:32
  156.2 2.5 %shard_map.145 = (f32[320,512]{1,0:T(8,128)S(1)}, f32[320,512]{1,0:T(8,128)S(1)}, f32[8,128]{1,0:T(8,128)S(1)}) custom-call(s32[10]{0:T(128)S(1)} %stack.35.scal, bf16[240,384]{1,0:T(8,128)(2,1)S(1)} %get-tuple-element.173.refs_0_.refs_1_, bf16[240,384]{1,0:T(8,128)(2,1)S(1)} %collective-permute-done.42.refs_1_.refs_2_, ...), custom_call_target="tpu_custom_call" | custom-call | flops 377487360 | bytes 2678784 | tf_op jit(solution)/shard_map/pallas_call | solution.py:491
  158.8 2.2 %collective-permute-start.64 = (bf16[240,384]{1,0:T(8,128)(2,1)S(1)}, bf16[240,384]{1,0:T(8,128)(2,1)S(1)}, u32[]{:S(2)}, u32[]{:S(2)}) collective-permute-start(bf16[240,384]{1,0:T(8,128)(2,1)S(1)} %broadcast_select_fusion), channel_id=1, source_target_pairs={{0,1},{1,0},{2,3},{3,2},{4,5},{5,4},{6,7},{7,6},{8,9},{9,8},{10,11... | collective-permute-start | bytes 552968 | tf_op jit(solution)/shard_map/ppermute | solution.py:32
  161.0 2.9 %shard_map.151 = (f32[2,2,128,512]{3,2,1,0:T(8,128)S(1)}, f32[2,2,128,512]{3,2,1,0:T(8,128)S(1)}, f32[8,128]{1,0:T(8,128)S(1)}) custom-call(s32[10]{0:T(128)S(1)} %stack.35.scal, f32[4,16,128]{2,1,0:T(8,128)S(1)} %get-tuple-element.121.refs_0_.routes, f32[320,512]{1,0:T(8,128)S(1)} %get-tuple-element.176.refs_1_, f32[320,512]{1,0:T(8,128)S(1)} %get-tuple-element.177.refs_2_, ...), custom_call_target="tpu_custom_call" | custom-call | flops 377487360 | bytes 2678784 | tf_op jit(solution)/shard_map/pallas_call | solution.py:506
  164.1 1.8 collective-permute-done.64.refs_1_
  168.7 8.3 %collective-permute-done.58.refs_0_.refs_2_ = bf16[240,384]{1,0:T(8,128)(2,1)S(1)} collective-permute-done((bf16[240,384]{1,0:T(8,128)(2,1)S(1)}, bf16[240,384]{1,0:T(8,128)(2,1)S(1)}, u32[]{:S(2)}, u32[]{:S(2)}) %collective-permute-start.58) | collective-permute-done | bytes 184352 | tf_op jit(solution)/shard_map/ppermute | solution.py:32
  177.6 4.1 %collective-permute-start.60 = (bf16[240,384]{1,0:T(8,128)(2,1)S(1)}, bf16[240,384]{1,0:T(8,128)(2,1)S(1)}, u32[]{:S(2)}, u32[]{:S(2)}) collective-permute-start(bf16[240,384]{1,0:T(8,128)(2,1)S(1)} %collective-permute-done.59.refs_4_), channel_id=1, source_target_pairs={{0,1},{1,0},{2,3},{3,2},{4,5},{5,4},{6,7},{7,6},{8,9},{9,8},{10,11... | collective-permute-start | bytes 552968 | tf_op jit(solution)/shard_map/ppermute | solution.py:32
  181.7 3.5 %collective-permute-start.62 = (bf16[240,384]{1,0:T(8,128)(2,1)S(1)}, bf16[240,384]{1,0:T(8,128)(2,1)S(1)}, u32[]{:S(2)}, u32[]{:S(2)}) collective-permute-start(bf16[240,384]{1,0:T(8,128)(2,1)S(1)} %collective-permute-done.61.refs_6_), channel_id=1, source_target_pairs={{0,1},{1,0},{2,3},{3,2},{4,5},{5,4},{6,7},{7,6},{8,9},{9,8},{10,11... | collective-permute-start | bytes 552968 | tf_op jit(solution)/shard_map/ppermute | solution.py:32
  185.2 4.2 %collective-permute-start.68 = (bf16[256,384]{1,0:T(8,128)(2,1)S(1)}, bf16[256,384]{1,0:T(8,128)(2,1)S(1)}, u32[]{:S(2)}, u32[]{:S(2)}) collective-permute-start(bf16[256,384]{1,0:T(8,128)(2,1)S(1)} %collective-permute-done.67.refs_8_.refs_4_), channel_id=1, source_target_pairs={{0,1},{1,0},{2,3},{3,2},{4,5},{5,4},{6,7},{7,6},{8,9},{9,8},{10,11... | collective-permute-start | bytes 589832 | tf_op jit(solution)/shard_map/ppermute | solution.py:32
  189.4 2.4 %collective-permute-start.70 = (bf16[256,384]{1,0:T(8,128)(2,1)S(1)}, bf16[256,384]{1,0:T(8,128)(2,1)S(1)}, u32[]{:S(2)}, u32[]{:S(2)}) collective-permute-start(bf16[256,384]{1,0:T(8,128)(2,1)S(1)} %collective-permute-done.69.refs_10_.refs_6_), channel_id=1, source_target_pairs={{0,1},{1,0},{2,3},{3,2},{4,5},{5,4},{6,7},{7,6},{8,9},{9,8},{10,11... | collective-permute-start | bytes 589832 | tf_op jit(solution)/shard_map/ppermute | solution.py:32
  191.7 2.2 %shard_map.155 = (bf16[4,512,768]{2,1,0:T(8,128)(2,1)}, bf16[4,512,768]{2,1,0:T(8,128)(2,1)}, bf16[4,768,512]{2,1,0:T(8,128)(2,1)}, f32[8,128]{1,0:T(8,128)S(1)}) custom-call(s32[10]{0:T(128)S(1)} %stack.35.scal, bf16[320,512]{1,0:T(8,128)(2,1)S(1)} %get-tuple-element.128.refs_1_.in_ref, ...), custom_call_target="tpu_custom_call", output_to_operand_aliasing={{0}: (10, {}), {1}: (11, {}), {2}: (12, {})} | custom-call | flops 377487360 | bytes 2678784 | tf_op jit(solution)/shard_map/pallas_call | solution.py:527
  193.9 2.5 %shard_map.156 = (f32[320,512]{1,0:T(8,128)S(1)}, f32[320,512]{1,0:T(8,128)S(1)}, f32[8,128]{1,0:T(8,128)}) custom-call(s32[10]{0:T(128)S(1)} %stack.35.scal, f32[8,128]{1,0:T(8,128)S(1)} %get-tuple-element.204.refs_0_, bf16[240,384]{1,0:T(8,128)(2,1)S(1)} %get-tuple-element.200.refs_1_, bf16[240,384]{1,0:T(8,128)(2,1)S(1)} %collective-permute-done.58.refs_0_.refs_2_, ...), custom_call_target="tpu_custom_call" | custom-call | flops 377487360 | bytes 2678784 | tf_op jit(solution)/shard_map/pallas_call | solution.py:491
  197.2 3.1 %shard_map.160 = (bf16[2,2,128,512]{3,2,1,0:T(8,128)(2,1)S(1)}, bf16[2,2,128,512]{3,2,1,0:T(8,128)(2,1)S(1)}, f32[8,128]{1,0:T(8,128)}) custom-call(s32[10]{0:T(128)S(1)} %stack.35.scal, f32[4,16,128]{2,1,0:T(8,128)S(1)} %get-tuple-element.121.refs_0_.routes, f32[320,512]{1,0:T(8,128)S(1)} %get-tuple-element.205.refs_1_, ...), custom_call_target="tpu_custom_call" | custom-call | flops 377487360 | bytes 2678784 | tf_op jit(solution)/shard_map/pallas_call | solution.py:506
  200.3 1.5 shard_map.164
  203.3 1.7 collective-permute-start.74
  205.3 2.2 %shard_map.161 = (bf16[4,512,768]{2,1,0:T(8,128)(2,1)}, bf16[4,512,768]{2,1,0:T(8,128)(2,1)}, bf16[4,768,512]{2,1,0:T(8,128)(2,1)}, f32[8,128]{1,0:T(8,128)}) custom-call(s32[10]{0:T(128)S(1)} %stack.35.scal, bf16[320,512]{1,0:T(8,128)(2,1)S(1)} %get-tuple-element.128.refs_1_.in_ref, ...), custom_call_target="tpu_custom_call", output_to_operand_aliasing={{0}: (10, {}), {1}: (11, {}), {2}: (12, {})} | custom-call | flops 377487360 | bytes 2678784 | tf_op jit(solution)/shard_map/pallas_call | solution.py:527
  207.5 2.2 %shard_map.162 = (bf16[4,512,768]{2,1,0:T(8,128)(2,1)}, bf16[4,512,768]{2,1,0:T(8,128)(2,1)}, bf16[4,768,512]{2,1,0:T(8,128)(2,1)}, f32[8,128]{1,0:T(8,128)}) custom-call(s32[10]{0:T(128)S(1)} %stack.35.scal, bf16[320,512]{1,0:T(8,128)(2,1)S(1)} %get-tuple-element.187.refs_1_.in_ref, ...), custom_call_target="tpu_custom_call", output_to_operand_aliasing={{0}: (10, {}), {1}: (11, {}), {2}: (12, {})} | custom-call | flops 377487360 | bytes 2678784 | tf_op jit(solution)/shard_map/pallas_call | solution.py:527
  209.7 2.2 %shard_map.163 = (bf16[4,512,768]{2,1,0:T(8,128)(2,1)}, bf16[4,512,768]{2,1,0:T(8,128)(2,1)}, bf16[4,768,512]{2,1,0:T(8,128)(2,1)}, f32[8,128]{1,0:T(8,128)}) custom-call(s32[10]{0:T(128)S(1)} %stack.35.scal, bf16[320,512]{1,0:T(8,128)(2,1)S(1)} %get-tuple-element.187.refs_1_.in_ref, ...), custom_call_target="tpu_custom_call", output_to_operand_aliasing={{0}: (10, {}), {1}: (11, {}), {2}: (12, {})} | custom-call | flops 377487360 | bytes 2678784 | tf_op jit(solution)/shard_map/pallas_call | solution.py:527
  (175 shorter events, 27.6 us)
Async XLA Ops:
  1.7 9.7 %collective-permute-start = (bf16[272,512]{1,0:T(8,128)(2,1)S(1)}, bf16[272,512]{1,0:T(8,128)(2,1)S(1)}, u32[]{:S(2)}, u32[]{:S(2)}) collective-permute-start(bf16[272,512]{1,0:T(8,128)(2,1)S(1)} %shard_map.118.refs_0_.refs_1_), channel_id=1, source_target_pairs={{0,8},{4,12},{8,0},{12,4},{1,9},{5,13},{9,1},{13,5},{2,10},{6,14},... | collective-permute-start | bytes 835592 | tf_op jit(solution)/shard_map/ppermute | solution.py:32
  4.7 6.7 %collective-permute-start.1 = (bf16[272,512]{1,0:T(8,128)(2,1)S(1)}, bf16[272,512]{1,0:T(8,128)(2,1)S(1)}, u32[]{:S(2)}, u32[]{:S(2)}) collective-permute-start(bf16[272,512]{1,0:T(8,128)(2,1)S(1)} %shard_map.118.refs_0_.refs_1_), channel_id=1, source_target_pairs={{0,4},{4,0},{8,12},{12,8},{1,5},{5,1},{9,13},{13,9},{2,6},{6,2},{1... | collective-permute-start | bytes 835592 | tf_op jit(solution)/shard_map/ppermute | solution.py:32
  16.1 9.8 %collective-permute-start.6 = (bf16[240,384]{1,0:T(8,128)(2,1)S(1)}, bf16[240,384]{1,0:T(8,128)(2,1)S(1)}, u32[]{:S(2)}, u32[]{:S(2)}) collective-permute-start(bf16[240,384]{1,0:T(8,128)(2,1)S(1)} %get-tuple-element.126), channel_id=1, source_target_pairs={{0,1},{1,0},{2,3},{3,2},{4,5},{5,4},{6,7},{7,6},{8,9},{9,8},{10,11... | collective-permute-start | bytes 552968 | tf_op jit(solution)/shard_map/ppermute | solution.py:32
  18.0 9.6 %collective-permute-start.3 = (bf16[240,384]{1,0:T(8,128)(2,1)S(1)}, bf16[240,384]{1,0:T(8,128)(2,1)S(1)}, u32[]{:S(2)}, u32[]{:S(2)}) collective-permute-start(bf16[240,384]{1,0:T(8,128)(2,1)S(1)} %get-tuple-element.125.refs_1_), channel_id=1, source_target_pairs={{0,1},{1,0},{2,3},{3,2},{4,5},{5,4},{6,7},{7,6},{8,9},{9,8},{10,11... | collective-permute-start | bytes 552968 | tf_op jit(solution)/shard_map/ppermute | solution.py:32
  20.6 11.0 %collective-permute-start.16 = (bf16[240,384]{1,0:T(8,128)(2,1)S(1)}, bf16[240,384]{1,0:T(8,128)(2,1)S(1)}, u32[]{:S(2)}, u32[]{:S(2)}) collective-permute-start(bf16[240,384]{1,0:T(8,128)(2,1)S(1)} %get-tuple-element.142), channel_id=1, source_target_pairs={{0,1},{1,0},{2,3},{3,2},{4,5},{5,4},{6,7},{7,6},{8,9},{9,8},{10,11... | collective-permute-start | bytes 552968 | tf_op jit(solution)/shard_map/ppermute | solution.py:32
  22.5 12.3 %collective-permute-start.13 = (bf16[240,384]{1,0:T(8,128)(2,1)S(1)}, bf16[240,384]{1,0:T(8,128)(2,1)S(1)}, u32[]{:S(2)}, u32[]{:S(2)}) collective-permute-start(bf16[240,384]{1,0:T(8,128)(2,1)S(1)} %get-tuple-element.141.refs_1_), channel_id=1, source_target_pairs={{0,1},{1,0},{2,3},{3,2},{4,5},{5,4},{6,7},{7,6},{8,9},{9,8},{10,11... | collective-permute-start | bytes 552968 | tf_op jit(solution)/shard_map/ppermute | solution.py:32
  26.0 19.4 %collective-permute-start.7 = (bf16[240,384]{1,0:T(8,128)(2,1)S(1)}, bf16[240,384]{1,0:T(8,128)(2,1)S(1)}, u32[]{:S(2)}, u32[]{:S(2)}) collective-permute-start(bf16[240,384]{1,0:T(8,128)(2,1)S(1)} %fusion.6), channel_id=1, source_target_pairs={{1,2},{2,1},{0,4},{3,7},{5,6},{6,5},{4,0},{7,3},{9,10},{10,9},{8,1... | collective-permute-start | bytes 552968 | tf_op jit(solution)/shard_map/ppermute | solution.py:581
  27.7 7.3 %collective-permute-start.4 = (bf16[240,384]{1,0:T(8,128)(2,1)S(1)}, bf16[240,384]{1,0:T(8,128)(2,1)S(1)}, u32[]{:S(2)}, u32[]{:S(2)}) collective-permute-start(bf16[240,384]{1,0:T(8,128)(2,1)S(1)} %shard_map.121.refs_0_), channel_id=1, source_target_pairs={{1,2},{2,1},{0,4},{3,7},{5,6},{6,5},{4,0},{7,3},{9,10},{10,9},{8,1... | collective-permute-start | bytes 552968 | tf_op jit(solution)/shard_map/ppermute | solution.py:581
  31.6 15.6 %collective-permute-start.17 = (bf16[240,384]{1,0:T(8,128)(2,1)S(1)}, bf16[240,384]{1,0:T(8,128)(2,1)S(1)}, u32[]{:S(2)}, u32[]{:S(2)}) collective-permute-start(bf16[240,384]{1,0:T(8,128)(2,1)S(1)} %fusion.7), channel_id=1, source_target_pairs={{1,2},{2,1},{0,4},{3,7},{5,6},{6,5},{4,0},{7,3},{9,10},{10,9},{8,1... | collective-permute-start | bytes 552968 | tf_op jit(solution)/shard_map/ppermute | solution.py:581
  35.0 10.4 %collective-permute-start.5 = (bf16[240,384]{1,0:T(8,128)(2,1)S(1)}, bf16[240,384]{1,0:T(8,128)(2,1)S(1)}, u32[]{:S(2)}, u32[]{:S(2)}) collective-permute-start(bf16[240,384]{1,0:T(8,128)(2,1)S(1)} %fusion.1), channel_id=1, source_target_pairs={{0,1},{1,0},{2,3},{3,2},{4,5},{5,4},{6,7},{7,6},{8,9},{9,8},{10,11... | collective-permute-start | bytes 552968 | tf_op jit(solution)/shard_map/ppermute | solution.py:32
  39.6 10.8 %collective-permute-start.15 = (bf16[240,384]{1,0:T(8,128)(2,1)S(1)}, bf16[240,384]{1,0:T(8,128)(2,1)S(1)}, u32[]{:S(2)}, u32[]{:S(2)}) collective-permute-start(bf16[240,384]{1,0:T(8,128)(2,1)S(1)} %fusion.2), channel_id=1, source_target_pairs={{0,1},{1,0},{2,3},{3,2},{4,5},{5,4},{6,7},{7,6},{8,9},{9,8},{10,11... | collective-permute-start | bytes 552968 | tf_op jit(solution)/shard_map/ppermute | solution.py:32
  45.6 9.1 %collective-permute-start.8 = (bf16[240,384]{1,0:T(8,128)(2,1)S(1)}, bf16[240,384]{1,0:T(8,128)(2,1)S(1)}, u32[]{:S(2)}, u32[]{:S(2)}) collective-permute-start(bf16[240,384]{1,0:T(8,128)(2,1)S(1)} %get-tuple-element.127.refs_0_.refs_1_), channel_id=1, source_target_pairs={{1,2},{2,1},{0,4},{3,7},{5,6},{6,5},{4,0},{7,3},{9,10},{10,9},{8,1... | collective-permute-start | bytes 552968 | tf_op jit(solution)/shard_map/ppermute | solution.py:581
  45.7 14.5 %collective-permute-start.9 = (bf16[240,384]{1,0:T(8,128)(2,1)S(1)}, bf16[240,384]{1,0:T(8,128)(2,1)S(1)}, u32[]{:S(2)}, u32[]{:S(2)}) collective-permute-start(bf16[240,384]{1,0:T(8,128)(2,1)S(1)} %get-tuple-element.127.refs_0_.refs_1_), channel_id=1, source_target_pairs={{0,1},{1,0},{2,3},{3,2},{4,5},{5,4},{6,7},{7,6},{8,9},{9,8},{10,11... | collective-permute-start | bytes 552968 | tf_op jit(solution)/shard_map/ppermute | solution.py:32
  50.6 7.5 %collective-permute-start.19 = (bf16[240,384]{1,0:T(8,128)(2,1)S(1)}, bf16[240,384]{1,0:T(8,128)(2,1)S(1)}, u32[]{:S(2)}, u32[]{:S(2)}) collective-permute-start(bf16[240,384]{1,0:T(8,128)(2,1)S(1)} %get-tuple-element.143.refs_3_.refs_1_), channel_id=1, source_target_pairs={{1,2},{2,1},{0,4},{3,7},{5,6},{6,5},{4,0},{7,3},{9,10},{10,9},{8,1... | collective-permute-start | bytes 552968 | tf_op jit(solution)/shard_map/ppermute | solution.py:581
  50.6 9.6 %collective-permute-start.18 = (bf16[240,384]{1,0:T(8,128)(2,1)S(1)}, bf16[240,384]{1,0:T(8,128)(2,1)S(1)}, u32[]{:S(2)}, u32[]{:S(2)}) collective-permute-start(bf16[240,384]{1,0:T(8,128)(2,1)S(1)} %get-tuple-element.143.refs_3_.refs_1_), channel_id=1, source_target_pairs={{0,1},{1,0},{2,3},{3,2},{4,5},{5,4},{6,7},{7,6},{8,9},{9,8},{10,11... | collective-permute-start | bytes 552968 | tf_op jit(solution)/shard_map/ppermute | solution.py:32
  54.7 8.9 %collective-permute-start.10 = (bf16[240,384]{1,0:T(8,128)(2,1)S(1)}, bf16[240,384]{1,0:T(8,128)(2,1)S(1)}, u32[]{:S(2)}, u32[]{:S(2)}) collective-permute-start(bf16[240,384]{1,0:T(8,128)(2,1)S(1)} %broadcast_select_fusion.14), channel_id=1, source_target_pairs={{0,1},{1,0},{2,3},{3,2},{4,5},{5,4},{6,7},{7,6},{8,9},{9,8},{10,11... | collective-permute-start | bytes 552968 | tf_op jit(solution)/shard_map/ppermute | solution.py:32
  58.1 7.6 %collective-permute-start.20 = (bf16[240,384]{1,0:T(8,128)(2,1)S(1)}, bf16[240,384]{1,0:T(8,128)(2,1)S(1)}, u32[]{:S(2)}, u32[]{:S(2)}) collective-permute-start(bf16[240,384]{1,0:T(8,128)(2,1)S(1)} %broadcast_select_fusion.12), channel_id=1, source_target_pairs={{0,1},{1,0},{2,3},{3,2},{4,5},{5,4},{6,7},{7,6},{8,9},{9,8},{10,11... | collective-permute-start | bytes 552968 | tf_op jit(solution)/shard_map/ppermute | solution.py:32
  60.2 6.1 %collective-permute-start.11 = (bf16[240,384]{1,0:T(8,128)(2,1)S(1)}, bf16[240,384]{1,0:T(8,128)(2,1)S(1)}, u32[]{:S(2)}, u32[]{:S(2)}) collective-permute-start(bf16[240,384]{1,0:T(8,128)(2,1)S(1)} %collective-permute-done.9.refs_1_.refs_2_), channel_id=1, source_target_pairs={{1,2},{2,1},{0,4},{3,7},{5,6},{6,5},{4,0},{7,3},{9,10},{10,9},{8,1... | collective-permute-start | bytes 552968 | tf_op jit(solution)/shard_map/ppermute | solution.py:581
  60.2 8.9 %collective-permute-start.21 = (bf16[240,384]{1,0:T(8,128)(2,1)S(1)}, bf16[240,384]{1,0:T(8,128)(2,1)S(1)}, u32[]{:S(2)}, u32[]{:S(2)}) collective-permute-start(bf16[240,384]{1,0:T(8,128)(2,1)S(1)} %collective-permute-done.18.refs_4_.refs_2_), channel_id=1, source_target_pairs={{1,2},{2,1},{0,4},{3,7},{5,6},{6,5},{4,0},{7,3},{9,10},{10,9},{8,1... | collective-permute-start | bytes 552968 | tf_op jit(solution)/shard_map/ppermute | solution.py:581
  63.7 14.3 %collective-permute-start.23 = (bf16[240,384]{1,0:T(8,128)(2,1)S(1)}, bf16[240,384]{1,0:T(8,128)(2,1)S(1)}, u32[]{:S(2)}, u32[]{:S(2)}) collective-permute-start(bf16[240,384]{1,0:T(8,128)(2,1)S(1)} %shard_map.131.refs_0_), channel_id=1, source_target_pairs={{1,2},{2,1},{0,4},{3,7},{5,6},{6,5},{4,0},{7,3},{9,10},{10,9},{8,1... | collective-permute-start | bytes 552968 | tf_op jit(solution)/shard_map/ppermute | solution.py:581
  65.8 11.4 %collective-permute-start.31 = (bf16[240,384]{1,0:T(8,128)(2,1)S(1)}, bf16[240,384]{1,0:T(8,128)(2,1)S(1)}, u32[]{:S(2)}, u32[]{:S(2)}) collective-permute-start(bf16[240,384]{1,0:T(8,128)(2,1)S(1)} %shard_map.136), channel_id=1, source_target_pairs={{1,2},{2,1},{0,4},{3,7},{5,6},{6,5},{4,0},{7,3},{9,10},{10,9},{8,1... | collective-permute-start | bytes 552968 | tf_op jit(solution)/shard_map/ppermute | solution.py:581
  66.3 8.3 %collective-permute-start.12 = (bf16[240,384]{1,0:T(8,128)(2,1)S(1)}, bf16[240,384]{1,0:T(8,128)(2,1)S(1)}, u32[]{:S(2)}, u32[]{:S(2)}) collective-permute-start(bf16[240,384]{1,0:T(8,128)(2,1)S(1)} %broadcast_select_fusion.13), channel_id=1, source_target_pairs={{0,1},{1,0},{2,3},{3,2},{4,5},{5,4},{6,7},{7,6},{8,9},{9,8},{10,11... | collective-permute-start | bytes 552968 | tf_op jit(solution)/shard_map/ppermute | solution.py:32
  69.1 10.5 %collective-permute-start.22 = (bf16[240,384]{1,0:T(8,128)(2,1)S(1)}, bf16[240,384]{1,0:T(8,128)(2,1)S(1)}, u32[]{:S(2)}, u32[]{:S(2)}) collective-permute-start(bf16[240,384]{1,0:T(8,128)(2,1)S(1)} %broadcast_select_fusion.11), channel_id=1, source_target_pairs={{0,1},{1,0},{2,3},{3,2},{4,5},{5,4},{6,7},{7,6},{8,9},{9,8},{10,11... | collective-permute-start | bytes 552968 | tf_op jit(solution)/shard_map/ppermute | solution.py:32
  77.3 10.0 %collective-permute-start.32 = (bf16[240,384]{1,0:T(8,128)(2,1)S(1)}, bf16[240,384]{1,0:T(8,128)(2,1)S(1)}, u32[]{:S(2)}, u32[]{:S(2)}) collective-permute-start(bf16[240,384]{1,0:T(8,128)(2,1)S(1)} %broadcast_select_fusion.8), channel_id=1, source_target_pairs={{0,1},{1,0},{2,3},{3,2},{4,5},{5,4},{6,7},{7,6},{8,9},{9,8},{10,11... | collective-permute-start | bytes 552968 | tf_op jit(solution)/shard_map/ppermute | solution.py:32
  78.0 6.9 %collective-permute-start.24 = (bf16[240,384]{1,0:T(8,128)(2,1)S(1)}, bf16[240,384]{1,0:T(8,128)(2,1)S(1)}, u32[]{:S(2)}, u32[]{:S(2)}) collective-permute-start(bf16[240,384]{1,0:T(8,128)(2,1)S(1)} %fusion.3), channel_id=1, source_target_pairs={{0,1},{1,0},{2,3},{3,2},{4,5},{5,4},{6,7},{7,6},{8,9},{9,8},{10,11... | collective-permute-start | bytes 552968 | tf_op jit(solution)/shard_map/ppermute | solution.py:32
  79.6 5.3 %collective-permute-start.25 = (bf16[240,384]{1,0:T(8,128)(2,1)S(1)}, bf16[240,384]{1,0:T(8,128)(2,1)S(1)}, u32[]{:S(2)}, u32[]{:S(2)}) collective-permute-start(bf16[240,384]{1,0:T(8,128)(2,1)S(1)} %fusion.8), channel_id=1, source_target_pairs={{1,2},{2,1},{0,4},{3,7},{5,6},{6,5},{4,0},{7,3},{9,10},{10,9},{8,1... | collective-permute-start | bytes 552968 | tf_op jit(solution)/shard_map/ppermute | solution.py:581
  79.7 7.6 %collective-permute-start.33 = (bf16[240,384]{1,0:T(8,128)(2,1)S(1)}, bf16[240,384]{1,0:T(8,128)(2,1)S(1)}, u32[]{:S(2)}, u32[]{:S(2)}) collective-permute-start(bf16[240,384]{1,0:T(8,128)(2,1)S(1)} %fusion.9), channel_id=1, source_target_pairs={{1,2},{2,1},{0,4},{3,7},{5,6},{6,5},{4,0},{7,3},{9,10},{10,9},{8,1... | collective-permute-start | bytes 552968 | tf_op jit(solution)/shard_map/ppermute | solution.py:581
  85.0 9.4 %collective-permute-start.27 = (bf16[240,384]{1,0:T(8,128)(2,1)S(1)}, bf16[240,384]{1,0:T(8,128)(2,1)S(1)}, u32[]{:S(2)}, u32[]{:S(2)}) collective-permute-start(bf16[240,384]{1,0:T(8,128)(2,1)S(1)} %get-tuple-element.150.refs_0_.refs_1_), channel_id=1, source_target_pairs={{1,2},{2,1},{0,4},{3,7},{5,6},{6,5},{4,0},{7,3},{9,10},{10,9},{8,1... | collective-permute-start | bytes 552968 | tf_op jit(solution)/shard_map/ppermute | solution.py:581
  87.4 11.9 %collective-permute-start.34 = (bf16[240,384]{1,0:T(8,128)(2,1)S(1)}, bf16[240,384]{1,0:T(8,128)(2,1)S(1)}, u32[]{:S(2)}, u32[]{:S(2)}) collective-permute-start(bf16[240,384]{1,0:T(8,128)(2,1)S(1)} %get-tuple-element.162.refs_5_.refs_0_.refs_1_), channel_id=1, source_target_pairs={{0,1},{1,0},{2,3},{3,2},{4,5},{5,4},{6,7},{7,6},{8,9},{9,8},{10,11... | collective-permute-start | bytes 552968 | tf_op jit(solution)/shard_map/ppermute | solution.py:32
  91.8 7.7 %collective-permute-start.35 = (bf16[240,384]{1,0:T(8,128)(2,1)S(1)}, bf16[240,384]{1,0:T(8,128)(2,1)S(1)}, u32[]{:S(2)}, u32[]{:S(2)}) collective-permute-start(bf16[240,384]{1,0:T(8,128)(2,1)S(1)} %get-tuple-element.162.refs_5_.refs_0_.refs_1_), channel_id=1, source_target_pairs={{1,2},{2,1},{0,4},{3,7},{5,6},{6,5},{4,0},{7,3},{9,10},{10,9},{8,1... | collective-permute-start | bytes 552968 | tf_op jit(solution)/shard_map/ppermute | solution.py:581
  91.8 9.9 %collective-permute-start.26 = (bf16[240,384]{1,0:T(8,128)(2,1)S(1)}, bf16[240,384]{1,0:T(8,128)(2,1)S(1)}, u32[]{:S(2)}, u32[]{:S(2)}) collective-permute-start(bf16[240,384]{1,0:T(8,128)(2,1)S(1)} %get-tuple-element.150.refs_0_.refs_1_), channel_id=1, source_target_pairs={{0,1},{1,0},{2,3},{3,2},{4,5},{5,4},{6,7},{7,6},{8,9},{9,8},{10,11... | collective-permute-start | bytes 552968 | tf_op jit(solution)/shard_map/ppermute | solution.py:32
  94.4 13.1 %collective-permute-start.28 = (bf16[240,384]{1,0:T(8,128)(2,1)S(1)}, bf16[240,384]{1,0:T(8,128)(2,1)S(1)}, u32[]{:S(2)}, u32[]{:S(2)}) collective-permute-start(bf16[240,384]{1,0:T(8,128)(2,1)S(1)} %broadcast_select_fusion.10), channel_id=1, source_target_pairs={{0,1},{1,0},{2,3},{3,2},{4,5},{5,4},{6,7},{7,6},{8,9},{9,8},{10,11... | collective-permute-start | bytes 552968 | tf_op jit(solution)/shard_map/ppermute | solution.py:32
  99.5 10.1 %collective-permute-start.36 = (bf16[240,384]{1,0:T(8,128)(2,1)S(1)}, bf16[240,384]{1,0:T(8,128)(2,1)S(1)}, u32[]{:S(2)}, u32[]{:S(2)}) collective-permute-start(bf16[240,384]{1,0:T(8,128)(2,1)S(1)} %broadcast_select_fusion.7), channel_id=1, source_target_pairs={{0,1},{1,0},{2,3},{3,2},{4,5},{5,4},{6,7},{7,6},{8,9},{9,8},{10,11... | collective-permute-start | bytes 552968 | tf_op jit(solution)/shard_map/ppermute | solution.py:32
  101.6 8.5 %collective-permute-start.29 = (bf16[240,384]{1,0:T(8,128)(2,1)S(1)}, bf16[240,384]{1,0:T(8,128)(2,1)S(1)}, u32[]{:S(2)}, u32[]{:S(2)}) collective-permute-start(bf16[240,384]{1,0:T(8,128)(2,1)S(1)} %collective-permute-done.26.refs_1_.refs_2_), channel_id=1, source_target_pairs={{1,2},{2,1},{0,4},{3,7},{5,6},{6,5},{4,0},{7,3},{9,10},{10,9},{8,1... | collective-permute-start | bytes 552968 | tf_op jit(solution)/shard_map/ppermute | solution.py:581
  101.7 10.1 %collective-permute-start.38 = (bf16[240,384]{1,0:T(8,128)(2,1)S(1)}, bf16[240,384]{1,0:T(8,128)(2,1)S(1)}, u32[]{:S(2)}, u32[]{:S(2)}) collective-permute-start(bf16[240,384]{1,0:T(8,128)(2,1)S(1)} %broadcast_select_fusion.6), channel_id=1, source_target_pairs={{0,1},{1,0},{2,3},{3,2},{4,5},{5,4},{6,7},{7,6},{8,9},{9,8},{10,11... | collective-permute-start | bytes 552968 | tf_op jit(solution)/shard_map/ppermute | solution.py:32
  109.6 10.8 %collective-permute-start.47 = (bf16[240,384]{1,0:T(8,128)(2,1)S(1)}, bf16[240,384]{1,0:T(8,128)(2,1)S(1)}, u32[]{:S(2)}, u32[]{:S(2)}) collective-permute-start(bf16[240,384]{1,0:T(8,128)(2,1)S(1)} %shard_map.148), channel_id=1, source_target_pairs={{1,2},{2,1},{0,4},{3,7},{5,6},{6,5},{4,0},{7,3},{9,10},{10,9},{8,1... | collective-permute-start | bytes 552968 | tf_op jit(solution)/shard_map/ppermute | solution.py:581
  110.2 7.6 %collective-permute-start.30 = (bf16[240,384]{1,0:T(8,128)(2,1)S(1)}, bf16[240,384]{1,0:T(8,128)(2,1)S(1)}, u32[]{:S(2)}, u32[]{:S(2)}) collective-permute-start(bf16[240,384]{1,0:T(8,128)(2,1)S(1)} %broadcast_select_fusion.9), channel_id=1, source_target_pairs={{0,1},{1,0},{2,3},{3,2},{4,5},{5,4},{6,7},{7,6},{8,9},{9,8},{10,11... | collective-permute-start | bytes 552968 | tf_op jit(solution)/shard_map/ppermute | solution.py:32
  111.9 17.1 %collective-permute-start.49 = (bf16[240,384]{1,0:T(8,128)(2,1)S(1)}, bf16[240,384]{1,0:T(8,128)(2,1)S(1)}, u32[]{:S(2)}, u32[]{:S(2)}) collective-permute-start(bf16[240,384]{1,0:T(8,128)(2,1)S(1)} %fusion.11), channel_id=1, source_target_pairs={{1,2},{2,1},{0,4},{3,7},{5,6},{6,5},{4,0},{7,3},{9,10},{10,9},{8,1... | collective-permute-start | bytes 552968 | tf_op jit(solution)/shard_map/ppermute | solution.py:581
  112.0 14.5 %collective-permute-start.40 = (bf16[240,384]{1,0:T(8,128)(2,1)S(1)}, bf16[240,384]{1,0:T(8,128)(2,1)S(1)}, u32[]{:S(2)}, u32[]{:S(2)}) collective-permute-start(bf16[240,384]{1,0:T(8,128)(2,1)S(1)} %fusion.4), channel_id=1, source_target_pairs={{0,1},{1,0},{2,3},{3,2},{4,5},{5,4},{6,7},{7,6},{8,9},{9,8},{10,11... | collective-permute-start | bytes 552968 | tf_op jit(solution)/shard_map/ppermute | solution.py:32
  117.8 8.7 %collective-permute-start.41 = (bf16[240,384]{1,0:T(8,128)(2,1)S(1)}, bf16[240,384]{1,0:T(8,128)(2,1)S(1)}, u32[]{:S(2)}, u32[]{:S(2)}) collective-permute-start(bf16[240,384]{1,0:T(8,128)(2,1)S(1)} %fusion.10), channel_id=1, source_target_pairs={{1,2},{2,1},{0,4},{3,7},{5,6},{6,5},{4,0},{7,3},{9,10},{10,9},{8,1... | collective-permute-start | bytes 552968 | tf_op jit(solution)/shard_map/ppermute | solution.py:581
  120.5 8.4 %collective-permute-start.48 = (bf16[240,384]{1,0:T(8,128)(2,1)S(1)}, bf16[240,384]{1,0:T(8,128)(2,1)S(1)}, u32[]{:S(2)}, u32[]{:S(2)}) collective-permute-start(bf16[240,384]{1,0:T(8,128)(2,1)S(1)} %broadcast_select_fusion.3), channel_id=1, source_target_pairs={{0,1},{1,0},{2,3},{3,2},{4,5},{5,4},{6,7},{7,6},{8,9},{9,8},{10,11... | collective-permute-start | bytes 552968 | tf_op jit(solution)/shard_map/ppermute | solution.py:32
  129.2 7.5 %collective-permute-start.50 = (bf16[240,384]{1,0:T(8,128)(2,1)S(1)}, bf16[240,384]{1,0:T(8,128)(2,1)S(1)}, u32[]{:S(2)}, u32[]{:S(2)}) collective-permute-start(bf16[240,384]{1,0:T(8,128)(2,1)S(1)} %get-tuple-element.190.refs_5_.refs_0_.refs_1_), channel_id=1, source_target_pairs={{0,1},{1,0},{2,3},{3,2},{4,5},{5,4},{6,7},{7,6},{8,9},{9,8},{10,11... | collective-permute-start | bytes 552968 | tf_op jit(solution)/shard_map/ppermute | solution.py:32
  129.7 10.9 %collective-permute-start.42 = (bf16[240,384]{1,0:T(8,128)(2,1)S(1)}, bf16[240,384]{1,0:T(8,128)(2,1)S(1)}, u32[]{:S(2)}, u32[]{:S(2)}) collective-permute-start(bf16[240,384]{1,0:T(8,128)(2,1)S(1)} %get-tuple-element.173.refs_0_.refs_1_), channel_id=1, source_target_pairs={{0,1},{1,0},{2,3},{3,2},{4,5},{5,4},{6,7},{7,6},{8,9},{9,8},{10,11... | collective-permute-start | bytes 552968 | tf_op jit(solution)/shard_map/ppermute | solution.py:32
  131.2 5.4 %collective-permute-start.43 = (bf16[240,384]{1,0:T(8,128)(2,1)S(1)}, bf16[240,384]{1,0:T(8,128)(2,1)S(1)}, u32[]{:S(2)}, u32[]{:S(2)}) collective-permute-start(bf16[240,384]{1,0:T(8,128)(2,1)S(1)} %get-tuple-element.173.refs_0_.refs_1_), channel_id=1, source_target_pairs={{1,2},{2,1},{0,4},{3,7},{5,6},{6,5},{4,0},{7,3},{9,10},{10,9},{8,1... | collective-permute-start | bytes 552968 | tf_op jit(solution)/shard_map/ppermute | solution.py:581
  133.5 11.1 %collective-permute-start.52 = (bf16[240,384]{1,0:T(8,128)(2,1)S(1)}, bf16[240,384]{1,0:T(8,128)(2,1)S(1)}, u32[]{:S(2)}, u32[]{:S(2)}) collective-permute-start(bf16[240,384]{1,0:T(8,128)(2,1)S(1)} %broadcast_select_fusion.2), channel_id=1, source_target_pairs={{0,1},{1,0},{2,3},{3,2},{4,5},{5,4},{6,7},{7,6},{8,9},{9,8},{10,11... | collective-permute-start | bytes 552968 | tf_op jit(solution)/shard_map/ppermute | solution.py:32
  136.7 11.8 %collective-permute-start.44 = (bf16[240,384]{1,0:T(8,128)(2,1)S(1)}, bf16[240,384]{1,0:T(8,128)(2,1)S(1)}, u32[]{:S(2)}, u32[]{:S(2)}) collective-permute-start(bf16[240,384]{1,0:T(8,128)(2,1)S(1)} %broadcast_select_fusion.5), channel_id=1, source_target_pairs={{0,1},{1,0},{2,3},{3,2},{4,5},{5,4},{6,7},{7,6},{8,9},{9,8},{10,11... | collective-permute-start | bytes 552968 | tf_op jit(solution)/shard_map/ppermute | solution.py:32
  140.6 11.8 %collective-permute-start.54 = (bf16[240,384]{1,0:T(8,128)(2,1)S(1)}, bf16[240,384]{1,0:T(8,128)(2,1)S(1)}, u32[]{:S(2)}, u32[]{:S(2)}) collective-permute-start(bf16[240,384]{1,0:T(8,128)(2,1)S(1)} %broadcast_select_fusion.1), channel_id=1, source_target_pairs={{0,1},{1,0},{2,3},{3,2},{4,5},{5,4},{6,7},{7,6},{8,9},{9,8},{10,11... | collective-permute-start | bytes 552968 | tf_op jit(solution)/shard_map/ppermute | solution.py:32
  144.6 14.1 %collective-permute-start.63 = (bf16[240,384]{1,0:T(8,128)(2,1)S(1)}, bf16[240,384]{1,0:T(8,128)(2,1)S(1)}, u32[]{:S(2)}, u32[]{:S(2)}) collective-permute-start(bf16[240,384]{1,0:T(8,128)(2,1)S(1)} %shard_map.157), channel_id=1, source_target_pairs={{1,2},{2,1},{0,4},{3,7},{5,6},{6,5},{4,0},{7,3},{9,10},{10,9},{8,1... | collective-permute-start | bytes 552968 | tf_op jit(solution)/shard_map/ppermute | solution.py:581
  144.7 11.3 %collective-permute-start.46 = (bf16[240,384]{1,0:T(8,128)(2,1)S(1)}, bf16[240,384]{1,0:T(8,128)(2,1)S(1)}, u32[]{:S(2)}, u32[]{:S(2)}) collective-permute-start(bf16[240,384]{1,0:T(8,128)(2,1)S(1)} %broadcast_select_fusion.4), channel_id=1, source_target_pairs={{0,1},{1,0},{2,3},{3,2},{4,5},{5,4},{6,7},{7,6},{8,9},{9,8},{10,11... | collective-permute-start | bytes 552968 | tf_op jit(solution)/shard_map/ppermute | solution.py:32
  152.5 11.6 %collective-permute-start.65 = (bf16[240,384]{1,0:T(8,128)(2,1)S(1)}, bf16[240,384]{1,0:T(8,128)(2,1)S(1)}, u32[]{:S(2)}, u32[]{:S(2)}) collective-permute-start(bf16[240,384]{1,0:T(8,128)(2,1)S(1)} %fusion.13), channel_id=1, source_target_pairs={{1,2},{2,1},{0,4},{3,7},{5,6},{6,5},{4,0},{7,3},{9,10},{10,9},{8,1... | collective-permute-start | bytes 552968 | tf_op jit(solution)/shard_map/ppermute | solution.py:581
  152.7 11.2 %collective-permute-start.56 = (bf16[240,384]{1,0:T(8,128)(2,1)S(1)}, bf16[240,384]{1,0:T(8,128)(2,1)S(1)}, u32[]{:S(2)}, u32[]{:S(2)}) collective-permute-start(bf16[240,384]{1,0:T(8,128)(2,1)S(1)} %fusion.5), channel_id=1, source_target_pairs={{0,1},{1,0},{2,3},{3,2},{4,5},{5,4},{6,7},{7,6},{8,9},{9,8},{10,11... | collective-permute-start | bytes 552968 | tf_op jit(solution)/shard_map/ppermute | solution.py:32
  156.1 7.8 %collective-permute-start.57 = (bf16[240,384]{1,0:T(8,128)(2,1)S(1)}, bf16[240,384]{1,0:T(8,128)(2,1)S(1)}, u32[]{:S(2)}, u32[]{:S(2)}) collective-permute-start(bf16[240,384]{1,0:T(8,128)(2,1)S(1)} %fusion.12), channel_id=1, source_target_pairs={{1,2},{2,1},{0,4},{3,7},{5,6},{6,5},{4,0},{7,3},{9,10},{10,9},{8,1... | collective-permute-start | bytes 552968 | tf_op jit(solution)/shard_map/ppermute | solution.py:581
  158.8 7.1 %collective-permute-start.64 = (bf16[240,384]{1,0:T(8,128)(2,1)S(1)}, bf16[240,384]{1,0:T(8,128)(2,1)S(1)}, u32[]{:S(2)}, u32[]{:S(2)}) collective-permute-start(bf16[240,384]{1,0:T(8,128)(2,1)S(1)} %broadcast_select_fusion), channel_id=1, source_target_pairs={{0,1},{1,0},{2,3},{3,2},{4,5},{5,4},{6,7},{7,6},{8,9},{9,8},{10,11... | collective-permute-start | bytes 552968 | tf_op jit(solution)/shard_map/ppermute | solution.py:32
  166.7 10.9 %collective-permute-start.66 = (bf16[256,384]{1,0:T(8,128)(2,1)S(1)}, bf16[256,384]{1,0:T(8,128)(2,1)S(1)}, u32[]{:S(2)}, u32[]{:S(2)}) collective-permute-start(bf16[256,384]{1,0:T(8,128)(2,1)S(1)} %get-tuple-element.219.refs_5_.refs_1_), channel_id=1, source_target_pairs={{0,1},{1,0},{2,3},{3,2},{4,5},{5,4},{6,7},{7,6},{8,9},{9,8},{10,11... | collective-permute-start | bytes 589832 | tf_op jit(solution)/shard_map/ppermute | solution.py:32
  167.3 9.7 %collective-permute-start.58 = (bf16[240,384]{1,0:T(8,128)(2,1)S(1)}, bf16[240,384]{1,0:T(8,128)(2,1)S(1)}, u32[]{:S(2)}, u32[]{:S(2)}) collective-permute-start(bf16[240,384]{1,0:T(8,128)(2,1)S(1)} %get-tuple-element.200.refs_1_), channel_id=1, source_target_pairs={{0,1},{1,0},{2,3},{3,2},{4,5},{5,4},{6,7},{7,6},{8,9},{9,8},{10,11... | collective-permute-start | bytes 552968 | tf_op jit(solution)/shard_map/ppermute | solution.py:32
  168.7 8.8 %collective-permute-start.59 = (bf16[240,384]{1,0:T(8,128)(2,1)S(1)}, bf16[240,384]{1,0:T(8,128)(2,1)S(1)}, u32[]{:S(2)}, u32[]{:S(2)}) collective-permute-start(bf16[240,384]{1,0:T(8,128)(2,1)S(1)} %get-tuple-element.200.refs_1_), channel_id=1, source_target_pairs={{1,2},{2,1},{0,4},{3,7},{5,6},{6,5},{4,0},{7,3},{9,10},{10,9},{8,1... | collective-permute-start | bytes 552968 | tf_op jit(solution)/shard_map/ppermute | solution.py:581
  177.0 8.1 %collective-permute-start.67 = (bf16[256,384]{1,0:T(8,128)(2,1)S(1)}, bf16[256,384]{1,0:T(8,128)(2,1)S(1)}, u32[]{:S(2)}, u32[]{:S(2)}) collective-permute-start(bf16[256,384]{1,0:T(8,128)(2,1)S(1)} %get-tuple-element.219.refs_5_.refs_1_), channel_id=1, source_target_pairs={{1,2},{2,1},{0,4},{3,7},{5,6},{6,5},{4,0},{7,3},{9,10},{10,9},{8,1... | collective-permute-start | bytes 589832 | tf_op jit(solution)/shard_map/ppermute | solution.py:581
  177.5 11.8 %collective-permute-start.69 = (bf16[256,384]{1,0:T(8,128)(2,1)S(1)}, bf16[256,384]{1,0:T(8,128)(2,1)S(1)}, u32[]{:S(2)}, u32[]{:S(2)}) collective-permute-start(bf16[256,384]{1,0:T(8,128)(2,1)S(1)} %collective-permute-done.66.refs_6_.refs_2_), channel_id=1, source_target_pairs={{1,2},{2,1},{0,4},{3,7},{5,6},{6,5},{4,0},{7,3},{9,10},{10,9},{8,1... | collective-permute-start | bytes 589832 | tf_op jit(solution)/shard_map/ppermute | solution.py:581
  177.6 16.4 %collective-permute-start.60 = (bf16[240,384]{1,0:T(8,128)(2,1)S(1)}, bf16[240,384]{1,0:T(8,128)(2,1)S(1)}, u32[]{:S(2)}, u32[]{:S(2)}) collective-permute-start(bf16[240,384]{1,0:T(8,128)(2,1)S(1)} %collective-permute-done.59.refs_4_), channel_id=1, source_target_pairs={{0,1},{1,0},{2,3},{3,2},{4,5},{5,4},{6,7},{7,6},{8,9},{9,8},{10,11... | collective-permute-start | bytes 552968 | tf_op jit(solution)/shard_map/ppermute | solution.py:32
  181.7 12.3 %collective-permute-start.62 = (bf16[240,384]{1,0:T(8,128)(2,1)S(1)}, bf16[240,384]{1,0:T(8,128)(2,1)S(1)}, u32[]{:S(2)}, u32[]{:S(2)}) collective-permute-start(bf16[240,384]{1,0:T(8,128)(2,1)S(1)} %collective-permute-done.61.refs_6_), channel_id=1, source_target_pairs={{0,1},{1,0},{2,3},{3,2},{4,5},{5,4},{6,7},{7,6},{8,9},{9,8},{10,11... | collective-permute-start | bytes 552968 | tf_op jit(solution)/shard_map/ppermute | solution.py:32
  185.2 11.3 %collective-permute-start.68 = (bf16[256,384]{1,0:T(8,128)(2,1)S(1)}, bf16[256,384]{1,0:T(8,128)(2,1)S(1)}, u32[]{:S(2)}, u32[]{:S(2)}) collective-permute-start(bf16[256,384]{1,0:T(8,128)(2,1)S(1)} %collective-permute-done.67.refs_8_.refs_4_), channel_id=1, source_target_pairs={{0,1},{1,0},{2,3},{3,2},{4,5},{5,4},{6,7},{7,6},{8,9},{9,8},{10,11... | collective-permute-start | bytes 589832 | tf_op jit(solution)/shard_map/ppermute | solution.py:32
  189.4 7.8 %collective-permute-start.70 = (bf16[256,384]{1,0:T(8,128)(2,1)S(1)}, bf16[256,384]{1,0:T(8,128)(2,1)S(1)}, u32[]{:S(2)}, u32[]{:S(2)}) collective-permute-start(bf16[256,384]{1,0:T(8,128)(2,1)S(1)} %collective-permute-done.69.refs_10_.refs_6_), channel_id=1, source_target_pairs={{0,1},{1,0},{2,3},{3,2},{4,5},{5,4},{6,7},{7,6},{8,9},{9,8},{10,11... | collective-permute-start | bytes 589832 | tf_op jit(solution)/shard_map/ppermute | solution.py:32
  203.3 8.6 %collective-permute-start.74 = (f32[16,128]{1,0:T(8,128)S(1)}, f32[16,128]{1,0:T(8,128)S(1)}, u32[]{:S(2)}, u32[]{:S(2)}) collective-permute-start(f32[16,128]{1,0:T(8,128)S(1)} %slice_bitcast_fusion.4), channel_id=1, source_target_pairs={{0,8},{4,12},{8,0},{12,4},{1,9},{5,13},{9,1},{13,5},{2,10},{6,14},... | collective-permute-start | bytes 24584 | tf_op jit(solution)/shard_map/ppermute | solution.py:32
  205.0 8.3 %collective-permute-start.72 = (bf16[2,128,512]{2,1,0:T(8,128)(2,1)S(1)}, bf16[2,128,512]{2,1,0:T(8,128)(2,1)S(1)}, u32[]{:S(2)}, u32[]{:S(2)}) collective-permute-start(bf16[2,128,512]{2,1,0:T(8,128)(2,1)S(1)} %slice_bitcast_fusion), channel_id=1, source_target_pairs={{0,8},{4,12},{8,0},{12,4},{1,9},{5,13},{9,1},{13,5},{2,10},{6,14},... | collective-permute-start | bytes 786440 | tf_op jit(solution)/shard_map/ppermute | solution.py:32
  (13 other events, 42.0 us)

commit v9 on v6

--- a/solution.py
+++ b/solution.py
@@ -9,6 +9,7 @@
 
 F32, BF16 = jnp.float32, jnp.bfloat16
 VMEM_BYTES = 20 << 20
+STREAMS = 3
 
 
 def line_pairs(n, gather, step):
@@ -69,9 +70,10 @@
     n = len(routes)
     choose, tokens = routes[0].shape[0] // 2, routes[0].shape[1]
     which = (scal[2 * n] + expert).astype(F32)
-    hits = [route[0:choose, :] == which for route in routes]
+    routes = [route[...] for route in routes]
+    hits = [route[0:choose] == which for route in routes]
     weights = [
-        jnp.sum(jnp.where(hit, route[choose:, :], 0.0), axis=0, keepdims=True)
+        jnp.sum(jnp.where(hit, route[choose:], 0.0), axis=0, keepdims=True)
         for hit, route in zip(hits, routes)
     ]
     chosen = jnp.concatenate(
@@ -92,10 +94,10 @@
 
 def weight_copies(expert, weights, held, sems):
     halves = []
-    for h in range(2):
+    for h in range(STREAMS):
         copies = []
         for k, (source, target) in enumerate(zip(weights, held)):
-            size = target.shape[0 if k == 2 else 1] // 2
+            size = target.shape[0 if k == 2 else 1] // STREAMS
             span = pl.ds(h * size, size)
             src, dst = (
                 (source.at[expert, span, :], target.at[span, :])
@@ -107,24 +109,54 @@
     return halves
 
 
-def pre_kernel(n, expert, deps, scal, *refs):
+def route_blocks(choose, count, width):
+    wide = max(1, width // count)
+    return [(16 * (b // wide), count * (b % wide)) for b in range(4 * choose // 16)]
+
+
+def pack_kernel(ids, combine, tokens, grads, pack):
+    count, width = tokens.shape
+    choose = ids.shape[0]
+    pack[0:count, :] = tokens[...]
+    pack[count : 2 * count, :] = grads[...]
+    lines = [ids[...].astype(F32)] + [part.astype(F32) for part in thirds(combine[...])]
+    lines = jnp.concatenate(lines, axis=0).astype(BF16)
+    blocks = route_blocks(choose, count, width)
+    pack[2 * count :, :] = jnp.zeros((pack.shape[0] - 2 * count, width), BF16)
+    for b, (row, lane) in enumerate(blocks):
+        pack[2 * count + row : 2 * count + row + 16, lane : lane + count] = lines[16 * b : 16 * b + 16]
+
+
+def unpack_route(pack, choose, count):
+    lines = [
+        pack[2 * count + row : 2 * count + row + 16, lane : lane + count]
+        for row, lane in route_blocks(choose, count, pack.shape[1])
+    ]
+    lines = jnp.concatenate(lines, axis=0).astype(F32)
+    ids, high, middle, low = (lines[k * choose : (k + 1) * choose] for k in range(4))
+    return jnp.concatenate([ids, (high + middle) + low], axis=0)
+
+
+def pre_kernel(n, expert, choose, deps, scal, *refs):
     refs = refs[deps:]
-    routes, packs, refs = refs[:n], refs[n : 2 * n], refs[2 * n :]
-    weights, (in_ref, cot_ref, *refs) = refs[:3], refs[3:]
-    outs, (token, gw, uw, dw, sems) = refs[: 2 * n], refs[2 * n :]
-    rows, tile = in_ref.shape[0] // n, gw.shape[1] // 2
+    packs, weights, (in_ref, cot_ref, *refs) = refs[:n], refs[n : n + 3], refs[n + 3 :]
+    outs, (token, routes, gw, uw, dw, sems) = refs[: STREAMS * n], refs[STREAMS * n :]
+    rows, tile, count = in_ref.shape[0] // n, gw.shape[1] // STREAMS, routes.shape[2]
     copies = weight_copies(expert, weights, (gw, uw, dw), sems)
     for group in copies:
         for copy in group:
             copy.start()
     token[...] = jnp.zeros_like(token)
-    for k, (position, weight, hit) in enumerate(routing(scal, routes, expert, rows)):
+    found = [unpack_route(pack, choose, count) for pack in packs]
+    for k in range(n):
+        routes[k] = found[k]
+    for k, (position, weight, hit) in enumerate(routing(scal, found, expert, rows)):
         pick = hit.astype(F32).astype(BF16)
         span = span_of(position, rows)
-        in_ref[span, :] = dot(pick, packs[k][0]).astype(BF16)
+        in_ref[span, :] = dot(pick, packs[k][0:count, :]).astype(BF16)
         scale = jnp.sum(jnp.where(hit, weight, 0.0), axis=1, keepdims=True)
-        cot_ref[span, :] = (dot(pick, packs[k][1]) * scale).astype(BF16)
-    for h in range(2):
+        cot_ref[span, :] = (dot(pick, packs[k][count : 2 * count, :]) * scale).astype(BF16)
+    for h in range(STREAMS):
         for copy in copies[h]:
             copy.wait()
         part = slice(h * tile, (h + 1) * tile)
@@ -165,8 +197,8 @@
         partial = [ref[...] for ref in earlier] + [acc]
         ones, fill = jnp.ones((8, lanes), BF16), jnp.zeros((lanes - rows, lanes), F32)
         lines = []
-        for e in range(len(partial) // 2):
-            wide = jnp.concatenate([partial[2 * e] + partial[2 * e + 1], fill], axis=0)
+        for e in range(len(partial) // STREAMS):
+            wide = jnp.concatenate([sum(partial[STREAMS * e : STREAMS * (e + 1)]), fill], axis=0)
             total = sum(dot(ones, part, ((1,), (1,))) for part in thirds(wide))[0:1]
             lines += [part.astype(F32) for part in thirds(total)]
         extra = out.shape[0] - 3 * rows
@@ -175,13 +207,6 @@
         out[3 * rows :, 0:lanes] = jnp.concatenate(lines, axis=0).astype(BF16)
 
 
-def pack_kernel(ids, combine, tokens, grads, pack, route):
-    pack[0] = tokens[...]
-    pack[1] = grads[...]
-    route[0 : ids.shape[0], :] = ids[...].astype(F32)
-    route[ids.shape[0] :, :] = combine[...]
-
-
 def add_kernel(deps, *refs):
     a, b, out = refs[deps:]
     out[...] = (a[...].astype(F32) + b[...].astype(F32)).astype(out.dtype)
@@ -203,7 +228,7 @@
 
 def split_pieces(refs, sizes):
     halves, at = [], 0
-    for _ in range(2):
+    for _ in range(STREAMS):
         pieces = [refs[at : at + 1]]
         at += 1
         for size in sizes:
@@ -215,7 +240,7 @@
 
 def out_kernel(n, expert, has_prev, last, sizes, deps, scal, *refs):
     refs = refs[deps:]
-    routes, refs = refs[:n], refs[n:]
+    routes, refs = [refs[0].at[k] for k in range(n)], refs[1:]
     if has_prev:
         prev, refs = refs[:2], refs[2:]
     halves, refs = split_pieces(refs, sizes)
@@ -230,10 +255,10 @@
     token[...] = jnp.zeros_like(token)
     spots = routing(scal, routes, expert, halves[0][0][0].shape[0] // 48 * 16)
     if last:
-        send_products(scal, routes, expert + 1, halves[1], held, near_p, far_p)
-    tile = gw.shape[1] // 2
+        send_products(scal, routes, expert + 1, halves[-1], held, near_p, far_p)
+    tile = gw.shape[1] // STREAMS
     eo, idl = 0.0, 0.0
-    for h in range(2):
+    for h in range(STREAMS):
         for copy in copies[h]:
             copy.wait()
         part = slice(h * tile, (h + 1) * tile)
@@ -264,7 +289,7 @@
     gg, ug, dg, token = refs
     step = pl.program_id(0)
     token[...] = jnp.zeros_like(token)
-    for h in range(2):
+    for h in range(STREAMS):
 
         @pl.when(step == h)
         def _():
@@ -338,7 +363,7 @@
     capacity = count * choose * 5 // (4 * experts_all)
     rows = -(-capacity // 16) * 16
     all_rows = n * rows
-    tile = hidden // 2
+    tile = hidden // STREAMS
     swaps = n == 4
 
     me, here = lax.axis_index("expert"), lax.axis_index("dp")
@@ -374,17 +399,19 @@
         ]
         return found + [across.send(piece, swap) for piece in found]
 
-    pack, route = call(
+    route_rows = 16 + max(row for row, _ in route_blocks(choose, count, width))
+    pack_shape = (2 * count + route_rows, width)
+    pack = call(
         pack_kernel,
         1,
         [spec_of(ids_t), spec_of(combine_t), spec_of(tokens), spec_of(out_grad)],
-        [whole_spec((2, count, width)), whole_spec((2 * choose, count))],
-        [like((2, count, width)), like((2 * choose, count), F32)],
+        whole_spec(pack_shape),
+        like(pack_shape),
         count * width,
         8 * count * width,
     )(*(in_hbm(x) for x in (ids_t, combine_t, tokens, out_grad)))
-    routes, packs = gather_blocks(route), gather_blocks(pack)
-    route_specs, pack_specs = [spec_of(x) for x in routes], [spec_of(x) for x in packs]
+    packs = gather_blocks(pack)
+    route_shape = (n, 2 * choose, count)
 
     mac = all_rows * width * hidden
     weight_bytes = 2 * width * hidden
@@ -396,7 +423,7 @@
 
     weights = [in_hbm(w) for w in (gate_weight, up_weight, down_weight)]
     held_weights = [pltpu.VMEM(w.shape[1:], BF16) for w in weights] + [
-        pltpu.SemaphoreType.DMA((2, 3))
+        pltpu.SemaphoreType.DMA((STREAMS, 3))
     ]
 
     def grad_specs(e):
@@ -404,20 +431,25 @@
         return [wide, wide, pl.BlockSpec((1, tile, width), lambda g: (e, g, 0))]
 
     def pre(e, deps):
-        inputs, cot, *parts, token = call(
-            functools.partial(pre_kernel, n, e, len(deps)),
+        inputs, cot, *parts, token, found = call(
+            functools.partial(pre_kernel, n, e, choose, len(deps)),
             1,
-            [SMEM_SPEC] + [ANY_SPEC] * len(deps) + route_specs + pack_specs + [HBM_SPEC] * 3,
-            [whole_spec(slot_shape)] * 2 + [whole_spec(piece_shape)] * (2 * n) + [whole_spec(TOKEN)],
-            [like(slot_shape)] * 2 + [like(piece_shape)] * (2 * n) + [like(TOKEN, F32)],
+            [SMEM_SPEC] + [ANY_SPEC] * len(deps) + [spec_of(x) for x in packs] + [HBM_SPEC] * 3,
+            [whole_spec(slot_shape)] * 2
+            + [whole_spec(piece_shape)] * (STREAMS * n)
+            + [whole_spec(TOKEN), whole_spec(route_shape)],
+            [like(slot_shape)] * 2
+            + [like(piece_shape)] * (STREAMS * n)
+            + [like(TOKEN, F32), like(route_shape, F32)],
             6 * mac,
-            3 * weight_bytes + 2 * n * piece_bytes,
+            3 * weight_bytes + STREAMS * n * piece_bytes,
             scratch_shapes=held_weights,
-        )(scal, *deps, *routes, *packs, *weights)
-        return (inputs, cot), [parts[:n], parts[n:]], token
+        )(scal, *deps, *packs, *weights)
+        parts = [parts[h * n : (h + 1) * n] for h in range(STREAMS)]
+        return (inputs, cot), parts, token, found
 
     def mid(e, h, totals, products, deps=()):
-        others = products if e == local - 1 and h == 1 else []
+        others = products if e == local - 1 and h == STREAMS - 1 else []
         shape = wide_shape if others else piece_shape
         return call(
             functools.partial(mid_kernel, len(deps), len(others)),
@@ -458,7 +490,7 @@
             1,
             [SMEM_SPEC]
             + [ANY_SPEC] * len(deps)
-            + route_specs
+            + [whole_spec(route_shape)]
             + ([whole_spec(sum_shape)] * 2 if e > 0 else [])
             + [spec_of(x) for x in flat]
             + [HBM_SPEC] * 3,
@@ -473,14 +505,14 @@
             scratch_shapes=held_weights
             + [pltpu.VMEM(slot_shape, BF16)] * 2
             + ([pltpu.VMEM((n, extra, 128), BF16)] if last else []),
-        )(scal, *deps, *routes, *prev, *flat, *weights)
+        )(scal, *deps, routes, *prev, *flat, *weights)
 
     def grad(e, slots, halves, prev, deps):
         flat = flatten(halves)
         base = 3 + len(deps) + len(flat)
         return call(
             functools.partial(grad_kernel, n, e > 0, sizes_of(halves[0]), len(deps)),
-            2,
+            STREAMS,
             [SMEM_SPEC]
             + [whole_spec(slot_shape)] * 2
             + [ANY_SPEC] * len(deps)
@@ -517,32 +549,33 @@
         return near, home if left is None else home + left.astype(F32)
 
     if swaps:
-        flight, arrived = [None, None], None
-        slots, parts, _ = pre(0, [])
+        flight, arrived, streams = [None] * STREAMS, None, range(STREAMS)
+        slots, parts, _, routes = pre(0, [])
         grad_token = None
         for e in range(local):
-            more = e < local - 1
+            following = e < local - 1
             first, second, totals, halves = [], [], [], []
-            for h in range(2):
+            for h in streams:
                 x = parts[h]
                 if e == 0:
                     first.append((outer(x[3]), None))
                 else:
                     y, got_a, got_b = flight[h]
                     first.append((outer(jnp.where(at_end, x[3], got_b)), inner(got_a)))
-            if more:
-                begun = pre(e + 1, [first[0][0]] if e == 0 else [flight[1][2]])
-            for h in range(2):
+            seen = [[] for _ in streams]
+            if following:
+                next_slots, next_parts, token, _ = pre(e + 1, [] if e == 0 else [flight[1][2]])
+                seen[0 if e == 0 else STREAMS - 1].append(token)
+            if grad_token is not None:
+                seen[0].append(grad_token)
+            for h in streams:
                 x, (a1, b1) = parts[h], first[h]
-                tokens_seen = [begun[2]] if more and h == 1 else []
-                if grad_token is not None and h == 0:
-                    tokens_seen = [grad_token]
                 send_a2 = x[2] if e == 0 else jnp.where(at_end, x[2], b1)
-                second.append((outer(send_a2), inner(add(x[3], a1, tokens_seen))))
+                second.append((outer(send_a2), inner(add(x[3], a1, seen[h]))))
                 if e > 0:
                     y, got_a, got_b = flight[h]
                     halves.append([(y,), (got_a,), (a1, got_b), (second[h][0], b1)])
-            for h in range(2):
+            for h in streams:
                 x, (a2, b2) = parts[h], second[h]
                 a3 = outer(jnp.where(at_end, x[1], add_rounded(x[1], b2)))
                 b3 = inner(unless_end(add_rounded(x[2], a2)))
@@ -551,17 +584,17 @@
             if e > 0:
                 *sums, out_token = out(e - 1, halves, sums, [])
                 wait = [out_token]
-            for h in range(2):
+            for h in streams:
                 y, product = mid(e, h, totals[h], products, wait if h == 0 else [])
                 products.append(product)
                 flight[h] = (y, outer(y), inner(y))
             if e > 0:
-                *grads, grad_token = grad(e - 1, arrived, halves, grads, [flight[1][0]])
+                *grads, grad_token = grad(e - 1, arrived, halves, grads, [flight[-1][0]])
             arrived = slots
-            if more:
-                slots, parts, _ = begun
+            if following:
+                slots, parts = next_slots, next_parts
         halves = []
-        for h in range(2):
+        for h in streams:
             y, got_a, got_b = flight[h]
             a1, b1 = outer(got_b), inner(got_a)
             a2 = outer(b1)
@@ -570,11 +603,11 @@
     else:
         begun = []
         for e in range(local):
-            slots, parts, _ = pre(e, [])
+            slots, parts, _, routes = pre(e, [])
             begun.append((slots, [(x[0], *along_z.scatter(x, add_rounded)) for x in parts]))
         for e in range(local):
             halves, arrived, wait = [], begun[e][0], []
-            for h in range(2):
+            for h in range(STREAMS):
                 y, product = mid(e, h, begun[e][1][h], products)
                 products.append(product)
                 halves.append([(y,)] + along_z.gather(y))
@@ -584,8 +617,8 @@
 
     near, far, _, near_p, far_p = out(local - 1, halves, sums, wait)
     hop, home = send_home(near, far, add_rounded)
-    _, per_expert = send_home(near_p, far_p, lambda a, b: add(a, b, [hop]))
-    *grads, _ = grad(local - 1, arrived, halves, grads, [hop])
+    *grads, token = grad(local - 1, arrived, halves, grads, [hop])
+    _, per_expert = send_home(near_p, far_p, lambda a, b: add(a, b, [token]))
     combine_grad = jnp.sum(jnp.where(named, per_expert[None], 0.0), axis=1) / combine_t
     return (home[0].astype(BF16), home[1].astype(BF16), *grads, combine_grad.T)
 

time: 205 us -> 220 us (1.073)
  starting transfers between devices: 92.5 us -> 130 us
  waiting for transfers between devices: 62.1 us -> 37.7 us
    ppermute x46 -> x61, starting transfers between devices: 89.6 us -> 123 us  [send(): return lax.ppermute(value, self.axis, wide)]
    ppermute x46 -> x61, waiting for transfers between devices: 62 us -> 37.6 us  [send(): return lax.ppermute(value, self.axis, wide)]
    ppermute x32 -> x48, starting transfers between devices: 2.98 us -> 6.48 us  [inner(): return lax.ppermute(value, ('expert', 'dp'), pairs)]
  transfers between devices with their start and end apart: 78 -> 109, of which waited for: 23 -> 18; matrix products, arithmetic and copies ran while one was open for 1% -> 1% of each run, Pallas kernels for 18% -> 17%
where the time goes in v9:
time: 220 us; the launch traced here: 219 us
  starting transfers between devices  130 us (59%)
  Pallas kernels  47.2 us (21%)
  waiting for transfers between devices  37.7 us (17%)
    ppermute x61, starting transfers between devices, send(): return lax.ppermute(value, self.axis, wide)  123 us
    ppermute x61, waiting for transfers between devices, send(): return lax.ppermute(value, self.axis, wide)  37.6 us
    pallas_call x4, Pallas kernels, pre(): call(functools.partial(pre_kernel, n, e, choose, len(deps)), 1, [SMEM_SPE...  16 us
    pallas_call x4, Pallas kernels, grad(): call(functools.partial(grad_kernel, n, e > 0, sizes_of(halves[0]), len(de...  14.5 us
    pallas_call x4, Pallas kernels, out(): call(functools.partial(out_kernel, n, e, e > 0, last, sizes_of(halves[0])...  13.5 us
    ppermute x48, starting transfers between devices, inner(): return lax.ppermute(value, ('expert', 'dp'), pairs)  6.48 us
  transfers between devices with their start and end apart: 109, of which 18 were waited for; matrix products, arithmetic and copies ran while one was open for 1% of the time, Pallas kernels for 17%

profile of v9, /device:TPU:0, one launch (start us, length us, event | category | flops | bytes accessed | tf_op | source)
XLA Modules:
  0.0 219.2 jit_solution(16586819187272793720)
XLA Ops:
  1.7 3.0 %collective-permute-start = (bf16[272,512]{1,0:T(8,128)(2,1)S(1)}, bf16[272,512]{1,0:T(8,128)(2,1)S(1)}, u32[]{:S(2)}, u32[]{:S(2)}) collective-permute-start(bf16[272,512]{1,0:T(8,128)(2,1)S(1)} %shard_map.118.refs_0_.refs_1_), channel_id=1, source_target_pairs={{0,8},{4,12},{8,0},{12,4},{1,9},{5,13},{9,1},{13,5},{2,10},{6,14},... | collective-permute-start | bytes 835592 | tf_op jit(solution)/shard_map/ppermute | solution.py:33
  4.7 6.7 %collective-permute-done.refs_1_.refs_2_ = bf16[272,512]{1,0:T(8,128)(2,1)S(1)} collective-permute-done((bf16[272,512]{1,0:T(8,128)(2,1)S(1)}, bf16[272,512]{1,0:T(8,128)(2,1)S(1)}, u32[]{:S(2)}, u32[]{:S(2)}) %collective-permute-start) | collective-permute-done | bytes 278560 | tf_op jit(solution)/shard_map/ppermute | solution.py:33
  11.4 1.5 collective-permute-done.2.refs_3_.refs_4_
  12.9 3.7 %shard_map.119 = (bf16[320,512]{1,0:T(8,128)(2,1)S(1)}, bf16[320,512]{1,0:T(8,128)(2,1)S(1)}, bf16[240,256]{1,0:T(8,128)(2,1)S(1)}, bf16[240,256]{1,0:T(8,128)(2...) custom-call(s32[10]{0:T(128)S(1)} %stack.35.scal, ...), custom_call_target="tpu_custom_call" | custom-call | flops 754974720 | bytes 3833856 | tf_op jit(solution)/shard_map/pallas_call | solution.py:434
  16.6 1.9 collective-permute-start.6
  18.7 1.8 collective-permute-start.46
  20.7 1.8 collective-permute-start.17
  22.5 4.1 %shard_map.123 = (bf16[320,512]{1,0:T(8,128)(2,1)S(1)}, bf16[320,512]{1,0:T(8,128)(2,1)S(1)}, bf16[240,256]{1,0:T(8,128)(2,1)S(1)}, bf16[240,256]{1,0:T(8,128)(2...) custom-call(s32[10]{0:T(128)S(1)} %stack.35.scal, ...), custom_call_target="tpu_custom_call" | custom-call | flops 754974720 | bytes 3833856 | tf_op jit(solution)/shard_map/pallas_call | solution.py:434
  28.1 2.6 %collective-permute-done.49 = bf16[240,256]{1,0:T(8,128)(2,1)S(1)} collective-permute-done((bf16[240,256]{1,0:T(8,128)(2,1)S(1)}, bf16[240,256]{1,0:T(8,128)(2,1)S(1)}, u32[]{:S(2)}, u32[]{:S(2)}) %collective-permute-start.49) | collective-permute-done | bytes 122912 | tf_op jit(solution)/shard_map/ppermute | solution.py:33
  30.8 2.6 %collective-permute-done.17.refs_1_ = bf16[240,256]{1,0:T(8,128)(2,1)S(1)} collective-permute-done((bf16[240,256]{1,0:T(8,128)(2,1)S(1)}, bf16[240,256]{1,0:T(8,128)(2,1)S(1)}, u32[]{:S(2)}, u32[]{:S(2)}) %collective-permute-start.17) | collective-permute-done | bytes 122912 | tf_op jit(solution)/shard_map/ppermute | solution.py:33
  33.4 1.9 collective-permute-done.20
  36.0 3.5 %collective-permute-start.5 = (bf16[240,256]{1,0:T(8,128)(2,1)S(1)}, bf16[240,256]{1,0:T(8,128)(2,1)S(1)}, u32[]{:S(2)}, u32[]{:S(2)}) collective-permute-start(bf16[240,256]{1,0:T(8,128)(2,1)S(1)} %fusion.1), channel_id=1, source_target_pairs={{0,1},{1,0},{2,3},{3,2},{4,5},{5,4},{6,7},{7,6},{8,9},{9,8},{10,11... | collective-permute-start | bytes 368648 | tf_op jit(solution)/shard_map/ppermute | solution.py:33
  39.5 5.0 %collective-permute-start.48 = (bf16[240,256]{1,0:T(8,128)(2,1)S(1)}, bf16[240,256]{1,0:T(8,128)(2,1)S(1)}, u32[]{:S(2)}, u32[]{:S(2)}) collective-permute-start(bf16[240,256]{1,0:T(8,128)(2,1)S(1)} %fusion.7), channel_id=1, source_target_pairs={{0,1},{1,0},{2,3},{3,2},{4,5},{5,4},{6,7},{7,6},{8,9},{9,8},{10,11... | collective-permute-start | bytes 368648 | tf_op jit(solution)/shard_map/ppermute | solution.py:33
  44.8 3.5 %collective-permute-start.12 = (bf16[240,256]{1,0:T(8,128)(2,1)S(1)}, bf16[240,256]{1,0:T(8,128)(2,1)S(1)}, u32[]{:S(2)}, u32[]{:S(2)}) collective-permute-start(bf16[240,256]{1,0:T(8,128)(2,1)S(1)} %get-tuple-element.122.refs_7_), channel_id=1, source_target_pairs={{0,1},{1,0},{2,3},{3,2},{4,5},{5,4},{6,7},{7,6},{8,9},{9,8},{10,11... | collective-permute-start | bytes 368648 | tf_op jit(solution)/shard_map/ppermute | solution.py:33
  48.4 2.3 %collective-permute-start.51 = (bf16[240,256]{1,0:T(8,128)(2,1)S(1)}, bf16[240,256]{1,0:T(8,128)(2,1)S(1)}, u32[]{:S(2)}, u32[]{:S(2)}) collective-permute-start(bf16[240,256]{1,0:T(8,128)(2,1)S(1)} %get-tuple-element.160.refs_1_), channel_id=1, source_target_pairs={{0,1},{1,0},{2,3},{3,2},{4,5},{5,4},{6,7},{7,6},{8,9},{9,8},{10,11... | collective-permute-start | bytes 368648 | tf_op jit(solution)/shard_map/ppermute | solution.py:33
  50.9 2.4 %collective-permute-start.26 = (bf16[240,256]{1,0:T(8,128)(2,1)S(1)}, bf16[240,256]{1,0:T(8,128)(2,1)S(1)}, u32[]{:S(2)}, u32[]{:S(2)}) collective-permute-start(bf16[240,256]{1,0:T(8,128)(2,1)S(1)} %get-tuple-element.145.refs_13_), channel_id=1, source_target_pairs={{0,1},{1,0},{2,3},{3,2},{4,5},{5,4},{6,7},{7,6},{8,9},{9,8},{10,11... | collective-permute-start | bytes 368648 | tf_op jit(solution)/shard_map/ppermute | solution.py:33
  53.4 2.3 %collective-permute-start.9 = (bf16[240,256]{1,0:T(8,128)(2,1)S(1)}, bf16[240,256]{1,0:T(8,128)(2,1)S(1)}, u32[]{:S(2)}, u32[]{:S(2)}) collective-permute-start(bf16[240,256]{1,0:T(8,128)(2,1)S(1)} %broadcast_select_fusion.17), channel_id=1, source_target_pairs={{0,1},{1,0},{2,3},{3,2},{4,5},{5,4},{6,7},{7,6},{8,9},{9,8},{10,11... | collective-permute-start | bytes 368648 | tf_op jit(solution)/shard_map/ppermute | solution.py:33
  55.9 4.1 %shard_map.122 = (bf16[320,512]{1,0:T(8,128)(2,1)S(1)}, bf16[320,512]{1,0:T(8,128)(2,1)S(1)}, bf16[240,256]{1,0:T(8,128)(2,1)S(1)}, bf16[240,256]{1,0:T(8,128)(2...) custom-call(s32[10]{0:T(128)S(1)} %stack.35.scal, ...), custom_call_target="tpu_custom_call" | custom-call | flops 754974720 | bytes 3833856 | tf_op jit(solution)/shard_map/pallas_call | solution.py:434
  60.0 4.1 %collective-permute-start.23 = (bf16[240,256]{1,0:T(8,128)(2,1)S(1)}, bf16[240,256]{1,0:T(8,128)(2,1)S(1)}, u32[]{:S(2)}, u32[]{:S(2)}) collective-permute-start(bf16[240,256]{1,0:T(8,128)(2,1)S(1)} %broadcast_select_fusion.15), channel_id=1, source_target_pairs={{0,1},{1,0},{2,3},{3,2},{4,5},{5,4},{6,7},{7,6},{8,9},{9,8},{10,11... | collective-permute-start | bytes 368648 | tf_op jit(solution)/shard_map/ppermute | solution.py:33
  64.6 1.7 collective-permute-start.14
  66.4 5.4 %collective-permute-start.55 = (bf16[240,256]{1,0:T(8,128)(2,1)S(1)}, bf16[240,256]{1,0:T(8,128)(2,1)S(1)}, u32[]{:S(2)}, u32[]{:S(2)}) collective-permute-start(bf16[240,256]{1,0:T(8,128)(2,1)S(1)} %broadcast_select_fusion.8), channel_id=1, source_target_pairs={{0,1},{1,0},{2,3},{3,2},{4,5},{5,4},{6,7},{7,6},{8,9},{9,8},{10,11... | collective-permute-start | bytes 368648 | tf_op jit(solution)/shard_map/ppermute | solution.py:33
  72.9 4.8 %collective-permute-done.28.refs_17_ = bf16[240,256]{1,0:T(8,128)(2,1)S(1)} collective-permute-done((bf16[240,256]{1,0:T(8,128)(2,1)S(1)}, bf16[240,256]{1,0:T(8,128)(2,1)S(1)}, u32[]{:S(2)}, u32[]{:S(2)}) %collective-permute-start.28) | collective-permute-done | bytes 122912 | tf_op jit(solution)/shard_map/ppermute | solution.py:33
  77.7 1.4 collective-permute-start.11
  79.9 4.3 %collective-permute-start.57 = (bf16[240,256]{1,0:T(8,128)(2,1)S(1)}, bf16[240,256]{1,0:T(8,128)(2,1)S(1)}, u32[]{:S(2)}, u32[]{:S(2)}) collective-permute-start(bf16[240,256]{1,0:T(8,128)(2,1)S(1)} %fusion.8), channel_id=1, source_target_pairs={{0,1},{1,0},{2,3},{3,2},{4,5},{5,4},{6,7},{7,6},{8,9},{9,8},{10,11... | collective-permute-start | bytes 368648 | tf_op jit(solution)/shard_map/ppermute | solution.py:33
  84.5 3.3 %shard_map.136 = (f32[2,2,128,512]{3,2,1,0:T(8,128)S(1)}, f32[2,2,128,512]{3,2,1,0:T(8,128)S(1)}, f32[8,128]{1,0:T(8,128)S(1)}) custom-call(s32[10]{0:T(128)S(1)} %stack.35.scal, f32[4,16,128]{2,1,0:T(8,128)S(1)} %get-tuple-element.159.refs_0_.refs_1_, bf16[240,256]{1,0:T(8,128)(2,1)S(1)} %get-tuple-element.160.refs_1_, ...), custom_call_target="tpu_custom_call" | custom-call | flops 754974720 | bytes 4571136 | tf_op jit(solution)/shard_map/pallas_call | solution.py:488
  87.8 2.7 %collective-permute-start.64 = (bf16[240,256]{1,0:T(8,128)(2,1)S(1)}, bf16[240,256]{1,0:T(8,128)(2,1)S(1)}, u32[]{:S(2)}, u32[]{:S(2)}) collective-permute-start(bf16[240,256]{1,0:T(8,128)(2,1)S(1)} %get-tuple-element.129.refs_9_.refs_7_), channel_id=1, source_target_pairs={{0,1},{1,0},{2,3},{3,2},{4,5},{5,4},{6,7},{7,6},{8,9},{9,8},{10,11... | collective-permute-start | bytes 368648 | tf_op jit(solution)/shard_map/ppermute | solution.py:33
  93.0 3.6 %shard_map.140 = (bf16[4,512,768]{2,1,0:T(8,128)(2,1)}, bf16[4,512,768]{2,1,0:T(8,128)(2,1)}, bf16[4,768,512]{2,1,0:T(8,128)(2,1)}, f32[8,128]{1,0:T(8,128)S(1)}) custom-call(s32[10]{0:T(128)S(1)} %stack.35.scal, bf16[320,512]{1,0:T(8,128)(2,1)S(1)} %get-tuple-element.179.in_ref, bf16[320,512]{1,0:T(8,128)(2,1)S(1)} %get-tuple-element.180.cot_ref, ...), custom_call_target="tpu_custom_call" | custom-call | flops 754974720 | bytes 4571136 | tf_op jit(solution)/shard_map/pallas_call | solution.py:513
  96.6 2.0 collective-permute-start.65
  98.9 4.1 %shard_map.126 = (bf16[320,512]{1,0:T(8,128)(2,1)S(1)}, bf16[320,512]{1,0:T(8,128)(2,1)S(1)}, bf16[240,256]{1,0:T(8,128)(2,1)S(1)}, bf16[240,256]{1,0:T(8,128)(2...) custom-call(s32[10]{0:T(128)S(1)} %stack.35.scal, ...), custom_call_target="tpu_custom_call" | custom-call | flops 754974720 | bytes 3833856 | tf_op jit(solution)/shard_map/pallas_call | solution.py:434
  103.0 4.7 %collective-permute-start.31 = (bf16[240,256]{1,0:T(8,128)(2,1)S(1)}, bf16[240,256]{1,0:T(8,128)(2,1)S(1)}, u32[]{:S(2)}, u32[]{:S(2)}) collective-permute-start(bf16[240,256]{1,0:T(8,128)(2,1)S(1)} %broadcast_select_fusion.13), channel_id=1, source_target_pairs={{0,1},{1,0},{2,3},{3,2},{4,5},{5,4},{6,7},{7,6},{8,9},{9,8},{10,11... | collective-permute-start | bytes 368648 | tf_op jit(solution)/shard_map/ppermute | solution.py:33
  108.5 2.8 %collective-permute-start.67 = (bf16[240,256]{1,0:T(8,128)(2,1)S(1)}, bf16[240,256]{1,0:T(8,128)(2,1)S(1)}, u32[]{:S(2)}, u32[]{:S(2)}) collective-permute-start(bf16[240,256]{1,0:T(8,128)(2,1)S(1)} %broadcast_select_fusion.4), channel_id=1, source_target_pairs={{0,1},{1,0},{2,3},{3,2},{4,5},{5,4},{6,7},{7,6},{8,9},{9,8},{10,11... | collective-permute-start | bytes 368648 | tf_op jit(solution)/shard_map/ppermute | solution.py:33
  111.4 5.3 %collective-permute-start.63 = (bf16[240,256]{1,0:T(8,128)(2,1)S(1)}, bf16[240,256]{1,0:T(8,128)(2,1)S(1)}, u32[]{:S(2)}, u32[]{:S(2)}) collective-permute-start(bf16[240,256]{1,0:T(8,128)(2,1)S(1)} %broadcast_select_fusion.6), channel_id=1, source_target_pairs={{0,1},{1,0},{2,3},{3,2},{4,5},{5,4},{6,7},{7,6},{8,9},{9,8},{10,11... | collective-permute-start | bytes 368648 | tf_op jit(solution)/shard_map/ppermute | solution.py:33
  117.0 2.9 %collective-permute-start.72 = (bf16[240,256]{1,0:T(8,128)(2,1)S(1)}, bf16[240,256]{1,0:T(8,128)(2,1)S(1)}, u32[]{:S(2)}, u32[]{:S(2)}) collective-permute-start(bf16[240,256]{1,0:T(8,128)(2,1)S(1)} %fusion.10), channel_id=1, source_target_pairs={{0,1},{1,0},{2,3},{3,2},{4,5},{5,4},{6,7},{7,6},{8,9},{9,8},{10,11... | collective-permute-start | bytes 368648 | tf_op jit(solution)/shard_map/ppermute | solution.py:33
  120.3 2.5 %collective-permute-start.69 = (bf16[240,256]{1,0:T(8,128)(2,1)S(1)}, bf16[240,256]{1,0:T(8,128)(2,1)S(1)}, u32[]{:S(2)}, u32[]{:S(2)}) collective-permute-start(bf16[240,256]{1,0:T(8,128)(2,1)S(1)} %fusion.9), channel_id=1, source_target_pairs={{0,1},{1,0},{2,3},{3,2},{4,5},{5,4},{6,7},{7,6},{8,9},{9,8},{10,11... | collective-permute-start | bytes 368648 | tf_op jit(solution)/shard_map/ppermute | solution.py:33
  123.6 1.3 collective-permute-done.72.refs_1_
  124.9 2.2 %collective-permute-start.33 = (bf16[240,256]{1,0:T(8,128)(2,1)S(1)}, bf16[240,256]{1,0:T(8,128)(2,1)S(1)}, u32[]{:S(2)}, u32[]{:S(2)}) collective-permute-start(bf16[240,256]{1,0:T(8,128)(2,1)S(1)} %fusion.5), channel_id=1, source_target_pairs={{0,1},{1,0},{2,3},{3,2},{4,5},{5,4},{6,7},{7,6},{8,9},{9,8},{10,11... | collective-permute-start | bytes 368648 | tf_op jit(solution)/shard_map/ppermute | solution.py:33
  127.3 3.3 %shard_map.139 = (f32[2,2,128,512]{3,2,1,0:T(8,128)S(1)}, f32[2,2,128,512]{3,2,1,0:T(8,128)S(1)}, f32[8,128]{1,0:T(8,128)S(1)}) custom-call(s32[10]{0:T(128)S(1)} %stack.35.scal, f32[4,16,128]{2,1,0:T(8,128)S(1)} %get-tuple-element.159.refs_0_.refs_1_, f32[2,2,128,512]{3,2,1,0:T(8,128)S(1)} %get-tuple-element.169.refs_1_, ...), custom_call_target="tpu_custom_call" | custom-call | flops 754974720 | bytes 4571136 | tf_op jit(solution)/shard_map/pallas_call | solution.py:488
  131.1 1.8 collective-permute-start.74
  133.0 2.1 collective-permute-start.42
  135.0 3.6 %shard_map.146 = (bf16[4,512,768]{2,1,0:T(8,128)(2,1)}, bf16[4,512,768]{2,1,0:T(8,128)(2,1)}, bf16[4,768,512]{2,1,0:T(8,128)(2,1)}, f32[8,128]{1,0:T(8,128)S(1)}) custom-call(s32[10]{0:T(128)S(1)} %stack.35.scal, bf16[320,512]{1,0:T(8,128)(2,1)S(1)} %get-tuple-element.198.in_ref, ...), custom_call_target="tpu_custom_call", output_to_operand_aliasing={{0}: (22, {}), {1}: (23, {}), {2}: (24, {})} | custom-call | flops 754974720 | bytes 4571136 | tf_op jit(solution)/shard_map/pallas_call | solution.py:513
  139.2 1.7 collective-permute-start.76
  140.9 3.7 %collective-permute-start.39 = (bf16[240,256]{1,0:T(8,128)(2,1)S(1)}, bf16[240,256]{1,0:T(8,128)(2,1)S(1)}, u32[]{:S(2)}, u32[]{:S(2)}) collective-permute-start(bf16[240,256]{1,0:T(8,128)(2,1)S(1)} %broadcast_select_fusion.11), channel_id=1, source_target_pairs={{0,1},{1,0},{2,3},{3,2},{4,5},{5,4},{6,7},{7,6},{8,9},{9,8},{10,11... | collective-permute-start | bytes 368648 | tf_op jit(solution)/shard_map/ppermute | solution.py:33
  145.1 5.6 %collective-permute-start.83 = (bf16[240,256]{1,0:T(8,128)(2,1)S(1)}, bf16[240,256]{1,0:T(8,128)(2,1)S(1)}, u32[]{:S(2)}, u32[]{:S(2)}) collective-permute-start(bf16[240,256]{1,0:T(8,128)(2,1)S(1)} %broadcast_select_fusion), channel_id=1, source_target_pairs={{0,1},{1,0},{2,3},{3,2},{4,5},{5,4},{6,7},{7,6},{8,9},{9,8},{10,11... | collective-permute-start | bytes 368648 | tf_op jit(solution)/shard_map/ppermute | solution.py:33
  150.9 2.4 %collective-permute-start.78 = (bf16[240,256]{1,0:T(8,128)(2,1)S(1)}, bf16[240,256]{1,0:T(8,128)(2,1)S(1)}, u32[]{:S(2)}, u32[]{:S(2)}) collective-permute-start(bf16[240,256]{1,0:T(8,128)(2,1)S(1)} %broadcast_select_fusion.2), channel_id=1, source_target_pairs={{0,1},{1,0},{2,3},{3,2},{4,5},{5,4},{6,7},{7,6},{8,9},{9,8},{10,11... | collective-permute-start | bytes 368648 | tf_op jit(solution)/shard_map/ppermute | solution.py:33
  153.5 2.5 %collective-permute-start.44 = (bf16[240,256]{1,0:T(8,128)(2,1)S(1)}, bf16[240,256]{1,0:T(8,128)(2,1)S(1)}, u32[]{:S(2)}, u32[]{:S(2)}) collective-permute-start(bf16[240,256]{1,0:T(8,128)(2,1)S(1)} %broadcast_select_fusion.10), channel_id=1, source_target_pairs={{0,1},{1,0},{2,3},{3,2},{4,5},{5,4},{6,7},{7,6},{8,9},{9,8},{10,11... | collective-permute-start | bytes 368648 | tf_op jit(solution)/shard_map/ppermute | solution.py:33
  156.9 2.5 %collective-permute-start.88 = (bf16[240,256]{1,0:T(8,128)(2,1)S(1)}, bf16[240,256]{1,0:T(8,128)(2,1)S(1)}, u32[]{:S(2)}, u32[]{:S(2)}) collective-permute-start(bf16[240,256]{1,0:T(8,128)(2,1)S(1)} %fusion.12), channel_id=1, source_target_pairs={{0,1},{1,0},{2,3},{3,2},{4,5},{5,4},{6,7},{7,6},{8,9},{9,8},{10,11... | collective-permute-start | bytes 368648 | tf_op jit(solution)/shard_map/ppermute | solution.py:33
  159.6 2.4 %collective-permute-start.85 = (bf16[240,256]{1,0:T(8,128)(2,1)S(1)}, bf16[240,256]{1,0:T(8,128)(2,1)S(1)}, u32[]{:S(2)}, u32[]{:S(2)}) collective-permute-start(bf16[240,256]{1,0:T(8,128)(2,1)S(1)} %fusion.11), channel_id=1, source_target_pairs={{0,1},{1,0},{2,3},{3,2},{4,5},{5,4},{6,7},{7,6},{8,9},{9,8},{10,11... | collective-permute-start | bytes 368648 | tf_op jit(solution)/shard_map/ppermute | solution.py:33
  162.1 4.6 %collective-permute-start.41 = (bf16[240,256]{1,0:T(8,128)(2,1)S(1)}, bf16[240,256]{1,0:T(8,128)(2,1)S(1)}, u32[]{:S(2)}, u32[]{:S(2)}) collective-permute-start(bf16[240,256]{1,0:T(8,128)(2,1)S(1)} %fusion.6), channel_id=1, source_target_pairs={{0,1},{1,0},{2,3},{3,2},{4,5},{5,4},{6,7},{7,6},{8,9},{9,8},{10,11... | collective-permute-start | bytes 368648 | tf_op jit(solution)/shard_map/ppermute | solution.py:33
  166.8 3.2 %shard_map.145 = (f32[2,2,128,512]{3,2,1,0:T(8,128)S(1)}, f32[2,2,128,512]{3,2,1,0:T(8,128)S(1)}, f32[8,128]{1,0:T(8,128)S(1)}) custom-call(s32[10]{0:T(128)S(1)} %stack.35.scal, f32[4,16,128]{2,1,0:T(8,128)S(1)} %get-tuple-element.159.refs_0_.refs_1_, f32[2,2,128,512]{3,2,1,0:T(8,128)S(1)} %get-tuple-element.187.refs_1_, ...), custom_call_target="tpu_custom_call" | custom-call | flops 754974720 | bytes 4571136 | tf_op jit(solution)/shard_map/pallas_call | solution.py:488
  171.0 1.4 collective-permute-start.100
  173.1 1.8 collective-permute-start.90
  174.9 3.5 %collective-permute-done.95.refs_11_.refs_8_ = bf16[240,256]{1,0:T(8,128)(2,1)S(1)} collective-permute-done((bf16[240,256]{1,0:T(8,128)(2,1)S(1)}, bf16[240,256]{1,0:T(8,128)(2,1)S(1)}, u32[]{:S(2)}, u32[]{:S(2)}) %collective-permute-start.95) | collective-permute-done | bytes 122912 | tf_op jit(solution)/shard_map/ppermute | solution.py:33
  179.9 2.5 %collective-permute-start.97 = (bf16[240,256]{1,0:T(8,128)(2,1)S(1)}, bf16[240,256]{1,0:T(8,128)(2,1)S(1)}, u32[]{:S(2)}, u32[]{:S(2)}) collective-permute-start(bf16[240,256]{1,0:T(8,128)(2,1)S(1)} %collective-permute-done.96.refs_13_.refs_10_), channel_id=1, source_target_pairs={{0,1},{1,0},{2,3},{3,2},{4,5},{5,4},{6,7},{7,6},{8,9},{9,8},{10,11... | collective-permute-start | bytes 368648 | tf_op jit(solution)/shard_map/ppermute | solution.py:33
  182.5 3.9 %collective-permute-start.102 = (bf16[256,256]{1,0:T(8,128)(2,1)S(1)}, bf16[256,256]{1,0:T(8,128)(2,1)S(1)}, u32[]{:S(2)}, u32[]{:S(2)}) collective-permute-start(bf16[256,256]{1,0:T(8,128)(2,1)S(1)} %collective-permute-done.101.refs_19_.refs_16_), channel_id=1, source_target_pairs={{0,1},{1,0},{2,3},{3,2},{4,5},{5,4},{6,7},{7,6},{8,9},{9,8},{10,11... | collective-permute-start | bytes 393224 | tf_op jit(solution)/shard_map/ppermute | solution.py:33
  186.4 2.8 %collective-permute-start.104 = (bf16[256,256]{1,0:T(8,128)(2,1)S(1)}, bf16[256,256]{1,0:T(8,128)(2,1)S(1)}, u32[]{:S(2)}, u32[]{:S(2)}) collective-permute-start(bf16[256,256]{1,0:T(8,128)(2,1)S(1)} %collective-permute-done.103.refs_21_.refs_18_), channel_id=1, source_target_pairs={{0,1},{1,0},{2,3},{3,2},{4,5},{5,4},{6,7},{7,6},{8,9},{9,8},{10,11... | collective-permute-start | bytes 393224 | tf_op jit(solution)/shard_map/ppermute | solution.py:33
  189.2 2.2 collective-permute-start.92
  191.5 2.0 collective-permute-start.94
  193.5 3.6 %shard_map.152 = (bf16[4,512,768]{2,1,0:T(8,128)(2,1)}, bf16[4,512,768]{2,1,0:T(8,128)(2,1)}, bf16[4,768,512]{2,1,0:T(8,128)(2,1)}, f32[8,128]{1,0:T(8,128)S(1)}) custom-call(s32[10]{0:T(128)S(1)} %stack.35.scal, bf16[320,512]{1,0:T(8,128)(2,1)S(1)} %get-tuple-element.123.in_ref, ...), custom_call_target="tpu_custom_call", output_to_operand_aliasing={{0}: (22, {}), {1}: (23, {}), {2}: (24, {})} | custom-call | flops 754974720 | bytes 4571136 | tf_op jit(solution)/shard_map/pallas_call | solution.py:513
  199.1 3.7 %shard_map.153 = (bf16[2,2,128,512]{3,2,1,0:T(8,128)(2,1)S(1)}, bf16[2,2,128,512]{3,2,1,0:T(8,128)(2,1)S(1)}, f32[8,128]{1,0:T(8,128)}, f32[2,16,128]{2,1,0:T(8,128)S(1)}, f32[2,16,128]{2,1,0:T(8,128)S(1)}) custom-call(s32[10]{0:T(128)S(1)} %stack.35.scal, f32[8,128]{1,0:T(8,128)S(1)} %get-tuple-element.212.refs_0_, ...), custom_call_target="tpu_custom_call" | custom-call | flops 754974720 | bytes 4571136 | tf_op jit(solution)/shard_map/pallas_call | solution.py:488
  203.4 1.4 collective-permute-done.105
  205.0 3.7 %shard_map.154 = (bf16[4,512,768]{2,1,0:T(8,128)(2,1)}, bf16[4,512,768]{2,1,0:T(8,128)(2,1)}, bf16[4,768,512]{2,1,0:T(8,128)(2,1)}, f32[8,128]{1,0:T(8,128)S(1)}) custom-call(s32[10]{0:T(128)S(1)} %stack.35.scal, bf16[320,512]{1,0:T(8,128)(2,1)S(1)} %get-tuple-element.219.in_ref, ...), custom_call_target="tpu_custom_call", output_to_operand_aliasing={{0}: (22, {}), {1}: (23, {}), {2}: (24, {})} | custom-call | flops 754974720 | bytes 4571136 | tf_op jit(solution)/shard_map/pallas_call | solution.py:513
  208.7 1.6 collective-permute-start.108
  210.9 1.5 collective-permute-done.108
  213.0 5.3 %collective-permute-done.106 = bf16[2,128,512]{2,1,0:T(8,128)(2,1)S(1)} collective-permute-done((bf16[2,128,512]{2,1,0:T(8,128)(2,1)S(1)}, bf16[2,128,512]{2,1,0:T(8,128)(2,1)S(1)}, u32[]{:S(2)}, u32[]{:S(2)}) %collective-permute-start.106) | collective-permute-done | bytes 262176 | tf_op jit(solution)/shard_map/ppermute | solution.py:33
  (247 shorter events, 23.4 us)
Async XLA Ops:
  1.7 9.7 %collective-permute-start = (bf16[272,512]{1,0:T(8,128)(2,1)S(1)}, bf16[272,512]{1,0:T(8,128)(2,1)S(1)}, u32[]{:S(2)}, u32[]{:S(2)}) collective-permute-start(bf16[272,512]{1,0:T(8,128)(2,1)S(1)} %shard_map.118.refs_0_.refs_1_), channel_id=1, source_target_pairs={{0,8},{4,12},{8,0},{12,4},{1,9},{5,13},{9,1},{13,5},{2,10},{6,14},... | collective-permute-start | bytes 835592 | tf_op jit(solution)/shard_map/ppermute | solution.py:33
  16.6 10.0 %collective-permute-start.6 = (bf16[240,256]{1,0:T(8,128)(2,1)S(1)}, bf16[240,256]{1,0:T(8,128)(2,1)S(1)}, u32[]{:S(2)}, u32[]{:S(2)}) collective-permute-start(bf16[240,256]{1,0:T(8,128)(2,1)S(1)} %get-tuple-element.121), channel_id=1, source_target_pairs={{0,1},{1,0},{2,3},{3,2},{4,5},{5,4},{6,7},{7,6},{8,9},{9,8},{10,11... | collective-permute-start | bytes 368648 | tf_op jit(solution)/shard_map/ppermute | solution.py:33
  18.5 8.5 %collective-permute-start.3 = (bf16[240,256]{1,0:T(8,128)(2,1)S(1)}, bf16[240,256]{1,0:T(8,128)(2,1)S(1)}, u32[]{:S(2)}, u32[]{:S(2)}) collective-permute-start(bf16[240,256]{1,0:T(8,128)(2,1)S(1)} %get-tuple-element.120.refs_0_), channel_id=1, source_target_pairs={{0,1},{1,0},{2,3},{3,2},{4,5},{5,4},{6,7},{7,6},{8,9},{9,8},{10,11... | collective-permute-start | bytes 368648 | tf_op jit(solution)/shard_map/ppermute | solution.py:33
  18.7 9.4 %collective-permute-start.46 = (bf16[240,256]{1,0:T(8,128)(2,1)S(1)}, bf16[240,256]{1,0:T(8,128)(2,1)S(1)}, u32[]{:S(2)}, u32[]{:S(2)}) collective-permute-start(bf16[240,256]{1,0:T(8,128)(2,1)S(1)} %get-tuple-element.154.refs_1_), channel_id=1, source_target_pairs={{0,1},{1,0},{2,3},{3,2},{4,5},{5,4},{6,7},{7,6},{8,9},{9,8},{10,11... | collective-permute-start | bytes 368648 | tf_op jit(solution)/shard_map/ppermute | solution.py:33
  20.5 10.2 %collective-permute-start.49 = (bf16[240,256]{1,0:T(8,128)(2,1)S(1)}, bf16[240,256]{1,0:T(8,128)(2,1)S(1)}, u32[]{:S(2)}, u32[]{:S(2)}) collective-permute-start(bf16[240,256]{1,0:T(8,128)(2,1)S(1)} %get-tuple-element.155), channel_id=1, source_target_pairs={{0,1},{1,0},{2,3},{3,2},{4,5},{5,4},{6,7},{7,6},{8,9},{9,8},{10,11... | collective-permute-start | bytes 368648 | tf_op jit(solution)/shard_map/ppermute | solution.py:33
  20.7 12.6 %collective-permute-start.17 = (bf16[240,256]{1,0:T(8,128)(2,1)S(1)}, bf16[240,256]{1,0:T(8,128)(2,1)S(1)}, u32[]{:S(2)}, u32[]{:S(2)}) collective-permute-start(bf16[240,256]{1,0:T(8,128)(2,1)S(1)} %get-tuple-element.143.refs_0_), channel_id=1, source_target_pairs={{0,1},{1,0},{2,3},{3,2},{4,5},{5,4},{6,7},{7,6},{8,9},{9,8},{10,11... | collective-permute-start | bytes 368648 | tf_op jit(solution)/shard_map/ppermute | solution.py:33
  26.6 8.6 %collective-permute-start.20 = (bf16[240,256]{1,0:T(8,128)(2,1)S(1)}, bf16[240,256]{1,0:T(8,128)(2,1)S(1)}, u32[]{:S(2)}, u32[]{:S(2)}) collective-permute-start(bf16[240,256]{1,0:T(8,128)(2,1)S(1)} %get-tuple-element.144), channel_id=1, source_target_pairs={{0,1},{1,0},{2,3},{3,2},{4,5},{5,4},{6,7},{7,6},{8,9},{9,8},{10,11... | collective-permute-start | bytes 368648 | tf_op jit(solution)/shard_map/ppermute | solution.py:33
  26.9 17.6 %collective-permute-start.7 = (bf16[240,256]{1,0:T(8,128)(2,1)S(1)}, bf16[240,256]{1,0:T(8,128)(2,1)S(1)}, u32[]{:S(2)}, u32[]{:S(2)}) collective-permute-start(bf16[240,256]{1,0:T(8,128)(2,1)S(1)} %fusion.13), channel_id=1, source_target_pairs={{1,2},{2,1},{0,4},{3,7},{5,6},{6,5},{4,0},{7,3},{9,10},{10,9},{8,1... | collective-permute-start | bytes 368648 | tf_op jit(solution)/shard_map/ppermute | solution.py:538
  33.3 11.4 %collective-permute-start.50 = (bf16[240,256]{1,0:T(8,128)(2,1)S(1)}, bf16[240,256]{1,0:T(8,128)(2,1)S(1)}, u32[]{:S(2)}, u32[]{:S(2)}) collective-permute-start(bf16[240,256]{1,0:T(8,128)(2,1)S(1)} %fusion.19), channel_id=1, source_target_pairs={{1,2},{2,1},{0,4},{3,7},{5,6},{6,5},{4,0},{7,3},{9,10},{10,9},{8,1... | collective-permute-start | bytes 368648 | tf_op jit(solution)/shard_map/ppermute | solution.py:538
  35.3 15.4 %collective-permute-start.21 = (bf16[240,256]{1,0:T(8,128)(2,1)S(1)}, bf16[240,256]{1,0:T(8,128)(2,1)S(1)}, u32[]{:S(2)}, u32[]{:S(2)}) collective-permute-start(bf16[240,256]{1,0:T(8,128)(2,1)S(1)} %fusion.15), channel_id=1, source_target_pairs={{1,2},{2,1},{0,4},{3,7},{5,6},{6,5},{4,0},{7,3},{9,10},{10,9},{8,1... | collective-permute-start | bytes 368648 | tf_op jit(solution)/shard_map/ppermute | solution.py:538
  36.0 8.6 %collective-permute-start.5 = (bf16[240,256]{1,0:T(8,128)(2,1)S(1)}, bf16[240,256]{1,0:T(8,128)(2,1)S(1)}, u32[]{:S(2)}, u32[]{:S(2)}) collective-permute-start(bf16[240,256]{1,0:T(8,128)(2,1)S(1)} %fusion.1), channel_id=1, source_target_pairs={{0,1},{1,0},{2,3},{3,2},{4,5},{5,4},{6,7},{7,6},{8,9},{9,8},{10,11... | collective-permute-start | bytes 368648 | tf_op jit(solution)/shard_map/ppermute | solution.py:33
  39.5 8.8 %collective-permute-start.48 = (bf16[240,256]{1,0:T(8,128)(2,1)S(1)}, bf16[240,256]{1,0:T(8,128)(2,1)S(1)}, u32[]{:S(2)}, u32[]{:S(2)}) collective-permute-start(bf16[240,256]{1,0:T(8,128)(2,1)S(1)} %fusion.7), channel_id=1, source_target_pairs={{0,1},{1,0},{2,3},{3,2},{4,5},{5,4},{6,7},{7,6},{8,9},{9,8},{10,11... | collective-permute-start | bytes 368648 | tf_op jit(solution)/shard_map/ppermute | solution.py:33
  44.7 8.6 %collective-permute-start.8 = (bf16[240,256]{1,0:T(8,128)(2,1)S(1)}, bf16[240,256]{1,0:T(8,128)(2,1)S(1)}, u32[]{:S(2)}, u32[]{:S(2)}) collective-permute-start(bf16[240,256]{1,0:T(8,128)(2,1)S(1)} %get-tuple-element.122.refs_7_), channel_id=1, source_target_pairs={{1,2},{2,1},{0,4},{3,7},{5,6},{6,5},{4,0},{7,3},{9,10},{10,9},{8,1... | collective-permute-start | bytes 368648 | tf_op jit(solution)/shard_map/ppermute | solution.py:538
  44.8 10.9 %collective-permute-start.12 = (bf16[240,256]{1,0:T(8,128)(2,1)S(1)}, bf16[240,256]{1,0:T(8,128)(2,1)S(1)}, u32[]{:S(2)}, u32[]{:S(2)}) collective-permute-start(bf16[240,256]{1,0:T(8,128)(2,1)S(1)} %get-tuple-element.122.refs_7_), channel_id=1, source_target_pairs={{0,1},{1,0},{2,3},{3,2},{4,5},{5,4},{6,7},{7,6},{8,9},{9,8},{10,11... | collective-permute-start | bytes 368648 | tf_op jit(solution)/shard_map/ppermute | solution.py:33
  48.4 11.6 %collective-permute-start.51 = (bf16[240,256]{1,0:T(8,128)(2,1)S(1)}, bf16[240,256]{1,0:T(8,128)(2,1)S(1)}, u32[]{:S(2)}, u32[]{:S(2)}) collective-permute-start(bf16[240,256]{1,0:T(8,128)(2,1)S(1)} %get-tuple-element.160.refs_1_), channel_id=1, source_target_pairs={{0,1},{1,0},{2,3},{3,2},{4,5},{5,4},{6,7},{7,6},{8,9},{9,8},{10,11... | collective-permute-start | bytes 368648 | tf_op jit(solution)/shard_map/ppermute | solution.py:33
  50.9 13.2 %collective-permute-start.26 = (bf16[240,256]{1,0:T(8,128)(2,1)S(1)}, bf16[240,256]{1,0:T(8,128)(2,1)S(1)}, u32[]{:S(2)}, u32[]{:S(2)}) collective-permute-start(bf16[240,256]{1,0:T(8,128)(2,1)S(1)} %get-tuple-element.145.refs_13_), channel_id=1, source_target_pairs={{0,1},{1,0},{2,3},{3,2},{4,5},{5,4},{6,7},{7,6},{8,9},{9,8},{10,11... | collective-permute-start | bytes 368648 | tf_op jit(solution)/shard_map/ppermute | solution.py:33
  53.4 11.2 %collective-permute-start.9 = (bf16[240,256]{1,0:T(8,128)(2,1)S(1)}, bf16[240,256]{1,0:T(8,128)(2,1)S(1)}, u32[]{:S(2)}, u32[]{:S(2)}) collective-permute-start(bf16[240,256]{1,0:T(8,128)(2,1)S(1)} %broadcast_select_fusion.17), channel_id=1, source_target_pairs={{0,1},{1,0},{2,3},{3,2},{4,5},{5,4},{6,7},{7,6},{8,9},{9,8},{10,11... | collective-permute-start | bytes 368648 | tf_op jit(solution)/shard_map/ppermute | solution.py:33
  55.7 16.3 %collective-permute-start.53 = (bf16[240,256]{1,0:T(8,128)(2,1)S(1)}, bf16[240,256]{1,0:T(8,128)(2,1)S(1)}, u32[]{:S(2)}, u32[]{:S(2)}) collective-permute-start(bf16[240,256]{1,0:T(8,128)(2,1)S(1)} %broadcast_select_fusion.9), channel_id=1, source_target_pairs={{0,1},{1,0},{2,3},{3,2},{4,5},{5,4},{6,7},{7,6},{8,9},{9,8},{10,11... | collective-permute-start | bytes 368648 | tf_op jit(solution)/shard_map/ppermute | solution.py:33
  55.8 8.3 %collective-permute-start.13 = (bf16[240,256]{1,0:T(8,128)(2,1)S(1)}, bf16[240,256]{1,0:T(8,128)(2,1)S(1)}, u32[]{:S(2)}, u32[]{:S(2)}) collective-permute-start(bf16[240,256]{1,0:T(8,128)(2,1)S(1)} %collective-permute-done.12.refs_8_), channel_id=1, source_target_pairs={{1,2},{2,1},{0,4},{3,7},{5,6},{6,5},{4,0},{7,3},{9,10},{10,9},{8,1... | collective-permute-start | bytes 368648 | tf_op jit(solution)/shard_map/ppermute | solution.py:538
  60.0 11.9 %collective-permute-start.23 = (bf16[240,256]{1,0:T(8,128)(2,1)S(1)}, bf16[240,256]{1,0:T(8,128)(2,1)S(1)}, u32[]{:S(2)}, u32[]{:S(2)}) collective-permute-start(bf16[240,256]{1,0:T(8,128)(2,1)S(1)} %broadcast_select_fusion.15), channel_id=1, source_target_pairs={{0,1},{1,0},{2,3},{3,2},{4,5},{5,4},{6,7},{7,6},{8,9},{9,8},{10,11... | collective-permute-start | bytes 368648 | tf_op jit(solution)/shard_map/ppermute | solution.py:33
  66.4 12.7 %collective-permute-start.55 = (bf16[240,256]{1,0:T(8,128)(2,1)S(1)}, bf16[240,256]{1,0:T(8,128)(2,1)S(1)}, u32[]{:S(2)}, u32[]{:S(2)}) collective-permute-start(bf16[240,256]{1,0:T(8,128)(2,1)S(1)} %broadcast_select_fusion.8), channel_id=1, source_target_pairs={{0,1},{1,0},{2,3},{3,2},{4,5},{5,4},{6,7},{7,6},{8,9},{9,8},{10,11... | collective-permute-start | bytes 368648 | tf_op jit(solution)/shard_map/ppermute | solution.py:33
  72.0 7.9 %collective-permute-start.24 = (bf16[240,256]{1,0:T(8,128)(2,1)S(1)}, bf16[240,256]{1,0:T(8,128)(2,1)S(1)}, u32[]{:S(2)}, u32[]{:S(2)}) collective-permute-start(bf16[240,256]{1,0:T(8,128)(2,1)S(1)} %shard_map.129), channel_id=1, source_target_pairs={{1,2},{2,1},{0,4},{3,7},{5,6},{6,5},{4,0},{7,3},{9,10},{10,9},{8,1... | collective-permute-start | bytes 368648 | tf_op jit(solution)/shard_map/ppermute | solution.py:538
  72.7 11.5 %collective-permute-start.15 = (bf16[240,256]{1,0:T(8,128)(2,1)S(1)}, bf16[240,256]{1,0:T(8,128)(2,1)S(1)}, u32[]{:S(2)}, u32[]{:S(2)}) collective-permute-start(bf16[240,256]{1,0:T(8,128)(2,1)S(1)} %fusion.14), channel_id=1, source_target_pairs={{1,2},{2,1},{0,4},{3,7},{5,6},{6,5},{4,0},{7,3},{9,10},{10,9},{8,1... | collective-permute-start | bytes 368648 | tf_op jit(solution)/shard_map/ppermute | solution.py:538
  79.2 11.6 %collective-permute-start.29 = (bf16[240,256]{1,0:T(8,128)(2,1)S(1)}, bf16[240,256]{1,0:T(8,128)(2,1)S(1)}, u32[]{:S(2)}, u32[]{:S(2)}) collective-permute-start(bf16[240,256]{1,0:T(8,128)(2,1)S(1)} %fusion.16), channel_id=1, source_target_pairs={{1,2},{2,1},{0,4},{3,7},{5,6},{6,5},{4,0},{7,3},{9,10},{10,9},{8,1... | collective-permute-start | bytes 368648 | tf_op jit(solution)/shard_map/ppermute | solution.py:538
  79.3 8.5 %collective-permute-start.58 = (bf16[240,256]{1,0:T(8,128)(2,1)S(1)}, bf16[240,256]{1,0:T(8,128)(2,1)S(1)}, u32[]{:S(2)}, u32[]{:S(2)}) collective-permute-start(bf16[240,256]{1,0:T(8,128)(2,1)S(1)} %fusion.20), channel_id=1, source_target_pairs={{1,2},{2,1},{0,4},{3,7},{5,6},{6,5},{4,0},{7,3},{9,10},{10,9},{8,1... | collective-permute-start | bytes 368648 | tf_op jit(solution)/shard_map/ppermute | solution.py:538
  79.9 10.6 %collective-permute-start.57 = (bf16[240,256]{1,0:T(8,128)(2,1)S(1)}, bf16[240,256]{1,0:T(8,128)(2,1)S(1)}, u32[]{:S(2)}, u32[]{:S(2)}) collective-permute-start(bf16[240,256]{1,0:T(8,128)(2,1)S(1)} %fusion.8), channel_id=1, source_target_pairs={{0,1},{1,0},{2,3},{3,2},{4,5},{5,4},{6,7},{7,6},{8,9},{9,8},{10,11... | collective-permute-start | bytes 368648 | tf_op jit(solution)/shard_map/ppermute | solution.py:33
  84.5 12.2 %collective-permute-start.16 = (bf16[240,256]{1,0:T(8,128)(2,1)S(1)}, bf16[240,256]{1,0:T(8,128)(2,1)S(1)}, u32[]{:S(2)}, u32[]{:S(2)}) collective-permute-start(bf16[240,256]{1,0:T(8,128)(2,1)S(1)} %get-tuple-element.129.refs_9_.refs_7_), channel_id=1, source_target_pairs={{1,2},{2,1},{0,4},{3,7},{5,6},{6,5},{4,0},{7,3},{9,10},{10,9},{8,1... | collective-permute-start | bytes 368648 | tf_op jit(solution)/shard_map/ppermute | solution.py:538
  87.8 10.9 %collective-permute-start.64 = (bf16[240,256]{1,0:T(8,128)(2,1)S(1)}, bf16[240,256]{1,0:T(8,128)(2,1)S(1)}, u32[]{:S(2)}, u32[]{:S(2)}) collective-permute-start(bf16[240,256]{1,0:T(8,128)(2,1)S(1)} %get-tuple-element.129.refs_9_.refs_7_), channel_id=1, source_target_pairs={{0,1},{1,0},{2,3},{3,2},{4,5},{5,4},{6,7},{7,6},{8,9},{9,8},{10,11... | collective-permute-start | bytes 368648 | tf_op jit(solution)/shard_map/ppermute | solution.py:33
  90.7 12.3 %collective-permute-start.59 = (bf16[240,256]{1,0:T(8,128)(2,1)S(1)}, bf16[240,256]{1,0:T(8,128)(2,1)S(1)}, u32[]{:S(2)}, u32[]{:S(2)}) collective-permute-start(bf16[240,256]{1,0:T(8,128)(2,1)S(1)} %get-tuple-element.171.refs_3_.refs_1_), channel_id=1, source_target_pairs={{0,1},{1,0},{2,3},{3,2},{4,5},{5,4},{6,7},{7,6},{8,9},{9,8},{10,11... | collective-permute-start | bytes 368648 | tf_op jit(solution)/shard_map/ppermute | solution.py:33
  92.2 15.6 %collective-permute-start.34 = (bf16[240,256]{1,0:T(8,128)(2,1)S(1)}, bf16[240,256]{1,0:T(8,128)(2,1)S(1)}, u32[]{:S(2)}, u32[]{:S(2)}) collective-permute-start(bf16[240,256]{1,0:T(8,128)(2,1)S(1)} %get-tuple-element.147.refs_15_.refs_0_.refs_13_), channel_id=1, source_target_pairs={{0,1},{1,0},{2,3},{3,2},{4,5},{5,4},{6,7},{7,6},{8,9},{9,8},{10,11... | collective-permute-start | bytes 368648 | tf_op jit(solution)/shard_map/ppermute | solution.py:33
  96.6 11.1 %collective-permute-start.65 = (bf16[240,256]{1,0:T(8,128)(2,1)S(1)}, bf16[240,256]{1,0:T(8,128)(2,1)S(1)}, u32[]{:S(2)}, u32[]{:S(2)}) collective-permute-start(bf16[240,256]{1,0:T(8,128)(2,1)S(1)} %broadcast_select_fusion.5), channel_id=1, source_target_pairs={{0,1},{1,0},{2,3},{3,2},{4,5},{5,4},{6,7},{7,6},{8,9},{9,8},{10,11... | collective-permute-start | bytes 368648 | tf_op jit(solution)/shard_map/ppermute | solution.py:33
  98.7 9.8 %collective-permute-start.61 = (bf16[240,256]{1,0:T(8,128)(2,1)S(1)}, bf16[240,256]{1,0:T(8,128)(2,1)S(1)}, u32[]{:S(2)}, u32[]{:S(2)}) collective-permute-start(bf16[240,256]{1,0:T(8,128)(2,1)S(1)} %broadcast_select_fusion.7), channel_id=1, source_target_pairs={{0,1},{1,0},{2,3},{3,2},{4,5},{5,4},{6,7},{7,6},{8,9},{9,8},{10,11... | collective-permute-start | bytes 368648 | tf_op jit(solution)/shard_map/ppermute | solution.py:33
  98.8 9.5 %collective-permute-start.66 = (bf16[240,256]{1,0:T(8,128)(2,1)S(1)}, bf16[240,256]{1,0:T(8,128)(2,1)S(1)}, u32[]{:S(2)}, u32[]{:S(2)}) collective-permute-start(bf16[240,256]{1,0:T(8,128)(2,1)S(1)} %collective-permute-done.64.refs_10_.refs_8_), channel_id=1, source_target_pairs={{1,2},{2,1},{0,4},{3,7},{5,6},{6,5},{4,0},{7,3},{9,10},{10,9},{8,1... | collective-permute-start | bytes 368648 | tf_op jit(solution)/shard_map/ppermute | solution.py:538
  103.0 13.7 %collective-permute-start.31 = (bf16[240,256]{1,0:T(8,128)(2,1)S(1)}, bf16[240,256]{1,0:T(8,128)(2,1)S(1)}, u32[]{:S(2)}, u32[]{:S(2)}) collective-permute-start(bf16[240,256]{1,0:T(8,128)(2,1)S(1)} %broadcast_select_fusion.13), channel_id=1, source_target_pairs={{0,1},{1,0},{2,3},{3,2},{4,5},{5,4},{6,7},{7,6},{8,9},{9,8},{10,11... | collective-permute-start | bytes 368648 | tf_op jit(solution)/shard_map/ppermute | solution.py:33
  108.3 8.6 %collective-permute-start.71 = (bf16[240,256]{1,0:T(8,128)(2,1)S(1)}, bf16[240,256]{1,0:T(8,128)(2,1)S(1)}, u32[]{:S(2)}, u32[]{:S(2)}) collective-permute-start(bf16[240,256]{1,0:T(8,128)(2,1)S(1)} %shard_map.143), channel_id=1, source_target_pairs={{1,2},{2,1},{0,4},{3,7},{5,6},{6,5},{4,0},{7,3},{9,10},{10,9},{8,1... | collective-permute-start | bytes 368648 | tf_op jit(solution)/shard_map/ppermute | solution.py:538
  108.5 8.5 %collective-permute-start.67 = (bf16[240,256]{1,0:T(8,128)(2,1)S(1)}, bf16[240,256]{1,0:T(8,128)(2,1)S(1)}, u32[]{:S(2)}, u32[]{:S(2)}) collective-permute-start(bf16[240,256]{1,0:T(8,128)(2,1)S(1)} %broadcast_select_fusion.4), channel_id=1, source_target_pairs={{0,1},{1,0},{2,3},{3,2},{4,5},{5,4},{6,7},{7,6},{8,9},{9,8},{10,11... | collective-permute-start | bytes 368648 | tf_op jit(solution)/shard_map/ppermute | solution.py:33
  111.3 8.7 %collective-permute-start.68 = (bf16[240,256]{1,0:T(8,128)(2,1)S(1)}, bf16[240,256]{1,0:T(8,128)(2,1)S(1)}, u32[]{:S(2)}, u32[]{:S(2)}) collective-permute-start(bf16[240,256]{1,0:T(8,128)(2,1)S(1)} %shard_map.141), channel_id=1, source_target_pairs={{1,2},{2,1},{0,4},{3,7},{5,6},{6,5},{4,0},{7,3},{9,10},{10,9},{8,1... | collective-permute-start | bytes 368648 | tf_op jit(solution)/shard_map/ppermute | solution.py:538
  111.4 8.8 %collective-permute-start.63 = (bf16[240,256]{1,0:T(8,128)(2,1)S(1)}, bf16[240,256]{1,0:T(8,128)(2,1)S(1)}, u32[]{:S(2)}, u32[]{:S(2)}) collective-permute-start(bf16[240,256]{1,0:T(8,128)(2,1)S(1)} %broadcast_select_fusion.6), channel_id=1, source_target_pairs={{0,1},{1,0},{2,3},{3,2},{4,5},{5,4},{6,7},{7,6},{8,9},{9,8},{10,11... | collective-permute-start | bytes 368648 | tf_op jit(solution)/shard_map/ppermute | solution.py:33
  117.0 7.9 %collective-permute-start.72 = (bf16[240,256]{1,0:T(8,128)(2,1)S(1)}, bf16[240,256]{1,0:T(8,128)(2,1)S(1)}, u32[]{:S(2)}, u32[]{:S(2)}) collective-permute-start(bf16[240,256]{1,0:T(8,128)(2,1)S(1)} %fusion.10), channel_id=1, source_target_pairs={{0,1},{1,0},{2,3},{3,2},{4,5},{5,4},{6,7},{7,6},{8,9},{9,8},{10,11... | collective-permute-start | bytes 368648 | tf_op jit(solution)/shard_map/ppermute | solution.py:33
  120.3 10.3 %collective-permute-start.69 = (bf16[240,256]{1,0:T(8,128)(2,1)S(1)}, bf16[240,256]{1,0:T(8,128)(2,1)S(1)}, u32[]{:S(2)}, u32[]{:S(2)}) collective-permute-start(bf16[240,256]{1,0:T(8,128)(2,1)S(1)} %fusion.9), channel_id=1, source_target_pairs={{0,1},{1,0},{2,3},{3,2},{4,5},{5,4},{6,7},{7,6},{8,9},{9,8},{10,11... | collective-permute-start | bytes 368648 | tf_op jit(solution)/shard_map/ppermute | solution.py:33
  122.8 8.2 %collective-permute-start.70 = (bf16[240,256]{1,0:T(8,128)(2,1)S(1)}, bf16[240,256]{1,0:T(8,128)(2,1)S(1)}, u32[]{:S(2)}, u32[]{:S(2)}) collective-permute-start(bf16[240,256]{1,0:T(8,128)(2,1)S(1)} %fusion.21), channel_id=1, source_target_pairs={{1,2},{2,1},{0,4},{3,7},{5,6},{6,5},{4,0},{7,3},{9,10},{10,9},{8,1... | collective-permute-start | bytes 368648 | tf_op jit(solution)/shard_map/ppermute | solution.py:538
  123.0 9.9 %collective-permute-start.37 = (bf16[240,256]{1,0:T(8,128)(2,1)S(1)}, bf16[240,256]{1,0:T(8,128)(2,1)S(1)}, u32[]{:S(2)}, u32[]{:S(2)}) collective-permute-start(bf16[240,256]{1,0:T(8,128)(2,1)S(1)} %fusion.17), channel_id=1, source_target_pairs={{1,2},{2,1},{0,4},{3,7},{5,6},{6,5},{4,0},{7,3},{9,10},{10,9},{8,1... | collective-permute-start | bytes 368648 | tf_op jit(solution)/shard_map/ppermute | solution.py:538
  124.9 8.0 %collective-permute-start.33 = (bf16[240,256]{1,0:T(8,128)(2,1)S(1)}, bf16[240,256]{1,0:T(8,128)(2,1)S(1)}, u32[]{:S(2)}, u32[]{:S(2)}) collective-permute-start(bf16[240,256]{1,0:T(8,128)(2,1)S(1)} %fusion.5), channel_id=1, source_target_pairs={{0,1},{1,0},{2,3},{3,2},{4,5},{5,4},{6,7},{7,6},{8,9},{9,8},{10,11... | collective-permute-start | bytes 368648 | tf_op jit(solution)/shard_map/ppermute | solution.py:33
  127.2 11.4 %collective-permute-start.80 = (bf16[240,256]{1,0:T(8,128)(2,1)S(1)}, bf16[240,256]{1,0:T(8,128)(2,1)S(1)}, u32[]{:S(2)}, u32[]{:S(2)}) collective-permute-start(bf16[240,256]{1,0:T(8,128)(2,1)S(1)} %get-tuple-element.192.refs_9_.refs_7_), channel_id=1, source_target_pairs={{1,2},{2,1},{0,4},{3,7},{5,6},{6,5},{4,0},{7,3},{9,10},{10,9},{8,1... | collective-permute-start | bytes 368648 | tf_op jit(solution)/shard_map/ppermute | solution.py:538
  130.6 8.6 %collective-permute-start.79 = (bf16[240,256]{1,0:T(8,128)(2,1)S(1)}, bf16[240,256]{1,0:T(8,128)(2,1)S(1)}, u32[]{:S(2)}, u32[]{:S(2)}) collective-permute-start(bf16[240,256]{1,0:T(8,128)(2,1)S(1)} %get-tuple-element.192.refs_9_.refs_7_), channel_id=1, source_target_pairs={{0,1},{1,0},{2,3},{3,2},{4,5},{5,4},{6,7},{7,6},{8,9},{9,8},{10,11... | collective-permute-start | bytes 368648 | tf_op jit(solution)/shard_map/ppermute | solution.py:33
  131.1 9.8 %collective-permute-start.74 = (bf16[240,256]{1,0:T(8,128)(2,1)S(1)}, bf16[240,256]{1,0:T(8,128)(2,1)S(1)}, u32[]{:S(2)}, u32[]{:S(2)}) collective-permute-start(bf16[240,256]{1,0:T(8,128)(2,1)S(1)} %get-tuple-element.189.refs_3_.refs_1_), channel_id=1, source_target_pairs={{0,1},{1,0},{2,3},{3,2},{4,5},{5,4},{6,7},{7,6},{8,9},{9,8},{10,11... | collective-permute-start | bytes 368648 | tf_op jit(solution)/shard_map/ppermute | solution.py:33
  133.0 11.6 %collective-permute-start.42 = (bf16[240,256]{1,0:T(8,128)(2,1)S(1)}, bf16[240,256]{1,0:T(8,128)(2,1)S(1)}, u32[]{:S(2)}, u32[]{:S(2)}) collective-permute-start(bf16[240,256]{1,0:T(8,128)(2,1)S(1)} %get-tuple-element.149.refs_15_.refs_0_.refs_13_), channel_id=1, source_target_pairs={{0,1},{1,0},{2,3},{3,2},{4,5},{5,4},{6,7},{7,6},{8,9},{9,8},{10,11... | collective-permute-start | bytes 368648 | tf_op jit(solution)/shard_map/ppermute | solution.py:33
  139.2 11.7 %collective-permute-start.76 = (bf16[240,256]{1,0:T(8,128)(2,1)S(1)}, bf16[240,256]{1,0:T(8,128)(2,1)S(1)}, u32[]{:S(2)}, u32[]{:S(2)}) collective-permute-start(bf16[240,256]{1,0:T(8,128)(2,1)S(1)} %broadcast_select_fusion.3), channel_id=1, source_target_pairs={{0,1},{1,0},{2,3},{3,2},{4,5},{5,4},{6,7},{7,6},{8,9},{9,8},{10,11... | collective-permute-start | bytes 368648 | tf_op jit(solution)/shard_map/ppermute | solution.py:33
  140.9 12.6 %collective-permute-start.39 = (bf16[240,256]{1,0:T(8,128)(2,1)S(1)}, bf16[240,256]{1,0:T(8,128)(2,1)S(1)}, u32[]{:S(2)}, u32[]{:S(2)}) collective-permute-start(bf16[240,256]{1,0:T(8,128)(2,1)S(1)} %broadcast_select_fusion.11), channel_id=1, source_target_pairs={{0,1},{1,0},{2,3},{3,2},{4,5},{5,4},{6,7},{7,6},{8,9},{9,8},{10,11... | collective-permute-start | bytes 368648 | tf_op jit(solution)/shard_map/ppermute | solution.py:33
  144.6 8.8 %collective-permute-start.43 = (bf16[240,256]{1,0:T(8,128)(2,1)S(1)}, bf16[240,256]{1,0:T(8,128)(2,1)S(1)}, u32[]{:S(2)}, u32[]{:S(2)}) collective-permute-start(bf16[240,256]{1,0:T(8,128)(2,1)S(1)} %collective-permute-done.42.refs_16_.refs_14_), channel_id=1, source_target_pairs={{1,2},{2,1},{0,4},{3,7},{5,6},{6,5},{4,0},{7,3},{9,10},{10,9},{8,1... | collective-permute-start | bytes 368648 | tf_op jit(solution)/shard_map/ppermute | solution.py:538
  145.1 10.9 %collective-permute-start.83 = (bf16[240,256]{1,0:T(8,128)(2,1)S(1)}, bf16[240,256]{1,0:T(8,128)(2,1)S(1)}, u32[]{:S(2)}, u32[]{:S(2)}) collective-permute-start(bf16[240,256]{1,0:T(8,128)(2,1)S(1)} %broadcast_select_fusion), channel_id=1, source_target_pairs={{0,1},{1,0},{2,3},{3,2},{4,5},{5,4},{6,7},{7,6},{8,9},{9,8},{10,11... | collective-permute-start | bytes 368648 | tf_op jit(solution)/shard_map/ppermute | solution.py:33
  156.9 13.1 %collective-permute-start.88 = (bf16[240,256]{1,0:T(8,128)(2,1)S(1)}, bf16[240,256]{1,0:T(8,128)(2,1)S(1)}, u32[]{:S(2)}, u32[]{:S(2)}) collective-permute-start(bf16[240,256]{1,0:T(8,128)(2,1)S(1)} %fusion.12), channel_id=1, source_target_pairs={{0,1},{1,0},{2,3},{3,2},{4,5},{5,4},{6,7},{7,6},{8,9},{9,8},{10,11... | collective-permute-start | bytes 368648 | tf_op jit(solution)/shard_map/ppermute | solution.py:33
  159.4 10.7 %collective-permute-start.86 = (bf16[240,256]{1,0:T(8,128)(2,1)S(1)}, bf16[240,256]{1,0:T(8,128)(2,1)S(1)}, u32[]{:S(2)}, u32[]{:S(2)}) collective-permute-start(bf16[240,256]{1,0:T(8,128)(2,1)S(1)} %fusion.23), channel_id=1, source_target_pairs={{1,2},{2,1},{0,4},{3,7},{5,6},{6,5},{4,0},{7,3},{9,10},{10,9},{8,1... | collective-permute-start | bytes 368648 | tf_op jit(solution)/shard_map/ppermute | solution.py:538
  159.6 10.6 %collective-permute-start.85 = (bf16[240,256]{1,0:T(8,128)(2,1)S(1)}, bf16[240,256]{1,0:T(8,128)(2,1)S(1)}, u32[]{:S(2)}, u32[]{:S(2)}) collective-permute-start(bf16[240,256]{1,0:T(8,128)(2,1)S(1)} %fusion.11), channel_id=1, source_target_pairs={{0,1},{1,0},{2,3},{3,2},{4,5},{5,4},{6,7},{7,6},{8,9},{9,8},{10,11... | collective-permute-start | bytes 368648 | tf_op jit(solution)/shard_map/ppermute | solution.py:33
  162.0 8.3 %collective-permute-start.45 = (bf16[240,256]{1,0:T(8,128)(2,1)S(1)}, bf16[240,256]{1,0:T(8,128)(2,1)S(1)}, u32[]{:S(2)}, u32[]{:S(2)}) collective-permute-start(bf16[240,256]{1,0:T(8,128)(2,1)S(1)} %fusion.18), channel_id=1, source_target_pairs={{1,2},{2,1},{0,4},{3,7},{5,6},{6,5},{4,0},{7,3},{9,10},{10,9},{8,1... | collective-permute-start | bytes 368648 | tf_op jit(solution)/shard_map/ppermute | solution.py:538
  162.1 8.1 %collective-permute-start.41 = (bf16[240,256]{1,0:T(8,128)(2,1)S(1)}, bf16[240,256]{1,0:T(8,128)(2,1)S(1)}, u32[]{:S(2)}, u32[]{:S(2)}) collective-permute-start(bf16[240,256]{1,0:T(8,128)(2,1)S(1)} %fusion.6), channel_id=1, source_target_pairs={{0,1},{1,0},{2,3},{3,2},{4,5},{5,4},{6,7},{7,6},{8,9},{9,8},{10,11... | collective-permute-start | bytes 368648 | tf_op jit(solution)/shard_map/ppermute | solution.py:33
  178.4 8.0 %collective-permute-start.103 = (bf16[256,256]{1,0:T(8,128)(2,1)S(1)}, bf16[256,256]{1,0:T(8,128)(2,1)S(1)}, u32[]{:S(2)}, u32[]{:S(2)}) collective-permute-start(bf16[256,256]{1,0:T(8,128)(2,1)S(1)} %collective-permute-done.100.refs_17_.refs_14_), channel_id=1, source_target_pairs={{1,2},{2,1},{0,4},{3,7},{5,6},{6,5},{4,0},{7,3},{9,10},{10,9},{8,1... | collective-permute-start | bytes 393224 | tf_op jit(solution)/shard_map/ppermute | solution.py:538
  178.9 10.3 %collective-permute-start.98 = (bf16[240,256]{1,0:T(8,128)(2,1)S(1)}, bf16[240,256]{1,0:T(8,128)(2,1)S(1)}, u32[]{:S(2)}, u32[]{:S(2)}) collective-permute-start(bf16[240,256]{1,0:T(8,128)(2,1)S(1)} %collective-permute-done.95.refs_11_.refs_8_), channel_id=1, source_target_pairs={{1,2},{2,1},{0,4},{3,7},{5,6},{6,5},{4,0},{7,3},{9,10},{10,9},{8,1... | collective-permute-start | bytes 368648 | tf_op jit(solution)/shard_map/ppermute | solution.py:538
  179.9 11.5 %collective-permute-start.97 = (bf16[240,256]{1,0:T(8,128)(2,1)S(1)}, bf16[240,256]{1,0:T(8,128)(2,1)S(1)}, u32[]{:S(2)}, u32[]{:S(2)}) collective-permute-start(bf16[240,256]{1,0:T(8,128)(2,1)S(1)} %collective-permute-done.96.refs_13_.refs_10_), channel_id=1, source_target_pairs={{0,1},{1,0},{2,3},{3,2},{4,5},{5,4},{6,7},{7,6},{8,9},{9,8},{10,11... | collective-permute-start | bytes 368648 | tf_op jit(solution)/shard_map/ppermute | solution.py:33
  182.5 9.0 %collective-permute-start.93 = (bf16[240,256]{1,0:T(8,128)(2,1)S(1)}, bf16[240,256]{1,0:T(8,128)(2,1)S(1)}, u32[]{:S(2)}, u32[]{:S(2)}) collective-permute-start(bf16[240,256]{1,0:T(8,128)(2,1)S(1)} %collective-permute-done.90.refs_5_.refs_2_), channel_id=1, source_target_pairs={{1,2},{2,1},{0,4},{3,7},{5,6},{6,5},{4,0},{7,3},{9,10},{10,9},{8,1... | collective-permute-start | bytes 368648 | tf_op jit(solution)/shard_map/ppermute | solution.py:538
  182.5 14.6 %collective-permute-start.102 = (bf16[256,256]{1,0:T(8,128)(2,1)S(1)}, bf16[256,256]{1,0:T(8,128)(2,1)S(1)}, u32[]{:S(2)}, u32[]{:S(2)}) collective-permute-start(bf16[256,256]{1,0:T(8,128)(2,1)S(1)} %collective-permute-done.101.refs_19_.refs_16_), channel_id=1, source_target_pairs={{0,1},{1,0},{2,3},{3,2},{4,5},{5,4},{6,7},{7,6},{8,9},{9,8},{10,11... | collective-permute-start | bytes 393224 | tf_op jit(solution)/shard_map/ppermute | solution.py:33
  186.4 12.7 %collective-permute-start.104 = (bf16[256,256]{1,0:T(8,128)(2,1)S(1)}, bf16[256,256]{1,0:T(8,128)(2,1)S(1)}, u32[]{:S(2)}, u32[]{:S(2)}) collective-permute-start(bf16[256,256]{1,0:T(8,128)(2,1)S(1)} %collective-permute-done.103.refs_21_.refs_18_), channel_id=1, source_target_pairs={{0,1},{1,0},{2,3},{3,2},{4,5},{5,4},{6,7},{7,6},{8,9},{9,8},{10,11... | collective-permute-start | bytes 393224 | tf_op jit(solution)/shard_map/ppermute | solution.py:33
  189.2 7.8 %collective-permute-start.92 = (bf16[240,256]{1,0:T(8,128)(2,1)S(1)}, bf16[240,256]{1,0:T(8,128)(2,1)S(1)}, u32[]{:S(2)}, u32[]{:S(2)}) collective-permute-start(bf16[240,256]{1,0:T(8,128)(2,1)S(1)} %collective-permute-done.91.refs_7_.refs_4_), channel_id=1, source_target_pairs={{0,1},{1,0},{2,3},{3,2},{4,5},{5,4},{6,7},{7,6},{8,9},{9,8},{10,11... | collective-permute-start | bytes 368648 | tf_op jit(solution)/shard_map/ppermute | solution.py:33
  210.3 8.1 %collective-permute-start.106 = (bf16[2,128,512]{2,1,0:T(8,128)(2,1)S(1)}, bf16[2,128,512]{2,1,0:T(8,128)(2,1)S(1)}, u32[]{:S(2)}, u32[]{:S(2)}) collective-permute-start(bf16[2,128,512]{2,1,0:T(8,128)(2,1)S(1)} %slice_bitcast_fusion), channel_id=1, source_target_pairs={{0,8},{4,12},{8,0},{12,4},{1,9},{5,13},{9,1},{13,5},{2,10},{6,14},... | collective-permute-start | bytes 786440 | tf_op jit(solution)/shard_map/ppermute | solution.py:33
  (47 other events, 254.9 us)

commit v10 on v9

--- a/solution.py
+++ b/solution.py
@@ -9,7 +9,7 @@
 
 F32, BF16 = jnp.float32, jnp.bfloat16
 VMEM_BYTES = 20 << 20
-STREAMS = 3
+STREAMS = 2
 
 
 def line_pairs(n, gather, step):
@@ -244,14 +244,10 @@
     if has_prev:
         prev, refs = refs[:2], refs[2:]
     halves, refs = split_pieces(refs, sizes)
-    weights, (near, far, token, *refs) = refs[:3], refs[3:]
+    (gw, uw, dw), (near, far, token, *refs) = refs[:3], refs[3:]
     if last:
         near_p, far_p, *refs, held = refs
-    gw, uw, dw, sems, eo_ref, idl_ref = refs
-    copies = weight_copies(expert, weights, (gw, uw, dw), sems)
-    for group in copies:
-        for copy in group:
-            copy.start()
+    eo_ref, idl_ref = refs
     token[...] = jnp.zeros_like(token)
     spots = routing(scal, routes, expert, halves[0][0][0].shape[0] // 48 * 16)
     if last:
@@ -259,8 +255,6 @@
     tile = gw.shape[1] // STREAMS
     eo, idl = 0.0, 0.0
     for h in range(STREAMS):
-        for copy in copies[h]:
-            copy.wait()
         part = slice(h * tile, (h + 1) * tile)
         eo = eo + dot(load_rows(scal, n, 0, halves[h]), dw[part, :])
         idl = idl + dot(load_rows(scal, n, 1, halves[h]), gw[:, part], ((1,), (1,)))
@@ -293,8 +287,9 @@
 
         @pl.when(step == h)
         def _():
-            gg[0] = dot(in_ref[...], load_rows(scal, n, 1, halves[h]), ((0,), (0,))).astype(BF16)
-            ug[0] = dot(in_ref[...], load_rows(scal, n, 2, halves[h]), ((0,), (0,))).astype(BF16)
+            deltas = [load_rows(scal, n, k, halves[h]) for k in (1, 2)]
+            both = dot(in_ref[...], jnp.concatenate(deltas, axis=1), ((0,), (0,))).astype(BF16)
+            gg[0], ug[0] = both[:, : gg.shape[2]], both[:, gg.shape[2] :]
             dg[0] = dot(load_rows(scal, n, 0, halves[h]), cot_ref[...], ((0,), (0,))).astype(BF16)
 
 
@@ -422,30 +417,31 @@
     slot_shape = (all_rows, width)
 
     weights = [in_hbm(w) for w in (gate_weight, up_weight, down_weight)]
-    held_weights = [pltpu.VMEM(w.shape[1:], BF16) for w in weights] + [
-        pltpu.SemaphoreType.DMA((STREAMS, 3))
-    ]
-
     def grad_specs(e):
         wide = pl.BlockSpec((1, width, tile), lambda g: (e, 0, g))
         return [wide, wide, pl.BlockSpec((1, tile, width), lambda g: (e, g, 0))]
 
+    own_weights = []
+
     def pre(e, deps):
-        inputs, cot, *parts, token, found = call(
+        inputs, cot, *parts, token, found, gw, uw, dw = call(
             functools.partial(pre_kernel, n, e, choose, len(deps)),
             1,
             [SMEM_SPEC] + [ANY_SPEC] * len(deps) + [spec_of(x) for x in packs] + [HBM_SPEC] * 3,
             [whole_spec(slot_shape)] * 2
             + [whole_spec(piece_shape)] * (STREAMS * n)
-            + [whole_spec(TOKEN), whole_spec(route_shape)],
+            + [whole_spec(TOKEN), whole_spec(route_shape)]
+            + [whole_spec(w.shape[1:]) for w in weights],
             [like(slot_shape)] * 2
             + [like(piece_shape)] * (STREAMS * n)
-            + [like(TOKEN, F32), like(route_shape, F32)],
+            + [like(TOKEN, F32), like(route_shape, F32)]
+            + [like(w.shape[1:]) for w in weights],
             6 * mac,
             3 * weight_bytes + STREAMS * n * piece_bytes,
-            scratch_shapes=held_weights,
+            scratch_shapes=[pltpu.SemaphoreType.DMA((STREAMS, 3))],
         )(scal, *deps, *packs, *weights)
         parts = [parts[h * n : (h + 1) * n] for h in range(STREAMS)]
+        own_weights.append((gw, uw, dw))
         return (inputs, cot), parts, token, found
 
     def mid(e, h, totals, products, deps=()):
@@ -493,7 +489,7 @@
             + [whole_spec(route_shape)]
             + ([whole_spec(sum_shape)] * 2 if e > 0 else [])
             + [spec_of(x) for x in flat]
-            + [HBM_SPEC] * 3,
+            + [whole_spec(w.shape[1:]) for w in weights],
             [whole_spec(sum_shape)] * 2
             + [whole_spec(TOKEN)]
             + ([whole_spec(dense_shape)] * 2 if last else []),
@@ -502,10 +498,9 @@
             + ([like(dense_shape, F32)] * 2 if last else []),
             6 * mac,
             3 * weight_bytes + len(flat) * piece_bytes,
-            scratch_shapes=held_weights
-            + [pltpu.VMEM(slot_shape, BF16)] * 2
+            scratch_shapes=[pltpu.VMEM(slot_shape, BF16)] * 2
             + ([pltpu.VMEM((n, extra, 128), BF16)] if last else []),
-        )(scal, *deps, routes, *prev, *flat, *weights)
+        )(scal, *deps, routes, *prev, *flat, *own_weights[e])
 
     def grad(e, slots, halves, prev, deps):
         flat = flatten(halves)
@@ -617,8 +612,8 @@
 
     near, far, _, near_p, far_p = out(local - 1, halves, sums, wait)
     hop, home = send_home(near, far, add_rounded)
-    *grads, token = grad(local - 1, arrived, halves, grads, [hop])
-    _, per_expert = send_home(near_p, far_p, lambda a, b: add(a, b, [token]))
+    _, per_expert = send_home(near_p, far_p, lambda a, b: add(a, b, [hop]))
+    *grads, _ = grad(local - 1, arrived, halves, grads, [hop])
     combine_grad = jnp.sum(jnp.where(named, per_expert[None], 0.0), axis=1) / combine_t
     return (home[0].astype(BF16), home[1].astype(BF16), *grads, combine_grad.T)
 

time: 220 us -> 196 us (0.89)
  starting transfers between devices: 130 us -> 95.4 us
  waiting for transfers between devices: 37.7 us -> 54.7 us
  Pallas kernels: 47.2 us -> 41.2 us
    ppermute x61 -> x43, starting transfers between devices: 123 us -> 92.2 us  [send(): return lax.ppermute(value, self.axis, wide)]
    ppermute x61 -> x43, waiting for transfers between devices: 37.6 us -> 54.6 us  [send(): return lax.ppermute(value, self.axis, wide)]
    pallas_call x4, Pallas kernels: 13.5 us -> 9.88 us  [out(): call(functools.partial(out_kernel, n, e, e > 0, last, sizes_of(halves[0])...]
    ppermute x48 -> x32, starting transfers between devices: 6.48 us -> 3.27 us  [inner(): return lax.ppermute(value, ('expert', 'dp'), pairs)]
  transfers between devices with their start and end apart: 109 -> 75, of which waited for: 18 -> 21; matrix products, arithmetic and copies ran while one was open for 1% -> 1% of each run, Pallas kernels for 17% -> 17%
where the time goes in v10:
time: 196 us
  starting transfers between devices  95.4 us (49%)
  waiting for transfers between devices  54.7 us (28%)
  Pallas kernels  41.2 us (21%)
  other arithmetic  2.16 us (1%)
    ppermute x43, starting transfers between devices, send(): return lax.ppermute(value, self.axis, wide)  92.2 us
    ppermute x43, waiting for transfers between devices, send(): return lax.ppermute(value, self.axis, wide)  54.6 us
    pallas_call x4, Pallas kernels, pre(): call(functools.partial(pre_kernel, n, e, choose, len(deps)), 1, [SMEM_SPE...  14.7 us
    pallas_call x4, Pallas kernels, grad(): call(functools.partial(grad_kernel, n, e > 0, sizes_of(halves[0]), len(de...  13.4 us
    pallas_call x4, Pallas kernels, out(): call(functools.partial(out_kernel, n, e, e > 0, last, sizes_of(halves[0])...  9.88 us
  transfers between devices with their start and end apart: 75, of which 21 were waited for; matrix products, arithmetic and copies ran while one was open for 1% of the time, Pallas kernels for 17%

profile of v10, /device:TPU:0, one launch (start us, length us, event | category | flops | bytes accessed | tf_op | source)
XLA Modules:
  0.0 195.5 jit_solution(10565689503998492114)
XLA Ops:
  0.6 1.0 shard_map.118.refs_0_.refs_1_
  1.7 3.0 %collective-permute-start = (bf16[272,512]{1,0:T(8,128)(2,1)S(1)}, bf16[272,512]{1,0:T(8,128)(2,1)S(1)}, u32[]{:S(2)}, u32[]{:S(2)}) collective-permute-start(bf16[272,512]{1,0:T(8,128)(2,1)S(1)} %shard_map.118.refs_0_.refs_1_), channel_id=1, source_target_pairs={{0,8},{4,12},{8,0},{12,4},{1,9},{5,13},{9,1},{13,5},{2,10},{6,14},... | collective-permute-start | bytes 835592 | tf_op jit(solution)/shard_map/ppermute | solution.py:33
  4.7 6.7 %collective-permute-done.refs_1_.refs_2_ = bf16[272,512]{1,0:T(8,128)(2,1)S(1)} collective-permute-done((bf16[272,512]{1,0:T(8,128)(2,1)S(1)}, bf16[272,512]{1,0:T(8,128)(2,1)S(1)}, u32[]{:S(2)}, u32[]{:S(2)}) %collective-permute-start) | collective-permute-done | bytes 278560 | tf_op jit(solution)/shard_map/ppermute | solution.py:33
  11.4 1.5 collective-permute-done.2.refs_3_.refs_4_
  12.9 3.5 %shard_map.119 = (bf16[320,512]{1,0:T(8,128)(2,1)S(1)}, bf16[320,512]{1,0:T(8,128)(2,1)S(1)}, bf16[240,384]{1,0:T(8,128)(2,1)S(1)}, bf16[240,384]{1,0:T(8,128)(2...) custom-call(s32[10]{0:T(128)S(1)} %stack.35.scal, ...), custom_call_target="tpu_custom_call" | custom-call | flops 754974720 | bytes 3833856 | tf_op jit(solution)/shard_map/pallas_call | solution.py:427
  16.4 1.9 collective-permute-start.3
  18.5 1.8 collective-permute-start.32
  20.6 3.7 %shard_map.123 = (bf16[320,512]{1,0:T(8,128)(2,1)S(1)}, bf16[320,512]{1,0:T(8,128)(2,1)S(1)}, bf16[240,384]{1,0:T(8,128)(2,1)S(1)}, bf16[240,384]{1,0:T(8,128)(2...) custom-call(s32[10]{0:T(128)S(1)} %stack.35.scal, ...), custom_call_target="tpu_custom_call" | custom-call | flops 754974720 | bytes 3833856 | tf_op jit(solution)/shard_map/pallas_call | solution.py:427
  24.4 3.5 %collective-permute-done.6 = bf16[240,384]{1,0:T(8,128)(2,1)S(1)} collective-permute-done((bf16[240,384]{1,0:T(8,128)(2,1)S(1)}, bf16[240,384]{1,0:T(8,128)(2,1)S(1)}, u32[]{:S(2)}, u32[]{:S(2)}) %collective-permute-start.6) | collective-permute-done | bytes 184352 | tf_op jit(solution)/shard_map/ppermute | solution.py:33
  28.1 3.8 %collective-permute-done.32.refs_2_ = bf16[240,384]{1,0:T(8,128)(2,1)S(1)} collective-permute-done((bf16[240,384]{1,0:T(8,128)(2,1)S(1)}, bf16[240,384]{1,0:T(8,128)(2,1)S(1)}, u32[]{:S(2)}, u32[]{:S(2)}) %collective-permute-start.32) | collective-permute-done | bytes 184352 | tf_op jit(solution)/shard_map/ppermute | solution.py:33
  32.0 3.1 %collective-permute-done.35 = bf16[240,384]{1,0:T(8,128)(2,1)S(1)} collective-permute-done((bf16[240,384]{1,0:T(8,128)(2,1)S(1)}, bf16[240,384]{1,0:T(8,128)(2,1)S(1)}, u32[]{:S(2)}, u32[]{:S(2)}) %collective-permute-start.35) | collective-permute-done | bytes 184352 | tf_op jit(solution)/shard_map/ppermute | solution.py:33
  35.3 3.4 %collective-permute-start.5 = (bf16[240,384]{1,0:T(8,128)(2,1)S(1)}, bf16[240,384]{1,0:T(8,128)(2,1)S(1)}, u32[]{:S(2)}, u32[]{:S(2)}) collective-permute-start(bf16[240,384]{1,0:T(8,128)(2,1)S(1)} %fusion.1), channel_id=1, source_target_pairs={{0,1},{1,0},{2,3},{3,2},{4,5},{5,4},{6,7},{7,6},{8,9},{9,8},{10,11... | collective-permute-start | bytes 552968 | tf_op jit(solution)/shard_map/ppermute | solution.py:33
  38.8 1.8 collective-permute-start.34
  40.5 3.7 %collective-permute-done.5.refs_1_ = bf16[240,384]{1,0:T(8,128)(2,1)S(1)} collective-permute-done((bf16[240,384]{1,0:T(8,128)(2,1)S(1)}, bf16[240,384]{1,0:T(8,128)(2,1)S(1)}, u32[]{:S(2)}, u32[]{:S(2)}) %collective-permute-start.5) | collective-permute-done | bytes 184352 | tf_op jit(solution)/shard_map/ppermute | solution.py:33
  44.5 2.4 %collective-permute-start.12 = (bf16[240,384]{1,0:T(8,128)(2,1)S(1)}, bf16[240,384]{1,0:T(8,128)(2,1)S(1)}, u32[]{:S(2)}, u32[]{:S(2)}) collective-permute-start(bf16[240,384]{1,0:T(8,128)(2,1)S(1)} %get-tuple-element.109.refs_7_), channel_id=1, source_target_pairs={{0,1},{1,0},{2,3},{3,2},{4,5},{5,4},{6,7},{7,6},{8,9},{9,8},{10,11... | collective-permute-start | bytes 552968 | tf_op jit(solution)/shard_map/ppermute | solution.py:33
  47.0 1.7 collective-permute-start.37
  48.8 3.5 %collective-permute-start.9 = (bf16[240,384]{1,0:T(8,128)(2,1)S(1)}, bf16[240,384]{1,0:T(8,128)(2,1)S(1)}, u32[]{:S(2)}, u32[]{:S(2)}) collective-permute-start(bf16[240,384]{1,0:T(8,128)(2,1)S(1)} %broadcast_select_fusion.11), channel_id=1, source_target_pairs={{0,1},{1,0},{2,3},{3,2},{4,5},{5,4},{6,7},{7,6},{8,9},{9,8},{10,11... | collective-permute-start | bytes 552968 | tf_op jit(solution)/shard_map/ppermute | solution.py:33
  52.4 4.9 %collective-permute-start.39 = (bf16[240,384]{1,0:T(8,128)(2,1)S(1)}, bf16[240,384]{1,0:T(8,128)(2,1)S(1)}, u32[]{:S(2)}, u32[]{:S(2)}) collective-permute-start(bf16[240,384]{1,0:T(8,128)(2,1)S(1)} %broadcast_select_fusion.5), channel_id=1, source_target_pairs={{0,1},{1,0},{2,3},{3,2},{4,5},{5,4},{6,7},{7,6},{8,9},{9,8},{10,11... | collective-permute-start | bytes 552968 | tf_op jit(solution)/shard_map/ppermute | solution.py:33
  57.3 3.7 %shard_map.122 = (bf16[320,512]{1,0:T(8,128)(2,1)S(1)}, bf16[320,512]{1,0:T(8,128)(2,1)S(1)}, bf16[240,384]{1,0:T(8,128)(2,1)S(1)}, bf16[240,384]{1,0:T(8,128)(2...) custom-call(s32[10]{0:T(128)S(1)} %stack.35.scal, ...), custom_call_target="tpu_custom_call" | custom-call | flops 754974720 | bytes 3833856 | tf_op jit(solution)/shard_map/pallas_call | solution.py:427
  61.7 2.7 %collective-permute-start.14 = (bf16[240,384]{1,0:T(8,128)(2,1)S(1)}, bf16[240,384]{1,0:T(8,128)(2,1)S(1)}, u32[]{:S(2)}, u32[]{:S(2)}) collective-permute-start(bf16[240,384]{1,0:T(8,128)(2,1)S(1)} %broadcast_select_fusion.10), channel_id=1, source_target_pairs={{0,1},{1,0},{2,3},{3,2},{4,5},{5,4},{6,7},{7,6},{8,9},{9,8},{10,11... | collective-permute-start | bytes 552968 | tf_op jit(solution)/shard_map/ppermute | solution.py:33
  64.4 1.2 collective-permute-start.41
  65.8 4.9 %collective-permute-start.11 = (bf16[240,384]{1,0:T(8,128)(2,1)S(1)}, bf16[240,384]{1,0:T(8,128)(2,1)S(1)}, u32[]{:S(2)}, u32[]{:S(2)}) collective-permute-start(bf16[240,384]{1,0:T(8,128)(2,1)S(1)} %fusion.2), channel_id=1, source_target_pairs={{0,1},{1,0},{2,3},{3,2},{4,5},{5,4},{6,7},{7,6},{8,9},{9,8},{10,11... | collective-permute-start | bytes 552968 | tf_op jit(solution)/shard_map/ppermute | solution.py:33
  70.9 3.3 %collective-permute-start.43 = (bf16[240,384]{1,0:T(8,128)(2,1)S(1)}, bf16[240,384]{1,0:T(8,128)(2,1)S(1)}, u32[]{:S(2)}, u32[]{:S(2)}) collective-permute-start(bf16[240,384]{1,0:T(8,128)(2,1)S(1)} %fusion.6), channel_id=1, source_target_pairs={{0,1},{1,0},{2,3},{3,2},{4,5},{5,4},{6,7},{7,6},{8,9},{9,8},{10,11... | collective-permute-start | bytes 552968 | tf_op jit(solution)/shard_map/ppermute | solution.py:33
  74.4 3.5 %collective-permute-done.11.refs_1_ = bf16[240,384]{1,0:T(8,128)(2,1)S(1)} collective-permute-done((bf16[240,384]{1,0:T(8,128)(2,1)S(1)}, bf16[240,384]{1,0:T(8,128)(2,1)S(1)}, u32[]{:S(2)}, u32[]{:S(2)}) %collective-permute-start.11) | collective-permute-done | bytes 184352 | tf_op jit(solution)/shard_map/ppermute | solution.py:33
  78.1 2.2 %shard_map.132 = (f32[2,2,128,512]{3,2,1,0:T(8,128)S(1)}, f32[2,2,128,512]{3,2,1,0:T(8,128)S(1)}, f32[8,128]{1,0:T(8,128)S(1)}) custom-call(s32[10]{0:T(128)S(1)} %stack.35.scal, f32[4,16,128]{2,1,0:T(8,128)S(1)} %get-tuple-element.135.refs_0_.refs_1_, bf16[240,384]{1,0:T(8,128)(2,1)S(1)} %get-tuple-element.136.refs_1_, ...), custom_call_target="tpu_custom_call" | custom-call | flops 754974720 | bytes 4571136 | tf_op jit(solution)/shard_map/pallas_call | solution.py:484
  80.3 3.3 %collective-permute-start.20 = (bf16[240,384]{1,0:T(8,128)(2,1)S(1)}, bf16[240,384]{1,0:T(8,128)(2,1)S(1)}, u32[]{:S(2)}, u32[]{:S(2)}) collective-permute-start(bf16[240,384]{1,0:T(8,128)(2,1)S(1)} %get-tuple-element.117.refs_9_.refs_0_.refs_7_), channel_id=1, source_target_pairs={{0,1},{1,0},{2,3},{3,2},{4,5},{5,4},{6,7},{7,6},{8,9},{9,8},{10,11... | collective-permute-start | bytes 552968 | tf_op jit(solution)/shard_map/ppermute | solution.py:33
  83.8 3.5 %shard_map.136 = (bf16[4,512,768]{2,1,0:T(8,128)(2,1)}, bf16[4,512,768]{2,1,0:T(8,128)(2,1)}, bf16[4,768,512]{2,1,0:T(8,128)(2,1)}, f32[8,128]{1,0:T(8,128)S(1)}) custom-call(s32[10]{0:T(128)S(1)} %stack.35.scal, bf16[320,512]{1,0:T(8,128)(2,1)S(1)} %get-tuple-element.158.in_ref, bf16[320,512]{1,0:T(8,128)(2,1)S(1)} %get-tuple-element.159.cot_ref, ...), custom_call_target="tpu_custom_call" | custom-call | flops 754974720 | bytes 4571136 | tf_op jit(solution)/shard_map/pallas_call | solution.py:508
  87.4 1.9 collective-permute-start.17
  89.3 2.1 %collective-permute-start.47 = (bf16[240,384]{1,0:T(8,128)(2,1)S(1)}, bf16[240,384]{1,0:T(8,128)(2,1)S(1)}, u32[]{:S(2)}, u32[]{:S(2)}) collective-permute-start(bf16[240,384]{1,0:T(8,128)(2,1)S(1)} %broadcast_select_fusion.3), channel_id=1, source_target_pairs={{0,1},{1,0},{2,3},{3,2},{4,5},{5,4},{6,7},{7,6},{8,9},{9,8},{10,11... | collective-permute-start | bytes 552968 | tf_op jit(solution)/shard_map/ppermute | solution.py:33
  91.4 0.8 collective-permute-done.45.refs_4_.refs_2_
  92.2 3.7 %shard_map.126 = (bf16[320,512]{1,0:T(8,128)(2,1)S(1)}, bf16[320,512]{1,0:T(8,128)(2,1)S(1)}, bf16[240,384]{1,0:T(8,128)(2,1)S(1)}, bf16[240,384]{1,0:T(8,128)(2...) custom-call(s32[10]{0:T(128)S(1)} %stack.35.scal, ...), custom_call_target="tpu_custom_call" | custom-call | flops 754974720 | bytes 3833856 | tf_op jit(solution)/shard_map/pallas_call | solution.py:427
  96.6 2.3 %collective-permute-start.22 = (bf16[240,384]{1,0:T(8,128)(2,1)S(1)}, bf16[240,384]{1,0:T(8,128)(2,1)S(1)}, u32[]{:S(2)}, u32[]{:S(2)}) collective-permute-start(bf16[240,384]{1,0:T(8,128)(2,1)S(1)} %broadcast_select_fusion.8), channel_id=1, source_target_pairs={{0,1},{1,0},{2,3},{3,2},{4,5},{5,4},{6,7},{7,6},{8,9},{9,8},{10,11... | collective-permute-start | bytes 552968 | tf_op jit(solution)/shard_map/ppermute | solution.py:33
  99.0 1.3 collective-permute-start.49
  100.5 5.6 %collective-permute-start.19 = (bf16[240,384]{1,0:T(8,128)(2,1)S(1)}, bf16[240,384]{1,0:T(8,128)(2,1)S(1)}, u32[]{:S(2)}, u32[]{:S(2)}) collective-permute-start(bf16[240,384]{1,0:T(8,128)(2,1)S(1)} %fusion.3), channel_id=1, source_target_pairs={{0,1},{1,0},{2,3},{3,2},{4,5},{5,4},{6,7},{7,6},{8,9},{9,8},{10,11... | collective-permute-start | bytes 552968 | tf_op jit(solution)/shard_map/ppermute | solution.py:33
  106.3 3.7 %collective-permute-start.51 = (bf16[240,384]{1,0:T(8,128)(2,1)S(1)}, bf16[240,384]{1,0:T(8,128)(2,1)S(1)}, u32[]{:S(2)}, u32[]{:S(2)}) collective-permute-start(bf16[240,384]{1,0:T(8,128)(2,1)S(1)} %fusion.7), channel_id=1, source_target_pairs={{0,1},{1,0},{2,3},{3,2},{4,5},{5,4},{6,7},{7,6},{8,9},{9,8},{10,11... | collective-permute-start | bytes 552968 | tf_op jit(solution)/shard_map/ppermute | solution.py:33
  110.1 2.2 %collective-permute-done.19.refs_1_ = bf16[240,384]{1,0:T(8,128)(2,1)S(1)} collective-permute-done((bf16[240,384]{1,0:T(8,128)(2,1)S(1)}, bf16[240,384]{1,0:T(8,128)(2,1)S(1)}, u32[]{:S(2)}, u32[]{:S(2)}) %collective-permute-start.19) | collective-permute-done | bytes 184352 | tf_op jit(solution)/shard_map/ppermute | solution.py:33
  112.6 2.2 %shard_map.135 = (f32[2,2,128,512]{3,2,1,0:T(8,128)S(1)}, f32[2,2,128,512]{3,2,1,0:T(8,128)S(1)}, f32[8,128]{1,0:T(8,128)S(1)}) custom-call(s32[10]{0:T(128)S(1)} %stack.35.scal, f32[4,16,128]{2,1,0:T(8,128)S(1)} %get-tuple-element.135.refs_0_.refs_1_, f32[2,2,128,512]{3,2,1,0:T(8,128)S(1)} %get-tuple-element.147.refs_1_, ...), custom_call_target="tpu_custom_call" | custom-call | flops 754974720 | bytes 4571136 | tf_op jit(solution)/shard_map/pallas_call | solution.py:484
  114.8 3.3 %collective-permute-start.28 = (bf16[240,384]{1,0:T(8,128)(2,1)S(1)}, bf16[240,384]{1,0:T(8,128)(2,1)S(1)}, u32[]{:S(2)}, u32[]{:S(2)}) collective-permute-start(bf16[240,384]{1,0:T(8,128)(2,1)S(1)} %get-tuple-element.126.refs_9_.refs_0_.refs_7_), channel_id=1, source_target_pairs={{0,1},{1,0},{2,3},{3,2},{4,5},{5,4},{6,7},{7,6},{8,9},{9,8},{10,11... | collective-permute-start | bytes 552968 | tf_op jit(solution)/shard_map/ppermute | solution.py:33
  118.4 3.3 %shard_map.140 = (bf16[4,512,768]{2,1,0:T(8,128)(2,1)}, bf16[4,512,768]{2,1,0:T(8,128)(2,1)}, bf16[4,768,512]{2,1,0:T(8,128)(2,1)}, f32[8,128]{1,0:T(8,128)S(1)}) custom-call(s32[10]{0:T(128)S(1)} %stack.35.scal, bf16[320,512]{1,0:T(8,128)(2,1)S(1)} %get-tuple-element.174.in_ref, ...), custom_call_target="tpu_custom_call", output_to_operand_aliasing={{0}: (16, {}), {1}: (17, {}), {2}: (18, {})} | custom-call | flops 754974720 | bytes 4571136 | tf_op jit(solution)/shard_map/pallas_call | solution.py:508
  121.7 2.0 %collective-permute-start.25 = (bf16[240,384]{1,0:T(8,128)(2,1)S(1)}, bf16[240,384]{1,0:T(8,128)(2,1)S(1)}, u32[]{:S(2)}, u32[]{:S(2)}) collective-permute-start(bf16[240,384]{1,0:T(8,128)(2,1)S(1)} %broadcast_select_fusion.7), channel_id=1, source_target_pairs={{0,1},{1,0},{2,3},{3,2},{4,5},{5,4},{6,7},{7,6},{8,9},{9,8},{10,11... | collective-permute-start | bytes 552968 | tf_op jit(solution)/shard_map/ppermute | solution.py:33
  123.8 2.2 %collective-permute-start.55 = (bf16[240,384]{1,0:T(8,128)(2,1)S(1)}, bf16[240,384]{1,0:T(8,128)(2,1)S(1)}, u32[]{:S(2)}, u32[]{:S(2)}) collective-permute-start(bf16[240,384]{1,0:T(8,128)(2,1)S(1)} %broadcast_select_fusion.1), channel_id=1, source_target_pairs={{0,1},{1,0},{2,3},{3,2},{4,5},{5,4},{6,7},{7,6},{8,9},{9,8},{10,11... | collective-permute-start | bytes 552968 | tf_op jit(solution)/shard_map/ppermute | solution.py:33
  125.9 0.8 collective-permute-done.53.refs_4_.refs_2_
  126.8 3.9 %collective-permute-done.25.refs_1_.refs_11_.refs_9_ = bf16[240,384]{1,0:T(8,128)(2,1)S(1)} collective-permute-done((bf16[240,384]{1,0:T(8,128)(2,1)S(1)}, bf16[240,384]{1,0:T(8,128)(2,1)S(1)}, u32[]{:S(2)}, u32[]{:S(2)}) %collective-permute-start.25) | collective-permute-done | bytes 184352 | tf_op jit(solution)/shard_map/ppermute | solution.py:33
  130.9 2.6 %collective-permute-start.30 = (bf16[240,384]{1,0:T(8,128)(2,1)S(1)}, bf16[240,384]{1,0:T(8,128)(2,1)S(1)}, u32[]{:S(2)}, u32[]{:S(2)}) collective-permute-start(bf16[240,384]{1,0:T(8,128)(2,1)S(1)} %broadcast_select_fusion.6), channel_id=1, source_target_pairs={{0,1},{1,0},{2,3},{3,2},{4,5},{5,4},{6,7},{7,6},{8,9},{9,8},{10,11... | collective-permute-start | bytes 552968 | tf_op jit(solution)/shard_map/ppermute | solution.py:33
  133.5 2.2 %collective-permute-start.57 = (bf16[240,384]{1,0:T(8,128)(2,1)S(1)}, bf16[240,384]{1,0:T(8,128)(2,1)S(1)}, u32[]{:S(2)}, u32[]{:S(2)}) collective-permute-start(bf16[240,384]{1,0:T(8,128)(2,1)S(1)} %broadcast_select_fusion), channel_id=1, source_target_pairs={{0,1},{1,0},{2,3},{3,2},{4,5},{5,4},{6,7},{7,6},{8,9},{9,8},{10,11... | collective-permute-start | bytes 552968 | tf_op jit(solution)/shard_map/ppermute | solution.py:33
  135.9 3.8 %collective-permute-start.27 = (bf16[240,384]{1,0:T(8,128)(2,1)S(1)}, bf16[240,384]{1,0:T(8,128)(2,1)S(1)}, u32[]{:S(2)}, u32[]{:S(2)}) collective-permute-start(bf16[240,384]{1,0:T(8,128)(2,1)S(1)} %fusion.4), channel_id=1, source_target_pairs={{0,1},{1,0},{2,3},{3,2},{4,5},{5,4},{6,7},{7,6},{8,9},{9,8},{10,11... | collective-permute-start | bytes 552968 | tf_op jit(solution)/shard_map/ppermute | solution.py:33
  139.8 2.7 %collective-permute-start.59 = (bf16[240,384]{1,0:T(8,128)(2,1)S(1)}, bf16[240,384]{1,0:T(8,128)(2,1)S(1)}, u32[]{:S(2)}, u32[]{:S(2)}) collective-permute-start(bf16[240,384]{1,0:T(8,128)(2,1)S(1)} %fusion.8), channel_id=1, source_target_pairs={{0,1},{1,0},{2,3},{3,2},{4,5},{5,4},{6,7},{7,6},{8,9},{9,8},{10,11... | collective-permute-start | bytes 552968 | tf_op jit(solution)/shard_map/ppermute | solution.py:33
  143.7 2.2 %shard_map.139 = (f32[2,2,128,512]{3,2,1,0:T(8,128)S(1)}, f32[2,2,128,512]{3,2,1,0:T(8,128)S(1)}, f32[8,128]{1,0:T(8,128)S(1)}) custom-call(s32[10]{0:T(128)S(1)} %stack.35.scal, f32[4,16,128]{2,1,0:T(8,128)S(1)} %get-tuple-element.135.refs_0_.refs_1_, f32[2,2,128,512]{3,2,1,0:T(8,128)S(1)} %get-tuple-element.163.refs_1_, ...), custom_call_target="tpu_custom_call" | custom-call | flops 754974720 | bytes 4571136 | tf_op jit(solution)/shard_map/pallas_call | solution.py:484
  145.9 3.9 %collective-permute-done.59.refs_2_ = bf16[240,384]{1,0:T(8,128)(2,1)S(1)} collective-permute-done((bf16[240,384]{1,0:T(8,128)(2,1)S(1)}, bf16[240,384]{1,0:T(8,128)(2,1)S(1)}, u32[]{:S(2)}, u32[]{:S(2)}) %collective-permute-start.59) | collective-permute-done | bytes 184352 | tf_op jit(solution)/shard_map/ppermute | solution.py:33
  150.8 2.1 %collective-permute-start.66 = (bf16[256,384]{1,0:T(8,128)(2,1)S(1)}, bf16[256,384]{1,0:T(8,128)(2,1)S(1)}, u32[]{:S(2)}, u32[]{:S(2)}) collective-permute-start(bf16[256,384]{1,0:T(8,128)(2,1)S(1)} %get-tuple-element.181.refs_0_.refs_10_.refs_7_), channel_id=1, source_target_pairs={{0,1},{1,0},{2,3},{3,2},{4,5},{5,4},{6,7},{7,6},{8,9},{9,8},{10,11... | collective-permute-start | bytes 589832 | tf_op jit(solution)/shard_map/ppermute | solution.py:33
  153.0 5.7 %collective-permute-done.66.refs_11_.refs_8_ = bf16[256,384]{1,0:T(8,128)(2,1)S(1)} collective-permute-done((bf16[256,384]{1,0:T(8,128)(2,1)S(1)}, bf16[256,384]{1,0:T(8,128)(2,1)S(1)}, u32[]{:S(2)}, u32[]{:S(2)}) %collective-permute-start.66) | collective-permute-done | bytes 196640 | tf_op jit(solution)/shard_map/ppermute | solution.py:33
  159.2 1.5 collective-permute-done.61.refs_5_.refs_2_
  160.7 2.3 %collective-permute-start.68 = (bf16[256,384]{1,0:T(8,128)(2,1)S(1)}, bf16[256,384]{1,0:T(8,128)(2,1)S(1)}, u32[]{:S(2)}, u32[]{:S(2)}) collective-permute-start(bf16[256,384]{1,0:T(8,128)(2,1)S(1)} %collective-permute-done.67.refs_13_.refs_10_), channel_id=1, source_target_pairs={{0,1},{1,0},{2,3},{3,2},{4,5},{5,4},{6,7},{7,6},{8,9},{9,8},{10,11... | collective-permute-start | bytes 589832 | tf_op jit(solution)/shard_map/ppermute | solution.py:33
  163.0 3.9 %collective-permute-start.70 = (bf16[256,384]{1,0:T(8,128)(2,1)S(1)}, bf16[256,384]{1,0:T(8,128)(2,1)S(1)}, u32[]{:S(2)}, u32[]{:S(2)}) collective-permute-start(bf16[256,384]{1,0:T(8,128)(2,1)S(1)} %collective-permute-done.69.refs_15_.refs_12_), channel_id=1, source_target_pairs={{0,1},{1,0},{2,3},{3,2},{4,5},{5,4},{6,7},{7,6},{8,9},{9,8},{10,11... | collective-permute-start | bytes 589832 | tf_op jit(solution)/shard_map/ppermute | solution.py:33
  166.9 3.3 %collective-permute-start.63 = (bf16[240,384]{1,0:T(8,128)(2,1)S(1)}, bf16[240,384]{1,0:T(8,128)(2,1)S(1)}, u32[]{:S(2)}, u32[]{:S(2)}) collective-permute-start(bf16[240,384]{1,0:T(8,128)(2,1)S(1)} %collective-permute-done.62.refs_7_.refs_4_), channel_id=1, source_target_pairs={{0,1},{1,0},{2,3},{3,2},{4,5},{5,4},{6,7},{7,6},{8,9},{9,8},{10,11... | collective-permute-start | bytes 552968 | tf_op jit(solution)/shard_map/ppermute | solution.py:33
  170.2 2.0 %collective-permute-start.65 = (bf16[240,384]{1,0:T(8,128)(2,1)S(1)}, bf16[240,384]{1,0:T(8,128)(2,1)S(1)}, u32[]{:S(2)}, u32[]{:S(2)}) collective-permute-start(bf16[240,384]{1,0:T(8,128)(2,1)S(1)} %collective-permute-done.64.refs_9_.refs_6_), channel_id=1, source_target_pairs={{0,1},{1,0},{2,3},{3,2},{4,5},{5,4},{6,7},{7,6},{8,9},{9,8},{10,11... | collective-permute-start | bytes 552968 | tf_op jit(solution)/shard_map/ppermute | solution.py:33
  172.2 3.3 %shard_map.144 = (bf16[4,512,768]{2,1,0:T(8,128)(2,1)}, bf16[4,512,768]{2,1,0:T(8,128)(2,1)}, bf16[4,768,512]{2,1,0:T(8,128)(2,1)}, f32[8,128]{1,0:T(8,128)S(1)}) custom-call(s32[10]{0:T(128)S(1)} %stack.35.scal, bf16[320,512]{1,0:T(8,128)(2,1)S(1)} %get-tuple-element.110.in_ref, ...), custom_call_target="tpu_custom_call", output_to_operand_aliasing={{0}: (16, {}), {1}: (17, {}), {2}: (18, {})} | custom-call | flops 754974720 | bytes 4571136 | tf_op jit(solution)/shard_map/pallas_call | solution.py:508
  175.4 1.5 collective-permute-done.63.refs_6_.refs_3_
  176.9 3.2 %collective-permute-done.65.refs_8_.refs_5_ = bf16[240,384]{1,0:T(8,128)(2,1)S(1)} collective-permute-done((bf16[240,384]{1,0:T(8,128)(2,1)S(1)}, bf16[240,384]{1,0:T(8,128)(2,1)S(1)}, u32[]{:S(2)}, u32[]{:S(2)}) %collective-permute-start.65) | collective-permute-done | bytes 184352 | tf_op jit(solution)/shard_map/ppermute | solution.py:33
  180.1 3.3 %shard_map.145 = (bf16[2,2,128,512]{3,2,1,0:T(8,128)(2,1)S(1)}, bf16[2,2,128,512]{3,2,1,0:T(8,128)(2,1)S(1)}, f32[8,128]{1,0:T(8,128)}, f32[2,16,128]{2,1,0:T(8,128)S(1)}, f32[2,16,128]{2,1,0:T(8,128)S(1)}) custom-call(s32[10]{0:T(128)S(1)} %stack.35.scal, f32[8,128]{1,0:T(8,128)S(1)} %get-tuple-element.185.refs_0_, ...), custom_call_target="tpu_custom_call" | custom-call | flops 754974720 | bytes 4571136 | tf_op jit(solution)/shard_map/pallas_call | solution.py:484
  183.9 1.4 collective-permute-done.71
  185.5 1.7 collective-permute-start.72
  187.7 3.3 %shard_map.146 = (bf16[4,512,768]{2,1,0:T(8,128)(2,1)}, bf16[4,512,768]{2,1,0:T(8,128)(2,1)}, bf16[4,768,512]{2,1,0:T(8,128)(2,1)}, f32[8,128]{1,0:T(8,128)}) custom-call(s32[10]{0:T(128)S(1)} %stack.35.scal, bf16[320,512]{1,0:T(8,128)(2,1)S(1)} %get-tuple-element.194.in_ref, ...), custom_call_target="tpu_custom_call", output_to_operand_aliasing={{0}: (16, {}), {1}: (17, {}), {2}: (18, {})} | custom-call | flops 754974720 | bytes 4571136 | tf_op jit(solution)/shard_map/pallas_call | solution.py:508
  190.9 3.1 %collective-permute-done.74 = f32[16,128]{1,0:T(8,128)S(1)} collective-permute-done((f32[16,128]{1,0:T(8,128)S(1)}, f32[16,128]{1,0:T(8,128)S(1)}, u32[]{:S(2)}, u32[]{:S(2)}) %collective-permute-start.74) | collective-permute-done | bytes 8224 | tf_op jit(solution)/shard_map/ppermute | solution.py:33
  (157 shorter events, 10.9 us)
Async XLA Ops:
  1.7 9.7 %collective-permute-start = (bf16[272,512]{1,0:T(8,128)(2,1)S(1)}, bf16[272,512]{1,0:T(8,128)(2,1)S(1)}, u32[]{:S(2)}, u32[]{:S(2)}) collective-permute-start(bf16[272,512]{1,0:T(8,128)(2,1)S(1)} %shard_map.118.refs_0_.refs_1_), channel_id=1, source_target_pairs={{0,8},{4,12},{8,0},{12,4},{1,9},{5,13},{9,1},{13,5},{2,10},{6,14},... | collective-permute-start | bytes 835592 | tf_op jit(solution)/shard_map/ppermute | solution.py:33
  4.7 6.7 %collective-permute-start.1 = (bf16[272,512]{1,0:T(8,128)(2,1)S(1)}, bf16[272,512]{1,0:T(8,128)(2,1)S(1)}, u32[]{:S(2)}, u32[]{:S(2)}) collective-permute-start(bf16[272,512]{1,0:T(8,128)(2,1)S(1)} %shard_map.118.refs_0_.refs_1_), channel_id=1, source_target_pairs={{0,4},{4,0},{8,12},{12,8},{1,5},{5,1},{9,13},{13,9},{2,6},{6,2},{1... | collective-permute-start | bytes 835592 | tf_op jit(solution)/shard_map/ppermute | solution.py:33
  16.4 7.8 %collective-permute-start.3 = (bf16[240,384]{1,0:T(8,128)(2,1)S(1)}, bf16[240,384]{1,0:T(8,128)(2,1)S(1)}, u32[]{:S(2)}, u32[]{:S(2)}) collective-permute-start(bf16[240,384]{1,0:T(8,128)(2,1)S(1)} %get-tuple-element.107.refs_0_), channel_id=1, source_target_pairs={{0,1},{1,0},{2,3},{3,2},{4,5},{5,4},{6,7},{7,6},{8,9},{9,8},{10,11... | collective-permute-start | bytes 552968 | tf_op jit(solution)/shard_map/ppermute | solution.py:33
  18.3 9.6 %collective-permute-start.6 = (bf16[240,384]{1,0:T(8,128)(2,1)S(1)}, bf16[240,384]{1,0:T(8,128)(2,1)S(1)}, u32[]{:S(2)}, u32[]{:S(2)}) collective-permute-start(bf16[240,384]{1,0:T(8,128)(2,1)S(1)} %get-tuple-element.108), channel_id=1, source_target_pairs={{0,1},{1,0},{2,3},{3,2},{4,5},{5,4},{6,7},{7,6},{8,9},{9,8},{10,11... | collective-permute-start | bytes 552968 | tf_op jit(solution)/shard_map/ppermute | solution.py:33
  18.5 13.3 %collective-permute-start.32 = (bf16[240,384]{1,0:T(8,128)(2,1)S(1)}, bf16[240,384]{1,0:T(8,128)(2,1)S(1)}, u32[]{:S(2)}, u32[]{:S(2)}) collective-permute-start(bf16[240,384]{1,0:T(8,128)(2,1)S(1)} %get-tuple-element.131.refs_1_), channel_id=1, source_target_pairs={{0,1},{1,0},{2,3},{3,2},{4,5},{5,4},{6,7},{7,6},{8,9},{9,8},{10,11... | collective-permute-start | bytes 552968 | tf_op jit(solution)/shard_map/ppermute | solution.py:33
  20.3 14.8 %collective-permute-start.35 = (bf16[240,384]{1,0:T(8,128)(2,1)S(1)}, bf16[240,384]{1,0:T(8,128)(2,1)S(1)}, u32[]{:S(2)}, u32[]{:S(2)}) collective-permute-start(bf16[240,384]{1,0:T(8,128)(2,1)S(1)} %get-tuple-element.132), channel_id=1, source_target_pairs={{0,1},{1,0},{2,3},{3,2},{4,5},{5,4},{6,7},{7,6},{8,9},{9,8},{10,11... | collective-permute-start | bytes 552968 | tf_op jit(solution)/shard_map/ppermute | solution.py:33
  24.3 10.9 %collective-permute-start.4 = (bf16[240,384]{1,0:T(8,128)(2,1)S(1)}, bf16[240,384]{1,0:T(8,128)(2,1)S(1)}, u32[]{:S(2)}, u32[]{:S(2)}) collective-permute-start(bf16[240,384]{1,0:T(8,128)(2,1)S(1)} %shard_map.120), channel_id=1, source_target_pairs={{1,2},{2,1},{0,4},{3,7},{5,6},{6,5},{4,0},{7,3},{9,10},{10,9},{8,1... | collective-permute-start | bytes 552968 | tf_op jit(solution)/shard_map/ppermute | solution.py:533
  28.0 12.6 %collective-permute-start.7 = (bf16[240,384]{1,0:T(8,128)(2,1)S(1)}, bf16[240,384]{1,0:T(8,128)(2,1)S(1)}, u32[]{:S(2)}, u32[]{:S(2)}) collective-permute-start(bf16[240,384]{1,0:T(8,128)(2,1)S(1)} %fusion.9), channel_id=1, source_target_pairs={{1,2},{2,1},{0,4},{3,7},{5,6},{6,5},{4,0},{7,3},{9,10},{10,9},{8,1... | collective-permute-start | bytes 552968 | tf_op jit(solution)/shard_map/ppermute | solution.py:533
  31.9 6.8 %collective-permute-start.33 = (bf16[240,384]{1,0:T(8,128)(2,1)S(1)}, bf16[240,384]{1,0:T(8,128)(2,1)S(1)}, u32[]{:S(2)}, u32[]{:S(2)}) collective-permute-start(bf16[240,384]{1,0:T(8,128)(2,1)S(1)} %shard_map.130), channel_id=1, source_target_pairs={{1,2},{2,1},{0,4},{3,7},{5,6},{6,5},{4,0},{7,3},{9,10},{10,9},{8,1... | collective-permute-start | bytes 552968 | tf_op jit(solution)/shard_map/ppermute | solution.py:533
  35.2 11.7 %collective-permute-start.36 = (bf16[240,384]{1,0:T(8,128)(2,1)S(1)}, bf16[240,384]{1,0:T(8,128)(2,1)S(1)}, u32[]{:S(2)}, u32[]{:S(2)}) collective-permute-start(bf16[240,384]{1,0:T(8,128)(2,1)S(1)} %fusion.13), channel_id=1, source_target_pairs={{1,2},{2,1},{0,4},{3,7},{5,6},{6,5},{4,0},{7,3},{9,10},{10,9},{8,1... | collective-permute-start | bytes 552968 | tf_op jit(solution)/shard_map/ppermute | solution.py:533
  35.3 8.9 %collective-permute-start.5 = (bf16[240,384]{1,0:T(8,128)(2,1)S(1)}, bf16[240,384]{1,0:T(8,128)(2,1)S(1)}, u32[]{:S(2)}, u32[]{:S(2)}) collective-permute-start(bf16[240,384]{1,0:T(8,128)(2,1)S(1)} %fusion.1), channel_id=1, source_target_pairs={{0,1},{1,0},{2,3},{3,2},{4,5},{5,4},{6,7},{7,6},{8,9},{9,8},{10,11... | collective-permute-start | bytes 552968 | tf_op jit(solution)/shard_map/ppermute | solution.py:33
  38.8 8.1 %collective-permute-start.34 = (bf16[240,384]{1,0:T(8,128)(2,1)S(1)}, bf16[240,384]{1,0:T(8,128)(2,1)S(1)}, u32[]{:S(2)}, u32[]{:S(2)}) collective-permute-start(bf16[240,384]{1,0:T(8,128)(2,1)S(1)} %fusion.5), channel_id=1, source_target_pairs={{0,1},{1,0},{2,3},{3,2},{4,5},{5,4},{6,7},{7,6},{8,9},{9,8},{10,11... | collective-permute-start | bytes 552968 | tf_op jit(solution)/shard_map/ppermute | solution.py:33
  44.5 7.9 %collective-permute-start.12 = (bf16[240,384]{1,0:T(8,128)(2,1)S(1)}, bf16[240,384]{1,0:T(8,128)(2,1)S(1)}, u32[]{:S(2)}, u32[]{:S(2)}) collective-permute-start(bf16[240,384]{1,0:T(8,128)(2,1)S(1)} %get-tuple-element.109.refs_7_), channel_id=1, source_target_pairs={{0,1},{1,0},{2,3},{3,2},{4,5},{5,4},{6,7},{7,6},{8,9},{9,8},{10,11... | collective-permute-start | bytes 552968 | tf_op jit(solution)/shard_map/ppermute | solution.py:33
  47.0 10.2 %collective-permute-start.37 = (bf16[240,384]{1,0:T(8,128)(2,1)S(1)}, bf16[240,384]{1,0:T(8,128)(2,1)S(1)}, u32[]{:S(2)}, u32[]{:S(2)}) collective-permute-start(bf16[240,384]{1,0:T(8,128)(2,1)S(1)} %get-tuple-element.136.refs_1_), channel_id=1, source_target_pairs={{0,1},{1,0},{2,3},{3,2},{4,5},{5,4},{6,7},{7,6},{8,9},{9,8},{10,11... | collective-permute-start | bytes 552968 | tf_op jit(solution)/shard_map/ppermute | solution.py:33
  48.8 12.2 %collective-permute-start.9 = (bf16[240,384]{1,0:T(8,128)(2,1)S(1)}, bf16[240,384]{1,0:T(8,128)(2,1)S(1)}, u32[]{:S(2)}, u32[]{:S(2)}) collective-permute-start(bf16[240,384]{1,0:T(8,128)(2,1)S(1)} %broadcast_select_fusion.11), channel_id=1, source_target_pairs={{0,1},{1,0},{2,3},{3,2},{4,5},{5,4},{6,7},{7,6},{8,9},{9,8},{10,11... | collective-permute-start | bytes 552968 | tf_op jit(solution)/shard_map/ppermute | solution.py:33
  52.3 9.3 %collective-permute-start.13 = (bf16[240,384]{1,0:T(8,128)(2,1)S(1)}, bf16[240,384]{1,0:T(8,128)(2,1)S(1)}, u32[]{:S(2)}, u32[]{:S(2)}) collective-permute-start(bf16[240,384]{1,0:T(8,128)(2,1)S(1)} %collective-permute-done.12.refs_8_), channel_id=1, source_target_pairs={{1,2},{2,1},{0,4},{3,7},{5,6},{6,5},{4,0},{7,3},{9,10},{10,9},{8,1... | collective-permute-start | bytes 552968 | tf_op jit(solution)/shard_map/ppermute | solution.py:533
  52.4 13.2 %collective-permute-start.39 = (bf16[240,384]{1,0:T(8,128)(2,1)S(1)}, bf16[240,384]{1,0:T(8,128)(2,1)S(1)}, u32[]{:S(2)}, u32[]{:S(2)}) collective-permute-start(bf16[240,384]{1,0:T(8,128)(2,1)S(1)} %broadcast_select_fusion.5), channel_id=1, source_target_pairs={{0,1},{1,0},{2,3},{3,2},{4,5},{5,4},{6,7},{7,6},{8,9},{9,8},{10,11... | collective-permute-start | bytes 552968 | tf_op jit(solution)/shard_map/ppermute | solution.py:33
  57.3 7.1 %collective-permute-start.40 = (bf16[240,384]{1,0:T(8,128)(2,1)S(1)}, bf16[240,384]{1,0:T(8,128)(2,1)S(1)}, u32[]{:S(2)}, u32[]{:S(2)}) collective-permute-start(bf16[240,384]{1,0:T(8,128)(2,1)S(1)} %collective-permute-done.37.refs_2_), channel_id=1, source_target_pairs={{1,2},{2,1},{0,4},{3,7},{5,6},{6,5},{4,0},{7,3},{9,10},{10,9},{8,1... | collective-permute-start | bytes 552968 | tf_op jit(solution)/shard_map/ppermute | solution.py:533
  61.7 9.0 %collective-permute-start.14 = (bf16[240,384]{1,0:T(8,128)(2,1)S(1)}, bf16[240,384]{1,0:T(8,128)(2,1)S(1)}, u32[]{:S(2)}, u32[]{:S(2)}) collective-permute-start(bf16[240,384]{1,0:T(8,128)(2,1)S(1)} %broadcast_select_fusion.10), channel_id=1, source_target_pairs={{0,1},{1,0},{2,3},{3,2},{4,5},{5,4},{6,7},{7,6},{8,9},{9,8},{10,11... | collective-permute-start | bytes 552968 | tf_op jit(solution)/shard_map/ppermute | solution.py:33
  64.4 9.8 %collective-permute-start.41 = (bf16[240,384]{1,0:T(8,128)(2,1)S(1)}, bf16[240,384]{1,0:T(8,128)(2,1)S(1)}, u32[]{:S(2)}, u32[]{:S(2)}) collective-permute-start(bf16[240,384]{1,0:T(8,128)(2,1)S(1)} %broadcast_select_fusion.4), channel_id=1, source_target_pairs={{0,1},{1,0},{2,3},{3,2},{4,5},{5,4},{6,7},{7,6},{8,9},{9,8},{10,11... | collective-permute-start | bytes 552968 | tf_op jit(solution)/shard_map/ppermute | solution.py:33
  65.8 12.1 %collective-permute-start.11 = (bf16[240,384]{1,0:T(8,128)(2,1)S(1)}, bf16[240,384]{1,0:T(8,128)(2,1)S(1)}, u32[]{:S(2)}, u32[]{:S(2)}) collective-permute-start(bf16[240,384]{1,0:T(8,128)(2,1)S(1)} %fusion.2), channel_id=1, source_target_pairs={{0,1},{1,0},{2,3},{3,2},{4,5},{5,4},{6,7},{7,6},{8,9},{9,8},{10,11... | collective-permute-start | bytes 552968 | tf_op jit(solution)/shard_map/ppermute | solution.py:33
  70.8 7.1 %collective-permute-start.15 = (bf16[240,384]{1,0:T(8,128)(2,1)S(1)}, bf16[240,384]{1,0:T(8,128)(2,1)S(1)}, u32[]{:S(2)}, u32[]{:S(2)}) collective-permute-start(bf16[240,384]{1,0:T(8,128)(2,1)S(1)} %fusion.10), channel_id=1, source_target_pairs={{1,2},{2,1},{0,4},{3,7},{5,6},{6,5},{4,0},{7,3},{9,10},{10,9},{8,1... | collective-permute-start | bytes 552968 | tf_op jit(solution)/shard_map/ppermute | solution.py:533
  70.9 12.6 %collective-permute-start.43 = (bf16[240,384]{1,0:T(8,128)(2,1)S(1)}, bf16[240,384]{1,0:T(8,128)(2,1)S(1)}, u32[]{:S(2)}, u32[]{:S(2)}) collective-permute-start(bf16[240,384]{1,0:T(8,128)(2,1)S(1)} %fusion.6), channel_id=1, source_target_pairs={{0,1},{1,0},{2,3},{3,2},{4,5},{5,4},{6,7},{7,6},{8,9},{9,8},{10,11... | collective-permute-start | bytes 552968 | tf_op jit(solution)/shard_map/ppermute | solution.py:33
  74.3 9.2 %collective-permute-start.44 = (bf16[240,384]{1,0:T(8,128)(2,1)S(1)}, bf16[240,384]{1,0:T(8,128)(2,1)S(1)}, u32[]{:S(2)}, u32[]{:S(2)}) collective-permute-start(bf16[240,384]{1,0:T(8,128)(2,1)S(1)} %fusion.14), channel_id=1, source_target_pairs={{1,2},{2,1},{0,4},{3,7},{5,6},{6,5},{4,0},{7,3},{9,10},{10,9},{8,1... | collective-permute-start | bytes 552968 | tf_op jit(solution)/shard_map/ppermute | solution.py:533
  78.0 9.3 %collective-permute-start.16 = (bf16[240,384]{1,0:T(8,128)(2,1)S(1)}, bf16[240,384]{1,0:T(8,128)(2,1)S(1)}, u32[]{:S(2)}, u32[]{:S(2)}) collective-permute-start(bf16[240,384]{1,0:T(8,128)(2,1)S(1)} %get-tuple-element.117.refs_9_.refs_0_.refs_7_), channel_id=1, source_target_pairs={{1,2},{2,1},{0,4},{3,7},{5,6},{6,5},{4,0},{7,3},{9,10},{10,9},{8,1... | collective-permute-start | bytes 552968 | tf_op jit(solution)/shard_map/ppermute | solution.py:533
  80.3 9.0 %collective-permute-start.20 = (bf16[240,384]{1,0:T(8,128)(2,1)S(1)}, bf16[240,384]{1,0:T(8,128)(2,1)S(1)}, u32[]{:S(2)}, u32[]{:S(2)}) collective-permute-start(bf16[240,384]{1,0:T(8,128)(2,1)S(1)} %get-tuple-element.117.refs_9_.refs_0_.refs_7_), channel_id=1, source_target_pairs={{0,1},{1,0},{2,3},{3,2},{4,5},{5,4},{6,7},{7,6},{8,9},{9,8},{10,11... | collective-permute-start | bytes 552968 | tf_op jit(solution)/shard_map/ppermute | solution.py:33
  83.7 8.6 %collective-permute-start.45 = (bf16[240,384]{1,0:T(8,128)(2,1)S(1)}, bf16[240,384]{1,0:T(8,128)(2,1)S(1)}, u32[]{:S(2)}, u32[]{:S(2)}) collective-permute-start(bf16[240,384]{1,0:T(8,128)(2,1)S(1)} %get-tuple-element.149.refs_3_.refs_1_), channel_id=1, source_target_pairs={{0,1},{1,0},{2,3},{3,2},{4,5},{5,4},{6,7},{7,6},{8,9},{9,8},{10,11... | collective-permute-start | bytes 552968 | tf_op jit(solution)/shard_map/ppermute | solution.py:33
  83.8 5.5 %collective-permute-start.46 = (bf16[240,384]{1,0:T(8,128)(2,1)S(1)}, bf16[240,384]{1,0:T(8,128)(2,1)S(1)}, u32[]{:S(2)}, u32[]{:S(2)}) collective-permute-start(bf16[240,384]{1,0:T(8,128)(2,1)S(1)} %get-tuple-element.149.refs_3_.refs_1_), channel_id=1, source_target_pairs={{1,2},{2,1},{0,4},{3,7},{5,6},{6,5},{4,0},{7,3},{9,10},{10,9},{8,1... | collective-permute-start | bytes 552968 | tf_op jit(solution)/shard_map/ppermute | solution.py:533
  87.4 8.8 %collective-permute-start.17 = (bf16[240,384]{1,0:T(8,128)(2,1)S(1)}, bf16[240,384]{1,0:T(8,128)(2,1)S(1)}, u32[]{:S(2)}, u32[]{:S(2)}) collective-permute-start(bf16[240,384]{1,0:T(8,128)(2,1)S(1)} %broadcast_select_fusion.9), channel_id=1, source_target_pairs={{0,1},{1,0},{2,3},{3,2},{4,5},{5,4},{6,7},{7,6},{8,9},{9,8},{10,11... | collective-permute-start | bytes 552968 | tf_op jit(solution)/shard_map/ppermute | solution.py:33
  89.3 7.3 %collective-permute-start.21 = (bf16[240,384]{1,0:T(8,128)(2,1)S(1)}, bf16[240,384]{1,0:T(8,128)(2,1)S(1)}, u32[]{:S(2)}, u32[]{:S(2)}) collective-permute-start(bf16[240,384]{1,0:T(8,128)(2,1)S(1)} %collective-permute-done.20.refs_10_.refs_8_), channel_id=1, source_target_pairs={{1,2},{2,1},{0,4},{3,7},{5,6},{6,5},{4,0},{7,3},{9,10},{10,9},{8,1... | collective-permute-start | bytes 552968 | tf_op jit(solution)/shard_map/ppermute | solution.py:533
  89.3 10.9 %collective-permute-start.47 = (bf16[240,384]{1,0:T(8,128)(2,1)S(1)}, bf16[240,384]{1,0:T(8,128)(2,1)S(1)}, u32[]{:S(2)}, u32[]{:S(2)}) collective-permute-start(bf16[240,384]{1,0:T(8,128)(2,1)S(1)} %broadcast_select_fusion.3), channel_id=1, source_target_pairs={{0,1},{1,0},{2,3},{3,2},{4,5},{5,4},{6,7},{7,6},{8,9},{9,8},{10,11... | collective-permute-start | bytes 552968 | tf_op jit(solution)/shard_map/ppermute | solution.py:33
  92.2 6.7 %collective-permute-start.48 = (bf16[240,384]{1,0:T(8,128)(2,1)S(1)}, bf16[240,384]{1,0:T(8,128)(2,1)S(1)}, u32[]{:S(2)}, u32[]{:S(2)}) collective-permute-start(bf16[240,384]{1,0:T(8,128)(2,1)S(1)} %collective-permute-done.45.refs_4_.refs_2_), channel_id=1, source_target_pairs={{1,2},{2,1},{0,4},{3,7},{5,6},{6,5},{4,0},{7,3},{9,10},{10,9},{8,1... | collective-permute-start | bytes 552968 | tf_op jit(solution)/shard_map/ppermute | solution.py:533
  96.6 9.4 %collective-permute-start.22 = (bf16[240,384]{1,0:T(8,128)(2,1)S(1)}, bf16[240,384]{1,0:T(8,128)(2,1)S(1)}, u32[]{:S(2)}, u32[]{:S(2)}) collective-permute-start(bf16[240,384]{1,0:T(8,128)(2,1)S(1)} %broadcast_select_fusion.8), channel_id=1, source_target_pairs={{0,1},{1,0},{2,3},{3,2},{4,5},{5,4},{6,7},{7,6},{8,9},{9,8},{10,11... | collective-permute-start | bytes 552968 | tf_op jit(solution)/shard_map/ppermute | solution.py:33
  99.0 11.0 %collective-permute-start.49 = (bf16[240,384]{1,0:T(8,128)(2,1)S(1)}, bf16[240,384]{1,0:T(8,128)(2,1)S(1)}, u32[]{:S(2)}, u32[]{:S(2)}) collective-permute-start(bf16[240,384]{1,0:T(8,128)(2,1)S(1)} %broadcast_select_fusion.2), channel_id=1, source_target_pairs={{0,1},{1,0},{2,3},{3,2},{4,5},{5,4},{6,7},{7,6},{8,9},{9,8},{10,11... | collective-permute-start | bytes 552968 | tf_op jit(solution)/shard_map/ppermute | solution.py:33
  100.3 5.9 %collective-permute-start.50 = (bf16[240,384]{1,0:T(8,128)(2,1)S(1)}, bf16[240,384]{1,0:T(8,128)(2,1)S(1)}, u32[]{:S(2)}, u32[]{:S(2)}) collective-permute-start(bf16[240,384]{1,0:T(8,128)(2,1)S(1)} %shard_map.137), channel_id=1, source_target_pairs={{1,2},{2,1},{0,4},{3,7},{5,6},{6,5},{4,0},{7,3},{9,10},{10,9},{8,1... | collective-permute-start | bytes 552968 | tf_op jit(solution)/shard_map/ppermute | solution.py:533
  100.5 11.9 %collective-permute-start.19 = (bf16[240,384]{1,0:T(8,128)(2,1)S(1)}, bf16[240,384]{1,0:T(8,128)(2,1)S(1)}, u32[]{:S(2)}, u32[]{:S(2)}) collective-permute-start(bf16[240,384]{1,0:T(8,128)(2,1)S(1)} %fusion.3), channel_id=1, source_target_pairs={{0,1},{1,0},{2,3},{3,2},{4,5},{5,4},{6,7},{7,6},{8,9},{9,8},{10,11... | collective-permute-start | bytes 552968 | tf_op jit(solution)/shard_map/ppermute | solution.py:33
  106.1 6.3 %collective-permute-start.23 = (bf16[240,384]{1,0:T(8,128)(2,1)S(1)}, bf16[240,384]{1,0:T(8,128)(2,1)S(1)}, u32[]{:S(2)}, u32[]{:S(2)}) collective-permute-start(bf16[240,384]{1,0:T(8,128)(2,1)S(1)} %fusion.11), channel_id=1, source_target_pairs={{1,2},{2,1},{0,4},{3,7},{5,6},{6,5},{4,0},{7,3},{9,10},{10,9},{8,1... | collective-permute-start | bytes 552968 | tf_op jit(solution)/shard_map/ppermute | solution.py:533
  106.3 11.8 %collective-permute-start.51 = (bf16[240,384]{1,0:T(8,128)(2,1)S(1)}, bf16[240,384]{1,0:T(8,128)(2,1)S(1)}, u32[]{:S(2)}, u32[]{:S(2)}) collective-permute-start(bf16[240,384]{1,0:T(8,128)(2,1)S(1)} %fusion.7), channel_id=1, source_target_pairs={{0,1},{1,0},{2,3},{3,2},{4,5},{5,4},{6,7},{7,6},{8,9},{9,8},{10,11... | collective-permute-start | bytes 552968 | tf_op jit(solution)/shard_map/ppermute | solution.py:33
  110.0 8.0 %collective-permute-start.52 = (bf16[240,384]{1,0:T(8,128)(2,1)S(1)}, bf16[240,384]{1,0:T(8,128)(2,1)S(1)}, u32[]{:S(2)}, u32[]{:S(2)}) collective-permute-start(bf16[240,384]{1,0:T(8,128)(2,1)S(1)} %fusion.15), channel_id=1, source_target_pairs={{1,2},{2,1},{0,4},{3,7},{5,6},{6,5},{4,0},{7,3},{9,10},{10,9},{8,1... | collective-permute-start | bytes 552968 | tf_op jit(solution)/shard_map/ppermute | solution.py:533
  112.5 9.2 %collective-permute-start.24 = (bf16[240,384]{1,0:T(8,128)(2,1)S(1)}, bf16[240,384]{1,0:T(8,128)(2,1)S(1)}, u32[]{:S(2)}, u32[]{:S(2)}) collective-permute-start(bf16[240,384]{1,0:T(8,128)(2,1)S(1)} %get-tuple-element.126.refs_9_.refs_0_.refs_7_), channel_id=1, source_target_pairs={{1,2},{2,1},{0,4},{3,7},{5,6},{6,5},{4,0},{7,3},{9,10},{10,9},{8,1... | collective-permute-start | bytes 552968 | tf_op jit(solution)/shard_map/ppermute | solution.py:533
  114.8 8.9 %collective-permute-start.28 = (bf16[240,384]{1,0:T(8,128)(2,1)S(1)}, bf16[240,384]{1,0:T(8,128)(2,1)S(1)}, u32[]{:S(2)}, u32[]{:S(2)}) collective-permute-start(bf16[240,384]{1,0:T(8,128)(2,1)S(1)} %get-tuple-element.126.refs_9_.refs_0_.refs_7_), channel_id=1, source_target_pairs={{0,1},{1,0},{2,3},{3,2},{4,5},{5,4},{6,7},{7,6},{8,9},{9,8},{10,11... | collective-permute-start | bytes 552968 | tf_op jit(solution)/shard_map/ppermute | solution.py:33
  118.2 8.5 %collective-permute-start.53 = (bf16[240,384]{1,0:T(8,128)(2,1)S(1)}, bf16[240,384]{1,0:T(8,128)(2,1)S(1)}, u32[]{:S(2)}, u32[]{:S(2)}) collective-permute-start(bf16[240,384]{1,0:T(8,128)(2,1)S(1)} %get-tuple-element.165.refs_3_.refs_1_), channel_id=1, source_target_pairs={{0,1},{1,0},{2,3},{3,2},{4,5},{5,4},{6,7},{7,6},{8,9},{9,8},{10,11... | collective-permute-start | bytes 552968 | tf_op jit(solution)/shard_map/ppermute | solution.py:33
  118.3 5.4 %collective-permute-start.54 = (bf16[240,384]{1,0:T(8,128)(2,1)S(1)}, bf16[240,384]{1,0:T(8,128)(2,1)S(1)}, u32[]{:S(2)}, u32[]{:S(2)}) collective-permute-start(bf16[240,384]{1,0:T(8,128)(2,1)S(1)} %get-tuple-element.165.refs_3_.refs_1_), channel_id=1, source_target_pairs={{1,2},{2,1},{0,4},{3,7},{5,6},{6,5},{4,0},{7,3},{9,10},{10,9},{8,1... | collective-permute-start | bytes 552968 | tf_op jit(solution)/shard_map/ppermute | solution.py:533
  121.7 9.0 %collective-permute-start.25 = (bf16[240,384]{1,0:T(8,128)(2,1)S(1)}, bf16[240,384]{1,0:T(8,128)(2,1)S(1)}, u32[]{:S(2)}, u32[]{:S(2)}) collective-permute-start(bf16[240,384]{1,0:T(8,128)(2,1)S(1)} %broadcast_select_fusion.7), channel_id=1, source_target_pairs={{0,1},{1,0},{2,3},{3,2},{4,5},{5,4},{6,7},{7,6},{8,9},{9,8},{10,11... | collective-permute-start | bytes 552968 | tf_op jit(solution)/shard_map/ppermute | solution.py:33
  123.7 7.1 %collective-permute-start.29 = (bf16[240,384]{1,0:T(8,128)(2,1)S(1)}, bf16[240,384]{1,0:T(8,128)(2,1)S(1)}, u32[]{:S(2)}, u32[]{:S(2)}) collective-permute-start(bf16[240,384]{1,0:T(8,128)(2,1)S(1)} %collective-permute-done.28.refs_10_.refs_8_), channel_id=1, source_target_pairs={{1,2},{2,1},{0,4},{3,7},{5,6},{6,5},{4,0},{7,3},{9,10},{10,9},{8,1... | collective-permute-start | bytes 552968 | tf_op jit(solution)/shard_map/ppermute | solution.py:533
  123.8 12.0 %collective-permute-start.55 = (bf16[240,384]{1,0:T(8,128)(2,1)S(1)}, bf16[240,384]{1,0:T(8,128)(2,1)S(1)}, u32[]{:S(2)}, u32[]{:S(2)}) collective-permute-start(bf16[240,384]{1,0:T(8,128)(2,1)S(1)} %broadcast_select_fusion.1), channel_id=1, source_target_pairs={{0,1},{1,0},{2,3},{3,2},{4,5},{5,4},{6,7},{7,6},{8,9},{9,8},{10,11... | collective-permute-start | bytes 552968 | tf_op jit(solution)/shard_map/ppermute | solution.py:33
  126.8 6.7 %collective-permute-start.56 = (bf16[240,384]{1,0:T(8,128)(2,1)S(1)}, bf16[240,384]{1,0:T(8,128)(2,1)S(1)}, u32[]{:S(2)}, u32[]{:S(2)}) collective-permute-start(bf16[240,384]{1,0:T(8,128)(2,1)S(1)} %collective-permute-done.53.refs_4_.refs_2_), channel_id=1, source_target_pairs={{1,2},{2,1},{0,4},{3,7},{5,6},{6,5},{4,0},{7,3},{9,10},{10,9},{8,1... | collective-permute-start | bytes 552968 | tf_op jit(solution)/shard_map/ppermute | solution.py:533
  130.9 12.2 %collective-permute-start.30 = (bf16[240,384]{1,0:T(8,128)(2,1)S(1)}, bf16[240,384]{1,0:T(8,128)(2,1)S(1)}, u32[]{:S(2)}, u32[]{:S(2)}) collective-permute-start(bf16[240,384]{1,0:T(8,128)(2,1)S(1)} %broadcast_select_fusion.6), channel_id=1, source_target_pairs={{0,1},{1,0},{2,3},{3,2},{4,5},{5,4},{6,7},{7,6},{8,9},{9,8},{10,11... | collective-permute-start | bytes 552968 | tf_op jit(solution)/shard_map/ppermute | solution.py:33
  133.5 9.4 %collective-permute-start.57 = (bf16[240,384]{1,0:T(8,128)(2,1)S(1)}, bf16[240,384]{1,0:T(8,128)(2,1)S(1)}, u32[]{:S(2)}, u32[]{:S(2)}) collective-permute-start(bf16[240,384]{1,0:T(8,128)(2,1)S(1)} %broadcast_select_fusion), channel_id=1, source_target_pairs={{0,1},{1,0},{2,3},{3,2},{4,5},{5,4},{6,7},{7,6},{8,9},{9,8},{10,11... | collective-permute-start | bytes 552968 | tf_op jit(solution)/shard_map/ppermute | solution.py:33
  135.9 14.1 %collective-permute-start.27 = (bf16[240,384]{1,0:T(8,128)(2,1)S(1)}, bf16[240,384]{1,0:T(8,128)(2,1)S(1)}, u32[]{:S(2)}, u32[]{:S(2)}) collective-permute-start(bf16[240,384]{1,0:T(8,128)(2,1)S(1)} %fusion.4), channel_id=1, source_target_pairs={{0,1},{1,0},{2,3},{3,2},{4,5},{5,4},{6,7},{7,6},{8,9},{9,8},{10,11... | collective-permute-start | bytes 552968 | tf_op jit(solution)/shard_map/ppermute | solution.py:33
  139.8 10.1 %collective-permute-start.59 = (bf16[240,384]{1,0:T(8,128)(2,1)S(1)}, bf16[240,384]{1,0:T(8,128)(2,1)S(1)}, u32[]{:S(2)}, u32[]{:S(2)}) collective-permute-start(bf16[240,384]{1,0:T(8,128)(2,1)S(1)} %fusion.8), channel_id=1, source_target_pairs={{0,1},{1,0},{2,3},{3,2},{4,5},{5,4},{6,7},{7,6},{8,9},{9,8},{10,11... | collective-permute-start | bytes 552968 | tf_op jit(solution)/shard_map/ppermute | solution.py:33
  143.0 6.8 %collective-permute-start.60 = (bf16[240,384]{1,0:T(8,128)(2,1)S(1)}, bf16[240,384]{1,0:T(8,128)(2,1)S(1)}, u32[]{:S(2)}, u32[]{:S(2)}) collective-permute-start(bf16[240,384]{1,0:T(8,128)(2,1)S(1)} %fusion.16), channel_id=1, source_target_pairs={{1,2},{2,1},{0,4},{3,7},{5,6},{6,5},{4,0},{7,3},{9,10},{10,9},{8,1... | collective-permute-start | bytes 552968 | tf_op jit(solution)/shard_map/ppermute | solution.py:533
  143.2 6.8 %collective-permute-start.31 = (bf16[240,384]{1,0:T(8,128)(2,1)S(1)}, bf16[240,384]{1,0:T(8,128)(2,1)S(1)}, u32[]{:S(2)}, u32[]{:S(2)}) collective-permute-start(bf16[240,384]{1,0:T(8,128)(2,1)S(1)} %fusion.12), channel_id=1, source_target_pairs={{1,2},{2,1},{0,4},{3,7},{5,6},{6,5},{4,0},{7,3},{9,10},{10,9},{8,1... | collective-permute-start | bytes 552968 | tf_op jit(solution)/shard_map/ppermute | solution.py:533
  150.8 7.9 %collective-permute-start.66 = (bf16[256,384]{1,0:T(8,128)(2,1)S(1)}, bf16[256,384]{1,0:T(8,128)(2,1)S(1)}, u32[]{:S(2)}, u32[]{:S(2)}) collective-permute-start(bf16[256,384]{1,0:T(8,128)(2,1)S(1)} %get-tuple-element.181.refs_0_.refs_10_.refs_7_), channel_id=1, source_target_pairs={{0,1},{1,0},{2,3},{3,2},{4,5},{5,4},{6,7},{7,6},{8,9},{9,8},{10,11... | collective-permute-start | bytes 589832 | tf_op jit(solution)/shard_map/ppermute | solution.py:33
  152.9 7.7 %collective-permute-start.61 = (bf16[240,384]{1,0:T(8,128)(2,1)S(1)}, bf16[240,384]{1,0:T(8,128)(2,1)S(1)}, u32[]{:S(2)}, u32[]{:S(2)}) collective-permute-start(bf16[240,384]{1,0:T(8,128)(2,1)S(1)} %get-tuple-element.188.refs_4_.refs_1_), channel_id=1, source_target_pairs={{0,1},{1,0},{2,3},{3,2},{4,5},{5,4},{6,7},{7,6},{8,9},{9,8},{10,11... | collective-permute-start | bytes 552968 | tf_op jit(solution)/shard_map/ppermute | solution.py:33
  153.0 7.7 %collective-permute-start.67 = (bf16[256,384]{1,0:T(8,128)(2,1)S(1)}, bf16[256,384]{1,0:T(8,128)(2,1)S(1)}, u32[]{:S(2)}, u32[]{:S(2)}) collective-permute-start(bf16[256,384]{1,0:T(8,128)(2,1)S(1)} %get-tuple-element.181.refs_0_.refs_10_.refs_7_), channel_id=1, source_target_pairs={{1,2},{2,1},{0,4},{3,7},{5,6},{6,5},{4,0},{7,3},{9,10},{10,9},{8,1... | collective-permute-start | bytes 589832 | tf_op jit(solution)/shard_map/ppermute | solution.py:533
  158.7 8.2 %collective-permute-start.62 = (bf16[240,384]{1,0:T(8,128)(2,1)S(1)}, bf16[240,384]{1,0:T(8,128)(2,1)S(1)}, u32[]{:S(2)}, u32[]{:S(2)}) collective-permute-start(bf16[240,384]{1,0:T(8,128)(2,1)S(1)} %get-tuple-element.188.refs_4_.refs_1_), channel_id=1, source_target_pairs={{1,2},{2,1},{0,4},{3,7},{5,6},{6,5},{4,0},{7,3},{9,10},{10,9},{8,1... | collective-permute-start | bytes 552968 | tf_op jit(solution)/shard_map/ppermute | solution.py:533
  160.7 9.5 %collective-permute-start.64 = (bf16[240,384]{1,0:T(8,128)(2,1)S(1)}, bf16[240,384]{1,0:T(8,128)(2,1)S(1)}, u32[]{:S(2)}, u32[]{:S(2)}) collective-permute-start(bf16[240,384]{1,0:T(8,128)(2,1)S(1)} %collective-permute-done.61.refs_5_.refs_2_), channel_id=1, source_target_pairs={{1,2},{2,1},{0,4},{3,7},{5,6},{6,5},{4,0},{7,3},{9,10},{10,9},{8,1... | collective-permute-start | bytes 552968 | tf_op jit(solution)/shard_map/ppermute | solution.py:533
  160.7 16.2 %collective-permute-start.68 = (bf16[256,384]{1,0:T(8,128)(2,1)S(1)}, bf16[256,384]{1,0:T(8,128)(2,1)S(1)}, u32[]{:S(2)}, u32[]{:S(2)}) collective-permute-start(bf16[256,384]{1,0:T(8,128)(2,1)S(1)} %collective-permute-done.67.refs_13_.refs_10_), channel_id=1, source_target_pairs={{0,1},{1,0},{2,3},{3,2},{4,5},{5,4},{6,7},{7,6},{8,9},{9,8},{10,11... | collective-permute-start | bytes 589832 | tf_op jit(solution)/shard_map/ppermute | solution.py:33
  163.0 17.1 %collective-permute-start.70 = (bf16[256,384]{1,0:T(8,128)(2,1)S(1)}, bf16[256,384]{1,0:T(8,128)(2,1)S(1)}, u32[]{:S(2)}, u32[]{:S(2)}) collective-permute-start(bf16[256,384]{1,0:T(8,128)(2,1)S(1)} %collective-permute-done.69.refs_15_.refs_12_), channel_id=1, source_target_pairs={{0,1},{1,0},{2,3},{3,2},{4,5},{5,4},{6,7},{7,6},{8,9},{9,8},{10,11... | collective-permute-start | bytes 589832 | tf_op jit(solution)/shard_map/ppermute | solution.py:33
  166.9 10.0 %collective-permute-start.63 = (bf16[240,384]{1,0:T(8,128)(2,1)S(1)}, bf16[240,384]{1,0:T(8,128)(2,1)S(1)}, u32[]{:S(2)}, u32[]{:S(2)}) collective-permute-start(bf16[240,384]{1,0:T(8,128)(2,1)S(1)} %collective-permute-done.62.refs_7_.refs_4_), channel_id=1, source_target_pairs={{0,1},{1,0},{2,3},{3,2},{4,5},{5,4},{6,7},{7,6},{8,9},{9,8},{10,11... | collective-permute-start | bytes 552968 | tf_op jit(solution)/shard_map/ppermute | solution.py:33
  170.2 9.9 %collective-permute-start.65 = (bf16[240,384]{1,0:T(8,128)(2,1)S(1)}, bf16[240,384]{1,0:T(8,128)(2,1)S(1)}, u32[]{:S(2)}, u32[]{:S(2)}) collective-permute-start(bf16[240,384]{1,0:T(8,128)(2,1)S(1)} %collective-permute-done.64.refs_9_.refs_6_), channel_id=1, source_target_pairs={{0,1},{1,0},{2,3},{3,2},{4,5},{5,4},{6,7},{7,6},{8,9},{9,8},{10,11... | collective-permute-start | bytes 552968 | tf_op jit(solution)/shard_map/ppermute | solution.py:33
  185.5 9.2 %collective-permute-start.72 = (bf16[2,128,512]{2,1,0:T(8,128)(2,1)S(1)}, bf16[2,128,512]{2,1,0:T(8,128)(2,1)S(1)}, u32[]{:S(2)}, u32[]{:S(2)}) collective-permute-start(bf16[2,128,512]{2,1,0:T(8,128)(2,1)S(1)} %slice_bitcast_fusion), channel_id=1, source_target_pairs={{0,8},{4,12},{8,0},{12,4},{1,9},{5,13},{9,1},{13,5},{2,10},{6,14},... | collective-permute-start | bytes 786440 | tf_op jit(solution)/shard_map/ppermute | solution.py:33
  187.2 6.8 %collective-permute-start.74 = (f32[16,128]{1,0:T(8,128)S(1)}, f32[16,128]{1,0:T(8,128)S(1)}, u32[]{:S(2)}, u32[]{:S(2)}) collective-permute-start(f32[16,128]{1,0:T(8,128)S(1)} %slice_bitcast_fusion.4), channel_id=1, source_target_pairs={{0,8},{4,12},{8,0},{12,4},{1,9},{5,13},{9,1},{13,5},{2,10},{6,14},... | collective-permute-start | bytes 24584 | tf_op jit(solution)/shard_map/ppermute | solution.py:33
  (13 other events, 55.5 us)

commit v11 on v10

--- a/solution.py
+++ b/solution.py
@@ -137,12 +137,13 @@
     return jnp.concatenate([ids, (high + middle) + low], axis=0)
 
 
-def pre_kernel(n, expert, choose, deps, scal, *refs):
+def pre_kernel(n, expert, choose, handed, deps, scal, *refs):
     refs = refs[deps:]
     packs, weights, (in_ref, cot_ref, *refs) = refs[:n], refs[n : n + 3], refs[n + 3 :]
-    outs, (token, routes, gw, uw, dw, sems) = refs[: STREAMS * n], refs[STREAMS * n :]
+    outs, (token, routes, *refs) = refs[: STREAMS * n], refs[STREAMS * n :]
+    gw, uw, dw, *sems = weights if handed else refs
     rows, tile, count = in_ref.shape[0] // n, gw.shape[1] // STREAMS, routes.shape[2]
-    copies = weight_copies(expert, weights, (gw, uw, dw), sems)
+    copies = [] if handed else weight_copies(expert, weights, (gw, uw, dw), sems[0])
     for group in copies:
         for copy in group:
             copy.start()
@@ -157,7 +158,7 @@
         scale = jnp.sum(jnp.where(hit, weight, 0.0), axis=1, keepdims=True)
         cot_ref[span, :] = (dot(pick, packs[k][count : 2 * count, :]) * scale).astype(BF16)
     for h in range(STREAMS):
-        for copy in copies[h]:
+        for copy in copies[h] if copies else []:
             copy.wait()
         part = slice(h * tile, (h + 1) * tile)
         gate = dot(in_ref[...], gw[:, part]).astype(BF16)
@@ -238,20 +239,28 @@
     return halves, refs[at:]
 
 
-def out_kernel(n, expert, has_prev, last, sizes, deps, scal, *refs):
+def out_kernel(n, expert, local, fetch, sizes, deps, scal, *refs):
+    has_prev, last = expert > 0, expert == local - 1
     refs = refs[deps:]
     routes, refs = [refs[0].at[k] for k in range(n)], refs[1:]
     if has_prev:
         prev, refs = refs[:2], refs[2:]
     halves, refs = split_pieces(refs, sizes)
-    (gw, uw, dw), (near, far, token, *refs) = refs[:3], refs[3:]
-    if last:
-        near_p, far_p, *refs, held = refs
-    eo_ref, idl_ref = refs
+    (gw, uw, dw), refs = refs[:3], refs[3:]
+    copies = []
+    if fetch:
+        sources, (near, far, token, *held), refs = refs[:3], refs[3:9], refs[9:]
+        copies = weight_copies(expert + 2, sources, held, refs[0])
+    else:
+        (near, far, token), refs = refs[:3], refs[3:]
+    eo_ref, idl_ref = refs[-2:]
+    for group in copies:
+        for copy in group:
+            copy.start()
     token[...] = jnp.zeros_like(token)
     spots = routing(scal, routes, expert, halves[0][0][0].shape[0] // 48 * 16)
     if last:
-        send_products(scal, routes, expert + 1, halves[-1], held, near_p, far_p)
+        send_products(scal, routes, local, halves[-1], refs[0], near, far)
     tile = gw.shape[1] // STREAMS
     eo, idl = 0.0, 0.0
     for h in range(STREAMS):
@@ -259,7 +268,7 @@
         eo = eo + dot(load_rows(scal, n, 0, halves[h]), dw[part, :])
         idl = idl + dot(load_rows(scal, n, 1, halves[h]), gw[:, part], ((1,), (1,)))
         idl = idl + dot(load_rows(scal, n, 2, halves[h]), uw[:, part], ((1,), (1,)))
-    rows = eo.shape[0] // n
+    rows, count = eo.shape[0] // n, routes[0].shape[1]
     eo_ref[...], idl_ref[...] = eo.astype(BF16), idl.astype(BF16)
     for k, (position, weight, hit) in enumerate(spots):
         pick = hit.astype(F32)
@@ -270,9 +279,12 @@
         which, place = (near, k) if k < n // 2 else (far, k - n // 2)
         if has_prev:
             before = prev[0 if k < n // 2 else 1]
-            layer, back = layer + before[place, 0], back + before[place, 1]
-        which[place, 0] = layer.astype(which.dtype)
-        which[place, 1] = back.astype(which.dtype)
+            layer, back = layer + before[place, 0:count], back + before[place, count : 2 * count]
+        which[place, 0:count] = layer.astype(which.dtype)
+        which[place, count : 2 * count] = back.astype(which.dtype)
+    for group in copies:
+        for copy in group:
+            copy.wait()
 
 
 def grad_kernel(n, has_prev, sizes, deps, scal, in_ref, cot_ref, *refs):
@@ -293,24 +305,30 @@
             dg[0] = dot(load_rows(scal, n, 0, halves[h]), cot_ref[...], ((0,), (0,))).astype(BF16)
 
 
+def product_rows(peers, extra, count, width):
+    wide = width // count
+    return [(extra * (p // wide), count * (p % wide)) for p in range(peers)], extra * -(-peers // wide)
+
+
 def send_products(scal, routes, local, pieces, held, near, far):
     n, (_, extra, lanes) = len(routes), held.shape
     first = pieces[0][0].shape[0] - extra
     for q, group in enumerate(pieces):
         held[q] = part_of(scal, n, q, group, first, extra)[:, 0:lanes]
-    experts_all, tokens = near.shape[1:]
-    ids = lax.broadcasted_iota(jnp.int32, (experts_all, tokens), 0)
-    sums = [jnp.zeros((experts_all, tokens), F32) for _ in range(n)]
+    tokens = routes[0].shape[1]
+    line = lax.broadcasted_iota(jnp.int32, (extra, tokens), 0)
+    blocks = [jnp.zeros((extra, tokens), F32) for _ in range(n)]
     for e in range(local):
         for k, (position, _, hit) in enumerate(routing(scal, routes, e, lanes)):
             found = dot(held[position], hit.astype(F32).astype(BF16))
-            value = found[3 * e : 3 * e + 1] + found[3 * e + 1 : 3 * e + 2] + found[3 * e + 2 : 3 * e + 3]
-            sums[k] = sums[k] + jnp.where(ids == scal[2 * n] + e, value, 0.0)
+            blocks[k] = jnp.where((line >= 3 * e) & (line < 3 * e + 3), found, blocks[k])
+    spots, _ = product_rows(n, extra, tokens, near.shape[2])
     for k in range(n):
-        if k < n // 2:
-            near[k] = sums[k]
-        else:
-            far[k - n // 2] = sums[k]
+        which, place = (near, k) if k < n // 2 else (far, k - n // 2)
+        for p, (row, lane) in enumerate(spots):
+            value = jnp.where(scal[2 * n] == p * local, blocks[k], 0.0).astype(BF16)
+            start = 2 * tokens + row
+            which[place, start : start + extra, lane : lane + tokens] = value
 
 
 def in_hbm(array):
@@ -413,6 +431,7 @@
     piece_shape = (3 * rows, tile)
     extra = -(-3 * local // 16) * 16
     wide_shape = (3 * rows + extra, tile)
+    spots, below = product_rows(peers, extra, count, width)
     piece_bytes = 2 * 3 * rows * tile
     slot_shape = (all_rows, width)
 
@@ -421,28 +440,34 @@
         wide = pl.BlockSpec((1, width, tile), lambda g: (e, 0, g))
         return [wide, wide, pl.BlockSpec((1, tile, width), lambda g: (e, g, 0))]
 
-    own_weights = []
+    own_weights = {}
 
     def pre(e, deps):
-        inputs, cot, *parts, token, found, gw, uw, dw = call(
-            functools.partial(pre_kernel, n, e, choose, len(deps)),
+        handed = e in own_weights
+        weight_shapes = [w.shape[1:] for w in weights]
+        inputs, cot, *parts = call(
+            functools.partial(pre_kernel, n, e, choose, handed, len(deps)),
             1,
-            [SMEM_SPEC] + [ANY_SPEC] * len(deps) + [spec_of(x) for x in packs] + [HBM_SPEC] * 3,
+            [SMEM_SPEC]
+            + [ANY_SPEC] * len(deps)
+            + [spec_of(x) for x in packs]
+            + ([whole_spec(shape) for shape in weight_shapes] if handed else [HBM_SPEC] * 3),
             [whole_spec(slot_shape)] * 2
             + [whole_spec(piece_shape)] * (STREAMS * n)
             + [whole_spec(TOKEN), whole_spec(route_shape)]
-            + [whole_spec(w.shape[1:]) for w in weights],
+            + ([] if handed else [whole_spec(shape) for shape in weight_shapes]),
             [like(slot_shape)] * 2
             + [like(piece_shape)] * (STREAMS * n)
             + [like(TOKEN, F32), like(route_shape, F32)]
-            + [like(w.shape[1:]) for w in weights],
+            + ([] if handed else [like(shape) for shape in weight_shapes]),
             6 * mac,
             3 * weight_bytes + STREAMS * n * piece_bytes,
-            scratch_shapes=[pltpu.SemaphoreType.DMA((STREAMS, 3))],
-        )(scal, *deps, *packs, *weights)
-        parts = [parts[h * n : (h + 1) * n] for h in range(STREAMS)]
-        own_weights.append((gw, uw, dw))
-        return (inputs, cot), parts, token, found
+            scratch_shapes=[] if handed else [pltpu.SemaphoreType.DMA((STREAMS, 3))],
+        )(scal, *deps, *packs, *(own_weights[e] if handed else weights))
+        parts, (token, found, *held) = parts[: STREAMS * n], parts[STREAMS * n :]
+        if not handed:
+            own_weights[e] = held
+        return (inputs, cot), [parts[h * n : (h + 1) * n] for h in range(STREAMS)], token, found
 
     def mid(e, h, totals, products, deps=()):
         others = products if e == local - 1 and h == STREAMS - 1 else []
@@ -478,29 +503,41 @@
 
     def out(e, halves, prev, deps):
         flat = flatten(halves)
-        last = e == local - 1
-        dense_shape = (chips, experts_all, count)
-        sum_shape = (chips, 2, count, width)
-        return call(
-            functools.partial(out_kernel, n, e, e > 0, last, sizes_of(halves[0]), len(deps)),
+        last, fetch = e == local - 1, swaps and e + 2 < local
+        sum_shape = (chips, 2 * count, width)
+        out_shape = (chips, 2 * count + below, width) if last else sum_shape
+        weight_specs = [whole_spec(w.shape[1:]) for w in weights]
+        near, far, token, *held = call(
+            functools.partial(out_kernel, n, e, local, fetch, sizes_of(halves[0]), len(deps)),
             1,
             [SMEM_SPEC]
             + [ANY_SPEC] * len(deps)
             + [whole_spec(route_shape)]
             + ([whole_spec(sum_shape)] * 2 if e > 0 else [])
             + [spec_of(x) for x in flat]
-            + [whole_spec(w.shape[1:]) for w in weights],
-            [whole_spec(sum_shape)] * 2
-            + [whole_spec(TOKEN)]
-            + ([whole_spec(dense_shape)] * 2 if last else []),
-            [like(sum_shape, BF16 if last else F32)] * 2
+            + weight_specs
+            + ([HBM_SPEC] * 3 if fetch else []),
+            [whole_spec(out_shape)] * 2 + [whole_spec(TOKEN)] + (weight_specs if fetch else []),
+            [like(out_shape, BF16 if last else F32)] * 2
             + [like(TOKEN, F32)]
-            + ([like(dense_shape, F32)] * 2 if last else []),
+            + ([like(w.shape[1:]) for w in weights] if fetch else []),
             6 * mac,
             3 * weight_bytes + len(flat) * piece_bytes,
-            scratch_shapes=[pltpu.VMEM(slot_shape, BF16)] * 2
-            + ([pltpu.VMEM((n, extra, 128), BF16)] if last else []),
-        )(scal, *deps, routes, *prev, *flat, *own_weights[e])
+            scratch_shapes=([pltpu.SemaphoreType.DMA((STREAMS, 3))] if fetch else [])
+            + ([pltpu.VMEM((n, extra, 128), BF16)] if last else [])
+            + [pltpu.VMEM(slot_shape, BF16)] * 2,
+        )(
+            scal,
+            *deps,
+            routes,
+            *prev,
+            *flat,
+            *own_weights[e],
+            *(weights if fetch else []),
+        )
+        if fetch:
+            own_weights[e + 2] = held
+        return near, far, token
 
     def grad(e, slots, halves, prev, deps):
         flat = flatten(halves)
@@ -610,12 +647,20 @@
                 *sums, _ = out(e, halves, sums, [])
                 *grads, _ = grad(e, arrived, halves, grads, [])
 
-    near, far, _, near_p, far_p = out(local - 1, halves, sums, wait)
+    near, far, _ = out(local - 1, halves, sums, wait)
     hop, home = send_home(near, far, add_rounded)
-    _, per_expert = send_home(near_p, far_p, lambda a, b: add(a, b, [hop]))
     *grads, _ = grad(local - 1, arrived, halves, grads, [hop])
+    per_expert = jnp.concatenate(
+        [
+            home[2 * count + row : 2 * count + row + 3 * local, lane : lane + count]
+            .reshape(local, 3, count)
+            .sum(axis=1)
+            for row, lane in spots
+        ]
+    )
     combine_grad = jnp.sum(jnp.where(named, per_expert[None], 0.0), axis=1) / combine_t
-    return (home[0].astype(BF16), home[1].astype(BF16), *grads, combine_grad.T)
+    layer_out, token_grad = home[:count].astype(BF16), home[count : 2 * count].astype(BF16)
+    return (layer_out, token_grad, *grads, combine_grad.T)
 
 
 def solution(mesh):

time: 196 us -> 199 us (1.015)
  waiting for transfers between devices: 54.7 us -> 50 us
  Pallas kernels: 41.2 us -> 45.2 us
  starting transfers between devices: 95.4 us -> 99.4 us
    ppermute x43 -> x41, waiting for transfers between devices: 54.6 us -> 49.9 us  [send(): return lax.ppermute(value, self.axis, wide)]
    pallas_call x8, Pallas kernels: 24.6 us -> 28.6 us  [the longest x4 15.9 us: pre(): call(functools.partial(pre_kernel, n, e, choose, handed, len(deps)), 1, [...]
    ppermute x43 -> x41, starting transfers between devices: 92.2 us -> 95.9 us  [send(): return lax.ppermute(value, self.axis, wide)]
  transfers between devices with their start and end apart: 75 -> 73, of which waited for: 21 -> 19; matrix products, arithmetic and copies ran while one was open for 1% -> 1% of each run, Pallas kernels for 17% -> 18%
where the time goes in v11:
time: 199 us
  starting transfers between devices  99.4 us (50%)
  waiting for transfers between devices  50 us (25%)
  Pallas kernels  45.2 us (23%)
  other arithmetic  2.28 us (1%)
    ppermute x41, starting transfers between devices, send(): return lax.ppermute(value, self.axis, wide)  95.9 us
    ppermute x41, waiting for transfers between devices, send(): return lax.ppermute(value, self.axis, wide)  49.9 us
    pallas_call x4, Pallas kernels, pre(): call(functools.partial(pre_kernel, n, e, choose, handed, len(deps)), 1, [...  15.9 us
    pallas_call x4, Pallas kernels, grad(): call(functools.partial(grad_kernel, n, e > 0, sizes_of(halves[0]), len(de...  13.4 us
    pallas_call x4, Pallas kernels, out(): call(functools.partial(out_kernel, n, e, local, fetch, sizes_of(halves[0]...  12.7 us
  transfers between devices with their start and end apart: 73, of which 19 were waited for; matrix products, arithmetic and copies ran while one was open for 1% of the time, Pallas kernels for 18%

profile of v11, /device:TPU:0, one launch (start us, length us, event | category | flops | bytes accessed | tf_op | source)
XLA Modules:
  0.0 199.0 jit_solution(6515327824897374034)
XLA Ops:
  0.6 1.0 shard_map.118.refs_0_.refs_1_
  1.7 3.0 %collective-permute-start = (bf16[272,512]{1,0:T(8,128)(2,1)S(1)}, bf16[272,512]{1,0:T(8,128)(2,1)S(1)}, u32[]{:S(2)}, u32[]{:S(2)}) collective-permute-start(bf16[272,512]{1,0:T(8,128)(2,1)S(1)} %shard_map.118.refs_0_.refs_1_), channel_id=1, source_target_pairs={{0,8},{4,12},{8,0},{12,4},{1,9},{5,13},{9,1},{13,5},{2,10},{6,14},... | collective-permute-start | bytes 835592 | tf_op jit(solution)/shard_map/ppermute | solution.py:33
  4.7 6.7 %collective-permute-done.refs_1_.refs_2_ = bf16[272,512]{1,0:T(8,128)(2,1)S(1)} collective-permute-done((bf16[272,512]{1,0:T(8,128)(2,1)S(1)}, bf16[272,512]{1,0:T(8,128)(2,1)S(1)}, u32[]{:S(2)}, u32[]{:S(2)}) %collective-permute-start) | collective-permute-done | bytes 278560 | tf_op jit(solution)/shard_map/ppermute | solution.py:33
  11.4 1.5 collective-permute-done.2.refs_3_.refs_4_
  12.9 3.6 %shard_map.119 = (bf16[320,512]{1,0:T(8,128)(2,1)S(1)}, bf16[320,512]{1,0:T(8,128)(2,1)S(1)}, bf16[240,384]{1,0:T(8,128)(2,1)S(1)}, bf16[240,384]{1,0:T(8,128)(2...) custom-call(s32[10]{0:T(128)S(1)} %stack.35.scal, ...), custom_call_target="tpu_custom_call" | custom-call | flops 754974720 | bytes 3833856 | tf_op jit(solution)/shard_map/pallas_call | solution.py:448
  16.4 1.9 collective-permute-start.3
  18.5 1.8 collective-permute-start.32
  20.6 3.7 %shard_map.123 = (bf16[320,512]{1,0:T(8,128)(2,1)S(1)}, bf16[320,512]{1,0:T(8,128)(2,1)S(1)}, bf16[240,384]{1,0:T(8,128)(2,1)S(1)}, bf16[240,384]{1,0:T(8,128)(2...) custom-call(s32[10]{0:T(128)S(1)} %stack.35.scal, ...), custom_call_target="tpu_custom_call" | custom-call | flops 754974720 | bytes 3833856 | tf_op jit(solution)/shard_map/pallas_call | solution.py:448
  24.4 3.5 %collective-permute-done.6 = bf16[240,384]{1,0:T(8,128)(2,1)S(1)} collective-permute-done((bf16[240,384]{1,0:T(8,128)(2,1)S(1)}, bf16[240,384]{1,0:T(8,128)(2,1)S(1)}, u32[]{:S(2)}, u32[]{:S(2)}) %collective-permute-start.6) | collective-permute-done | bytes 184352 | tf_op jit(solution)/shard_map/ppermute | solution.py:33
  28.1 3.8 %collective-permute-done.32.refs_2_ = bf16[240,384]{1,0:T(8,128)(2,1)S(1)} collective-permute-done((bf16[240,384]{1,0:T(8,128)(2,1)S(1)}, bf16[240,384]{1,0:T(8,128)(2,1)S(1)}, u32[]{:S(2)}, u32[]{:S(2)}) %collective-permute-start.32) | collective-permute-done | bytes 184352 | tf_op jit(solution)/shard_map/ppermute | solution.py:33
  32.0 3.1 %collective-permute-done.35 = bf16[240,384]{1,0:T(8,128)(2,1)S(1)} collective-permute-done((bf16[240,384]{1,0:T(8,128)(2,1)S(1)}, bf16[240,384]{1,0:T(8,128)(2,1)S(1)}, u32[]{:S(2)}, u32[]{:S(2)}) %collective-permute-start.35) | collective-permute-done | bytes 184352 | tf_op jit(solution)/shard_map/ppermute | solution.py:33
  35.4 3.4 %collective-permute-start.5 = (bf16[240,384]{1,0:T(8,128)(2,1)S(1)}, bf16[240,384]{1,0:T(8,128)(2,1)S(1)}, u32[]{:S(2)}, u32[]{:S(2)}) collective-permute-start(bf16[240,384]{1,0:T(8,128)(2,1)S(1)} %fusion), channel_id=1, source_target_pairs={{0,1},{1,0},{2,3},{3,2},{4,5},{5,4},{6,7},{7,6},{8,9},{9,8},{10,11... | collective-permute-start | bytes 552968 | tf_op jit(solution)/shard_map/ppermute | solution.py:33
  38.8 1.8 collective-permute-start.34
  40.6 3.7 %collective-permute-done.5.refs_1_ = bf16[240,384]{1,0:T(8,128)(2,1)S(1)} collective-permute-done((bf16[240,384]{1,0:T(8,128)(2,1)S(1)}, bf16[240,384]{1,0:T(8,128)(2,1)S(1)}, u32[]{:S(2)}, u32[]{:S(2)}) %collective-permute-start.5) | collective-permute-done | bytes 184352 | tf_op jit(solution)/shard_map/ppermute | solution.py:33
  44.5 2.4 %collective-permute-start.12 = (bf16[240,384]{1,0:T(8,128)(2,1)S(1)}, bf16[240,384]{1,0:T(8,128)(2,1)S(1)}, u32[]{:S(2)}, u32[]{:S(2)}) collective-permute-start(bf16[240,384]{1,0:T(8,128)(2,1)S(1)} %get-tuple-element.107.refs_7_), channel_id=1, source_target_pairs={{0,1},{1,0},{2,3},{3,2},{4,5},{5,4},{6,7},{7,6},{8,9},{9,8},{10,11... | collective-permute-start | bytes 552968 | tf_op jit(solution)/shard_map/ppermute | solution.py:33
  47.1 1.7 collective-permute-start.37
  48.8 3.5 %collective-permute-start.9 = (bf16[240,384]{1,0:T(8,128)(2,1)S(1)}, bf16[240,384]{1,0:T(8,128)(2,1)S(1)}, u32[]{:S(2)}, u32[]{:S(2)}) collective-permute-start(bf16[240,384]{1,0:T(8,128)(2,1)S(1)} %broadcast_select_fusion.11), channel_id=1, source_target_pairs={{0,1},{1,0},{2,3},{3,2},{4,5},{5,4},{6,7},{7,6},{8,9},{9,8},{10,11... | collective-permute-start | bytes 552968 | tf_op jit(solution)/shard_map/ppermute | solution.py:33
  52.4 4.9 %collective-permute-start.39 = (bf16[240,384]{1,0:T(8,128)(2,1)S(1)}, bf16[240,384]{1,0:T(8,128)(2,1)S(1)}, u32[]{:S(2)}, u32[]{:S(2)}) collective-permute-start(bf16[240,384]{1,0:T(8,128)(2,1)S(1)} %broadcast_select_fusion.5), channel_id=1, source_target_pairs={{0,1},{1,0},{2,3},{3,2},{4,5},{5,4},{6,7},{7,6},{8,9},{9,8},{10,11... | collective-permute-start | bytes 552968 | tf_op jit(solution)/shard_map/ppermute | solution.py:33
  57.3 4.3 %shard_map.122 = (bf16[320,512]{1,0:T(8,128)(2,1)S(1)}, bf16[320,512]{1,0:T(8,128)(2,1)S(1)}, bf16[240,384]{1,0:T(8,128)(2,1)S(1)}, bf16[240,384]{1,0:T(8,128)(2...) custom-call(s32[10]{0:T(128)S(1)} %stack.35.scal, ...), custom_call_target="tpu_custom_call" | custom-call | flops 754974720 | bytes 3833856 | tf_op jit(solution)/shard_map/pallas_call | solution.py:448
  62.3 2.7 %collective-permute-start.14 = (bf16[240,384]{1,0:T(8,128)(2,1)S(1)}, bf16[240,384]{1,0:T(8,128)(2,1)S(1)}, u32[]{:S(2)}, u32[]{:S(2)}) collective-permute-start(bf16[240,384]{1,0:T(8,128)(2,1)S(1)} %broadcast_select_fusion.10), channel_id=1, source_target_pairs={{0,1},{1,0},{2,3},{3,2},{4,5},{5,4},{6,7},{7,6},{8,9},{9,8},{10,11... | collective-permute-start | bytes 552968 | tf_op jit(solution)/shard_map/ppermute | solution.py:33
  65.3 6.4 %collective-permute-start.11 = (bf16[240,384]{1,0:T(8,128)(2,1)S(1)}, bf16[240,384]{1,0:T(8,128)(2,1)S(1)}, u32[]{:S(2)}, u32[]{:S(2)}) collective-permute-start(bf16[240,384]{1,0:T(8,128)(2,1)S(1)} %fusion.1), channel_id=1, source_target_pairs={{0,1},{1,0},{2,3},{3,2},{4,5},{5,4},{6,7},{7,6},{8,9},{9,8},{10,11... | collective-permute-start | bytes 552968 | tf_op jit(solution)/shard_map/ppermute | solution.py:33
  71.9 3.4 %collective-permute-start.43 = (bf16[240,384]{1,0:T(8,128)(2,1)S(1)}, bf16[240,384]{1,0:T(8,128)(2,1)S(1)}, u32[]{:S(2)}, u32[]{:S(2)}) collective-permute-start(bf16[240,384]{1,0:T(8,128)(2,1)S(1)} %fusion.5), channel_id=1, source_target_pairs={{0,1},{1,0},{2,3},{3,2},{4,5},{5,4},{6,7},{7,6},{8,9},{9,8},{10,11... | collective-permute-start | bytes 552968 | tf_op jit(solution)/shard_map/ppermute | solution.py:33
  75.4 3.0 %collective-permute-done.11.refs_1_ = bf16[240,384]{1,0:T(8,128)(2,1)S(1)} collective-permute-done((bf16[240,384]{1,0:T(8,128)(2,1)S(1)}, bf16[240,384]{1,0:T(8,128)(2,1)S(1)}, u32[]{:S(2)}, u32[]{:S(2)}) %collective-permute-start.11) | collective-permute-done | bytes 184352 | tf_op jit(solution)/shard_map/ppermute | solution.py:33
  78.7 3.6 %shard_map.132 = (f32[2,256,512]{2,1,0:T(8,128)S(1)}, f32[2,256,512]{2,1,0:T(8,128)S(1)}, f32[8,128]{1,0:T(8,128)S(1)}, bf16[512,768]{1,0:T(8,128)(2,1)S(1)}, bf...) custom-call(s32[10]{0:T(128)S(1)} %stack.35.scal, f32[4,16,128]{2,1,0:T(8,128)S(1)} %get-tuple-element.133.refs_0_.refs_1_, ...), custom_call_target="tpu_custom_call" | custom-call | flops 754974720 | bytes 4571136 | tf_op jit(solution)/shard_map/pallas_call | solution.py:510
  82.3 3.3 %collective-permute-start.20 = (bf16[240,384]{1,0:T(8,128)(2,1)S(1)}, bf16[240,384]{1,0:T(8,128)(2,1)S(1)}, u32[]{:S(2)}, u32[]{:S(2)}) collective-permute-start(bf16[240,384]{1,0:T(8,128)(2,1)S(1)} %get-tuple-element.115.refs_9_.refs_0_.refs_7_), channel_id=1, source_target_pairs={{0,1},{1,0},{2,3},{3,2},{4,5},{5,4},{6,7},{7,6},{8,9},{9,8},{10,11... | collective-permute-start | bytes 552968 | tf_op jit(solution)/shard_map/ppermute | solution.py:33
  85.9 3.5 %shard_map.136 = (bf16[4,512,768]{2,1,0:T(8,128)(2,1)}, bf16[4,512,768]{2,1,0:T(8,128)(2,1)}, bf16[4,768,512]{2,1,0:T(8,128)(2,1)}, f32[8,128]{1,0:T(8,128)S(1)}) custom-call(s32[10]{0:T(128)S(1)} %stack.35.scal, bf16[320,512]{1,0:T(8,128)(2,1)S(1)} %get-tuple-element.156.in_ref, bf16[320,512]{1,0:T(8,128)(2,1)S(1)} %get-tuple-element.157.cot_ref, ...), custom_call_target="tpu_custom_call" | custom-call | flops 754974720 | bytes 4571136 | tf_op jit(solution)/shard_map/pallas_call | solution.py:545
  89.4 1.8 collective-permute-start.17
  91.3 2.2 %collective-permute-start.47 = (bf16[240,384]{1,0:T(8,128)(2,1)S(1)}, bf16[240,384]{1,0:T(8,128)(2,1)S(1)}, u32[]{:S(2)}, u32[]{:S(2)}) collective-permute-start(bf16[240,384]{1,0:T(8,128)(2,1)S(1)} %broadcast_select_fusion.3), channel_id=1, source_target_pairs={{0,1},{1,0},{2,3},{3,2},{4,5},{5,4},{6,7},{7,6},{8,9},{9,8},{10,11... | collective-permute-start | bytes 552968 | tf_op jit(solution)/shard_map/ppermute | solution.py:33
  93.5 0.8 collective-permute-done.45.refs_4_.refs_2_
  94.3 4.3 %shard_map.126 = (bf16[320,512]{1,0:T(8,128)(2,1)S(1)}, bf16[320,512]{1,0:T(8,128)(2,1)S(1)}, bf16[240,384]{1,0:T(8,128)(2,1)S(1)}, bf16[240,384]{1,0:T(8,128)(2...) custom-call(s32[10]{0:T(128)S(1)} %stack.35.scal, ...), custom_call_target="tpu_custom_call" | custom-call | flops 754974720 | bytes 3833856 | tf_op jit(solution)/shard_map/pallas_call | solution.py:448
  99.3 2.4 %collective-permute-start.22 = (bf16[240,384]{1,0:T(8,128)(2,1)S(1)}, bf16[240,384]{1,0:T(8,128)(2,1)S(1)}, u32[]{:S(2)}, u32[]{:S(2)}) collective-permute-start(bf16[240,384]{1,0:T(8,128)(2,1)S(1)} %broadcast_select_fusion.8), channel_id=1, source_target_pairs={{0,1},{1,0},{2,3},{3,2},{4,5},{5,4},{6,7},{7,6},{8,9},{9,8},{10,11... | collective-permute-start | bytes 552968 | tf_op jit(solution)/shard_map/ppermute | solution.py:33
  102.3 7.0 %collective-permute-start.19 = (bf16[240,384]{1,0:T(8,128)(2,1)S(1)}, bf16[240,384]{1,0:T(8,128)(2,1)S(1)}, u32[]{:S(2)}, u32[]{:S(2)}) collective-permute-start(bf16[240,384]{1,0:T(8,128)(2,1)S(1)} %fusion.2), channel_id=1, source_target_pairs={{0,1},{1,0},{2,3},{3,2},{4,5},{5,4},{6,7},{7,6},{8,9},{9,8},{10,11... | collective-permute-start | bytes 552968 | tf_op jit(solution)/shard_map/ppermute | solution.py:33
  109.5 2.8 %collective-permute-start.51 = (bf16[240,384]{1,0:T(8,128)(2,1)S(1)}, bf16[240,384]{1,0:T(8,128)(2,1)S(1)}, u32[]{:S(2)}, u32[]{:S(2)}) collective-permute-start(bf16[240,384]{1,0:T(8,128)(2,1)S(1)} %fusion.6), channel_id=1, source_target_pairs={{0,1},{1,0},{2,3},{3,2},{4,5},{5,4},{6,7},{7,6},{8,9},{9,8},{10,11... | collective-permute-start | bytes 552968 | tf_op jit(solution)/shard_map/ppermute | solution.py:33
  112.5 2.4 %collective-permute-done.19.refs_1_ = bf16[240,384]{1,0:T(8,128)(2,1)S(1)} collective-permute-done((bf16[240,384]{1,0:T(8,128)(2,1)S(1)}, bf16[240,384]{1,0:T(8,128)(2,1)S(1)}, u32[]{:S(2)}, u32[]{:S(2)}) %collective-permute-start.19) | collective-permute-done | bytes 184352 | tf_op jit(solution)/shard_map/ppermute | solution.py:33
  115.2 3.6 %shard_map.135 = (f32[2,256,512]{2,1,0:T(8,128)S(1)}, f32[2,256,512]{2,1,0:T(8,128)S(1)}, f32[8,128]{1,0:T(8,128)S(1)}, bf16[512,768]{1,0:T(8,128)(2,1)S(1)}, bf...) custom-call(s32[10]{0:T(128)S(1)} %stack.35.scal, f32[4,16,128]{2,1,0:T(8,128)S(1)} %get-tuple-element.133.refs_0_.refs_1_, ...), custom_call_target="tpu_custom_call" | custom-call | flops 754974720 | bytes 4571136 | tf_op jit(solution)/shard_map/pallas_call | solution.py:510
  118.7 4.0 %collective-permute-start.28 = (bf16[240,384]{1,0:T(8,128)(2,1)S(1)}, bf16[240,384]{1,0:T(8,128)(2,1)S(1)}, u32[]{:S(2)}, u32[]{:S(2)}) collective-permute-start(bf16[240,384]{1,0:T(8,128)(2,1)S(1)} %get-tuple-element.124.refs_9_.refs_0_.refs_7_), channel_id=1, source_target_pairs={{0,1},{1,0},{2,3},{3,2},{4,5},{5,4},{6,7},{7,6},{8,9},{9,8},{10,11... | collective-permute-start | bytes 552968 | tf_op jit(solution)/shard_map/ppermute | solution.py:33
  123.1 3.3 %shard_map.140 = (bf16[4,512,768]{2,1,0:T(8,128)(2,1)}, bf16[4,512,768]{2,1,0:T(8,128)(2,1)}, bf16[4,768,512]{2,1,0:T(8,128)(2,1)}, f32[8,128]{1,0:T(8,128)S(1)}) custom-call(s32[10]{0:T(128)S(1)} %stack.35.scal, bf16[320,512]{1,0:T(8,128)(2,1)S(1)} %get-tuple-element.172.in_ref, ...), custom_call_target="tpu_custom_call", output_to_operand_aliasing={{0}: (16, {}), {1}: (17, {}), {2}: (18, {})} | custom-call | flops 754974720 | bytes 4571136 | tf_op jit(solution)/shard_map/pallas_call | solution.py:545
  126.4 2.0 collective-permute-start.25
  128.5 2.2 %collective-permute-start.55 = (bf16[240,384]{1,0:T(8,128)(2,1)S(1)}, bf16[240,384]{1,0:T(8,128)(2,1)S(1)}, u32[]{:S(2)}, u32[]{:S(2)}) collective-permute-start(bf16[240,384]{1,0:T(8,128)(2,1)S(1)} %broadcast_select_fusion.1), channel_id=1, source_target_pairs={{0,1},{1,0},{2,3},{3,2},{4,5},{5,4},{6,7},{7,6},{8,9},{9,8},{10,11... | collective-permute-start | bytes 552968 | tf_op jit(solution)/shard_map/ppermute | solution.py:33
  130.6 3.4 %collective-permute-done.25.refs_1_.refs_11_.refs_9_ = bf16[240,384]{1,0:T(8,128)(2,1)S(1)} collective-permute-done((bf16[240,384]{1,0:T(8,128)(2,1)S(1)}, bf16[240,384]{1,0:T(8,128)(2,1)S(1)}, u32[]{:S(2)}, u32[]{:S(2)}) %collective-permute-start.25) | collective-permute-done | bytes 184352 | tf_op jit(solution)/shard_map/ppermute | solution.py:33
  134.2 3.9 %collective-permute-start.30 = (bf16[240,384]{1,0:T(8,128)(2,1)S(1)}, bf16[240,384]{1,0:T(8,128)(2,1)S(1)}, u32[]{:S(2)}, u32[]{:S(2)}) collective-permute-start(bf16[240,384]{1,0:T(8,128)(2,1)S(1)} %broadcast_select_fusion.6), channel_id=1, source_target_pairs={{0,1},{1,0},{2,3},{3,2},{4,5},{5,4},{6,7},{7,6},{8,9},{9,8},{10,11... | collective-permute-start | bytes 552968 | tf_op jit(solution)/shard_map/ppermute | solution.py:33
  138.1 2.0 collective-permute-start.57
  140.3 3.8 %collective-permute-start.27 = (bf16[240,384]{1,0:T(8,128)(2,1)S(1)}, bf16[240,384]{1,0:T(8,128)(2,1)S(1)}, u32[]{:S(2)}, u32[]{:S(2)}) collective-permute-start(bf16[240,384]{1,0:T(8,128)(2,1)S(1)} %fusion.3), channel_id=1, source_target_pairs={{0,1},{1,0},{2,3},{3,2},{4,5},{5,4},{6,7},{7,6},{8,9},{9,8},{10,11... | collective-permute-start | bytes 552968 | tf_op jit(solution)/shard_map/ppermute | solution.py:33
  144.1 3.1 %collective-permute-start.59 = (bf16[240,384]{1,0:T(8,128)(2,1)S(1)}, bf16[240,384]{1,0:T(8,128)(2,1)S(1)}, u32[]{:S(2)}, u32[]{:S(2)}) collective-permute-start(bf16[240,384]{1,0:T(8,128)(2,1)S(1)} %fusion.7), channel_id=1, source_target_pairs={{0,1},{1,0},{2,3},{3,2},{4,5},{5,4},{6,7},{7,6},{8,9},{9,8},{10,11... | collective-permute-start | bytes 552968 | tf_op jit(solution)/shard_map/ppermute | solution.py:33
  148.4 2.2 %shard_map.139 = (f32[2,256,512]{2,1,0:T(8,128)S(1)}, f32[2,256,512]{2,1,0:T(8,128)S(1)}, f32[8,128]{1,0:T(8,128)S(1)}) custom-call(s32[10]{0:T(128)S(1)} %stack.35.scal, f32[4,16,128]{2,1,0:T(8,128)S(1)} %get-tuple-element.133.refs_0_.refs_1_, f32[2,256,512]{2,1,0:T(8,128)S(1)} %get-tuple-element.161.refs_1_, ...), custom_call_target="tpu_custom_call" | custom-call | flops 754974720 | bytes 4571136 | tf_op jit(solution)/shard_map/pallas_call | solution.py:510
  150.6 2.9 %collective-permute-done.59.refs_2_ = bf16[240,384]{1,0:T(8,128)(2,1)S(1)} collective-permute-done((bf16[240,384]{1,0:T(8,128)(2,1)S(1)}, bf16[240,384]{1,0:T(8,128)(2,1)S(1)}, u32[]{:S(2)}, u32[]{:S(2)}) %collective-permute-start.59) | collective-permute-done | bytes 184352 | tf_op jit(solution)/shard_map/ppermute | solution.py:33
  153.6 0.8 shard_map.143
  154.4 3.6 %collective-permute-start.66 = (bf16[256,384]{1,0:T(8,128)(2,1)S(1)}, bf16[256,384]{1,0:T(8,128)(2,1)S(1)}, u32[]{:S(2)}, u32[]{:S(2)}) collective-permute-start(bf16[256,384]{1,0:T(8,128)(2,1)S(1)} %get-tuple-element.179.refs_0_.refs_10_.refs_7_), channel_id=1, source_target_pairs={{0,1},{1,0},{2,3},{3,2},{4,5},{5,4},{6,7},{7,6},{8,9},{9,8},{10,11... | collective-permute-start | bytes 589832 | tf_op jit(solution)/shard_map/ppermute | solution.py:33
  158.1 3.6 %collective-permute-done.66.refs_11_.refs_8_ = bf16[256,384]{1,0:T(8,128)(2,1)S(1)} collective-permute-done((bf16[256,384]{1,0:T(8,128)(2,1)S(1)}, bf16[256,384]{1,0:T(8,128)(2,1)S(1)}, u32[]{:S(2)}, u32[]{:S(2)}) %collective-permute-start.66) | collective-permute-done | bytes 196640 | tf_op jit(solution)/shard_map/ppermute | solution.py:33
  162.3 1.5 collective-permute-done.61.refs_5_.refs_2_
  163.7 4.2 %collective-permute-start.68 = (bf16[256,384]{1,0:T(8,128)(2,1)S(1)}, bf16[256,384]{1,0:T(8,128)(2,1)S(1)}, u32[]{:S(2)}, u32[]{:S(2)}) collective-permute-start(bf16[256,384]{1,0:T(8,128)(2,1)S(1)} %collective-permute-done.67.refs_13_.refs_10_), channel_id=1, source_target_pairs={{0,1},{1,0},{2,3},{3,2},{4,5},{5,4},{6,7},{7,6},{8,9},{9,8},{10,11... | collective-permute-start | bytes 589832 | tf_op jit(solution)/shard_map/ppermute | solution.py:33
  167.9 4.2 %collective-permute-start.70 = (bf16[256,384]{1,0:T(8,128)(2,1)S(1)}, bf16[256,384]{1,0:T(8,128)(2,1)S(1)}, u32[]{:S(2)}, u32[]{:S(2)}) collective-permute-start(bf16[256,384]{1,0:T(8,128)(2,1)S(1)} %collective-permute-done.69.refs_15_.refs_12_), channel_id=1, source_target_pairs={{0,1},{1,0},{2,3},{3,2},{4,5},{5,4},{6,7},{7,6},{8,9},{9,8},{10,11... | collective-permute-start | bytes 589832 | tf_op jit(solution)/shard_map/ppermute | solution.py:33
  172.1 2.2 %collective-permute-start.63 = (bf16[240,384]{1,0:T(8,128)(2,1)S(1)}, bf16[240,384]{1,0:T(8,128)(2,1)S(1)}, u32[]{:S(2)}, u32[]{:S(2)}) collective-permute-start(bf16[240,384]{1,0:T(8,128)(2,1)S(1)} %collective-permute-done.62.refs_7_.refs_4_), channel_id=1, source_target_pairs={{0,1},{1,0},{2,3},{3,2},{4,5},{5,4},{6,7},{7,6},{8,9},{9,8},{10,11... | collective-permute-start | bytes 552968 | tf_op jit(solution)/shard_map/ppermute | solution.py:33
  174.3 2.0 collective-permute-start.65
  176.3 3.3 %shard_map.144 = (bf16[4,512,768]{2,1,0:T(8,128)(2,1)}, bf16[4,512,768]{2,1,0:T(8,128)(2,1)}, bf16[4,768,512]{2,1,0:T(8,128)(2,1)}, f32[8,128]{1,0:T(8,128)S(1)}) custom-call(s32[10]{0:T(128)S(1)} %stack.35.scal, bf16[320,512]{1,0:T(8,128)(2,1)S(1)} %get-tuple-element.108.in_ref, ...), custom_call_target="tpu_custom_call", output_to_operand_aliasing={{0}: (16, {}), {1}: (17, {}), {2}: (18, {})} | custom-call | flops 754974720 | bytes 4571136 | tf_op jit(solution)/shard_map/pallas_call | solution.py:545
  179.6 1.6 collective-permute-done.63.refs_6_.refs_3_
  181.2 2.0 collective-permute-done.65.refs_8_.refs_5_
  183.2 3.3 %shard_map.145 = (bf16[2,272,512]{2,1,0:T(8,128)(2,1)S(1)}, bf16[2,272,512]{2,1,0:T(8,128)(2,1)S(1)}, f32[8,128]{1,0:T(8,128)}) custom-call(s32[10]{0:T(128)S(1)} %stack.35.scal, f32[8,128]{1,0:T(8,128)S(1)} %get-tuple-element.183.refs_0_, f32[4,16,128]{2,1,0:T(8,128)S(1)} %get-tuple-element.133.refs_0_.refs_1_, ...), custom_call_target="tpu_custom_call" | custom-call | flops 754974720 | bytes 4571136 | tf_op jit(solution)/shard_map/pallas_call | solution.py:510
  186.5 2.0 collective-permute-done.71
  188.6 1.5 collective-permute-start.72
  190.1 3.3 %shard_map.146 = (bf16[4,512,768]{2,1,0:T(8,128)(2,1)}, bf16[4,512,768]{2,1,0:T(8,128)(2,1)}, bf16[4,768,512]{2,1,0:T(8,128)(2,1)}, f32[8,128]{1,0:T(8,128)}) custom-call(s32[10]{0:T(128)S(1)} %stack.35.scal, bf16[320,512]{1,0:T(8,128)(2,1)S(1)} %get-tuple-element.192.in_ref, ...), custom_call_target="tpu_custom_call", output_to_operand_aliasing={{0}: (16, {}), {1}: (17, {}), {2}: (18, {})} | custom-call | flops 754974720 | bytes 4571136 | tf_op jit(solution)/shard_map/pallas_call | solution.py:545
  193.4 4.0 %collective-permute-done.72 = bf16[272,512]{1,0:T(8,128)(2,1)S(1)} collective-permute-done((bf16[272,512]{1,0:T(8,128)(2,1)S(1)}, bf16[272,512]{1,0:T(8,128)(2,1)S(1)}, u32[]{:S(2)}, u32[]{:S(2)}) %collective-permute-start.72) | collective-permute-done | bytes 278560 | tf_op jit(solution)/shard_map/ppermute | solution.py:33
  197.5 0.7 fusion.18
  198.4 0.6 bitcast_divide_fusion
  (160 shorter events, 8.4 us)
Async XLA Ops:
  1.7 9.7 %collective-permute-start = (bf16[272,512]{1,0:T(8,128)(2,1)S(1)}, bf16[272,512]{1,0:T(8,128)(2,1)S(1)}, u32[]{:S(2)}, u32[]{:S(2)}) collective-permute-start(bf16[272,512]{1,0:T(8,128)(2,1)S(1)} %shard_map.118.refs_0_.refs_1_), channel_id=1, source_target_pairs={{0,8},{4,12},{8,0},{12,4},{1,9},{5,13},{9,1},{13,5},{2,10},{6,14},... | collective-permute-start | bytes 835592 | tf_op jit(solution)/shard_map/ppermute | solution.py:33
  4.7 6.7 %collective-permute-start.1 = (bf16[272,512]{1,0:T(8,128)(2,1)S(1)}, bf16[272,512]{1,0:T(8,128)(2,1)S(1)}, u32[]{:S(2)}, u32[]{:S(2)}) collective-permute-start(bf16[272,512]{1,0:T(8,128)(2,1)S(1)} %shard_map.118.refs_0_.refs_1_), channel_id=1, source_target_pairs={{0,4},{4,0},{8,12},{12,8},{1,5},{5,1},{9,13},{13,9},{2,6},{6,2},{1... | collective-permute-start | bytes 835592 | tf_op jit(solution)/shard_map/ppermute | solution.py:33
  16.4 7.8 %collective-permute-start.3 = (bf16[240,384]{1,0:T(8,128)(2,1)S(1)}, bf16[240,384]{1,0:T(8,128)(2,1)S(1)}, u32[]{:S(2)}, u32[]{:S(2)}) collective-permute-start(bf16[240,384]{1,0:T(8,128)(2,1)S(1)} %get-tuple-element.105.refs_0_), channel_id=1, source_target_pairs={{0,1},{1,0},{2,3},{3,2},{4,5},{5,4},{6,7},{7,6},{8,9},{9,8},{10,11... | collective-permute-start | bytes 552968 | tf_op jit(solution)/shard_map/ppermute | solution.py:33
  18.3 9.6 %collective-permute-start.6 = (bf16[240,384]{1,0:T(8,128)(2,1)S(1)}, bf16[240,384]{1,0:T(8,128)(2,1)S(1)}, u32[]{:S(2)}, u32[]{:S(2)}) collective-permute-start(bf16[240,384]{1,0:T(8,128)(2,1)S(1)} %get-tuple-element.106), channel_id=1, source_target_pairs={{0,1},{1,0},{2,3},{3,2},{4,5},{5,4},{6,7},{7,6},{8,9},{9,8},{10,11... | collective-permute-start | bytes 552968 | tf_op jit(solution)/shard_map/ppermute | solution.py:33
  18.5 13.3 %collective-permute-start.32 = (bf16[240,384]{1,0:T(8,128)(2,1)S(1)}, bf16[240,384]{1,0:T(8,128)(2,1)S(1)}, u32[]{:S(2)}, u32[]{:S(2)}) collective-permute-start(bf16[240,384]{1,0:T(8,128)(2,1)S(1)} %get-tuple-element.129.refs_1_), channel_id=1, source_target_pairs={{0,1},{1,0},{2,3},{3,2},{4,5},{5,4},{6,7},{7,6},{8,9},{9,8},{10,11... | collective-permute-start | bytes 552968 | tf_op jit(solution)/shard_map/ppermute | solution.py:33
  20.4 14.8 %collective-permute-start.35 = (bf16[240,384]{1,0:T(8,128)(2,1)S(1)}, bf16[240,384]{1,0:T(8,128)(2,1)S(1)}, u32[]{:S(2)}, u32[]{:S(2)}) collective-permute-start(bf16[240,384]{1,0:T(8,128)(2,1)S(1)} %get-tuple-element.130), channel_id=1, source_target_pairs={{0,1},{1,0},{2,3},{3,2},{4,5},{5,4},{6,7},{7,6},{8,9},{9,8},{10,11... | collective-permute-start | bytes 552968 | tf_op jit(solution)/shard_map/ppermute | solution.py:33
  24.3 10.9 %collective-permute-start.4 = (bf16[240,384]{1,0:T(8,128)(2,1)S(1)}, bf16[240,384]{1,0:T(8,128)(2,1)S(1)}, u32[]{:S(2)}, u32[]{:S(2)}) collective-permute-start(bf16[240,384]{1,0:T(8,128)(2,1)S(1)} %shard_map.120), channel_id=1, source_target_pairs={{1,2},{2,1},{0,4},{3,7},{5,6},{6,5},{4,0},{7,3},{9,10},{10,9},{8,1... | collective-permute-start | bytes 552968 | tf_op jit(solution)/shard_map/ppermute | solution.py:570
  28.0 12.6 %collective-permute-start.7 = (bf16[240,384]{1,0:T(8,128)(2,1)S(1)}, bf16[240,384]{1,0:T(8,128)(2,1)S(1)}, u32[]{:S(2)}, u32[]{:S(2)}) collective-permute-start(bf16[240,384]{1,0:T(8,128)(2,1)S(1)} %fusion.8), channel_id=1, source_target_pairs={{1,2},{2,1},{0,4},{3,7},{5,6},{6,5},{4,0},{7,3},{9,10},{10,9},{8,1... | collective-permute-start | bytes 552968 | tf_op jit(solution)/shard_map/ppermute | solution.py:570
  31.9 6.8 %collective-permute-start.33 = (bf16[240,384]{1,0:T(8,128)(2,1)S(1)}, bf16[240,384]{1,0:T(8,128)(2,1)S(1)}, u32[]{:S(2)}, u32[]{:S(2)}) collective-permute-start(bf16[240,384]{1,0:T(8,128)(2,1)S(1)} %shard_map.130), channel_id=1, source_target_pairs={{1,2},{2,1},{0,4},{3,7},{5,6},{6,5},{4,0},{7,3},{9,10},{10,9},{8,1... | collective-permute-start | bytes 552968 | tf_op jit(solution)/shard_map/ppermute | solution.py:570
  35.2 11.7 %collective-permute-start.36 = (bf16[240,384]{1,0:T(8,128)(2,1)S(1)}, bf16[240,384]{1,0:T(8,128)(2,1)S(1)}, u32[]{:S(2)}, u32[]{:S(2)}) collective-permute-start(bf16[240,384]{1,0:T(8,128)(2,1)S(1)} %fusion.12), channel_id=1, source_target_pairs={{1,2},{2,1},{0,4},{3,7},{5,6},{6,5},{4,0},{7,3},{9,10},{10,9},{8,1... | collective-permute-start | bytes 552968 | tf_op jit(solution)/shard_map/ppermute | solution.py:570
  35.4 8.9 %collective-permute-start.5 = (bf16[240,384]{1,0:T(8,128)(2,1)S(1)}, bf16[240,384]{1,0:T(8,128)(2,1)S(1)}, u32[]{:S(2)}, u32[]{:S(2)}) collective-permute-start(bf16[240,384]{1,0:T(8,128)(2,1)S(1)} %fusion), channel_id=1, source_target_pairs={{0,1},{1,0},{2,3},{3,2},{4,5},{5,4},{6,7},{7,6},{8,9},{9,8},{10,11... | collective-permute-start | bytes 552968 | tf_op jit(solution)/shard_map/ppermute | solution.py:33
  38.8 8.1 %collective-permute-start.34 = (bf16[240,384]{1,0:T(8,128)(2,1)S(1)}, bf16[240,384]{1,0:T(8,128)(2,1)S(1)}, u32[]{:S(2)}, u32[]{:S(2)}) collective-permute-start(bf16[240,384]{1,0:T(8,128)(2,1)S(1)} %fusion.4), channel_id=1, source_target_pairs={{0,1},{1,0},{2,3},{3,2},{4,5},{5,4},{6,7},{7,6},{8,9},{9,8},{10,11... | collective-permute-start | bytes 552968 | tf_op jit(solution)/shard_map/ppermute | solution.py:33
  44.5 7.9 %collective-permute-start.12 = (bf16[240,384]{1,0:T(8,128)(2,1)S(1)}, bf16[240,384]{1,0:T(8,128)(2,1)S(1)}, u32[]{:S(2)}, u32[]{:S(2)}) collective-permute-start(bf16[240,384]{1,0:T(8,128)(2,1)S(1)} %get-tuple-element.107.refs_7_), channel_id=1, source_target_pairs={{0,1},{1,0},{2,3},{3,2},{4,5},{5,4},{6,7},{7,6},{8,9},{9,8},{10,11... | collective-permute-start | bytes 552968 | tf_op jit(solution)/shard_map/ppermute | solution.py:33
  47.1 10.2 %collective-permute-start.37 = (bf16[240,384]{1,0:T(8,128)(2,1)S(1)}, bf16[240,384]{1,0:T(8,128)(2,1)S(1)}, u32[]{:S(2)}, u32[]{:S(2)}) collective-permute-start(bf16[240,384]{1,0:T(8,128)(2,1)S(1)} %get-tuple-element.134.refs_1_), channel_id=1, source_target_pairs={{0,1},{1,0},{2,3},{3,2},{4,5},{5,4},{6,7},{7,6},{8,9},{9,8},{10,11... | collective-permute-start | bytes 552968 | tf_op jit(solution)/shard_map/ppermute | solution.py:33
  48.8 12.8 %collective-permute-start.9 = (bf16[240,384]{1,0:T(8,128)(2,1)S(1)}, bf16[240,384]{1,0:T(8,128)(2,1)S(1)}, u32[]{:S(2)}, u32[]{:S(2)}) collective-permute-start(bf16[240,384]{1,0:T(8,128)(2,1)S(1)} %broadcast_select_fusion.11), channel_id=1, source_target_pairs={{0,1},{1,0},{2,3},{3,2},{4,5},{5,4},{6,7},{7,6},{8,9},{9,8},{10,11... | collective-permute-start | bytes 552968 | tf_op jit(solution)/shard_map/ppermute | solution.py:33
  52.3 9.9 %collective-permute-start.13 = (bf16[240,384]{1,0:T(8,128)(2,1)S(1)}, bf16[240,384]{1,0:T(8,128)(2,1)S(1)}, u32[]{:S(2)}, u32[]{:S(2)}) collective-permute-start(bf16[240,384]{1,0:T(8,128)(2,1)S(1)} %collective-permute-done.12.refs_8_), channel_id=1, source_target_pairs={{1,2},{2,1},{0,4},{3,7},{5,6},{6,5},{4,0},{7,3},{9,10},{10,9},{8,1... | collective-permute-start | bytes 552968 | tf_op jit(solution)/shard_map/ppermute | solution.py:570
  52.4 12.7 %collective-permute-start.39 = (bf16[240,384]{1,0:T(8,128)(2,1)S(1)}, bf16[240,384]{1,0:T(8,128)(2,1)S(1)}, u32[]{:S(2)}, u32[]{:S(2)}) collective-permute-start(bf16[240,384]{1,0:T(8,128)(2,1)S(1)} %broadcast_select_fusion.5), channel_id=1, source_target_pairs={{0,1},{1,0},{2,3},{3,2},{4,5},{5,4},{6,7},{7,6},{8,9},{9,8},{10,11... | collective-permute-start | bytes 552968 | tf_op jit(solution)/shard_map/ppermute | solution.py:33
  57.3 7.7 %collective-permute-start.40 = (bf16[240,384]{1,0:T(8,128)(2,1)S(1)}, bf16[240,384]{1,0:T(8,128)(2,1)S(1)}, u32[]{:S(2)}, u32[]{:S(2)}) collective-permute-start(bf16[240,384]{1,0:T(8,128)(2,1)S(1)} %collective-permute-done.37.refs_2_), channel_id=1, source_target_pairs={{1,2},{2,1},{0,4},{3,7},{5,6},{6,5},{4,0},{7,3},{9,10},{10,9},{8,1... | collective-permute-start | bytes 552968 | tf_op jit(solution)/shard_map/ppermute | solution.py:570
  62.3 9.4 %collective-permute-start.14 = (bf16[240,384]{1,0:T(8,128)(2,1)S(1)}, bf16[240,384]{1,0:T(8,128)(2,1)S(1)}, u32[]{:S(2)}, u32[]{:S(2)}) collective-permute-start(bf16[240,384]{1,0:T(8,128)(2,1)S(1)} %broadcast_select_fusion.10), channel_id=1, source_target_pairs={{0,1},{1,0},{2,3},{3,2},{4,5},{5,4},{6,7},{7,6},{8,9},{9,8},{10,11... | collective-permute-start | bytes 552968 | tf_op jit(solution)/shard_map/ppermute | solution.py:33
  65.0 10.3 %collective-permute-start.41 = (bf16[240,384]{1,0:T(8,128)(2,1)S(1)}, bf16[240,384]{1,0:T(8,128)(2,1)S(1)}, u32[]{:S(2)}, u32[]{:S(2)}) collective-permute-start(bf16[240,384]{1,0:T(8,128)(2,1)S(1)} %broadcast_select_fusion.4), channel_id=1, source_target_pairs={{0,1},{1,0},{2,3},{3,2},{4,5},{5,4},{6,7},{7,6},{8,9},{9,8},{10,11... | collective-permute-start | bytes 552968 | tf_op jit(solution)/shard_map/ppermute | solution.py:33
  65.2 6.7 %collective-permute-start.42 = (bf16[240,384]{1,0:T(8,128)(2,1)S(1)}, bf16[240,384]{1,0:T(8,128)(2,1)S(1)}, u32[]{:S(2)}, u32[]{:S(2)}) collective-permute-start(bf16[240,384]{1,0:T(8,128)(2,1)S(1)} %shard_map.133), channel_id=1, source_target_pairs={{1,2},{2,1},{0,4},{3,7},{5,6},{6,5},{4,0},{7,3},{9,10},{10,9},{8,1... | collective-permute-start | bytes 552968 | tf_op jit(solution)/shard_map/ppermute | solution.py:570
  65.3 13.1 %collective-permute-start.11 = (bf16[240,384]{1,0:T(8,128)(2,1)S(1)}, bf16[240,384]{1,0:T(8,128)(2,1)S(1)}, u32[]{:S(2)}, u32[]{:S(2)}) collective-permute-start(bf16[240,384]{1,0:T(8,128)(2,1)S(1)} %fusion.1), channel_id=1, source_target_pairs={{0,1},{1,0},{2,3},{3,2},{4,5},{5,4},{6,7},{7,6},{8,9},{9,8},{10,11... | collective-permute-start | bytes 552968 | tf_op jit(solution)/shard_map/ppermute | solution.py:33
  71.8 6.7 %collective-permute-start.15 = (bf16[240,384]{1,0:T(8,128)(2,1)S(1)}, bf16[240,384]{1,0:T(8,128)(2,1)S(1)}, u32[]{:S(2)}, u32[]{:S(2)}) collective-permute-start(bf16[240,384]{1,0:T(8,128)(2,1)S(1)} %fusion.9), channel_id=1, source_target_pairs={{1,2},{2,1},{0,4},{3,7},{5,6},{6,5},{4,0},{7,3},{9,10},{10,9},{8,1... | collective-permute-start | bytes 552968 | tf_op jit(solution)/shard_map/ppermute | solution.py:570
  71.9 13.7 %collective-permute-start.43 = (bf16[240,384]{1,0:T(8,128)(2,1)S(1)}, bf16[240,384]{1,0:T(8,128)(2,1)S(1)}, u32[]{:S(2)}, u32[]{:S(2)}) collective-permute-start(bf16[240,384]{1,0:T(8,128)(2,1)S(1)} %fusion.5), channel_id=1, source_target_pairs={{0,1},{1,0},{2,3},{3,2},{4,5},{5,4},{6,7},{7,6},{8,9},{9,8},{10,11... | collective-permute-start | bytes 552968 | tf_op jit(solution)/shard_map/ppermute | solution.py:33
  75.3 10.2 %collective-permute-start.44 = (bf16[240,384]{1,0:T(8,128)(2,1)S(1)}, bf16[240,384]{1,0:T(8,128)(2,1)S(1)}, u32[]{:S(2)}, u32[]{:S(2)}) collective-permute-start(bf16[240,384]{1,0:T(8,128)(2,1)S(1)} %fusion.13), channel_id=1, source_target_pairs={{1,2},{2,1},{0,4},{3,7},{5,6},{6,5},{4,0},{7,3},{9,10},{10,9},{8,1... | collective-permute-start | bytes 552968 | tf_op jit(solution)/shard_map/ppermute | solution.py:570
  78.6 10.8 %collective-permute-start.16 = (bf16[240,384]{1,0:T(8,128)(2,1)S(1)}, bf16[240,384]{1,0:T(8,128)(2,1)S(1)}, u32[]{:S(2)}, u32[]{:S(2)}) collective-permute-start(bf16[240,384]{1,0:T(8,128)(2,1)S(1)} %get-tuple-element.115.refs_9_.refs_0_.refs_7_), channel_id=1, source_target_pairs={{1,2},{2,1},{0,4},{3,7},{5,6},{6,5},{4,0},{7,3},{9,10},{10,9},{8,1... | collective-permute-start | bytes 552968 | tf_op jit(solution)/shard_map/ppermute | solution.py:570
  82.3 8.9 %collective-permute-start.20 = (bf16[240,384]{1,0:T(8,128)(2,1)S(1)}, bf16[240,384]{1,0:T(8,128)(2,1)S(1)}, u32[]{:S(2)}, u32[]{:S(2)}) collective-permute-start(bf16[240,384]{1,0:T(8,128)(2,1)S(1)} %get-tuple-element.115.refs_9_.refs_0_.refs_7_), channel_id=1, source_target_pairs={{0,1},{1,0},{2,3},{3,2},{4,5},{5,4},{6,7},{7,6},{8,9},{9,8},{10,11... | collective-permute-start | bytes 552968 | tf_op jit(solution)/shard_map/ppermute | solution.py:33
  85.7 8.6 %collective-permute-start.45 = (bf16[240,384]{1,0:T(8,128)(2,1)S(1)}, bf16[240,384]{1,0:T(8,128)(2,1)S(1)}, u32[]{:S(2)}, u32[]{:S(2)}) collective-permute-start(bf16[240,384]{1,0:T(8,128)(2,1)S(1)} %get-tuple-element.147.refs_3_.refs_1_), channel_id=1, source_target_pairs={{0,1},{1,0},{2,3},{3,2},{4,5},{5,4},{6,7},{7,6},{8,9},{9,8},{10,11... | collective-permute-start | bytes 552968 | tf_op jit(solution)/shard_map/ppermute | solution.py:33
  89.4 9.2 %collective-permute-start.17 = (bf16[240,384]{1,0:T(8,128)(2,1)S(1)}, bf16[240,384]{1,0:T(8,128)(2,1)S(1)}, u32[]{:S(2)}, u32[]{:S(2)}) collective-permute-start(bf16[240,384]{1,0:T(8,128)(2,1)S(1)} %broadcast_select_fusion.9), channel_id=1, source_target_pairs={{0,1},{1,0},{2,3},{3,2},{4,5},{5,4},{6,7},{7,6},{8,9},{9,8},{10,11... | collective-permute-start | bytes 552968 | tf_op jit(solution)/shard_map/ppermute | solution.py:33
  91.3 8.0 %collective-permute-start.21 = (bf16[240,384]{1,0:T(8,128)(2,1)S(1)}, bf16[240,384]{1,0:T(8,128)(2,1)S(1)}, u32[]{:S(2)}, u32[]{:S(2)}) collective-permute-start(bf16[240,384]{1,0:T(8,128)(2,1)S(1)} %collective-permute-done.20.refs_10_.refs_8_), channel_id=1, source_target_pairs={{1,2},{2,1},{0,4},{3,7},{5,6},{6,5},{4,0},{7,3},{9,10},{10,9},{8,1... | collective-permute-start | bytes 552968 | tf_op jit(solution)/shard_map/ppermute | solution.py:570
  91.3 10.8 %collective-permute-start.47 = (bf16[240,384]{1,0:T(8,128)(2,1)S(1)}, bf16[240,384]{1,0:T(8,128)(2,1)S(1)}, u32[]{:S(2)}, u32[]{:S(2)}) collective-permute-start(bf16[240,384]{1,0:T(8,128)(2,1)S(1)} %broadcast_select_fusion.3), channel_id=1, source_target_pairs={{0,1},{1,0},{2,3},{3,2},{4,5},{5,4},{6,7},{7,6},{8,9},{9,8},{10,11... | collective-permute-start | bytes 552968 | tf_op jit(solution)/shard_map/ppermute | solution.py:33
  94.3 7.4 %collective-permute-start.48 = (bf16[240,384]{1,0:T(8,128)(2,1)S(1)}, bf16[240,384]{1,0:T(8,128)(2,1)S(1)}, u32[]{:S(2)}, u32[]{:S(2)}) collective-permute-start(bf16[240,384]{1,0:T(8,128)(2,1)S(1)} %collective-permute-done.45.refs_4_.refs_2_), channel_id=1, source_target_pairs={{1,2},{2,1},{0,4},{3,7},{5,6},{6,5},{4,0},{7,3},{9,10},{10,9},{8,1... | collective-permute-start | bytes 552968 | tf_op jit(solution)/shard_map/ppermute | solution.py:570
  99.3 10.0 %collective-permute-start.22 = (bf16[240,384]{1,0:T(8,128)(2,1)S(1)}, bf16[240,384]{1,0:T(8,128)(2,1)S(1)}, u32[]{:S(2)}, u32[]{:S(2)}) collective-permute-start(bf16[240,384]{1,0:T(8,128)(2,1)S(1)} %broadcast_select_fusion.8), channel_id=1, source_target_pairs={{0,1},{1,0},{2,3},{3,2},{4,5},{5,4},{6,7},{7,6},{8,9},{9,8},{10,11... | collective-permute-start | bytes 552968 | tf_op jit(solution)/shard_map/ppermute | solution.py:33
  101.7 10.6 %collective-permute-start.49 = (bf16[240,384]{1,0:T(8,128)(2,1)S(1)}, bf16[240,384]{1,0:T(8,128)(2,1)S(1)}, u32[]{:S(2)}, u32[]{:S(2)}) collective-permute-start(bf16[240,384]{1,0:T(8,128)(2,1)S(1)} %broadcast_select_fusion.2), channel_id=1, source_target_pairs={{0,1},{1,0},{2,3},{3,2},{4,5},{5,4},{6,7},{7,6},{8,9},{9,8},{10,11... | collective-permute-start | bytes 552968 | tf_op jit(solution)/shard_map/ppermute | solution.py:33
  102.2 7.3 %collective-permute-start.50 = (bf16[240,384]{1,0:T(8,128)(2,1)S(1)}, bf16[240,384]{1,0:T(8,128)(2,1)S(1)}, u32[]{:S(2)}, u32[]{:S(2)}) collective-permute-start(bf16[240,384]{1,0:T(8,128)(2,1)S(1)} %shard_map.137), channel_id=1, source_target_pairs={{1,2},{2,1},{0,4},{3,7},{5,6},{6,5},{4,0},{7,3},{9,10},{10,9},{8,1... | collective-permute-start | bytes 552968 | tf_op jit(solution)/shard_map/ppermute | solution.py:570
  102.3 12.6 %collective-permute-start.19 = (bf16[240,384]{1,0:T(8,128)(2,1)S(1)}, bf16[240,384]{1,0:T(8,128)(2,1)S(1)}, u32[]{:S(2)}, u32[]{:S(2)}) collective-permute-start(bf16[240,384]{1,0:T(8,128)(2,1)S(1)} %fusion.2), channel_id=1, source_target_pairs={{0,1},{1,0},{2,3},{3,2},{4,5},{5,4},{6,7},{7,6},{8,9},{9,8},{10,11... | collective-permute-start | bytes 552968 | tf_op jit(solution)/shard_map/ppermute | solution.py:33
  109.4 5.6 %collective-permute-start.23 = (bf16[240,384]{1,0:T(8,128)(2,1)S(1)}, bf16[240,384]{1,0:T(8,128)(2,1)S(1)}, u32[]{:S(2)}, u32[]{:S(2)}) collective-permute-start(bf16[240,384]{1,0:T(8,128)(2,1)S(1)} %fusion.10), channel_id=1, source_target_pairs={{1,2},{2,1},{0,4},{3,7},{5,6},{6,5},{4,0},{7,3},{9,10},{10,9},{8,1... | collective-permute-start | bytes 552968 | tf_op jit(solution)/shard_map/ppermute | solution.py:570
  109.5 13.2 %collective-permute-start.51 = (bf16[240,384]{1,0:T(8,128)(2,1)S(1)}, bf16[240,384]{1,0:T(8,128)(2,1)S(1)}, u32[]{:S(2)}, u32[]{:S(2)}) collective-permute-start(bf16[240,384]{1,0:T(8,128)(2,1)S(1)} %fusion.6), channel_id=1, source_target_pairs={{0,1},{1,0},{2,3},{3,2},{4,5},{5,4},{6,7},{7,6},{8,9},{9,8},{10,11... | collective-permute-start | bytes 552968 | tf_op jit(solution)/shard_map/ppermute | solution.py:33
  112.4 10.3 %collective-permute-start.52 = (bf16[240,384]{1,0:T(8,128)(2,1)S(1)}, bf16[240,384]{1,0:T(8,128)(2,1)S(1)}, u32[]{:S(2)}, u32[]{:S(2)}) collective-permute-start(bf16[240,384]{1,0:T(8,128)(2,1)S(1)} %fusion.14), channel_id=1, source_target_pairs={{1,2},{2,1},{0,4},{3,7},{5,6},{6,5},{4,0},{7,3},{9,10},{10,9},{8,1... | collective-permute-start | bytes 552968 | tf_op jit(solution)/shard_map/ppermute | solution.py:570
  115.1 11.3 %collective-permute-start.24 = (bf16[240,384]{1,0:T(8,128)(2,1)S(1)}, bf16[240,384]{1,0:T(8,128)(2,1)S(1)}, u32[]{:S(2)}, u32[]{:S(2)}) collective-permute-start(bf16[240,384]{1,0:T(8,128)(2,1)S(1)} %get-tuple-element.124.refs_9_.refs_0_.refs_7_), channel_id=1, source_target_pairs={{1,2},{2,1},{0,4},{3,7},{5,6},{6,5},{4,0},{7,3},{9,10},{10,9},{8,1... | collective-permute-start | bytes 552968 | tf_op jit(solution)/shard_map/ppermute | solution.py:570
  118.7 9.7 %collective-permute-start.28 = (bf16[240,384]{1,0:T(8,128)(2,1)S(1)}, bf16[240,384]{1,0:T(8,128)(2,1)S(1)}, u32[]{:S(2)}, u32[]{:S(2)}) collective-permute-start(bf16[240,384]{1,0:T(8,128)(2,1)S(1)} %get-tuple-element.124.refs_9_.refs_0_.refs_7_), channel_id=1, source_target_pairs={{0,1},{1,0},{2,3},{3,2},{4,5},{5,4},{6,7},{7,6},{8,9},{9,8},{10,11... | collective-permute-start | bytes 552968 | tf_op jit(solution)/shard_map/ppermute | solution.py:33
  122.9 7.7 %collective-permute-start.53 = (bf16[240,384]{1,0:T(8,128)(2,1)S(1)}, bf16[240,384]{1,0:T(8,128)(2,1)S(1)}, u32[]{:S(2)}, u32[]{:S(2)}) collective-permute-start(bf16[240,384]{1,0:T(8,128)(2,1)S(1)} %get-tuple-element.163.refs_3_.refs_1_), channel_id=1, source_target_pairs={{0,1},{1,0},{2,3},{3,2},{4,5},{5,4},{6,7},{7,6},{8,9},{9,8},{10,11... | collective-permute-start | bytes 552968 | tf_op jit(solution)/shard_map/ppermute | solution.py:33
  126.4 7.6 %collective-permute-start.25 = (bf16[240,384]{1,0:T(8,128)(2,1)S(1)}, bf16[240,384]{1,0:T(8,128)(2,1)S(1)}, u32[]{:S(2)}, u32[]{:S(2)}) collective-permute-start(bf16[240,384]{1,0:T(8,128)(2,1)S(1)} %broadcast_select_fusion.7), channel_id=1, source_target_pairs={{0,1},{1,0},{2,3},{3,2},{4,5},{5,4},{6,7},{7,6},{8,9},{9,8},{10,11... | collective-permute-start | bytes 552968 | tf_op jit(solution)/shard_map/ppermute | solution.py:33
  128.4 5.7 %collective-permute-start.29 = (bf16[240,384]{1,0:T(8,128)(2,1)S(1)}, bf16[240,384]{1,0:T(8,128)(2,1)S(1)}, u32[]{:S(2)}, u32[]{:S(2)}) collective-permute-start(bf16[240,384]{1,0:T(8,128)(2,1)S(1)} %collective-permute-done.28.refs_10_.refs_8_), channel_id=1, source_target_pairs={{1,2},{2,1},{0,4},{3,7},{5,6},{6,5},{4,0},{7,3},{9,10},{10,9},{8,1... | collective-permute-start | bytes 552968 | tf_op jit(solution)/shard_map/ppermute | solution.py:570
  128.5 11.6 %collective-permute-start.55 = (bf16[240,384]{1,0:T(8,128)(2,1)S(1)}, bf16[240,384]{1,0:T(8,128)(2,1)S(1)}, u32[]{:S(2)}, u32[]{:S(2)}) collective-permute-start(bf16[240,384]{1,0:T(8,128)(2,1)S(1)} %broadcast_select_fusion.1), channel_id=1, source_target_pairs={{0,1},{1,0},{2,3},{3,2},{4,5},{5,4},{6,7},{7,6},{8,9},{9,8},{10,11... | collective-permute-start | bytes 552968 | tf_op jit(solution)/shard_map/ppermute | solution.py:33
  130.6 7.4 %collective-permute-start.56 = (bf16[240,384]{1,0:T(8,128)(2,1)S(1)}, bf16[240,384]{1,0:T(8,128)(2,1)S(1)}, u32[]{:S(2)}, u32[]{:S(2)}) collective-permute-start(bf16[240,384]{1,0:T(8,128)(2,1)S(1)} %collective-permute-done.53.refs_4_.refs_2_), channel_id=1, source_target_pairs={{1,2},{2,1},{0,4},{3,7},{5,6},{6,5},{4,0},{7,3},{9,10},{10,9},{8,1... | collective-permute-start | bytes 552968 | tf_op jit(solution)/shard_map/ppermute | solution.py:570
  134.1 6.1 %collective-permute-start.26 = (bf16[240,384]{1,0:T(8,128)(2,1)S(1)}, bf16[240,384]{1,0:T(8,128)(2,1)S(1)}, u32[]{:S(2)}, u32[]{:S(2)}) collective-permute-start(bf16[240,384]{1,0:T(8,128)(2,1)S(1)} %shard_map.129), channel_id=1, source_target_pairs={{1,2},{2,1},{0,4},{3,7},{5,6},{6,5},{4,0},{7,3},{9,10},{10,9},{8,1... | collective-permute-start | bytes 552968 | tf_op jit(solution)/shard_map/ppermute | solution.py:570
  134.2 13.5 %collective-permute-start.30 = (bf16[240,384]{1,0:T(8,128)(2,1)S(1)}, bf16[240,384]{1,0:T(8,128)(2,1)S(1)}, u32[]{:S(2)}, u32[]{:S(2)}) collective-permute-start(bf16[240,384]{1,0:T(8,128)(2,1)S(1)} %broadcast_select_fusion.6), channel_id=1, source_target_pairs={{0,1},{1,0},{2,3},{3,2},{4,5},{5,4},{6,7},{7,6},{8,9},{9,8},{10,11... | collective-permute-start | bytes 552968 | tf_op jit(solution)/shard_map/ppermute | solution.py:33
  138.1 9.5 %collective-permute-start.57 = (bf16[240,384]{1,0:T(8,128)(2,1)S(1)}, bf16[240,384]{1,0:T(8,128)(2,1)S(1)}, u32[]{:S(2)}, u32[]{:S(2)}) collective-permute-start(bf16[240,384]{1,0:T(8,128)(2,1)S(1)} %broadcast_select_fusion), channel_id=1, source_target_pairs={{0,1},{1,0},{2,3},{3,2},{4,5},{5,4},{6,7},{7,6},{8,9},{9,8},{10,11... | collective-permute-start | bytes 552968 | tf_op jit(solution)/shard_map/ppermute | solution.py:33
  140.3 13.3 %collective-permute-start.27 = (bf16[240,384]{1,0:T(8,128)(2,1)S(1)}, bf16[240,384]{1,0:T(8,128)(2,1)S(1)}, u32[]{:S(2)}, u32[]{:S(2)}) collective-permute-start(bf16[240,384]{1,0:T(8,128)(2,1)S(1)} %fusion.3), channel_id=1, source_target_pairs={{0,1},{1,0},{2,3},{3,2},{4,5},{5,4},{6,7},{7,6},{8,9},{9,8},{10,11... | collective-permute-start | bytes 552968 | tf_op jit(solution)/shard_map/ppermute | solution.py:33
  144.1 9.4 %collective-permute-start.59 = (bf16[240,384]{1,0:T(8,128)(2,1)S(1)}, bf16[240,384]{1,0:T(8,128)(2,1)S(1)}, u32[]{:S(2)}, u32[]{:S(2)}) collective-permute-start(bf16[240,384]{1,0:T(8,128)(2,1)S(1)} %fusion.7), channel_id=1, source_target_pairs={{0,1},{1,0},{2,3},{3,2},{4,5},{5,4},{6,7},{7,6},{8,9},{9,8},{10,11... | collective-permute-start | bytes 552968 | tf_op jit(solution)/shard_map/ppermute | solution.py:33
  147.6 5.8 %collective-permute-start.60 = (bf16[240,384]{1,0:T(8,128)(2,1)S(1)}, bf16[240,384]{1,0:T(8,128)(2,1)S(1)}, u32[]{:S(2)}, u32[]{:S(2)}) collective-permute-start(bf16[240,384]{1,0:T(8,128)(2,1)S(1)} %fusion.15), channel_id=1, source_target_pairs={{1,2},{2,1},{0,4},{3,7},{5,6},{6,5},{4,0},{7,3},{9,10},{10,9},{8,1... | collective-permute-start | bytes 552968 | tf_op jit(solution)/shard_map/ppermute | solution.py:570
  147.8 5.8 %collective-permute-start.31 = (bf16[240,384]{1,0:T(8,128)(2,1)S(1)}, bf16[240,384]{1,0:T(8,128)(2,1)S(1)}, u32[]{:S(2)}, u32[]{:S(2)}) collective-permute-start(bf16[240,384]{1,0:T(8,128)(2,1)S(1)} %fusion.11), channel_id=1, source_target_pairs={{1,2},{2,1},{0,4},{3,7},{5,6},{6,5},{4,0},{7,3},{9,10},{10,9},{8,1... | collective-permute-start | bytes 552968 | tf_op jit(solution)/shard_map/ppermute | solution.py:570
  154.4 7.3 %collective-permute-start.66 = (bf16[256,384]{1,0:T(8,128)(2,1)S(1)}, bf16[256,384]{1,0:T(8,128)(2,1)S(1)}, u32[]{:S(2)}, u32[]{:S(2)}) collective-permute-start(bf16[256,384]{1,0:T(8,128)(2,1)S(1)} %get-tuple-element.179.refs_0_.refs_10_.refs_7_), channel_id=1, source_target_pairs={{0,1},{1,0},{2,3},{3,2},{4,5},{5,4},{6,7},{7,6},{8,9},{9,8},{10,11... | collective-permute-start | bytes 589832 | tf_op jit(solution)/shard_map/ppermute | solution.py:33
  158.1 5.7 %collective-permute-start.61 = (bf16[240,384]{1,0:T(8,128)(2,1)S(1)}, bf16[240,384]{1,0:T(8,128)(2,1)S(1)}, u32[]{:S(2)}, u32[]{:S(2)}) collective-permute-start(bf16[240,384]{1,0:T(8,128)(2,1)S(1)} %get-tuple-element.186.refs_4_.refs_1_), channel_id=1, source_target_pairs={{0,1},{1,0},{2,3},{3,2},{4,5},{5,4},{6,7},{7,6},{8,9},{9,8},{10,11... | collective-permute-start | bytes 552968 | tf_op jit(solution)/shard_map/ppermute | solution.py:33
  158.1 5.6 %collective-permute-start.67 = (bf16[256,384]{1,0:T(8,128)(2,1)S(1)}, bf16[256,384]{1,0:T(8,128)(2,1)S(1)}, u32[]{:S(2)}, u32[]{:S(2)}) collective-permute-start(bf16[256,384]{1,0:T(8,128)(2,1)S(1)} %get-tuple-element.179.refs_0_.refs_10_.refs_7_), channel_id=1, source_target_pairs={{1,2},{2,1},{0,4},{3,7},{5,6},{6,5},{4,0},{7,3},{9,10},{10,9},{8,1... | collective-permute-start | bytes 589832 | tf_op jit(solution)/shard_map/ppermute | solution.py:570
  161.7 6.2 %collective-permute-start.69 = (bf16[256,384]{1,0:T(8,128)(2,1)S(1)}, bf16[256,384]{1,0:T(8,128)(2,1)S(1)}, u32[]{:S(2)}, u32[]{:S(2)}) collective-permute-start(bf16[256,384]{1,0:T(8,128)(2,1)S(1)} %collective-permute-done.66.refs_11_.refs_8_), channel_id=1, source_target_pairs={{1,2},{2,1},{0,4},{3,7},{5,6},{6,5},{4,0},{7,3},{9,10},{10,9},{8,1... | collective-permute-start | bytes 589832 | tf_op jit(solution)/shard_map/ppermute | solution.py:570
  161.7 10.4 %collective-permute-start.62 = (bf16[240,384]{1,0:T(8,128)(2,1)S(1)}, bf16[240,384]{1,0:T(8,128)(2,1)S(1)}, u32[]{:S(2)}, u32[]{:S(2)}) collective-permute-start(bf16[240,384]{1,0:T(8,128)(2,1)S(1)} %get-tuple-element.186.refs_4_.refs_1_), channel_id=1, source_target_pairs={{1,2},{2,1},{0,4},{3,7},{5,6},{6,5},{4,0},{7,3},{9,10},{10,9},{8,1... | collective-permute-start | bytes 552968 | tf_op jit(solution)/shard_map/ppermute | solution.py:570
  163.7 10.6 %collective-permute-start.64 = (bf16[240,384]{1,0:T(8,128)(2,1)S(1)}, bf16[240,384]{1,0:T(8,128)(2,1)S(1)}, u32[]{:S(2)}, u32[]{:S(2)}) collective-permute-start(bf16[240,384]{1,0:T(8,128)(2,1)S(1)} %collective-permute-done.61.refs_5_.refs_2_), channel_id=1, source_target_pairs={{1,2},{2,1},{0,4},{3,7},{5,6},{6,5},{4,0},{7,3},{9,10},{10,9},{8,1... | collective-permute-start | bytes 552968 | tf_op jit(solution)/shard_map/ppermute | solution.py:570
  163.7 17.5 %collective-permute-start.68 = (bf16[256,384]{1,0:T(8,128)(2,1)S(1)}, bf16[256,384]{1,0:T(8,128)(2,1)S(1)}, u32[]{:S(2)}, u32[]{:S(2)}) collective-permute-start(bf16[256,384]{1,0:T(8,128)(2,1)S(1)} %collective-permute-done.67.refs_13_.refs_10_), channel_id=1, source_target_pairs={{0,1},{1,0},{2,3},{3,2},{4,5},{5,4},{6,7},{7,6},{8,9},{9,8},{10,11... | collective-permute-start | bytes 589832 | tf_op jit(solution)/shard_map/ppermute | solution.py:33
  167.9 15.2 %collective-permute-start.70 = (bf16[256,384]{1,0:T(8,128)(2,1)S(1)}, bf16[256,384]{1,0:T(8,128)(2,1)S(1)}, u32[]{:S(2)}, u32[]{:S(2)}) collective-permute-start(bf16[256,384]{1,0:T(8,128)(2,1)S(1)} %collective-permute-done.69.refs_15_.refs_12_), channel_id=1, source_target_pairs={{0,1},{1,0},{2,3},{3,2},{4,5},{5,4},{6,7},{7,6},{8,9},{9,8},{10,11... | collective-permute-start | bytes 589832 | tf_op jit(solution)/shard_map/ppermute | solution.py:33
  172.1 9.0 %collective-permute-start.63 = (bf16[240,384]{1,0:T(8,128)(2,1)S(1)}, bf16[240,384]{1,0:T(8,128)(2,1)S(1)}, u32[]{:S(2)}, u32[]{:S(2)}) collective-permute-start(bf16[240,384]{1,0:T(8,128)(2,1)S(1)} %collective-permute-done.62.refs_7_.refs_4_), channel_id=1, source_target_pairs={{0,1},{1,0},{2,3},{3,2},{4,5},{5,4},{6,7},{7,6},{8,9},{9,8},{10,11... | collective-permute-start | bytes 552968 | tf_op jit(solution)/shard_map/ppermute | solution.py:33
  174.3 8.8 %collective-permute-start.65 = (bf16[240,384]{1,0:T(8,128)(2,1)S(1)}, bf16[240,384]{1,0:T(8,128)(2,1)S(1)}, u32[]{:S(2)}, u32[]{:S(2)}) collective-permute-start(bf16[240,384]{1,0:T(8,128)(2,1)S(1)} %collective-permute-done.64.refs_9_.refs_6_), channel_id=1, source_target_pairs={{0,1},{1,0},{2,3},{3,2},{4,5},{5,4},{6,7},{7,6},{8,9},{9,8},{10,11... | collective-permute-start | bytes 552968 | tf_op jit(solution)/shard_map/ppermute | solution.py:33
  188.6 8.8 %collective-permute-start.72 = (bf16[272,512]{1,0:T(8,128)(2,1)S(1)}, bf16[272,512]{1,0:T(8,128)(2,1)S(1)}, u32[]{:S(2)}, u32[]{:S(2)}) collective-permute-start(bf16[272,512]{1,0:T(8,128)(2,1)S(1)} %slice_bitcast_fusion), channel_id=1, source_target_pairs={{0,8},{4,12},{8,0},{12,4},{1,9},{5,13},{9,1},{13,5},{2,10},{6,14},... | collective-permute-start | bytes 835592 | tf_op jit(solution)/shard_map/ppermute | solution.py:33
  (11 other events, 49.9 us)

commit v12 on v10

--- a/solution.py
+++ b/solution.py
@@ -531,6 +531,9 @@
             pairs += [(p * n + 1, p * n + 2), (p * n + 2, p * n + 1)]
             pairs += [(p * n + end, (p ^ 1) * n + end) for end in (0, n - 1)]
         return lax.ppermute(value, ("expert", "dp"), pairs)
+
+    def mirror(value):
+        return along_z.send(value, [(0, 3), (3, 0), (1, 2), (2, 1)])
 
     def unless_end(value):
         return jnp.where(at_end, jnp.zeros_like(value), value)
@@ -591,9 +594,8 @@
         halves = []
         for h in streams:
             y, got_a, got_b = flight[h]
-            a1, b1 = outer(got_b), inner(got_a)
-            a2 = outer(b1)
-            halves.append([(y,), (got_a,), (a1, got_b), (a2, b1)])
+            a1, far_end = outer(got_b), mirror(jnp.where(at_end, y, got_a))
+            halves.append([(y,), (got_a,), (a1, got_b), (far_end,)])
         wait = [grad_token]
     else:
         begun = []

time: 196 us -> 194 us (0.990)
  waiting for transfers between devices: 54.7 us -> 52 us
    ppermute x43, waiting for transfers between devices: 54.6 us -> 51.8 us  [send(): return lax.ppermute(value, self.axis, wide)]
    ppermute x43, starting transfers between devices: 92.2 us -> 94.2 us  [send(): return lax.ppermute(value, self.axis, wide)]
  transfers between devices with their start and end apart: 75 -> 73, of which waited for: 21 -> 19; matrix products, arithmetic and copies ran while one was open for 1% -> 1% of each run, Pallas kernels for 17% -> 17%
where the time goes in v12:
time: 194 us
  starting transfers between devices  96.9 us (50%)
  waiting for transfers between devices  52 us (27%)
  Pallas kernels  40.7 us (21%)
  other arithmetic  2.22 us (1%)
    ppermute x43, starting transfers between devices, send(): return lax.ppermute(value, self.axis, wide)  94.2 us
    ppermute x43, waiting for transfers between devices, send(): return lax.ppermute(value, self.axis, wide)  51.8 us
    pallas_call x4, Pallas kernels, pre(): call(functools.partial(pre_kernel, n, e, choose, len(deps)), 1, [SMEM_SPE...  14.7 us
    pallas_call x4, Pallas kernels, grad(): call(functools.partial(grad_kernel, n, e > 0, sizes_of(halves[0]), len(de...  13.4 us
    pallas_call x4, Pallas kernels, out(): call(functools.partial(out_kernel, n, e, e > 0, last, sizes_of(halves[0])...  9.39 us
  transfers between devices with their start and end apart: 73, of which 19 were waited for; matrix products, arithmetic and copies ran while one was open for 1% of the time, Pallas kernels for 17%

profile of v12, /device:TPU:0, one launch (start us, length us, event | category | flops | bytes accessed | tf_op | source)
XLA Modules:
  0.0 193.9 jit_solution(9832554663983271328)
XLA Ops:
  0.6 1.0 shard_map.118.refs_0_.refs_1_
  1.7 3.0 %collective-permute-start = (bf16[272,512]{1,0:T(8,128)(2,1)S(1)}, bf16[272,512]{1,0:T(8,128)(2,1)S(1)}, u32[]{:S(2)}, u32[]{:S(2)}) collective-permute-start(bf16[272,512]{1,0:T(8,128)(2,1)S(1)} %shard_map.118.refs_0_.refs_1_), channel_id=1, source_target_pairs={{0,8},{4,12},{8,0},{12,4},{1,9},{5,13},{9,1},{13,5},{2,10},{6,14},... | collective-permute-start | bytes 835592 | tf_op jit(solution)/shard_map/ppermute | solution.py:33
  4.7 6.7 %collective-permute-done.refs_1_.refs_2_ = bf16[272,512]{1,0:T(8,128)(2,1)S(1)} collective-permute-done((bf16[272,512]{1,0:T(8,128)(2,1)S(1)}, bf16[272,512]{1,0:T(8,128)(2,1)S(1)}, u32[]{:S(2)}, u32[]{:S(2)}) %collective-permute-start) | collective-permute-done | bytes 278560 | tf_op jit(solution)/shard_map/ppermute | solution.py:33
  11.4 1.5 collective-permute-done.2.refs_3_.refs_4_
  12.9 3.6 %shard_map.119 = (bf16[320,512]{1,0:T(8,128)(2,1)S(1)}, bf16[320,512]{1,0:T(8,128)(2,1)S(1)}, bf16[240,384]{1,0:T(8,128)(2,1)S(1)}, bf16[240,384]{1,0:T(8,128)(2...) custom-call(s32[10]{0:T(128)S(1)} %stack.35.scal, ...), custom_call_target="tpu_custom_call" | custom-call | flops 754974720 | bytes 3833856 | tf_op jit(solution)/shard_map/pallas_call | solution.py:427
  16.4 1.9 collective-permute-start.3
  18.5 1.8 collective-permute-start.32
  20.6 3.7 %shard_map.123 = (bf16[320,512]{1,0:T(8,128)(2,1)S(1)}, bf16[320,512]{1,0:T(8,128)(2,1)S(1)}, bf16[240,384]{1,0:T(8,128)(2,1)S(1)}, bf16[240,384]{1,0:T(8,128)(2...) custom-call(s32[10]{0:T(128)S(1)} %stack.35.scal, ...), custom_call_target="tpu_custom_call" | custom-call | flops 754974720 | bytes 3833856 | tf_op jit(solution)/shard_map/pallas_call | solution.py:427
  24.4 3.5 %collective-permute-done.6 = bf16[240,384]{1,0:T(8,128)(2,1)S(1)} collective-permute-done((bf16[240,384]{1,0:T(8,128)(2,1)S(1)}, bf16[240,384]{1,0:T(8,128)(2,1)S(1)}, u32[]{:S(2)}, u32[]{:S(2)}) %collective-permute-start.6) | collective-permute-done | bytes 184352 | tf_op jit(solution)/shard_map/ppermute | solution.py:33
  28.1 3.8 %collective-permute-done.32.refs_2_ = bf16[240,384]{1,0:T(8,128)(2,1)S(1)} collective-permute-done((bf16[240,384]{1,0:T(8,128)(2,1)S(1)}, bf16[240,384]{1,0:T(8,128)(2,1)S(1)}, u32[]{:S(2)}, u32[]{:S(2)}) %collective-permute-start.32) | collective-permute-done | bytes 184352 | tf_op jit(solution)/shard_map/ppermute | solution.py:33
  32.0 3.1 %collective-permute-done.35 = bf16[240,384]{1,0:T(8,128)(2,1)S(1)} collective-permute-done((bf16[240,384]{1,0:T(8,128)(2,1)S(1)}, bf16[240,384]{1,0:T(8,128)(2,1)S(1)}, u32[]{:S(2)}, u32[]{:S(2)}) %collective-permute-start.35) | collective-permute-done | bytes 184352 | tf_op jit(solution)/shard_map/ppermute | solution.py:33
  35.3 3.4 %collective-permute-start.5 = (bf16[240,384]{1,0:T(8,128)(2,1)S(1)}, bf16[240,384]{1,0:T(8,128)(2,1)S(1)}, u32[]{:S(2)}, u32[]{:S(2)}) collective-permute-start(bf16[240,384]{1,0:T(8,128)(2,1)S(1)} %fusion.1), channel_id=1, source_target_pairs={{0,1},{1,0},{2,3},{3,2},{4,5},{5,4},{6,7},{7,6},{8,9},{9,8},{10,11... | collective-permute-start | bytes 552968 | tf_op jit(solution)/shard_map/ppermute | solution.py:33
  38.8 1.8 collective-permute-start.34
  40.6 3.7 %collective-permute-done.5.refs_1_ = bf16[240,384]{1,0:T(8,128)(2,1)S(1)} collective-permute-done((bf16[240,384]{1,0:T(8,128)(2,1)S(1)}, bf16[240,384]{1,0:T(8,128)(2,1)S(1)}, u32[]{:S(2)}, u32[]{:S(2)}) %collective-permute-start.5) | collective-permute-done | bytes 184352 | tf_op jit(solution)/shard_map/ppermute | solution.py:33
  44.5 2.4 %collective-permute-start.12 = (bf16[240,384]{1,0:T(8,128)(2,1)S(1)}, bf16[240,384]{1,0:T(8,128)(2,1)S(1)}, u32[]{:S(2)}, u32[]{:S(2)}) collective-permute-start(bf16[240,384]{1,0:T(8,128)(2,1)S(1)} %get-tuple-element.109.refs_7_), channel_id=1, source_target_pairs={{0,1},{1,0},{2,3},{3,2},{4,5},{5,4},{6,7},{7,6},{8,9},{9,8},{10,11... | collective-permute-start | bytes 552968 | tf_op jit(solution)/shard_map/ppermute | solution.py:33
  47.0 1.7 collective-permute-start.37
  48.8 3.5 %collective-permute-start.9 = (bf16[240,384]{1,0:T(8,128)(2,1)S(1)}, bf16[240,384]{1,0:T(8,128)(2,1)S(1)}, u32[]{:S(2)}, u32[]{:S(2)}) collective-permute-start(bf16[240,384]{1,0:T(8,128)(2,1)S(1)} %broadcast_select_fusion.13), channel_id=1, source_target_pairs={{0,1},{1,0},{2,3},{3,2},{4,5},{5,4},{6,7},{7,6},{8,9},{9,8},{10,11... | collective-permute-start | bytes 552968 | tf_op jit(solution)/shard_map/ppermute | solution.py:33
  52.4 4.9 %collective-permute-start.39 = (bf16[240,384]{1,0:T(8,128)(2,1)S(1)}, bf16[240,384]{1,0:T(8,128)(2,1)S(1)}, u32[]{:S(2)}, u32[]{:S(2)}) collective-permute-start(bf16[240,384]{1,0:T(8,128)(2,1)S(1)} %broadcast_select_fusion.7), channel_id=1, source_target_pairs={{0,1},{1,0},{2,3},{3,2},{4,5},{5,4},{6,7},{7,6},{8,9},{9,8},{10,11... | collective-permute-start | bytes 552968 | tf_op jit(solution)/shard_map/ppermute | solution.py:33
  57.3 3.7 %shard_map.122 = (bf16[320,512]{1,0:T(8,128)(2,1)S(1)}, bf16[320,512]{1,0:T(8,128)(2,1)S(1)}, bf16[240,384]{1,0:T(8,128)(2,1)S(1)}, bf16[240,384]{1,0:T(8,128)(2...) custom-call(s32[10]{0:T(128)S(1)} %stack.35.scal, ...), custom_call_target="tpu_custom_call" | custom-call | flops 754974720 | bytes 3833856 | tf_op jit(solution)/shard_map/pallas_call | solution.py:427
  61.7 2.7 %collective-permute-start.14 = (bf16[240,384]{1,0:T(8,128)(2,1)S(1)}, bf16[240,384]{1,0:T(8,128)(2,1)S(1)}, u32[]{:S(2)}, u32[]{:S(2)}) collective-permute-start(bf16[240,384]{1,0:T(8,128)(2,1)S(1)} %broadcast_select_fusion.12), channel_id=1, source_target_pairs={{0,1},{1,0},{2,3},{3,2},{4,5},{5,4},{6,7},{7,6},{8,9},{9,8},{10,11... | collective-permute-start | bytes 552968 | tf_op jit(solution)/shard_map/ppermute | solution.py:33
  64.4 1.2 collective-permute-start.41
  65.8 4.9 %collective-permute-start.11 = (bf16[240,384]{1,0:T(8,128)(2,1)S(1)}, bf16[240,384]{1,0:T(8,128)(2,1)S(1)}, u32[]{:S(2)}, u32[]{:S(2)}) collective-permute-start(bf16[240,384]{1,0:T(8,128)(2,1)S(1)} %fusion.2), channel_id=1, source_target_pairs={{0,1},{1,0},{2,3},{3,2},{4,5},{5,4},{6,7},{7,6},{8,9},{9,8},{10,11... | collective-permute-start | bytes 552968 | tf_op jit(solution)/shard_map/ppermute | solution.py:33
  70.9 3.3 %collective-permute-start.43 = (bf16[240,384]{1,0:T(8,128)(2,1)S(1)}, bf16[240,384]{1,0:T(8,128)(2,1)S(1)}, u32[]{:S(2)}, u32[]{:S(2)}) collective-permute-start(bf16[240,384]{1,0:T(8,128)(2,1)S(1)} %fusion.6), channel_id=1, source_target_pairs={{0,1},{1,0},{2,3},{3,2},{4,5},{5,4},{6,7},{7,6},{8,9},{9,8},{10,11... | collective-permute-start | bytes 552968 | tf_op jit(solution)/shard_map/ppermute | solution.py:33
  74.4 3.5 %collective-permute-done.11.refs_1_ = bf16[240,384]{1,0:T(8,128)(2,1)S(1)} collective-permute-done((bf16[240,384]{1,0:T(8,128)(2,1)S(1)}, bf16[240,384]{1,0:T(8,128)(2,1)S(1)}, u32[]{:S(2)}, u32[]{:S(2)}) %collective-permute-start.11) | collective-permute-done | bytes 184352 | tf_op jit(solution)/shard_map/ppermute | solution.py:33
  78.1 2.2 %shard_map.132 = (f32[2,2,128,512]{3,2,1,0:T(8,128)S(1)}, f32[2,2,128,512]{3,2,1,0:T(8,128)S(1)}, f32[8,128]{1,0:T(8,128)S(1)}) custom-call(s32[10]{0:T(128)S(1)} %stack.35.scal, f32[4,16,128]{2,1,0:T(8,128)S(1)} %get-tuple-element.135.refs_0_.refs_1_, bf16[240,384]{1,0:T(8,128)(2,1)S(1)} %get-tuple-element.136.refs_1_, ...), custom_call_target="tpu_custom_call" | custom-call | flops 754974720 | bytes 4571136 | tf_op jit(solution)/shard_map/pallas_call | solution.py:484
  80.3 3.3 %collective-permute-start.20 = (bf16[240,384]{1,0:T(8,128)(2,1)S(1)}, bf16[240,384]{1,0:T(8,128)(2,1)S(1)}, u32[]{:S(2)}, u32[]{:S(2)}) collective-permute-start(bf16[240,384]{1,0:T(8,128)(2,1)S(1)} %get-tuple-element.117.refs_9_.refs_0_.refs_7_), channel_id=1, source_target_pairs={{0,1},{1,0},{2,3},{3,2},{4,5},{5,4},{6,7},{7,6},{8,9},{9,8},{10,11... | collective-permute-start | bytes 552968 | tf_op jit(solution)/shard_map/ppermute | solution.py:33
  83.8 3.5 %shard_map.136 = (bf16[4,512,768]{2,1,0:T(8,128)(2,1)}, bf16[4,512,768]{2,1,0:T(8,128)(2,1)}, bf16[4,768,512]{2,1,0:T(8,128)(2,1)}, f32[8,128]{1,0:T(8,128)S(1)}) custom-call(s32[10]{0:T(128)S(1)} %stack.35.scal, bf16[320,512]{1,0:T(8,128)(2,1)S(1)} %get-tuple-element.158.in_ref, bf16[320,512]{1,0:T(8,128)(2,1)S(1)} %get-tuple-element.159.cot_ref, ...), custom_call_target="tpu_custom_call" | custom-call | flops 754974720 | bytes 4571136 | tf_op jit(solution)/shard_map/pallas_call | solution.py:508
  87.4 1.9 collective-permute-start.17
  89.3 2.1 %collective-permute-start.47 = (bf16[240,384]{1,0:T(8,128)(2,1)S(1)}, bf16[240,384]{1,0:T(8,128)(2,1)S(1)}, u32[]{:S(2)}, u32[]{:S(2)}) collective-permute-start(bf16[240,384]{1,0:T(8,128)(2,1)S(1)} %broadcast_select_fusion.5), channel_id=1, source_target_pairs={{0,1},{1,0},{2,3},{3,2},{4,5},{5,4},{6,7},{7,6},{8,9},{9,8},{10,11... | collective-permute-start | bytes 552968 | tf_op jit(solution)/shard_map/ppermute | solution.py:33
  91.4 0.8 collective-permute-done.45.refs_4_.refs_2_
  92.2 3.7 %shard_map.126 = (bf16[320,512]{1,0:T(8,128)(2,1)S(1)}, bf16[320,512]{1,0:T(8,128)(2,1)S(1)}, bf16[240,384]{1,0:T(8,128)(2,1)S(1)}, bf16[240,384]{1,0:T(8,128)(2...) custom-call(s32[10]{0:T(128)S(1)} %stack.35.scal, ...), custom_call_target="tpu_custom_call" | custom-call | flops 754974720 | bytes 3833856 | tf_op jit(solution)/shard_map/pallas_call | solution.py:427
  96.6 2.3 %collective-permute-start.22 = (bf16[240,384]{1,0:T(8,128)(2,1)S(1)}, bf16[240,384]{1,0:T(8,128)(2,1)S(1)}, u32[]{:S(2)}, u32[]{:S(2)}) collective-permute-start(bf16[240,384]{1,0:T(8,128)(2,1)S(1)} %broadcast_select_fusion.10), channel_id=1, source_target_pairs={{0,1},{1,0},{2,3},{3,2},{4,5},{5,4},{6,7},{7,6},{8,9},{9,8},{10,11... | collective-permute-start | bytes 552968 | tf_op jit(solution)/shard_map/ppermute | solution.py:33
  99.0 1.2 collective-permute-start.49
  100.4 5.6 %collective-permute-start.19 = (bf16[240,384]{1,0:T(8,128)(2,1)S(1)}, bf16[240,384]{1,0:T(8,128)(2,1)S(1)}, u32[]{:S(2)}, u32[]{:S(2)}) collective-permute-start(bf16[240,384]{1,0:T(8,128)(2,1)S(1)} %fusion.3), channel_id=1, source_target_pairs={{0,1},{1,0},{2,3},{3,2},{4,5},{5,4},{6,7},{7,6},{8,9},{9,8},{10,11... | collective-permute-start | bytes 552968 | tf_op jit(solution)/shard_map/ppermute | solution.py:33
  106.3 3.7 %collective-permute-start.51 = (bf16[240,384]{1,0:T(8,128)(2,1)S(1)}, bf16[240,384]{1,0:T(8,128)(2,1)S(1)}, u32[]{:S(2)}, u32[]{:S(2)}) collective-permute-start(bf16[240,384]{1,0:T(8,128)(2,1)S(1)} %fusion.7), channel_id=1, source_target_pairs={{0,1},{1,0},{2,3},{3,2},{4,5},{5,4},{6,7},{7,6},{8,9},{9,8},{10,11... | collective-permute-start | bytes 552968 | tf_op jit(solution)/shard_map/ppermute | solution.py:33
  110.1 2.2 %collective-permute-done.19.refs_1_ = bf16[240,384]{1,0:T(8,128)(2,1)S(1)} collective-permute-done((bf16[240,384]{1,0:T(8,128)(2,1)S(1)}, bf16[240,384]{1,0:T(8,128)(2,1)S(1)}, u32[]{:S(2)}, u32[]{:S(2)}) %collective-permute-start.19) | collective-permute-done | bytes 184352 | tf_op jit(solution)/shard_map/ppermute | solution.py:33
  112.6 2.2 %shard_map.135 = (f32[2,2,128,512]{3,2,1,0:T(8,128)S(1)}, f32[2,2,128,512]{3,2,1,0:T(8,128)S(1)}, f32[8,128]{1,0:T(8,128)S(1)}) custom-call(s32[10]{0:T(128)S(1)} %stack.35.scal, f32[4,16,128]{2,1,0:T(8,128)S(1)} %get-tuple-element.135.refs_0_.refs_1_, f32[2,2,128,512]{3,2,1,0:T(8,128)S(1)} %get-tuple-element.147.refs_1_, ...), custom_call_target="tpu_custom_call" | custom-call | flops 754974720 | bytes 4571136 | tf_op jit(solution)/shard_map/pallas_call | solution.py:484
  114.8 3.3 %collective-permute-start.28 = (bf16[240,384]{1,0:T(8,128)(2,1)S(1)}, bf16[240,384]{1,0:T(8,128)(2,1)S(1)}, u32[]{:S(2)}, u32[]{:S(2)}) collective-permute-start(bf16[240,384]{1,0:T(8,128)(2,1)S(1)} %get-tuple-element.126.refs_9_.refs_0_.refs_7_), channel_id=1, source_target_pairs={{0,1},{1,0},{2,3},{3,2},{4,5},{5,4},{6,7},{7,6},{8,9},{9,8},{10,11... | collective-permute-start | bytes 552968 | tf_op jit(solution)/shard_map/ppermute | solution.py:33
  118.4 3.3 %shard_map.140 = (bf16[4,512,768]{2,1,0:T(8,128)(2,1)}, bf16[4,512,768]{2,1,0:T(8,128)(2,1)}, bf16[4,768,512]{2,1,0:T(8,128)(2,1)}, f32[8,128]{1,0:T(8,128)S(1)}) custom-call(s32[10]{0:T(128)S(1)} %stack.35.scal, bf16[320,512]{1,0:T(8,128)(2,1)S(1)} %get-tuple-element.174.in_ref, ...), custom_call_target="tpu_custom_call", output_to_operand_aliasing={{0}: (16, {}), {1}: (17, {}), {2}: (18, {})} | custom-call | flops 754974720 | bytes 4571136 | tf_op jit(solution)/shard_map/pallas_call | solution.py:508
  121.7 2.0 %collective-permute-start.25 = (bf16[240,384]{1,0:T(8,128)(2,1)S(1)}, bf16[240,384]{1,0:T(8,128)(2,1)S(1)}, u32[]{:S(2)}, u32[]{:S(2)}) collective-permute-start(bf16[240,384]{1,0:T(8,128)(2,1)S(1)} %broadcast_select_fusion.9), channel_id=1, source_target_pairs={{0,1},{1,0},{2,3},{3,2},{4,5},{5,4},{6,7},{7,6},{8,9},{9,8},{10,11... | collective-permute-start | bytes 552968 | tf_op jit(solution)/shard_map/ppermute | solution.py:33
  123.8 2.2 %collective-permute-start.55 = (bf16[240,384]{1,0:T(8,128)(2,1)S(1)}, bf16[240,384]{1,0:T(8,128)(2,1)S(1)}, u32[]{:S(2)}, u32[]{:S(2)}) collective-permute-start(bf16[240,384]{1,0:T(8,128)(2,1)S(1)} %broadcast_select_fusion.3), channel_id=1, source_target_pairs={{0,1},{1,0},{2,3},{3,2},{4,5},{5,4},{6,7},{7,6},{8,9},{9,8},{10,11... | collective-permute-start | bytes 552968 | tf_op jit(solution)/shard_map/ppermute | solution.py:33
  126.0 0.8 collective-permute-done.53.refs_4_.refs_2_
  126.7 3.9 %collective-permute-done.25.refs_1_.refs_11_.refs_9_ = bf16[240,384]{1,0:T(8,128)(2,1)S(1)} collective-permute-done((bf16[240,384]{1,0:T(8,128)(2,1)S(1)}, bf16[240,384]{1,0:T(8,128)(2,1)S(1)}, u32[]{:S(2)}, u32[]{:S(2)}) %collective-permute-start.25) | collective-permute-done | bytes 184352 | tf_op jit(solution)/shard_map/ppermute | solution.py:33
  130.8 2.7 %collective-permute-start.30 = (bf16[240,384]{1,0:T(8,128)(2,1)S(1)}, bf16[240,384]{1,0:T(8,128)(2,1)S(1)}, u32[]{:S(2)}, u32[]{:S(2)}) collective-permute-start(bf16[240,384]{1,0:T(8,128)(2,1)S(1)} %broadcast_select_fusion.8), channel_id=1, source_target_pairs={{0,1},{1,0},{2,3},{3,2},{4,5},{5,4},{6,7},{7,6},{8,9},{9,8},{10,11... | collective-permute-start | bytes 552968 | tf_op jit(solution)/shard_map/ppermute | solution.py:33
  133.5 2.2 %collective-permute-start.57 = (bf16[240,384]{1,0:T(8,128)(2,1)S(1)}, bf16[240,384]{1,0:T(8,128)(2,1)S(1)}, u32[]{:S(2)}, u32[]{:S(2)}) collective-permute-start(bf16[240,384]{1,0:T(8,128)(2,1)S(1)} %broadcast_select_fusion.2), channel_id=1, source_target_pairs={{0,1},{1,0},{2,3},{3,2},{4,5},{5,4},{6,7},{7,6},{8,9},{9,8},{10,11... | collective-permute-start | bytes 552968 | tf_op jit(solution)/shard_map/ppermute | solution.py:33
  135.9 3.8 %collective-permute-start.27 = (bf16[240,384]{1,0:T(8,128)(2,1)S(1)}, bf16[240,384]{1,0:T(8,128)(2,1)S(1)}, u32[]{:S(2)}, u32[]{:S(2)}) collective-permute-start(bf16[240,384]{1,0:T(8,128)(2,1)S(1)} %fusion.4), channel_id=1, source_target_pairs={{0,1},{1,0},{2,3},{3,2},{4,5},{5,4},{6,7},{7,6},{8,9},{9,8},{10,11... | collective-permute-start | bytes 552968 | tf_op jit(solution)/shard_map/ppermute | solution.py:33
  139.7 2.8 %collective-permute-start.59 = (bf16[240,384]{1,0:T(8,128)(2,1)S(1)}, bf16[240,384]{1,0:T(8,128)(2,1)S(1)}, u32[]{:S(2)}, u32[]{:S(2)}) collective-permute-start(bf16[240,384]{1,0:T(8,128)(2,1)S(1)} %fusion.8), channel_id=1, source_target_pairs={{0,1},{1,0},{2,3},{3,2},{4,5},{5,4},{6,7},{7,6},{8,9},{9,8},{10,11... | collective-permute-start | bytes 552968 | tf_op jit(solution)/shard_map/ppermute | solution.py:33
  143.7 2.2 %shard_map.139 = (f32[2,2,128,512]{3,2,1,0:T(8,128)S(1)}, f32[2,2,128,512]{3,2,1,0:T(8,128)S(1)}, f32[8,128]{1,0:T(8,128)S(1)}) custom-call(s32[10]{0:T(128)S(1)} %stack.35.scal, f32[4,16,128]{2,1,0:T(8,128)S(1)} %get-tuple-element.135.refs_0_.refs_1_, f32[2,2,128,512]{3,2,1,0:T(8,128)S(1)} %get-tuple-element.163.refs_1_, ...), custom_call_target="tpu_custom_call" | custom-call | flops 754974720 | bytes 4571136 | tf_op jit(solution)/shard_map/pallas_call | solution.py:484
  145.9 3.9 %collective-permute-done.59.refs_2_ = bf16[240,384]{1,0:T(8,128)(2,1)S(1)} collective-permute-done((bf16[240,384]{1,0:T(8,128)(2,1)S(1)}, bf16[240,384]{1,0:T(8,128)(2,1)S(1)}, u32[]{:S(2)}, u32[]{:S(2)}) %collective-permute-start.59) | collective-permute-done | bytes 184352 | tf_op jit(solution)/shard_map/ppermute | solution.py:33
  150.0 0.8 shard_map.143
  150.8 2.2 %collective-permute-start.65 = (bf16[256,384]{1,0:T(8,128)(2,1)S(1)}, bf16[256,384]{1,0:T(8,128)(2,1)S(1)}, u32[]{:S(2)}, u32[]{:S(2)}) collective-permute-start(bf16[256,384]{1,0:T(8,128)(2,1)S(1)} %get-tuple-element.181.refs_0_.refs_9_.refs_6_), channel_id=1, source_target_pairs={{0,1},{1,0},{2,3},{3,2},{4,5},{5,4},{6,7},{7,6},{8,9},{9,8},{10,11... | collective-permute-start | bytes 589832 | tf_op jit(solution)/shard_map/ppermute | solution.py:33
  153.0 1.3 collective-permute-start.61
  154.4 4.8 %collective-permute-start.63 = (bf16[240,384]{1,0:T(8,128)(2,1)S(1)}, bf16[240,384]{1,0:T(8,128)(2,1)S(1)}, u32[]{:S(2)}, u32[]{:S(2)}) collective-permute-start(bf16[240,384]{1,0:T(8,128)(2,1)S(1)} %collective-permute-done.62.refs_7_.refs_4_), channel_id=1, source_target_pairs={{0,1},{1,0},{2,3},{3,2},{4,5},{5,4},{6,7},{7,6},{8,9},{9,8},{10,11... | collective-permute-start | bytes 552968 | tf_op jit(solution)/shard_map/ppermute | solution.py:33
  159.2 3.1 %collective-permute-start.68 = (bf16[256,384]{1,0:T(8,128)(2,1)S(1)}, bf16[256,384]{1,0:T(8,128)(2,1)S(1)}, u32[]{:S(2)}, u32[]{:S(2)}) collective-permute-start(bf16[256,384]{1,0:T(8,128)(2,1)S(1)} %broadcast_select_fusion), channel_id=1, source_target_pairs={{0,3},{3,0},{1,2},{2,1},{4,7},{7,4},{5,6},{6,5},{8,11},{11,8},{9,1... | collective-permute-start | bytes 589832 | tf_op jit(solution)/shard_map/ppermute | solution.py:33
  162.3 1.1 collective-permute-start.67
  163.4 3.1 %collective-permute-start.64 = (bf16[240,384]{1,0:T(8,128)(2,1)S(1)}, bf16[240,384]{1,0:T(8,128)(2,1)S(1)}, u32[]{:S(2)}, u32[]{:S(2)}) collective-permute-start(bf16[240,384]{1,0:T(8,128)(2,1)S(1)} %broadcast_select_fusion.1), channel_id=1, source_target_pairs={{0,3},{3,0},{1,2},{2,1},{4,7},{7,4},{5,6},{6,5},{8,11},{11,8},{9,1... | collective-permute-start | bytes 552968 | tf_op jit(solution)/shard_map/ppermute | solution.py:33
  166.5 3.3 %shard_map.144 = (bf16[4,512,768]{2,1,0:T(8,128)(2,1)}, bf16[4,512,768]{2,1,0:T(8,128)(2,1)}, bf16[4,768,512]{2,1,0:T(8,128)(2,1)}, f32[8,128]{1,0:T(8,128)S(1)}) custom-call(s32[10]{0:T(128)S(1)} %stack.35.scal, bf16[320,512]{1,0:T(8,128)(2,1)S(1)} %get-tuple-element.110.in_ref, ...), custom_call_target="tpu_custom_call", output_to_operand_aliasing={{0}: (16, {}), {1}: (17, {}), {2}: (18, {})} | custom-call | flops 754974720 | bytes 4571136 | tf_op jit(solution)/shard_map/pallas_call | solution.py:508
  169.8 9.1 %collective-permute-done.64.refs_8_.refs_5_ = bf16[240,384]{1,0:T(8,128)(2,1)S(1)} collective-permute-done((bf16[240,384]{1,0:T(8,128)(2,1)S(1)}, bf16[240,384]{1,0:T(8,128)(2,1)S(1)}, u32[]{:S(2)}, u32[]{:S(2)}) %collective-permute-start.64) | collective-permute-done | bytes 184352 | tf_op jit(solution)/shard_map/ppermute | solution.py:33
  178.9 2.8 %shard_map.145 = (bf16[2,2,128,512]{3,2,1,0:T(8,128)(2,1)S(1)}, bf16[2,2,128,512]{3,2,1,0:T(8,128)(2,1)S(1)}, f32[8,128]{1,0:T(8,128)}, f32[2,16,128]{2,1,0:T(8,128)S(1)}, f32[2,16,128]{2,1,0:T(8,128)S(1)}) custom-call(s32[10]{0:T(128)S(1)} %stack.35.scal, f32[8,128]{1,0:T(8,128)S(1)} %get-tuple-element.185.refs_0_, ...), custom_call_target="tpu_custom_call" | custom-call | flops 754974720 | bytes 4202496 | tf_op jit(solution)/shard_map/pallas_call | solution.py:484
  182.3 1.4 collective-permute-done.69
  183.9 1.6 collective-permute-start.70
  186.1 3.3 %shard_map.146 = (bf16[4,512,768]{2,1,0:T(8,128)(2,1)}, bf16[4,512,768]{2,1,0:T(8,128)(2,1)}, bf16[4,768,512]{2,1,0:T(8,128)(2,1)}, f32[8,128]{1,0:T(8,128)}) custom-call(s32[10]{0:T(128)S(1)} %stack.35.scal, bf16[320,512]{1,0:T(8,128)(2,1)S(1)} %get-tuple-element.194.in_ref, ...), custom_call_target="tpu_custom_call", output_to_operand_aliasing={{0}: (14, {}), {1}: (15, {}), {2}: (16, {})} | custom-call | flops 754974720 | bytes 4202496 | tf_op jit(solution)/shard_map/pallas_call | solution.py:508
  189.3 3.2 %collective-permute-done.72 = f32[16,128]{1,0:T(8,128)S(1)} collective-permute-done((f32[16,128]{1,0:T(8,128)S(1)}, f32[16,128]{1,0:T(8,128)S(1)}, u32[]{:S(2)}, u32[]{:S(2)}) %collective-permute-start.72) | collective-permute-done | bytes 8224 | tf_op jit(solution)/shard_map/ppermute | solution.py:33
  193.2 0.7 slice_bitcast_fusion.2
  (155 shorter events, 9.3 us)
Async XLA Ops:
  1.7 9.7 %collective-permute-start = (bf16[272,512]{1,0:T(8,128)(2,1)S(1)}, bf16[272,512]{1,0:T(8,128)(2,1)S(1)}, u32[]{:S(2)}, u32[]{:S(2)}) collective-permute-start(bf16[272,512]{1,0:T(8,128)(2,1)S(1)} %shard_map.118.refs_0_.refs_1_), channel_id=1, source_target_pairs={{0,8},{4,12},{8,0},{12,4},{1,9},{5,13},{9,1},{13,5},{2,10},{6,14},... | collective-permute-start | bytes 835592 | tf_op jit(solution)/shard_map/ppermute | solution.py:33
  4.7 6.7 %collective-permute-start.1 = (bf16[272,512]{1,0:T(8,128)(2,1)S(1)}, bf16[272,512]{1,0:T(8,128)(2,1)S(1)}, u32[]{:S(2)}, u32[]{:S(2)}) collective-permute-start(bf16[272,512]{1,0:T(8,128)(2,1)S(1)} %shard_map.118.refs_0_.refs_1_), channel_id=1, source_target_pairs={{0,4},{4,0},{8,12},{12,8},{1,5},{5,1},{9,13},{13,9},{2,6},{6,2},{1... | collective-permute-start | bytes 835592 | tf_op jit(solution)/shard_map/ppermute | solution.py:33
  16.4 7.8 %collective-permute-start.3 = (bf16[240,384]{1,0:T(8,128)(2,1)S(1)}, bf16[240,384]{1,0:T(8,128)(2,1)S(1)}, u32[]{:S(2)}, u32[]{:S(2)}) collective-permute-start(bf16[240,384]{1,0:T(8,128)(2,1)S(1)} %get-tuple-element.107.refs_0_), channel_id=1, source_target_pairs={{0,1},{1,0},{2,3},{3,2},{4,5},{5,4},{6,7},{7,6},{8,9},{9,8},{10,11... | collective-permute-start | bytes 552968 | tf_op jit(solution)/shard_map/ppermute | solution.py:33
  18.3 9.6 %collective-permute-start.6 = (bf16[240,384]{1,0:T(8,128)(2,1)S(1)}, bf16[240,384]{1,0:T(8,128)(2,1)S(1)}, u32[]{:S(2)}, u32[]{:S(2)}) collective-permute-start(bf16[240,384]{1,0:T(8,128)(2,1)S(1)} %get-tuple-element.108), channel_id=1, source_target_pairs={{0,1},{1,0},{2,3},{3,2},{4,5},{5,4},{6,7},{7,6},{8,9},{9,8},{10,11... | collective-permute-start | bytes 552968 | tf_op jit(solution)/shard_map/ppermute | solution.py:33
  18.5 13.3 %collective-permute-start.32 = (bf16[240,384]{1,0:T(8,128)(2,1)S(1)}, bf16[240,384]{1,0:T(8,128)(2,1)S(1)}, u32[]{:S(2)}, u32[]{:S(2)}) collective-permute-start(bf16[240,384]{1,0:T(8,128)(2,1)S(1)} %get-tuple-element.131.refs_1_), channel_id=1, source_target_pairs={{0,1},{1,0},{2,3},{3,2},{4,5},{5,4},{6,7},{7,6},{8,9},{9,8},{10,11... | collective-permute-start | bytes 552968 | tf_op jit(solution)/shard_map/ppermute | solution.py:33
  20.4 14.8 %collective-permute-start.35 = (bf16[240,384]{1,0:T(8,128)(2,1)S(1)}, bf16[240,384]{1,0:T(8,128)(2,1)S(1)}, u32[]{:S(2)}, u32[]{:S(2)}) collective-permute-start(bf16[240,384]{1,0:T(8,128)(2,1)S(1)} %get-tuple-element.132), channel_id=1, source_target_pairs={{0,1},{1,0},{2,3},{3,2},{4,5},{5,4},{6,7},{7,6},{8,9},{9,8},{10,11... | collective-permute-start | bytes 552968 | tf_op jit(solution)/shard_map/ppermute | solution.py:33
  24.3 10.9 %collective-permute-start.4 = (bf16[240,384]{1,0:T(8,128)(2,1)S(1)}, bf16[240,384]{1,0:T(8,128)(2,1)S(1)}, u32[]{:S(2)}, u32[]{:S(2)}) collective-permute-start(bf16[240,384]{1,0:T(8,128)(2,1)S(1)} %shard_map.120), channel_id=1, source_target_pairs={{1,2},{2,1},{0,4},{3,7},{5,6},{6,5},{4,0},{7,3},{9,10},{10,9},{8,1... | collective-permute-start | bytes 552968 | tf_op jit(solution)/shard_map/ppermute | solution.py:533
  28.0 12.6 %collective-permute-start.7 = (bf16[240,384]{1,0:T(8,128)(2,1)S(1)}, bf16[240,384]{1,0:T(8,128)(2,1)S(1)}, u32[]{:S(2)}, u32[]{:S(2)}) collective-permute-start(bf16[240,384]{1,0:T(8,128)(2,1)S(1)} %fusion.9), channel_id=1, source_target_pairs={{1,2},{2,1},{0,4},{3,7},{5,6},{6,5},{4,0},{7,3},{9,10},{10,9},{8,1... | collective-permute-start | bytes 552968 | tf_op jit(solution)/shard_map/ppermute | solution.py:533
  31.9 6.8 %collective-permute-start.33 = (bf16[240,384]{1,0:T(8,128)(2,1)S(1)}, bf16[240,384]{1,0:T(8,128)(2,1)S(1)}, u32[]{:S(2)}, u32[]{:S(2)}) collective-permute-start(bf16[240,384]{1,0:T(8,128)(2,1)S(1)} %shard_map.130), channel_id=1, source_target_pairs={{1,2},{2,1},{0,4},{3,7},{5,6},{6,5},{4,0},{7,3},{9,10},{10,9},{8,1... | collective-permute-start | bytes 552968 | tf_op jit(solution)/shard_map/ppermute | solution.py:533
  35.2 11.7 %collective-permute-start.36 = (bf16[240,384]{1,0:T(8,128)(2,1)S(1)}, bf16[240,384]{1,0:T(8,128)(2,1)S(1)}, u32[]{:S(2)}, u32[]{:S(2)}) collective-permute-start(bf16[240,384]{1,0:T(8,128)(2,1)S(1)} %fusion.13), channel_id=1, source_target_pairs={{1,2},{2,1},{0,4},{3,7},{5,6},{6,5},{4,0},{7,3},{9,10},{10,9},{8,1... | collective-permute-start | bytes 552968 | tf_op jit(solution)/shard_map/ppermute | solution.py:533
  35.3 8.9 %collective-permute-start.5 = (bf16[240,384]{1,0:T(8,128)(2,1)S(1)}, bf16[240,384]{1,0:T(8,128)(2,1)S(1)}, u32[]{:S(2)}, u32[]{:S(2)}) collective-permute-start(bf16[240,384]{1,0:T(8,128)(2,1)S(1)} %fusion.1), channel_id=1, source_target_pairs={{0,1},{1,0},{2,3},{3,2},{4,5},{5,4},{6,7},{7,6},{8,9},{9,8},{10,11... | collective-permute-start | bytes 552968 | tf_op jit(solution)/shard_map/ppermute | solution.py:33
  38.8 8.1 %collective-permute-start.34 = (bf16[240,384]{1,0:T(8,128)(2,1)S(1)}, bf16[240,384]{1,0:T(8,128)(2,1)S(1)}, u32[]{:S(2)}, u32[]{:S(2)}) collective-permute-start(bf16[240,384]{1,0:T(8,128)(2,1)S(1)} %fusion.5), channel_id=1, source_target_pairs={{0,1},{1,0},{2,3},{3,2},{4,5},{5,4},{6,7},{7,6},{8,9},{9,8},{10,11... | collective-permute-start | bytes 552968 | tf_op jit(solution)/shard_map/ppermute | solution.py:33
  44.5 7.9 %collective-permute-start.12 = (bf16[240,384]{1,0:T(8,128)(2,1)S(1)}, bf16[240,384]{1,0:T(8,128)(2,1)S(1)}, u32[]{:S(2)}, u32[]{:S(2)}) collective-permute-start(bf16[240,384]{1,0:T(8,128)(2,1)S(1)} %get-tuple-element.109.refs_7_), channel_id=1, source_target_pairs={{0,1},{1,0},{2,3},{3,2},{4,5},{5,4},{6,7},{7,6},{8,9},{9,8},{10,11... | collective-permute-start | bytes 552968 | tf_op jit(solution)/shard_map/ppermute | solution.py:33
  47.0 10.2 %collective-permute-start.37 = (bf16[240,384]{1,0:T(8,128)(2,1)S(1)}, bf16[240,384]{1,0:T(8,128)(2,1)S(1)}, u32[]{:S(2)}, u32[]{:S(2)}) collective-permute-start(bf16[240,384]{1,0:T(8,128)(2,1)S(1)} %get-tuple-element.136.refs_1_), channel_id=1, source_target_pairs={{0,1},{1,0},{2,3},{3,2},{4,5},{5,4},{6,7},{7,6},{8,9},{9,8},{10,11... | collective-permute-start | bytes 552968 | tf_op jit(solution)/shard_map/ppermute | solution.py:33
  48.8 12.2 %collective-permute-start.9 = (bf16[240,384]{1,0:T(8,128)(2,1)S(1)}, bf16[240,384]{1,0:T(8,128)(2,1)S(1)}, u32[]{:S(2)}, u32[]{:S(2)}) collective-permute-start(bf16[240,384]{1,0:T(8,128)(2,1)S(1)} %broadcast_select_fusion.13), channel_id=1, source_target_pairs={{0,1},{1,0},{2,3},{3,2},{4,5},{5,4},{6,7},{7,6},{8,9},{9,8},{10,11... | collective-permute-start | bytes 552968 | tf_op jit(solution)/shard_map/ppermute | solution.py:33
  52.3 9.3 %collective-permute-start.13 = (bf16[240,384]{1,0:T(8,128)(2,1)S(1)}, bf16[240,384]{1,0:T(8,128)(2,1)S(1)}, u32[]{:S(2)}, u32[]{:S(2)}) collective-permute-start(bf16[240,384]{1,0:T(8,128)(2,1)S(1)} %collective-permute-done.12.refs_8_), channel_id=1, source_target_pairs={{1,2},{2,1},{0,4},{3,7},{5,6},{6,5},{4,0},{7,3},{9,10},{10,9},{8,1... | collective-permute-start | bytes 552968 | tf_op jit(solution)/shard_map/ppermute | solution.py:533
  52.4 13.2 %collective-permute-start.39 = (bf16[240,384]{1,0:T(8,128)(2,1)S(1)}, bf16[240,384]{1,0:T(8,128)(2,1)S(1)}, u32[]{:S(2)}, u32[]{:S(2)}) collective-permute-start(bf16[240,384]{1,0:T(8,128)(2,1)S(1)} %broadcast_select_fusion.7), channel_id=1, source_target_pairs={{0,1},{1,0},{2,3},{3,2},{4,5},{5,4},{6,7},{7,6},{8,9},{9,8},{10,11... | collective-permute-start | bytes 552968 | tf_op jit(solution)/shard_map/ppermute | solution.py:33
  57.3 7.1 %collective-permute-start.40 = (bf16[240,384]{1,0:T(8,128)(2,1)S(1)}, bf16[240,384]{1,0:T(8,128)(2,1)S(1)}, u32[]{:S(2)}, u32[]{:S(2)}) collective-permute-start(bf16[240,384]{1,0:T(8,128)(2,1)S(1)} %collective-permute-done.37.refs_2_), channel_id=1, source_target_pairs={{1,2},{2,1},{0,4},{3,7},{5,6},{6,5},{4,0},{7,3},{9,10},{10,9},{8,1... | collective-permute-start | bytes 552968 | tf_op jit(solution)/shard_map/ppermute | solution.py:533
  61.7 9.0 %collective-permute-start.14 = (bf16[240,384]{1,0:T(8,128)(2,1)S(1)}, bf16[240,384]{1,0:T(8,128)(2,1)S(1)}, u32[]{:S(2)}, u32[]{:S(2)}) collective-permute-start(bf16[240,384]{1,0:T(8,128)(2,1)S(1)} %broadcast_select_fusion.12), channel_id=1, source_target_pairs={{0,1},{1,0},{2,3},{3,2},{4,5},{5,4},{6,7},{7,6},{8,9},{9,8},{10,11... | collective-permute-start | bytes 552968 | tf_op jit(solution)/shard_map/ppermute | solution.py:33
  64.4 9.8 %collective-permute-start.41 = (bf16[240,384]{1,0:T(8,128)(2,1)S(1)}, bf16[240,384]{1,0:T(8,128)(2,1)S(1)}, u32[]{:S(2)}, u32[]{:S(2)}) collective-permute-start(bf16[240,384]{1,0:T(8,128)(2,1)S(1)} %broadcast_select_fusion.6), channel_id=1, source_target_pairs={{0,1},{1,0},{2,3},{3,2},{4,5},{5,4},{6,7},{7,6},{8,9},{9,8},{10,11... | collective-permute-start | bytes 552968 | tf_op jit(solution)/shard_map/ppermute | solution.py:33
  65.6 5.2 %collective-permute-start.42 = (bf16[240,384]{1,0:T(8,128)(2,1)S(1)}, bf16[240,384]{1,0:T(8,128)(2,1)S(1)}, u32[]{:S(2)}, u32[]{:S(2)}) collective-permute-start(bf16[240,384]{1,0:T(8,128)(2,1)S(1)} %shard_map.133), channel_id=1, source_target_pairs={{1,2},{2,1},{0,4},{3,7},{5,6},{6,5},{4,0},{7,3},{9,10},{10,9},{8,1... | collective-permute-start | bytes 552968 | tf_op jit(solution)/shard_map/ppermute | solution.py:533
  65.8 12.1 %collective-permute-start.11 = (bf16[240,384]{1,0:T(8,128)(2,1)S(1)}, bf16[240,384]{1,0:T(8,128)(2,1)S(1)}, u32[]{:S(2)}, u32[]{:S(2)}) collective-permute-start(bf16[240,384]{1,0:T(8,128)(2,1)S(1)} %fusion.2), channel_id=1, source_target_pairs={{0,1},{1,0},{2,3},{3,2},{4,5},{5,4},{6,7},{7,6},{8,9},{9,8},{10,11... | collective-permute-start | bytes 552968 | tf_op jit(solution)/shard_map/ppermute | solution.py:33
  70.8 7.1 %collective-permute-start.15 = (bf16[240,384]{1,0:T(8,128)(2,1)S(1)}, bf16[240,384]{1,0:T(8,128)(2,1)S(1)}, u32[]{:S(2)}, u32[]{:S(2)}) collective-permute-start(bf16[240,384]{1,0:T(8,128)(2,1)S(1)} %fusion.10), channel_id=1, source_target_pairs={{1,2},{2,1},{0,4},{3,7},{5,6},{6,5},{4,0},{7,3},{9,10},{10,9},{8,1... | collective-permute-start | bytes 552968 | tf_op jit(solution)/shard_map/ppermute | solution.py:533
  70.9 12.6 %collective-permute-start.43 = (bf16[240,384]{1,0:T(8,128)(2,1)S(1)}, bf16[240,384]{1,0:T(8,128)(2,1)S(1)}, u32[]{:S(2)}, u32[]{:S(2)}) collective-permute-start(bf16[240,384]{1,0:T(8,128)(2,1)S(1)} %fusion.6), channel_id=1, source_target_pairs={{0,1},{1,0},{2,3},{3,2},{4,5},{5,4},{6,7},{7,6},{8,9},{9,8},{10,11... | collective-permute-start | bytes 552968 | tf_op jit(solution)/shard_map/ppermute | solution.py:33
  74.3 9.2 %collective-permute-start.44 = (bf16[240,384]{1,0:T(8,128)(2,1)S(1)}, bf16[240,384]{1,0:T(8,128)(2,1)S(1)}, u32[]{:S(2)}, u32[]{:S(2)}) collective-permute-start(bf16[240,384]{1,0:T(8,128)(2,1)S(1)} %fusion.14), channel_id=1, source_target_pairs={{1,2},{2,1},{0,4},{3,7},{5,6},{6,5},{4,0},{7,3},{9,10},{10,9},{8,1... | collective-permute-start | bytes 552968 | tf_op jit(solution)/shard_map/ppermute | solution.py:533
  78.0 9.3 %collective-permute-start.16 = (bf16[240,384]{1,0:T(8,128)(2,1)S(1)}, bf16[240,384]{1,0:T(8,128)(2,1)S(1)}, u32[]{:S(2)}, u32[]{:S(2)}) collective-permute-start(bf16[240,384]{1,0:T(8,128)(2,1)S(1)} %get-tuple-element.117.refs_9_.refs_0_.refs_7_), channel_id=1, source_target_pairs={{1,2},{2,1},{0,4},{3,7},{5,6},{6,5},{4,0},{7,3},{9,10},{10,9},{8,1... | collective-permute-start | bytes 552968 | tf_op jit(solution)/shard_map/ppermute | solution.py:533
  80.3 9.0 %collective-permute-start.20 = (bf16[240,384]{1,0:T(8,128)(2,1)S(1)}, bf16[240,384]{1,0:T(8,128)(2,1)S(1)}, u32[]{:S(2)}, u32[]{:S(2)}) collective-permute-start(bf16[240,384]{1,0:T(8,128)(2,1)S(1)} %get-tuple-element.117.refs_9_.refs_0_.refs_7_), channel_id=1, source_target_pairs={{0,1},{1,0},{2,3},{3,2},{4,5},{5,4},{6,7},{7,6},{8,9},{9,8},{10,11... | collective-permute-start | bytes 552968 | tf_op jit(solution)/shard_map/ppermute | solution.py:33
  83.7 8.6 %collective-permute-start.45 = (bf16[240,384]{1,0:T(8,128)(2,1)S(1)}, bf16[240,384]{1,0:T(8,128)(2,1)S(1)}, u32[]{:S(2)}, u32[]{:S(2)}) collective-permute-start(bf16[240,384]{1,0:T(8,128)(2,1)S(1)} %get-tuple-element.149.refs_3_.refs_1_), channel_id=1, source_target_pairs={{0,1},{1,0},{2,3},{3,2},{4,5},{5,4},{6,7},{7,6},{8,9},{9,8},{10,11... | collective-permute-start | bytes 552968 | tf_op jit(solution)/shard_map/ppermute | solution.py:33
  83.8 5.5 %collective-permute-start.46 = (bf16[240,384]{1,0:T(8,128)(2,1)S(1)}, bf16[240,384]{1,0:T(8,128)(2,1)S(1)}, u32[]{:S(2)}, u32[]{:S(2)}) collective-permute-start(bf16[240,384]{1,0:T(8,128)(2,1)S(1)} %get-tuple-element.149.refs_3_.refs_1_), channel_id=1, source_target_pairs={{1,2},{2,1},{0,4},{3,7},{5,6},{6,5},{4,0},{7,3},{9,10},{10,9},{8,1... | collective-permute-start | bytes 552968 | tf_op jit(solution)/shard_map/ppermute | solution.py:533
  87.4 8.8 %collective-permute-start.17 = (bf16[240,384]{1,0:T(8,128)(2,1)S(1)}, bf16[240,384]{1,0:T(8,128)(2,1)S(1)}, u32[]{:S(2)}, u32[]{:S(2)}) collective-permute-start(bf16[240,384]{1,0:T(8,128)(2,1)S(1)} %broadcast_select_fusion.11), channel_id=1, source_target_pairs={{0,1},{1,0},{2,3},{3,2},{4,5},{5,4},{6,7},{7,6},{8,9},{9,8},{10,11... | collective-permute-start | bytes 552968 | tf_op jit(solution)/shard_map/ppermute | solution.py:33
  89.3 7.3 %collective-permute-start.21 = (bf16[240,384]{1,0:T(8,128)(2,1)S(1)}, bf16[240,384]{1,0:T(8,128)(2,1)S(1)}, u32[]{:S(2)}, u32[]{:S(2)}) collective-permute-start(bf16[240,384]{1,0:T(8,128)(2,1)S(1)} %collective-permute-done.20.refs_10_.refs_8_), channel_id=1, source_target_pairs={{1,2},{2,1},{0,4},{3,7},{5,6},{6,5},{4,0},{7,3},{9,10},{10,9},{8,1... | collective-permute-start | bytes 552968 | tf_op jit(solution)/shard_map/ppermute | solution.py:533
  89.3 10.9 %collective-permute-start.47 = (bf16[240,384]{1,0:T(8,128)(2,1)S(1)}, bf16[240,384]{1,0:T(8,128)(2,1)S(1)}, u32[]{:S(2)}, u32[]{:S(2)}) collective-permute-start(bf16[240,384]{1,0:T(8,128)(2,1)S(1)} %broadcast_select_fusion.5), channel_id=1, source_target_pairs={{0,1},{1,0},{2,3},{3,2},{4,5},{5,4},{6,7},{7,6},{8,9},{9,8},{10,11... | collective-permute-start | bytes 552968 | tf_op jit(solution)/shard_map/ppermute | solution.py:33
  92.2 6.7 %collective-permute-start.48 = (bf16[240,384]{1,0:T(8,128)(2,1)S(1)}, bf16[240,384]{1,0:T(8,128)(2,1)S(1)}, u32[]{:S(2)}, u32[]{:S(2)}) collective-permute-start(bf16[240,384]{1,0:T(8,128)(2,1)S(1)} %collective-permute-done.45.refs_4_.refs_2_), channel_id=1, source_target_pairs={{1,2},{2,1},{0,4},{3,7},{5,6},{6,5},{4,0},{7,3},{9,10},{10,9},{8,1... | collective-permute-start | bytes 552968 | tf_op jit(solution)/shard_map/ppermute | solution.py:533
  96.6 9.4 %collective-permute-start.22 = (bf16[240,384]{1,0:T(8,128)(2,1)S(1)}, bf16[240,384]{1,0:T(8,128)(2,1)S(1)}, u32[]{:S(2)}, u32[]{:S(2)}) collective-permute-start(bf16[240,384]{1,0:T(8,128)(2,1)S(1)} %broadcast_select_fusion.10), channel_id=1, source_target_pairs={{0,1},{1,0},{2,3},{3,2},{4,5},{5,4},{6,7},{7,6},{8,9},{9,8},{10,11... | collective-permute-start | bytes 552968 | tf_op jit(solution)/shard_map/ppermute | solution.py:33
  99.0 11.0 %collective-permute-start.49 = (bf16[240,384]{1,0:T(8,128)(2,1)S(1)}, bf16[240,384]{1,0:T(8,128)(2,1)S(1)}, u32[]{:S(2)}, u32[]{:S(2)}) collective-permute-start(bf16[240,384]{1,0:T(8,128)(2,1)S(1)} %broadcast_select_fusion.4), channel_id=1, source_target_pairs={{0,1},{1,0},{2,3},{3,2},{4,5},{5,4},{6,7},{7,6},{8,9},{9,8},{10,11... | collective-permute-start | bytes 552968 | tf_op jit(solution)/shard_map/ppermute | solution.py:33
  100.3 5.9 %collective-permute-start.50 = (bf16[240,384]{1,0:T(8,128)(2,1)S(1)}, bf16[240,384]{1,0:T(8,128)(2,1)S(1)}, u32[]{:S(2)}, u32[]{:S(2)}) collective-permute-start(bf16[240,384]{1,0:T(8,128)(2,1)S(1)} %shard_map.137), channel_id=1, source_target_pairs={{1,2},{2,1},{0,4},{3,7},{5,6},{6,5},{4,0},{7,3},{9,10},{10,9},{8,1... | collective-permute-start | bytes 552968 | tf_op jit(solution)/shard_map/ppermute | solution.py:533
  100.4 11.9 %collective-permute-start.19 = (bf16[240,384]{1,0:T(8,128)(2,1)S(1)}, bf16[240,384]{1,0:T(8,128)(2,1)S(1)}, u32[]{:S(2)}, u32[]{:S(2)}) collective-permute-start(bf16[240,384]{1,0:T(8,128)(2,1)S(1)} %fusion.3), channel_id=1, source_target_pairs={{0,1},{1,0},{2,3},{3,2},{4,5},{5,4},{6,7},{7,6},{8,9},{9,8},{10,11... | collective-permute-start | bytes 552968 | tf_op jit(solution)/shard_map/ppermute | solution.py:33
  106.1 6.2 %collective-permute-start.23 = (bf16[240,384]{1,0:T(8,128)(2,1)S(1)}, bf16[240,384]{1,0:T(8,128)(2,1)S(1)}, u32[]{:S(2)}, u32[]{:S(2)}) collective-permute-start(bf16[240,384]{1,0:T(8,128)(2,1)S(1)} %fusion.11), channel_id=1, source_target_pairs={{1,2},{2,1},{0,4},{3,7},{5,6},{6,5},{4,0},{7,3},{9,10},{10,9},{8,1... | collective-permute-start | bytes 552968 | tf_op jit(solution)/shard_map/ppermute | solution.py:533
  106.3 11.8 %collective-permute-start.51 = (bf16[240,384]{1,0:T(8,128)(2,1)S(1)}, bf16[240,384]{1,0:T(8,128)(2,1)S(1)}, u32[]{:S(2)}, u32[]{:S(2)}) collective-permute-start(bf16[240,384]{1,0:T(8,128)(2,1)S(1)} %fusion.7), channel_id=1, source_target_pairs={{0,1},{1,0},{2,3},{3,2},{4,5},{5,4},{6,7},{7,6},{8,9},{9,8},{10,11... | collective-permute-start | bytes 552968 | tf_op jit(solution)/shard_map/ppermute | solution.py:33
  110.0 8.1 %collective-permute-start.52 = (bf16[240,384]{1,0:T(8,128)(2,1)S(1)}, bf16[240,384]{1,0:T(8,128)(2,1)S(1)}, u32[]{:S(2)}, u32[]{:S(2)}) collective-permute-start(bf16[240,384]{1,0:T(8,128)(2,1)S(1)} %fusion.15), channel_id=1, source_target_pairs={{1,2},{2,1},{0,4},{3,7},{5,6},{6,5},{4,0},{7,3},{9,10},{10,9},{8,1... | collective-permute-start | bytes 552968 | tf_op jit(solution)/shard_map/ppermute | solution.py:533
  112.5 9.2 %collective-permute-start.24 = (bf16[240,384]{1,0:T(8,128)(2,1)S(1)}, bf16[240,384]{1,0:T(8,128)(2,1)S(1)}, u32[]{:S(2)}, u32[]{:S(2)}) collective-permute-start(bf16[240,384]{1,0:T(8,128)(2,1)S(1)} %get-tuple-element.126.refs_9_.refs_0_.refs_7_), channel_id=1, source_target_pairs={{1,2},{2,1},{0,4},{3,7},{5,6},{6,5},{4,0},{7,3},{9,10},{10,9},{8,1... | collective-permute-start | bytes 552968 | tf_op jit(solution)/shard_map/ppermute | solution.py:533
  114.8 8.9 %collective-permute-start.28 = (bf16[240,384]{1,0:T(8,128)(2,1)S(1)}, bf16[240,384]{1,0:T(8,128)(2,1)S(1)}, u32[]{:S(2)}, u32[]{:S(2)}) collective-permute-start(bf16[240,384]{1,0:T(8,128)(2,1)S(1)} %get-tuple-element.126.refs_9_.refs_0_.refs_7_), channel_id=1, source_target_pairs={{0,1},{1,0},{2,3},{3,2},{4,5},{5,4},{6,7},{7,6},{8,9},{9,8},{10,11... | collective-permute-start | bytes 552968 | tf_op jit(solution)/shard_map/ppermute | solution.py:33
  118.2 8.5 %collective-permute-start.53 = (bf16[240,384]{1,0:T(8,128)(2,1)S(1)}, bf16[240,384]{1,0:T(8,128)(2,1)S(1)}, u32[]{:S(2)}, u32[]{:S(2)}) collective-permute-start(bf16[240,384]{1,0:T(8,128)(2,1)S(1)} %get-tuple-element.165.refs_3_.refs_1_), channel_id=1, source_target_pairs={{0,1},{1,0},{2,3},{3,2},{4,5},{5,4},{6,7},{7,6},{8,9},{9,8},{10,11... | collective-permute-start | bytes 552968 | tf_op jit(solution)/shard_map/ppermute | solution.py:33
  118.3 5.4 %collective-permute-start.54 = (bf16[240,384]{1,0:T(8,128)(2,1)S(1)}, bf16[240,384]{1,0:T(8,128)(2,1)S(1)}, u32[]{:S(2)}, u32[]{:S(2)}) collective-permute-start(bf16[240,384]{1,0:T(8,128)(2,1)S(1)} %get-tuple-element.165.refs_3_.refs_1_), channel_id=1, source_target_pairs={{1,2},{2,1},{0,4},{3,7},{5,6},{6,5},{4,0},{7,3},{9,10},{10,9},{8,1... | collective-permute-start | bytes 552968 | tf_op jit(solution)/shard_map/ppermute | solution.py:533
  121.7 8.9 %collective-permute-start.25 = (bf16[240,384]{1,0:T(8,128)(2,1)S(1)}, bf16[240,384]{1,0:T(8,128)(2,1)S(1)}, u32[]{:S(2)}, u32[]{:S(2)}) collective-permute-start(bf16[240,384]{1,0:T(8,128)(2,1)S(1)} %broadcast_select_fusion.9), channel_id=1, source_target_pairs={{0,1},{1,0},{2,3},{3,2},{4,5},{5,4},{6,7},{7,6},{8,9},{9,8},{10,11... | collective-permute-start | bytes 552968 | tf_op jit(solution)/shard_map/ppermute | solution.py:33
  123.7 7.1 %collective-permute-start.29 = (bf16[240,384]{1,0:T(8,128)(2,1)S(1)}, bf16[240,384]{1,0:T(8,128)(2,1)S(1)}, u32[]{:S(2)}, u32[]{:S(2)}) collective-permute-start(bf16[240,384]{1,0:T(8,128)(2,1)S(1)} %collective-permute-done.28.refs_10_.refs_8_), channel_id=1, source_target_pairs={{1,2},{2,1},{0,4},{3,7},{5,6},{6,5},{4,0},{7,3},{9,10},{10,9},{8,1... | collective-permute-start | bytes 552968 | tf_op jit(solution)/shard_map/ppermute | solution.py:533
  123.8 11.9 %collective-permute-start.55 = (bf16[240,384]{1,0:T(8,128)(2,1)S(1)}, bf16[240,384]{1,0:T(8,128)(2,1)S(1)}, u32[]{:S(2)}, u32[]{:S(2)}) collective-permute-start(bf16[240,384]{1,0:T(8,128)(2,1)S(1)} %broadcast_select_fusion.3), channel_id=1, source_target_pairs={{0,1},{1,0},{2,3},{3,2},{4,5},{5,4},{6,7},{7,6},{8,9},{9,8},{10,11... | collective-permute-start | bytes 552968 | tf_op jit(solution)/shard_map/ppermute | solution.py:33
  126.7 6.8 %collective-permute-start.56 = (bf16[240,384]{1,0:T(8,128)(2,1)S(1)}, bf16[240,384]{1,0:T(8,128)(2,1)S(1)}, u32[]{:S(2)}, u32[]{:S(2)}) collective-permute-start(bf16[240,384]{1,0:T(8,128)(2,1)S(1)} %collective-permute-done.53.refs_4_.refs_2_), channel_id=1, source_target_pairs={{1,2},{2,1},{0,4},{3,7},{5,6},{6,5},{4,0},{7,3},{9,10},{10,9},{8,1... | collective-permute-start | bytes 552968 | tf_op jit(solution)/shard_map/ppermute | solution.py:533
  130.7 5.1 %collective-permute-start.26 = (bf16[240,384]{1,0:T(8,128)(2,1)S(1)}, bf16[240,384]{1,0:T(8,128)(2,1)S(1)}, u32[]{:S(2)}, u32[]{:S(2)}) collective-permute-start(bf16[240,384]{1,0:T(8,128)(2,1)S(1)} %shard_map.129), channel_id=1, source_target_pairs={{1,2},{2,1},{0,4},{3,7},{5,6},{6,5},{4,0},{7,3},{9,10},{10,9},{8,1... | collective-permute-start | bytes 552968 | tf_op jit(solution)/shard_map/ppermute | solution.py:533
  130.8 12.3 %collective-permute-start.30 = (bf16[240,384]{1,0:T(8,128)(2,1)S(1)}, bf16[240,384]{1,0:T(8,128)(2,1)S(1)}, u32[]{:S(2)}, u32[]{:S(2)}) collective-permute-start(bf16[240,384]{1,0:T(8,128)(2,1)S(1)} %broadcast_select_fusion.8), channel_id=1, source_target_pairs={{0,1},{1,0},{2,3},{3,2},{4,5},{5,4},{6,7},{7,6},{8,9},{9,8},{10,11... | collective-permute-start | bytes 552968 | tf_op jit(solution)/shard_map/ppermute | solution.py:33
  133.5 9.4 %collective-permute-start.57 = (bf16[240,384]{1,0:T(8,128)(2,1)S(1)}, bf16[240,384]{1,0:T(8,128)(2,1)S(1)}, u32[]{:S(2)}, u32[]{:S(2)}) collective-permute-start(bf16[240,384]{1,0:T(8,128)(2,1)S(1)} %broadcast_select_fusion.2), channel_id=1, source_target_pairs={{0,1},{1,0},{2,3},{3,2},{4,5},{5,4},{6,7},{7,6},{8,9},{9,8},{10,11... | collective-permute-start | bytes 552968 | tf_op jit(solution)/shard_map/ppermute | solution.py:33
  135.9 14.0 %collective-permute-start.27 = (bf16[240,384]{1,0:T(8,128)(2,1)S(1)}, bf16[240,384]{1,0:T(8,128)(2,1)S(1)}, u32[]{:S(2)}, u32[]{:S(2)}) collective-permute-start(bf16[240,384]{1,0:T(8,128)(2,1)S(1)} %fusion.4), channel_id=1, source_target_pairs={{0,1},{1,0},{2,3},{3,2},{4,5},{5,4},{6,7},{7,6},{8,9},{9,8},{10,11... | collective-permute-start | bytes 552968 | tf_op jit(solution)/shard_map/ppermute | solution.py:33
  139.7 10.0 %collective-permute-start.59 = (bf16[240,384]{1,0:T(8,128)(2,1)S(1)}, bf16[240,384]{1,0:T(8,128)(2,1)S(1)}, u32[]{:S(2)}, u32[]{:S(2)}) collective-permute-start(bf16[240,384]{1,0:T(8,128)(2,1)S(1)} %fusion.8), channel_id=1, source_target_pairs={{0,1},{1,0},{2,3},{3,2},{4,5},{5,4},{6,7},{7,6},{8,9},{9,8},{10,11... | collective-permute-start | bytes 552968 | tf_op jit(solution)/shard_map/ppermute | solution.py:33
  143.0 6.8 %collective-permute-start.60 = (bf16[240,384]{1,0:T(8,128)(2,1)S(1)}, bf16[240,384]{1,0:T(8,128)(2,1)S(1)}, u32[]{:S(2)}, u32[]{:S(2)}) collective-permute-start(bf16[240,384]{1,0:T(8,128)(2,1)S(1)} %fusion.16), channel_id=1, source_target_pairs={{1,2},{2,1},{0,4},{3,7},{5,6},{6,5},{4,0},{7,3},{9,10},{10,9},{8,1... | collective-permute-start | bytes 552968 | tf_op jit(solution)/shard_map/ppermute | solution.py:533
  143.2 6.8 %collective-permute-start.31 = (bf16[240,384]{1,0:T(8,128)(2,1)S(1)}, bf16[240,384]{1,0:T(8,128)(2,1)S(1)}, u32[]{:S(2)}, u32[]{:S(2)}) collective-permute-start(bf16[240,384]{1,0:T(8,128)(2,1)S(1)} %fusion.12), channel_id=1, source_target_pairs={{1,2},{2,1},{0,4},{3,7},{5,6},{6,5},{4,0},{7,3},{9,10},{10,9},{8,1... | collective-permute-start | bytes 552968 | tf_op jit(solution)/shard_map/ppermute | solution.py:533
  150.8 8.4 %collective-permute-start.65 = (bf16[256,384]{1,0:T(8,128)(2,1)S(1)}, bf16[256,384]{1,0:T(8,128)(2,1)S(1)}, u32[]{:S(2)}, u32[]{:S(2)}) collective-permute-start(bf16[256,384]{1,0:T(8,128)(2,1)S(1)} %get-tuple-element.181.refs_0_.refs_9_.refs_6_), channel_id=1, source_target_pairs={{0,1},{1,0},{2,3},{3,2},{4,5},{5,4},{6,7},{7,6},{8,9},{9,8},{10,11... | collective-permute-start | bytes 589832 | tf_op jit(solution)/shard_map/ppermute | solution.py:33
  153.0 10.4 %collective-permute-start.61 = (bf16[240,384]{1,0:T(8,128)(2,1)S(1)}, bf16[240,384]{1,0:T(8,128)(2,1)S(1)}, u32[]{:S(2)}, u32[]{:S(2)}) collective-permute-start(bf16[240,384]{1,0:T(8,128)(2,1)S(1)} %get-tuple-element.188.refs_4_.refs_1_), channel_id=1, source_target_pairs={{0,1},{1,0},{2,3},{3,2},{4,5},{5,4},{6,7},{7,6},{8,9},{9,8},{10,11... | collective-permute-start | bytes 552968 | tf_op jit(solution)/shard_map/ppermute | solution.py:33
  154.3 8.0 %collective-permute-start.66 = (bf16[256,384]{1,0:T(8,128)(2,1)S(1)}, bf16[256,384]{1,0:T(8,128)(2,1)S(1)}, u32[]{:S(2)}, u32[]{:S(2)}) collective-permute-start(bf16[256,384]{1,0:T(8,128)(2,1)S(1)} %get-tuple-element.181.refs_0_.refs_9_.refs_6_), channel_id=1, source_target_pairs={{1,2},{2,1},{0,4},{3,7},{5,6},{6,5},{4,0},{7,3},{9,10},{10,9},{8,1... | collective-permute-start | bytes 589832 | tf_op jit(solution)/shard_map/ppermute | solution.py:533
  154.4 15.4 %collective-permute-start.63 = (bf16[240,384]{1,0:T(8,128)(2,1)S(1)}, bf16[240,384]{1,0:T(8,128)(2,1)S(1)}, u32[]{:S(2)}, u32[]{:S(2)}) collective-permute-start(bf16[240,384]{1,0:T(8,128)(2,1)S(1)} %collective-permute-done.62.refs_7_.refs_4_), channel_id=1, source_target_pairs={{0,1},{1,0},{2,3},{3,2},{4,5},{5,4},{6,7},{7,6},{8,9},{9,8},{10,11... | collective-permute-start | bytes 552968 | tf_op jit(solution)/shard_map/ppermute | solution.py:33
  159.2 19.7 %collective-permute-start.68 = (bf16[256,384]{1,0:T(8,128)(2,1)S(1)}, bf16[256,384]{1,0:T(8,128)(2,1)S(1)}, u32[]{:S(2)}, u32[]{:S(2)}) collective-permute-start(bf16[256,384]{1,0:T(8,128)(2,1)S(1)} %broadcast_select_fusion), channel_id=1, source_target_pairs={{0,3},{3,0},{1,2},{2,1},{4,7},{7,4},{5,6},{6,5},{8,11},{11,8},{9,1... | collective-permute-start | bytes 589832 | tf_op jit(solution)/shard_map/ppermute | solution.py:33
  162.3 16.6 %collective-permute-start.67 = (bf16[256,384]{1,0:T(8,128)(2,1)S(1)}, bf16[256,384]{1,0:T(8,128)(2,1)S(1)}, u32[]{:S(2)}, u32[]{:S(2)}) collective-permute-start(bf16[256,384]{1,0:T(8,128)(2,1)S(1)} %collective-permute-done.66.refs_12_.refs_9_), channel_id=1, source_target_pairs={{0,1},{1,0},{2,3},{3,2},{4,5},{5,4},{6,7},{7,6},{8,9},{9,8},{10,11... | collective-permute-start | bytes 589832 | tf_op jit(solution)/shard_map/ppermute | solution.py:33
  163.4 15.5 %collective-permute-start.64 = (bf16[240,384]{1,0:T(8,128)(2,1)S(1)}, bf16[240,384]{1,0:T(8,128)(2,1)S(1)}, u32[]{:S(2)}, u32[]{:S(2)}) collective-permute-start(bf16[240,384]{1,0:T(8,128)(2,1)S(1)} %broadcast_select_fusion.1), channel_id=1, source_target_pairs={{0,3},{3,0},{1,2},{2,1},{4,7},{7,4},{5,6},{6,5},{8,11},{11,8},{9,1... | collective-permute-start | bytes 552968 | tf_op jit(solution)/shard_map/ppermute | solution.py:33
  183.9 9.2 %collective-permute-start.70 = (bf16[2,128,512]{2,1,0:T(8,128)(2,1)S(1)}, bf16[2,128,512]{2,1,0:T(8,128)(2,1)S(1)}, u32[]{:S(2)}, u32[]{:S(2)}) collective-permute-start(bf16[2,128,512]{2,1,0:T(8,128)(2,1)S(1)} %slice_bitcast_fusion), channel_id=1, source_target_pairs={{0,8},{4,12},{8,0},{12,4},{1,9},{5,13},{9,1},{13,5},{2,10},{6,14},... | collective-permute-start | bytes 786440 | tf_op jit(solution)/shard_map/ppermute | solution.py:33
  185.5 7.0 %collective-permute-start.72 = (f32[16,128]{1,0:T(8,128)S(1)}, f32[16,128]{1,0:T(8,128)S(1)}, u32[]{:S(2)}, u32[]{:S(2)}) collective-permute-start(f32[16,128]{1,0:T(8,128)S(1)} %slice_bitcast_fusion.4), channel_id=1, source_target_pairs={{0,8},{4,12},{8,0},{12,4},{1,9},{5,13},{9,1},{13,5},{2,10},{6,14},... | collective-permute-start | bytes 24584 | tf_op jit(solution)/shard_map/ppermute | solution.py:33
  (11 other events, 42.1 us)
